TPU v7x, 32 devices: a whole 2x2x4 slice. The times are simulated.
32 devices in a mesh: user: 32 (over z, y, x, core).
Axes of the slice: x: 2, y: 2, z: 4, core: 2. Of those that a mesh axis runs over, the one named last changes fastest.
Arguments:
- ratings: bfloat16 [32, 3, 6, 128, 128], P('user'), may hold values from -6 to 6
- tile_index: int32 [32, 3, 6], P('user'), may hold values from 0 to 8, as said below
- tile_count: int32 [32, 3], P('user'), may hold values from 1 to 6, as said below
- side_features: bfloat16 [12288, 1024], P('user'), may hold values from -6 to 6
- user_factors: float32 [12288, 256], P('user'), may hold values from -3 to 3
- item_factors: float32 [12288, 256], P('user'), may hold values from -3 to 3
- prior_weights: float32 [1024, 256], replicated, may hold values from -0.1875 to 0.1875
- user_noise: bfloat16 [3, 12288, 256], P(None, 'user'), may hold values from -6 to 6
- item_noise: bfloat16 [3, 12288, 256], P(None, 'user'), may hold values from -6 to 6
Outputs:
- users_out: float32 [12288, 256], P('user')
- items_held: float32 [12288, 256], P('user')
- weights_out: float32 [1024, 256], P('user')
Inputs may be any that keep to these rules, and one draw needn't show every extreme that they name: `tile_index`: code r * 3 + c of a tile; the codes of one device and stratum are distinct. `tile_count`: live slots are the first ones; in every stratum some device has 6.
All inputs are finite; a program needn't handle non-finite values.
Results may differ from a plain program's by a relative error of at most 0.0013.
The roundings to bfloat16 on the way count: a program that leaves them out, or rounds other values in their place, can miss the bound.
Values sent between devices are 32-bit elements; how exact they have to be, the bound alone decides.
No kernel may reach another device: no remote copies, remote signals or barrier semaphores. Data moves between devices by JAX's collectives and lax.ppermute only.
A program may use at most 64 MiB of HBM per device.

v0:
```python
import math

import jax
import jax.numpy as jnp
from jax import lax
from jax.sharding import PartitionSpec as P

step_size = 0.01
prior_prec = 8.0
item_prec = 1.0
weight_decay = 1.0
rate_scale = 0.04


def shifted(array, axis, by):
    devices = lax.axis_size(axis)
    return lax.ppermute(array, axis, [(i, (i + by) % devices) for i in range(devices)])


def tile_pass(tiles, codes, count, user_b, item_b):
    tile = tiles.shape[-1]
    grid = user_b.shape[0] // tile
    slots = tiles.shape[0]

    def one(step, carry):
        sse, grad_u, grad_v = carry
        code = codes[step]
        row_start = code // grid * tile
        col_start = code % grid * tile
        user_tile = lax.dynamic_slice_in_dim(user_b, row_start, tile, 0)
        item_tile = lax.dynamic_slice_in_dim(item_b, col_start, tile, 0)
        pred = lax.dot_general(
            user_tile, item_tile, (((1,), (1,)), ((), ())), preferred_element_type=jnp.float32
        )
        err = lax.dynamic_index_in_dim(tiles, step, 0, keepdims=False).astype(jnp.float32) - pred
        err = err * (step < count).astype(jnp.float32)
        sse = sse + jnp.sum(err * err)
        err_b = err.astype(jnp.bfloat16)
        upd_u = jnp.dot(err_b, item_tile, preferred_element_type=jnp.float32)
        upd_v = lax.dot_general(
            err_b, user_tile, (((0,), (0,)), ((), ())), preferred_element_type=jnp.float32
        )
        grad_u = lax.dynamic_update_slice_in_dim(
            grad_u, lax.dynamic_slice_in_dim(grad_u, row_start, tile, 0) + upd_u, row_start, 0
        )
        grad_v = lax.dynamic_update_slice_in_dim(
            grad_v, lax.dynamic_slice_in_dim(grad_v, col_start, tile, 0) + upd_v, col_start, 0
        )
        return (sse, grad_u, grad_v)

    start = (
        jnp.zeros((), jnp.float32),
        jnp.zeros(user_b.shape, jnp.float32),
        jnp.zeros(item_b.shape, jnp.float32),
    )
    return lax.fori_loop(0, slots, one, start)


def local(
    ratings,
    tile_index,
    tile_count,
    side_features,
    user_factors,
    item_factors,
    prior_weights,
    user_noise,
    item_noise,
):
    devices = lax.axis_size("user")
    own = lax.axis_index("user")
    tile = ratings.shape[-1]
    strata = ratings.shape[1]
    rows_dev = user_factors.shape[0]
    feat_rows = prior_weights.shape[0] // devices
    rate = rate_scale / (rows_dev * devices)
    noise_scale = math.sqrt(2.0 * step_size)
    users = user_factors
    items = item_factors
    weights = prior_weights
    final_rows = weights
    for stratum in range(strata):
        mean = jnp.dot(
            side_features, weights.astype(jnp.bfloat16), preferred_element_type=jnp.float32
        )
        offset = (users - mean).astype(jnp.bfloat16)
        user_b = users.astype(jnp.bfloat16)
        item_b = items.astype(jnp.bfloat16)
        count = tile_count[0, stratum]
        sse, grad_u, grad_v = tile_pass(
            ratings[0, stratum], tile_index[0, stratum], count, user_b, item_b
        )
        count_here = count.astype(jnp.float32) * float(tile * tile)
        total_sse, total_count = lax.psum((sse, count_here), "user")
        precision = (1.0 + total_count / 2.0) / (1.0 + total_sse / 2.0)
        last = stratum + 1 == strata
        grad_w = lax.dot_general(
            side_features, offset, (((0,), (0,)), ((), ())), preferred_element_type=jnp.float32
        )
        total = lax.psum(grad_w, "user")
        full_new = weights + rate * (prior_prec * total - weight_decay * weights)
        if last:
            final_rows = lax.dynamic_slice_in_dim(full_new, own * feat_rows, feat_rows, 0)
        else:
            weights = full_new
        new_users = (
            users
            + step_size * (precision * grad_u - prior_prec * (users - mean))
            + noise_scale * user_noise[stratum].astype(jnp.float32)
        )
        new_items = (
            items
            + step_size * (precision * grad_v - item_prec * items)
            + noise_scale * item_noise[stratum].astype(jnp.float32)
        )
        users = new_users
        if last:
            items = new_items
        else:
            items = shifted(new_items, "user", 1)
    return (users, items, final_rows)


def solution(mesh):
    return jax.shard_map(
        local,
        mesh=mesh,
        in_specs=(
            P("user", None, None, None, None),
            P("user", None, None),
            P("user", None),
            P("user", None),
            P("user", None),
            P("user", None),
            P(),
            P(None, "user", None),
            P(None, "user", None),
        ),
        out_specs=(P("user", None), P("user", None), P("user", None)),
        check_vma=False,
    )
```

profile of v0, /device:TPU:0, one launch (start us, length us, event | category | flops | bytes accessed | tf_op | source)
XLA Modules:
  0.0 500.0 jit_solution(8497258103140062843)
XLA Ops:
  12.0 29.9 %while.57 = (s32[]{:T(128)}, f32[]{:T(128)}, f32[384,256]{1,0:T(8,128)S(1)}, f32[384,256]{1,0:T(8,128)S(1)}, bf16[6,128,128]{2,1,0:T(8,128)(2,1)S(1)}, /*index=5...) while((s32[]{:T(128)}, f32[]{:T(128)}, ...), condition=%wide.region_3.4_spmd, body=%wide.region_1.3_spmd.sunk | while | flops 25329688 | bytes 917950 | solution.py:56
  41.9 42.7 %all-reduce.2 = (f32[]{:T(128)}, f32[]{:T(128)}) all-reduce(f32[]{:T(128)S(6)} %mul.273, f32[]{:T(128)} %get-tuple-element.678), channel_id=1, replica_groups=mesh['user'=32] {'user'}, use_global_device_ids=true, to_apply=%region_0.1 | all-reduce | flops 2 | bytes 16 | tf_op jit(solution)/shard_map/psum | solution.py:94
  86.0 1.8 bitcast_add_fusion.4
  87.8 1.5 fusion.50
  89.3 1.5 convolution_bitcast_fusion.2
  92.4 6.5 %collective-permute-done = f32[384,256]{1,0:T(8,128)} collective-permute-done((f32[384,256]{1,0:T(8,128)}, f32[384,256]{1,0:T(8,128)}, u32[]{:S(2)}, u32[]{:S(2)}) %collective-permute-start) | collective-permute-done | bytes 393248 | tf_op jit(solution)/shard_map/ppermute | solution.py:17
  100.0 34.6 %while.58 = (s32[]{:T(128)}, f32[]{:T(128)}, f32[384,256]{1,0:T(8,128)S(1)}, f32[384,256]{1,0:T(8,128)S(1)}, bf16[6,128,128]{2,1,0:T(8,128)(2,1)}, /*index=5*/s3...) while((s32[]{:T(128)}, f32[]{:T(128)}, ...), condition=%wide.region_8.9_spmd, body=%wide.region_6.8_spmd.sunk | while | flops 25329688 | bytes 917950 | solution.py:56
  103.2 1.5 multiply_reduce_fusion.7
  108.9 1.5 multiply_reduce_fusion.7
  114.7 1.5 multiply_reduce_fusion.7
  120.5 1.5 multiply_reduce_fusion.7
  126.3 1.5 multiply_reduce_fusion.7
  132.0 1.5 multiply_reduce_fusion.7
  134.6 38.2 %all-reduce.1 = (f32[]{:T(128)}, f32[]{:T(128)}) all-reduce(f32[]{:T(128)S(6)} %mul.280, f32[]{:T(128)} %get-tuple-element.681), channel_id=1, replica_groups=mesh['user'=32] {'user'}, use_global_device_ids=true, to_apply=%region_5.6 | all-reduce | flops 2 | bytes 16 | tf_op jit(solution)/shard_map/psum | solution.py:94
  174.1 1.9 bitcast_add_fusion.2
  176.0 46.7 %all-reduce.7.cloned.1.call-done = f32[1024,256]{0,1:T(8,128)} async-done(((f32[1024,256]{0,1:T(8,128)}), f32[1024,256]{0,1:T(8,128)}) %all-reduce.7.cloned.1.call-update) | async-done | bytes 1048592 | tf_op jit(solution)/shard_map/psum | solution.py:100
  222.7 1.7 fusion.37
  224.4 1.5 convolution_bitcast_fusion.1
  225.9 1.8 fusion.49
  228.8 34.6 %while.59 = (s32[]{:T(128)}, f32[]{:T(128)}, f32[384,256]{1,0:T(8,128)S(1)}, f32[384,256]{1,0:T(8,128)S(1)}, bf16[6,128,128]{2,1,0:T(8,128)(2,1)}, /*index=5*/s3...) while((s32[]{:T(128)}, f32[]{:T(128)}, ...), condition=%wide.region_14.15_spmd, body=%wide.region_12.14_spmd.sunk | while | flops 25329688 | bytes 917950 | solution.py:56
  232.0 1.5 multiply_reduce_fusion.8
  237.7 1.5 multiply_reduce_fusion.8
  243.5 1.6 multiply_reduce_fusion.8
  249.3 1.5 multiply_reduce_fusion.8
  255.0 1.5 multiply_reduce_fusion.8
  260.8 1.6 multiply_reduce_fusion.8
  263.4 39.9 %all-reduce = (f32[]{:T(128)}, f32[]{:T(128)}) all-reduce(f32[]{:T(128)S(6)} %mul.293, f32[]{:T(128)} %get-tuple-element.684), channel_id=1, replica_groups=mesh['user'=32] {'user'}, use_global_device_ids=true, to_apply=%region_11.12 | all-reduce | flops 2 | bytes 16 | tf_op jit(solution)/shard_map/psum | solution.py:94
  304.6 53.2 %all-reduce.9.cloned.1.call-done = f32[1024,256]{0,1:T(8,128)} async-done(((f32[1024,256]{0,1:T(8,128)}), f32[1024,256]{0,1:T(8,128)}) %all-reduce.9.cloned.1.call-update) | async-done | bytes 1048592 | tf_op jit(solution)/shard_map/psum | solution.py:100
  357.7 1.9 multiply_add_fusion
  362.1 1.9 bitcast_add_fusion
  364.0 1.8 bitcast_add_fusion.1
  365.7 126.0 %all-reduce.11.cloned.1.call-done = f32[1024,256]{0,1:T(8,128)} async-done(((f32[1024,256]{0,1:T(8,128)}), f32[1024,256]{0,1:T(8,128)}) %all-reduce.11.cloned.1.call-update) | async-done | bytes 1048592 | tf_op jit(solution)/shard_map/psum | solution.py:100
  (99 shorter events, 33.1 us)
Async XLA Ops:
  7.2 80.6 %copy-start = (bf16[384,1024]{1,0:T(8,128)(2,1)S(1)}, bf16[384,1024]{1,0:T(8,128)(2,1)}, u32[]{:S(2)}) copy-start(bf16[384,1024]{1,0:T(8,128)(2,1)} %param.18) | copy-start | bytes 2359300
  7.2 3.9 copy-start.4
  7.2 215.5 %all-reduce.7.cloned.1.call-start = ((), (), s32[]{:S(2)}) async-start(), calls=%async_computation | async-start | bytes 2097152 | tf_op jit(solution)/shard_map/psum | solution.py:100
  10.0 1.2 copy-start.5
  41.9 45.8 %copy-start.2 = (f32[1024,256]{1,0:T(8,128)S(1)}, f32[1024,256]{1,0:T(8,128)}, u32[]{:S(2)}) copy-start(f32[1024,256]{1,0:T(8,128)} %param.21) | copy-start | bytes 3145732
  87.8 11.1 %collective-permute-start = (f32[384,256]{1,0:T(8,128)}, f32[384,256]{1,0:T(8,128)}, u32[]{:S(2)}, u32[]{:S(2)}) collective-permute-start(f32[384,256]{1,0:T(8,128)} %bitcast_add_fusion.4), channel_id=1, source_target_pairs={{0,1},{1,2},{2,3},{3,4},{4,5},{5,6},{6,7},{7,8},{8,9},{9,10},{10,1... | collective-permute-start | bytes 1179656 | tf_op jit(solution)/shard_map/ppermute | solution.py:17
  90.8 267.0 %all-reduce.9.cloned.1.call-start = ((), (), s32[]{:S(2)}) async-start(), calls=%async_computation.1 | async-start | bytes 2097152 | tf_op jit(solution)/shard_map/psum | solution.py:100
  176.0 51.7 %collective-permute-start.1 = (f32[384,256]{1,0:T(8,128)}, f32[384,256]{1,0:T(8,128)}, u32[]{:S(2)}, u32[]{:S(2)}) collective-permute-start(f32[384,256]{1,0:T(8,128)} %bitcast_add_fusion.2), channel_id=1, source_target_pairs={{0,1},{1,2},{2,3},{3,4},{4,5},{5,6},{6,7},{7,8},{8,9},{9,10},{10,1... | collective-permute-start | bytes 1179656 | tf_op jit(solution)/shard_map/ppermute | solution.py:17
  225.9 265.9 %all-reduce.11.cloned.1.call-start = ((), (), s32[]{:S(2)}) async-start(), calls=%async_computation.2 | async-start | bytes 2097152 | tf_op jit(solution)/shard_map/psum | solution.py:100
  304.6 55.1 %copy-start.3 = (f32[384,256]{1,0:T(8,128)S(1)}, f32[384,256]{1,0:T(8,128)}, u32[]{:S(2)}) copy-start(f32[384,256]{1,0:T(8,128)} %get-tuple-element.751) | copy-start | bytes 1179652
  359.6 1.0 copy-start.1
Sparse Core Ops, SparseCore 0:
  90.9 131.7 all-reduce.6
  228.7 128.9 all-reduce.8
  362.9 128.7 all-reduce.10
where the time goes:
time: 502 us; the launch traced here: 500 us
  waiting for transfers between devices  232 us (46%)
  blocking collectives  121 us (24%)
  loops' own time  58.4 us (12%)
  matrix products  38 us (8%)
  between operations  19.8 us (4%)
  local copies, waits for them, and re-layouts  15.3 us (3%)
  other arithmetic  15.2 us (3%)
    psum x3, waiting for transfers between devices, local(): total = lax.psum(grad_w, 'user')  226 us
    psum x3, blocking collectives, local(): total_sse, total_count = lax.psum((sse, count_here), 'user')  121 us
    another operation x3, loops' own time, tile_pass(): return lax.fori_loop(0, slots, one, start)  58.4 us
    dot_general x18, matrix products, one(): lax.dot_general(user_tile, item_tile, (((1,), (1,)), ((), ())), preferred...  23.7 us
    dynamic_slice x18, local copies, waits for them, and re-layouts, one(): code = codes[step]  10.6 us
  transfers between devices with their start and end apart: 5, of which 4 were waited for; matrix products, arithmetic and copies ran while one was open for 9% of the time, Pallas kernels for 0%

commit v1 on v0

v1 whole, which is shorter than its diff:
```python
import functools
import math

import jax
import jax.numpy as jnp
from jax import lax
from jax.experimental import pallas as pl
from jax.experimental.pallas import tpu as pltpu
from jax.sharding import PartitionSpec as P

step_size = 0.01
prior_prec = 8.0
item_prec = 1.0
weight_decay = 1.0
rate_scale = 0.04

NT = (((1,), (1,)), ((), ()))
TN = (((0,), (0,)), ((), ()))
VMEM = pl.BlockSpec(memory_space=pltpu.VMEM)
SMEM = pl.BlockSpec(memory_space=pltpu.SMEM)


def dot(a, b, dims=(((1,), (0,)), ((), ()))):
    return lax.dot_general(a, b, dims, preferred_element_type=jnp.float32)


def tile_kernel(codes, count, tiles, users, items, grad_u, grad_v, stats, pred, err_b):
    slots, tile, _ = tiles.shape
    grid = items.shape[0] // tile
    user_b = users[...].astype(jnp.bfloat16)
    item_b = items[...].astype(jnp.bfloat16)
    pred[...] = dot(user_b, item_b, NT)
    err_b[...] = jnp.zeros_like(err_b)
    live_slots = count[0]
    sse = jnp.zeros((tile, tile), jnp.float32)
    for slot in range(slots):
        code = codes[slot]
        rows = pl.ds(pl.multiple_of(code // grid * tile, tile), tile)
        cols = pl.ds(pl.multiple_of(code % grid * tile, tile), tile)
        live = (slot < live_slots).astype(jnp.float32)
        err = (tiles[slot].astype(jnp.float32) - pred[rows, cols]) * live
        sse = sse + err * err
        err_b[rows, cols] = err.astype(jnp.bfloat16)
    err_all = err_b[...]
    grad_u[...] = dot(err_all, item_b)
    grad_v[...] = dot(err_all, user_b, TN)
    total = jnp.sum(sse)
    counted = live_slots.astype(jnp.float32) * float(tile * tile)
    lane = lax.broadcasted_iota(jnp.int32, stats.shape, 1)
    stats[...] = jnp.where(lane == 0, total, jnp.where(lane == 1, counted, 0.0))


def tile_pass(codes, count, tiles, users, items):
    rows, rank = users.shape
    f32 = jnp.float32
    return pl.pallas_call(
        tile_kernel,
        out_shape=(
            jax.ShapeDtypeStruct((rows, rank), f32),
            jax.ShapeDtypeStruct((rows, rank), f32),
            jax.ShapeDtypeStruct((8, rank), f32),
        ),
        in_specs=[SMEM, SMEM, VMEM, VMEM, VMEM],
        out_specs=(VMEM, VMEM, VMEM),
        scratch_shapes=[
            pltpu.VMEM((rows, rows), f32),
            pltpu.VMEM((rows, rows), jnp.bfloat16),
        ],
        compiler_params=pltpu.CompilerParams(vmem_limit_bytes=16 << 20),
        cost_estimate=pl.CostEstimate(
            flops=6 * rows * rows * rank, bytes_accessed=4 * rows * rank * 4, transcendentals=0
        ),
        name="tile_pass",
    )(codes, count, tiles, users, items)


def prior_kernel(order, feats, weights, users, mean, grad_w):
    weights_b = weights[...].astype(jnp.bfloat16)
    mean_now = dot(feats[...], weights_b)
    mean[...] = mean_now
    offset = (users[...] - mean_now).astype(jnp.bfloat16)
    full = dot(feats[...], offset, TN)
    if order is None:
        grad_w[...] = full
    else:
        block = full.shape[0] // len(order)
        for place, source in enumerate(order):
            grad_w[place * block : (place + 1) * block, :] = full[
                source * block : (source + 1) * block, :
            ]


def prior_pass(feats, weights, users, order=None):
    rows, rank = users.shape
    feat = weights.shape[0]
    return pl.pallas_call(
        functools.partial(prior_kernel, order),
        out_shape=(
            jax.ShapeDtypeStruct((rows, rank), jnp.float32),
            jax.ShapeDtypeStruct((feat, rank), jnp.float32),
        ),
        in_specs=[VMEM, VMEM, VMEM],
        out_specs=(VMEM, VMEM),
        compiler_params=pltpu.CompilerParams(vmem_limit_bytes=16 << 20),
        cost_estimate=pl.CostEstimate(
            flops=4 * rows * feat * rank, bytes_accessed=8 * feat * rank, transcendentals=0
        ),
        name="prior_pass",
    )(feats, weights, users)


def bit_orders(devices):
    bits = devices.bit_length() - 1
    high = list(range(3, bits))
    return [1, 2] + high[::-1], [2, 1] + high


def exchange(array, devices, stage):
    first, second = bit_orders(devices)
    if stage == 0:
        pairs = [(i, i ^ 1) for i in range(devices)]
    else:
        pairs = [(i, i ^ (1 << (second if i & 1 else first)[stage - 1])) for i in range(devices)]
    return lax.ppermute(array, "user", pairs)


def final_order(devices):
    orders = bit_orders(devices)
    bits = devices.bit_length() - 1
    result = []
    for place in range(devices):
        core = place >> (bits - 1)
        index = core
        for stage, bit in enumerate(orders[core]):
            index |= ((place >> (bits - 2 - stage)) & 1) << bit
        result.append(index)
    return result


def local(
    ratings,
    tile_index,
    tile_count,
    side_features,
    user_factors,
    item_factors,
    prior_weights,
    user_noise,
    item_noise,
):
    devices = lax.axis_size("user")
    own = lax.axis_index("user")
    stages = devices.bit_length() - 1
    strata = ratings.shape[1]
    rows_dev = user_factors.shape[0]
    feat, rank = prior_weights.shape
    feat_rows = feat // devices
    rate = rate_scale / (rows_dev * devices)
    noise_scale = math.sqrt(2.0 * step_size)
    core = own & 1
    first, second = bit_orders(devices)

    def my_bit(stage):
        if stage == 0:
            return core
        return jnp.where(core == 0, own >> first[stage - 1], own >> second[stage - 1]) & 1

    def halve(array, stage, rider=None):
        half = array.shape[0] // 2
        bit = my_bit(stage)
        send = lax.dynamic_slice_in_dim(array, (1 - bit) * half, half, 0)
        keep = lax.dynamic_slice_in_dim(array, bit * half, half, 0)
        if rider is None:
            return keep + exchange(send, devices, stage), None
        got = exchange(jnp.concatenate([send, rider], 0), devices, stage)
        return keep + got[:half], rider + got[half:]

    def whole(array, stage, rider):
        got = exchange(jnp.concatenate([array, rider], 0), devices, stage)
        return array + got[: array.shape[0]], rider + got[array.shape[0] :]

    def gather(array, stage):
        got = exchange(array, devices, stage)
        return jnp.where(
            my_bit(stage) == 0,
            jnp.concatenate([array, got], 0),
            jnp.concatenate([got, array], 0),
        )

    users = user_factors
    items = item_factors
    weights = prior_weights
    final_rows = None
    piece = feat // 8
    piece_start = core * (feat // 2) + my_bit(1) * (feat // 4) + my_bit(2) * piece
    for stratum in range(strata):
        last = stratum + 1 == strata
        mean, grad_w = prior_pass(
            side_features, weights, users, final_order(devices) if last else None
        )
        grad_u, grad_v, stats = tile_pass(
            tile_index[0, stratum], tile_count[0, stratum : stratum + 1], ratings[0, stratum], users, items
        )
        part, _ = halve(grad_w, 0)
        for stage in (1, 2):
            part, stats = halve(part, stage, stats)
        for stage in range(3, stages):
            part, stats = (halve if last else whole)(part, stage, stats)
        stats = stats + exchange(stats, devices, 0)
        precision = (1.0 + stats[0, 1] / 2.0) / (1.0 + stats[0, 0] / 2.0)
        new_items = (
            items
            + step_size * (precision * grad_v - item_prec * items)
            + noise_scale * item_noise[stratum].astype(jnp.float32)
        )
        new_users = (
            users
            + step_size * (precision * grad_u - prior_prec * (users - mean))
            + noise_scale * user_noise[stratum].astype(jnp.float32)
        )
        start = own * feat_rows if last else piece_start
        old = lax.dynamic_slice_in_dim(weights, start, part.shape[0], 0)
        part = old + rate * (prior_prec * part - weight_decay * old)
        if last:
            final_rows = part
            items = new_items
        else:
            items = lax.ppermute(
                new_items, "user", [(i, (i + 1) % devices) for i in range(devices)]
            )
            for stage in (2, 1, 0):
                part = gather(part, stage)
            weights = part
        users = new_users
    return (users, items, final_rows)


def solution(mesh):
    return jax.shard_map(
        local,
        mesh=mesh,
        in_specs=(
            P("user", None, None, None, None),
            P("user", None, None),
            P("user", None),
            P("user", None),
            P("user", None),
            P("user", None),
            P(),
            P(None, "user", None),
            P(None, "user", None),
        ),
        out_specs=(P("user", None), P("user", None), P("user", None)),
        check_vma=False,
    )
```

time: 502 us -> 162 us (0.32)
  waiting for transfers between devices: 232 us -> 105 us
  blocking collectives: 121 us -> 0 us
  loops' own time: 58.4 us -> 0 us
  matrix products: 38 us -> 0 us
  starting transfers between devices: 0.13 us -> 21.4 us
  between operations: 19.8 us -> 5.22 us
  Pallas kernels: 0 us -> 9.07 us
  other arithmetic: 15.2 us -> 9.51 us
    psum x3 -> x0, waiting for transfers between devices: 226 us -> none  [local(): total = lax.psum(grad_w, 'user')]
    psum x3 -> x0, blocking collectives: 121 us -> none  [local(): total_sse, total_count = lax.psum((sse, count_here), 'user')]
    ppermute x2 -> x26, waiting for transfers between devices: 6.47 us -> 105 us  [the longest x24 83.2 us: exchange(): return lax.ppermute(array, 'user', pairs)]
    another operation x3 -> x0, loops' own time: 58.4 us -> none  [tile_pass(): return lax.fori_loop(0, slots, one, start)]
    dot_general x60 -> x0, matrix products: 38 us -> none  [the longest x18 23.7 us: one(): lax.dot_general(user_tile, item_tile, (((1,), (1,)), ((), ())), preferred...]
    ppermute x2 -> x26, starting transfers between devices: 0.01 us -> 21.4 us  [the longest x24 20.6 us: exchange(): return lax.ppermute(array, 'user', pairs)]
    dynamic_slice x18 -> x11, local copies, waits for them, and re-layouts: 10.6 us -> 1.09 us  [halve(): send = lax.dynamic_slice_in_dim(array, (1 - bit) * half, half, 0)]
    pallas_call x0 -> x6, Pallas kernels: none -> 9.07 us  [the longest x3 5.72 us: tile_pass(): pl.pallas_call(tile_kernel, out_shape=(jax.ShapeDtypeStruct((rows, rank),...]
  transfers between devices with their start and end apart: 5 -> 26, of which waited for: 4 -> 21; matrix products, arithmetic and copies ran while one was open for 9% -> 3% of each run, Pallas kernels for 0% -> 4%
where the time goes in v1:
time: 162 us; the launch traced here: 161 us
  waiting for transfers between devices  105 us (65%)
  starting transfers between devices  21.4 us (13%)
  local copies, waits for them, and re-layouts  11.3 us (7%)
  other arithmetic  9.51 us (6%)
  Pallas kernels  9.07 us (6%)
  between operations  5.22 us (3%)
    ppermute x24, waiting for transfers between devices, exchange(): return lax.ppermute(array, 'user', pairs)  83.2 us
    ppermute x2, waiting for transfers between devices, local(): lax.ppermute(new_items, 'user', [(i, (i + 1) % devices) for i in range(de...  21.7 us
    ppermute x24, starting transfers between devices, exchange(): return lax.ppermute(array, 'user', pairs)  20.6 us
    unnamed x24, local copies, waits for them, and re-layouts  6.55 us
    pallas_call x3, Pallas kernels, tile_pass(): pl.pallas_call(tile_kernel, out_shape=(jax.ShapeDtypeStruct((rows, rank),...  5.72 us
    pallas_call x3, Pallas kernels, prior_pass(): pl.pallas_call(functools.partial(prior_kernel, order), out_shape=(jax.Sha...  3.36 us
  transfers between devices with their start and end apart: 26, of which 21 were waited for; matrix products, arithmetic and copies ran while one was open for 3% of the time, Pallas kernels for 4%

profile of v1, /device:TPU:0, one launch (start us, length us, event | category | flops | bytes accessed | tf_op | source)
XLA Modules:
  0.0 161.4 jit_solution(17386513465784260820)
XLA Ops:
  2.8 1.2 copy-done.5
  7.7 1.2 slice_bitcast_fusion
  9.1 1.9 %tile_pass.3 = (f32[384,256]{1,0:T(8,128)S(1)}, f32[384,256]{1,0:T(8,128)S(1)}, f32[8,256]{1,0:T(8,128)S(1)}) custom-call(s32[6]{0:T(128)S(1)} %get-tuple-element.43.codes, s32[1]{0:T(128)} %bitcast.1.count, bf16[6,128,128]{2,1,0:T(8,128)(2,1)S(1)} %get-tuple-element.34.tiles, f32[384,256]{1,0:T(8,128)S(1)} %copy-done.3, f32[384,256]{1,0:T(8,128)S(1)} %copy-done.4), custom_call_target="tpu_custom_call" | custom-call | flops 226492416 | bytes 1572864 | tf_op jit(solution)/shard_map/tile_pass/pallas_call | solution.py:56
  12.9 2.5 %collective-permute-start.1 = (f32[264,256]{1,0:T(8,128)S(1)}, f32[264,256]{1,0:T(8,128)S(1)}, u32[]{:S(2)}, u32[]{:S(2)}) collective-permute-start(f32[264,256]{1,0:T(8,128)S(1)} %pad_maximum_fusion), channel_id=1, source_target_pairs={{0,2},{1,5},{2,0},{3,7},{4,6},{5,1},{6,4},{7,3},{8,10},{9,13},{10,... | collective-permute-start | bytes 811016 | tf_op jit(solution)/shard_map/ppermute | solution.py:124
  15.4 4.4 %collective-permute-done.1 = f32[264,256]{1,0:T(8,128)S(1)} collective-permute-done((f32[264,256]{1,0:T(8,128)S(1)}, f32[264,256]{1,0:T(8,128)S(1)}, u32[]{:S(2)}, u32[]{:S(2)}) %collective-permute-start.1) | collective-permute-done | bytes 270368 | tf_op jit(solution)/shard_map/ppermute | solution.py:124
  20.9 2.1 %collective-permute-start.2 = (f32[136,256]{1,0:T(8,128)S(1)}, f32[136,256]{1,0:T(8,128)S(1)}, u32[]{:S(2)}, u32[]{:S(2)}) collective-permute-start(f32[136,256]{1,0:T(8,128)S(1)} %pad_maximum_fusion.3), channel_id=1, source_target_pairs={{0,4},{1,3},{2,6},{3,1},{4,0},{5,7},{6,2},{7,5},{8,12},{9,11},{10,... | collective-permute-start | bytes 417800 | tf_op jit(solution)/shard_map/ppermute | solution.py:124
  23.0 3.0 %collective-permute-done.2 = f32[136,256]{1,0:T(8,128)S(1)} collective-permute-done((f32[136,256]{1,0:T(8,128)S(1)}, f32[136,256]{1,0:T(8,128)S(1)}, u32[]{:S(2)}, u32[]{:S(2)}) %collective-permute-start.2) | collective-permute-done | bytes 139296 | tf_op jit(solution)/shard_map/ppermute | solution.py:124
  26.1 3.2 %collective-permute-start.3 = (f32[136,256]{1,0:T(8,128)S(1)}, f32[136,256]{1,0:T(8,128)S(1)}, u32[]{:S(2)}, u32[]{:S(2)}) collective-permute-start(f32[136,256]{1,0:T(8,128)S(1)} %pad_maximum_fusion.4), channel_id=1, source_target_pairs={{0,16},{1,9},{2,18},{3,11},{4,20},{5,13},{6,22},{7,15},{8,24},{9,1... | collective-permute-start | bytes 417800 | tf_op jit(solution)/shard_map/ppermute | solution.py:124
  29.3 4.5 %collective-permute-done.3 = f32[136,256]{1,0:T(8,128)S(1)} collective-permute-done((f32[136,256]{1,0:T(8,128)S(1)}, f32[136,256]{1,0:T(8,128)S(1)}, u32[]{:S(2)}, u32[]{:S(2)}) %collective-permute-start.3) | collective-permute-done | bytes 139296 | tf_op jit(solution)/shard_map/ppermute | solution.py:124
  33.8 3.6 %collective-permute-start.4 = (f32[136,256]{1,0:T(8,128)S(1)}, f32[136,256]{1,0:T(8,128)S(1)}, u32[]{:S(2)}, u32[]{:S(2)}) collective-permute-start(f32[136,256]{1,0:T(8,128)S(1)} %pad_maximum_fusion.5), channel_id=1, source_target_pairs={{0,8},{1,17},{2,10},{3,19},{4,12},{5,21},{6,14},{7,23},{8,0},{9,25... | collective-permute-start | bytes 417800 | tf_op jit(solution)/shard_map/ppermute | solution.py:124
  37.5 3.0 %collective-permute-done.4 = f32[136,256]{1,0:T(8,128)S(1)} collective-permute-done((f32[136,256]{1,0:T(8,128)S(1)}, f32[136,256]{1,0:T(8,128)S(1)}, u32[]{:S(2)}, u32[]{:S(2)}) %collective-permute-start.4) | collective-permute-done | bytes 139296 | tf_op jit(solution)/shard_map/ppermute | solution.py:124
  41.5 2.2 %collective-permute-start.7 = (f32[128,256]{1,0:T(8,128)S(1)}, f32[128,256]{1,0:T(8,128)S(1)}, u32[]{:S(2)}, u32[]{:S(2)}) collective-permute-start(f32[128,256]{1,0:T(8,128)S(1)} %fusion.7), channel_id=1, source_target_pairs={{0,4},{1,3},{2,6},{3,1},{4,0},{5,7},{6,2},{7,5},{8,12},{9,11},{10,... | collective-permute-start | bytes 393224 | tf_op jit(solution)/shard_map/ppermute | solution.py:124
  43.7 4.3 %collective-permute-done.7 = f32[128,256]{1,0:T(8,128)S(1)} collective-permute-done((f32[128,256]{1,0:T(8,128)S(1)}, f32[128,256]{1,0:T(8,128)S(1)}, u32[]{:S(2)}, u32[]{:S(2)}) %collective-permute-start.7) | collective-permute-done | bytes 131104 | tf_op jit(solution)/shard_map/ppermute | solution.py:124
  48.1 2.1 %collective-permute-start.8 = (f32[256,256]{1,0:T(8,128)S(1)}, f32[256,256]{1,0:T(8,128)S(1)}, u32[]{:S(2)}, u32[]{:S(2)}) collective-permute-start(f32[256,256]{1,0:T(8,128)S(1)} %maximum_select_fusion.4), channel_id=1, source_target_pairs={{0,2},{1,5},{2,0},{3,7},{4,6},{5,1},{6,4},{7,3},{8,10},{9,13},{10,... | collective-permute-start | bytes 786440 | tf_op jit(solution)/shard_map/ppermute | solution.py:124
  50.1 4.4 %collective-permute-done.8 = f32[256,256]{1,0:T(8,128)S(1)} collective-permute-done((f32[256,256]{1,0:T(8,128)S(1)}, f32[256,256]{1,0:T(8,128)S(1)}, u32[]{:S(2)}, u32[]{:S(2)}) %collective-permute-start.8) | collective-permute-done | bytes 262176 | tf_op jit(solution)/shard_map/ppermute | solution.py:124
  62.6 11.3 %collective-permute-done.6.items = f32[384,256]{1,0:T(8,128)S(1)} collective-permute-done((f32[384,256]{1,0:T(8,128)S(1)}, f32[384,256]{1,0:T(8,128)S(1)}, u32[]{:S(2)}, u32[]{:S(2)}) %collective-permute-start.6) | collective-permute-done | bytes 393248 | tf_op jit(solution)/shard_map/ppermute | solution.py:228
  73.9 1.9 %tile_pass.4 = (f32[384,256]{1,0:T(8,128)S(1)}, f32[384,256]{1,0:T(8,128)S(1)}, f32[8,256]{1,0:T(8,128)S(1)}) custom-call(s32[6]{0:T(128)S(1)} %get-tuple-element.44.codes, s32[1]{0:T(128)} %bitcast.6.count, bf16[6,128,128]{2,1,0:T(8,128)(2,1)S(1)} %get-tuple-element.35.tiles, f32[384,256]{1,0:T(8,128)S(1)} %bitcast_add_fusion.5.users, ...), custom_call_target="tpu_custom_call" | custom-call | flops 226492416 | bytes 1572864 | tf_op jit(solution)/shard_map/tile_pass/pallas_call | solution.py:56
  76.0 7.7 %collective-permute-done.11 = f32[264,256]{1,0:T(8,128)S(1)} collective-permute-done((f32[264,256]{1,0:T(8,128)S(1)}, f32[264,256]{1,0:T(8,128)S(1)}, u32[]{:S(2)}, u32[]{:S(2)}) %collective-permute-start.11) | collective-permute-done | bytes 270368 | tf_op jit(solution)/shard_map/ppermute | solution.py:124
  83.9 5.0 %collective-permute-done.12 = f32[136,256]{1,0:T(8,128)S(1)} collective-permute-done((f32[136,256]{1,0:T(8,128)S(1)}, f32[136,256]{1,0:T(8,128)S(1)}, u32[]{:S(2)}, u32[]{:S(2)}) %collective-permute-start.12) | collective-permute-done | bytes 139296 | tf_op jit(solution)/shard_map/ppermute | solution.py:124
  89.1 6.7 %collective-permute-done.13 = f32[136,256]{1,0:T(8,128)S(1)} collective-permute-done((f32[136,256]{1,0:T(8,128)S(1)}, f32[136,256]{1,0:T(8,128)S(1)}, u32[]{:S(2)}, u32[]{:S(2)}) %collective-permute-start.13) | collective-permute-done | bytes 139296 | tf_op jit(solution)/shard_map/ppermute | solution.py:124
  96.1 4.9 %collective-permute-done.14 = f32[136,256]{1,0:T(8,128)S(1)} collective-permute-done((f32[136,256]{1,0:T(8,128)S(1)}, f32[136,256]{1,0:T(8,128)S(1)}, u32[]{:S(2)}, u32[]{:S(2)}) %collective-permute-start.14) | collective-permute-done | bytes 139296 | tf_op jit(solution)/shard_map/ppermute | solution.py:124
  101.3 5.3 %collective-permute-done.17 = f32[128,256]{1,0:T(8,128)S(1)} collective-permute-done((f32[128,256]{1,0:T(8,128)S(1)}, f32[128,256]{1,0:T(8,128)S(1)}, u32[]{:S(2)}, u32[]{:S(2)}) %collective-permute-start.17) | collective-permute-done | bytes 131104 | tf_op jit(solution)/shard_map/ppermute | solution.py:124
  106.7 1.8 %collective-permute-start.18 = (f32[256,256]{1,0:T(8,128)S(1)}, f32[256,256]{1,0:T(8,128)S(1)}, u32[]{:S(2)}, u32[]{:S(2)}) collective-permute-start(f32[256,256]{1,0:T(8,128)S(1)} %maximum_select_fusion.5), channel_id=1, source_target_pairs={{0,2},{1,5},{2,0},{3,7},{4,6},{5,1},{6,4},{7,3},{8,10},{9,13},{10,... | collective-permute-start | bytes 786440 | tf_op jit(solution)/shard_map/ppermute | solution.py:124
  108.5 4.6 %collective-permute-done.18 = f32[256,256]{1,0:T(8,128)S(1)} collective-permute-done((f32[256,256]{1,0:T(8,128)S(1)}, f32[256,256]{1,0:T(8,128)S(1)}, u32[]{:S(2)}, u32[]{:S(2)}) %collective-permute-start.18) | collective-permute-done | bytes 262176 | tf_op jit(solution)/shard_map/ppermute | solution.py:124
  113.7 1.4 collective-permute-done.15
  119.2 10.4 %collective-permute-done.16.items = f32[384,256]{1,0:T(8,128)S(1)} collective-permute-done((f32[384,256]{1,0:T(8,128)S(1)}, f32[384,256]{1,0:T(8,128)S(1)}, u32[]{:S(2)}, u32[]{:S(2)}) %collective-permute-start.16) | collective-permute-done | bytes 393248 | tf_op jit(solution)/shard_map/ppermute | solution.py:228
  129.7 1.9 %tile_pass.5 = (f32[384,256]{1,0:T(8,128)S(1)}, f32[384,256]{1,0:T(8,128)S(1)}, f32[8,256]{1,0:T(8,128)S(1)}) custom-call(s32[6]{0:T(128)S(1)} %get-tuple-element.42.codes, s32[1]{0:T(128)} %bitcast.12.count, bf16[6,128,128]{2,1,0:T(8,128)(2,1)S(1)} %get-tuple-element.33.tiles, f32[384,256]{1,0:T(8,128)S(1)} %bitcast_add_fusion.3.users, ...), custom_call_target="tpu_custom_call" | custom-call | flops 226492416 | bytes 1572864 | tf_op jit(solution)/shard_map/tile_pass/pallas_call | solution.py:56
  131.8 7.9 %collective-permute-done.21 = f32[264,256]{1,0:T(8,128)S(1)} collective-permute-done((f32[264,256]{1,0:T(8,128)S(1)}, f32[264,256]{1,0:T(8,128)S(1)}, u32[]{:S(2)}, u32[]{:S(2)}) %collective-permute-start.21) | collective-permute-done | bytes 270368 | tf_op jit(solution)/shard_map/ppermute | solution.py:124
  139.9 5.1 %collective-permute-done.22 = f32[136,256]{1,0:T(8,128)} collective-permute-done((f32[136,256]{1,0:T(8,128)S(1)}, f32[136,256]{1,0:T(8,128)}, u32[]{:S(2)}, u32[]{:S(2)}) %collective-permute-start.22) | collective-permute-done | bytes 139296 | tf_op jit(solution)/shard_map/ppermute | solution.py:124
  146.8 5.2 %collective-permute-done.23 = f32[72,256]{1,0:T(8,128)S(1)} collective-permute-done((f32[72,256]{1,0:T(8,128)S(1)}, f32[72,256]{1,0:T(8,128)S(1)}, u32[]{:S(2)}, u32[]{:S(2)}) %collective-permute-start.23) | collective-permute-done | bytes 73760 | tf_op jit(solution)/shard_map/ppermute | solution.py:124
  152.2 4.0 %collective-permute-done.24 = f32[40,256]{1,0:T(8,128)S(1)} collective-permute-done((f32[40,256]{1,0:T(8,128)S(1)}, f32[40,256]{1,0:T(8,128)S(1)}, u32[]{:S(2)}, u32[]{:S(2)}) %collective-permute-start.24) | collective-permute-done | bytes 40992 | tf_op jit(solution)/shard_map/ppermute | solution.py:124
  159.3 2.1 %bitcast_add_fusion = (f32[384,256]{1,0:T(8,128)}, f32[384,256]{1,0:T(8,128)}) fusion(f32[384,256]{1,0:T(8,128)S(1)} %collective-permute-done.16.items, f32[384,256]{1,0:T(8,128)S(1)} %get-tuple-element.32, bf16[3,384,256]{2,1,0:T(8,128)(2,1)} %param.17, f32[]{:T(128)} %bitcast.15, bf16[3,384,256]{2,1,0:T(8,128)(2,1)} %param.16, ...), kind=kLoop, calls=%fused_computation.7 | loop fusion | flops 1572864 | bytes 3145732 | tf_op jit(solution)/shard_map/add | solution.py:212
  (120 shorter events, 24.9 us)
Async XLA Ops:
  0.6 1.1 copy-start
  2.8 1.2 copy-start.5
  5.1 1.3 copy-start.10
  6.0 5.0 %collective-permute-start = (f32[512,256]{1,0:T(8,128)}, f32[512,256]{1,0:T(8,128)}, u32[]{:S(2)}, u32[]{:S(2)}) collective-permute-start(f32[512,256]{1,0:T(8,128)} %constant_dynamic-slice_fusion.10), channel_id=1, source_target_pairs={{0,1},{1,0},{2,3},{3,2},{4,5},{5,4},{6,7},{7,6},{8,9},{9,8},{10,11... | collective-permute-start | bytes 1572872 | tf_op jit(solution)/shard_map/ppermute | solution.py:124
  7.7 1.3 copy-start.3
  7.7 1.4 copy-start.4
  12.9 6.9 %collective-permute-start.1 = (f32[264,256]{1,0:T(8,128)S(1)}, f32[264,256]{1,0:T(8,128)S(1)}, u32[]{:S(2)}, u32[]{:S(2)}) collective-permute-start(f32[264,256]{1,0:T(8,128)S(1)} %pad_maximum_fusion), channel_id=1, source_target_pairs={{0,2},{1,5},{2,0},{3,7},{4,6},{5,1},{6,4},{7,3},{8,10},{9,13},{10,... | collective-permute-start | bytes 811016 | tf_op jit(solution)/shard_map/ppermute | solution.py:124
  20.9 5.2 %collective-permute-start.2 = (f32[136,256]{1,0:T(8,128)S(1)}, f32[136,256]{1,0:T(8,128)S(1)}, u32[]{:S(2)}, u32[]{:S(2)}) collective-permute-start(f32[136,256]{1,0:T(8,128)S(1)} %pad_maximum_fusion.3), channel_id=1, source_target_pairs={{0,4},{1,3},{2,6},{3,1},{4,0},{5,7},{6,2},{7,5},{8,12},{9,11},{10,... | collective-permute-start | bytes 417800 | tf_op jit(solution)/shard_map/ppermute | solution.py:124
  26.1 7.7 %collective-permute-start.3 = (f32[136,256]{1,0:T(8,128)S(1)}, f32[136,256]{1,0:T(8,128)S(1)}, u32[]{:S(2)}, u32[]{:S(2)}) collective-permute-start(f32[136,256]{1,0:T(8,128)S(1)} %pad_maximum_fusion.4), channel_id=1, source_target_pairs={{0,16},{1,9},{2,18},{3,11},{4,20},{5,13},{6,22},{7,15},{8,24},{9,1... | collective-permute-start | bytes 417800 | tf_op jit(solution)/shard_map/ppermute | solution.py:124
  33.8 6.7 %collective-permute-start.4 = (f32[136,256]{1,0:T(8,128)S(1)}, f32[136,256]{1,0:T(8,128)S(1)}, u32[]{:S(2)}, u32[]{:S(2)}) collective-permute-start(f32[136,256]{1,0:T(8,128)S(1)} %pad_maximum_fusion.5), channel_id=1, source_target_pairs={{0,8},{1,17},{2,10},{3,19},{4,12},{5,21},{6,14},{7,23},{8,0},{9,25... | collective-permute-start | bytes 417800 | tf_op jit(solution)/shard_map/ppermute | solution.py:124
  41.5 6.5 %collective-permute-start.7 = (f32[128,256]{1,0:T(8,128)S(1)}, f32[128,256]{1,0:T(8,128)S(1)}, u32[]{:S(2)}, u32[]{:S(2)}) collective-permute-start(f32[128,256]{1,0:T(8,128)S(1)} %fusion.7), channel_id=1, source_target_pairs={{0,4},{1,3},{2,6},{3,1},{4,0},{5,7},{6,2},{7,5},{8,12},{9,11},{10,... | collective-permute-start | bytes 393224 | tf_op jit(solution)/shard_map/ppermute | solution.py:124
  48.1 10.6 %copy-start.8 = (bf16[3,384,256]{2,1,0:T(8,128)(2,1)S(1)}, bf16[3,384,256]{2,1,0:T(8,128)(2,1)}, u32[]{:S(2)}) copy-start(bf16[3,384,256]{2,1,0:T(8,128)(2,1)} %param.16) | copy-start | bytes 1769476
  48.1 6.4 %collective-permute-start.8 = (f32[256,256]{1,0:T(8,128)S(1)}, f32[256,256]{1,0:T(8,128)S(1)}, u32[]{:S(2)}, u32[]{:S(2)}) collective-permute-start(f32[256,256]{1,0:T(8,128)S(1)} %maximum_select_fusion.4), channel_id=1, source_target_pairs={{0,2},{1,5},{2,0},{3,7},{4,6},{5,1},{6,4},{7,3},{8,10},{9,13},{10,... | collective-permute-start | bytes 786440 | tf_op jit(solution)/shard_map/ppermute | solution.py:124
  54.6 4.2 %collective-permute-start.9 = (f32[512,256]{1,0:T(8,128)S(1)}, f32[512,256]{1,0:T(8,128)S(1)}, u32[]{:S(2)}, u32[]{:S(2)}) collective-permute-start(f32[512,256]{1,0:T(8,128)S(1)} %maximum_select_fusion.2), channel_id=1, source_target_pairs={{0,1},{1,0},{2,3},{3,2},{4,5},{5,4},{6,7},{7,6},{8,9},{9,8},{10,11... | collective-permute-start | bytes 1572872 | tf_op jit(solution)/shard_map/ppermute | solution.py:124
  55.3 1.3 collective-permute-start.5
  61.1 14.7 %collective-permute-start.10 = (f32[512,256]{1,0:T(8,128)S(1)}, f32[512,256]{1,0:T(8,128)S(1)}, u32[]{:S(2)}, u32[]{:S(2)}) collective-permute-start(f32[512,256]{1,0:T(8,128)S(1)} %constant_dynamic-slice_fusion.7), channel_id=1, source_target_pairs={{0,1},{1,0},{2,3},{3,2},{4,5},{5,4},{6,7},{7,6},{8,9},{9,8},{10,11... | collective-permute-start | bytes 1572872 | tf_op jit(solution)/shard_map/ppermute | solution.py:124
  62.2 11.7 %collective-permute-start.6 = (f32[384,256]{1,0:T(8,128)S(1)}, f32[384,256]{1,0:T(8,128)S(1)}, u32[]{:S(2)}, u32[]{:S(2)}) collective-permute-start(f32[384,256]{1,0:T(8,128)S(1)} %bitcast_add_fusion.4), channel_id=1, source_target_pairs={{0,1},{1,2},{2,3},{3,4},{4,5},{5,6},{6,7},{7,8},{8,9},{9,10},{10,1... | collective-permute-start | bytes 1179656 | tf_op jit(solution)/shard_map/ppermute | solution.py:228
  75.9 7.8 %collective-permute-start.11 = (f32[264,256]{1,0:T(8,128)S(1)}, f32[264,256]{1,0:T(8,128)S(1)}, u32[]{:S(2)}, u32[]{:S(2)}) collective-permute-start(f32[264,256]{1,0:T(8,128)S(1)} %pad_maximum_fusion.1), channel_id=1, source_target_pairs={{0,2},{1,5},{2,0},{3,7},{4,6},{5,1},{6,4},{7,3},{8,10},{9,13},{10,... | collective-permute-start | bytes 811016 | tf_op jit(solution)/shard_map/ppermute | solution.py:124
  83.8 5.1 %collective-permute-start.12 = (f32[136,256]{1,0:T(8,128)S(1)}, f32[136,256]{1,0:T(8,128)S(1)}, u32[]{:S(2)}, u32[]{:S(2)}) collective-permute-start(f32[136,256]{1,0:T(8,128)S(1)} %pad_maximum_fusion.6), channel_id=1, source_target_pairs={{0,4},{1,3},{2,6},{3,1},{4,0},{5,7},{6,2},{7,5},{8,12},{9,11},{10,... | collective-permute-start | bytes 417800 | tf_op jit(solution)/shard_map/ppermute | solution.py:124
  89.0 6.8 %collective-permute-start.13 = (f32[136,256]{1,0:T(8,128)S(1)}, f32[136,256]{1,0:T(8,128)S(1)}, u32[]{:S(2)}, u32[]{:S(2)}) collective-permute-start(f32[136,256]{1,0:T(8,128)S(1)} %pad_maximum_fusion.7), channel_id=1, source_target_pairs={{0,16},{1,9},{2,18},{3,11},{4,20},{5,13},{6,22},{7,15},{8,24},{9,1... | collective-permute-start | bytes 417800 | tf_op jit(solution)/shard_map/ppermute | solution.py:124
  95.9 5.1 %collective-permute-start.14 = (f32[136,256]{1,0:T(8,128)S(1)}, f32[136,256]{1,0:T(8,128)S(1)}, u32[]{:S(2)}, u32[]{:S(2)}) collective-permute-start(f32[136,256]{1,0:T(8,128)S(1)} %pad_maximum_fusion.8), channel_id=1, source_target_pairs={{0,8},{1,17},{2,10},{3,19},{4,12},{5,21},{6,14},{7,23},{8,0},{9,25... | collective-permute-start | bytes 417800 | tf_op jit(solution)/shard_map/ppermute | solution.py:124
  101.1 5.6 %collective-permute-start.17 = (f32[128,256]{1,0:T(8,128)S(1)}, f32[128,256]{1,0:T(8,128)S(1)}, u32[]{:S(2)}, u32[]{:S(2)}) collective-permute-start(f32[128,256]{1,0:T(8,128)S(1)} %fusion.3), channel_id=1, source_target_pairs={{0,4},{1,3},{2,6},{3,1},{4,0},{5,7},{6,2},{7,5},{8,12},{9,11},{10,... | collective-permute-start | bytes 393224 | tf_op jit(solution)/shard_map/ppermute | solution.py:124
  106.7 6.4 %collective-permute-start.18 = (f32[256,256]{1,0:T(8,128)S(1)}, f32[256,256]{1,0:T(8,128)S(1)}, u32[]{:S(2)}, u32[]{:S(2)}) collective-permute-start(f32[256,256]{1,0:T(8,128)S(1)} %maximum_select_fusion.5), channel_id=1, source_target_pairs={{0,2},{1,5},{2,0},{3,7},{4,6},{5,1},{6,4},{7,3},{8,10},{9,13},{10,... | collective-permute-start | bytes 786440 | tf_op jit(solution)/shard_map/ppermute | solution.py:124
  113.2 4.1 %collective-permute-start.19 = (f32[512,256]{1,0:T(8,128)S(1)}, f32[512,256]{1,0:T(8,128)S(1)}, u32[]{:S(2)}, u32[]{:S(2)}) collective-permute-start(f32[512,256]{1,0:T(8,128)S(1)} %maximum_select_fusion.3), channel_id=1, source_target_pairs={{0,1},{1,0},{2,3},{3,2},{4,5},{5,4},{6,7},{7,6},{8,9},{9,8},{10,11... | collective-permute-start | bytes 1572872 | tf_op jit(solution)/shard_map/ppermute | solution.py:124
  113.2 1.9 %collective-permute-start.15 = (f32[8,256]{1,0:T(8,128)S(1)}, f32[8,256]{1,0:T(8,128)S(1)}, u32[]{:S(2)}, u32[]{:S(2)}) collective-permute-start(f32[8,256]{1,0:T(8,128)S(1)} %slice_add_fusion.16), channel_id=1, source_target_pairs={{0,1},{1,0},{2,3},{3,2},{4,5},{5,4},{6,7},{7,6},{8,9},{9,8},{10,11... | collective-permute-start | bytes 24584 | tf_op jit(solution)/shard_map/ppermute | solution.py:124
  118.5 13.1 %collective-permute-start.20 = (f32[512,256]{1,0:T(8,128)S(1)}, f32[512,256]{1,0:T(8,128)S(1)}, u32[]{:S(2)}, u32[]{:S(2)}) collective-permute-start(f32[512,256]{1,0:T(8,128)S(1)} %constant_dynamic-slice_fusion.4), channel_id=1, source_target_pairs={{0,1},{1,0},{2,3},{3,2},{4,5},{5,4},{6,7},{7,6},{8,9},{9,8},{10,11... | collective-permute-start | bytes 1572872 | tf_op jit(solution)/shard_map/ppermute | solution.py:124
  118.8 10.8 %collective-permute-start.16 = (f32[384,256]{1,0:T(8,128)S(1)}, f32[384,256]{1,0:T(8,128)S(1)}, u32[]{:S(2)}, u32[]{:S(2)}) collective-permute-start(f32[384,256]{1,0:T(8,128)S(1)} %bitcast_add_fusion.2), channel_id=1, source_target_pairs={{0,1},{1,2},{2,3},{3,4},{4,5},{5,6},{6,7},{7,8},{8,9},{9,10},{10,1... | collective-permute-start | bytes 1179656 | tf_op jit(solution)/shard_map/ppermute | solution.py:228
  131.7 8.0 %collective-permute-start.21 = (f32[264,256]{1,0:T(8,128)S(1)}, f32[264,256]{1,0:T(8,128)S(1)}, u32[]{:S(2)}, u32[]{:S(2)}) collective-permute-start(f32[264,256]{1,0:T(8,128)S(1)} %pad_maximum_fusion.2), channel_id=1, source_target_pairs={{0,2},{1,5},{2,0},{3,7},{4,6},{5,1},{6,4},{7,3},{8,10},{9,13},{10,... | collective-permute-start | bytes 811016 | tf_op jit(solution)/shard_map/ppermute | solution.py:124
  139.9 5.2 %collective-permute-start.22 = (f32[136,256]{1,0:T(8,128)S(1)}, f32[136,256]{1,0:T(8,128)}, u32[]{:S(2)}, u32[]{:S(2)}) collective-permute-start(f32[136,256]{1,0:T(8,128)S(1)} %pad_maximum_fusion.9), channel_id=1, source_target_pairs={{0,4},{1,3},{2,6},{3,1},{4,0},{5,7},{6,2},{7,5},{8,12},{9,11},{10,... | collective-permute-start | bytes 417800 | tf_op jit(solution)/shard_map/ppermute | solution.py:124
  146.7 5.3 %collective-permute-start.23 = (f32[72,256]{1,0:T(8,128)S(1)}, f32[72,256]{1,0:T(8,128)S(1)}, u32[]{:S(2)}, u32[]{:S(2)}) collective-permute-start(f32[72,256]{1,0:T(8,128)S(1)} %pad_maximum_fusion.10), channel_id=1, source_target_pairs={{0,16},{1,9},{2,18},{3,11},{4,20},{5,13},{6,22},{7,15},{8,24},{9,1... | collective-permute-start | bytes 221192 | tf_op jit(solution)/shard_map/ppermute | solution.py:124
  152.1 4.1 %collective-permute-start.24 = (f32[40,256]{1,0:T(8,128)S(1)}, f32[40,256]{1,0:T(8,128)S(1)}, u32[]{:S(2)}, u32[]{:S(2)}) collective-permute-start(f32[40,256]{1,0:T(8,128)S(1)} %pad_maximum_fusion.11), channel_id=1, source_target_pairs={{0,8},{1,17},{2,10},{3,19},{4,12},{5,21},{6,14},{7,23},{8,0},{9,25... | collective-permute-start | bytes 122888 | tf_op jit(solution)/shard_map/ppermute | solution.py:124
  156.2 1.2 collective-permute-start.25
  (6 other events, 5.7 us)

commit v2 on v1

v2 whole, which is shorter than its diff:
```python
import functools
import math

import jax
import jax.numpy as jnp
from jax import lax
from jax.experimental import pallas as pl
from jax.experimental.pallas import tpu as pltpu
from jax.sharding import PartitionSpec as P

step_size = 0.01
prior_prec = 8.0
item_prec = 1.0
weight_decay = 1.0
rate_scale = 0.04

CHUNKS = 2
NT = (((1,), (1,)), ((), ()))
TN = (((0,), (0,)), ((), ()))
VMEM = pl.BlockSpec(memory_space=pltpu.VMEM)
SMEM = pl.BlockSpec(memory_space=pltpu.SMEM)


def dot(a, b, dims=(((1,), (0,)), ((), ()))):
    return lax.dot_general(a, b, dims, preferred_element_type=jnp.float32)


def tile_kernel(codes, count, tiles, users, items, grad_u, grad_v, stats, pred, err_b):
    slots, tile, _ = tiles.shape
    grid = items.shape[0] // tile
    user_b = users[...].astype(jnp.bfloat16)
    item_b = items[...].astype(jnp.bfloat16)
    pred[...] = dot(user_b, item_b, NT)
    err_b[...] = jnp.zeros_like(err_b)
    live_slots = count[0]
    sse = jnp.zeros((tile, tile), jnp.float32)
    for slot in range(slots):
        code = codes[slot]
        rows = pl.ds(pl.multiple_of(code // grid * tile, tile), tile)
        cols = pl.ds(pl.multiple_of(code % grid * tile, tile), tile)
        live = (slot < live_slots).astype(jnp.float32)
        err = (tiles[slot].astype(jnp.float32) - pred[rows, cols]) * live
        sse = sse + err * err
        err_b[rows, cols] = err.astype(jnp.bfloat16)
    err_all = err_b[...]
    total = jnp.sum(sse)
    counted = live_slots.astype(jnp.float32) * float(tile * tile)
    row = lax.broadcasted_iota(jnp.int32, stats.shape, 0)
    stats[...] = jnp.where(row == 0, total, jnp.where(row == 1, counted, 0.0))
    grad_u[...] = dot(err_all, item_b)
    grad_v[...] = dot(err_all, user_b, TN)


def tile_pass(codes, count, tiles, users, items):
    rows, rank = users.shape
    f32 = jnp.float32
    return pl.pallas_call(
        tile_kernel,
        out_shape=(
            jax.ShapeDtypeStruct((rows, rank), f32),
            jax.ShapeDtypeStruct((rows, rank), f32),
            jax.ShapeDtypeStruct((8, rank // CHUNKS), f32),
        ),
        in_specs=[SMEM, SMEM, VMEM, VMEM, VMEM],
        out_specs=(VMEM, VMEM, VMEM),
        scratch_shapes=[
            pltpu.VMEM((rows, rows), f32),
            pltpu.VMEM((rows, rows), jnp.bfloat16),
        ],
        compiler_params=pltpu.CompilerParams(vmem_limit_bytes=16 << 20),
        cost_estimate=pl.CostEstimate(
            flops=6 * rows * rows * rank, bytes_accessed=4 * rows * rank * 4, transcendentals=0
        ),
        name="tile_pass",
    )(codes, count, tiles, users, items)


def prior_kernel(places, core, feats, weights, users, mean, send, keep, *full):
    half = send.shape[0]
    weights_b = weights[...].astype(jnp.bfloat16)
    mean_now = dot(feats[...], weights_b)
    mean[...] = mean_now
    offset = (users[...] - mean_now).astype(jnp.bfloat16)
    here = core[0]
    if places is None:
        for ref, which in ((send, 1 - here), (keep, here)):
            ref[...] = dot(feats[:, pl.ds(pl.multiple_of(which * half, half), half)], offset, TN)
    else:
        full[0][...] = dot(feats[...], offset, TN)
        block = half // len(places[0])
        for ref, which in ((send, 1 - here), (keep, here)):
            for place, (zero, one) in enumerate(zip(*places, strict=True)):
                source = jnp.where(which == 0, zero, one) * block
                if block % 8 == 0:
                    source = pl.multiple_of(source, block)
                ref[pl.ds(place * block, block), :] = full[0][pl.ds(source, block), :]


def prior_pass(core, feats, weights, users, places=None):
    rows, rank = users.shape
    feat = weights.shape[0]
    f32 = jnp.float32
    return pl.pallas_call(
        functools.partial(prior_kernel, places),
        out_shape=(
            jax.ShapeDtypeStruct((rows, rank), f32),
            jax.ShapeDtypeStruct((feat // 2, rank), f32),
            jax.ShapeDtypeStruct((feat // 2, rank), f32),
        ),
        in_specs=[SMEM, VMEM, VMEM, VMEM],
        out_specs=(VMEM, VMEM, VMEM),
        scratch_shapes=[] if places is None else [pltpu.VMEM((feat, rank), f32)],
        compiler_params=pltpu.CompilerParams(vmem_limit_bytes=16 << 20),
        cost_estimate=pl.CostEstimate(
            flops=4 * rows * feat * rank, bytes_accessed=8 * feat * rank, transcendentals=0
        ),
        name="prior_pass",
    )(core, feats, weights, users)


def bit_order(devices, core, chunk):
    bits = devices.bit_length() - 1
    near = [1, 2] if core == chunk % 2 else [2, 1]
    far = list(range(3, bits))
    return near + (far if chunk % 2 == 0 else far[::-1])


def exchange(array, devices, chunk, stage):
    if stage == 0:
        pairs = [(i, i ^ 1) for i in range(devices)]
    else:
        orders = [bit_order(devices, core, chunk) for core in (0, 1)]
        pairs = [(i, i ^ (1 << orders[i & 1][stage - 1])) for i in range(devices)]
    return lax.ppermute(array, "user", pairs)


def final_places(devices, chunk):
    bits = devices.bit_length() - 1
    result = []
    for core in (0, 1):
        order = bit_order(devices, core, chunk)
        result.append(
            [
                core
                | sum(((place >> (bits - 2 - n)) & 1) << bit for n, bit in enumerate(order))
                for place in range(devices // 2)
            ]
        )
    return result


def local(
    ratings,
    tile_index,
    tile_count,
    side_features,
    user_factors,
    item_factors,
    prior_weights,
    user_noise,
    item_noise,
):
    devices = lax.axis_size("user")
    own = lax.axis_index("user")
    stages = devices.bit_length() - 1
    strata = ratings.shape[1]
    rows_dev = user_factors.shape[0]
    feat, rank = prior_weights.shape
    feat_rows = feat // devices
    width = rank // CHUNKS
    rate = rate_scale / (rows_dev * devices)
    noise_scale = math.sqrt(2.0 * step_size)
    core = own & 1
    core_ref = core.reshape(1)

    def my_bit(chunk, stage):
        if stage == 0:
            return core
        zero, one = (bit_order(devices, c, chunk)[stage - 1] for c in (0, 1))
        return jnp.where(core == 0, own >> zero, own >> one) & 1

    def add(send, keep, chunk, stage, rider):
        if rider is None:
            return keep + exchange(send, devices, chunk, stage), None
        got = exchange(jnp.concatenate([send, rider], 0), devices, chunk, stage)
        return keep + got[: keep.shape[0]], rider + got[keep.shape[0] :]

    def halve(array, chunk, stage, rider):
        half = array.shape[0] // 2
        bit = my_bit(chunk, stage)
        send = lax.dynamic_slice_in_dim(array, (1 - bit) * half, half, 0)
        keep = lax.dynamic_slice_in_dim(array, bit * half, half, 0)
        return add(send, keep, chunk, stage, rider)

    def gather(array, chunk, stage):
        got = exchange(array, devices, chunk, stage)
        return jnp.where(
            my_bit(chunk, stage) == 0,
            jnp.concatenate([array, got], 0),
            jnp.concatenate([got, array], 0),
        )

    users = user_factors
    items = item_factors
    weights = [prior_weights[:, c * width : (c + 1) * width] for c in range(CHUNKS)]
    both = range(CHUNKS)
    for stratum in range(strata):
        last = stratum + 1 == strata
        means, parts = [], []
        for c in both:
            mean, send, keep = prior_pass(
                core_ref,
                side_features,
                weights[c],
                users[:, c * width : (c + 1) * width],
                final_places(devices, c) if last else None,
            )
            means.append(mean)
            parts.append(add(send, keep, c, 0, None)[0])
        grad_u, grad_v, stats = tile_pass(
            tile_index[0, stratum], tile_count[0, stratum : stratum + 1], ratings[0, stratum], users, items
        )
        stats = stats + exchange(stats, devices, 0, 0)
        for stage in range(1, stages):
            for c in both:
                rider = stats if c == CHUNKS - 1 else None
                if stage < 3 or last:
                    parts[c], rider = halve(parts[c], c, stage, rider)
                else:
                    parts[c], rider = add(parts[c], parts[c], c, stage, rider)
                if c == CHUNKS - 1:
                    stats = rider
        precision = (1.0 + stats[1:2, :] / 2.0) / (1.0 + stats[0:1, :] / 2.0)
        precision = jnp.concatenate([precision] * CHUNKS, 1)
        new_items = (
            items
            + step_size * (precision * grad_v - item_prec * items)
            + noise_scale * item_noise[stratum].astype(jnp.float32)
        )
        mean = jnp.concatenate(means, 1)
        new_users = (
            users
            + step_size * (precision * grad_u - prior_prec * (users - mean))
            + noise_scale * user_noise[stratum].astype(jnp.float32)
        )
        for c in both:
            if last:
                start = own * feat_rows
            else:
                start = core * (feat // 2) + my_bit(c, 1) * (feat // 4) + my_bit(c, 2) * (feat // 8)
            old = lax.dynamic_slice_in_dim(weights[c], start, parts[c].shape[0], 0)
            parts[c] = old + rate * (prior_prec * parts[c] - weight_decay * old)
        if last:
            items = new_items
        else:
            items = lax.ppermute(
                new_items, "user", [(i, (i + 1) % devices) for i in range(devices)]
            )
            for stage in (2, 1, 0):
                for c in both:
                    parts[c] = gather(parts[c], c, stage)
        weights = list(parts)
        users = new_users
    return (users, items, jnp.concatenate(weights, 1))


def solution(mesh):
    return jax.shard_map(
        local,
        mesh=mesh,
        in_specs=(
            P("user", None, None, None, None),
            P("user", None, None),
            P("user", None),
            P("user", None),
            P("user", None),
            P("user", None),
            P(),
            P(None, "user", None),
            P(None, "user", None),
        ),
        out_specs=(P("user", None), P("user", None), P("user", None)),
        check_vma=False,
    )
```

time: 162 us -> 143 us (0.88)
  waiting for transfers between devices: 105 us -> 68.2 us
  starting transfers between devices: 21.4 us -> 38.9 us
  local copies, waits for them, and re-layouts: 11.3 us -> 5.7 us
  Pallas kernels: 9.07 us -> 14.6 us
  other arithmetic: 9.51 us -> 13.5 us
  between operations: 5.22 us -> 1.39 us
    ppermute x24 -> x45, waiting for transfers between devices: 83.2 us -> 55.9 us  [exchange(): return lax.ppermute(array, 'user', pairs)]
    ppermute x24 -> x45, starting transfers between devices: 20.6 us -> 38.1 us  [exchange(): return lax.ppermute(array, 'user', pairs)]
    ppermute x2, waiting for transfers between devices: 21.7 us -> 12.2 us  [local(): lax.ppermute(new_items, 'user', [(i, (i + 1) % devices) for i in range(de...]
    pallas_call x3 -> x6, Pallas kernels: 3.36 us -> 8.82 us  [prior_pass(): pl.pallas_call(functools.partial(prior_kernel, places), out_shape=(jax.Sh...]
    unnamed x24 -> x36, local copies, waits for them, and re-layouts: 6.55 us -> 2.34 us
    add x3, other arithmetic: 2.34 us -> 4.38 us  [local(): items + step_size * (precision * grad_v - item_prec * items)]
    add x32 -> x45, other arithmetic: 6.71 us -> 7.5 us  [the longest x15 5.65 us: add(): return (keep + exchange(send, devices, chunk, stage), None)]
  transfers between devices with their start and end apart: 26 -> 47, of which waited for: 21 -> 28; matrix products, arithmetic and copies ran while one was open for 3% -> 8% of each run, Pallas kernels for 4% -> 9%
where the time goes in v2:
time: 143 us; the launch traced here: 142 us
  waiting for transfers between devices  68.2 us (48%)
  starting transfers between devices  38.9 us (27%)
  Pallas kernels  14.6 us (10%)
  other arithmetic  13.5 us (9%)
  local copies, waits for them, and re-layouts  5.7 us (4%)
    ppermute x45, waiting for transfers between devices, exchange(): return lax.ppermute(array, 'user', pairs)  55.9 us
    ppermute x45, starting transfers between devices, exchange(): return lax.ppermute(array, 'user', pairs)  38.1 us
    ppermute x2, waiting for transfers between devices, local(): lax.ppermute(new_items, 'user', [(i, (i + 1) % devices) for i in range(de...  12.2 us
    pallas_call x6, Pallas kernels, prior_pass(): pl.pallas_call(functools.partial(prior_kernel, places), out_shape=(jax.Sh...  8.82 us
    pallas_call x3, Pallas kernels, tile_pass(): pl.pallas_call(tile_kernel, out_shape=(jax.ShapeDtypeStruct((rows, rank),...  5.75 us
    add x15, other arithmetic, add(): return (keep + exchange(send, devices, chunk, stage), None)  5.65 us
    add x3, other arithmetic, local(): items + step_size * (precision * grad_v - item_prec * items)  4.38 us
  transfers between devices with their start and end apart: 47, of which 28 were waited for; matrix products, arithmetic and copies ran while one was open for 8% of the time, Pallas kernels for 9%

profile of v2, /device:TPU:0, one launch (start us, length us, event | category | flops | bytes accessed | tf_op | source)
XLA Modules:
  0.0 142.3 jit_solution(13026511244508073235)
XLA Ops:
  9.0 1.9 %tile_pass.3 = (f32[384,256]{1,0:T(8,128)S(1)}, f32[384,256]{1,0:T(8,128)S(1)}, f32[8,128]{1,0:T(8,128)S(1)}) custom-call(s32[6]{0:T(128)S(1)} %get-tuple-element.69.codes, s32[1]{0:T(128)} %bitcast.1.count, bf16[6,128,128]{2,1,0:T(8,128)(2,1)S(1)} %get-tuple-element.60.tiles, f32[384,256]{1,0:T(8,128)S(1)} %copy-done.1, f32[384,256]{1,0:T(8,128)S(1)} %copy-done.2), custom_call_target="tpu_custom_call" | custom-call | flops 226492416 | bytes 1572864 | tf_op jit(solution)/shard_map/tile_pass/pallas_call | solution.py:57
  14.0 2.9 %collective-permute-start.17 = (f32[256,128]{1,0:T(8,128)S(1)}, f32[256,128]{1,0:T(8,128)S(1)}, u32[]{:S(2)}, u32[]{:S(2)}) collective-permute-start(f32[256,128]{1,0:T(8,128)S(1)} %constant_dynamic-slice_fusion.11), channel_id=1, source_target_pairs={{0,2},{1,5},{2,0},{3,7},{4,6},{5,1},{6,4},{7,3},{8,10},{9,13},{10,... | collective-permute-start | bytes 393224 | tf_op jit(solution)/shard_map/ppermute | solution.py:134
  17.8 1.6 %collective-permute-start.2 = (f32[264,128]{1,0:T(8,128)S(1)}, f32[264,128]{1,0:T(8,128)S(1)}, u32[]{:S(2)}, u32[]{:S(2)}) collective-permute-start(f32[264,128]{1,0:T(8,128)S(1)} %pad_maximum_fusion), channel_id=1, source_target_pairs={{0,4},{1,3},{2,6},{3,1},{4,0},{5,7},{6,2},{7,5},{8,12},{9,11},{10,... | collective-permute-start | bytes 405512 | tf_op jit(solution)/shard_map/ppermute | solution.py:134
  19.8 3.1 %collective-permute-done.2 = f32[264,128]{1,0:T(8,128)S(1)} collective-permute-done((f32[264,128]{1,0:T(8,128)S(1)}, f32[264,128]{1,0:T(8,128)S(1)}, u32[]{:S(2)}, u32[]{:S(2)}) %collective-permute-start.2) | collective-permute-done | bytes 135200 | tf_op jit(solution)/shard_map/ppermute | solution.py:134
  25.4 1.9 %collective-permute-done.3 = f32[136,128]{1,0:T(8,128)S(1)} collective-permute-done((f32[136,128]{1,0:T(8,128)S(1)}, f32[136,128]{1,0:T(8,128)S(1)}, u32[]{:S(2)}, u32[]{:S(2)}) %collective-permute-start.3) | collective-permute-done | bytes 69664 | tf_op jit(solution)/shard_map/ppermute | solution.py:134
  28.0 2.6 %collective-permute-start.4 = (f32[136,128]{1,0:T(8,128)}, f32[136,128]{1,0:T(8,128)}, u32[]{:S(2)}, u32[]{:S(2)}) collective-permute-start(f32[136,128]{1,0:T(8,128)} %pad_maximum_fusion.4), channel_id=1, source_target_pairs={{0,16},{1,17},{2,18},{3,19},{4,20},{5,21},{6,22},{7,23},{8,24},{9,... | collective-permute-start | bytes 208904 | tf_op jit(solution)/shard_map/ppermute | solution.py:134
  31.3 1.6 %collective-permute-start.19 = (f32[128,128]{1,0:T(8,128)}, f32[128,128]{1,0:T(8,128)}, u32[]{:S(2)}, u32[]{:S(2)}) collective-permute-start(f32[128,128]{1,0:T(8,128)} %dynamic-slice_add_fusion.5), channel_id=1, source_target_pairs={{0,8},{1,9},{2,10},{3,11},{4,12},{5,13},{6,14},{7,15},{8,0},{9,1},... | collective-permute-start | bytes 196616 | tf_op jit(solution)/shard_map/ppermute | solution.py:134
  32.8 3.0 %collective-permute-done.19 = f32[128,128]{1,0:T(8,128)} collective-permute-done((f32[128,128]{1,0:T(8,128)}, f32[128,128]{1,0:T(8,128)}, u32[]{:S(2)}, u32[]{:S(2)}) %collective-permute-start.19) | collective-permute-done | bytes 65568 | tf_op jit(solution)/shard_map/ppermute | solution.py:134
  38.7 2.4 %collective-permute-start.5 = (f32[136,128]{1,0:T(8,128)S(1)}, f32[136,128]{1,0:T(8,128)S(1)}, u32[]{:S(2)}, u32[]{:S(2)}) collective-permute-start(f32[136,128]{1,0:T(8,128)S(1)} %pad_maximum_fusion.5), channel_id=1, source_target_pairs={{0,8},{1,9},{2,10},{3,11},{4,12},{5,13},{6,14},{7,15},{8,0},{9,1},... | collective-permute-start | bytes 208904 | tf_op jit(solution)/shard_map/ppermute | solution.py:134
  42.0 1.6 %collective-permute-start.21 = (f32[128,128]{1,0:T(8,128)S(1)}, f32[128,128]{1,0:T(8,128)S(1)}, u32[]{:S(2)}, u32[]{:S(2)}) collective-permute-start(f32[128,128]{1,0:T(8,128)S(1)} %multiply_add_fusion.1), channel_id=1, source_target_pairs={{0,4},{1,3},{2,6},{3,1},{4,0},{5,7},{6,2},{7,5},{8,12},{9,11},{10,... | collective-permute-start | bytes 196616 | tf_op jit(solution)/shard_map/ppermute | solution.py:134
  57.2 6.8 %collective-permute-done.6.items = f32[384,256]{1,0:T(8,128)S(1)} collective-permute-done((f32[384,256]{1,0:T(8,128)S(1)}, f32[384,256]{1,0:T(8,128)S(1)}, u32[]{:S(2)}, u32[]{:S(2)}) %collective-permute-start.6) | collective-permute-done | bytes 393248 | tf_op jit(solution)/shard_map/ppermute | solution.py:256
  64.0 1.9 %tile_pass.4 = (f32[384,256]{1,0:T(8,128)S(1)}, f32[384,256]{1,0:T(8,128)S(1)}, f32[8,128]{1,0:T(8,128)S(1)}) custom-call(s32[6]{0:T(128)S(1)} %get-tuple-element.70.codes, s32[1]{0:T(128)} %bitcast.7.count, bf16[6,128,128]{2,1,0:T(8,128)(2,1)S(1)} %get-tuple-element.61.tiles, f32[384,256]{1,0:T(8,128)S(1)} %get-tuple-element.76.users, ...), custom_call_target="tpu_custom_call" | custom-call | flops 226492416 | bytes 1572864 | tf_op jit(solution)/shard_map/tile_pass/pallas_call | solution.py:57
  67.5 5.6 %collective-permute-done.35 = f32[256,128]{1,0:T(8,128)S(1)} collective-permute-done((f32[256,128]{1,0:T(8,128)S(1)}, f32[256,128]{1,0:T(8,128)S(1)}, u32[]{:S(2)}, u32[]{:S(2)}) %collective-permute-start.35) | collective-permute-done | bytes 131104 | tf_op jit(solution)/shard_map/ppermute | solution.py:134
  74.6 2.9 %collective-permute-done.13 = f32[136,128]{1,0:T(8,128)S(1)} collective-permute-done((f32[136,128]{1,0:T(8,128)S(1)}, f32[136,128]{1,0:T(8,128)S(1)}, u32[]{:S(2)}, u32[]{:S(2)}) %collective-permute-start.13) | collective-permute-done | bytes 69664 | tf_op jit(solution)/shard_map/ppermute | solution.py:134
  80.3 4.5 %collective-permute-done.37 = f32[128,128]{1,0:T(8,128)S(1)} collective-permute-done((f32[128,128]{1,0:T(8,128)S(1)}, f32[128,128]{1,0:T(8,128)S(1)}, u32[]{:S(2)}, u32[]{:S(2)}) %collective-permute-start.37) | collective-permute-done | bytes 65568 | tf_op jit(solution)/shard_map/ppermute | solution.py:134
  85.1 1.6 %collective-permute-start.15 = (f32[136,128]{1,0:T(8,128)S(1)}, f32[136,128]{1,0:T(8,128)S(1)}, u32[]{:S(2)}, u32[]{:S(2)}) collective-permute-start(f32[136,128]{1,0:T(8,128)S(1)} %pad_maximum_fusion.8), channel_id=1, source_target_pairs={{0,8},{1,9},{2,10},{3,11},{4,12},{5,13},{6,14},{7,15},{8,0},{9,1},... | collective-permute-start | bytes 208904 | tf_op jit(solution)/shard_map/ppermute | solution.py:134
  86.7 3.5 %collective-permute-done.38 = f32[128,128]{1,0:T(8,128)S(1)} collective-permute-done((f32[128,128]{1,0:T(8,128)S(1)}, f32[128,128]{1,0:T(8,128)S(1)}, u32[]{:S(2)}, u32[]{:S(2)}) %collective-permute-start.38) | collective-permute-done | bytes 65568 | tf_op jit(solution)/shard_map/ppermute | solution.py:134
  91.5 3.0 %collective-permute-done.39 = f32[128,128]{1,0:T(8,128)S(1)} collective-permute-done((f32[128,128]{1,0:T(8,128)S(1)}, f32[128,128]{1,0:T(8,128)S(1)}, u32[]{:S(2)}, u32[]{:S(2)}) %collective-permute-start.39) | collective-permute-done | bytes 65568 | tf_op jit(solution)/shard_map/ppermute | solution.py:134
  94.6 2.1 %collective-permute-start.27 = (f32[256,128]{1,0:T(8,128)S(1)}, f32[256,128]{1,0:T(8,128)S(1)}, u32[]{:S(2)}, u32[]{:S(2)}) collective-permute-start(f32[256,128]{1,0:T(8,128)S(1)} %maximum_select_fusion.10), channel_id=1, source_target_pairs={{0,4},{1,3},{2,6},{3,1},{4,0},{5,7},{6,2},{7,5},{8,12},{9,11},{10,... | collective-permute-start | bytes 393224 | tf_op jit(solution)/shard_map/ppermute | solution.py:134
  97.8 1.7 %collective-permute-done.40 = f32[256,128]{1,0:T(8,128)S(1)} collective-permute-done((f32[256,128]{1,0:T(8,128)S(1)}, f32[256,128]{1,0:T(8,128)S(1)}, u32[]{:S(2)}, u32[]{:S(2)}) %collective-permute-start.40) | collective-permute-done | bytes 131104 | tf_op jit(solution)/shard_map/ppermute | solution.py:134
  101.2 1.8 %prior_pass.11 = (f32[384,128]{1,0:T(8,128)S(1)}, f32[512,128]{1,0:T(8,128)}, f32[512,128]{1,0:T(8,128)S(1)}) custom-call(s32[1]{0:T(128)} %bitcast.3.core, bf16[384,1024]{1,0:T(8,128)(2,1)S(1)} %copy-done, f32[1024,128]{1,0:T(8,128)S(1)} %maximum_select_fusion.3.weights, f32[384,128]{1,0:T(8,128)S(1)} %get-tuple-element.62.users), custom_call_target="tpu_custom_call" | custom-call | flops 201326592 | bytes 1048576 | tf_op jit(solution)/shard_map/prior_pass/pallas_call | solution.py:103
  104.0 1.8 %prior_pass.10 = (f32[384,128]{1,0:T(8,128)S(1)}, f32[512,128]{1,0:T(8,128)}, f32[512,128]{1,0:T(8,128)S(1)}) custom-call(s32[1]{0:T(128)} %bitcast.3.core, bf16[384,1024]{1,0:T(8,128)(2,1)S(1)} %copy-done, f32[1024,128]{1,0:T(8,128)S(1)} %maximum_select_fusion.2.weights, f32[384,128]{1,0:T(8,128)S(1)} %get-tuple-element.63.users), custom_call_target="tpu_custom_call" | custom-call | flops 201326592 | bytes 1048576 | tf_op jit(solution)/shard_map/prior_pass/pallas_call | solution.py:103
  105.8 5.4 %collective-permute-done.24.items = f32[384,256]{1,0:T(8,128)S(1)} collective-permute-done((f32[384,256]{1,0:T(8,128)S(1)}, f32[384,256]{1,0:T(8,128)S(1)}, u32[]{:S(2)}, u32[]{:S(2)}) %collective-permute-start.24) | collective-permute-done | bytes 393248 | tf_op jit(solution)/shard_map/ppermute | solution.py:256
  111.3 1.9 %tile_pass.5 = (f32[384,256]{1,0:T(8,128)S(1)}, f32[384,256]{1,0:T(8,128)S(1)}, f32[8,128]{1,0:T(8,128)S(1)}) custom-call(s32[6]{0:T(128)S(1)} %get-tuple-element.68.codes, s32[1]{0:T(128)} %bitcast.13.count, bf16[6,128,128]{2,1,0:T(8,128)(2,1)S(1)} %get-tuple-element.59.tiles, f32[384,256]{1,0:T(8,128)S(1)} %get-tuple-element.74.users, ...), custom_call_target="tpu_custom_call" | custom-call | flops 226492416 | bytes 1572864 | tf_op jit(solution)/shard_map/tile_pass/pallas_call | solution.py:57
  116.7 4.9 %collective-permute-done.43 = f32[256,128]{1,0:T(8,128)S(1)} collective-permute-done((f32[256,128]{1,0:T(8,128)S(1)}, f32[256,128]{1,0:T(8,128)S(1)}, u32[]{:S(2)}, u32[]{:S(2)}) %collective-permute-start.43) | collective-permute-done | bytes 131104 | tf_op jit(solution)/shard_map/ppermute | solution.py:134
  121.8 4.4 %collective-permute-done.44 = f32[128,128]{1,0:T(8,128)S(1)} collective-permute-done((f32[128,128]{1,0:T(8,128)S(1)}, f32[128,128]{1,0:T(8,128)S(1)}, u32[]{:S(2)}, u32[]{:S(2)}) %collective-permute-start.44) | collective-permute-done | bytes 65568 | tf_op jit(solution)/shard_map/ppermute | solution.py:134
  126.4 3.8 %collective-permute-done.45 = f32[64,128]{1,0:T(8,128)S(1)} collective-permute-done((f32[64,128]{1,0:T(8,128)S(1)}, f32[64,128]{1,0:T(8,128)S(1)}, u32[]{:S(2)}, u32[]{:S(2)}) %collective-permute-start.45) | collective-permute-done | bytes 32800 | tf_op jit(solution)/shard_map/ppermute | solution.py:134
  130.7 1.6 %collective-permute-start.32 = (f32[72,128]{1,0:T(8,128)S(1)}, f32[72,128]{1,0:T(8,128)S(1)}, u32[]{:S(2)}, u32[]{:S(2)}) collective-permute-start(f32[72,128]{1,0:T(8,128)S(1)} %pad_maximum_fusion.10), channel_id=1, source_target_pairs={{0,16},{1,17},{2,18},{3,19},{4,20},{5,21},{6,22},{7,23},{8,24},{9,... | collective-permute-start | bytes 110600 | tf_op jit(solution)/shard_map/ppermute | solution.py:134
  133.7 1.9 %collective-permute-done.32 = f32[72,128]{1,0:T(8,128)S(1)} collective-permute-done((f32[72,128]{1,0:T(8,128)S(1)}, f32[72,128]{1,0:T(8,128)S(1)}, u32[]{:S(2)}, u32[]{:S(2)}) %collective-permute-start.32) | collective-permute-done | bytes 36896 | tf_op jit(solution)/shard_map/ppermute | solution.py:134
  135.7 2.0 %collective-permute-start.33 = (f32[40,128]{1,0:T(8,128)S(1)}, f32[40,128]{1,0:T(8,128)S(1)}, u32[]{:S(2)}, u32[]{:S(2)}) collective-permute-start(f32[40,128]{1,0:T(8,128)S(1)} %pad_maximum_fusion.12), channel_id=1, source_target_pairs={{0,8},{1,9},{2,10},{3,11},{4,12},{5,13},{6,14},{7,15},{8,0},{9,1},... | collective-permute-start | bytes 61448 | tf_op jit(solution)/shard_map/ppermute | solution.py:134
  137.7 1.8 %collective-permute-done.33 = f32[40,128]{1,0:T(8,128)S(1)} collective-permute-done((f32[40,128]{1,0:T(8,128)S(1)}, f32[40,128]{1,0:T(8,128)S(1)}, u32[]{:S(2)}, u32[]{:S(2)}) %collective-permute-start.33) | collective-permute-done | bytes 20512 | tf_op jit(solution)/shard_map/ppermute | solution.py:134
  140.2 2.1 %bitcast_add_fusion = (f32[384,256]{1,0:T(8,128)}, f32[384,256]{1,0:T(8,128)}) fusion(f32[384,256]{1,0:T(8,128)S(1)} %collective-permute-done.24.items, f32[384,256]{1,0:T(8,128)S(1)} %get-tuple-element.54, bf16[3,384,256]{2,1,0:T(8,128)(2,1)} %param.17, f32[256]{0:T(256)S(1)} %bitcast.33, bf16[3,384,256]{2,1,0:T(8,128)(2,1)} %param.16, ...), kind=kLoop, calls=%fused_computation.22 | loop fusion | flops 1671168 | bytes 3146752 | tf_op jit(solution)/shard_map/add | solution.py:236
  (209 shorter events, 51.2 us)
Async XLA Ops:
  4.7 8.2 %collective-permute-start.16 = (f32[512,128]{1,0:T(8,128)}, f32[512,128]{1,0:T(8,128)}, u32[]{:S(2)}, u32[]{:S(2)}) collective-permute-start(f32[512,128]{1,0:T(8,128)} %get-tuple-element.42), channel_id=1, source_target_pairs={{0,1},{1,0},{2,3},{3,2},{4,5},{5,4},{6,7},{7,6},{8,9},{9,8},{10,11... | collective-permute-start | bytes 786440 | tf_op jit(solution)/shard_map/ppermute | solution.py:134
  7.4 9.4 %collective-permute-start.1 = (f32[512,128]{1,0:T(8,128)}, f32[512,128]{1,0:T(8,128)}, u32[]{:S(2)}, u32[]{:S(2)}) collective-permute-start(f32[512,128]{1,0:T(8,128)} %get-tuple-element.32), channel_id=1, source_target_pairs={{0,1},{1,0},{2,3},{3,2},{4,5},{5,4},{6,7},{7,6},{8,9},{9,8},{10,11... | collective-permute-start | bytes 786440 | tf_op jit(solution)/shard_map/ppermute | solution.py:134
  14.0 5.8 %collective-permute-start.17 = (f32[256,128]{1,0:T(8,128)S(1)}, f32[256,128]{1,0:T(8,128)S(1)}, u32[]{:S(2)}, u32[]{:S(2)}) collective-permute-start(f32[256,128]{1,0:T(8,128)S(1)} %constant_dynamic-slice_fusion.11), channel_id=1, source_target_pairs={{0,2},{1,5},{2,0},{3,7},{4,6},{5,1},{6,4},{7,3},{8,10},{9,13},{10,... | collective-permute-start | bytes 393224 | tf_op jit(solution)/shard_map/ppermute | solution.py:134
  17.8 5.1 %collective-permute-start.2 = (f32[264,128]{1,0:T(8,128)S(1)}, f32[264,128]{1,0:T(8,128)S(1)}, u32[]{:S(2)}, u32[]{:S(2)}) collective-permute-start(f32[264,128]{1,0:T(8,128)S(1)} %pad_maximum_fusion), channel_id=1, source_target_pairs={{0,4},{1,3},{2,6},{3,1},{4,0},{5,7},{6,2},{7,5},{8,12},{9,11},{10,... | collective-permute-start | bytes 405512 | tf_op jit(solution)/shard_map/ppermute | solution.py:134
  23.0 4.4 %collective-permute-start.3 = (f32[136,128]{1,0:T(8,128)S(1)}, f32[136,128]{1,0:T(8,128)S(1)}, u32[]{:S(2)}, u32[]{:S(2)}) collective-permute-start(f32[136,128]{1,0:T(8,128)S(1)} %pad_maximum_fusion.3), channel_id=1, source_target_pairs={{0,2},{1,5},{2,0},{3,7},{4,6},{5,1},{6,4},{7,3},{8,10},{9,13},{10,... | collective-permute-start | bytes 208904 | tf_op jit(solution)/shard_map/ppermute | solution.py:134
  23.9 6.7 %collective-permute-start.18 = (f32[128,128]{1,0:T(8,128)S(1)}, f32[128,128]{1,0:T(8,128)S(1)}, u32[]{:S(2)}, u32[]{:S(2)}) collective-permute-start(f32[128,128]{1,0:T(8,128)S(1)} %constant_dynamic-slice_fusion.10), channel_id=1, source_target_pairs={{0,4},{1,3},{2,6},{3,1},{4,0},{5,7},{6,2},{7,5},{8,12},{9,11},{10,... | collective-permute-start | bytes 196616 | tf_op jit(solution)/shard_map/ppermute | solution.py:134
  28.0 9.1 %collective-permute-start.4 = (f32[136,128]{1,0:T(8,128)}, f32[136,128]{1,0:T(8,128)}, u32[]{:S(2)}, u32[]{:S(2)}) collective-permute-start(f32[136,128]{1,0:T(8,128)} %pad_maximum_fusion.4), channel_id=1, source_target_pairs={{0,16},{1,17},{2,18},{3,19},{4,20},{5,21},{6,22},{7,23},{8,24},{9,... | collective-permute-start | bytes 208904 | tf_op jit(solution)/shard_map/ppermute | solution.py:134
  31.3 4.6 %collective-permute-start.19 = (f32[128,128]{1,0:T(8,128)}, f32[128,128]{1,0:T(8,128)}, u32[]{:S(2)}, u32[]{:S(2)}) collective-permute-start(f32[128,128]{1,0:T(8,128)} %dynamic-slice_add_fusion.5), channel_id=1, source_target_pairs={{0,8},{1,9},{2,10},{3,11},{4,12},{5,13},{6,14},{7,15},{8,0},{9,1},... | collective-permute-start | bytes 196616 | tf_op jit(solution)/shard_map/ppermute | solution.py:134
  36.7 5.2 %collective-permute-start.20 = (f32[128,128]{1,0:T(8,128)S(1)}, f32[128,128]{1,0:T(8,128)S(1)}, u32[]{:S(2)}, u32[]{:S(2)}) collective-permute-start(f32[128,128]{1,0:T(8,128)S(1)} %add.344), channel_id=1, source_target_pairs={{0,16},{1,17},{2,18},{3,19},{4,20},{5,21},{6,22},{7,23},{8,24},{9,... | collective-permute-start | bytes 196616 | tf_op jit(solution)/shard_map/ppermute | solution.py:134
  38.7 4.8 %collective-permute-start.5 = (f32[136,128]{1,0:T(8,128)S(1)}, f32[136,128]{1,0:T(8,128)S(1)}, u32[]{:S(2)}, u32[]{:S(2)}) collective-permute-start(f32[136,128]{1,0:T(8,128)S(1)} %pad_maximum_fusion.5), channel_id=1, source_target_pairs={{0,8},{1,9},{2,10},{3,11},{4,12},{5,13},{6,14},{7,15},{8,0},{9,1},... | collective-permute-start | bytes 208904 | tf_op jit(solution)/shard_map/ppermute | solution.py:134
  46.3 5.0 %collective-permute-start.22 = (f32[256,128]{1,0:T(8,128)S(1)}, f32[256,128]{1,0:T(8,128)S(1)}, u32[]{:S(2)}, u32[]{:S(2)}) collective-permute-start(f32[256,128]{1,0:T(8,128)S(1)} %maximum_select_fusion.9), channel_id=1, source_target_pairs={{0,2},{1,5},{2,0},{3,7},{4,6},{5,1},{6,4},{7,3},{8,10},{9,13},{10,... | collective-permute-start | bytes 393224 | tf_op jit(solution)/shard_map/ppermute | solution.py:134
  48.0 5.0 %collective-permute-start.9 = (f32[256,128]{1,0:T(8,128)S(1)}, f32[256,128]{1,0:T(8,128)S(1)}, u32[]{:S(2)}, u32[]{:S(2)}) collective-permute-start(f32[256,128]{1,0:T(8,128)S(1)} %maximum_select_fusion.8), channel_id=1, source_target_pairs={{0,4},{1,3},{2,6},{3,1},{4,0},{5,7},{6,2},{7,5},{8,12},{9,11},{10,... | collective-permute-start | bytes 393224 | tf_op jit(solution)/shard_map/ppermute | solution.py:134
  53.1 10.8 %collective-permute-start.6 = (f32[384,256]{1,0:T(8,128)S(1)}, f32[384,256]{1,0:T(8,128)S(1)}, u32[]{:S(2)}, u32[]{:S(2)}) collective-permute-start(f32[384,256]{1,0:T(8,128)S(1)} %get-tuple-element.75), channel_id=1, source_target_pairs={{0,1},{1,2},{2,3},{3,4},{4,5},{5,6},{6,7},{7,8},{8,9},{9,10},{10,1... | collective-permute-start | bytes 1179656 | tf_op jit(solution)/shard_map/ppermute | solution.py:256
  54.8 12.4 %collective-permute-start.34 = (f32[512,128]{1,0:T(8,128)S(1)}, f32[512,128]{1,0:T(8,128)S(1)}, u32[]{:S(2)}, u32[]{:S(2)}) collective-permute-start(f32[512,128]{1,0:T(8,128)S(1)} %get-tuple-element.51), channel_id=1, source_target_pairs={{0,1},{1,0},{2,3},{3,2},{4,5},{5,4},{6,7},{7,6},{8,9},{9,8},{10,11... | collective-permute-start | bytes 786440 | tf_op jit(solution)/shard_map/ppermute | solution.py:134
  57.1 10.2 %collective-permute-start.11 = (f32[512,128]{1,0:T(8,128)S(1)}, f32[512,128]{1,0:T(8,128)S(1)}, u32[]{:S(2)}, u32[]{:S(2)}) collective-permute-start(f32[512,128]{1,0:T(8,128)S(1)} %get-tuple-element.39), channel_id=1, source_target_pairs={{0,1},{1,0},{2,3},{3,2},{4,5},{5,4},{6,7},{7,6},{8,9},{9,8},{10,11... | collective-permute-start | bytes 786440 | tf_op jit(solution)/shard_map/ppermute | solution.py:134
  67.2 5.9 %collective-permute-start.35 = (f32[256,128]{1,0:T(8,128)S(1)}, f32[256,128]{1,0:T(8,128)S(1)}, u32[]{:S(2)}, u32[]{:S(2)}) collective-permute-start(f32[256,128]{1,0:T(8,128)S(1)} %constant_dynamic-slice_fusion.5), channel_id=1, source_target_pairs={{0,2},{1,5},{2,0},{3,7},{4,6},{5,1},{6,4},{7,3},{8,10},{9,13},{10,... | collective-permute-start | bytes 393224 | tf_op jit(solution)/shard_map/ppermute | solution.py:134
  67.4 5.7 %collective-permute-start.12 = (f32[264,128]{1,0:T(8,128)S(1)}, f32[264,128]{1,0:T(8,128)S(1)}, u32[]{:S(2)}, u32[]{:S(2)}) collective-permute-start(f32[264,128]{1,0:T(8,128)S(1)} %pad_maximum_fusion.1), channel_id=1, source_target_pairs={{0,4},{1,3},{2,6},{3,1},{4,0},{5,7},{6,2},{7,5},{8,12},{9,11},{10,... | collective-permute-start | bytes 405512 | tf_op jit(solution)/shard_map/ppermute | solution.py:134
  73.2 4.4 %collective-permute-start.13 = (f32[136,128]{1,0:T(8,128)S(1)}, f32[136,128]{1,0:T(8,128)S(1)}, u32[]{:S(2)}, u32[]{:S(2)}) collective-permute-start(f32[136,128]{1,0:T(8,128)S(1)} %pad_maximum_fusion.6), channel_id=1, source_target_pairs={{0,2},{1,5},{2,0},{3,7},{4,6},{5,1},{6,4},{7,3},{8,10},{9,13},{10,... | collective-permute-start | bytes 208904 | tf_op jit(solution)/shard_map/ppermute | solution.py:134
  77.6 7.4 %collective-permute-start.14 = (f32[136,128]{1,0:T(8,128)S(1)}, f32[136,128]{1,0:T(8,128)S(1)}, u32[]{:S(2)}, u32[]{:S(2)}) collective-permute-start(f32[136,128]{1,0:T(8,128)S(1)} %pad_maximum_fusion.7), channel_id=1, source_target_pairs={{0,16},{1,17},{2,18},{3,19},{4,20},{5,21},{6,22},{7,23},{8,24},{9,... | collective-permute-start | bytes 208904 | tf_op jit(solution)/shard_map/ppermute | solution.py:134
  78.9 5.9 %collective-permute-start.37 = (f32[128,128]{1,0:T(8,128)S(1)}, f32[128,128]{1,0:T(8,128)S(1)}, u32[]{:S(2)}, u32[]{:S(2)}) collective-permute-start(f32[128,128]{1,0:T(8,128)S(1)} %dynamic-slice_add_fusion.4), channel_id=1, source_target_pairs={{0,8},{1,9},{2,10},{3,11},{4,12},{5,13},{6,14},{7,15},{8,0},{9,1},... | collective-permute-start | bytes 196616 | tf_op jit(solution)/shard_map/ppermute | solution.py:134
  84.8 5.3 %collective-permute-start.38 = (f32[128,128]{1,0:T(8,128)S(1)}, f32[128,128]{1,0:T(8,128)S(1)}, u32[]{:S(2)}, u32[]{:S(2)}) collective-permute-start(f32[128,128]{1,0:T(8,128)S(1)} %add.370), channel_id=1, source_target_pairs={{0,16},{1,17},{2,18},{3,19},{4,20},{5,21},{6,22},{7,23},{8,24},{9,... | collective-permute-start | bytes 196616 | tf_op jit(solution)/shard_map/ppermute | solution.py:134
  85.1 5.2 %collective-permute-start.15 = (f32[136,128]{1,0:T(8,128)S(1)}, f32[136,128]{1,0:T(8,128)S(1)}, u32[]{:S(2)}, u32[]{:S(2)}) collective-permute-start(f32[136,128]{1,0:T(8,128)S(1)} %pad_maximum_fusion.8), channel_id=1, source_target_pairs={{0,8},{1,9},{2,10},{3,11},{4,12},{5,13},{6,14},{7,15},{8,0},{9,1},... | collective-permute-start | bytes 208904 | tf_op jit(solution)/shard_map/ppermute | solution.py:134
  94.5 5.0 %collective-permute-start.40 = (f32[256,128]{1,0:T(8,128)S(1)}, f32[256,128]{1,0:T(8,128)S(1)}, u32[]{:S(2)}, u32[]{:S(2)}) collective-permute-start(f32[256,128]{1,0:T(8,128)S(1)} %maximum_select_fusion.11), channel_id=1, source_target_pairs={{0,2},{1,5},{2,0},{3,7},{4,6},{5,1},{6,4},{7,3},{8,10},{9,13},{10,... | collective-permute-start | bytes 393224 | tf_op jit(solution)/shard_map/ppermute | solution.py:134
  94.6 5.0 %collective-permute-start.27 = (f32[256,128]{1,0:T(8,128)S(1)}, f32[256,128]{1,0:T(8,128)S(1)}, u32[]{:S(2)}, u32[]{:S(2)}) collective-permute-start(f32[256,128]{1,0:T(8,128)S(1)} %maximum_select_fusion.10), channel_id=1, source_target_pairs={{0,4},{1,3},{2,6},{3,1},{4,0},{5,7},{6,2},{7,5},{8,12},{9,11},{10,... | collective-permute-start | bytes 393224 | tf_op jit(solution)/shard_map/ppermute | solution.py:134
  100.3 11.0 %collective-permute-start.24 = (f32[384,256]{1,0:T(8,128)S(1)}, f32[384,256]{1,0:T(8,128)S(1)}, u32[]{:S(2)}, u32[]{:S(2)}) collective-permute-start(f32[384,256]{1,0:T(8,128)S(1)} %get-tuple-element.73), channel_id=1, source_target_pairs={{0,1},{1,2},{2,3},{3,4},{4,5},{5,6},{6,7},{7,8},{8,9},{9,10},{10,1... | collective-permute-start | bytes 1179656 | tf_op jit(solution)/shard_map/ppermute | solution.py:256
  103.0 11.4 %collective-permute-start.42 = (f32[512,128]{1,0:T(8,128)}, f32[512,128]{1,0:T(8,128)}, u32[]{:S(2)}, u32[]{:S(2)}) collective-permute-start(f32[512,128]{1,0:T(8,128)} %get-tuple-element.56), channel_id=1, source_target_pairs={{0,1},{1,0},{2,3},{3,2},{4,5},{5,4},{6,7},{7,6},{8,9},{9,8},{10,11... | collective-permute-start | bytes 786440 | tf_op jit(solution)/shard_map/ppermute | solution.py:134
  105.8 9.7 %collective-permute-start.29 = (f32[512,128]{1,0:T(8,128)}, f32[512,128]{1,0:T(8,128)}, u32[]{:S(2)}, u32[]{:S(2)}) collective-permute-start(f32[512,128]{1,0:T(8,128)} %get-tuple-element.48), channel_id=1, source_target_pairs={{0,1},{1,0},{2,3},{3,2},{4,5},{5,4},{6,7},{7,6},{8,9},{9,8},{10,11... | collective-permute-start | bytes 786440 | tf_op jit(solution)/shard_map/ppermute | solution.py:134
  115.5 6.1 %collective-permute-start.43 = (f32[256,128]{1,0:T(8,128)S(1)}, f32[256,128]{1,0:T(8,128)S(1)}, u32[]{:S(2)}, u32[]{:S(2)}) collective-permute-start(f32[256,128]{1,0:T(8,128)S(1)} %constant_dynamic-slice_fusion.3), channel_id=1, source_target_pairs={{0,2},{1,5},{2,0},{3,7},{4,6},{5,1},{6,4},{7,3},{8,10},{9,13},{10,... | collective-permute-start | bytes 393224 | tf_op jit(solution)/shard_map/ppermute | solution.py:134
  116.6 5.1 %collective-permute-start.30 = (f32[264,128]{1,0:T(8,128)S(1)}, f32[264,128]{1,0:T(8,128)S(1)}, u32[]{:S(2)}, u32[]{:S(2)}) collective-permute-start(f32[264,128]{1,0:T(8,128)S(1)} %pad_maximum_fusion.2), channel_id=1, source_target_pairs={{0,4},{1,3},{2,6},{3,1},{4,0},{5,7},{6,2},{7,5},{8,12},{9,11},{10,... | collective-permute-start | bytes 405512 | tf_op jit(solution)/shard_map/ppermute | solution.py:134
  121.6 4.5 %collective-permute-start.44 = (f32[128,128]{1,0:T(8,128)S(1)}, f32[128,128]{1,0:T(8,128)S(1)}, u32[]{:S(2)}, u32[]{:S(2)}) collective-permute-start(f32[128,128]{1,0:T(8,128)S(1)} %constant_dynamic-slice_fusion.2), channel_id=1, source_target_pairs={{0,4},{1,3},{2,6},{3,1},{4,0},{5,7},{6,2},{7,5},{8,12},{9,11},{10,... | collective-permute-start | bytes 196616 | tf_op jit(solution)/shard_map/ppermute | solution.py:134
  130.7 4.9 %collective-permute-start.32 = (f32[72,128]{1,0:T(8,128)S(1)}, f32[72,128]{1,0:T(8,128)S(1)}, u32[]{:S(2)}, u32[]{:S(2)}) collective-permute-start(f32[72,128]{1,0:T(8,128)S(1)} %pad_maximum_fusion.10), channel_id=1, source_target_pairs={{0,16},{1,17},{2,18},{3,19},{4,20},{5,21},{6,22},{7,23},{8,24},{9,... | collective-permute-start | bytes 110600 | tf_op jit(solution)/shard_map/ppermute | solution.py:134
  132.3 5.4 %collective-permute-start.46 = (f32[32,128]{1,0:T(8,128)S(1)}, f32[32,128]{1,0:T(8,128)S(1)}, u32[]{:S(2)}, u32[]{:S(2)}) collective-permute-start(f32[32,128]{1,0:T(8,128)S(1)} %constant_dynamic-slice_fusion), channel_id=1, source_target_pairs={{0,16},{1,17},{2,18},{3,19},{4,20},{5,21},{6,22},{7,23},{8,24},{9,... | collective-permute-start | bytes 49160 | tf_op jit(solution)/shard_map/ppermute | solution.py:134
  (33 other events, 105.7 us)

commit v3 on v2

v3 whole, which is shorter than its diff:
```python
import functools
import math

import jax
import jax.numpy as jnp
from jax import lax
from jax.experimental import pallas as pl
from jax.experimental.pallas import tpu as pltpu
from jax.sharding import PartitionSpec as P

step_size = 0.01
prior_prec = 8.0
item_prec = 1.0
weight_decay = 1.0
rate_scale = 0.04

CHUNKS = 2
CORES = 2
NT = (((1,), (1,)), ((), ()))
TN = (((0,), (0,)), ((), ()))
VMEM = pl.BlockSpec(memory_space=pltpu.VMEM)
SMEM = pl.BlockSpec(memory_space=pltpu.SMEM)


def dot(a, b, dims=(((1,), (0,)), ((), ()))):
    return lax.dot_general(a, b, dims, preferred_element_type=jnp.float32)


def tile_kernel(codes, count, tiles, users, items, grad_u, grad_v, stats, pred, err_b):
    slots, tile, _ = tiles.shape
    grid = items.shape[0] // tile
    user_b = users[...].astype(jnp.bfloat16)
    item_b = items[...].astype(jnp.bfloat16)
    pred[...] = dot(user_b, item_b, NT)
    err_b[...] = jnp.zeros_like(err_b)
    live_slots = count[0]
    sse = jnp.zeros((tile, tile), jnp.float32)
    for slot in range(slots):
        code = codes[slot]
        rows = pl.ds(pl.multiple_of(code // grid * tile, tile), tile)
        cols = pl.ds(pl.multiple_of(code % grid * tile, tile), tile)
        live = (slot < live_slots).astype(jnp.float32)
        err = (tiles[slot].astype(jnp.float32) - pred[rows, cols]) * live
        sse = sse + err * err
        err_b[rows, cols] = err.astype(jnp.bfloat16)
    err_all = err_b[...]
    total = jnp.sum(sse)
    counted = live_slots.astype(jnp.float32) * float(tile * tile)
    row = lax.broadcasted_iota(jnp.int32, stats.shape, 0)
    stats[...] = jnp.where(row == 0, total, jnp.where(row == 1, counted, 0.0))
    grad_u[...] = dot(err_all, item_b)
    grad_v[...] = dot(err_all, user_b, TN)


def tile_pass(codes, count, tiles, users, items):
    rows, rank = users.shape
    f32 = jnp.float32
    return pl.pallas_call(
        tile_kernel,
        out_shape=(
            jax.ShapeDtypeStruct((rows, rank), f32),
            jax.ShapeDtypeStruct((rows, rank), f32),
            jax.ShapeDtypeStruct((8, rank // CORES), f32),
        ),
        in_specs=[SMEM, SMEM, VMEM, VMEM, VMEM],
        out_specs=(VMEM, VMEM, VMEM),
        scratch_shapes=[
            pltpu.VMEM((rows, rows), f32),
            pltpu.VMEM((rows, rows), jnp.bfloat16),
        ],
        compiler_params=pltpu.CompilerParams(vmem_limit_bytes=16 << 20),
        cost_estimate=pl.CostEstimate(
            flops=6 * rows * rows * rank, bytes_accessed=4 * rows * rank * 4, transcendentals=0
        ),
        name="tile_pass",
    )(codes, count, tiles, users, items)


def half_of(ref, core, count=CORES):
    width = ref.shape[1] // count
    return ref[:, pl.ds(pl.multiple_of(core * width, width), width)]


def first_kernel(core, feats, weights, users, mean, *outs):
    mean_now = dot(feats[...], weights[...].astype(jnp.bfloat16))
    mean[...] = mean_now
    here = core[0]
    width = outs[0].shape[1]
    rows = outs[0].shape[0]
    for group, which in ((outs[:CHUNKS], 1 - here), (outs[CHUNKS:], here)):
        offset = (half_of(users, which) - half_of(mean, which)).astype(jnp.bfloat16)
        for chunk, ref in enumerate(group):
            ref[...] = dot(feats[:, chunk * rows : (chunk + 1) * rows], offset, TN)


def first_pass(core, feats, weights, users):
    rows, rank = users.shape
    feat = weights.shape[0]
    f32 = jnp.float32
    return pl.pallas_call(
        first_kernel,
        out_shape=(jax.ShapeDtypeStruct((rows, rank), f32),)
        + (jax.ShapeDtypeStruct((feat // CHUNKS, rank // CORES), f32),) * (2 * CHUNKS),
        in_specs=[SMEM, VMEM, VMEM, VMEM],
        out_specs=(VMEM,) * (1 + 2 * CHUNKS),
        compiler_params=pltpu.CompilerParams(vmem_limit_bytes=8 << 20),
        cost_estimate=pl.CostEstimate(
            flops=4 * rows * feat * rank, bytes_accessed=8 * feat * rank, transcendentals=0
        ),
        name="first_pass",
    )(core, feats, weights, users)


def widen_kernel(narrow, wide):
    wide[...] = narrow[...].astype(jnp.float32)


def join_kernel(own, other, both):
    rows = own.shape[0]
    both[:rows, :] = own[...]
    both[rows:, :] = other[...].astype(jnp.bfloat16)


def part_kernel(feats, weights, part):
    part[...] = dot(feats[:, : weights.shape[0]], weights[...].astype(jnp.bfloat16))


def part_pass(feats, weights):
    rows = feats.shape[0]
    depth, width = weights.shape
    return pl.pallas_call(
        part_kernel,
        out_shape=jax.ShapeDtypeStruct((rows, width), jnp.float32),
        in_specs=[VMEM, VMEM],
        out_specs=VMEM,
        compiler_params=pltpu.CompilerParams(vmem_limit_bytes=8 << 20),
        cost_estimate=pl.CostEstimate(
            flops=2 * rows * depth * width, bytes_accessed=2 * rows * depth, transcendentals=0
        ),
        name="part_pass",
    )(feats, weights)


def prior_kernel(places, core, feats, weights, part, users, others, own_mean, other_mean, offset, *outs):
    depth = weights.shape[0]
    rows = users.shape[0]
    mean = part[...] + dot(feats[:, depth:], weights[...].astype(jnp.bfloat16))
    own_mean[...] = mean[:rows]
    other_mean[...] = mean[rows:]
    offset[:rows, :] = (half_of(users, core[0]) - mean[:rows]).astype(jnp.bfloat16)
    offset[rows:, :] = (others[...] - mean[rows:]).astype(jnp.bfloat16)
    if places is None:
        outs[0][...] = dot(feats[:, :depth], offset[...], TN)
        return
    full = outs[-1]
    full[...] = dot(feats[...], offset[...], TN)
    for ref, (zero, one) in zip(outs[:-1], places, strict=True):
        block = depth // len(zero)
        for place, (first, second) in enumerate(zip(zero, one, strict=True)):
            source = jnp.where(core[0] == 0, first, second) * block
            if block % 8 == 0:
                source = pl.multiple_of(source, block)
            ref[place * block : (place + 1) * block, :] = full[pl.ds(source, block), :]


def prior_pass(core, feats, weights, part, users, others, places=None):
    rows = users.shape[0]
    depth, width = weights.shape
    f32 = jnp.float32
    chunks = 1 if places is None else CHUNKS
    return pl.pallas_call(
        functools.partial(prior_kernel, places),
        out_shape=(
            jax.ShapeDtypeStruct((rows, width), f32),
            jax.ShapeDtypeStruct((rows, width), f32),
            jax.ShapeDtypeStruct((CORES * rows, width), jnp.bfloat16),
        )
        + (jax.ShapeDtypeStruct((depth, width), f32),) * chunks,
        in_specs=[SMEM] + [VMEM] * 5,
        out_specs=(VMEM,) * (3 + chunks),
        scratch_shapes=[] if places is None else [pltpu.VMEM((CHUNKS * depth, width), f32)],
        compiler_params=pltpu.CompilerParams(vmem_limit_bytes=8 << 20),
        cost_estimate=pl.CostEstimate(
            flops=8 * rows * depth * width, bytes_accessed=8 * rows * depth, transcendentals=0
        ),
        name="prior_pass",
    )(core, feats, weights, part, users, others)


def rest_kernel(feats, offset, grad):
    grad[...] = dot(feats[:, grad.shape[0] :], offset[...], TN)


def rest_pass(feats, offset):
    rows, width = offset.shape
    depth = feats.shape[1] // CHUNKS
    return pl.pallas_call(
        rest_kernel,
        out_shape=jax.ShapeDtypeStruct((depth, width), jnp.float32),
        in_specs=[VMEM, VMEM],
        out_specs=VMEM,
        compiler_params=pltpu.CompilerParams(vmem_limit_bytes=8 << 20),
        cost_estimate=pl.CostEstimate(
            flops=2 * rows * depth * width, bytes_accessed=2 * rows * depth, transcendentals=0
        ),
        name="rest_pass",
    )(feats, offset)


def bit_order(devices, core, chunk):
    bits = devices.bit_length() - 1
    near = [1, 2] if core == chunk % 2 else [2, 1]
    far = list(range(3, bits))
    return near + (far if chunk % 2 == 0 else far[::-1])


def swap(array, devices):
    return lax.ppermute(array, "user", [(i, i ^ 1) for i in range(devices)])


def roll(array, devices):
    return lax.ppermute(array, "user", [(i, (i + 1) % devices) for i in range(devices)])


def exchange(array, devices, chunk, stage):
    orders = [bit_order(devices, core, chunk) for core in range(CORES)]
    pairs = [(i, i ^ (1 << orders[i & 1][stage])) for i in range(devices)]
    return lax.ppermute(array, "user", pairs)


def final_places(devices, chunk):
    bits = devices.bit_length() - 1
    result = []
    for core in range(CORES):
        order = bit_order(devices, core, chunk)
        result.append(
            [
                chunk
                | sum(((place >> (bits - 2 - n)) & 1) << bit for n, bit in enumerate(order))
                for place in range(devices // 2)
            ]
        )
    return result


def local(
    ratings,
    tile_index,
    tile_count,
    side_features,
    user_factors,
    item_factors,
    prior_weights,
    user_noise,
    item_noise,
):
    devices = lax.axis_size("user")
    own = lax.axis_index("user")
    stages = devices.bit_length() - 2
    strata = ratings.shape[1]
    rows_dev = user_factors.shape[0]
    feat, rank = prior_weights.shape
    feat_rows = feat // devices
    depth = feat // CHUNKS
    width = rank // CORES
    rate = rate_scale / (rows_dev * devices)
    noise_scale = math.sqrt(2.0 * step_size)
    core = own & 1
    core_ref = core.reshape(1)
    f32 = jnp.float32
    both = range(CHUNKS)

    def my_bit(chunk, stage):
        zero, one = (bit_order(devices, c, chunk)[stage] for c in range(CORES))
        return jnp.where(core == 0, own >> zero, own >> one) & 1

    def columns(array, which):
        return jnp.where(which == 0, array[:, :width], array[:, width:])

    def across(mine, other):
        return jnp.where(
            core == 0, jnp.concatenate([mine, other], 1), jnp.concatenate([other, mine], 1)
        )

    def add(send, keep, chunk, stage, rider):
        if rider is None:
            return keep + exchange(send, devices, chunk, stage), None
        got = exchange(jnp.concatenate([send, rider], 0), devices, chunk, stage)
        return keep + got[: keep.shape[0]], rider + got[keep.shape[0] :]

    def halve(array, chunk, stage, rider):
        half = array.shape[0] // 2
        bit = my_bit(chunk, stage)
        send = lax.dynamic_slice_in_dim(array, (1 - bit) * half, half, 0)
        keep = lax.dynamic_slice_in_dim(array, bit * half, half, 0)
        return add(send, keep, chunk, stage, rider)

    def gather(array, chunk, stage):
        got = exchange(array, devices, chunk, stage)
        return jnp.where(
            my_bit(chunk, stage) == 0,
            jnp.concatenate([array, got], 0),
            jnp.concatenate([got, array], 0),
        )

    def tiles_of(stratum, users, items):
        grad_u, grad_v, stats = tile_pass(
            tile_index[0, stratum], tile_count[0, stratum : stratum + 1], ratings[0, stratum], users, items
        )
        return grad_u, grad_v, stats + swap(stats, devices)

    users = user_factors
    items = item_factors
    mean, *outs = first_pass(core_ref, side_features, prior_weights, users)
    parts = [outs[CHUNKS + c] + swap(outs[c], devices) for c in both]
    grad_u, grad_v, stats = tiles_of(0, users, items)
    mine = columns(prior_weights, core)
    weights = [mine[c * depth : (c + 1) * depth] for c in both]
    wide = pl.pallas_call(
        widen_kernel,
        out_shape=jax.ShapeDtypeStruct(side_features.shape, f32),
        in_specs=[VMEM],
        out_specs=VMEM,
        compiler_params=pltpu.CompilerParams(vmem_limit_bytes=8 << 20),
        name="widen",
    )(side_features)
    feats = pl.pallas_call(
        join_kernel,
        out_shape=jax.ShapeDtypeStruct((CORES * rows_dev, feat), jnp.bfloat16),
        in_specs=[VMEM, VMEM],
        out_specs=VMEM,
        compiler_params=pltpu.CompilerParams(vmem_limit_bytes=8 << 20),
        name="join",
    )(side_features, swap(wide, devices))
    others = None
    for stratum in range(strata):
        last = stratum + 1 == strata
        if stratum:
            part = part_pass(feats, weights[0])
            own_mean, other_mean, offset, *parts = prior_pass(
                core_ref,
                feats,
                weights[1],
                part,
                users,
                others,
                [final_places(devices, c) for c in both] if last else None,
            )
            if not last:
                parts.append(rest_pass(feats, offset))
            mean = across(own_mean, swap(other_mean, devices))
        base = (
            items
            - (step_size * item_prec) * items
            + noise_scale * item_noise[stratum].astype(f32)
        )
        push = step_size * grad_v
        if not last:
            base = roll(base, devices)
            push = roll(push, devices)
        for stage in range(stages):
            for c in both:
                rider = stats if c == CHUNKS - 1 else None
                if stage < 2 or last:
                    parts[c], rider = halve(parts[c], c, stage, rider)
                else:
                    parts[c], rider = add(parts[c], parts[c], c, stage, rider)
                if c == CHUNKS - 1:
                    stats = rider
        precision = (1.0 + stats[1:2, :] / 2.0) / (1.0 + stats[0:1, :] / 2.0)
        precision = jnp.concatenate([precision] * CORES, 1)
        items = base + precision * push
        users = (
            users
            + step_size * (precision * grad_u - prior_prec * (users - mean))
            + noise_scale * user_noise[stratum].astype(f32)
        )
        if not last:
            others = swap(columns(users, 1 - core), devices)
            grad_u, grad_v, stats = tiles_of(stratum + 1, users, items)
        for c in both:
            if last:
                old = jnp.concatenate(weights, 0)
                start = ((own & -2) + c) * feat_rows
            else:
                old = weights[c]
                start = my_bit(c, 0) * (depth // 2) + my_bit(c, 1) * (depth // 4)
            old = lax.dynamic_slice_in_dim(old, start, parts[c].shape[0], 0)
            parts[c] = old + rate * (prior_prec * parts[c] - weight_decay * old)
        if not last:
            for stage in (1, 0):
                for c in both:
                    parts[c] = gather(parts[c], c, stage)
        weights = list(parts)
    zero, one = weights
    rows = across(jnp.where(core == 0, zero, one), swap(jnp.where(core == 0, one, zero), devices))
    return (users, items, rows)


def solution(mesh):
    return jax.shard_map(
        local,
        mesh=mesh,
        in_specs=(
            P("user", None, None, None, None),
            P("user", None, None),
            P("user", None),
            P("user", None),
            P("user", None),
            P("user", None),
            P(),
            P(None, "user", None),
            P(None, "user", None),
        ),
        out_specs=(P("user", None), P("user", None), P("user", None)),
        check_vma=False,
    )
```

time: 143 us -> 134 us (0.937)
  waiting for transfers between devices: 68.2 us -> 48.5 us
  starting transfers between devices: 38.9 us -> 46.7 us
  other arithmetic: 13.5 us -> 16.9 us
  Pallas kernels: 14.6 us -> 12.7 us
  local copies, waits for them, and re-layouts: 5.7 us -> 7.16 us
    ppermute x2 -> x15, waiting for transfers between devices: 12.2 us -> 0.04 us  [the longest x11 0.03 us: swap(): return lax.ppermute(array, 'user', [(i, i ^ 1) for i in range(devices)])]
    ppermute x45 -> x32, waiting for transfers between devices: 55.9 us -> 48.4 us  [exchange(): return lax.ppermute(array, 'user', pairs)]
    pallas_call x6 -> x2, Pallas kernels: 8.82 us -> 2.26 us  [prior_pass(): pl.pallas_call(functools.partial(prior_kernel, places), out_shape=(jax.Sh...]
    ppermute x2 -> x15, starting transfers between devices: 0.83 us -> 6.72 us  [the longest x11 5.95 us: swap(): return lax.ppermute(array, 'user', [(i, i ^ 1) for i in range(devices)])]
    pallas_call x0 -> x6, Pallas kernels: none -> 4.67 us  [the longest x1 1.85 us: first_pass(): pl.pallas_call(first_kernel, out_shape=(jax.ShapeDtypeStruct((rows, rank)...]
    add x6 -> x10, other arithmetic: 4.39 us -> 8.47 us  [the longest x2 3.47 us: local(): items - step_size * item_prec * items]
    add x15 -> x9, other arithmetic: 5.65 us -> 1.59 us  [add(): return (keep + exchange(send, devices, chunk, stage), None)]
    unnamed x36 -> x32, local copies, waits for them, and re-layouts: 2.34 us -> 5.43 us
  transfers between devices with their start and end apart: 47 -> 47, of which waited for: 28 -> 22; matrix products, arithmetic and copies ran while one was open for 8% -> 12% of each run, Pallas kernels for 9% -> 9%
where the time goes in v3:
time: 134 us; the launch traced here: 133 us
  waiting for transfers between devices  48.5 us (36%)
  starting transfers between devices  46.7 us (35%)
  other arithmetic  16.9 us (13%)
  Pallas kernels  12.7 us (9%)
  local copies, waits for them, and re-layouts  7.16 us (5%)
  between operations  1.49 us (1%)
    ppermute x32, waiting for transfers between devices, exchange(): return lax.ppermute(array, 'user', pairs)  48.4 us
    ppermute x32, starting transfers between devices, exchange(): return lax.ppermute(array, 'user', pairs)  40 us
    ppermute x11, starting transfers between devices, swap(): return lax.ppermute(array, 'user', [(i, i ^ 1) for i in range(devices)])  5.95 us
    pallas_call x3, Pallas kernels, tile_pass(): pl.pallas_call(tile_kernel, out_shape=(jax.ShapeDtypeStruct((rows, rank),...  5.78 us
    unnamed x32, local copies, waits for them, and re-layouts  5.43 us
    add x2, other arithmetic, local(): items - step_size * item_prec * items  3.47 us
  transfers between devices with their start and end apart: 47, of which 22 were waited for; matrix products, arithmetic and copies ran while one was open for 12% of the time, Pallas kernels for 9%

profile of v3, /device:TPU:0, one launch (start us, length us, event | category | flops | bytes accessed | tf_op | source)
XLA Modules:
  0.0 133.4 jit_solution(11068878415532036085)
XLA Ops:
  0.7 1.9 %fusion = f32[384,256]{1,0:T(8,128)} fusion(f32[384,256]{1,0:T(8,128)} %items.1, bf16[3,384,256]{2,1,0:T(8,128)(2,1)} %param.17), kind=kLoop, calls=%fused_computation.8 | loop fusion | flops 491520 | bytes 983040 | tf_op jit(solution)/shard_map/add | solution.py:353
  6.3 1.9 %first_pass.1 = (f32[384,256]{1,0:T(8,128)S(1)}, f32[512,128]{1,0:T(8,128)}, f32[512,128]{1,0:T(8,128)}, f32[512,128]{1,0:T(8,128)S(1)}, f32[512,128]{1,0:T(8,128)S(1)}) custom-call(s32[1]{0:T(128)} %bitcast.3.core, bf16[384,1024]{1,0:T(8,128)(2,1)S(1)} %copy-done, f32[1024,256]{1,0:T(8,128)S(1)} %copy-done.2, f32[384,256]{1,0:T(8,128)S(1)} %copy-done.4), custom_call_target="tpu_custom_call" | custom-call | flops 402653184 | bytes 2097152 | tf_op jit(solution)/shard_map/first_pass/pallas_call | solution.py:100
  9.6 2.6 %collective-permute-start.12 = (f32[512,128]{1,0:T(8,128)}, f32[512,128]{1,0:T(8,128)}, u32[]{:S(2)}, u32[]{:S(2)}) collective-permute-start(f32[512,128]{1,0:T(8,128)} %get-tuple-element.33), channel_id=1, source_target_pairs={{0,1},{1,0},{2,3},{3,2},{4,5},{5,4},{6,7},{7,6},{8,9},{9,8},{10,11... | collective-permute-start | bytes 786440 | tf_op jit(solution)/shard_map/ppermute | solution.py:218
  12.9 2.0 %tile_pass.3 = (f32[384,256]{1,0:T(8,128)S(1)}, f32[384,256]{1,0:T(8,128)S(1)}, f32[8,128]{1,0:T(8,128)S(1)}) custom-call(s32[6]{0:T(128)S(1)} %get-tuple-element.58.codes, s32[1]{0:T(128)} %bitcast.1.count, bf16[6,128,128]{2,1,0:T(8,128)(2,1)S(1)} %get-tuple-element.53.tiles, f32[384,256]{1,0:T(8,128)S(1)} %copy-done.5, f32[384,256]{1,0:T(8,128)S(1)} %copy-done.6), custom_call_target="tpu_custom_call" | custom-call | flops 226492416 | bytes 1572864 | tf_op jit(solution)/shard_map/tile_pass/pallas_call | solution.py:58
  25.9 4.4 %collective-permute-start.14 = (f32[128,128]{1,0:T(8,128)S(1)}, f32[128,128]{1,0:T(8,128)S(1)}, u32[]{:S(2)}, u32[]{:S(2)}) collective-permute-start(f32[128,128]{1,0:T(8,128)S(1)} %constant_dynamic-slice_fusion.12), channel_id=1, source_target_pairs={{0,4},{1,3},{2,6},{3,1},{4,0},{5,7},{6,2},{7,5},{8,12},{9,11},{10,... | collective-permute-start | bytes 196616 | tf_op jit(solution)/shard_map/ppermute | solution.py:228
  30.4 2.3 %collective-permute-done.14 = f32[128,128]{1,0:T(8,128)S(1)} collective-permute-done((f32[128,128]{1,0:T(8,128)S(1)}, f32[128,128]{1,0:T(8,128)S(1)}, u32[]{:S(2)}, u32[]{:S(2)}) %collective-permute-start.14) | collective-permute-done | bytes 65568 | tf_op jit(solution)/shard_map/ppermute | solution.py:228
  40.7 2.8 %collective-permute-done.4 = f32[136,128]{1,0:T(8,128)} collective-permute-done((f32[136,128]{1,0:T(8,128)}, f32[136,128]{1,0:T(8,128)}, u32[]{:S(2)}, u32[]{:S(2)}) %collective-permute-start.4) | collective-permute-done | bytes 69664 | tf_op jit(solution)/shard_map/ppermute | solution.py:228
  47.6 1.9 %collective-permute-done.5 = f32[136,128]{1,0:T(8,128)S(1)} collective-permute-done((f32[136,128]{1,0:T(8,128)S(1)}, f32[136,128]{1,0:T(8,128)S(1)}, u32[]{:S(2)}, u32[]{:S(2)}) %collective-permute-start.5) | collective-permute-done | bytes 69664 | tf_op jit(solution)/shard_map/ppermute | solution.py:228
  51.2 1.9 %tile_pass.4 = (f32[384,256]{1,0:T(8,128)S(1)}, f32[384,256]{1,0:T(8,128)S(1)}, f32[8,128]{1,0:T(8,128)S(1)}) custom-call(s32[6]{0:T(128)S(1)} %get-tuple-element.59.codes, s32[1]{0:T(128)} %bitcast.7.count, bf16[6,128,128]{2,1,0:T(8,128)(2,1)S(1)} %get-tuple-element.54.tiles, f32[384,256]{1,0:T(8,128)S(1)} %get-tuple-element.62.users, ...), custom_call_target="tpu_custom_call" | custom-call | flops 226492416 | bytes 1572864 | tf_op jit(solution)/shard_map/tile_pass/pallas_call | solution.py:58
  54.5 2.0 %collective-permute-start.18 = (f32[256,128]{1,0:T(8,128)S(1)}, f32[256,128]{1,0:T(8,128)S(1)}, u32[]{:S(2)}, u32[]{:S(2)}) collective-permute-start(f32[256,128]{1,0:T(8,128)S(1)} %maximum_select_fusion.7), channel_id=1, source_target_pairs={{0,2},{1,5},{2,0},{3,7},{4,6},{5,1},{6,4},{7,3},{8,10},{9,13},{10,... | collective-permute-start | bytes 393224 | tf_op jit(solution)/shard_map/ppermute | solution.py:228
  56.5 2.2 %collective-permute-done.10 = f32[128,128]{1,0:T(8,128)S(1)} collective-permute-done((f32[128,128]{1,0:T(8,128)S(1)}, f32[128,128]{1,0:T(8,128)S(1)}, u32[]{:S(2)}, u32[]{:S(2)}) %collective-permute-start.10) | collective-permute-done | bytes 65568 | tf_op jit(solution)/shard_map/ppermute | solution.py:228
  58.7 5.3 %collective-permute-start.11 = (f32[256,128]{1,0:T(8,128)S(1)}, f32[256,128]{1,0:T(8,128)S(1)}, u32[]{:S(2)}, u32[]{:S(2)}) collective-permute-start(f32[256,128]{1,0:T(8,128)S(1)} %maximum_select_fusion.6), channel_id=1, source_target_pairs={{0,4},{1,3},{2,6},{3,1},{4,0},{5,7},{6,2},{7,5},{8,12},{9,11},{10,... | collective-permute-start | bytes 393224 | tf_op jit(solution)/shard_map/ppermute | solution.py:228
  64.1 2.8 %collective-permute-done.11 = f32[256,128]{1,0:T(8,128)S(1)} collective-permute-done((f32[256,128]{1,0:T(8,128)S(1)}, f32[256,128]{1,0:T(8,128)S(1)}, u32[]{:S(2)}, u32[]{:S(2)}) %collective-permute-start.11) | collective-permute-done | bytes 131104 | tf_op jit(solution)/shard_map/ppermute | solution.py:228
  70.5 2.1 %collective-permute-start.20 = (f32[264,128]{1,0:T(8,128)S(1)}, f32[264,128]{1,0:T(8,128)S(1)}, u32[]{:S(2)}, u32[]{:S(2)}) collective-permute-start(f32[264,128]{1,0:T(8,128)S(1)} %pad_maximum_fusion.1), channel_id=1, source_target_pairs={{0,4},{1,3},{2,6},{3,1},{4,0},{5,7},{6,2},{7,5},{8,12},{9,11},{10,... | collective-permute-start | bytes 405512 | tf_op jit(solution)/shard_map/ppermute | solution.py:228
  72.5 3.5 %collective-permute-done.30 = f32[256,128]{1,0:T(8,128)S(1)} collective-permute-done((f32[256,128]{1,0:T(8,128)S(1)}, f32[256,128]{1,0:T(8,128)S(1)}, u32[]{:S(2)}, u32[]{:S(2)}) %collective-permute-start.30) | collective-permute-done | bytes 131104 | tf_op jit(solution)/shard_map/ppermute | solution.py:228
  76.1 1.7 %collective-permute-start.31 = (f32[128,128]{1,0:T(8,128)S(1)}, f32[128,128]{1,0:T(8,128)S(1)}, u32[]{:S(2)}, u32[]{:S(2)}) collective-permute-start(f32[128,128]{1,0:T(8,128)S(1)} %constant_dynamic-slice_fusion.8), channel_id=1, source_target_pairs={{0,4},{1,3},{2,6},{3,1},{4,0},{5,7},{6,2},{7,5},{8,12},{9,11},{10,... | collective-permute-start | bytes 196616 | tf_op jit(solution)/shard_map/ppermute | solution.py:228
  78.4 2.0 %collective-permute-done.31 = f32[128,128]{1,0:T(8,128)S(1)} collective-permute-done((f32[128,128]{1,0:T(8,128)S(1)}, f32[128,128]{1,0:T(8,128)S(1)}, u32[]{:S(2)}, u32[]{:S(2)}) %collective-permute-start.31) | collective-permute-done | bytes 65568 | tf_op jit(solution)/shard_map/ppermute | solution.py:228
  80.5 1.7 %collective-permute-done.21 = f32[136,128]{1,0:T(8,128)S(1)} collective-permute-done((f32[136,128]{1,0:T(8,128)S(1)}, f32[136,128]{1,0:T(8,128)S(1)}, u32[]{:S(2)}, u32[]{:S(2)}) %collective-permute-start.21) | collective-permute-done | bytes 69664 | tf_op jit(solution)/shard_map/ppermute | solution.py:228
  86.2 3.7 %collective-permute-done.22 = f32[136,128]{1,0:T(8,128)S(1)} collective-permute-done((f32[136,128]{1,0:T(8,128)S(1)}, f32[136,128]{1,0:T(8,128)S(1)}, u32[]{:S(2)}, u32[]{:S(2)}) %collective-permute-start.22) | collective-permute-done | bytes 69664 | tf_op jit(solution)/shard_map/ppermute | solution.py:228
  92.1 2.2 %collective-permute-done.23 = f32[136,128]{1,0:T(8,128)S(1)} collective-permute-done((f32[136,128]{1,0:T(8,128)S(1)}, f32[136,128]{1,0:T(8,128)S(1)}, u32[]{:S(2)}, u32[]{:S(2)}) %collective-permute-start.23) | collective-permute-done | bytes 69664 | tf_op jit(solution)/shard_map/ppermute | solution.py:228
  94.3 3.0 %collective-permute-start.28 = (f32[128,128]{1,0:T(8,128)S(1)}, f32[128,128]{1,0:T(8,128)S(1)}, u32[]{:S(2)}, u32[]{:S(2)}) collective-permute-start(f32[128,128]{1,0:T(8,128)S(1)} %fusion.19), channel_id=1, source_target_pairs={{0,2},{1,5},{2,0},{3,7},{4,6},{5,1},{6,4},{7,3},{8,10},{9,13},{10,... | collective-permute-start | bytes 196616 | tf_op jit(solution)/shard_map/ppermute | solution.py:228
  97.5 1.9 %tile_pass.5 = (f32[384,256]{1,0:T(8,128)S(1)}, f32[384,256]{1,0:T(8,128)S(1)}, f32[8,128]{1,0:T(8,128)S(1)}) custom-call(s32[6]{0:T(128)S(1)} %get-tuple-element.57.codes, s32[1]{0:T(128)} %bitcast.13.count, bf16[6,128,128]{2,1,0:T(8,128)(2,1)S(1)} %get-tuple-element.52.tiles, f32[384,256]{1,0:T(8,128)S(1)} %get-tuple-element.61.users, ...), custom_call_target="tpu_custom_call" | custom-call | flops 226492416 | bytes 1572864 | tf_op jit(solution)/shard_map/tile_pass/pallas_call | solution.py:58
  99.7 1.9 %collective-permute-start.29 = (f32[256,128]{1,0:T(8,128)S(1)}, f32[256,128]{1,0:T(8,128)S(1)}, u32[]{:S(2)}, u32[]{:S(2)}) collective-permute-start(f32[256,128]{1,0:T(8,128)S(1)} %maximum_select_fusion.8), channel_id=1, source_target_pairs={{0,4},{1,3},{2,6},{3,1},{4,0},{5,7},{6,2},{7,5},{8,12},{9,11},{10,... | collective-permute-start | bytes 393224 | tf_op jit(solution)/shard_map/ppermute | solution.py:228
  101.7 3.9 %collective-permute-done.35 = f32[256,128]{1,0:T(8,128)S(1)} collective-permute-done((f32[256,128]{1,0:T(8,128)S(1)}, f32[256,128]{1,0:T(8,128)S(1)}, u32[]{:S(2)}, u32[]{:S(2)}) %collective-permute-start.35) | collective-permute-done | bytes 131104 | tf_op jit(solution)/shard_map/ppermute | solution.py:228
  109.5 4.2 %collective-permute-done.42 = f32[256,128]{1,0:T(8,128)S(1)} collective-permute-done((f32[256,128]{1,0:T(8,128)S(1)}, f32[256,128]{1,0:T(8,128)S(1)}, u32[]{:S(2)}, u32[]{:S(2)}) %collective-permute-start.42) | collective-permute-done | bytes 131104 | tf_op jit(solution)/shard_map/ppermute | solution.py:228
  113.9 2.1 %collective-permute-start.38 = (f32[136,128]{1,0:T(8,128)S(1)}, f32[136,128]{1,0:T(8,128)S(1)}, u32[]{:S(2)}, u32[]{:S(2)}) collective-permute-start(f32[136,128]{1,0:T(8,128)S(1)} %pad_maximum_fusion.9), channel_id=1, source_target_pairs={{0,2},{1,5},{2,0},{3,7},{4,6},{5,1},{6,4},{7,3},{8,10},{9,13},{10,... | collective-permute-start | bytes 208904 | tf_op jit(solution)/shard_map/ppermute | solution.py:228
  116.0 2.1 %collective-permute-done.43 = f32[128,128]{1,0:T(8,128)S(1)} collective-permute-done((f32[128,128]{1,0:T(8,128)S(1)}, f32[128,128]{1,0:T(8,128)S(1)}, u32[]{:S(2)}, u32[]{:S(2)}) %collective-permute-start.43) | collective-permute-done | bytes 65568 | tf_op jit(solution)/shard_map/ppermute | solution.py:228
  120.1 2.0 %collective-permute-done.44 = f32[64,128]{1,0:T(8,128)S(1)} collective-permute-done((f32[64,128]{1,0:T(8,128)S(1)}, f32[64,128]{1,0:T(8,128)S(1)}, u32[]{:S(2)}, u32[]{:S(2)}) %collective-permute-start.44) | collective-permute-done | bytes 32800 | tf_op jit(solution)/shard_map/ppermute | solution.py:228
  123.4 2.0 %collective-permute-start.40 = (f32[40,128]{1,0:T(8,128)S(1)}, f32[40,128]{1,0:T(8,128)S(1)}, u32[]{:S(2)}, u32[]{:S(2)}) collective-permute-start(f32[40,128]{1,0:T(8,128)S(1)} %pad_maximum_fusion.11), channel_id=1, source_target_pairs={{0,8},{1,9},{2,10},{3,11},{4,12},{5,13},{6,14},{7,15},{8,0},{9,1},... | collective-permute-start | bytes 61448 | tf_op jit(solution)/shard_map/ppermute | solution.py:228
  125.3 1.9 %collective-permute-done.40 = f32[40,128]{1,0:T(8,128)S(1)} collective-permute-done((f32[40,128]{1,0:T(8,128)S(1)}, f32[40,128]{1,0:T(8,128)S(1)}, u32[]{:S(2)}, u32[]{:S(2)}) %collective-permute-start.40) | collective-permute-done | bytes 20512 | tf_op jit(solution)/shard_map/ppermute | solution.py:228
  127.2 2.7 %collective-permute-done.45 = f32[32,128]{1,0:T(8,128)S(1)} collective-permute-done((f32[32,128]{1,0:T(8,128)S(1)}, f32[32,128]{1,0:T(8,128)S(1)}, u32[]{:S(2)}, u32[]{:S(2)}) %collective-permute-start.45) | collective-permute-done | bytes 16416 | tf_op jit(solution)/shard_map/ppermute | solution.py:228
  130.1 1.8 %fusion.3 = f32[384,256]{1,0:T(8,128)} fusion(f32[384,256]{1,0:T(8,128)S(1)} %get-tuple-element.60.items, f32[384,256]{1,0:T(8,128)S(1)} %get-tuple-element.45, f32[256]{0:T(256)S(1)} %broadcast_multiply_fusion.2, bf16[3,384,256]{2,1,0:T(8,128)(2,1)} %param.17), kind=kLoop, calls=%fused_computation.11 | loop fusion | flops 688128 | bytes 1377280 | tf_op jit(solution)/shard_map/add | solution.py:372
  (204 shorter events, 51.8 us)
Async XLA Ops:
  2.5 47.0 %collective-permute-start.6 = (f32[384,256]{1,0:T(8,128)}, f32[384,256]{1,0:T(8,128)}, u32[]{:S(2)}, u32[]{:S(2)}) collective-permute-start(f32[384,256]{1,0:T(8,128)} %fusion), channel_id=1, source_target_pairs={{0,1},{1,2},{2,3},{3,4},{4,5},{5,6},{6,7},{7,8},{8,9},{9,10},{10,1... | collective-permute-start | bytes 1179656 | tf_op jit(solution)/shard_map/ppermute | solution.py:222
  9.6 9.4 %collective-permute-start.12 = (f32[512,128]{1,0:T(8,128)}, f32[512,128]{1,0:T(8,128)}, u32[]{:S(2)}, u32[]{:S(2)}) collective-permute-start(f32[512,128]{1,0:T(8,128)} %get-tuple-element.33), channel_id=1, source_target_pairs={{0,1},{1,0},{2,3},{3,2},{4,5},{5,4},{6,7},{7,6},{8,9},{9,8},{10,11... | collective-permute-start | bytes 786440 | tf_op jit(solution)/shard_map/ppermute | solution.py:218
  15.8 33.8 %collective-permute-start.7 = (f32[384,256]{1,0:T(8,128)}, f32[384,256]{1,0:T(8,128)}, u32[]{:S(2)}, u32[]{:S(2)}) collective-permute-start(f32[384,256]{1,0:T(8,128)} %broadcast_multiply_fusion.1), channel_id=1, source_target_pairs={{0,1},{1,2},{2,3},{3,4},{4,5},{5,6},{6,7},{7,8},{8,9},{9,10},{10,1... | collective-permute-start | bytes 1179656 | tf_op jit(solution)/shard_map/ppermute | solution.py:222
  18.4 48.5 %collective-permute-start.9 = (f32[384,1024]{1,0:T(8,128)S(1)}, f32[384,1024]{1,0:T(8,128)}, u32[]{:S(2)}, u32[]{:S(2)}) collective-permute-start(f32[384,1024]{1,0:T(8,128)S(1)} %widen.1), channel_id=1, source_target_pairs={{0,1},{1,0},{2,3},{3,2},{4,5},{5,4},{6,7},{7,6},{8,9},{9,8},{10,11... | collective-permute-start | bytes 4718600 | tf_op jit(solution)/shard_map/ppermute | solution.py:218
  20.1 5.8 %collective-permute-start.13 = (f32[256,128]{1,0:T(8,128)S(1)}, f32[256,128]{1,0:T(8,128)S(1)}, u32[]{:S(2)}, u32[]{:S(2)}) collective-permute-start(f32[256,128]{1,0:T(8,128)S(1)} %constant_dynamic-slice_fusion.13), channel_id=1, source_target_pairs={{0,2},{1,5},{2,0},{3,7},{4,6},{5,1},{6,4},{7,3},{8,10},{9,13},{10,... | collective-permute-start | bytes 393224 | tf_op jit(solution)/shard_map/ppermute | solution.py:228
  22.7 7.5 %collective-permute-start.2 = (f32[264,128]{1,0:T(8,128)S(1)}, f32[264,128]{1,0:T(8,128)S(1)}, u32[]{:S(2)}, u32[]{:S(2)}) collective-permute-start(f32[264,128]{1,0:T(8,128)S(1)} %pad_maximum_fusion), channel_id=1, source_target_pairs={{0,4},{1,3},{2,6},{3,1},{4,0},{5,7},{6,2},{7,5},{8,12},{9,11},{10,... | collective-permute-start | bytes 405512 | tf_op jit(solution)/shard_map/ppermute | solution.py:228
  25.9 6.8 %collective-permute-start.14 = (f32[128,128]{1,0:T(8,128)S(1)}, f32[128,128]{1,0:T(8,128)S(1)}, u32[]{:S(2)}, u32[]{:S(2)}) collective-permute-start(f32[128,128]{1,0:T(8,128)S(1)} %constant_dynamic-slice_fusion.12), channel_id=1, source_target_pairs={{0,4},{1,3},{2,6},{3,1},{4,0},{5,7},{6,2},{7,5},{8,12},{9,11},{10,... | collective-permute-start | bytes 196616 | tf_op jit(solution)/shard_map/ppermute | solution.py:228
  33.3 4.9 %collective-permute-start.15 = (f32[128,128]{1,0:T(8,128)}, f32[128,128]{1,0:T(8,128)}, u32[]{:S(2)}, u32[]{:S(2)}) collective-permute-start(f32[128,128]{1,0:T(8,128)} %dynamic-slice_add_fusion.5), channel_id=1, source_target_pairs={{0,8},{1,9},{2,10},{3,11},{4,12},{5,13},{6,14},{7,15},{8,0},{9,1},... | collective-permute-start | bytes 196616 | tf_op jit(solution)/shard_map/ppermute | solution.py:228
  36.0 7.5 %collective-permute-start.4 = (f32[136,128]{1,0:T(8,128)}, f32[136,128]{1,0:T(8,128)}, u32[]{:S(2)}, u32[]{:S(2)}) collective-permute-start(f32[136,128]{1,0:T(8,128)} %pad_maximum_fusion.4), channel_id=1, source_target_pairs={{0,16},{1,17},{2,18},{3,19},{4,20},{5,21},{6,22},{7,23},{8,24},{9,... | collective-permute-start | bytes 208904 | tf_op jit(solution)/shard_map/ppermute | solution.py:228
  39.2 6.0 %collective-permute-start.16 = (f32[128,128]{1,0:T(8,128)S(1)}, f32[128,128]{1,0:T(8,128)S(1)}, u32[]{:S(2)}, u32[]{:S(2)}) collective-permute-start(f32[128,128]{1,0:T(8,128)S(1)} %add.317), channel_id=1, source_target_pairs={{0,16},{1,17},{2,18},{3,19},{4,20},{5,21},{6,22},{7,23},{8,24},{9,... | collective-permute-start | bytes 196616 | tf_op jit(solution)/shard_map/ppermute | solution.py:228
  46.1 8.4 %collective-permute-start.17 = (f32[128,128]{1,0:T(8,128)S(1)}, f32[128,128]{1,0:T(8,128)S(1)}, u32[]{:S(2)}, u32[]{:S(2)}) collective-permute-start(f32[128,128]{1,0:T(8,128)S(1)} %multiply_add_fusion.3), channel_id=1, source_target_pairs={{0,4},{1,3},{2,6},{3,1},{4,0},{5,7},{6,2},{7,5},{8,12},{9,11},{10,... | collective-permute-start | bytes 196616 | tf_op jit(solution)/shard_map/ppermute | solution.py:228
  51.1 46.2 %collective-permute-start.25 = (f32[384,256]{1,0:T(8,128)S(1)}, f32[384,256]{1,0:T(8,128)S(1)}, u32[]{:S(2)}, u32[]{:S(2)}) collective-permute-start(f32[384,256]{1,0:T(8,128)S(1)} %get-tuple-element.50), channel_id=1, source_target_pairs={{0,1},{1,2},{2,3},{3,4},{4,5},{5,6},{6,7},{7,8},{8,9},{9,10},{10,1... | collective-permute-start | bytes 1179656 | tf_op jit(solution)/shard_map/ppermute | solution.py:222
  53.1 10.9 %collective-permute-start.8 = (f32[8,128]{1,0:T(8,128)S(1)}, f32[8,128]{1,0:T(8,128)S(1)}, u32[]{:S(2)}, u32[]{:S(2)}) collective-permute-start(f32[8,128]{1,0:T(8,128)S(1)} %get-tuple-element.31), channel_id=1, source_target_pairs={{0,1},{1,0},{2,3},{3,2},{4,5},{5,4},{6,7},{7,6},{8,9},{9,8},{10,11... | collective-permute-start | bytes 12296 | tf_op jit(solution)/shard_map/ppermute | solution.py:218
  54.5 9.6 %collective-permute-start.18 = (f32[256,128]{1,0:T(8,128)S(1)}, f32[256,128]{1,0:T(8,128)S(1)}, u32[]{:S(2)}, u32[]{:S(2)}) collective-permute-start(f32[256,128]{1,0:T(8,128)S(1)} %maximum_select_fusion.7), channel_id=1, source_target_pairs={{0,2},{1,5},{2,0},{3,7},{4,6},{5,1},{6,4},{7,3},{8,10},{9,13},{10,... | collective-permute-start | bytes 393224 | tf_op jit(solution)/shard_map/ppermute | solution.py:228
  58.7 8.2 %collective-permute-start.11 = (f32[256,128]{1,0:T(8,128)S(1)}, f32[256,128]{1,0:T(8,128)S(1)}, u32[]{:S(2)}, u32[]{:S(2)}) collective-permute-start(f32[256,128]{1,0:T(8,128)S(1)} %maximum_select_fusion.6), channel_id=1, source_target_pairs={{0,4},{1,3},{2,6},{3,1},{4,0},{5,7},{6,2},{7,5},{8,12},{9,11},{10,... | collective-permute-start | bytes 393224 | tf_op jit(solution)/shard_map/ppermute | solution.py:228
  64.0 4.9 %collective-permute-start.19 = (f32[384,128]{1,0:T(8,128)S(1)}, f32[384,128]{1,0:T(8,128)S(1)}, u32[]{:S(2)}, u32[]{:S(2)}) collective-permute-start(f32[384,128]{1,0:T(8,128)S(1)} %slice_select_fusion.2), channel_id=1, source_target_pairs={{0,1},{1,0},{2,3},{3,2},{4,5},{5,4},{6,7},{7,6},{8,9},{9,8},{10,11... | collective-permute-start | bytes 589832 | tf_op jit(solution)/shard_map/ppermute | solution.py:218
  70.3 5.7 %collective-permute-start.30 = (f32[256,128]{1,0:T(8,128)S(1)}, f32[256,128]{1,0:T(8,128)S(1)}, u32[]{:S(2)}, u32[]{:S(2)}) collective-permute-start(f32[256,128]{1,0:T(8,128)S(1)} %constant_dynamic-slice_fusion.9), channel_id=1, source_target_pairs={{0,2},{1,5},{2,0},{3,7},{4,6},{5,1},{6,4},{7,3},{8,10},{9,13},{10,... | collective-permute-start | bytes 393224 | tf_op jit(solution)/shard_map/ppermute | solution.py:228
  70.5 7.4 %collective-permute-start.20 = (f32[264,128]{1,0:T(8,128)S(1)}, f32[264,128]{1,0:T(8,128)S(1)}, u32[]{:S(2)}, u32[]{:S(2)}) collective-permute-start(f32[264,128]{1,0:T(8,128)S(1)} %pad_maximum_fusion.1), channel_id=1, source_target_pairs={{0,4},{1,3},{2,6},{3,1},{4,0},{5,7},{6,2},{7,5},{8,12},{9,11},{10,... | collective-permute-start | bytes 405512 | tf_op jit(solution)/shard_map/ppermute | solution.py:228
  82.3 7.6 %collective-permute-start.22 = (f32[136,128]{1,0:T(8,128)S(1)}, f32[136,128]{1,0:T(8,128)S(1)}, u32[]{:S(2)}, u32[]{:S(2)}) collective-permute-start(f32[136,128]{1,0:T(8,128)S(1)} %pad_maximum_fusion.7), channel_id=1, source_target_pairs={{0,16},{1,17},{2,18},{3,19},{4,20},{5,21},{6,22},{7,23},{8,24},{9,... | collective-permute-start | bytes 208904 | tf_op jit(solution)/shard_map/ppermute | solution.py:228
  82.4 14.9 %collective-permute-start.26 = (f32[384,256]{1,0:T(8,128)S(1)}, f32[384,256]{1,0:T(8,128)S(1)}, u32[]{:S(2)}, u32[]{:S(2)}) collective-permute-start(f32[384,256]{1,0:T(8,128)S(1)} %broadcast_multiply_fusion), channel_id=1, source_target_pairs={{0,1},{1,2},{2,3},{3,4},{4,5},{5,6},{6,7},{7,8},{8,9},{9,10},{10,1... | collective-permute-start | bytes 1179656 | tf_op jit(solution)/shard_map/ppermute | solution.py:222
  82.7 14.6 %collective-permute-start.24 = (f32[384,128]{1,0:T(8,128)S(1)}, f32[384,128]{1,0:T(8,128)S(1)}, u32[]{:S(2)}, u32[]{:S(2)}) collective-permute-start(f32[384,128]{1,0:T(8,128)S(1)} %get-tuple-element.37), channel_id=1, source_target_pairs={{0,1},{1,0},{2,3},{3,2},{4,5},{5,4},{6,7},{7,6},{8,9},{9,8},{10,11... | collective-permute-start | bytes 589832 | tf_op jit(solution)/shard_map/ppermute | solution.py:218
  84.8 6.0 %collective-permute-start.33 = (f32[128,128]{1,0:T(8,128)S(1)}, f32[128,128]{1,0:T(8,128)S(1)}, u32[]{:S(2)}, u32[]{:S(2)}) collective-permute-start(f32[128,128]{1,0:T(8,128)S(1)} %add.338), channel_id=1, source_target_pairs={{0,16},{1,17},{2,18},{3,19},{4,20},{5,21},{6,22},{7,23},{8,24},{9,... | collective-permute-start | bytes 196616 | tf_op jit(solution)/shard_map/ppermute | solution.py:228
  90.9 8.7 %collective-permute-start.34 = (f32[128,128]{1,0:T(8,128)S(1)}, f32[128,128]{1,0:T(8,128)S(1)}, u32[]{:S(2)}, u32[]{:S(2)}) collective-permute-start(f32[128,128]{1,0:T(8,128)S(1)} %multiply_add_fusion.2), channel_id=1, source_target_pairs={{0,4},{1,3},{2,6},{3,1},{4,0},{5,7},{6,2},{7,5},{8,12},{9,11},{10,... | collective-permute-start | bytes 196616 | tf_op jit(solution)/shard_map/ppermute | solution.py:228
  94.3 5.3 %collective-permute-start.28 = (f32[128,128]{1,0:T(8,128)S(1)}, f32[128,128]{1,0:T(8,128)S(1)}, u32[]{:S(2)}, u32[]{:S(2)}) collective-permute-start(f32[128,128]{1,0:T(8,128)S(1)} %fusion.19), channel_id=1, source_target_pairs={{0,2},{1,5},{2,0},{3,7},{4,6},{5,1},{6,4},{7,3},{8,10},{9,13},{10,... | collective-permute-start | bytes 196616 | tf_op jit(solution)/shard_map/ppermute | solution.py:228
  99.6 6.1 %collective-permute-start.35 = (f32[256,128]{1,0:T(8,128)S(1)}, f32[256,128]{1,0:T(8,128)S(1)}, u32[]{:S(2)}, u32[]{:S(2)}) collective-permute-start(f32[256,128]{1,0:T(8,128)S(1)} %maximum_select_fusion.9), channel_id=1, source_target_pairs={{0,2},{1,5},{2,0},{3,7},{4,6},{5,1},{6,4},{7,3},{8,10},{9,13},{10,... | collective-permute-start | bytes 393224 | tf_op jit(solution)/shard_map/ppermute | solution.py:228
  99.7 6.3 %collective-permute-start.29 = (f32[256,128]{1,0:T(8,128)S(1)}, f32[256,128]{1,0:T(8,128)S(1)}, u32[]{:S(2)}, u32[]{:S(2)}) collective-permute-start(f32[256,128]{1,0:T(8,128)S(1)} %maximum_select_fusion.8), channel_id=1, source_target_pairs={{0,4},{1,3},{2,6},{3,1},{4,0},{5,7},{6,2},{7,5},{8,12},{9,11},{10,... | collective-permute-start | bytes 393224 | tf_op jit(solution)/shard_map/ppermute | solution.py:228
  101.6 4.4 %collective-permute-start.36 = (f32[384,128]{1,0:T(8,128)S(1)}, f32[384,128]{1,0:T(8,128)S(1)}, u32[]{:S(2)}, u32[]{:S(2)}) collective-permute-start(f32[384,128]{1,0:T(8,128)S(1)} %slice_select_fusion.1), channel_id=1, source_target_pairs={{0,1},{1,0},{2,3},{3,2},{4,5},{5,4},{6,7},{7,6},{8,9},{9,8},{10,11... | collective-permute-start | bytes 589832 | tf_op jit(solution)/shard_map/ppermute | solution.py:218
  107.3 24.5 %collective-permute-start.41 = (f32[384,128]{1,0:T(8,128)S(1)}, f32[384,128]{1,0:T(8,128)S(1)}, u32[]{:S(2)}, u32[]{:S(2)}) collective-permute-start(f32[384,128]{1,0:T(8,128)S(1)} %get-tuple-element.44), channel_id=1, source_target_pairs={{0,1},{1,0},{2,3},{3,2},{4,5},{5,4},{6,7},{7,6},{8,9},{9,8},{10,11... | collective-permute-start | bytes 589832 | tf_op jit(solution)/shard_map/ppermute | solution.py:218
  107.4 6.4 %collective-permute-start.42 = (f32[256,128]{1,0:T(8,128)S(1)}, f32[256,128]{1,0:T(8,128)S(1)}, u32[]{:S(2)}, u32[]{:S(2)}) collective-permute-start(f32[256,128]{1,0:T(8,128)S(1)} %constant_dynamic-slice_fusion.3), channel_id=1, source_target_pairs={{0,2},{1,5},{2,0},{3,7},{4,6},{5,1},{6,4},{7,3},{8,10},{9,13},{10,... | collective-permute-start | bytes 393224 | tf_op jit(solution)/shard_map/ppermute | solution.py:228
  108.1 5.7 %collective-permute-start.37 = (f32[264,128]{1,0:T(8,128)S(1)}, f32[264,128]{1,0:T(8,128)S(1)}, u32[]{:S(2)}, u32[]{:S(2)}) collective-permute-start(f32[264,128]{1,0:T(8,128)S(1)} %pad_maximum_fusion.2), channel_id=1, source_target_pairs={{0,4},{1,3},{2,6},{3,1},{4,0},{5,7},{6,2},{7,5},{8,12},{9,11},{10,... | collective-permute-start | bytes 405512 | tf_op jit(solution)/shard_map/ppermute | solution.py:228
  118.4 4.9 %collective-permute-start.39 = (f32[72,128]{1,0:T(8,128)S(1)}, f32[72,128]{1,0:T(8,128)S(1)}, u32[]{:S(2)}, u32[]{:S(2)}) collective-permute-start(f32[72,128]{1,0:T(8,128)S(1)} %pad_maximum_fusion.10), channel_id=1, source_target_pairs={{0,16},{1,17},{2,18},{3,19},{4,20},{5,21},{6,22},{7,23},{8,24},{9,... | collective-permute-start | bytes 110600 | tf_op jit(solution)/shard_map/ppermute | solution.py:228
  125.3 4.6 %collective-permute-start.45 = (f32[32,128]{1,0:T(8,128)S(1)}, f32[32,128]{1,0:T(8,128)S(1)}, u32[]{:S(2)}, u32[]{:S(2)}) collective-permute-start(f32[32,128]{1,0:T(8,128)S(1)} %constant_dynamic-slice_fusion), channel_id=1, source_target_pairs={{0,16},{1,17},{2,18},{3,19},{4,20},{5,21},{6,22},{7,23},{8,24},{9,... | collective-permute-start | bytes 49160 | tf_op jit(solution)/shard_map/ppermute | solution.py:228
  (31 other events, 159.6 us)

commit v4 on v0

v4 whole, which is shorter than its diff:
```python
import functools
import math

import jax
import jax.numpy as jnp
from jax import lax
from jax.experimental import pallas as pl
from jax.experimental.pallas import tpu as pltpu
from jax.sharding import PartitionSpec as P

step_size = 0.01
prior_prec = 8.0
item_prec = 1.0
weight_decay = 1.0
rate_scale = 0.04

CORES = 2
NN = (((1,), (0,)), ((), ()))
NT = (((1,), (1,)), ((), ()))
TN = (((0,), (0,)), ((), ()))
VMEM = pl.BlockSpec(memory_space=pltpu.VMEM)
SMEM = pl.BlockSpec(memory_space=pltpu.SMEM)
HBM = pl.BlockSpec(memory_space=pltpu.HBM)
ANY = pl.BlockSpec(memory_space=pl.ANY)
PARAMS = pltpu.CompilerParams(vmem_limit_bytes=8 << 20)
f32 = jnp.float32
bf16 = jnp.bfloat16


def dot(a, b, dims=NN):
    return lax.dot_general(a, b, dims, preferred_element_type=f32)


def shape(*dims, dtype=f32):
    return jax.ShapeDtypeStruct(dims, dtype)


def cost(flops, size):
    return pl.CostEstimate(flops=flops, bytes_accessed=size, transcendentals=0)


def half_of(ref, core):
    width = ref.shape[1] // CORES
    return ref[:, pl.ds(pl.multiple_of(core * width, width), width)]


def precision_of(stats):
    return (1.0 + stats[1:2, :] / 2.0) / (1.0 + stats[0:1, :] / 2.0)


def tile_kernel(stratum, noise_scale, core, codes, count, ratings, user_noise, item_noise, *refs):
    if stratum == 0:
        users_in, items_in = refs[:2]
        base_u, grad_u, pushed, stats = refs[2:6]
        refs = refs[6:]
    else:
        old_base, old_grad, own_mean, other_mean, old_stats, pulled = refs[:6]
        base_u, grad_u, pushed, stats, own_cols, other_cols = refs[6:12]
        refs = refs[12:]
    tiles, noise_u, noise_v, users, items, pred, err_b, sems = refs
    rows, rank = users.shape
    width = rank // CORES
    tile = tiles.shape[-1]
    grid = rows // tile
    copies = [
        pltpu.make_async_copy(source, target, sems.at[n])
        for n, (source, target) in enumerate(
            [
                (ratings.at[0, stratum], tiles),
                (user_noise.at[stratum], noise_u),
                (item_noise.at[stratum], noise_v),
            ]
            + ([(users_in, users), (items_in, items)] if stratum == 0 else [])
        )
    ]
    for copy in copies[::-1]:
        copy.start()
    if stratum == 0:
        copies[4].wait()
        copies[3].wait()
    else:
        precision = precision_of(old_stats[...])
        precision = jnp.concatenate([precision] * CORES, 1)
        items[...] = pulled[:rows, :] + precision * pulled[rows:, :]
        new = old_base[...] + precision * old_grad[...]
        here = core[0] == 0
        pull = step_size * prior_prec
        left = jnp.where(here, own_mean[...], other_mean[...])
        right = jnp.where(here, other_mean[...], own_mean[...])
        users[:, :width] = new[:, :width] + pull * left
        users[:, width:] = new[:, width:] + pull * right
        own_cols[...] = half_of(users, core[0])
        other_cols[...] = half_of(users, 1 - core[0])
    user_b = users[...].astype(bf16)
    item_b = items[...].astype(bf16)
    pred[...] = dot(user_b, item_b, NT)
    err_b[...] = jnp.zeros_like(err_b)
    live_slots = count[0, stratum]
    sse = jnp.zeros((tile, tile), f32)
    copies[0].wait()
    for slot in range(tiles.shape[0]):
        code = codes[0, stratum, slot]
        at_rows = pl.ds(pl.multiple_of(code // grid * tile, tile), tile)
        at_cols = pl.ds(pl.multiple_of(code % grid * tile, tile), tile)
        live = (slot < live_slots).astype(f32)
        err = (tiles[slot].astype(f32) - pred[at_rows, at_cols]) * live
        sse = sse + err * err
        err_b[at_rows, at_cols] = err.astype(bf16)
    err_all = err_b[...]
    total = jnp.sum(sse)
    counted = live_slots.astype(f32) * float(tile * tile)
    row = lax.broadcasted_iota(jnp.int32, stats.shape, 0)
    stats[...] = jnp.where(row == 0, total, jnp.where(row == 1, counted, 0.0))
    grad_u[...] = step_size * dot(err_all, item_b)
    pushed[rows:, :] = step_size * dot(err_all, user_b, TN)
    copies[2].wait()
    pushed[:rows, :] = (1.0 - step_size * item_prec) * items[...] + noise_scale * noise_v[
        ...
    ].astype(f32)
    copies[1].wait()
    base_u[...] = (1.0 - step_size * prior_prec) * users[...] + noise_scale * noise_u[...].astype(
        f32
    )


def tile_pass(stratum, core, codes, count, ratings, user_noise, item_noise, *state):
    slots, tile = ratings.shape[2:4]
    rows, rank = user_noise.shape[1:]
    noise_scale = math.sqrt(2.0 * step_size)
    width = rank // CORES
    outs = [shape(rows, rank), shape(rows, rank), shape(2 * rows, rank), shape(8, width)]
    if stratum:
        outs += [shape(rows, width)] * 2
    return pl.pallas_call(
        functools.partial(tile_kernel, stratum, noise_scale),
        out_shape=tuple(outs),
        in_specs=[SMEM] * 3 + [HBM] * 3 + [VMEM if stratum else HBM] * len(state),
        out_specs=(VMEM,) * len(outs),
        scratch_shapes=[
            pltpu.VMEM((slots, tile, tile), bf16),
            pltpu.VMEM((rows, rank), bf16),
            pltpu.VMEM((rows, rank), bf16),
            pltpu.VMEM((rows, rank), f32),
            pltpu.VMEM((rows, rank), f32),
            pltpu.VMEM((rows, rows), f32),
            pltpu.VMEM((rows, rows), bf16),
            pltpu.SemaphoreType.DMA((5,)),
        ],
        compiler_params=PARAMS,
        cost_estimate=cost(6 * rows * rows * rank, 16 * rows * rank),
        name="tile_pass",
    )(core, codes, count, ratings, user_noise, item_noise, *state)


def first_kernel(core, feats_in, weights_in, users_in, mean, send, keep, mine, wide, feats, weights, users, sems):
    copies = [
        pltpu.make_async_copy(source, target, sems.at[n])
        for n, (source, target) in enumerate(
            [(weights_in, weights), (feats_in, feats), (users_in, users)]
        )
    ]
    for copy in copies:
        copy.start()
    here = core[0]
    copies[0].wait()
    weights_b = weights[...].astype(bf16)
    copies[1].wait()
    mean[...] = dot(feats[...], weights_b)
    copies[2].wait()
    for ref, which in ((send, 1 - here), (keep, here)):
        offset = (half_of(users, which) - half_of(mean, which)).astype(bf16)
        ref[...] = dot(feats[...], offset, TN)
    mine[...] = half_of(weights, here)
    wide[...] = feats[...].astype(f32)


def first_pass(core, feats, weights, users):
    rows, rank = users.shape
    feat = weights.shape[0]
    width = rank // CORES
    return pl.pallas_call(
        first_kernel,
        out_shape=(shape(rows, rank),) + (shape(feat, width),) * 3 + (shape(rows, feat),),
        in_specs=[SMEM] + [HBM] * 3,
        out_specs=(VMEM,) * 5,
        scratch_shapes=[
            pltpu.VMEM(feats.shape, bf16),
            pltpu.VMEM(weights.shape, f32),
            pltpu.VMEM(users.shape, f32),
            pltpu.SemaphoreType.DMA((3,)),
        ],
        compiler_params=PARAMS,
        cost_estimate=cost(4 * rows * feat * rank, 8 * feat * rank),
        name="first_pass",
    )(core, feats, weights, users)


def join_kernel(own, other, both, sem):
    rows = other.shape[0]
    copy = pltpu.make_async_copy(own, both.at[:rows], sem.at[0])
    copy.start()
    both[rows:, :] = other[...].astype(bf16)
    copy.wait()


def join_pass(own, other):
    rows, feat = own.shape
    return pl.pallas_call(
        join_kernel,
        out_shape=shape(CORES * rows, feat, dtype=bf16),
        in_specs=[HBM, VMEM],
        out_specs=VMEM,
        scratch_shapes=[pltpu.SemaphoreType.DMA((1,))],
        compiler_params=PARAMS,
        name="join_pass",
    )(own, other)


def prior_kernel(places, place, feats, weights, own_cols, other_cols, stats, more_stats, own_mean, other_mean, send, keep, offset, *full):
    rows = own_cols.shape[0]
    half = keep.shape[0]
    mean = dot(feats[...], weights[...].astype(bf16))
    own_mean[...] = mean[:rows]
    other_mean[...] = mean[rows:]
    offset[:rows, :] = (own_cols[...] - mean[:rows]).astype(bf16)
    offset[rows:, :] = (other_cols[...] - mean[rows:]).astype(bf16)
    send[half:, :] = stats[...] + more_stats[...]
    core, bit = place[0], place[1]
    if places is None:
        for ref, which in ((send, 1 - bit), (keep, bit)):
            at = pl.ds(pl.multiple_of(which * half, half), half)
            ref[:half, :] = dot(feats[:, at], offset[...], TN)
        return
    full = full[0]
    full[...] = dot(feats[...], offset[...], TN)
    blocks = len(places[0])
    block = 2 * half // blocks
    for ref, which in ((send, 1 - bit), (keep, bit)):
        for n in range(blocks // 2):
            source = jnp.int32(0)
            for c, order in enumerate(places):
                for b in range(2):
                    source = jnp.where((core == c) & (which == b), order[b * blocks // 2 + n], source)
            source = source * block
            if block % 8 == 0:
                source = pl.multiple_of(source, block)
            ref[n * block : (n + 1) * block, :] = full[pl.ds(source, block), :]


def prior_pass(place, feats, weights, own_cols, other_cols, stats, more_stats, places=None):
    rows, width = own_cols.shape
    feat = weights.shape[0]
    return pl.pallas_call(
        functools.partial(prior_kernel, places),
        out_shape=(
            shape(rows, width),
            shape(rows, width),
            shape(feat // 2 + stats.shape[0], width),
            shape(feat // 2, width),
        ),
        in_specs=[SMEM] + [VMEM] * 6,
        out_specs=(VMEM,) * 4,
        scratch_shapes=[pltpu.VMEM((CORES * rows, width), bf16)]
        + ([] if places is None else [pltpu.VMEM((feat, width), f32)]),
        compiler_params=PARAMS,
        cost_estimate=cost(8 * rows * feat * width, 8 * rows * feat),
        name="prior_pass",
    )(place, feats, weights, own_cols, other_cols, stats, more_stats)


def update_kernel(rate, start, part, got, stats, weights, later, new, new_stats):
    rows = part.shape[0]
    old = weights[pl.ds(pl.multiple_of(start[0], rows), rows), :]
    total = part[...] + got[:rows, :]
    new[...] = old + rate * (prior_prec * total - weight_decay * old)
    new_stats[...] = stats[...] + got[rows:, :]


def update_pass(rate, start, part, got, stats, weights, later):
    return pl.pallas_call(
        functools.partial(update_kernel, rate),
        out_shape=(shape(*part.shape), shape(*stats.shape)),
        in_specs=[SMEM] + [VMEM] * 4 + [ANY],
        out_specs=(VMEM,) * 2,
        compiler_params=PARAMS,
        cost_estimate=cost(4 * part.size, 16 * part.size),
        name="update_pass",
    )(start, part, got, stats, weights, later)


def bit_order(devices, core):
    bits = devices.bit_length() - 1
    far = list(range(3, bits))
    return [1, 2] + far if core == 0 else [2, 1] + far[::-1]


def swap(array, devices):
    return lax.ppermute(array, "user", [(i, i ^ 1) for i in range(devices)])


def roll(array, devices):
    return lax.ppermute(array, "user", [(i, (i + 1) % devices) for i in range(devices)])


def exchange(array, devices, stage):
    orders = [bit_order(devices, core) for core in range(CORES)]
    pairs = [(i, i ^ (1 << orders[i & 1][stage])) for i in range(devices)]
    return lax.ppermute(array, "user", pairs)


def final_places(devices):
    bits = devices.bit_length() - 1
    return [
        [
            sum(
                ((place >> (bits - 2 - n)) & 1) << (bit - 1)
                for n, bit in enumerate(bit_order(devices, core))
            )
            for place in range(devices // 2)
        ]
        for core in range(CORES)
    ]


def local(
    ratings,
    tile_index,
    tile_count,
    side_features,
    user_factors,
    item_factors,
    prior_weights,
    user_noise,
    item_noise,
):
    devices = lax.axis_size("user")
    own = lax.axis_index("user")
    stages = devices.bit_length() - 2
    strata = ratings.shape[1]
    rows_dev = user_factors.shape[0]
    feat = prior_weights.shape[0]
    feat_rows = feat // devices
    rate = rate_scale / (rows_dev * devices)
    core = own & 1

    def my_bit(stage):
        zero, one = (bit_order(devices, c)[stage] for c in range(CORES))
        return jnp.where(core == 0, own >> zero, own >> one) & 1

    def across(mine, other):
        return jnp.where(
            core == 0, jnp.concatenate([mine, other], 1), jnp.concatenate([other, mine], 1)
        )

    def add(send, keep, stage, rider):
        got = exchange(jnp.concatenate([send, rider], 0), devices, stage)
        return keep + got[: keep.shape[0]], rider + got[keep.shape[0] :]

    def halve(array, stage, rider):
        half = array.shape[0] // 2
        bit = my_bit(stage)
        send = lax.dynamic_slice_in_dim(array, (1 - bit) * half, half, 0)
        keep = lax.dynamic_slice_in_dim(array, bit * half, half, 0)
        return add(send, keep, stage, rider)

    def gather(array, stage):
        got = exchange(array, devices, stage)
        return jnp.where(
            my_bit(stage) == 0,
            jnp.concatenate([array, got], 0),
            jnp.concatenate([got, array], 0),
        )

    core_ref = core.reshape(1)
    place = jnp.stack([core, my_bit(0)])
    tables = (core_ref, tile_index, tile_count, ratings, user_noise, item_noise)
    mean, send, part, weights, wide = first_pass(
        core_ref, side_features, prior_weights, user_factors
    )
    width = weights.shape[1]
    part = part + swap(send, devices)
    base, grad, pushed, stats = tile_pass(0, *tables, user_factors, item_factors)
    stats = stats + swap(stats, devices)
    part, stats = halve(part, 0, stats)
    feats = join_pass(side_features, swap(wide, devices))
    own_mean = jnp.where(core == 0, mean[:, :width], mean[:, width:])
    other_mean = jnp.where(core == 0, mean[:, width:], mean[:, :width])
    for stratum in range(strata):
        last = stratum + 1 == strata
        pulled = pushed if last else roll(pushed, devices)
        for stage in range(1, stages if last else stages - 1):
            if stage < 2 or last:
                part, stats = halve(part, stage, stats)
            else:
                part, stats = add(part, part, stage, stats)
        if last:
            start = (own >> 1) * (CORES * feat_rows)
            old = lax.dynamic_slice_in_dim(weights, start, part.shape[0], 0)
            part = old + rate * (prior_prec * part - weight_decay * old)
            break
        start = my_bit(0) * (feat // 2) + my_bit(1) * (feat // 4)
        got = exchange(jnp.concatenate([part, stats], 0), devices, stages - 1)
        part, stats = update_pass(rate, start.reshape(1), part, got, stats, weights, pulled)
        base, grad, pushed, new_stats, own_cols, other_cols = tile_pass(
            stratum + 1, *tables, base, grad, own_mean, other_mean, stats, pulled
        )
        more_stats = swap(new_stats, devices)
        other_cols = swap(other_cols, devices)
        for stage in (1, 0):
            part = gather(part, stage)
        weights = part
        own_mean, other_mean, send, keep = prior_pass(
            place,
            feats,
            weights,
            own_cols,
            other_cols,
            new_stats,
            more_stats,
            final_places(devices) if stratum + 2 == strata else None,
        )
        other_mean = swap(other_mean, devices)
        got = exchange(send, devices, 0)
        part = keep + got[: keep.shape[0]]
        stats = send[keep.shape[0] :] + got[keep.shape[0] :]
    precision = precision_of(stats)
    precision = jnp.concatenate([precision] * CORES, 1)
    items = pulled[:rows_dev] + precision * pulled[rows_dev:]
    users = base + precision * grad + (step_size * prior_prec) * across(own_mean, other_mean)
    first, second = part[:feat_rows], part[feat_rows:]
    rows = across(
        jnp.where(core == 0, first, second), swap(jnp.where(core == 0, second, first), devices)
    )
    return (users, items, rows)


def solution(mesh):
    return jax.shard_map(
        local,
        mesh=mesh,
        in_specs=(
            P("user", None, None, None, None),
            P("user", None, None),
            P("user", None),
            P("user", None),
            P("user", None),
            P("user", None),
            P(),
            P(None, "user", None),
            P(None, "user", None),
        ),
        out_specs=(P("user", None), P("user", None), P("user", None)),
        check_vma=False,
    )
```

time: 502 us -> 135 us (0.27)
  waiting for transfers between devices: 232 us -> 86.7 us
  blocking collectives: 121 us -> 0 us
  loops' own time: 58.4 us -> 0 us
  matrix products: 38 us -> 0 us
  between operations: 19.8 us -> 1.25 us
  Pallas kernels: 0 us -> 15.9 us
  starting transfers between devices: 0.13 us -> 14.7 us
  other arithmetic: 15.2 us -> 7.74 us
  local copies, waits for them, and re-layouts: 15.3 us -> 8.18 us
    psum x3 -> x0, waiting for transfers between devices: 226 us -> none  [local(): total = lax.psum(grad_w, 'user')]
    psum x3 -> x0, blocking collectives: 121 us -> none  [local(): total_sse, total_count = lax.psum((sse, count_here), 'user')]
    ppermute x2 -> x28, waiting for transfers between devices: 6.47 us -> 86.7 us  [the longest x16 63 us: exchange(): return lax.ppermute(array, 'user', pairs)]
    another operation x3 -> x0, loops' own time: 58.4 us -> none  [tile_pass(): return lax.fori_loop(0, slots, one, start)]
    dot_general x60 -> x0, matrix products: 38 us -> none  [the longest x18 23.7 us: one(): lax.dot_general(user_tile, item_tile, (((1,), (1,)), ((), ())), preferred...]
    pallas_call x0 -> x9, Pallas kernels: none -> 15.9 us  [the longest x3 7.2 us: tile_pass(): pl.pallas_call(functools.partial(tile_kernel, stratum, noise_scale), out_...]
    ppermute x2 -> x28, starting transfers between devices: 0.01 us -> 14.7 us  [the longest x16 12.7 us: exchange(): return lax.ppermute(array, 'user', pairs)]
    dynamic_slice x18 -> x6, local copies, waits for them, and re-layouts: 10.6 us -> 0.1 us  [halve(): send = lax.dynamic_slice_in_dim(array, (1 - bit) * half, half, 0)]
  transfers between devices with their start and end apart: 5 -> 28, of which waited for: 4 -> 18; matrix products, arithmetic and copies ran while one was open for 9% -> 3% of each run, Pallas kernels for 0% -> 7%
where the time goes in v4:
time: 135 us; the launch traced here: 134 us
  waiting for transfers between devices  86.7 us (64%)
  Pallas kernels  15.9 us (12%)
  starting transfers between devices  14.7 us (11%)
  local copies, waits for them, and re-layouts  8.18 us (6%)
  other arithmetic  7.74 us (6%)
    ppermute x16, waiting for transfers between devices, exchange(): return lax.ppermute(array, 'user', pairs)  63 us
    ppermute x2, waiting for transfers between devices, roll(): lax.ppermute(array, 'user', [(i, (i + 1) % devices) for i in range(device...  22.4 us
    ppermute x16, starting transfers between devices, exchange(): return lax.ppermute(array, 'user', pairs)  12.7 us
    unnamed x37, local copies, waits for them, and re-layouts  8.08 us
    pallas_call x3, Pallas kernels, tile_pass(): pl.pallas_call(functools.partial(tile_kernel, stratum, noise_scale), out_...  7.2 us
    pallas_call x2, Pallas kernels, prior_pass(): pl.pallas_call(functools.partial(prior_kernel, places), out_shape=(shape(...  4.72 us
  transfers between devices with their start and end apart: 28, of which 18 were waited for; matrix products, arithmetic and copies ran while one was open for 3% of the time, Pallas kernels for 7%

profile of v4, /device:TPU:0, one launch (start us, length us, event | category | flops | bytes accessed | tf_op | source)
XLA Modules:
  0.0 134.4 jit_solution(4719465591275275574)
XLA Ops:
  0.7 1.2 copy-done.3
  2.9 1.2 copy-done.7
  4.2 1.7 %first_pass.1 = (f32[384,256]{1,0:T(8,128)S(1)}, f32[1024,128]{1,0:T(8,128)S(1)}, f32[1024,128]{1,0:T(8,128)S(1)}, f32[1024,128]{1,0:T(8,128)S(1)}, f32[384,1024]{1,0:T(8,128)S(1)}) custom-call(s32[1]{0:T(128)} %bitcast.core, bf16[384,1024]{1,0:T(8,128)(2,1)S(1)} %copy-done.3, f32[1024,256]{1,0:T(8,128)S(1)} %copy-done.7, f32[384,256]{1,0:T(8,128)S(1)} %copy-done.5), custom_call_target="tpu_custom_call" | custom-call | flops 402653184 | bytes 2097152 | tf_op jit(solution)/shard_map/first_pass/pallas_call | solution.py:181
  5.9 1.2 copy-done.15
  8.6 2.6 %tile_pass.3 = (f32[384,256]{1,0:T(8,128)S(1)}, f32[384,256]{1,0:T(8,128)S(1)}, f32[768,256]{1,0:T(8,128)S(1)}, f32[8,128]{1,0:T(8,128)S(1)}) custom-call(s32[1]{0:T(128)} %bitcast.core, s32[1,3,6]{2,1,0:T(4,128)S(1)} %copy.14.codes, s32[1,3]{1,0:T(1,128)S(1)} %copy-done.14, bf16[1,3,6,128,128]{4,3,2,1,0:T(8,128)(2,1)S(1)} %copy-done, ...), custom_call_target="tpu_custom_call" | custom-call | flops 226492416 | bytes 1572864 | tf_op jit(solution)/shard_map/tile_pass/pallas_call | solution.py:134
  13.7 1.1 collective-permute-done.1
  14.8 1.1 add.120
  16.7 2.7 %collective-permute-start.2 = (f32[520,128]{1,0:T(8,128)}, f32[520,128]{1,0:T(8,128)}, u32[]{:S(2)}, u32[]{:S(2)}) collective-permute-start(f32[520,128]{1,0:T(8,128)} %pad_maximum_fusion), channel_id=1, source_target_pairs={{0,2},{1,5},{2,0},{3,7},{4,6},{5,1},{6,4},{7,3},{8,10},{9,13},{10,... | collective-permute-start | bytes 798728 | tf_op jit(solution)/shard_map/ppermute | solution.py:308
  19.3 4.7 %collective-permute-done.2 = f32[520,128]{1,0:T(8,128)} collective-permute-done((f32[520,128]{1,0:T(8,128)}, f32[520,128]{1,0:T(8,128)}, u32[]{:S(2)}, u32[]{:S(2)}) %collective-permute-start.2) | collective-permute-done | bytes 266272 | tf_op jit(solution)/shard_map/ppermute | solution.py:308
  25.7 2.1 %collective-permute-start.3 = (f32[264,128]{1,0:T(8,128)S(1)}, f32[264,128]{1,0:T(8,128)S(1)}, u32[]{:S(2)}, u32[]{:S(2)}) collective-permute-start(f32[264,128]{1,0:T(8,128)S(1)} %pad_maximum_fusion.1), channel_id=1, source_target_pairs={{0,4},{1,3},{2,6},{3,1},{4,0},{5,7},{6,2},{7,5},{8,12},{9,11},{10,... | collective-permute-start | bytes 405512 | tf_op jit(solution)/shard_map/ppermute | solution.py:308
  27.9 3.0 %collective-permute-done.3 = f32[264,128]{1,0:T(8,128)S(1)} collective-permute-done((f32[264,128]{1,0:T(8,128)S(1)}, f32[264,128]{1,0:T(8,128)S(1)}, u32[]{:S(2)}, u32[]{:S(2)}) %collective-permute-start.3) | collective-permute-done | bytes 135200 | tf_op jit(solution)/shard_map/ppermute | solution.py:308
  30.9 2.1 %collective-permute-start.4 = (f32[264,128]{1,0:T(8,128)S(1)}, f32[264,128]{1,0:T(8,128)S(1)}, u32[]{:S(2)}, u32[]{:S(2)}) collective-permute-start(f32[264,128]{1,0:T(8,128)S(1)} %pad_maximum_fusion.2), channel_id=1, source_target_pairs={{0,8},{1,17},{2,10},{3,19},{4,12},{5,21},{6,14},{7,23},{8,0},{9,25... | collective-permute-start | bytes 405512 | tf_op jit(solution)/shard_map/ppermute | solution.py:308
  33.0 3.4 %collective-permute-done.4 = f32[264,128]{1,0:T(8,128)S(1)} collective-permute-done((f32[264,128]{1,0:T(8,128)S(1)}, f32[264,128]{1,0:T(8,128)S(1)}, u32[]{:S(2)}, u32[]{:S(2)}) %collective-permute-start.4) | collective-permute-done | bytes 135200 | tf_op jit(solution)/shard_map/ppermute | solution.py:308
  36.5 2.8 %collective-permute-start.5 = (f32[264,128]{1,0:T(8,128)S(1)}, f32[264,128]{1,0:T(8,128)S(1)}, u32[]{:S(2)}, u32[]{:S(2)}) collective-permute-start(f32[264,128]{1,0:T(8,128)S(1)} %pad_maximum_fusion.3), channel_id=1, source_target_pairs={{0,16},{1,9},{2,18},{3,11},{4,20},{5,13},{6,22},{7,15},{8,24},{9,1... | collective-permute-start | bytes 405512 | tf_op jit(solution)/shard_map/ppermute | solution.py:308
  39.3 11.1 %collective-permute-done.6.later.refs_5_ = f32[768,256]{1,0:T(8,128)S(1)} collective-permute-done((f32[768,256]{1,0:T(8,128)}, f32[768,256]{1,0:T(8,128)S(1)}, u32[]{:S(2)}, u32[]{:S(2)}) %collective-permute-start.6) | collective-permute-done | bytes 786464 | tf_op jit(solution)/shard_map/ppermute | solution.py:302
  51.1 6.5 %collective-permute-done.8 = f32[256,128]{1,0:T(8,128)S(1)} collective-permute-done((f32[256,128]{1,0:T(8,128)}, f32[256,128]{1,0:T(8,128)S(1)}, u32[]{:S(2)}, u32[]{:S(2)}) %collective-permute-start.8) | collective-permute-done | bytes 131104 | tf_op jit(solution)/shard_map/ppermute | solution.py:308
  59.8 2.3 %tile_pass.4 = (f32[384,256]{1,0:T(8,128)S(1)}, f32[384,256]{1,0:T(8,128)S(1)}, f32[768,256]{1,0:T(8,128)S(1)}, f32[8,128]{1,0:T(8,128)S(1)}, f32[384,128]{1,0:T(8,128)S(1)}, /*index=5*/f32[384,128]{1,0:T(8,128)S(1)}) custom-call(s32[1]{0:T(128)} %bitcast.core, s32[1,3,6]{2,1,0:T(4,128)S(1)} %copy.14.codes, s32[1,3]{1,0:T(1,128)S(1)} %copy-done.14, ...), custom_call_target="tpu_custom_call" | custom-call | flops 226492416 | bytes 1572864 | tf_op jit(solution)/shard_map/tile_pass/pallas_call | solution.py:134
  62.7 1.5 %join_pass.1.feats = bf16[768,1024]{1,0:T(8,128)(2,1)S(1)} custom-call(bf16[384,1024]{1,0:T(8,128)(2,1)S(1)} %copy-done.4, f32[384,1024]{1,0:T(8,128)} %collective-permute-done.7.other), custom_call_target="tpu_custom_call" | custom-call | tf_op jit(solution)/shard_map/join_pass/pallas_call | solution.py:208
  65.1 2.3 %prior_pass.2 = (f32[384,128]{1,0:T(8,128)S(1)}, f32[384,128]{1,0:T(8,128)S(1)}, f32[520,128]{1,0:T(8,128)S(1)}, f32[512,128]{1,0:T(8,128)S(1)}) custom-call(s32[2]{0:T(128)S(1)} %pad_add_fusion.place, bf16[768,1024]{1,0:T(8,128)(2,1)S(1)} %join_pass.1.feats, f32[1024,128]{1,0:T(8,128)S(1)} %maximum_select_fusion.weights, ...), custom_call_target="tpu_custom_call" | custom-call | flops 402653184 | bytes 3145728 | tf_op jit(solution)/shard_map/prior_pass/pallas_call | solution.py:253
  67.5 1.3 collective-permute-start.13
  68.8 5.1 %collective-permute-done.13 = f32[520,128]{1,0:T(8,128)S(1)} collective-permute-done((f32[520,128]{1,0:T(8,128)S(1)}, f32[520,128]{1,0:T(8,128)S(1)}, u32[]{:S(2)}, u32[]{:S(2)}) %collective-permute-start.13) | collective-permute-done | bytes 266272 | tf_op jit(solution)/shard_map/ppermute | solution.py:308
  74.8 4.3 %collective-permute-done.14 = f32[264,128]{1,0:T(8,128)S(1)} collective-permute-done((f32[264,128]{1,0:T(8,128)S(1)}, f32[264,128]{1,0:T(8,128)S(1)}, u32[]{:S(2)}, u32[]{:S(2)}) %collective-permute-start.14) | collective-permute-done | bytes 135200 | tf_op jit(solution)/shard_map/ppermute | solution.py:308
  79.3 4.9 %collective-permute-done.15 = f32[264,128]{1,0:T(8,128)S(1)} collective-permute-done((f32[264,128]{1,0:T(8,128)S(1)}, f32[264,128]{1,0:T(8,128)S(1)}, u32[]{:S(2)}, u32[]{:S(2)}) %collective-permute-start.15) | collective-permute-done | bytes 135200 | tf_op jit(solution)/shard_map/ppermute | solution.py:308
  84.5 11.4 %collective-permute-done.17.later.refs_5_ = f32[768,256]{1,0:T(8,128)S(1)} collective-permute-done((f32[768,256]{1,0:T(8,128)S(1)}, f32[768,256]{1,0:T(8,128)S(1)}, u32[]{:S(2)}, u32[]{:S(2)}) %collective-permute-start.17) | collective-permute-done | bytes 786464 | tf_op jit(solution)/shard_map/ppermute | solution.py:302
  96.1 6.3 %collective-permute-done.18 = f32[256,128]{1,0:T(8,128)S(1)} collective-permute-done((f32[256,128]{1,0:T(8,128)S(1)}, f32[256,128]{1,0:T(8,128)S(1)}, u32[]{:S(2)}, u32[]{:S(2)}) %collective-permute-start.18) | collective-permute-done | bytes 131104 | tf_op jit(solution)/shard_map/ppermute | solution.py:308
  102.5 2.3 %tile_pass.5 = (f32[384,256]{1,0:T(8,128)S(1)}, f32[384,256]{1,0:T(8,128)S(1)}, f32[768,256]{1,0:T(8,128)S(1)}, f32[8,128]{1,0:T(8,128)S(1)}, f32[384,128]{1,0:T(8,128)S(1)}, /*index=5*/f32[384,128]{1,0:T(8,128)S(1)}) custom-call(s32[1]{0:T(128)} %bitcast.core, s32[1,3,6]{2,1,0:T(4,128)S(1)} %copy.14.codes, s32[1,3]{1,0:T(1,128)S(1)} %copy-done.14, ...), custom_call_target="tpu_custom_call" | custom-call | flops 226492416 | bytes 1572864 | tf_op jit(solution)/shard_map/tile_pass/pallas_call | solution.py:134
  105.4 3.5 %collective-permute-done.19 = f32[512,128]{1,0:T(8,128)S(1)} collective-permute-done((f32[512,128]{1,0:T(8,128)S(1)}, f32[512,128]{1,0:T(8,128)S(1)}, u32[]{:S(2)}, u32[]{:S(2)}) %collective-permute-start.19) | collective-permute-done | bytes 262176 | tf_op jit(solution)/shard_map/ppermute | solution.py:308
  108.9 2.4 %prior_pass.3 = (f32[384,128]{1,0:T(8,128)S(1)}, f32[384,128]{1,0:T(8,128)S(1)}, f32[520,128]{1,0:T(8,128)S(1)}, f32[512,128]{1,0:T(8,128)S(1)}) custom-call(s32[2]{0:T(128)S(1)} %pad_add_fusion.place, bf16[768,1024]{1,0:T(8,128)(2,1)S(1)} %join_pass.1.feats, f32[1024,128]{1,0:T(8,128)S(1)} %maximum_select_fusion.1.weights, ...), custom_call_target="tpu_custom_call" | custom-call | flops 402653184 | bytes 3145728 | tf_op jit(solution)/shard_map/prior_pass/pallas_call | solution.py:253
  111.4 6.5 %collective-permute-done.22 = f32[520,128]{1,0:T(8,128)S(1)} collective-permute-done((f32[520,128]{1,0:T(8,128)S(1)}, f32[520,128]{1,0:T(8,128)S(1)}, u32[]{:S(2)}, u32[]{:S(2)}) %collective-permute-start.22) | collective-permute-done | bytes 266272 | tf_op jit(solution)/shard_map/ppermute | solution.py:308
  118.1 5.0 %collective-permute-done.23 = f32[264,128]{1,0:T(8,128)S(1)} collective-permute-done((f32[264,128]{1,0:T(8,128)S(1)}, f32[264,128]{1,0:T(8,128)S(1)}, u32[]{:S(2)}, u32[]{:S(2)}) %collective-permute-start.23) | collective-permute-done | bytes 135200 | tf_op jit(solution)/shard_map/ppermute | solution.py:308
  123.2 4.3 %collective-permute-done.24 = f32[136,128]{1,0:T(8,128)S(1)} collective-permute-done((f32[136,128]{1,0:T(8,128)S(1)}, f32[136,128]{1,0:T(8,128)S(1)}, u32[]{:S(2)}, u32[]{:S(2)}) %collective-permute-start.24) | collective-permute-done | bytes 69664 | tf_op jit(solution)/shard_map/ppermute | solution.py:308
  127.7 4.8 %collective-permute-done.25 = f32[72,128]{1,0:T(8,128)S(1)} collective-permute-done((f32[72,128]{1,0:T(8,128)S(1)}, f32[72,128]{1,0:T(8,128)S(1)}, u32[]{:S(2)}, u32[]{:S(2)}) %collective-permute-start.25) | collective-permute-done | bytes 36896 | tf_op jit(solution)/shard_map/ppermute | solution.py:308
  (119 shorter events, 16.3 us)
Async XLA Ops:
  0.6 6.9 %copy-start = (bf16[1,3,6,128,128]{4,3,2,1,0:T(8,128)(2,1)S(1)}, bf16[1,3,6,128,128]{4,3,2,1,0:T(8,128)(2,1)}, u32[]{:S(2)}) copy-start(bf16[1,3,6,128,128]{4,3,2,1,0:T(8,128)(2,1)} %ratings.5) | copy-start | bytes 1769476
  0.6 6.9 %copy-start.1 = (bf16[3,384,256]{2,1,0:T(8,128)(2,1)S(1)}, bf16[3,384,256]{2,1,0:T(8,128)(2,1)}, u32[]{:S(2)}) copy-start(bf16[3,384,256]{2,1,0:T(8,128)(2,1)} %user_noise.5) | copy-start | bytes 1769476
  7.1 7.7 %collective-permute-start = (f32[1024,128]{1,0:T(8,128)S(1)}, f32[1024,128]{1,0:T(8,128)}, u32[]{:S(2)}, u32[]{:S(2)}) collective-permute-start(f32[1024,128]{1,0:T(8,128)S(1)} %get-tuple-element.40), channel_id=1, source_target_pairs={{0,1},{1,0},{2,3},{3,2},{4,5},{5,4},{6,7},{7,6},{8,9},{9,8},{10,11... | collective-permute-start | bytes 1572872 | tf_op jit(solution)/shard_map/ppermute | solution.py:298
  13.6 1.2 collective-permute-start.1
  16.7 7.4 %collective-permute-start.2 = (f32[520,128]{1,0:T(8,128)}, f32[520,128]{1,0:T(8,128)}, u32[]{:S(2)}, u32[]{:S(2)}) collective-permute-start(f32[520,128]{1,0:T(8,128)} %pad_maximum_fusion), channel_id=1, source_target_pairs={{0,2},{1,5},{2,0},{3,7},{4,6},{5,1},{6,4},{7,3},{8,10},{9,13},{10,... | collective-permute-start | bytes 798728 | tf_op jit(solution)/shard_map/ppermute | solution.py:308
  25.7 5.1 %collective-permute-start.3 = (f32[264,128]{1,0:T(8,128)S(1)}, f32[264,128]{1,0:T(8,128)S(1)}, u32[]{:S(2)}, u32[]{:S(2)}) collective-permute-start(f32[264,128]{1,0:T(8,128)S(1)} %pad_maximum_fusion.1), channel_id=1, source_target_pairs={{0,4},{1,3},{2,6},{3,1},{4,0},{5,7},{6,2},{7,5},{8,12},{9,11},{10,... | collective-permute-start | bytes 405512 | tf_op jit(solution)/shard_map/ppermute | solution.py:308
  27.9 34.9 %collective-permute-start.7 = (f32[384,1024]{1,0:T(8,128)}, f32[384,1024]{1,0:T(8,128)}, u32[]{:S(2)}, u32[]{:S(2)}) collective-permute-start(f32[384,1024]{1,0:T(8,128)} %copy-done.15), channel_id=1, source_target_pairs={{0,1},{1,0},{2,3},{3,2},{4,5},{5,4},{6,7},{7,6},{8,9},{9,8},{10,11... | collective-permute-start | bytes 4718600 | tf_op jit(solution)/shard_map/ppermute | solution.py:298
  30.9 5.5 %collective-permute-start.4 = (f32[264,128]{1,0:T(8,128)S(1)}, f32[264,128]{1,0:T(8,128)S(1)}, u32[]{:S(2)}, u32[]{:S(2)}) collective-permute-start(f32[264,128]{1,0:T(8,128)S(1)} %pad_maximum_fusion.2), channel_id=1, source_target_pairs={{0,8},{1,17},{2,10},{3,19},{4,12},{5,21},{6,14},{7,23},{8,0},{9,25... | collective-permute-start | bytes 405512 | tf_op jit(solution)/shard_map/ppermute | solution.py:308
  33.0 17.4 %collective-permute-start.6 = (f32[768,256]{1,0:T(8,128)}, f32[768,256]{1,0:T(8,128)S(1)}, u32[]{:S(2)}, u32[]{:S(2)}) collective-permute-start(f32[768,256]{1,0:T(8,128)} %copy-done.16), channel_id=1, source_target_pairs={{0,1},{1,2},{2,3},{3,4},{4,5},{5,6},{6,7},{7,8},{8,9},{9,10},{10,1... | collective-permute-start | bytes 2359304 | tf_op jit(solution)/shard_map/ppermute | solution.py:302
  36.5 13.9 %collective-permute-start.5 = (f32[264,128]{1,0:T(8,128)S(1)}, f32[264,128]{1,0:T(8,128)S(1)}, u32[]{:S(2)}, u32[]{:S(2)}) collective-permute-start(f32[264,128]{1,0:T(8,128)S(1)} %pad_maximum_fusion.3), channel_id=1, source_target_pairs={{0,16},{1,9},{2,18},{3,11},{4,20},{5,13},{6,22},{7,15},{8,24},{9,1... | collective-permute-start | bytes 405512 | tf_op jit(solution)/shard_map/ppermute | solution.py:308
  51.1 8.7 %copy-start.9 = (f32[384,256]{1,0:T(8,128)S(1)}, f32[384,256]{1,0:T(8,128)}, u32[]{:S(2)}) copy-start(f32[384,256]{1,0:T(8,128)} %copy-done.8) | copy-start | bytes 1179652
  51.1 8.7 %copy-start.11 = (f32[384,256]{1,0:T(8,128)S(1)}, f32[384,256]{1,0:T(8,128)}, u32[]{:S(2)}) copy-start(f32[384,256]{1,0:T(8,128)} %copy-done.10) | copy-start | bytes 1179652
  51.1 6.5 %collective-permute-start.8 = (f32[256,128]{1,0:T(8,128)}, f32[256,128]{1,0:T(8,128)S(1)}, u32[]{:S(2)}, u32[]{:S(2)}) collective-permute-start(f32[256,128]{1,0:T(8,128)} %get-tuple-element.48), channel_id=1, source_target_pairs={{0,4},{1,3},{2,6},{3,1},{4,0},{5,7},{6,2},{7,5},{8,12},{9,11},{10,... | collective-permute-start | bytes 393224 | tf_op jit(solution)/shard_map/ppermute | solution.py:308
  58.6 6.4 %collective-permute-start.9 = (f32[512,128]{1,0:T(8,128)S(1)}, f32[512,128]{1,0:T(8,128)S(1)}, u32[]{:S(2)}, u32[]{:S(2)}) collective-permute-start(f32[512,128]{1,0:T(8,128)S(1)} %maximum_select_fusion.3), channel_id=1, source_target_pairs={{0,2},{1,5},{2,0},{3,7},{4,6},{5,1},{6,4},{7,3},{8,10},{9,13},{10,... | collective-permute-start | bytes 786440 | tf_op jit(solution)/shard_map/ppermute | solution.py:308
  62.1 3.0 %collective-permute-start.10 = (f32[384,128]{1,0:T(8,128)S(1)}, f32[384,128]{1,0:T(8,128)S(1)}, u32[]{:S(2)}, u32[]{:S(2)}) collective-permute-start(f32[384,128]{1,0:T(8,128)S(1)} %get-tuple-element.50), channel_id=1, source_target_pairs={{0,1},{1,0},{2,3},{3,2},{4,5},{5,4},{6,7},{7,6},{8,9},{9,8},{10,11... | collective-permute-start | bytes 589832 | tf_op jit(solution)/shard_map/ppermute | solution.py:298
  62.2 2.9 %collective-permute-start.11 = (f32[8,128]{1,0:T(8,128)S(1)}, f32[8,128]{1,0:T(8,128)S(1)}, u32[]{:S(2)}, u32[]{:S(2)}) collective-permute-start(f32[8,128]{1,0:T(8,128)S(1)} %get-tuple-element.51.stats), channel_id=1, source_target_pairs={{0,1},{1,0},{2,3},{3,2},{4,5},{5,4},{6,7},{7,6},{8,9},{9,8},{10,11... | collective-permute-start | bytes 12296 | tf_op jit(solution)/shard_map/ppermute | solution.py:298
  67.5 6.5 %collective-permute-start.13 = (f32[520,128]{1,0:T(8,128)S(1)}, f32[520,128]{1,0:T(8,128)S(1)}, u32[]{:S(2)}, u32[]{:S(2)}) collective-permute-start(f32[520,128]{1,0:T(8,128)S(1)} %get-tuple-element.55), channel_id=1, source_target_pairs={{0,2},{1,5},{2,0},{3,7},{4,6},{5,1},{6,4},{7,3},{8,10},{9,13},{10,... | collective-permute-start | bytes 798728 | tf_op jit(solution)/shard_map/ppermute | solution.py:308
  74.0 5.1 %collective-permute-start.14 = (f32[264,128]{1,0:T(8,128)S(1)}, f32[264,128]{1,0:T(8,128)S(1)}, u32[]{:S(2)}, u32[]{:S(2)}) collective-permute-start(f32[264,128]{1,0:T(8,128)S(1)} %pad_maximum_fusion.4), channel_id=1, source_target_pairs={{0,4},{1,3},{2,6},{3,1},{4,0},{5,7},{6,2},{7,5},{8,12},{9,11},{10,... | collective-permute-start | bytes 405512 | tf_op jit(solution)/shard_map/ppermute | solution.py:308
  79.2 5.1 %collective-permute-start.15 = (f32[264,128]{1,0:T(8,128)S(1)}, f32[264,128]{1,0:T(8,128)S(1)}, u32[]{:S(2)}, u32[]{:S(2)}) collective-permute-start(f32[264,128]{1,0:T(8,128)S(1)} %pad_maximum_fusion.5), channel_id=1, source_target_pairs={{0,8},{1,17},{2,10},{3,19},{4,12},{5,21},{6,14},{7,23},{8,0},{9,25... | collective-permute-start | bytes 405512 | tf_op jit(solution)/shard_map/ppermute | solution.py:308
  79.2 16.7 %collective-permute-start.17 = (f32[768,256]{1,0:T(8,128)S(1)}, f32[768,256]{1,0:T(8,128)S(1)}, u32[]{:S(2)}, u32[]{:S(2)}) collective-permute-start(f32[768,256]{1,0:T(8,128)S(1)} %get-tuple-element.56), channel_id=1, source_target_pairs={{0,1},{1,2},{2,3},{3,4},{4,5},{5,6},{6,7},{7,8},{8,9},{9,10},{10,1... | collective-permute-start | bytes 2359304 | tf_op jit(solution)/shard_map/ppermute | solution.py:302
  84.3 11.6 %collective-permute-start.16 = (f32[264,128]{1,0:T(8,128)S(1)}, f32[264,128]{1,0:T(8,128)S(1)}, u32[]{:S(2)}, u32[]{:S(2)}) collective-permute-start(f32[264,128]{1,0:T(8,128)S(1)} %pad_maximum_fusion.6), channel_id=1, source_target_pairs={{0,16},{1,9},{2,18},{3,11},{4,20},{5,13},{6,22},{7,15},{8,24},{9,1... | collective-permute-start | bytes 405512 | tf_op jit(solution)/shard_map/ppermute | solution.py:308
  95.9 6.4 %collective-permute-start.18 = (f32[256,128]{1,0:T(8,128)S(1)}, f32[256,128]{1,0:T(8,128)S(1)}, u32[]{:S(2)}, u32[]{:S(2)}) collective-permute-start(f32[256,128]{1,0:T(8,128)S(1)} %get-tuple-element.59), channel_id=1, source_target_pairs={{0,4},{1,3},{2,6},{3,1},{4,0},{5,7},{6,2},{7,5},{8,12},{9,11},{10,... | collective-permute-start | bytes 393224 | tf_op jit(solution)/shard_map/ppermute | solution.py:308
  96.0 6.5 %collective-permute-start.12 = (f32[384,128]{1,0:T(8,128)S(1)}, f32[384,128]{1,0:T(8,128)S(1)}, u32[]{:S(2)}, u32[]{:S(2)}) collective-permute-start(f32[384,128]{1,0:T(8,128)S(1)} %get-tuple-element.53), channel_id=1, source_target_pairs={{0,1},{1,0},{2,3},{3,2},{4,5},{5,4},{6,7},{7,6},{8,9},{9,8},{10,11... | collective-permute-start | bytes 589832 | tf_op jit(solution)/shard_map/ppermute | solution.py:298
  102.4 6.4 %collective-permute-start.19 = (f32[512,128]{1,0:T(8,128)S(1)}, f32[512,128]{1,0:T(8,128)S(1)}, u32[]{:S(2)}, u32[]{:S(2)}) collective-permute-start(f32[512,128]{1,0:T(8,128)S(1)} %maximum_select_fusion.4), channel_id=1, source_target_pairs={{0,2},{1,5},{2,0},{3,7},{4,6},{5,1},{6,4},{7,3},{8,10},{9,13},{10,... | collective-permute-start | bytes 786440 | tf_op jit(solution)/shard_map/ppermute | solution.py:308
  104.8 4.1 %collective-permute-start.20 = (f32[384,128]{1,0:T(8,128)S(1)}, f32[384,128]{1,0:T(8,128)S(1)}, u32[]{:S(2)}, u32[]{:S(2)}) collective-permute-start(f32[384,128]{1,0:T(8,128)S(1)} %get-tuple-element.61), channel_id=1, source_target_pairs={{0,1},{1,0},{2,3},{3,2},{4,5},{5,4},{6,7},{7,6},{8,9},{9,8},{10,11... | collective-permute-start | bytes 589832 | tf_op jit(solution)/shard_map/ppermute | solution.py:298
  104.9 4.0 %collective-permute-start.21 = (f32[8,128]{1,0:T(8,128)S(1)}, f32[8,128]{1,0:T(8,128)S(1)}, u32[]{:S(2)}, u32[]{:S(2)}) collective-permute-start(f32[8,128]{1,0:T(8,128)S(1)} %get-tuple-element.62.stats), channel_id=1, source_target_pairs={{0,1},{1,0},{2,3},{3,2},{4,5},{5,4},{6,7},{7,6},{8,9},{9,8},{10,11... | collective-permute-start | bytes 12296 | tf_op jit(solution)/shard_map/ppermute | solution.py:298
  111.3 6.6 %collective-permute-start.22 = (f32[520,128]{1,0:T(8,128)S(1)}, f32[520,128]{1,0:T(8,128)S(1)}, u32[]{:S(2)}, u32[]{:S(2)}) collective-permute-start(f32[520,128]{1,0:T(8,128)S(1)} %get-tuple-element.63), channel_id=1, source_target_pairs={{0,2},{1,5},{2,0},{3,7},{4,6},{5,1},{6,4},{7,3},{8,10},{9,13},{10,... | collective-permute-start | bytes 798728 | tf_op jit(solution)/shard_map/ppermute | solution.py:308
  118.0 5.1 %collective-permute-start.23 = (f32[264,128]{1,0:T(8,128)S(1)}, f32[264,128]{1,0:T(8,128)S(1)}, u32[]{:S(2)}, u32[]{:S(2)}) collective-permute-start(f32[264,128]{1,0:T(8,128)S(1)} %pad_maximum_fusion.7), channel_id=1, source_target_pairs={{0,4},{1,3},{2,6},{3,1},{4,0},{5,7},{6,2},{7,5},{8,12},{9,11},{10,... | collective-permute-start | bytes 405512 | tf_op jit(solution)/shard_map/ppermute | solution.py:308
  123.1 4.4 %collective-permute-start.24 = (f32[136,128]{1,0:T(8,128)S(1)}, f32[136,128]{1,0:T(8,128)S(1)}, u32[]{:S(2)}, u32[]{:S(2)}) collective-permute-start(f32[136,128]{1,0:T(8,128)S(1)} %pad_maximum_fusion.8), channel_id=1, source_target_pairs={{0,8},{1,17},{2,10},{3,19},{4,12},{5,21},{6,14},{7,23},{8,0},{9,25... | collective-permute-start | bytes 208904 | tf_op jit(solution)/shard_map/ppermute | solution.py:308
  127.6 4.9 %collective-permute-start.25 = (f32[72,128]{1,0:T(8,128)S(1)}, f32[72,128]{1,0:T(8,128)S(1)}, u32[]{:S(2)}, u32[]{:S(2)}) collective-permute-start(f32[72,128]{1,0:T(8,128)S(1)} %pad_maximum_fusion.9), channel_id=1, source_target_pairs={{0,16},{1,9},{2,18},{3,11},{4,20},{5,13},{6,22},{7,15},{8,24},{9,1... | collective-permute-start | bytes 110600 | tf_op jit(solution)/shard_map/ppermute | solution.py:308
  127.7 5.0 %collective-permute-start.26 = (f32[384,128]{1,0:T(8,128)S(1)}, f32[384,128]{1,0:T(8,128)S(1)}, u32[]{:S(2)}, u32[]{:S(2)}) collective-permute-start(f32[384,128]{1,0:T(8,128)S(1)} %get-tuple-element.67), channel_id=1, source_target_pairs={{0,1},{1,0},{2,3},{3,2},{4,5},{5,4},{6,7},{7,6},{8,9},{9,8},{10,11... | collective-permute-start | bytes 589832 | tf_op jit(solution)/shard_map/ppermute | solution.py:298
  132.6 1.2 collective-permute-start.27
  (14 other events, 32.2 us)

commit v5 on v4

v5 whole, which is shorter than its diff:
```python
import functools
import math

import jax
import jax.numpy as jnp
from jax import lax
from jax.experimental import pallas as pl
from jax.experimental.pallas import tpu as pltpu
from jax.sharding import PartitionSpec as P

step_size = 0.01
prior_prec = 8.0
item_prec = 1.0
weight_decay = 1.0
rate_scale = 0.04

CORES = 2
RIDERS = 8
NN = (((1,), (0,)), ((), ()))
NT = (((1,), (1,)), ((), ()))
TN = (((0,), (0,)), ((), ()))
VMEM = pl.BlockSpec(memory_space=pltpu.VMEM)
SMEM = pl.BlockSpec(memory_space=pltpu.SMEM)
HBM = pl.BlockSpec(memory_space=pltpu.HBM)
ANY = pl.BlockSpec(memory_space=pl.ANY)
PARAMS = pltpu.CompilerParams(vmem_limit_bytes=8 << 20)
f32 = jnp.float32
bf16 = jnp.bfloat16


def dot(a, b, dims=NN):
    return lax.dot_general(a, b, dims, preferred_element_type=f32)


def shape(*dims, dtype=f32):
    return jax.ShapeDtypeStruct(dims, dtype)


def cost(flops, size):
    return pl.CostEstimate(flops=flops, bytes_accessed=size, transcendentals=0)


def half_of(ref, core):
    width = ref.shape[1] // CORES
    return ref[:, pl.ds(pl.multiple_of(core * width, width), width)]


def precision_of(stats):
    return (1.0 + stats[1:2, :] / 2.0) / (1.0 + stats[0:1, :] / 2.0)


def tile_kernel(stratum, noise_scale, place, codes, count, ratings, user_noise, item_noise, *refs):
    if stratum == 0:
        users_in, items_in = refs[:2]
        base_u, grad_u, base_v, grad_v, stats = refs[2:7]
        refs = refs[7:]
    else:
        old_base, old_grad, own_mean, other_mean, old_stats, old_base_v, old_grad_v = refs[:7]
        base_u, grad_u, base_v, grad_v, stats, own_cols, other_cols = refs[7:14]
        refs = refs[14:]
    tiles, noise_u, noise_v, users, items, pred, err_b, sems = refs
    rows, rank = users.shape
    width = rank // CORES
    tile = tiles.shape[-1]
    grid = rows // tile
    copies = [
        pltpu.make_async_copy(source, target, sems.at[n])
        for n, (source, target) in enumerate(
            [
                (ratings.at[0, stratum], tiles),
                (user_noise.at[stratum], noise_u),
                (item_noise.at[stratum], noise_v),
            ]
            + ([(users_in, users), (items_in, items)] if stratum == 0 else [])
        )
    ]
    for copy in copies[::-1]:
        copy.start()
    if stratum == 0:
        copies[4].wait()
        copies[3].wait()
    else:
        precision = precision_of(old_stats[...])
        precision = jnp.concatenate([precision] * CORES, 1)
        items[...] = old_base_v[...] + precision * old_grad_v[...]
        new = old_base[...] + precision * old_grad[...]
        here = place[0] == 0
        pull = step_size * prior_prec
        left = jnp.where(here, own_mean[...], other_mean[...])
        right = jnp.where(here, other_mean[...], own_mean[...])
        users[:, :width] = new[:, :width] + pull * left
        users[:, width:] = new[:, width:] + pull * right
        own_cols[...] = half_of(users, place[0])
        other_cols[...] = half_of(users, 1 - place[0])
    user_b = users[...].astype(bf16)
    item_b = items[...].astype(bf16)
    pred[...] = dot(user_b, item_b, NT)
    err_b[...] = jnp.zeros_like(err_b)
    live_slots = count[0, stratum]
    sse = jnp.zeros((tile, tile), f32)
    copies[0].wait()
    for slot in range(tiles.shape[0]):
        code = codes[0, stratum, slot]
        at_rows = pl.ds(pl.multiple_of(code // grid * tile, tile), tile)
        at_cols = pl.ds(pl.multiple_of(code % grid * tile, tile), tile)
        live = (slot < live_slots).astype(f32)
        err = (tiles[slot].astype(f32) - pred[at_rows, at_cols]) * live
        sse = sse + err * err
        err_b[at_rows, at_cols] = err.astype(bf16)
    err_all = err_b[...]
    total = jnp.sum(sse)
    counted = live_slots.astype(f32) * float(tile * tile)
    row = lax.broadcasted_iota(jnp.int32, stats.shape, 0)
    stats[...] = jnp.where(row == 0, total, jnp.where(row == 1, counted, 0.0))
    grad_u[...] = step_size * dot(err_all, item_b)
    grad_v[...] = step_size * dot(err_all, user_b, TN)
    copies[2].wait()
    base_v[...] = (1.0 - step_size * item_prec) * items[...] + noise_scale * noise_v[...].astype(
        f32
    )
    copies[1].wait()
    base_u[...] = (1.0 - step_size * prior_prec) * users[...] + noise_scale * noise_u[...].astype(
        f32
    )


def tile_pass(stratum, place, codes, count, ratings, user_noise, item_noise, *state):
    slots, tile = ratings.shape[2:4]
    rows, rank = user_noise.shape[1:]
    noise_scale = math.sqrt(2.0 * step_size)
    width = rank // CORES
    outs = [shape(rows, rank)] * 4 + [shape(RIDERS, width)]
    if stratum:
        outs += [shape(rows, width)] * 2
    return pl.pallas_call(
        functools.partial(tile_kernel, stratum, noise_scale),
        out_shape=tuple(outs),
        in_specs=[SMEM] * 3 + [HBM] * 3 + [VMEM if stratum else HBM] * len(state),
        out_specs=(VMEM,) * len(outs),
        scratch_shapes=[
            pltpu.VMEM((slots, tile, tile), bf16),
            pltpu.VMEM((rows, rank), bf16),
            pltpu.VMEM((rows, rank), bf16),
            pltpu.VMEM((rows, rank), f32),
            pltpu.VMEM((rows, rank), f32),
            pltpu.VMEM((rows, rows), f32),
            pltpu.VMEM((rows, rows), bf16),
            pltpu.SemaphoreType.DMA((5,)),
        ],
        compiler_params=PARAMS,
        cost_estimate=cost(6 * rows * rows * rank, 16 * rows * rank),
        name="tile_pass",
    )(place, codes, count, ratings, user_noise, item_noise, *state)


def first_kernel(place, feats_in, weights_in, users_in, own_mean, other_mean, send, keep, old, mean, feats, weights, users, sems):
    copies = [
        pltpu.make_async_copy(source, target, sems.at[n])
        for n, (source, target) in enumerate(
            [(weights_in, weights), (feats_in, feats), (users_in, users)]
        )
    ]
    for copy in copies:
        copy.start()
    here = place[0]
    copies[0].wait()
    weights_b = weights[...].astype(bf16)
    copies[1].wait()
    mean[...] = dot(feats[...], weights_b)
    copies[2].wait()
    for grad, means, which in ((send, other_mean, 1 - here), (keep, own_mean, here)):
        mean_now = half_of(mean, which)
        means[...] = mean_now
        offset = (half_of(users, which) - mean_now).astype(bf16)
        grad[...] = dot(feats[...], offset, TN)
    rows, width = old.shape
    start = place[1] * (weights.shape[0] // 2) + place[2] * rows
    cols = pl.ds(pl.multiple_of(here * width, width), width)
    old[...] = weights[pl.ds(pl.multiple_of(start, rows), rows), cols]


def first_pass(place, feats, weights, users):
    rows, rank = users.shape
    feat = weights.shape[0]
    width = rank // CORES
    return pl.pallas_call(
        first_kernel,
        out_shape=(shape(rows, width),) * 2 + (shape(feat, width),) * 2 + (shape(feat // 4, width),),
        in_specs=[SMEM] + [HBM] * 3,
        out_specs=(VMEM,) * 5,
        scratch_shapes=[
            pltpu.VMEM(users.shape, f32),
            pltpu.VMEM(feats.shape, bf16),
            pltpu.VMEM(weights.shape, f32),
            pltpu.VMEM(users.shape, f32),
            pltpu.SemaphoreType.DMA((3,)),
        ],
        compiler_params=PARAMS,
        cost_estimate=cost(4 * rows * feat * rank, 8 * feat * rank),
        name="first_pass",
    )(place, feats, weights, users)


def widen_kernel(narrow_in, wide, narrow, sem):
    copy = pltpu.make_async_copy(narrow_in, narrow, sem.at[0])
    copy.start()
    copy.wait()
    wide[...] = narrow[...].astype(f32)


def widen_pass(narrow):
    return pl.pallas_call(
        widen_kernel,
        out_shape=shape(*narrow.shape),
        in_specs=[HBM],
        out_specs=VMEM,
        scratch_shapes=[pltpu.VMEM(narrow.shape, bf16), pltpu.SemaphoreType.DMA((1,))],
        compiler_params=PARAMS,
        name="widen_pass",
    )(narrow)


def join_kernel(own, other, both, sem):
    rows = other.shape[0]
    copy = pltpu.make_async_copy(own, both.at[:rows], sem.at[0])
    copy.start()
    both[rows:, :] = other[...].astype(bf16)
    copy.wait()


def join_pass(own, other):
    rows, feat = own.shape
    return pl.pallas_call(
        join_kernel,
        out_shape=shape(CORES * rows, feat, dtype=bf16),
        in_specs=[HBM, VMEM],
        out_specs=VMEM,
        scratch_shapes=[pltpu.SemaphoreType.DMA((1,))],
        compiler_params=PARAMS,
        name="join_pass",
    )(own, other)


def prior_kernel(places, place, feats, part, got, own_cols, other_cols, stats, more_stats, own_mean, other_mean, send, keep, *refs):
    rows = own_cols.shape[0]
    half = keep.shape[0]
    core, bit = place[0], place[1]
    here = pl.ds(pl.multiple_of(bit * half, half), half)
    there = pl.ds(pl.multiple_of((1 - bit) * half, half), half)
    offset = refs[-1]
    mean = dot(feats[:, here], part[...].astype(bf16)) + dot(feats[:, there], got[...].astype(bf16))
    own_mean[...] = mean[:rows]
    other_mean[...] = mean[rows:]
    offset[:rows, :] = (own_cols[...] - mean[:rows]).astype(bf16)
    offset[rows:, :] = (other_cols[...] - mean[rows:]).astype(bf16)
    send[half:, :] = stats[...] + more_stats[...]
    if places is None:
        send[:half, :] = dot(feats[:, there], offset[...], TN)
        keep[...] = dot(feats[:, here], offset[...], TN)
        return
    old, full = refs[:2]
    full[here, :] = part[...]
    full[there, :] = got[...]
    start = place[place.shape[0] - 1] * old.shape[0]
    if old.shape[0] % 8 == 0:
        start = pl.multiple_of(start, old.shape[0])
    old[...] = full[pl.ds(start, old.shape[0]), :]
    full[...] = dot(feats[...], offset[...], TN)
    blocks = len(places[0])
    block = 2 * half // blocks
    for ref, which in ((send, 1 - bit), (keep, bit)):
        for n in range(blocks // 2):
            source = jnp.int32(0)
            for c, order in enumerate(places):
                for b in range(2):
                    source = jnp.where((core == c) & (which == b), order[b * blocks // 2 + n], source)
            source = source * block
            if block % 8 == 0:
                source = pl.multiple_of(source, block)
            ref[n * block : (n + 1) * block, :] = full[pl.ds(source, block), :]


def prior_pass(place, feats, part, got, own_cols, other_cols, stats, more_stats, places=None):
    rows, width = own_cols.shape
    half = part.shape[0]
    outs = [shape(rows, width)] * 2 + [shape(half + stats.shape[0], width), shape(half, width)]
    scratch = [pltpu.VMEM((CORES * rows, width), bf16)]
    if places is not None:
        outs.append(shape(2 * half // len(places[0]), width))
        scratch.insert(0, pltpu.VMEM((2 * half, width), f32))
    return pl.pallas_call(
        functools.partial(prior_kernel, places),
        out_shape=tuple(outs),
        in_specs=[SMEM] + [VMEM] * 7,
        out_specs=(VMEM,) * len(outs),
        scratch_shapes=scratch,
        compiler_params=PARAMS,
        cost_estimate=cost(16 * rows * half * width, 16 * rows * half),
        name="prior_pass",
    )(place, feats, part, got, own_cols, other_cols, stats, more_stats)


def step_kernel(halving, slot, place, held, got, sent, more, *refs):
    send = refs[-2] if halving else refs[-1]
    riders = sent.shape[0] - RIDERS, more.shape[0] - RIDERS
    rider = sent[riders[0] :, :] + more[riders[1] :, :]
    rows = send.shape[0] - RIDERS
    if halving:
        bit = place[slot]
        for ref, which in ((send, 1 - bit), (refs[-1], bit)):
            at = pl.ds(pl.multiple_of(which * rows, 8), rows) if rows % 8 == 0 else pl.ds(which * rows, rows)
            ref[:rows, :] = held[at, :] + got[at, :]
    else:
        send[:rows, :] = held[:rows, :] + got[:rows, :]
    send[rows:, :] = rider


def step_pass(halving, stage, place, held, got, sent, more, rows, later=()):
    width = held.shape[1]
    outs = [shape(rows // 2 + RIDERS, width), shape(rows // 2, width)] if halving else [shape(rows + RIDERS, width)]
    return pl.pallas_call(
        functools.partial(step_kernel, halving, 1 + stage),
        out_shape=tuple(outs),
        in_specs=[SMEM] + [VMEM] * 4 + [ANY] * len(later),
        out_specs=(VMEM,) * len(outs),
        compiler_params=PARAMS,
        cost_estimate=cost(rows * width, 12 * rows * width),
        name="step_pass",
    )(place, held, got, sent, more, *later)


def update_kernel(rate, held, got, sent, old, *refs):
    new, stats = refs[-2:]
    rows = old.shape[0]
    total = held[:rows, :] + got[:rows, :]
    before = old[...]
    new[...] = before + rate * (prior_prec * total - weight_decay * before)
    stats[...] = sent[sent.shape[0] - RIDERS :, :] + got[rows:, :]


def update_pass(rate, held, got, sent, old, later=()):
    return pl.pallas_call(
        functools.partial(update_kernel, rate),
        out_shape=(shape(*old.shape), shape(RIDERS, old.shape[1])),
        in_specs=[VMEM] * 4 + [ANY] * len(later),
        out_specs=(VMEM,) * 2,
        compiler_params=PARAMS,
        cost_estimate=cost(4 * old.size, 16 * old.size),
        name="update_pass",
    )(held, got, sent, old, *later)


def gather_kernel(slot, place, part, got, both):
    rows = part.shape[0]
    bit = place[slot]
    both[pl.ds(pl.multiple_of(bit * rows, rows), rows), :] = part[...]
    both[pl.ds(pl.multiple_of((1 - bit) * rows, rows), rows), :] = got[...]


def gather_pass(stage, place, part, got):
    rows, width = part.shape
    return pl.pallas_call(
        functools.partial(gather_kernel, 1 + stage),
        out_shape=shape(2 * rows, width),
        in_specs=[SMEM, VMEM, VMEM],
        out_specs=VMEM,
        compiler_params=PARAMS,
        cost_estimate=cost(rows * width, 16 * rows * width),
        name="gather_pass",
    )(place, part, got)


def split_kernel(place, both, mine, other):
    rows = mine.shape[0]
    for ref, which in ((mine, place[0]), (other, 1 - place[0])):
        at = pl.ds(pl.multiple_of(which * rows, 8), rows) if rows % 8 == 0 else pl.ds(which * rows, rows)
        ref[...] = both[at, :]


def split_pass(place, both):
    rows, width = both.shape
    return pl.pallas_call(
        split_kernel,
        out_shape=(shape(rows // CORES, width),) * 2,
        in_specs=[SMEM, VMEM],
        out_specs=(VMEM,) * 2,
        compiler_params=PARAMS,
        name="split_pass",
    )(place, both)


def across_kernel(place, mine, other, both):
    width = mine.shape[1]
    both[:, pl.ds(pl.multiple_of(place[0] * width, width), width)] = mine[...]
    both[:, pl.ds(pl.multiple_of((1 - place[0]) * width, width), width)] = other[...]


def across_pass(place, mine, other):
    rows, width = mine.shape
    return pl.pallas_call(
        across_kernel,
        out_shape=shape(rows, CORES * width),
        in_specs=[SMEM, VMEM, VMEM],
        out_specs=VMEM,
        compiler_params=PARAMS,
        name="across_pass",
    )(place, mine, other)


def last_kernel(place, stats, base, grad, own_mean, other_mean, base_v, grad_v, users, items):
    width = own_mean.shape[1]
    precision = precision_of(stats[...])
    precision = jnp.concatenate([precision] * CORES, 1)
    items[...] = base_v[...] + precision * grad_v[...]
    users[...] = base[...] + precision * grad[...]
    pull = step_size * prior_prec
    for mean, which in ((own_mean, place[0]), (other_mean, 1 - place[0])):
        at = pl.ds(pl.multiple_of(which * width, width), width)
        users[:, at] = users[:, at] + pull * mean[...]


def last_pass(place, stats, base, *state):
    return pl.pallas_call(
        last_kernel,
        out_shape=(shape(*base.shape),) * 2,
        in_specs=[SMEM] + [VMEM] * 7,
        out_specs=(VMEM,) * 2,
        compiler_params=PARAMS,
        cost_estimate=cost(8 * base.size, 32 * base.size),
        name="last_pass",
    )(place, stats, base, *state)


def bit_order(devices, core):
    bits = devices.bit_length() - 1
    far = list(range(3, bits))
    return [1, 2] + far if core == 0 else [2, 1] + far[::-1]


def swap(array, devices):
    return lax.ppermute(array, "user", [(i, i ^ 1) for i in range(devices)])


def roll(array, devices):
    return lax.ppermute(array, "user", [(i, (i + 1) % devices) for i in range(devices)])


def exchange(array, devices, stage):
    orders = [bit_order(devices, core) for core in range(CORES)]
    pairs = [(i, i ^ (1 << orders[i & 1][stage])) for i in range(devices)]
    return lax.ppermute(array, "user", pairs)


def final_places(devices):
    bits = devices.bit_length() - 1
    return [
        [
            sum(
                ((place >> (bits - 2 - n)) & 1) << (bit - 1)
                for n, bit in enumerate(bit_order(devices, core))
            )
            for place in range(devices // 2)
        ]
        for core in range(CORES)
    ]


def local(
    ratings,
    tile_index,
    tile_count,
    side_features,
    user_factors,
    item_factors,
    prior_weights,
    user_noise,
    item_noise,
):
    devices = lax.axis_size("user")
    own = lax.axis_index("user")
    stages = devices.bit_length() - 2
    strata = ratings.shape[1]
    feat = prior_weights.shape[0]
    rate = rate_scale / (user_factors.shape[0] * devices)
    core = own & 1
    zero, one = (bit_order(devices, c) for c in range(CORES))
    bits = [jnp.where(core == 0, own >> z, own >> o) & 1 for z, o in zip(zero, one, strict=True)]
    place = jnp.stack([core, *bits, own >> 1])
    tables = (place, tile_index, tile_count, ratings, user_noise, item_noise)

    own_mean, other_mean, send, held, old = first_pass(
        place, side_features, prior_weights, user_factors
    )
    got = swap(send, devices)
    base, grad, base_v, grad_v, stats = tile_pass(0, *tables, user_factors, item_factors)
    more = swap(stats, devices)
    send, held = step_pass(True, 0, place, held, got, stats, more, feat)
    feats = join_pass(side_features, swap(widen_pass(side_features), devices))
    for stratum in range(strata):
        last = stratum + 1 == strata
        if not last:
            base_v, grad_v = roll(base_v, devices), roll(grad_v, devices)
        got = exchange(send, devices, 0)
        send, held = step_pass(True, 1, place, held, got, send, got, feat // 2)
        for stage in range(1, stages - 1):
            got = exchange(send, devices, stage)
            rows = got.shape[0] - RIDERS
            if last:
                send, held = step_pass(True, stage + 1, place, held, got, send, got, rows)
            else:
                later = (base_v, grad_v) if stage == 2 else ()
                (send,) = step_pass(False, 0, place, held, got, send, got, rows, later)
                held = send
        got = exchange(send, devices, stages - 1)
        part, stats = update_pass(rate, held, got, send, old)
        if last:
            break
        old = part
        got = exchange(part, devices, 1)
        part = gather_pass(1, place, part, got)
        got = exchange(part, devices, 0)
        base, grad, base_v, grad_v, stats, own_cols, other_cols = tile_pass(
            stratum + 1, *tables, base, grad, own_mean, other_mean, stats, base_v, grad_v
        )
        more = swap(stats, devices)
        other_cols = swap(other_cols, devices)
        outs = prior_pass(
            place,
            feats,
            part,
            got,
            own_cols,
            other_cols,
            stats,
            more,
            final_places(devices) if stratum + 2 == strata else None,
        )
        own_mean, other_mean, send, held = outs[:4]
        if len(outs) > 4:
            old = outs[4]
        other_mean = swap(other_mean, devices)
    mine, other = split_pass(place, part)
    got = swap(other, devices)
    users, items = last_pass(place, stats, base, grad, own_mean, other_mean, base_v, grad_v)
    return (users, items, across_pass(place, mine, got))


def solution(mesh):
    return jax.shard_map(
        local,
        mesh=mesh,
        in_specs=(
            P("user", None, None, None, None),
            P("user", None, None),
            P("user", None),
            P("user", None),
            P("user", None),
            P("user", None),
            P(),
            P(None, "user", None),
            P(None, "user", None),
        ),
        out_specs=(P("user", None), P("user", None), P("user", None)),
        check_vma=False,
    )
```

time: 135 us -> 142 us (1.052)
  starting transfers between devices: 14.7 us -> 38.1 us
  waiting for transfers between devices: 86.7 us -> 73.7 us
  Pallas kernels: 15.9 us -> 24.7 us
  other arithmetic: 7.74 us -> 0 us
  local copies, waits for them, and re-layouts: 8.18 us -> 4.13 us
    ppermute x2 -> x4, waiting for transfers between devices: 22.4 us -> 0.01 us  [roll(): lax.ppermute(array, 'user', [(i, (i + 1) % devices) for i in range(device...]
    ppermute x16, starting transfers between devices: 12.7 us -> 34.5 us  [exchange(): return lax.ppermute(array, 'user', pairs)]
    pallas_call x3 -> x19, Pallas kernels: 6.45 us -> 17.1 us  [the longest x10 5.68 us: step_pass(): pl.pallas_call(functools.partial(step_kernel, halving, 1 + stage), out_sh...]
    ppermute x16, waiting for transfers between devices: 63 us -> 71.2 us  [exchange(): return lax.ppermute(array, 'user', pairs)]
    add x23 -> x0, other arithmetic: 4.05 us -> none  [the longest x15 1.79 us: add(): return (keep + got[:keep.shape[0]], rider + got[keep.shape[0]:])]
    unnamed x37 -> x23, local copies, waits for them, and re-layouts: 8.08 us -> 4.05 us
    select_n x7 -> x0, other arithmetic: 2.78 us -> none  [the longest x4 1.11 us: gather(): jnp.where(my_bit(stage) == 0, jnp.concatenate([array, got], 0), jnp.conca...]
  transfers between devices with their start and end apart: 28 -> 30, of which waited for: 18 -> 19; matrix products, arithmetic and copies ran while one was open for 3% -> 0% of each run, Pallas kernels for 7% -> 11%
where the time goes in v5:
time: 142 us
  waiting for transfers between devices  73.7 us (52%)
  starting transfers between devices  38.1 us (27%)
  Pallas kernels  24.7 us (17%)
  local copies, waits for them, and re-layouts  4.13 us (3%)
    ppermute x16, waiting for transfers between devices, exchange(): return lax.ppermute(array, 'user', pairs)  71.2 us
    ppermute x16, starting transfers between devices, exchange(): return lax.ppermute(array, 'user', pairs)  34.5 us
    pallas_call x3, Pallas kernels, tile_pass(): pl.pallas_call(functools.partial(tile_kernel, stratum, noise_scale), out_...  7.34 us
    pallas_call x10, Pallas kernels, step_pass(): pl.pallas_call(functools.partial(step_kernel, halving, 1 + stage), out_sh...  5.68 us
    pallas_call x2, Pallas kernels, prior_pass(): pl.pallas_call(functools.partial(prior_kernel, places), out_shape=tuple(o...  4.71 us
    unnamed x23, local copies, waits for them, and re-layouts  4.05 us
  transfers between devices with their start and end apart: 30, of which 19 were waited for; matrix products, arithmetic and copies ran while one was open for 0% of the time, Pallas kernels for 11%

profile of v5, /device:TPU:0, one launch (start us, length us, event | category | flops | bytes accessed | tf_op | source)
XLA Modules:
  0.0 141.5 jit_solution(7529899643896365372)
XLA Ops:
  4.1 2.2 %first_pass.1 = (f32[384,128]{1,0:T(8,128)S(1)}, f32[384,128]{1,0:T(8,128)S(1)}, f32[1024,128]{1,0:T(8,128)S(1)}, f32[1024,128]{1,0:T(8,128)S(1)}, f32[256,128]{1,0:T(8,128)S(1)}) custom-call(s32[6]{0:T(128)S(1)} %stack.27.place, bf16[384,1024]{1,0:T(8,128)(2,1)S(1)} %copy-done, f32[1024,256]{1,0:T(8,128)S(1)} %copy-done.7, f32[384,256]{1,0:T(8,128)S(1)} %copy-done.5), custom_call_target="tpu_custom_call" | custom-call | flops 402653184 | bytes 2097152 | tf_op jit(solution)/shard_map/first_pass/pallas_call | solution.py:186
  7.8 2.6 %tile_pass.3 = (f32[384,256]{1,0:T(8,128)S(1)}, f32[384,256]{1,0:T(8,128)S(1)}, f32[384,256]{1,0:T(8,128)S(1)}, f32[384,256]{1,0:T(8,128)S(1)}, f32[8,128]{1,0:T(8,128)S(1)}) custom-call(s32[6]{0:T(128)S(1)} %stack.27.place, s32[1,3,6]{2,1,0:T(4,128)S(1)} %copy.12.codes, s32[1,3]{1,0:T(1,128)S(1)} %copy-done.9, bf16[1,3,6,128,128]{4,3,2,1,0:T(8,128)(2,1)S(1)} %copy-done.2, ...), custom_call_target="tpu_custom_call" | custom-call | flops 226492416 | bytes 1572864 | tf_op jit(solution)/shard_map/tile_pass/pallas_call | solution.py:135
  12.4 2.9 %collective-permute-start.3 = (f32[520,128]{1,0:T(8,128)S(1)}, f32[520,128]{1,0:T(8,128)S(1)}, u32[]{:S(2)}, u32[]{:S(2)}) collective-permute-start(f32[520,128]{1,0:T(8,128)S(1)} %get-tuple-element.62.sent), channel_id=1, source_target_pairs={{0,2},{1,5},{2,0},{3,7},{4,6},{5,1},{6,4},{7,3},{8,10},{9,13},{10,... | collective-permute-start | bytes 798728 | tf_op jit(solution)/shard_map/ppermute | solution.py:451
  15.5 6.5 %collective-permute-done.3.got.more = f32[520,128]{1,0:T(8,128)S(1)} collective-permute-done((f32[520,128]{1,0:T(8,128)S(1)}, f32[520,128]{1,0:T(8,128)S(1)}, u32[]{:S(2)}, u32[]{:S(2)}) %collective-permute-start.3) | collective-permute-done | bytes 266272 | tf_op jit(solution)/shard_map/ppermute | solution.py:451
  22.6 1.7 %collective-permute-start.4 = (f32[264,128]{1,0:T(8,128)S(1)}, f32[264,128]{1,0:T(8,128)S(1)}, u32[]{:S(2)}, u32[]{:S(2)}) collective-permute-start(f32[264,128]{1,0:T(8,128)S(1)} %get-tuple-element.64.sent), channel_id=1, source_target_pairs={{0,4},{1,3},{2,6},{3,1},{4,0},{5,7},{6,2},{7,5},{8,12},{9,11},{10,... | collective-permute-start | bytes 405512 | tf_op jit(solution)/shard_map/ppermute | solution.py:451
  24.2 7.6 %collective-permute-done.4.got.more = f32[264,128]{1,0:T(8,128)S(1)} collective-permute-done((f32[264,128]{1,0:T(8,128)S(1)}, f32[264,128]{1,0:T(8,128)S(1)}, u32[]{:S(2)}, u32[]{:S(2)}) %collective-permute-start.4) | collective-permute-done | bytes 135200 | tf_op jit(solution)/shard_map/ppermute | solution.py:451
  32.4 4.5 %collective-permute-start.5 = (f32[264,128]{1,0:T(8,128)S(1)}, f32[264,128]{1,0:T(8,128)S(1)}, u32[]{:S(2)}, u32[]{:S(2)}) collective-permute-start(f32[264,128]{1,0:T(8,128)S(1)} %step_pass.12.held.sent), channel_id=1, source_target_pairs={{0,8},{1,17},{2,10},{3,19},{4,12},{5,21},{6,14},{7,23},{8,0},{9,25... | collective-permute-start | bytes 405512 | tf_op jit(solution)/shard_map/ppermute | solution.py:451
  36.9 3.6 %collective-permute-done.5.got.more = f32[264,128]{1,0:T(8,128)S(1)} collective-permute-done((f32[264,128]{1,0:T(8,128)S(1)}, f32[264,128]{1,0:T(8,128)S(1)}, u32[]{:S(2)}, u32[]{:S(2)}) %collective-permute-start.5) | collective-permute-done | bytes 135200 | tf_op jit(solution)/shard_map/ppermute | solution.py:451
  41.1 3.2 %collective-permute-start.8 = (f32[264,128]{1,0:T(8,128)S(1)}, f32[264,128]{1,0:T(8,128)S(1)}, u32[]{:S(2)}, u32[]{:S(2)}) collective-permute-start(f32[264,128]{1,0:T(8,128)S(1)} %step_pass.13.held.sent), channel_id=1, source_target_pairs={{0,16},{1,9},{2,18},{3,11},{4,20},{5,13},{6,22},{7,15},{8,24},{9,1... | collective-permute-start | bytes 405512 | tf_op jit(solution)/shard_map/ppermute | solution.py:451
  44.3 3.0 %collective-permute-done.8.got = f32[264,128]{1,0:T(8,128)S(1)} collective-permute-done((f32[264,128]{1,0:T(8,128)S(1)}, f32[264,128]{1,0:T(8,128)S(1)}, u32[]{:S(2)}, u32[]{:S(2)}) %collective-permute-start.8) | collective-permute-done | bytes 135200 | tf_op jit(solution)/shard_map/ppermute | solution.py:451
  47.3 2.6 %collective-permute-start.9 = (f32[256,128]{1,0:T(8,128)S(1)}, f32[256,128]{1,0:T(8,128)S(1)}, u32[]{:S(2)}, u32[]{:S(2)}) collective-permute-start(f32[256,128]{1,0:T(8,128)S(1)} %get-tuple-element.68.part.old), channel_id=1, source_target_pairs={{0,4},{1,3},{2,6},{3,1},{4,0},{5,7},{6,2},{7,5},{8,12},{9,11},{10,... | collective-permute-start | bytes 393224 | tf_op jit(solution)/shard_map/ppermute | solution.py:451
  49.9 3.2 %collective-permute-done.9.got = f32[256,128]{1,0:T(8,128)S(1)} collective-permute-done((f32[256,128]{1,0:T(8,128)S(1)}, f32[256,128]{1,0:T(8,128)S(1)}, u32[]{:S(2)}, u32[]{:S(2)}) %collective-permute-start.9) | collective-permute-done | bytes 131104 | tf_op jit(solution)/shard_map/ppermute | solution.py:451
  54.9 2.4 %tile_pass.4 = (f32[384,256]{1,0:T(8,128)S(1)}, f32[384,256]{1,0:T(8,128)S(1)}, f32[384,256]{1,0:T(8,128)S(1)}, f32[384,256]{1,0:T(8,128)S(1)}, f32[8,128]{1,0:T...) custom-call(s32[6]{0:T(128)S(1)} %stack.27.place, s32[1,3,6]{2,1,0:T(4,128)S(1)} %copy.12.codes, ...), custom_call_target="tpu_custom_call" | custom-call | flops 226492416 | bytes 1572864 | tf_op jit(solution)/shard_map/tile_pass/pallas_call | solution.py:135
  60.1 2.3 %prior_pass.2 = (f32[384,128]{1,0:T(8,128)S(1)}, f32[384,128]{1,0:T(8,128)S(1)}, f32[520,128]{1,0:T(8,128)S(1)}, f32[512,128]{1,0:T(8,128)S(1)}) custom-call(s32[6]{0:T(128)S(1)} %stack.27.place, bf16[768,1024]{1,0:T(8,128)(2,1)S(1)} %join_pass.1.feats, f32[512,128]{1,0:T(8,128)S(1)} %gather_pass.2.part, f32[512,128]{1,0:T(8,128)S(1)} %collective-permute-done.10.got, ...), custom_call_target="tpu_custom_call" | custom-call | flops 402653184 | bytes 3145728 | tf_op jit(solution)/shard_map/prior_pass/pallas_call | solution.py:291
  64.6 5.5 %collective-permute-done.13.got.more = f32[520,128]{1,0:T(8,128)S(1)} collective-permute-done((f32[520,128]{1,0:T(8,128)S(1)}, f32[520,128]{1,0:T(8,128)S(1)}, u32[]{:S(2)}, u32[]{:S(2)}) %collective-permute-start.13) | collective-permute-done | bytes 266272 | tf_op jit(solution)/shard_map/ppermute | solution.py:451
  70.7 1.7 %collective-permute-start.14 = (f32[264,128]{1,0:T(8,128)S(1)}, f32[264,128]{1,0:T(8,128)S(1)}, u32[]{:S(2)}, u32[]{:S(2)}) collective-permute-start(f32[264,128]{1,0:T(8,128)S(1)} %get-tuple-element.80.sent), channel_id=1, source_target_pairs={{0,4},{1,3},{2,6},{3,1},{4,0},{5,7},{6,2},{7,5},{8,12},{9,11},{10,... | collective-permute-start | bytes 405512 | tf_op jit(solution)/shard_map/ppermute | solution.py:451
  72.4 7.8 %collective-permute-done.14.got.more = f32[264,128]{1,0:T(8,128)S(1)} collective-permute-done((f32[264,128]{1,0:T(8,128)S(1)}, f32[264,128]{1,0:T(8,128)S(1)}, u32[]{:S(2)}, u32[]{:S(2)}) %collective-permute-start.14) | collective-permute-done | bytes 135200 | tf_op jit(solution)/shard_map/ppermute | solution.py:451
  80.8 6.3 %collective-permute-start.15 = (f32[264,128]{1,0:T(8,128)S(1)}, f32[264,128]{1,0:T(8,128)S(1)}, u32[]{:S(2)}, u32[]{:S(2)}) collective-permute-start(f32[264,128]{1,0:T(8,128)S(1)} %step_pass.15.held.sent), channel_id=1, source_target_pairs={{0,8},{1,17},{2,10},{3,19},{4,12},{5,21},{6,14},{7,23},{8,0},{9,25... | collective-permute-start | bytes 405512 | tf_op jit(solution)/shard_map/ppermute | solution.py:451
  87.1 4.2 %collective-permute-done.15.got.more = f32[264,128]{1,0:T(8,128)S(1)} collective-permute-done((f32[264,128]{1,0:T(8,128)S(1)}, f32[264,128]{1,0:T(8,128)S(1)}, u32[]{:S(2)}, u32[]{:S(2)}) %collective-permute-start.15) | collective-permute-done | bytes 135200 | tf_op jit(solution)/shard_map/ppermute | solution.py:451
  91.9 2.9 %collective-permute-start.18 = (f32[264,128]{1,0:T(8,128)S(1)}, f32[264,128]{1,0:T(8,128)S(1)}, u32[]{:S(2)}, u32[]{:S(2)}) collective-permute-start(f32[264,128]{1,0:T(8,128)S(1)} %step_pass.16.held.sent), channel_id=1, source_target_pairs={{0,16},{1,9},{2,18},{3,11},{4,20},{5,13},{6,22},{7,15},{8,24},{9,1... | collective-permute-start | bytes 405512 | tf_op jit(solution)/shard_map/ppermute | solution.py:451
  94.7 4.6 %collective-permute-done.18.got = f32[264,128]{1,0:T(8,128)S(1)} collective-permute-done((f32[264,128]{1,0:T(8,128)S(1)}, f32[264,128]{1,0:T(8,128)S(1)}, u32[]{:S(2)}, u32[]{:S(2)}) %collective-permute-start.18) | collective-permute-done | bytes 135200 | tf_op jit(solution)/shard_map/ppermute | solution.py:451
  99.3 2.2 %collective-permute-start.19 = (f32[256,128]{1,0:T(8,128)S(1)}, f32[256,128]{1,0:T(8,128)S(1)}, u32[]{:S(2)}, u32[]{:S(2)}) collective-permute-start(f32[256,128]{1,0:T(8,128)S(1)} %get-tuple-element.83.part), channel_id=1, source_target_pairs={{0,4},{1,3},{2,6},{3,1},{4,0},{5,7},{6,2},{7,5},{8,12},{9,11},{10,... | collective-permute-start | bytes 393224 | tf_op jit(solution)/shard_map/ppermute | solution.py:451
  101.5 4.3 %collective-permute-done.19.got = f32[256,128]{1,0:T(8,128)S(1)} collective-permute-done((f32[256,128]{1,0:T(8,128)S(1)}, f32[256,128]{1,0:T(8,128)S(1)}, u32[]{:S(2)}, u32[]{:S(2)}) %collective-permute-start.19) | collective-permute-done | bytes 131104 | tf_op jit(solution)/shard_map/ppermute | solution.py:451
  106.5 2.4 %tile_pass.5 = (f32[384,256]{1,0:T(8,128)S(1)}, f32[384,256]{1,0:T(8,128)S(1)}, f32[384,256]{1,0:T(8,128)S(1)}, f32[384,256]{1,0:T(8,128)S(1)}, f32[8,128]{1,0:T...) custom-call(s32[6]{0:T(128)S(1)} %stack.27.place, s32[1,3,6]{2,1,0:T(4,128)S(1)} %copy.12.codes, ...), custom_call_target="tpu_custom_call" | custom-call | flops 226492416 | bytes 1572864 | tf_op jit(solution)/shard_map/tile_pass/pallas_call | solution.py:135
  110.4 2.5 %collective-permute-done.20.got = f32[512,128]{1,0:T(8,128)S(1)} collective-permute-done((f32[512,128]{1,0:T(8,128)S(1)}, f32[512,128]{1,0:T(8,128)S(1)}, u32[]{:S(2)}, u32[]{:S(2)}) %collective-permute-start.20) | collective-permute-done | bytes 262176 | tf_op jit(solution)/shard_map/ppermute | solution.py:451
  112.8 2.4 %prior_pass.3 = (f32[384,128]{1,0:T(8,128)S(1)}, f32[384,128]{1,0:T(8,128)S(1)}, f32[520,128]{1,0:T(8,128)S(1)}, f32[512,128]{1,0:T(8,128)S(1)}, f32[64,128]{1,0:T(8,128)S(1)}) custom-call(s32[6]{0:T(128)S(1)} %stack.27.place, bf16[768,1024]{1,0:T(8,128)(2,1)S(1)} %join_pass.1.feats, f32[512,128]{1,0:T(8,128)S(1)} %gather_pass.3.part, ...), custom_call_target="tpu_custom_call" | custom-call | flops 402653184 | bytes 3145728 | tf_op jit(solution)/shard_map/prior_pass/pallas_call | solution.py:291
  115.3 6.4 %collective-permute-done.24.got.more = f32[520,128]{1,0:T(8,128)S(1)} collective-permute-done((f32[520,128]{1,0:T(8,128)S(1)}, f32[520,128]{1,0:T(8,128)S(1)}, u32[]{:S(2)}, u32[]{:S(2)}) %collective-permute-start.24) | collective-permute-done | bytes 266272 | tf_op jit(solution)/shard_map/ppermute | solution.py:451
  122.3 2.2 %collective-permute-start.25 = (f32[264,128]{1,0:T(8,128)S(1)}, f32[264,128]{1,0:T(8,128)S(1)}, u32[]{:S(2)}, u32[]{:S(2)}) collective-permute-start(f32[264,128]{1,0:T(8,128)S(1)} %get-tuple-element.95.sent), channel_id=1, source_target_pairs={{0,4},{1,3},{2,6},{3,1},{4,0},{5,7},{6,2},{7,5},{8,12},{9,11},{10,... | collective-permute-start | bytes 405512 | tf_op jit(solution)/shard_map/ppermute | solution.py:451
  124.4 3.0 %collective-permute-done.25.got.more = f32[264,128]{1,0:T(8,128)S(1)} collective-permute-done((f32[264,128]{1,0:T(8,128)S(1)}, f32[264,128]{1,0:T(8,128)S(1)}, u32[]{:S(2)}, u32[]{:S(2)}) %collective-permute-start.25) | collective-permute-done | bytes 135200 | tf_op jit(solution)/shard_map/ppermute | solution.py:451
  128.5 3.9 %collective-permute-done.26.got.more = f32[136,128]{1,0:T(8,128)S(1)} collective-permute-done((f32[136,128]{1,0:T(8,128)S(1)}, f32[136,128]{1,0:T(8,128)S(1)}, u32[]{:S(2)}, u32[]{:S(2)}) %collective-permute-start.26) | collective-permute-done | bytes 69664 | tf_op jit(solution)/shard_map/ppermute | solution.py:451
  134.3 3.8 %collective-permute-done.27.got = f32[72,128]{1,0:T(8,128)S(1)} collective-permute-done((f32[72,128]{1,0:T(8,128)S(1)}, f32[72,128]{1,0:T(8,128)S(1)}, u32[]{:S(2)}, u32[]{:S(2)}) %collective-permute-start.27) | collective-permute-done | bytes 36896 | tf_op jit(solution)/shard_map/ppermute | solution.py:451
  138.8 1.6 %last_pass.1 = (f32[384,256]{1,0:T(8,128)}, f32[384,256]{1,0:T(8,128)}) custom-call(s32[6]{0:T(128)S(1)} %stack.27.place, f32[8,128]{1,0:T(8,128)S(1)} %get-tuple-element.101.stats, f32[384,256]{1,0:T(8,128)S(1)} %get-tuple-element.102.base, f32[384,256]{1,0:T(8,128)S(1)} %get-tuple-element.103.grad, f32[384,128]{1,0:T(8,128)S(1)} %get-tuple-element.104.own_mean, ...), custom_call_target="tpu_custom_call" | custom-call | flops 786432 | bytes 3145728 | tf_op jit(solution)/shard_map/last_pass/pallas_call | solution.py:423
  (78 shorter events, 25.0 us)
Async XLA Ops:
  4.1 3.1 %copy-start.8 = (f32[384,256]{1,0:T(8,128)S(1)}, f32[384,256]{1,0:T(8,128)}, u32[]{:S(2)}) copy-start(f32[384,256]{1,0:T(8,128)} %refs_1_.1) | copy-start | bytes 1179652
  6.3 5.5 %collective-permute-start.1 = (f32[1024,128]{1,0:T(8,128)S(1)}, f32[1024,128]{1,0:T(8,128)S(1)}, u32[]{:S(2)}, u32[]{:S(2)}) collective-permute-start(f32[1024,128]{1,0:T(8,128)S(1)} %get-tuple-element.59), channel_id=1, source_target_pairs={{0,1},{1,0},{2,3},{3,2},{4,5},{5,4},{6,7},{7,6},{8,9},{9,8},{10,11... | collective-permute-start | bytes 1572872 | tf_op jit(solution)/shard_map/ppermute | solution.py:441
  7.0 50.8 %collective-permute-start = (f32[384,1024]{1,0:T(8,128)S(1)}, f32[384,1024]{1,0:T(8,128)S(1)}, u32[]{:S(2)}, u32[]{:S(2)}) collective-permute-start(f32[384,1024]{1,0:T(8,128)S(1)} %widen_pass.1), channel_id=1, source_target_pairs={{0,1},{1,0},{2,3},{3,2},{4,5},{5,4},{6,7},{7,6},{8,9},{9,8},{10,11... | collective-permute-start | bytes 4718600 | tf_op jit(solution)/shard_map/ppermute | solution.py:441
  10.4 1.3 collective-permute-start.2
  12.4 9.6 %collective-permute-start.3 = (f32[520,128]{1,0:T(8,128)S(1)}, f32[520,128]{1,0:T(8,128)S(1)}, u32[]{:S(2)}, u32[]{:S(2)}) collective-permute-start(f32[520,128]{1,0:T(8,128)S(1)} %get-tuple-element.62.sent), channel_id=1, source_target_pairs={{0,2},{1,5},{2,0},{3,7},{4,6},{5,1},{6,4},{7,3},{8,10},{9,13},{10,... | collective-permute-start | bytes 798728 | tf_op jit(solution)/shard_map/ppermute | solution.py:451
  15.3 21.6 %collective-permute-start.6 = (f32[384,256]{1,0:T(8,128)S(1)}, f32[384,256]{1,0:T(8,128)S(1)}, u32[]{:S(2)}, u32[]{:S(2)}) collective-permute-start(f32[384,256]{1,0:T(8,128)S(1)} %get-tuple-element.65), channel_id=1, source_target_pairs={{0,1},{1,2},{2,3},{3,4},{4,5},{5,6},{6,7},{7,8},{8,9},{9,10},{10,1... | collective-permute-start | bytes 1179656 | tf_op jit(solution)/shard_map/ppermute | solution.py:445
  15.3 21.6 %collective-permute-start.7 = (f32[384,256]{1,0:T(8,128)S(1)}, f32[384,256]{1,0:T(8,128)S(1)}, u32[]{:S(2)}, u32[]{:S(2)}) collective-permute-start(f32[384,256]{1,0:T(8,128)S(1)} %get-tuple-element.66), channel_id=1, source_target_pairs={{0,1},{1,2},{2,3},{3,4},{4,5},{5,6},{6,7},{7,8},{8,9},{9,10},{10,1... | collective-permute-start | bytes 1179656 | tf_op jit(solution)/shard_map/ppermute | solution.py:445
  22.6 9.3 %collective-permute-start.4 = (f32[264,128]{1,0:T(8,128)S(1)}, f32[264,128]{1,0:T(8,128)S(1)}, u32[]{:S(2)}, u32[]{:S(2)}) collective-permute-start(f32[264,128]{1,0:T(8,128)S(1)} %get-tuple-element.64.sent), channel_id=1, source_target_pairs={{0,4},{1,3},{2,6},{3,1},{4,0},{5,7},{6,2},{7,5},{8,12},{9,11},{10,... | collective-permute-start | bytes 405512 | tf_op jit(solution)/shard_map/ppermute | solution.py:451
  32.4 8.1 %collective-permute-start.5 = (f32[264,128]{1,0:T(8,128)S(1)}, f32[264,128]{1,0:T(8,128)S(1)}, u32[]{:S(2)}, u32[]{:S(2)}) collective-permute-start(f32[264,128]{1,0:T(8,128)S(1)} %step_pass.12.held.sent), channel_id=1, source_target_pairs={{0,8},{1,17},{2,10},{3,19},{4,12},{5,21},{6,14},{7,23},{8,0},{9,25... | collective-permute-start | bytes 405512 | tf_op jit(solution)/shard_map/ppermute | solution.py:451
  41.1 6.2 %collective-permute-start.8 = (f32[264,128]{1,0:T(8,128)S(1)}, f32[264,128]{1,0:T(8,128)S(1)}, u32[]{:S(2)}, u32[]{:S(2)}) collective-permute-start(f32[264,128]{1,0:T(8,128)S(1)} %step_pass.13.held.sent), channel_id=1, source_target_pairs={{0,16},{1,9},{2,18},{3,11},{4,20},{5,13},{6,22},{7,15},{8,24},{9,1... | collective-permute-start | bytes 405512 | tf_op jit(solution)/shard_map/ppermute | solution.py:451
  47.3 5.8 %collective-permute-start.9 = (f32[256,128]{1,0:T(8,128)S(1)}, f32[256,128]{1,0:T(8,128)S(1)}, u32[]{:S(2)}, u32[]{:S(2)}) collective-permute-start(f32[256,128]{1,0:T(8,128)S(1)} %get-tuple-element.68.part.old), channel_id=1, source_target_pairs={{0,4},{1,3},{2,6},{3,1},{4,0},{5,7},{6,2},{7,5},{8,12},{9,11},{10,... | collective-permute-start | bytes 393224 | tf_op jit(solution)/shard_map/ppermute | solution.py:451
  53.7 6.4 %collective-permute-start.10 = (f32[512,128]{1,0:T(8,128)S(1)}, f32[512,128]{1,0:T(8,128)S(1)}, u32[]{:S(2)}, u32[]{:S(2)}) collective-permute-start(f32[512,128]{1,0:T(8,128)S(1)} %gather_pass.2.part), channel_id=1, source_target_pairs={{0,2},{1,5},{2,0},{3,7},{4,6},{5,1},{6,4},{7,3},{8,10},{9,13},{10,... | collective-permute-start | bytes 786440 | tf_op jit(solution)/shard_map/ppermute | solution.py:451
  54.9 2.9 %copy-start.1 = (bf16[384,1024]{1,0:T(8,128)(2,1)S(1)}, bf16[384,1024]{1,0:T(8,128)(2,1)}, u32[]{:S(2)}) copy-start(bf16[384,1024]{1,0:T(8,128)(2,1)} %feats_in.1) | copy-start | bytes 2359300
  57.2 1.5 %collective-permute-start.11 = (f32[384,128]{1,0:T(8,128)S(1)}, f32[384,128]{1,0:T(8,128)S(1)}, u32[]{:S(2)}, u32[]{:S(2)}) collective-permute-start(f32[384,128]{1,0:T(8,128)S(1)} %get-tuple-element.75), channel_id=1, source_target_pairs={{0,1},{1,0},{2,3},{3,2},{4,5},{5,4},{6,7},{7,6},{8,9},{9,8},{10,11... | collective-permute-start | bytes 589832 | tf_op jit(solution)/shard_map/ppermute | solution.py:441
  57.3 1.4 %collective-permute-start.12 = (f32[8,128]{1,0:T(8,128)S(1)}, f32[8,128]{1,0:T(8,128)S(1)}, u32[]{:S(2)}, u32[]{:S(2)}) collective-permute-start(f32[8,128]{1,0:T(8,128)S(1)} %get-tuple-element.76.stats), channel_id=1, source_target_pairs={{0,1},{1,0},{2,3},{3,2},{4,5},{5,4},{6,7},{7,6},{8,9},{9,8},{10,11... | collective-permute-start | bytes 12296 | tf_op jit(solution)/shard_map/ppermute | solution.py:441
  62.4 7.7 %collective-permute-start.13 = (f32[520,128]{1,0:T(8,128)S(1)}, f32[520,128]{1,0:T(8,128)S(1)}, u32[]{:S(2)}, u32[]{:S(2)}) collective-permute-start(f32[520,128]{1,0:T(8,128)S(1)} %get-tuple-element.78.sent), channel_id=1, source_target_pairs={{0,2},{1,5},{2,0},{3,7},{4,6},{5,1},{6,4},{7,3},{8,10},{9,13},{10,... | collective-permute-start | bytes 798728 | tf_op jit(solution)/shard_map/ppermute | solution.py:451
  63.7 23.4 %collective-permute-start.16 = (f32[384,256]{1,0:T(8,128)S(1)}, f32[384,256]{1,0:T(8,128)S(1)}, u32[]{:S(2)}, u32[]{:S(2)}) collective-permute-start(f32[384,256]{1,0:T(8,128)S(1)} %get-tuple-element.81), channel_id=1, source_target_pairs={{0,1},{1,2},{2,3},{3,4},{4,5},{5,6},{6,7},{7,8},{8,9},{9,10},{10,1... | collective-permute-start | bytes 1179656 | tf_op jit(solution)/shard_map/ppermute | solution.py:445
  63.7 23.4 %collective-permute-start.17 = (f32[384,256]{1,0:T(8,128)S(1)}, f32[384,256]{1,0:T(8,128)S(1)}, u32[]{:S(2)}, u32[]{:S(2)}) collective-permute-start(f32[384,256]{1,0:T(8,128)S(1)} %get-tuple-element.82), channel_id=1, source_target_pairs={{0,1},{1,2},{2,3},{3,4},{4,5},{5,6},{6,7},{7,8},{8,9},{9,10},{10,1... | collective-permute-start | bytes 1179656 | tf_op jit(solution)/shard_map/ppermute | solution.py:445
  70.7 9.5 %collective-permute-start.14 = (f32[264,128]{1,0:T(8,128)S(1)}, f32[264,128]{1,0:T(8,128)S(1)}, u32[]{:S(2)}, u32[]{:S(2)}) collective-permute-start(f32[264,128]{1,0:T(8,128)S(1)} %get-tuple-element.80.sent), channel_id=1, source_target_pairs={{0,4},{1,3},{2,6},{3,1},{4,0},{5,7},{6,2},{7,5},{8,12},{9,11},{10,... | collective-permute-start | bytes 405512 | tf_op jit(solution)/shard_map/ppermute | solution.py:451
  80.8 10.5 %collective-permute-start.15 = (f32[264,128]{1,0:T(8,128)S(1)}, f32[264,128]{1,0:T(8,128)S(1)}, u32[]{:S(2)}, u32[]{:S(2)}) collective-permute-start(f32[264,128]{1,0:T(8,128)S(1)} %step_pass.15.held.sent), channel_id=1, source_target_pairs={{0,8},{1,17},{2,10},{3,19},{4,12},{5,21},{6,14},{7,23},{8,0},{9,25... | collective-permute-start | bytes 405512 | tf_op jit(solution)/shard_map/ppermute | solution.py:451
  91.9 7.4 %collective-permute-start.18 = (f32[264,128]{1,0:T(8,128)S(1)}, f32[264,128]{1,0:T(8,128)S(1)}, u32[]{:S(2)}, u32[]{:S(2)}) collective-permute-start(f32[264,128]{1,0:T(8,128)S(1)} %step_pass.16.held.sent), channel_id=1, source_target_pairs={{0,16},{1,9},{2,18},{3,11},{4,20},{5,13},{6,22},{7,15},{8,24},{9,1... | collective-permute-start | bytes 405512 | tf_op jit(solution)/shard_map/ppermute | solution.py:451
  94.7 11.7 %collective-permute-start.21 = (f32[384,128]{1,0:T(8,128)S(1)}, f32[384,128]{1,0:T(8,128)S(1)}, u32[]{:S(2)}, u32[]{:S(2)}) collective-permute-start(f32[384,128]{1,0:T(8,128)S(1)} %get-tuple-element.87), channel_id=1, source_target_pairs={{0,1},{1,0},{2,3},{3,2},{4,5},{5,4},{6,7},{7,6},{8,9},{9,8},{10,11... | collective-permute-start | bytes 589832 | tf_op jit(solution)/shard_map/ppermute | solution.py:441
  99.3 6.5 %collective-permute-start.19 = (f32[256,128]{1,0:T(8,128)S(1)}, f32[256,128]{1,0:T(8,128)S(1)}, u32[]{:S(2)}, u32[]{:S(2)}) collective-permute-start(f32[256,128]{1,0:T(8,128)S(1)} %get-tuple-element.83.part), channel_id=1, source_target_pairs={{0,4},{1,3},{2,6},{3,1},{4,0},{5,7},{6,2},{7,5},{8,12},{9,11},{10,... | collective-permute-start | bytes 393224 | tf_op jit(solution)/shard_map/ppermute | solution.py:451
  106.4 6.4 %collective-permute-start.20 = (f32[512,128]{1,0:T(8,128)S(1)}, f32[512,128]{1,0:T(8,128)S(1)}, u32[]{:S(2)}, u32[]{:S(2)}) collective-permute-start(f32[512,128]{1,0:T(8,128)S(1)} %gather_pass.3.part), channel_id=1, source_target_pairs={{0,2},{1,5},{2,0},{3,7},{4,6},{5,1},{6,4},{7,3},{8,10},{9,13},{10,... | collective-permute-start | bytes 786440 | tf_op jit(solution)/shard_map/ppermute | solution.py:451
  108.9 1.5 %collective-permute-start.22 = (f32[384,128]{1,0:T(8,128)S(1)}, f32[384,128]{1,0:T(8,128)S(1)}, u32[]{:S(2)}, u32[]{:S(2)}) collective-permute-start(f32[384,128]{1,0:T(8,128)S(1)} %get-tuple-element.90), channel_id=1, source_target_pairs={{0,1},{1,0},{2,3},{3,2},{4,5},{5,4},{6,7},{7,6},{8,9},{9,8},{10,11... | collective-permute-start | bytes 589832 | tf_op jit(solution)/shard_map/ppermute | solution.py:441
  108.9 1.4 %collective-permute-start.23 = (f32[8,128]{1,0:T(8,128)S(1)}, f32[8,128]{1,0:T(8,128)S(1)}, u32[]{:S(2)}, u32[]{:S(2)}) collective-permute-start(f32[8,128]{1,0:T(8,128)S(1)} %get-tuple-element.91.stats), channel_id=1, source_target_pairs={{0,1},{1,0},{2,3},{3,2},{4,5},{5,4},{6,7},{7,6},{8,9},{9,8},{10,11... | collective-permute-start | bytes 12296 | tf_op jit(solution)/shard_map/ppermute | solution.py:441
  115.2 6.5 %collective-permute-start.24 = (f32[520,128]{1,0:T(8,128)S(1)}, f32[520,128]{1,0:T(8,128)S(1)}, u32[]{:S(2)}, u32[]{:S(2)}) collective-permute-start(f32[520,128]{1,0:T(8,128)S(1)} %get-tuple-element.93.sent), channel_id=1, source_target_pairs={{0,2},{1,5},{2,0},{3,7},{4,6},{5,1},{6,4},{7,3},{8,10},{9,13},{10,... | collective-permute-start | bytes 798728 | tf_op jit(solution)/shard_map/ppermute | solution.py:451
  122.3 5.2 %collective-permute-start.25 = (f32[264,128]{1,0:T(8,128)S(1)}, f32[264,128]{1,0:T(8,128)S(1)}, u32[]{:S(2)}, u32[]{:S(2)}) collective-permute-start(f32[264,128]{1,0:T(8,128)S(1)} %get-tuple-element.95.sent), channel_id=1, source_target_pairs={{0,4},{1,3},{2,6},{3,1},{4,0},{5,7},{6,2},{7,5},{8,12},{9,11},{10,... | collective-permute-start | bytes 405512 | tf_op jit(solution)/shard_map/ppermute | solution.py:451
  124.4 14.3 %collective-permute-start.28 = (f32[384,128]{1,0:T(8,128)S(1)}, f32[384,128]{1,0:T(8,128)S(1)}, u32[]{:S(2)}, u32[]{:S(2)}) collective-permute-start(f32[384,128]{1,0:T(8,128)S(1)} %get-tuple-element.105), channel_id=1, source_target_pairs={{0,1},{1,0},{2,3},{3,2},{4,5},{5,4},{6,7},{7,6},{8,9},{9,8},{10,11... | collective-permute-start | bytes 589832 | tf_op jit(solution)/shard_map/ppermute | solution.py:441
  128.0 4.4 %collective-permute-start.26 = (f32[136,128]{1,0:T(8,128)S(1)}, f32[136,128]{1,0:T(8,128)S(1)}, u32[]{:S(2)}, u32[]{:S(2)}) collective-permute-start(f32[136,128]{1,0:T(8,128)S(1)} %get-tuple-element.97.sent), channel_id=1, source_target_pairs={{0,8},{1,17},{2,10},{3,19},{4,12},{5,21},{6,14},{7,23},{8,0},{9,25... | collective-permute-start | bytes 208904 | tf_op jit(solution)/shard_map/ppermute | solution.py:451
  132.9 5.2 %collective-permute-start.27 = (f32[72,128]{1,0:T(8,128)S(1)}, f32[72,128]{1,0:T(8,128)S(1)}, u32[]{:S(2)}, u32[]{:S(2)}) collective-permute-start(f32[72,128]{1,0:T(8,128)S(1)} %get-tuple-element.99.sent), channel_id=1, source_target_pairs={{0,16},{1,9},{2,18},{3,11},{4,20},{5,13},{6,22},{7,15},{8,24},{9,1... | collective-permute-start | bytes 110600 | tf_op jit(solution)/shard_map/ppermute | solution.py:451
  138.7 1.7 %collective-permute-start.29 = (f32[32,128]{1,0:T(8,128)S(1)}, f32[32,128]{1,0:T(8,128)S(1)}, u32[]{:S(2)}, u32[]{:S(2)}) collective-permute-start(f32[32,128]{1,0:T(8,128)S(1)} %get-tuple-element.112), channel_id=1, source_target_pairs={{0,1},{1,0},{2,3},{3,2},{4,5},{5,4},{6,7},{7,6},{8,9},{9,8},{10,11... | collective-permute-start | bytes 49160 | tf_op jit(solution)/shard_map/ppermute | solution.py:441
  (9 other events, 11.0 us)

commit v6 on v5

--- a/solution.py
+++ b/solution.py
@@ -40,6 +40,14 @@
     return pl.CostEstimate(flops=flops, bytes_accessed=size, transcendentals=0)
 
 
+def where_am_i(devices):
+    own = lax.axis_index("user")
+    core = own & 1
+    zero, one = (bit_order(devices, c) for c in range(CORES))
+    bits = [jnp.where(core == 0, own >> z, own >> o) & 1 for z, o in zip(zero, one, strict=True)]
+    return [core, *bits, own >> 1]
+
+
 def half_of(ref, core):
     width = ref.shape[1] // CORES
     return ref[:, pl.ds(pl.multiple_of(core * width, width), width)]
@@ -49,7 +57,7 @@
     return (1.0 + stats[1:2, :] / 2.0) / (1.0 + stats[0:1, :] / 2.0)
 
 
-def tile_kernel(stratum, noise_scale, place, codes, count, ratings, user_noise, item_noise, *refs):
+def tile_kernel(stratum, noise_scale, devices, codes, count, ratings, user_noise, item_noise, *refs):
     if stratum == 0:
         users_in, items_in = refs[:2]
         base_u, grad_u, base_v, grad_v, stats = refs[2:7]
@@ -59,6 +67,7 @@
         base_u, grad_u, base_v, grad_v, stats, own_cols, other_cols = refs[7:14]
         refs = refs[14:]
     tiles, noise_u, noise_v, users, items, pred, err_b, sems = refs
+    core = where_am_i(devices)[0]
     rows, rank = users.shape
     width = rank // CORES
     tile = tiles.shape[-1]
@@ -84,14 +93,14 @@
         precision = jnp.concatenate([precision] * CORES, 1)
         items[...] = old_base_v[...] + precision * old_grad_v[...]
         new = old_base[...] + precision * old_grad[...]
-        here = place[0] == 0
+        here = core == 0
         pull = step_size * prior_prec
         left = jnp.where(here, own_mean[...], other_mean[...])
         right = jnp.where(here, other_mean[...], own_mean[...])
         users[:, :width] = new[:, :width] + pull * left
         users[:, width:] = new[:, width:] + pull * right
-        own_cols[...] = half_of(users, place[0])
-        other_cols[...] = half_of(users, 1 - place[0])
+        own_cols[...] = half_of(users, core)
+        other_cols[...] = half_of(users, 1 - core)
     user_b = users[...].astype(bf16)
     item_b = items[...].astype(bf16)
     pred[...] = dot(user_b, item_b, NT)
@@ -124,7 +133,7 @@
     )
 
 
-def tile_pass(stratum, place, codes, count, ratings, user_noise, item_noise, *state):
+def tile_pass(stratum, devices, codes, count, ratings, user_noise, item_noise, *state):
     slots, tile = ratings.shape[2:4]
     rows, rank = user_noise.shape[1:]
     noise_scale = math.sqrt(2.0 * step_size)
@@ -133,9 +142,9 @@
     if stratum:
         outs += [shape(rows, width)] * 2
     return pl.pallas_call(
-        functools.partial(tile_kernel, stratum, noise_scale),
+        functools.partial(tile_kernel, stratum, noise_scale, devices),
         out_shape=tuple(outs),
-        in_specs=[SMEM] * 3 + [HBM] * 3 + [VMEM if stratum else HBM] * len(state),
+        in_specs=[SMEM] * 2 + [HBM] * 3 + [VMEM if stratum else HBM] * len(state),
         out_specs=(VMEM,) * len(outs),
         scratch_shapes=[
             pltpu.VMEM((slots, tile, tile), bf16),
@@ -150,10 +159,10 @@
         compiler_params=PARAMS,
         cost_estimate=cost(6 * rows * rows * rank, 16 * rows * rank),
         name="tile_pass",
-    )(place, codes, count, ratings, user_noise, item_noise, *state)
-
-
-def first_kernel(place, feats_in, weights_in, users_in, own_mean, other_mean, send, keep, old, mean, feats, weights, users, sems):
+    )(codes, count, ratings, user_noise, item_noise, *state)
+
+
+def first_kernel(devices, feats_in, weights_in, users_in, own_mean, other_mean, send, keep, old, mean, feats, weights, users, sems):
     copies = [
         pltpu.make_async_copy(source, target, sems.at[n])
         for n, (source, target) in enumerate(
@@ -162,6 +171,7 @@
     ]
     for copy in copies:
         copy.start()
+    place = where_am_i(devices)
     here = place[0]
     copies[0].wait()
     weights_b = weights[...].astype(bf16)
@@ -179,14 +189,14 @@
     old[...] = weights[pl.ds(pl.multiple_of(start, rows), rows), cols]
 
 
-def first_pass(place, feats, weights, users):
+def first_pass(devices, feats, weights, users):
     rows, rank = users.shape
     feat = weights.shape[0]
     width = rank // CORES
     return pl.pallas_call(
-        first_kernel,
+        functools.partial(first_kernel, devices),
         out_shape=(shape(rows, width),) * 2 + (shape(feat, width),) * 2 + (shape(feat // 4, width),),
-        in_specs=[SMEM] + [HBM] * 3,
+        in_specs=[HBM] * 3,
         out_specs=(VMEM,) * 5,
         scratch_shapes=[
             pltpu.VMEM(users.shape, f32),
@@ -198,7 +208,7 @@
         compiler_params=PARAMS,
         cost_estimate=cost(4 * rows * feat * rank, 8 * feat * rank),
         name="first_pass",
-    )(place, feats, weights, users)
+    )(feats, weights, users)
 
 
 def widen_kernel(narrow_in, wide, narrow, sem):
@@ -220,52 +230,74 @@
     )(narrow)
 
 
-def join_kernel(own, other, both, sem):
+def join_kernel(own, other, both, turned):
     rows = other.shape[0]
-    copy = pltpu.make_async_copy(own, both.at[:rows], sem.at[0])
-    copy.start()
+    both[:rows, :] = own[...]
     both[rows:, :] = other[...].astype(bf16)
-    copy.wait()
+    turned[:, :rows] = own[...].T
+    turned[:, rows:] = other[...].T.astype(bf16)
 
 
 def join_pass(own, other):
     rows, feat = own.shape
     return pl.pallas_call(
         join_kernel,
-        out_shape=shape(CORES * rows, feat, dtype=bf16),
-        in_specs=[HBM, VMEM],
-        out_specs=VMEM,
-        scratch_shapes=[pltpu.SemaphoreType.DMA((1,))],
-        compiler_params=PARAMS,
+        out_shape=(shape(CORES * rows, feat, dtype=bf16), shape(feat, CORES * rows, dtype=bf16)),
+        in_specs=[VMEM, VMEM],
+        out_specs=(VMEM, VMEM),
+        compiler_params=PARAMS,
+        cost_estimate=cost(rows * feat, 12 * rows * feat),
         name="join_pass",
     )(own, other)
 
 
-def prior_kernel(places, place, feats, part, got, own_cols, other_cols, stats, more_stats, own_mean, other_mean, send, keep, *refs):
+def part_kernel(devices, feats, part, mean):
+    half = part.shape[0]
+    bit = where_am_i(devices)[1]
+    here = pl.ds(pl.multiple_of(bit * half, half), half)
+    mean[...] = dot(feats[:, here], part[...].astype(bf16))
+
+
+def part_pass(devices, feats, part):
+    rows = feats.shape[0]
+    half, width = part.shape
+    return pl.pallas_call(
+        functools.partial(part_kernel, devices),
+        out_shape=shape(rows, width),
+        in_specs=[VMEM, VMEM],
+        out_specs=VMEM,
+        compiler_params=PARAMS,
+        cost_estimate=cost(2 * rows * half * width, 4 * rows * half),
+        name="part_pass",
+    )(feats, part)
+
+
+def prior_kernel(places, devices, feats, turned, begun, part, got, own_cols, other_cols, stats, more_stats, own_mean, other_mean, send, keep, *refs):
     rows = own_cols.shape[0]
     half = keep.shape[0]
+    place = where_am_i(devices)
     core, bit = place[0], place[1]
     here = pl.ds(pl.multiple_of(bit * half, half), half)
     there = pl.ds(pl.multiple_of((1 - bit) * half, half), half)
     offset = refs[-1]
-    mean = dot(feats[:, here], part[...].astype(bf16)) + dot(feats[:, there], got[...].astype(bf16))
+    mean = begun[...] + dot(feats[:, there], got[...].astype(bf16))
     own_mean[...] = mean[:rows]
     other_mean[...] = mean[rows:]
     offset[:rows, :] = (own_cols[...] - mean[:rows]).astype(bf16)
     offset[rows:, :] = (other_cols[...] - mean[rows:]).astype(bf16)
     send[half:, :] = stats[...] + more_stats[...]
     if places is None:
-        send[:half, :] = dot(feats[:, there], offset[...], TN)
-        keep[...] = dot(feats[:, here], offset[...], TN)
+        send[:half, :] = dot(turned[there, :], offset[...])
+        keep[...] = dot(turned[here, :], offset[...])
         return
     old, full = refs[:2]
     full[here, :] = part[...]
     full[there, :] = got[...]
-    start = place[place.shape[0] - 1] * old.shape[0]
+    start = place[-1] * old.shape[0]
     if old.shape[0] % 8 == 0:
         start = pl.multiple_of(start, old.shape[0])
     old[...] = full[pl.ds(start, old.shape[0]), :]
-    full[...] = dot(feats[...], offset[...], TN)
+    full[...] = dot(turned[...], offset[...])
     blocks = len(places[0])
     block = 2 * half // blocks
     for ref, which in ((send, 1 - bit), (keep, bit)):
@@ -280,7 +312,7 @@
             ref[n * block : (n + 1) * block, :] = full[pl.ds(source, block), :]
 
 
-def prior_pass(place, feats, part, got, own_cols, other_cols, stats, more_stats, places=None):
+def prior_pass(devices, feats, turned, begun, part, got, own_cols, other_cols, stats, more_stats, places=None):
     rows, width = own_cols.shape
     half = part.shape[0]
     outs = [shape(rows, width)] * 2 + [shape(half + stats.shape[0], width), shape(half, width)]
@@ -289,24 +321,24 @@
         outs.append(shape(2 * half // len(places[0]), width))
         scratch.insert(0, pltpu.VMEM((2 * half, width), f32))
     return pl.pallas_call(
-        functools.partial(prior_kernel, places),
+        functools.partial(prior_kernel, places, devices),
         out_shape=tuple(outs),
-        in_specs=[SMEM] + [VMEM] * 7,
+        in_specs=[VMEM] * 9,
         out_specs=(VMEM,) * len(outs),
         scratch_shapes=scratch,
         compiler_params=PARAMS,
         cost_estimate=cost(16 * rows * half * width, 16 * rows * half),
         name="prior_pass",
-    )(place, feats, part, got, own_cols, other_cols, stats, more_stats)
-
-
-def step_kernel(halving, slot, place, held, got, sent, more, *refs):
+    )(feats, turned, begun, part, got, own_cols, other_cols, stats, more_stats)
+
+
+def step_kernel(halving, slot, devices, held, got, sent, more, *refs):
     send = refs[-2] if halving else refs[-1]
     riders = sent.shape[0] - RIDERS, more.shape[0] - RIDERS
     rider = sent[riders[0] :, :] + more[riders[1] :, :]
     rows = send.shape[0] - RIDERS
     if halving:
-        bit = place[slot]
+        bit = where_am_i(devices)[slot]
         for ref, which in ((send, 1 - bit), (refs[-1], bit)):
             at = pl.ds(pl.multiple_of(which * rows, 8), rows) if rows % 8 == 0 else pl.ds(which * rows, rows)
             ref[:rows, :] = held[at, :] + got[at, :]
@@ -315,18 +347,18 @@
     send[rows:, :] = rider
 
 
-def step_pass(halving, stage, place, held, got, sent, more, rows, later=()):
+def step_pass(halving, stage, devices, held, got, sent, more, rows, later=()):
     width = held.shape[1]
     outs = [shape(rows // 2 + RIDERS, width), shape(rows // 2, width)] if halving else [shape(rows + RIDERS, width)]
     return pl.pallas_call(
-        functools.partial(step_kernel, halving, 1 + stage),
+        functools.partial(step_kernel, halving, 1 + stage, devices),
         out_shape=tuple(outs),
-        in_specs=[SMEM] + [VMEM] * 4 + [ANY] * len(later),
+        in_specs=[VMEM] * 4 + [ANY] * len(later),
         out_specs=(VMEM,) * len(outs),
         compiler_params=PARAMS,
         cost_estimate=cost(rows * width, 12 * rows * width),
         name="step_pass",
-    )(place, held, got, sent, more, *later)
+    )(held, got, sent, more, *later)
 
 
 def update_kernel(rate, held, got, sent, old, *refs):
@@ -350,64 +382,67 @@
     )(held, got, sent, old, *later)
 
 
-def gather_kernel(slot, place, part, got, both):
+def gather_kernel(slot, devices, part, got, both):
     rows = part.shape[0]
-    bit = place[slot]
+    bit = where_am_i(devices)[slot]
     both[pl.ds(pl.multiple_of(bit * rows, rows), rows), :] = part[...]
     both[pl.ds(pl.multiple_of((1 - bit) * rows, rows), rows), :] = got[...]
 
 
-def gather_pass(stage, place, part, got):
+def gather_pass(stage, devices, part, got):
     rows, width = part.shape
     return pl.pallas_call(
-        functools.partial(gather_kernel, 1 + stage),
+        functools.partial(gather_kernel, 1 + stage, devices),
         out_shape=shape(2 * rows, width),
-        in_specs=[SMEM, VMEM, VMEM],
+        in_specs=[VMEM, VMEM],
         out_specs=VMEM,
         compiler_params=PARAMS,
         cost_estimate=cost(rows * width, 16 * rows * width),
         name="gather_pass",
-    )(place, part, got)
-
-
-def split_kernel(place, both, mine, other):
+    )(part, got)
+
+
+def split_kernel(devices, both, mine, other):
+    place = where_am_i(devices)
     rows = mine.shape[0]
     for ref, which in ((mine, place[0]), (other, 1 - place[0])):
         at = pl.ds(pl.multiple_of(which * rows, 8), rows) if rows % 8 == 0 else pl.ds(which * rows, rows)
         ref[...] = both[at, :]
 
 
-def split_pass(place, both):
+def split_pass(devices, both):
     rows, width = both.shape
     return pl.pallas_call(
-        split_kernel,
+        functools.partial(split_kernel, devices),
         out_shape=(shape(rows // CORES, width),) * 2,
-        in_specs=[SMEM, VMEM],
+        in_specs=[VMEM],
         out_specs=(VMEM,) * 2,
         compiler_params=PARAMS,
         name="split_pass",
-    )(place, both)
-
-
-def across_kernel(place, mine, other, both):
+    )(both)
+
+
+def across_kernel(devices, mine, other, both):
+    place = where_am_i(devices)
     width = mine.shape[1]
     both[:, pl.ds(pl.multiple_of(place[0] * width, width), width)] = mine[...]
     both[:, pl.ds(pl.multiple_of((1 - place[0]) * width, width), width)] = other[...]
 
 
-def across_pass(place, mine, other):
+def across_pass(devices, mine, other):
     rows, width = mine.shape
     return pl.pallas_call(
-        across_kernel,
+        functools.partial(across_kernel, devices),
         out_shape=shape(rows, CORES * width),
-        in_specs=[SMEM, VMEM, VMEM],
+        in_specs=[VMEM, VMEM],
         out_specs=VMEM,
         compiler_params=PARAMS,
         name="across_pass",
-    )(place, mine, other)
-
-
-def last_kernel(place, stats, base, grad, own_mean, other_mean, base_v, grad_v, users, items):
+    )(mine, other)
+
+
+def last_kernel(devices, stats, base, grad, own_mean, other_mean, base_v, grad_v, users, items):
+    place = where_am_i(devices)
     width = own_mean.shape[1]
     precision = precision_of(stats[...])
     precision = jnp.concatenate([precision] * CORES, 1)
@@ -419,16 +454,16 @@
         users[:, at] = users[:, at] + pull * mean[...]
 
 
-def last_pass(place, stats, base, *state):
-    return pl.pallas_call(
-        last_kernel,
+def last_pass(devices, stats, base, *state):
+    return pl.pallas_call(
+        functools.partial(last_kernel, devices),
         out_shape=(shape(*base.shape),) * 2,
-        in_specs=[SMEM] + [VMEM] * 7,
+        in_specs=[VMEM] * 7,
         out_specs=(VMEM,) * 2,
         compiler_params=PARAMS,
         cost_estimate=cost(8 * base.size, 32 * base.size),
         name="last_pass",
-    )(place, stats, base, *state)
+    )(stats, base, *state)
 
 
 def bit_order(devices, core):
@@ -477,56 +512,54 @@
     item_noise,
 ):
     devices = lax.axis_size("user")
-    own = lax.axis_index("user")
     stages = devices.bit_length() - 2
     strata = ratings.shape[1]
     feat = prior_weights.shape[0]
     rate = rate_scale / (user_factors.shape[0] * devices)
-    core = own & 1
-    zero, one = (bit_order(devices, c) for c in range(CORES))
-    bits = [jnp.where(core == 0, own >> z, own >> o) & 1 for z, o in zip(zero, one, strict=True)]
-    place = jnp.stack([core, *bits, own >> 1])
-    tables = (place, tile_index, tile_count, ratings, user_noise, item_noise)
+    tables = (devices, tile_index, tile_count, ratings, user_noise, item_noise)
 
     own_mean, other_mean, send, held, old = first_pass(
-        place, side_features, prior_weights, user_factors
+        devices, side_features, prior_weights, user_factors
     )
     got = swap(send, devices)
     base, grad, base_v, grad_v, stats = tile_pass(0, *tables, user_factors, item_factors)
     more = swap(stats, devices)
-    send, held = step_pass(True, 0, place, held, got, stats, more, feat)
-    feats = join_pass(side_features, swap(widen_pass(side_features), devices))
+    send, held = step_pass(True, 0, devices, held, got, stats, more, feat)
+    feats, turned = join_pass(side_features, swap(widen_pass(side_features), devices))
     for stratum in range(strata):
         last = stratum + 1 == strata
         if not last:
             base_v, grad_v = roll(base_v, devices), roll(grad_v, devices)
         got = exchange(send, devices, 0)
-        send, held = step_pass(True, 1, place, held, got, send, got, feat // 2)
+        send, held = step_pass(True, 1, devices, held, got, send, got, feat // 2)
         for stage in range(1, stages - 1):
             got = exchange(send, devices, stage)
             rows = got.shape[0] - RIDERS
             if last:
-                send, held = step_pass(True, stage + 1, place, held, got, send, got, rows)
+                send, held = step_pass(True, stage + 1, devices, held, got, send, got, rows)
             else:
-                later = (base_v, grad_v) if stage == 2 else ()
-                (send,) = step_pass(False, 0, place, held, got, send, got, rows, later)
+                later = (base_v,) if stage == 1 else ()
+                (send,) = step_pass(False, 0, devices, held, got, send, got, rows, later)
                 held = send
         got = exchange(send, devices, stages - 1)
-        part, stats = update_pass(rate, held, got, send, old)
+        part, stats = update_pass(rate, held, got, send, old, () if last else (grad_v,))
         if last:
             break
         old = part
         got = exchange(part, devices, 1)
-        part = gather_pass(1, place, part, got)
+        part = gather_pass(1, devices, part, got)
         got = exchange(part, devices, 0)
+        begun = part_pass(devices, feats, part)
         base, grad, base_v, grad_v, stats, own_cols, other_cols = tile_pass(
             stratum + 1, *tables, base, grad, own_mean, other_mean, stats, base_v, grad_v
         )
         more = swap(stats, devices)
         other_cols = swap(other_cols, devices)
         outs = prior_pass(
-            place,
+            devices,
             feats,
+            turned,
+            begun,
             part,
             got,
             own_cols,
@@ -539,10 +572,10 @@
         if len(outs) > 4:
             old = outs[4]
         other_mean = swap(other_mean, devices)
-    mine, other = split_pass(place, part)
+    mine, other = split_pass(devices, part)
     got = swap(other, devices)
-    users, items = last_pass(place, stats, base, grad, own_mean, other_mean, base_v, grad_v)
-    return (users, items, across_pass(place, mine, got))
+    users, items = last_pass(devices, stats, base, grad, own_mean, other_mean, base_v, grad_v)
+    return (users, items, across_pass(devices, mine, got))
 
 
 def solution(mesh):

time: 142 us -> 129 us (0.908)
  Pallas kernels: 24.7 us -> 14.6 us
  starting transfers between devices: 38.1 us -> 33.2 us
  waiting for transfers between devices: 73.7 us -> 75.7 us
    pallas_call x22 -> x24, Pallas kernels: 24.4 us -> 14.4 us  [the longest x3 7.41 us: tile_pass(): pl.pallas_call(functools.partial(tile_kernel, stratum, noise_scale, devic...]
    ppermute x16, starting transfers between devices: 34.5 us -> 30.8 us  [exchange(): return lax.ppermute(array, 'user', pairs)]
    ppermute x4, waiting for transfers between devices: 0.01 us -> 2.55 us  [roll(): lax.ppermute(array, 'user', [(i, (i + 1) % devices) for i in range(device...]
  transfers between devices with their start and end apart: 30 -> 30, of which waited for: 19 -> 20; matrix products, arithmetic and copies ran while one was open for 0% -> 0% of each run, Pallas kernels for 11% -> 8%
where the time goes in v6:
time: 129 us; the launch traced here: 128 us
  waiting for transfers between devices  75.7 us (59%)
  starting transfers between devices  33.2 us (26%)
  Pallas kernels  14.6 us (11%)
  local copies, waits for them, and re-layouts  4.04 us (3%)
    ppermute x16, waiting for transfers between devices, exchange(): return lax.ppermute(array, 'user', pairs)  71.6 us
    ppermute x16, starting transfers between devices, exchange(): return lax.ppermute(array, 'user', pairs)  30.8 us
    pallas_call x3, Pallas kernels, tile_pass(): pl.pallas_call(functools.partial(tile_kernel, stratum, noise_scale, devic...  7.41 us
    unnamed x23, local copies, waits for them, and re-layouts  4.04 us
  transfers between devices with their start and end apart: 30, of which 20 were waited for; matrix products, arithmetic and copies ran while one was open for 0% of the time, Pallas kernels for 8%

profile of v6, /device:TPU:0, one launch (start us, length us, event | category | flops | bytes accessed | tf_op | source)
XLA Modules:
  0.0 128.4 jit_solution(3911804995188373905)
XLA Ops:
  2.8 1.2 copy-done.7
  4.0 1.6 %first_pass.1 = (f32[384,128]{1,0:T(8,128)S(1)}, f32[384,128]{1,0:T(8,128)S(1)}, f32[1024,128]{1,0:T(8,128)S(1)}, f32[1024,128]{1,0:T(8,128)S(1)}, f32[256,128]{1,0:T(8,128)S(1)}) custom-call(bf16[384,1024]{1,0:T(8,128)(2,1)S(1)} %copy-done, f32[1024,256]{1,0:T(8,128)S(1)} %copy-done.7, f32[384,256]{1,0:T(8,128)S(1)} %copy-done.5), custom_call_target="tpu_custom_call" | custom-call | flops 402653184 | bytes 2097152 | tf_op jit(solution)/shard_map/first_pass/pallas_call | solution.py:196
  7.2 2.6 %tile_pass.3 = (f32[384,256]{1,0:T(8,128)S(1)}, f32[384,256]{1,0:T(8,128)S(1)}, f32[384,256]{1,0:T(8,128)S(1)}, f32[384,256]{1,0:T(8,128)S(1)}, f32[8,128]{1,0:T(8,128)S(1)}) custom-call(s32[1,3,6]{2,1,0:T(4,128)S(1)} %copy.12.codes, s32[1,3]{1,0:T(1,128)S(1)} %copy-done.9, bf16[1,3,6,128,128]{4,3,2,1,0:T(8,128)(2,1)S(1)} %copy-done.2, ...), custom_call_target="tpu_custom_call" | custom-call | flops 226492416 | bytes 1572864 | tf_op jit(solution)/shard_map/tile_pass/pallas_call | solution.py:144
  11.2 2.9 %collective-permute-start.3 = (f32[520,128]{1,0:T(8,128)S(1)}, f32[520,128]{1,0:T(8,128)S(1)}, u32[]{:S(2)}, u32[]{:S(2)}) collective-permute-start(f32[520,128]{1,0:T(8,128)S(1)} %get-tuple-element.66.sent), channel_id=1, source_target_pairs={{0,2},{1,5},{2,0},{3,7},{4,6},{5,1},{6,4},{7,3},{8,10},{9,13},{10,... | collective-permute-start | bytes 798728 | tf_op jit(solution)/shard_map/ppermute | solution.py:486
  14.1 6.7 %collective-permute-done.3.got.more = f32[520,128]{1,0:T(8,128)S(1)} collective-permute-done((f32[520,128]{1,0:T(8,128)S(1)}, f32[520,128]{1,0:T(8,128)S(1)}, u32[]{:S(2)}, u32[]{:S(2)}) %collective-permute-start.3) | collective-permute-done | bytes 266272 | tf_op jit(solution)/shard_map/ppermute | solution.py:486
  20.9 1.7 %collective-permute-start.4 = (f32[264,128]{1,0:T(8,128)S(1)}, f32[264,128]{1,0:T(8,128)S(1)}, u32[]{:S(2)}, u32[]{:S(2)}) collective-permute-start(f32[264,128]{1,0:T(8,128)S(1)} %get-tuple-element.68.sent), channel_id=1, source_target_pairs={{0,4},{1,3},{2,6},{3,1},{4,0},{5,7},{6,2},{7,5},{8,12},{9,11},{10,... | collective-permute-start | bytes 405512 | tf_op jit(solution)/shard_map/ppermute | solution.py:486
  22.5 2.5 %collective-permute-done.5.refs_0_.refs_5_ = f32[384,256]{1,0:T(8,128)S(1)} collective-permute-done((f32[384,256]{1,0:T(8,128)S(1)}, f32[384,256]{1,0:T(8,128)S(1)}, u32[]{:S(2)}, u32[]{:S(2)}) %collective-permute-start.5) | collective-permute-done | bytes 393248 | tf_op jit(solution)/shard_map/ppermute | solution.py:480
  25.1 4.2 %collective-permute-done.4.got.more = f32[264,128]{1,0:T(8,128)S(1)} collective-permute-done((f32[264,128]{1,0:T(8,128)S(1)}, f32[264,128]{1,0:T(8,128)S(1)}, u32[]{:S(2)}, u32[]{:S(2)}) %collective-permute-start.4) | collective-permute-done | bytes 135200 | tf_op jit(solution)/shard_map/ppermute | solution.py:486
  29.3 4.9 %collective-permute-start.6 = (f32[264,128]{1,0:T(8,128)S(1)}, f32[264,128]{1,0:T(8,128)S(1)}, u32[]{:S(2)}, u32[]{:S(2)}) collective-permute-start(f32[264,128]{1,0:T(8,128)S(1)} %step_pass.12.held.sent), channel_id=1, source_target_pairs={{0,8},{1,17},{2,10},{3,19},{4,12},{5,21},{6,14},{7,23},{8,0},{9,25... | collective-permute-start | bytes 405512 | tf_op jit(solution)/shard_map/ppermute | solution.py:486
  34.2 3.4 %collective-permute-done.6.got.more = f32[264,128]{1,0:T(8,128)S(1)} collective-permute-done((f32[264,128]{1,0:T(8,128)S(1)}, f32[264,128]{1,0:T(8,128)S(1)}, u32[]{:S(2)}, u32[]{:S(2)}) %collective-permute-start.6) | collective-permute-done | bytes 135200 | tf_op jit(solution)/shard_map/ppermute | solution.py:486
  37.6 2.7 %collective-permute-start.7 = (f32[264,128]{1,0:T(8,128)S(1)}, f32[264,128]{1,0:T(8,128)S(1)}, u32[]{:S(2)}, u32[]{:S(2)}) collective-permute-start(f32[264,128]{1,0:T(8,128)S(1)} %step_pass.13.held.sent), channel_id=1, source_target_pairs={{0,16},{1,9},{2,18},{3,11},{4,20},{5,13},{6,22},{7,15},{8,24},{9,1... | collective-permute-start | bytes 405512 | tf_op jit(solution)/shard_map/ppermute | solution.py:486
  40.3 4.7 %collective-permute-done.7.got = f32[264,128]{1,0:T(8,128)S(1)} collective-permute-done((f32[264,128]{1,0:T(8,128)S(1)}, f32[264,128]{1,0:T(8,128)S(1)}, u32[]{:S(2)}, u32[]{:S(2)}) %collective-permute-start.7) | collective-permute-done | bytes 135200 | tf_op jit(solution)/shard_map/ppermute | solution.py:486
  45.1 2.3 %collective-permute-start.9 = (f32[256,128]{1,0:T(8,128)S(1)}, f32[256,128]{1,0:T(8,128)S(1)}, u32[]{:S(2)}, u32[]{:S(2)}) collective-permute-start(f32[256,128]{1,0:T(8,128)S(1)} %get-tuple-element.72.part.old), channel_id=1, source_target_pairs={{0,4},{1,3},{2,6},{3,1},{4,0},{5,7},{6,2},{7,5},{8,12},{9,11},{10,... | collective-permute-start | bytes 393224 | tf_op jit(solution)/shard_map/ppermute | solution.py:486
  47.3 3.8 %collective-permute-done.9.got = f32[256,128]{1,0:T(8,128)S(1)} collective-permute-done((f32[256,128]{1,0:T(8,128)S(1)}, f32[256,128]{1,0:T(8,128)S(1)}, u32[]{:S(2)}, u32[]{:S(2)}) %collective-permute-start.9) | collective-permute-done | bytes 131104 | tf_op jit(solution)/shard_map/ppermute | solution.py:486
  51.2 2.4 %tile_pass.4 = (f32[384,256]{1,0:T(8,128)S(1)}, f32[384,256]{1,0:T(8,128)S(1)}, f32[384,256]{1,0:T(8,128)S(1)}, f32[384,256]{1,0:T(8,128)S(1)}, f32[8,128]{1,0:T...) custom-call(s32[1,3,6]{2,1,0:T(4,128)S(1)} %copy.12.codes, s32[1,3]{1,0:T(1,128)S(1)} %copy-done.9, ...), custom_call_target="tpu_custom_call" | custom-call | flops 226492416 | bytes 1572864 | tf_op jit(solution)/shard_map/tile_pass/pallas_call | solution.py:144
  55.2 2.4 %collective-permute-done.10.got = f32[512,128]{1,0:T(8,128)S(1)} collective-permute-done((f32[512,128]{1,0:T(8,128)S(1)}, f32[512,128]{1,0:T(8,128)S(1)}, u32[]{:S(2)}, u32[]{:S(2)}) %collective-permute-start.10) | collective-permute-done | bytes 262176 | tf_op jit(solution)/shard_map/ppermute | solution.py:486
  58.5 8.6 %collective-permute-done.13.got.more = f32[520,128]{1,0:T(8,128)S(1)} collective-permute-done((f32[520,128]{1,0:T(8,128)S(1)}, f32[520,128]{1,0:T(8,128)S(1)}, u32[]{:S(2)}, u32[]{:S(2)}) %collective-permute-start.13) | collective-permute-done | bytes 266272 | tf_op jit(solution)/shard_map/ppermute | solution.py:486
  67.2 4.6 %collective-permute-start.14 = (f32[264,128]{1,0:T(8,128)S(1)}, f32[264,128]{1,0:T(8,128)S(1)}, u32[]{:S(2)}, u32[]{:S(2)}) collective-permute-start(f32[264,128]{1,0:T(8,128)S(1)} %get-tuple-element.84.sent), channel_id=1, source_target_pairs={{0,4},{1,3},{2,6},{3,1},{4,0},{5,7},{6,2},{7,5},{8,12},{9,11},{10,... | collective-permute-start | bytes 405512 | tf_op jit(solution)/shard_map/ppermute | solution.py:486
  71.7 6.7 %collective-permute-done.14.got.more = f32[264,128]{1,0:T(8,128)S(1)} collective-permute-done((f32[264,128]{1,0:T(8,128)S(1)}, f32[264,128]{1,0:T(8,128)S(1)}, u32[]{:S(2)}, u32[]{:S(2)}) %collective-permute-start.14) | collective-permute-done | bytes 135200 | tf_op jit(solution)/shard_map/ppermute | solution.py:486
  79.5 4.0 %collective-permute-done.16.got.more = f32[264,128]{1,0:T(8,128)S(1)} collective-permute-done((f32[264,128]{1,0:T(8,128)S(1)}, f32[264,128]{1,0:T(8,128)S(1)}, u32[]{:S(2)}, u32[]{:S(2)}) %collective-permute-start.16) | collective-permute-done | bytes 135200 | tf_op jit(solution)/shard_map/ppermute | solution.py:486
  83.6 2.9 %collective-permute-start.17 = (f32[264,128]{1,0:T(8,128)S(1)}, f32[264,128]{1,0:T(8,128)S(1)}, u32[]{:S(2)}, u32[]{:S(2)}) collective-permute-start(f32[264,128]{1,0:T(8,128)S(1)} %step_pass.16.held.sent), channel_id=1, source_target_pairs={{0,16},{1,9},{2,18},{3,11},{4,20},{5,13},{6,22},{7,15},{8,24},{9,1... | collective-permute-start | bytes 405512 | tf_op jit(solution)/shard_map/ppermute | solution.py:486
  86.5 4.5 %collective-permute-done.17.got = f32[264,128]{1,0:T(8,128)S(1)} collective-permute-done((f32[264,128]{1,0:T(8,128)S(1)}, f32[264,128]{1,0:T(8,128)S(1)}, u32[]{:S(2)}, u32[]{:S(2)}) %collective-permute-start.17) | collective-permute-done | bytes 135200 | tf_op jit(solution)/shard_map/ppermute | solution.py:486
  91.0 2.5 %collective-permute-start.19 = (f32[256,128]{1,0:T(8,128)S(1)}, f32[256,128]{1,0:T(8,128)S(1)}, u32[]{:S(2)}, u32[]{:S(2)}) collective-permute-start(f32[256,128]{1,0:T(8,128)S(1)} %get-tuple-element.87.part), channel_id=1, source_target_pairs={{0,4},{1,3},{2,6},{3,1},{4,0},{5,7},{6,2},{7,5},{8,12},{9,11},{10,... | collective-permute-start | bytes 393224 | tf_op jit(solution)/shard_map/ppermute | solution.py:486
  93.6 4.3 %collective-permute-done.19.got = f32[256,128]{1,0:T(8,128)S(1)} collective-permute-done((f32[256,128]{1,0:T(8,128)S(1)}, f32[256,128]{1,0:T(8,128)S(1)}, u32[]{:S(2)}, u32[]{:S(2)}) %collective-permute-start.19) | collective-permute-done | bytes 131104 | tf_op jit(solution)/shard_map/ppermute | solution.py:486
  98.0 2.4 %tile_pass.5 = (f32[384,256]{1,0:T(8,128)S(1)}, f32[384,256]{1,0:T(8,128)S(1)}, f32[384,256]{1,0:T(8,128)S(1)}, f32[384,256]{1,0:T(8,128)S(1)}, f32[8,128]{1,0:T...) custom-call(s32[1,3,6]{2,1,0:T(4,128)S(1)} %copy.12.codes, s32[1,3]{1,0:T(1,128)S(1)} %copy-done.9, ...), custom_call_target="tpu_custom_call" | custom-call | flops 226492416 | bytes 1572864 | tf_op jit(solution)/shard_map/tile_pass/pallas_call | solution.py:144
  101.9 2.4 %collective-permute-done.20.got = f32[512,128]{1,0:T(8,128)S(1)} collective-permute-done((f32[512,128]{1,0:T(8,128)S(1)}, f32[512,128]{1,0:T(8,128)S(1)}, u32[]{:S(2)}, u32[]{:S(2)}) %collective-permute-start.20) | collective-permute-done | bytes 262176 | tf_op jit(solution)/shard_map/ppermute | solution.py:486
  105.6 6.4 %collective-permute-done.24.got.more = f32[520,128]{1,0:T(8,128)S(1)} collective-permute-done((f32[520,128]{1,0:T(8,128)S(1)}, f32[520,128]{1,0:T(8,128)S(1)}, u32[]{:S(2)}, u32[]{:S(2)}) %collective-permute-start.24) | collective-permute-done | bytes 266272 | tf_op jit(solution)/shard_map/ppermute | solution.py:486
  112.1 2.1 %collective-permute-start.25 = (f32[264,128]{1,0:T(8,128)S(1)}, f32[264,128]{1,0:T(8,128)S(1)}, u32[]{:S(2)}, u32[]{:S(2)}) collective-permute-start(f32[264,128]{1,0:T(8,128)S(1)} %get-tuple-element.99.sent), channel_id=1, source_target_pairs={{0,4},{1,3},{2,6},{3,1},{4,0},{5,7},{6,2},{7,5},{8,12},{9,11},{10,... | collective-permute-start | bytes 405512 | tf_op jit(solution)/shard_map/ppermute | solution.py:486
  114.2 3.0 %collective-permute-done.25.got.more = f32[264,128]{1,0:T(8,128)S(1)} collective-permute-done((f32[264,128]{1,0:T(8,128)S(1)}, f32[264,128]{1,0:T(8,128)S(1)}, u32[]{:S(2)}, u32[]{:S(2)}) %collective-permute-start.25) | collective-permute-done | bytes 135200 | tf_op jit(solution)/shard_map/ppermute | solution.py:486
  118.3 3.3 %collective-permute-done.26.got.more = f32[136,128]{1,0:T(8,128)S(1)} collective-permute-done((f32[136,128]{1,0:T(8,128)S(1)}, f32[136,128]{1,0:T(8,128)S(1)}, u32[]{:S(2)}, u32[]{:S(2)}) %collective-permute-start.26) | collective-permute-done | bytes 69664 | tf_op jit(solution)/shard_map/ppermute | solution.py:486
  121.6 1.8 %collective-permute-start.27 = (f32[72,128]{1,0:T(8,128)S(1)}, f32[72,128]{1,0:T(8,128)S(1)}, u32[]{:S(2)}, u32[]{:S(2)}) collective-permute-start(f32[72,128]{1,0:T(8,128)S(1)} %get-tuple-element.103.sent), channel_id=1, source_target_pairs={{0,16},{1,9},{2,18},{3,11},{4,20},{5,13},{6,22},{7,15},{8,24},{9,1... | collective-permute-start | bytes 110600 | tf_op jit(solution)/shard_map/ppermute | solution.py:486
  123.4 3.1 %collective-permute-done.27.got = f32[72,128]{1,0:T(8,128)S(1)} collective-permute-done((f32[72,128]{1,0:T(8,128)S(1)}, f32[72,128]{1,0:T(8,128)S(1)}, u32[]{:S(2)}, u32[]{:S(2)}) %collective-permute-start.27) | collective-permute-done | bytes 36896 | tf_op jit(solution)/shard_map/ppermute | solution.py:486
  (79 shorter events, 14.7 us)
Async XLA Ops:
  4.0 2.5 %copy-start.8 = (f32[384,256]{1,0:T(8,128)S(1)}, f32[384,256]{1,0:T(8,128)}, u32[]{:S(2)}) copy-start(f32[384,256]{1,0:T(8,128)} %refs_1_.1) | copy-start | bytes 1179652
  5.7 5.5 %collective-permute-start.1 = (f32[1024,128]{1,0:T(8,128)S(1)}, f32[1024,128]{1,0:T(8,128)S(1)}, u32[]{:S(2)}, u32[]{:S(2)}) collective-permute-start(f32[1024,128]{1,0:T(8,128)S(1)} %get-tuple-element.63), channel_id=1, source_target_pairs={{0,1},{1,0},{2,3},{3,2},{4,5},{5,4},{6,7},{7,6},{8,9},{9,8},{10,11... | collective-permute-start | bytes 1572872 | tf_op jit(solution)/shard_map/ppermute | solution.py:476
  6.4 47.8 %collective-permute-start = (f32[384,1024]{1,0:T(8,128)S(1)}, f32[384,1024]{1,0:T(8,128)S(1)}, u32[]{:S(2)}, u32[]{:S(2)}) collective-permute-start(f32[384,1024]{1,0:T(8,128)S(1)} %widen_pass.1), channel_id=1, source_target_pairs={{0,1},{1,0},{2,3},{3,2},{4,5},{5,4},{6,7},{7,6},{8,9},{9,8},{10,11... | collective-permute-start | bytes 4718600 | tf_op jit(solution)/shard_map/ppermute | solution.py:476
  9.8 1.3 %collective-permute-start.2 = (f32[8,128]{1,0:T(8,128)S(1)}, f32[8,128]{1,0:T(8,128)S(1)}, u32[]{:S(2)}, u32[]{:S(2)}) collective-permute-start(f32[8,128]{1,0:T(8,128)S(1)} %get-tuple-element.64.sent), channel_id=1, source_target_pairs={{0,1},{1,0},{2,3},{3,2},{4,5},{5,4},{6,7},{7,6},{8,9},{9,8},{10,11... | collective-permute-start | bytes 12296 | tf_op jit(solution)/shard_map/ppermute | solution.py:476
  11.2 9.6 %collective-permute-start.3 = (f32[520,128]{1,0:T(8,128)S(1)}, f32[520,128]{1,0:T(8,128)S(1)}, u32[]{:S(2)}, u32[]{:S(2)}) collective-permute-start(f32[520,128]{1,0:T(8,128)S(1)} %get-tuple-element.66.sent), channel_id=1, source_target_pairs={{0,2},{1,5},{2,0},{3,7},{4,6},{5,1},{6,4},{7,3},{8,10},{9,13},{10,... | collective-permute-start | bytes 798728 | tf_op jit(solution)/shard_map/ppermute | solution.py:486
  14.1 11.0 %collective-permute-start.5 = (f32[384,256]{1,0:T(8,128)S(1)}, f32[384,256]{1,0:T(8,128)S(1)}, u32[]{:S(2)}, u32[]{:S(2)}) collective-permute-start(f32[384,256]{1,0:T(8,128)S(1)} %get-tuple-element.69), channel_id=1, source_target_pairs={{0,1},{1,2},{2,3},{3,4},{4,5},{5,6},{6,7},{7,8},{8,9},{9,10},{10,1... | collective-permute-start | bytes 1179656 | tf_op jit(solution)/shard_map/ppermute | solution.py:480
  20.9 8.4 %collective-permute-start.4 = (f32[264,128]{1,0:T(8,128)S(1)}, f32[264,128]{1,0:T(8,128)S(1)}, u32[]{:S(2)}, u32[]{:S(2)}) collective-permute-start(f32[264,128]{1,0:T(8,128)S(1)} %get-tuple-element.68.sent), channel_id=1, source_target_pairs={{0,4},{1,3},{2,6},{3,1},{4,0},{5,7},{6,2},{7,5},{8,12},{9,11},{10,... | collective-permute-start | bytes 405512 | tf_op jit(solution)/shard_map/ppermute | solution.py:486
  22.5 17.8 %collective-permute-start.8 = (f32[384,256]{1,0:T(8,128)S(1)}, f32[384,256]{1,0:T(8,128)S(1)}, u32[]{:S(2)}, u32[]{:S(2)}) collective-permute-start(f32[384,256]{1,0:T(8,128)S(1)} %get-tuple-element.71), channel_id=1, source_target_pairs={{0,1},{1,2},{2,3},{3,4},{4,5},{5,6},{6,7},{7,8},{8,9},{9,10},{10,1... | collective-permute-start | bytes 1179656 | tf_op jit(solution)/shard_map/ppermute | solution.py:480
  29.3 8.3 %collective-permute-start.6 = (f32[264,128]{1,0:T(8,128)S(1)}, f32[264,128]{1,0:T(8,128)S(1)}, u32[]{:S(2)}, u32[]{:S(2)}) collective-permute-start(f32[264,128]{1,0:T(8,128)S(1)} %step_pass.12.held.sent), channel_id=1, source_target_pairs={{0,8},{1,17},{2,10},{3,19},{4,12},{5,21},{6,14},{7,23},{8,0},{9,25... | collective-permute-start | bytes 405512 | tf_op jit(solution)/shard_map/ppermute | solution.py:486
  37.6 7.4 %collective-permute-start.7 = (f32[264,128]{1,0:T(8,128)S(1)}, f32[264,128]{1,0:T(8,128)S(1)}, u32[]{:S(2)}, u32[]{:S(2)}) collective-permute-start(f32[264,128]{1,0:T(8,128)S(1)} %step_pass.13.held.sent), channel_id=1, source_target_pairs={{0,16},{1,9},{2,18},{3,11},{4,20},{5,13},{6,22},{7,15},{8,24},{9,1... | collective-permute-start | bytes 405512 | tf_op jit(solution)/shard_map/ppermute | solution.py:486
  45.1 6.1 %collective-permute-start.9 = (f32[256,128]{1,0:T(8,128)S(1)}, f32[256,128]{1,0:T(8,128)S(1)}, u32[]{:S(2)}, u32[]{:S(2)}) collective-permute-start(f32[256,128]{1,0:T(8,128)S(1)} %get-tuple-element.72.part.old), channel_id=1, source_target_pairs={{0,4},{1,3},{2,6},{3,1},{4,0},{5,7},{6,2},{7,5},{8,12},{9,11},{10,... | collective-permute-start | bytes 393224 | tf_op jit(solution)/shard_map/ppermute | solution.py:486
  51.1 6.4 %collective-permute-start.10 = (f32[512,128]{1,0:T(8,128)S(1)}, f32[512,128]{1,0:T(8,128)S(1)}, u32[]{:S(2)}, u32[]{:S(2)}) collective-permute-start(f32[512,128]{1,0:T(8,128)S(1)} %gather_pass.2.part), channel_id=1, source_target_pairs={{0,2},{1,5},{2,0},{3,7},{4,6},{5,1},{6,4},{7,3},{8,10},{9,13},{10,... | collective-permute-start | bytes 786440 | tf_op jit(solution)/shard_map/ppermute | solution.py:486
  51.2 3.0 %copy-start.1 = (bf16[384,1024]{1,0:T(8,128)(2,1)S(1)}, bf16[384,1024]{1,0:T(8,128)(2,1)}, u32[]{:S(2)}) copy-start(bf16[384,1024]{1,0:T(8,128)(2,1)} %feats_in.1) | copy-start | bytes 2359300
  53.6 1.5 %collective-permute-start.11 = (f32[384,128]{1,0:T(8,128)S(1)}, f32[384,128]{1,0:T(8,128)S(1)}, u32[]{:S(2)}, u32[]{:S(2)}) collective-permute-start(f32[384,128]{1,0:T(8,128)S(1)} %get-tuple-element.79), channel_id=1, source_target_pairs={{0,1},{1,0},{2,3},{3,2},{4,5},{5,4},{6,7},{7,6},{8,9},{9,8},{10,11... | collective-permute-start | bytes 589832 | tf_op jit(solution)/shard_map/ppermute | solution.py:476
  53.7 1.4 %collective-permute-start.12 = (f32[8,128]{1,0:T(8,128)S(1)}, f32[8,128]{1,0:T(8,128)S(1)}, u32[]{:S(2)}, u32[]{:S(2)}) collective-permute-start(f32[8,128]{1,0:T(8,128)S(1)} %get-tuple-element.80.stats), channel_id=1, source_target_pairs={{0,1},{1,0},{2,3},{3,2},{4,5},{5,4},{6,7},{7,6},{8,9},{9,8},{10,11... | collective-permute-start | bytes 12296 | tf_op jit(solution)/shard_map/ppermute | solution.py:476
  58.4 8.7 %collective-permute-start.13 = (f32[520,128]{1,0:T(8,128)S(1)}, f32[520,128]{1,0:T(8,128)S(1)}, u32[]{:S(2)}, u32[]{:S(2)}) collective-permute-start(f32[520,128]{1,0:T(8,128)S(1)} %get-tuple-element.82.sent), channel_id=1, source_target_pairs={{0,2},{1,5},{2,0},{3,7},{4,6},{5,1},{6,4},{7,3},{8,10},{9,13},{10,... | collective-permute-start | bytes 798728 | tf_op jit(solution)/shard_map/ppermute | solution.py:486
  58.5 13.2 %collective-permute-start.15 = (f32[384,256]{1,0:T(8,128)S(1)}, f32[384,256]{1,0:T(8,128)S(1)}, u32[]{:S(2)}, u32[]{:S(2)}) collective-permute-start(f32[384,256]{1,0:T(8,128)S(1)} %get-tuple-element.85), channel_id=1, source_target_pairs={{0,1},{1,2},{2,3},{3,4},{4,5},{5,6},{6,7},{7,8},{8,9},{9,10},{10,1... | collective-permute-start | bytes 1179656 | tf_op jit(solution)/shard_map/ppermute | solution.py:480
  67.2 11.3 %collective-permute-start.14 = (f32[264,128]{1,0:T(8,128)S(1)}, f32[264,128]{1,0:T(8,128)S(1)}, u32[]{:S(2)}, u32[]{:S(2)}) collective-permute-start(f32[264,128]{1,0:T(8,128)S(1)} %get-tuple-element.84.sent), channel_id=1, source_target_pairs={{0,4},{1,3},{2,6},{3,1},{4,0},{5,7},{6,2},{7,5},{8,12},{9,11},{10,... | collective-permute-start | bytes 405512 | tf_op jit(solution)/shard_map/ppermute | solution.py:486
  71.7 14.8 %collective-permute-start.18 = (f32[384,256]{1,0:T(8,128)S(1)}, f32[384,256]{1,0:T(8,128)S(1)}, u32[]{:S(2)}, u32[]{:S(2)}) collective-permute-start(f32[384,256]{1,0:T(8,128)S(1)} %get-tuple-element.86), channel_id=1, source_target_pairs={{0,1},{1,2},{2,3},{3,4},{4,5},{5,6},{6,7},{7,8},{8,9},{9,10},{10,1... | collective-permute-start | bytes 1179656 | tf_op jit(solution)/shard_map/ppermute | solution.py:480
  78.5 5.1 %collective-permute-start.16 = (f32[264,128]{1,0:T(8,128)S(1)}, f32[264,128]{1,0:T(8,128)S(1)}, u32[]{:S(2)}, u32[]{:S(2)}) collective-permute-start(f32[264,128]{1,0:T(8,128)S(1)} %step_pass.15.held.sent), channel_id=1, source_target_pairs={{0,8},{1,17},{2,10},{3,19},{4,12},{5,21},{6,14},{7,23},{8,0},{9,25... | collective-permute-start | bytes 405512 | tf_op jit(solution)/shard_map/ppermute | solution.py:486
  83.6 7.4 %collective-permute-start.17 = (f32[264,128]{1,0:T(8,128)S(1)}, f32[264,128]{1,0:T(8,128)S(1)}, u32[]{:S(2)}, u32[]{:S(2)}) collective-permute-start(f32[264,128]{1,0:T(8,128)S(1)} %step_pass.16.held.sent), channel_id=1, source_target_pairs={{0,16},{1,9},{2,18},{3,11},{4,20},{5,13},{6,22},{7,15},{8,24},{9,1... | collective-permute-start | bytes 405512 | tf_op jit(solution)/shard_map/ppermute | solution.py:486
  86.5 11.5 %collective-permute-start.21 = (f32[384,128]{1,0:T(8,128)S(1)}, f32[384,128]{1,0:T(8,128)S(1)}, u32[]{:S(2)}, u32[]{:S(2)}) collective-permute-start(f32[384,128]{1,0:T(8,128)S(1)} %get-tuple-element.91), channel_id=1, source_target_pairs={{0,1},{1,0},{2,3},{3,2},{4,5},{5,4},{6,7},{7,6},{8,9},{9,8},{10,11... | collective-permute-start | bytes 589832 | tf_op jit(solution)/shard_map/ppermute | solution.py:476
  91.0 6.8 %collective-permute-start.19 = (f32[256,128]{1,0:T(8,128)S(1)}, f32[256,128]{1,0:T(8,128)S(1)}, u32[]{:S(2)}, u32[]{:S(2)}) collective-permute-start(f32[256,128]{1,0:T(8,128)S(1)} %get-tuple-element.87.part), channel_id=1, source_target_pairs={{0,4},{1,3},{2,6},{3,1},{4,0},{5,7},{6,2},{7,5},{8,12},{9,11},{10,... | collective-permute-start | bytes 393224 | tf_op jit(solution)/shard_map/ppermute | solution.py:486
  97.9 6.4 %collective-permute-start.20 = (f32[512,128]{1,0:T(8,128)S(1)}, f32[512,128]{1,0:T(8,128)S(1)}, u32[]{:S(2)}, u32[]{:S(2)}) collective-permute-start(f32[512,128]{1,0:T(8,128)S(1)} %gather_pass.3.part), channel_id=1, source_target_pairs={{0,2},{1,5},{2,0},{3,7},{4,6},{5,1},{6,4},{7,3},{8,10},{9,13},{10,... | collective-permute-start | bytes 786440 | tf_op jit(solution)/shard_map/ppermute | solution.py:486
  100.4 1.5 %collective-permute-start.22 = (f32[384,128]{1,0:T(8,128)S(1)}, f32[384,128]{1,0:T(8,128)S(1)}, u32[]{:S(2)}, u32[]{:S(2)}) collective-permute-start(f32[384,128]{1,0:T(8,128)S(1)} %get-tuple-element.94), channel_id=1, source_target_pairs={{0,1},{1,0},{2,3},{3,2},{4,5},{5,4},{6,7},{7,6},{8,9},{9,8},{10,11... | collective-permute-start | bytes 589832 | tf_op jit(solution)/shard_map/ppermute | solution.py:476
  100.5 1.4 %collective-permute-start.23 = (f32[8,128]{1,0:T(8,128)S(1)}, f32[8,128]{1,0:T(8,128)S(1)}, u32[]{:S(2)}, u32[]{:S(2)}) collective-permute-start(f32[8,128]{1,0:T(8,128)S(1)} %get-tuple-element.95.stats), channel_id=1, source_target_pairs={{0,1},{1,0},{2,3},{3,2},{4,5},{5,4},{6,7},{7,6},{8,9},{9,8},{10,11... | collective-permute-start | bytes 12296 | tf_op jit(solution)/shard_map/ppermute | solution.py:476
  105.6 6.5 %collective-permute-start.24 = (f32[520,128]{1,0:T(8,128)S(1)}, f32[520,128]{1,0:T(8,128)S(1)}, u32[]{:S(2)}, u32[]{:S(2)}) collective-permute-start(f32[520,128]{1,0:T(8,128)S(1)} %get-tuple-element.97.sent), channel_id=1, source_target_pairs={{0,2},{1,5},{2,0},{3,7},{4,6},{5,1},{6,4},{7,3},{8,10},{9,13},{10,... | collective-permute-start | bytes 798728 | tf_op jit(solution)/shard_map/ppermute | solution.py:486
  112.1 5.1 %collective-permute-start.25 = (f32[264,128]{1,0:T(8,128)S(1)}, f32[264,128]{1,0:T(8,128)S(1)}, u32[]{:S(2)}, u32[]{:S(2)}) collective-permute-start(f32[264,128]{1,0:T(8,128)S(1)} %get-tuple-element.99.sent), channel_id=1, source_target_pairs={{0,4},{1,3},{2,6},{3,1},{4,0},{5,7},{6,2},{7,5},{8,12},{9,11},{10,... | collective-permute-start | bytes 405512 | tf_op jit(solution)/shard_map/ppermute | solution.py:486
  114.2 12.4 %collective-permute-start.28 = (f32[384,128]{1,0:T(8,128)S(1)}, f32[384,128]{1,0:T(8,128)S(1)}, u32[]{:S(2)}, u32[]{:S(2)}) collective-permute-start(f32[384,128]{1,0:T(8,128)S(1)} %get-tuple-element.109), channel_id=1, source_target_pairs={{0,1},{1,0},{2,3},{3,2},{4,5},{5,4},{6,7},{7,6},{8,9},{9,8},{10,11... | collective-permute-start | bytes 589832 | tf_op jit(solution)/shard_map/ppermute | solution.py:476
  117.2 4.4 %collective-permute-start.26 = (f32[136,128]{1,0:T(8,128)S(1)}, f32[136,128]{1,0:T(8,128)S(1)}, u32[]{:S(2)}, u32[]{:S(2)}) collective-permute-start(f32[136,128]{1,0:T(8,128)S(1)} %get-tuple-element.101.sent), channel_id=1, source_target_pairs={{0,8},{1,17},{2,10},{3,19},{4,12},{5,21},{6,14},{7,23},{8,0},{9,25... | collective-permute-start | bytes 208904 | tf_op jit(solution)/shard_map/ppermute | solution.py:486
  121.6 4.9 %collective-permute-start.27 = (f32[72,128]{1,0:T(8,128)S(1)}, f32[72,128]{1,0:T(8,128)S(1)}, u32[]{:S(2)}, u32[]{:S(2)}) collective-permute-start(f32[72,128]{1,0:T(8,128)S(1)} %get-tuple-element.103.sent), channel_id=1, source_target_pairs={{0,16},{1,9},{2,18},{3,11},{4,20},{5,13},{6,22},{7,15},{8,24},{9,1... | collective-permute-start | bytes 110600 | tf_op jit(solution)/shard_map/ppermute | solution.py:486
  126.6 1.2 collective-permute-start.29
  (9 other events, 11.0 us)

commit v7 on v6

--- a/solution.py
+++ b/solution.py
@@ -15,6 +15,7 @@
 rate_scale = 0.04
 
 CORES = 2
+CHUNKS = 2
 RIDERS = 8
 NN = (((1,), (0,)), ((), ()))
 NT = (((1,), (1,)), ((), ()))
@@ -40,12 +41,17 @@
     return pl.CostEstimate(flops=flops, bytes_accessed=size, transcendentals=0)
 
 
-def where_am_i(devices):
+def where_am_i(devices, chunk=0):
     own = lax.axis_index("user")
     core = own & 1
-    zero, one = (bit_order(devices, c) for c in range(CORES))
+    zero, one = (bit_order(devices, c, chunk) for c in range(CORES))
     bits = [jnp.where(core == 0, own >> z, own >> o) & 1 for z, o in zip(zero, one, strict=True)]
     return [core, *bits, own >> 1]
+
+
+def rows_at(which, rows):
+    start = which * rows
+    return pl.ds(pl.multiple_of(start, rows) if rows % 8 == 0 else start, rows)
 
 
 def half_of(ref, core):
@@ -162,7 +168,9 @@
     )(codes, count, ratings, user_noise, item_noise, *state)
 
 
-def first_kernel(devices, feats_in, weights_in, users_in, own_mean, other_mean, send, keep, old, mean, feats, weights, users, sems):
+def first_kernel(devices, feats_in, weights_in, users_in, own_mean, other_mean, *refs):
+    sends, keeps, olds = refs[:CHUNKS], refs[CHUNKS : 2 * CHUNKS], refs[2 * CHUNKS : 3 * CHUNKS]
+    mean, feats, weights, users, sems = refs[3 * CHUNKS :]
     copies = [
         pltpu.make_async_copy(source, target, sems.at[n])
         for n, (source, target) in enumerate(
@@ -171,33 +179,38 @@
     ]
     for copy in copies:
         copy.start()
-    place = where_am_i(devices)
-    here = place[0]
+    here = where_am_i(devices)[0]
     copies[0].wait()
     weights_b = weights[...].astype(bf16)
     copies[1].wait()
     mean[...] = dot(feats[...], weights_b)
     copies[2].wait()
-    for grad, means, which in ((send, other_mean, 1 - here), (keep, own_mean, here)):
+    for grads, means, which in ((sends, other_mean, 1 - here), (keeps, own_mean, here)):
         mean_now = half_of(mean, which)
         means[...] = mean_now
         offset = (half_of(users, which) - mean_now).astype(bf16)
-        grad[...] = dot(feats[...], offset, TN)
-    rows, width = old.shape
-    start = place[1] * (weights.shape[0] // 2) + place[2] * rows
-    cols = pl.ds(pl.multiple_of(here * width, width), width)
-    old[...] = weights[pl.ds(pl.multiple_of(start, rows), rows), cols]
+        for chunk, grad in enumerate(grads):
+            depth = grad.shape[0]
+            grad[...] = dot(feats[:, chunk * depth : (chunk + 1) * depth], offset, TN)
+    for chunk, old in enumerate(olds):
+        rows, width = old.shape
+        _, first, second, *_ = where_am_i(devices, chunk)
+        cols = pl.ds(pl.multiple_of(here * width, width), width)
+        old[...] = weights[rows_at(chunk * 4 + first * 2 + second, rows), cols]
 
 
 def first_pass(devices, feats, weights, users):
     rows, rank = users.shape
     feat = weights.shape[0]
     width = rank // CORES
+    depth = feat // CHUNKS
     return pl.pallas_call(
         functools.partial(first_kernel, devices),
-        out_shape=(shape(rows, width),) * 2 + (shape(feat, width),) * 2 + (shape(feat // 4, width),),
+        out_shape=(shape(rows, width),) * 2
+        + (shape(depth, width),) * (2 * CHUNKS)
+        + (shape(depth // 4, width),) * CHUNKS,
         in_specs=[HBM] * 3,
-        out_specs=(VMEM,) * 5,
+        out_specs=(VMEM,) * (2 + 3 * CHUNKS),
         scratch_shapes=[
             pltpu.VMEM(users.shape, f32),
             pltpu.VMEM(feats.shape, bf16),
@@ -251,148 +264,194 @@
     )(own, other)
 
 
-def part_kernel(devices, feats, part, mean):
+def halves_mean(feats, chunk, bit, part, got):
     half = part.shape[0]
-    bit = where_am_i(devices)[1]
-    here = pl.ds(pl.multiple_of(bit * half, half), half)
-    mean[...] = dot(feats[:, here], part[...].astype(bf16))
-
-
-def part_pass(devices, feats, part):
+    return dot(feats[:, rows_at(2 * chunk + bit, half)], part[...].astype(bf16)) + dot(
+        feats[:, rows_at(2 * chunk + 1 - bit, half)], got[...].astype(bf16)
+    )
+
+
+def part_kernel(devices, feats, part, got, mean):
+    mean[...] = halves_mean(feats, 0, where_am_i(devices)[1], part, got)
+
+
+def part_pass(devices, feats, part, got):
     rows = feats.shape[0]
     half, width = part.shape
     return pl.pallas_call(
         functools.partial(part_kernel, devices),
         out_shape=shape(rows, width),
-        in_specs=[VMEM, VMEM],
+        in_specs=[VMEM] * 3,
         out_specs=VMEM,
         compiler_params=PARAMS,
-        cost_estimate=cost(2 * rows * half * width, 4 * rows * half),
+        cost_estimate=cost(4 * rows * half * width, 4 * rows * half),
         name="part_pass",
-    )(feats, part)
-
-
-def prior_kernel(places, devices, feats, turned, begun, part, got, own_cols, other_cols, stats, more_stats, own_mean, other_mean, send, keep, *refs):
+    )(feats, part, got)
+
+
+def find_offset(devices, feats, begun, part, got, own_cols, other_cols, own_mean, other_mean, offset):
     rows = own_cols.shape[0]
-    half = keep.shape[0]
-    place = where_am_i(devices)
-    core, bit = place[0], place[1]
-    here = pl.ds(pl.multiple_of(bit * half, half), half)
-    there = pl.ds(pl.multiple_of((1 - bit) * half, half), half)
-    offset = refs[-1]
-    mean = begun[...] + dot(feats[:, there], got[...].astype(bf16))
+    mean = begun[...] + halves_mean(feats, 1, where_am_i(devices, 1)[1], part, got)
     own_mean[...] = mean[:rows]
     other_mean[...] = mean[rows:]
     offset[:rows, :] = (own_cols[...] - mean[:rows]).astype(bf16)
     offset[rows:, :] = (other_cols[...] - mean[rows:]).astype(bf16)
+
+
+def prior_kernel(devices, feats, turned, begun, part, got, own_cols, other_cols, own_mean, other_mean, offset, send, keep):
+    find_offset(devices, feats, begun, part, got, own_cols, other_cols, own_mean, other_mean, offset)
+    bit = where_am_i(devices)[1]
+    half = keep.shape[0]
+    send[...] = dot(turned[rows_at(1 - bit, half), :], offset[...])
+    keep[...] = dot(turned[rows_at(bit, half), :], offset[...])
+
+
+def prior_pass(devices, feats, turned, begun, part, got, own_cols, other_cols):
+    rows, width = own_cols.shape
+    half = part.shape[0]
+    return pl.pallas_call(
+        functools.partial(prior_kernel, devices),
+        out_shape=(shape(rows, width),) * 2
+        + (shape(CORES * rows, width, dtype=bf16),)
+        + (shape(half, width),) * 2,
+        in_specs=[VMEM] * 7,
+        out_specs=(VMEM,) * 5,
+        compiler_params=PARAMS,
+        cost_estimate=cost(16 * rows * half * width, 16 * rows * half),
+        name="prior_pass",
+    )(feats, turned, begun, part, got, own_cols, other_cols)
+
+
+def rest_kernel(devices, turned, offset, stats, more_stats, send, keep):
+    bit = where_am_i(devices, 1)[1]
+    half = keep.shape[0]
+    send[:half, :] = dot(turned[rows_at(2 + 1 - bit, half), :], offset[...])
+    keep[...] = dot(turned[rows_at(2 + bit, half), :], offset[...])
     send[half:, :] = stats[...] + more_stats[...]
-    if places is None:
-        send[:half, :] = dot(turned[there, :], offset[...])
-        keep[...] = dot(turned[here, :], offset[...])
-        return
-    old, full = refs[:2]
-    full[here, :] = part[...]
-    full[there, :] = got[...]
-    start = place[-1] * old.shape[0]
-    if old.shape[0] % 8 == 0:
-        start = pl.multiple_of(start, old.shape[0])
-    old[...] = full[pl.ds(start, old.shape[0]), :]
+
+
+def rest_pass(devices, turned, offset, stats, more_stats):
+    rows, width = offset.shape
+    half = turned.shape[0] // (2 * CHUNKS)
+    return pl.pallas_call(
+        functools.partial(rest_kernel, devices),
+        out_shape=(shape(half + RIDERS, width), shape(half, width)),
+        in_specs=[VMEM] * 4,
+        out_specs=(VMEM,) * 2,
+        compiler_params=PARAMS,
+        cost_estimate=cost(4 * rows * half * width, 4 * rows * half),
+        name="rest_pass",
+    )(turned, offset, stats, more_stats)
+
+
+def final_kernel(places, devices, feats, turned, begun, part, got, first_part, first_got, own_cols, other_cols, stats, more_stats, own_mean, other_mean, send, keep, old, full, offset):
+    find_offset(devices, feats, begun, part, got, own_cols, other_cols, own_mean, other_mean, offset)
+    send[keep.shape[0] :, :] = stats[...] + more_stats[...]
+    rows = part.shape[0]
+    place = where_am_i(devices)
+    for chunk, mine, theirs in ((0, first_part, first_got), (1, part, got)):
+        bit = where_am_i(devices, chunk)[1]
+        full[rows_at(2 * chunk + bit, rows), :] = mine[...]
+        full[rows_at(2 * chunk + 1 - bit, rows), :] = theirs[...]
+    old[...] = full[rows_at(place[-1], old.shape[0]), :]
     full[...] = dot(turned[...], offset[...])
+    core, bit = place[0], place[1]
     blocks = len(places[0])
-    block = 2 * half // blocks
+    block = full.shape[0] // blocks
     for ref, which in ((send, 1 - bit), (keep, bit)):
         for n in range(blocks // 2):
             source = jnp.int32(0)
             for c, order in enumerate(places):
                 for b in range(2):
                     source = jnp.where((core == c) & (which == b), order[b * blocks // 2 + n], source)
-            source = source * block
-            if block % 8 == 0:
-                source = pl.multiple_of(source, block)
-            ref[n * block : (n + 1) * block, :] = full[pl.ds(source, block), :]
-
-
-def prior_pass(devices, feats, turned, begun, part, got, own_cols, other_cols, stats, more_stats, places=None):
+            ref[n * block : (n + 1) * block, :] = full[rows_at(source, block), :]
+
+
+def final_pass(places, devices, feats, turned, begun, part, got, first_part, first_got, own_cols, other_cols, stats, more_stats):
     rows, width = own_cols.shape
-    half = part.shape[0]
-    outs = [shape(rows, width)] * 2 + [shape(half + stats.shape[0], width), shape(half, width)]
-    scratch = [pltpu.VMEM((CORES * rows, width), bf16)]
-    if places is not None:
-        outs.append(shape(2 * half // len(places[0]), width))
-        scratch.insert(0, pltpu.VMEM((2 * half, width), f32))
-    return pl.pallas_call(
-        functools.partial(prior_kernel, places, devices),
-        out_shape=tuple(outs),
-        in_specs=[VMEM] * 9,
-        out_specs=(VMEM,) * len(outs),
-        scratch_shapes=scratch,
-        compiler_params=PARAMS,
-        cost_estimate=cost(16 * rows * half * width, 16 * rows * half),
-        name="prior_pass",
-    )(feats, turned, begun, part, got, own_cols, other_cols, stats, more_stats)
-
-
-def step_kernel(halving, slot, devices, held, got, sent, more, *refs):
+    feat = feats.shape[1]
+    return pl.pallas_call(
+        functools.partial(final_kernel, places, devices),
+        out_shape=(shape(rows, width),) * 2
+        + (shape(feat // 2 + RIDERS, width), shape(feat // 2, width), shape(feat // len(places[0]), width)),
+        in_specs=[VMEM] * 11,
+        out_specs=(VMEM,) * 5,
+        scratch_shapes=[pltpu.VMEM((feat, width), f32), pltpu.VMEM((CORES * rows, width), bf16)],
+        compiler_params=PARAMS,
+        cost_estimate=cost(8 * rows * feat * width, 8 * rows * feat),
+        name="final_pass",
+    )(feats, turned, begun, part, got, first_part, first_got, own_cols, other_cols, stats, more_stats)
+
+
+def step_kernel(halving, stage, chunk, riders, devices, held, got, *refs):
     send = refs[-2] if halving else refs[-1]
-    riders = sent.shape[0] - RIDERS, more.shape[0] - RIDERS
-    rider = sent[riders[0] :, :] + more[riders[1] :, :]
-    rows = send.shape[0] - RIDERS
+    rows = send.shape[0] - riders
     if halving:
-        bit = where_am_i(devices)[slot]
+        bit = where_am_i(devices, chunk)[1 + stage]
         for ref, which in ((send, 1 - bit), (refs[-1], bit)):
-            at = pl.ds(pl.multiple_of(which * rows, 8), rows) if rows % 8 == 0 else pl.ds(which * rows, rows)
+            at = rows_at(which, rows)
             ref[:rows, :] = held[at, :] + got[at, :]
     else:
         send[:rows, :] = held[:rows, :] + got[:rows, :]
-    send[rows:, :] = rider
-
-
-def step_pass(halving, stage, devices, held, got, sent, more, rows, later=()):
+    if riders:
+        sent, more = refs[:2]
+        send[rows:, :] = sent[sent.shape[0] - riders :, :] + more[more.shape[0] - riders :, :]
+
+
+def step_pass(halving, stage, chunk, devices, held, got, rows, riders=(), later=()):
     width = held.shape[1]
-    outs = [shape(rows // 2 + RIDERS, width), shape(rows // 2, width)] if halving else [shape(rows + RIDERS, width)]
-    return pl.pallas_call(
-        functools.partial(step_kernel, halving, 1 + stage, devices),
+    under = RIDERS if riders else 0
+    outs = [shape(rows // 2 + under, width), shape(rows // 2, width)] if halving else [shape(rows + under, width)]
+    return pl.pallas_call(
+        functools.partial(step_kernel, halving, stage, chunk, under, devices),
         out_shape=tuple(outs),
-        in_specs=[VMEM] * 4 + [ANY] * len(later),
+        in_specs=[VMEM] * (2 + len(riders)) + [ANY] * len(later),
         out_specs=(VMEM,) * len(outs),
         compiler_params=PARAMS,
         cost_estimate=cost(rows * width, 12 * rows * width),
         name="step_pass",
-    )(held, got, sent, more, *later)
-
-
-def update_kernel(rate, held, got, sent, old, *refs):
-    new, stats = refs[-2:]
+    )(held, got, *riders, *later)
+
+
+def update_kernel(rate, riding, held, got, old, *refs):
     rows = old.shape[0]
+    new = refs[-2] if riding else refs[-1]
     total = held[:rows, :] + got[:rows, :]
     before = old[...]
     new[...] = before + rate * (prior_prec * total - weight_decay * before)
-    stats[...] = sent[sent.shape[0] - RIDERS :, :] + got[rows:, :]
-
-
-def update_pass(rate, held, got, sent, old, later=()):
-    return pl.pallas_call(
-        functools.partial(update_kernel, rate),
-        out_shape=(shape(*old.shape), shape(RIDERS, old.shape[1])),
-        in_specs=[VMEM] * 4 + [ANY] * len(later),
-        out_specs=(VMEM,) * 2,
+    if riding:
+        refs[-1][...] = held_stats(refs[0]) + got[rows:, :]
+
+
+def held_stats(sent):
+    return sent[sent.shape[0] - RIDERS :, :]
+
+
+def update_pass(rate, held, got, old, sent=None, later=()):
+    riding = sent is not None
+    out = shape(*old.shape)
+    return pl.pallas_call(
+        functools.partial(update_kernel, rate, riding),
+        out_shape=(out, shape(RIDERS, old.shape[1])) if riding else out,
+        in_specs=[VMEM] * (3 + riding) + [ANY] * len(later),
+        out_specs=(VMEM,) * 2 if riding else VMEM,
         compiler_params=PARAMS,
         cost_estimate=cost(4 * old.size, 16 * old.size),
         name="update_pass",
-    )(held, got, sent, old, *later)
-
-
-def gather_kernel(slot, devices, part, got, both):
+    )(held, got, old, *([sent] if riding else []), *later)
+
+
+def gather_kernel(stage, chunk, devices, part, got, both):
     rows = part.shape[0]
-    bit = where_am_i(devices)[slot]
-    both[pl.ds(pl.multiple_of(bit * rows, rows), rows), :] = part[...]
-    both[pl.ds(pl.multiple_of((1 - bit) * rows, rows), rows), :] = got[...]
-
-
-def gather_pass(stage, devices, part, got):
+    bit = where_am_i(devices, chunk)[1 + stage]
+    both[rows_at(bit, rows), :] = part[...]
+    both[rows_at(1 - bit, rows), :] = got[...]
+
+
+def gather_pass(stage, chunk, devices, part, got):
     rows, width = part.shape
     return pl.pallas_call(
-        functools.partial(gather_kernel, 1 + stage, devices),
+        functools.partial(gather_kernel, stage, chunk, devices),
         out_shape=shape(2 * rows, width),
         in_specs=[VMEM, VMEM],
         out_specs=VMEM,
@@ -466,10 +525,11 @@
     )(stats, base, *state)
 
 
-def bit_order(devices, core):
+def bit_order(devices, core, chunk=0):
     bits = devices.bit_length() - 1
+    near = [1, 2] if core == chunk else [2, 1]
     far = list(range(3, bits))
-    return [1, 2] + far if core == 0 else [2, 1] + far[::-1]
+    return near + (far if chunk == 0 else far[::-1])
 
 
 def swap(array, devices):
@@ -480,8 +540,8 @@
     return lax.ppermute(array, "user", [(i, (i + 1) % devices) for i in range(devices)])
 
 
-def exchange(array, devices, stage):
-    orders = [bit_order(devices, core) for core in range(CORES)]
+def exchange(array, devices, stage, chunk=0):
+    orders = [bit_order(devices, core, chunk) for core in range(CORES)]
     pairs = [(i, i ^ (1 << orders[i & 1][stage])) for i in range(devices)]
     return lax.ppermute(array, "user", pairs)
 
@@ -518,60 +578,75 @@
     rate = rate_scale / (user_factors.shape[0] * devices)
     tables = (devices, tile_index, tile_count, ratings, user_noise, item_noise)
 
-    own_mean, other_mean, send, held, old = first_pass(
+    both = range(CHUNKS)
+    depth = feat // CHUNKS
+    own_mean, other_mean, *outs = first_pass(
         devices, side_features, prior_weights, user_factors
     )
-    got = swap(send, devices)
+    helds, olds = outs[CHUNKS : 2 * CHUNKS], outs[2 * CHUNKS :]
+    gots = [swap(send, devices) for send in outs[:CHUNKS]]
     base, grad, base_v, grad_v, stats = tile_pass(0, *tables, user_factors, item_factors)
     more = swap(stats, devices)
-    send, held = step_pass(True, 0, devices, held, got, stats, more, feat)
+    sends = [None] * CHUNKS
+    for c in both:
+        riders = (stats, more) if c else ()
+        sends[c], helds[c] = step_pass(True, 0, c, devices, helds[c], gots[c], depth, riders)
     feats, turned = join_pass(side_features, swap(widen_pass(side_features), devices))
-    for stratum in range(strata):
-        last = stratum + 1 == strata
-        if not last:
-            base_v, grad_v = roll(base_v, devices), roll(grad_v, devices)
-        got = exchange(send, devices, 0)
-        send, held = step_pass(True, 1, devices, held, got, send, got, feat // 2)
-        for stage in range(1, stages - 1):
-            got = exchange(send, devices, stage)
-            rows = got.shape[0] - RIDERS
-            if last:
-                send, held = step_pass(True, stage + 1, devices, held, got, send, got, rows)
+    for stratum in range(strata - 1):
+        base_v, grad_v = roll(base_v, devices), roll(grad_v, devices)
+        for stage in range(stages - 1):
+            for c in both:
+                gots[c] = exchange(sends[c], devices, stage, c)
+                riders = (sends[c], gots[c]) if c else ()
+                rows = gots[c].shape[0] - RIDERS * c
+                if stage < 1:
+                    sends[c], helds[c] = step_pass(True, stage + 1, c, devices, helds[c], gots[c], rows, riders)
+                else:
+                    (sends[c],) = step_pass(False, 0, c, devices, helds[c], gots[c], rows, riders)
+                    helds[c] = sends[c]
+        for c in both:
+            gots[c] = exchange(sends[c], devices, stages - 1, c)
+            if c:
+                olds[c], stats = update_pass(rate, helds[c], gots[c], olds[c], sends[c])
             else:
-                later = (base_v,) if stage == 1 else ()
-                (send,) = step_pass(False, 0, devices, held, got, send, got, rows, later)
-                held = send
-        got = exchange(send, devices, stages - 1)
-        part, stats = update_pass(rate, held, got, send, old, () if last else (grad_v,))
-        if last:
-            break
-        old = part
-        got = exchange(part, devices, 1)
-        part = gather_pass(1, devices, part, got)
-        got = exchange(part, devices, 0)
-        begun = part_pass(devices, feats, part)
+                olds[c] = update_pass(rate, helds[c], gots[c], olds[c])
+        parts = list(olds)
+        for c in both:
+            parts[c] = gather_pass(1, c, devices, parts[c], exchange(parts[c], devices, 1, c))
+        gots = [exchange(parts[c], devices, 0, c) for c in both]
         base, grad, base_v, grad_v, stats, own_cols, other_cols = tile_pass(
             stratum + 1, *tables, base, grad, own_mean, other_mean, stats, base_v, grad_v
         )
         more = swap(stats, devices)
         other_cols = swap(other_cols, devices)
-        outs = prior_pass(
-            devices,
-            feats,
-            turned,
-            begun,
-            part,
-            got,
-            own_cols,
-            other_cols,
-            stats,
-            more,
-            final_places(devices) if stratum + 2 == strata else None,
-        )
-        own_mean, other_mean, send, held = outs[:4]
-        if len(outs) > 4:
-            old = outs[4]
+        begun = part_pass(devices, feats, parts[0], gots[0])
+        if stratum + 2 < strata:
+            own_mean, other_mean, offset, sends[0], helds[0] = prior_pass(
+                devices, feats, turned, begun, parts[1], gots[1], own_cols, other_cols
+            )
+            sends[1], helds[1] = rest_pass(devices, turned, offset, stats, more)
+        else:
+            own_mean, other_mean, send, held, old = final_pass(
+                final_places(devices),
+                devices,
+                feats,
+                turned,
+                begun,
+                parts[1],
+                gots[1],
+                parts[0],
+                gots[0],
+                own_cols,
+                other_cols,
+                stats,
+                more,
+            )
         other_mean = swap(other_mean, devices)
+    for stage in range(stages - 1):
+        got = exchange(send, devices, stage)
+        send, held = step_pass(True, stage + 1, 0, devices, held, got, got.shape[0] - RIDERS, (send, got))
+    got = exchange(send, devices, stages - 1)
+    part, stats = update_pass(rate, held, got, old, send)
     mine, other = split_pass(devices, part)
     got = swap(other, devices)
     users, items = last_pass(devices, stats, base, grad, own_mean, other_mean, base_v, grad_v)

time: 129 us -> 122 us (0.946)
  waiting for transfers between devices: 75.7 us -> 51.8 us
  starting transfers between devices: 33.2 us -> 52.2 us
  local copies, waits for them, and re-layouts: 4.04 us -> 1.76 us
    ppermute x16 -> x28, waiting for transfers between devices: 71.6 us -> 50.9 us  [exchange(): return lax.ppermute(array, 'user', pairs)]
    ppermute x16 -> x28, starting transfers between devices: 30.8 us -> 47.2 us  [exchange(): return lax.ppermute(array, 'user', pairs)]
    ppermute x4, starting transfers between devices: 0.07 us -> 3.13 us  [roll(): lax.ppermute(array, 'user', [(i, (i + 1) % devices) for i in range(device...]
    ppermute x4, waiting for transfers between devices: 2.55 us -> 0.01 us  [roll(): lax.ppermute(array, 'user', [(i, (i + 1) % devices) for i in range(device...]
    unnamed x23 -> x21, local copies, waits for them, and re-layouts: 4.04 us -> 1.76 us
    pallas_call x17 -> x29, Pallas kernels: 2.44 us -> 2.69 us  [the longest x1 1.22 us: final_pass(): pl.pallas_call(functools.partial(final_kernel, places, devices), out_shap...]
  transfers between devices with their start and end apart: 30 -> 43, of which waited for: 20 -> 19; matrix products, arithmetic and copies ran while one was open for 0% -> 0% of each run, Pallas kernels for 8% -> 11%
where the time goes in v7:
time: 122 us
  starting transfers between devices  52.2 us (43%)
  waiting for transfers between devices  51.8 us (42%)
  Pallas kernels  15 us (12%)
  local copies, waits for them, and re-layouts  1.76 us (1%)
    ppermute x28, waiting for transfers between devices, exchange(): return lax.ppermute(array, 'user', pairs)  50.9 us
    ppermute x28, starting transfers between devices, exchange(): return lax.ppermute(array, 'user', pairs)  47.2 us
    pallas_call x3, Pallas kernels, tile_pass(): pl.pallas_call(functools.partial(tile_kernel, stratum, noise_scale, devic...  7.39 us
    ppermute x4, starting transfers between devices, roll(): lax.ppermute(array, 'user', [(i, (i + 1) % devices) for i in range(device...  3.13 us
  transfers between devices with their start and end apart: 43, of which 19 were waited for; matrix products, arithmetic and copies ran while one was open for 0% of the time, Pallas kernels for 11%

profile of v7, /device:TPU:0, one launch (start us, length us, event | category | flops | bytes accessed | tf_op | source)
XLA Modules:
  0.0 121.7 jit_solution(14529137906772207282)
XLA Ops:
  3.1 1.8 %first_pass.1 = (f32[384,128]{1,0:T(8,128)S(1)}, f32[384,128]{1,0:T(8,128)S(1)}, f32[512,128]{1,0:T(8,128)S(1)}, f32[512,128]{1,0:T(8,128)S(1)}, f32[512,128]{1,...) custom-call(bf16[384,1024]{1,0:T(8,128)(2,1)S(1)} %copy-done, ...), custom_call_target="tpu_custom_call" | custom-call | flops 402653184 | bytes 2097152 | tf_op jit(solution)/shard_map/first_pass/pallas_call | solution.py:207
  5.5 2.6 %tile_pass.3 = (f32[384,256]{1,0:T(8,128)S(1)}, f32[384,256]{1,0:T(8,128)S(1)}, f32[384,256]{1,0:T(8,128)S(1)}, f32[384,256]{1,0:T(8,128)S(1)}, f32[8,128]{1,0:T(8,128)S(1)}) custom-call(s32[1,3,6]{2,1,0:T(4,128)S(1)} %copy.12.codes, s32[1,3]{1,0:T(1,128)S(1)} %copy-done.8, bf16[1,3,6,128,128]{4,3,2,1,0:T(8,128)(2,1)S(1)} %copy-done.2, ...), custom_call_target="tpu_custom_call" | custom-call | flops 226492416 | bytes 1572864 | tf_op jit(solution)/shard_map/tile_pass/pallas_call | solution.py:150
  9.5 1.9 %collective-permute-start.17 = (f32[384,256]{1,0:T(8,128)S(1)}, f32[384,256]{1,0:T(8,128)S(1)}, u32[]{:S(2)}, u32[]{:S(2)}) collective-permute-start(f32[384,256]{1,0:T(8,128)S(1)} %get-tuple-element.96), channel_id=1, source_target_pairs={{0,1},{1,2},{2,3},{3,4},{4,5},{5,6},{6,7},{7,8},{8,9},{9,10},{10,1... | collective-permute-start | bytes 1179656 | tf_op jit(solution)/shard_map/ppermute | solution.py:540
  11.4 1.6 %collective-permute-start.10 = (f32[264,128]{1,0:T(8,128)S(1)}, f32[264,128]{1,0:T(8,128)S(1)}, u32[]{:S(2)}, u32[]{:S(2)}) collective-permute-start(f32[264,128]{1,0:T(8,128)S(1)} %get-tuple-element.85.refs_0_), channel_id=1, source_target_pairs={{0,4},{1,3},{2,6},{3,1},{4,0},{5,7},{6,2},{7,5},{8,12},{9,11},{10,... | collective-permute-start | bytes 405512 | tf_op jit(solution)/shard_map/ppermute | solution.py:546
  13.0 1.6 %collective-permute-start.2 = (f32[256,128]{1,0:T(8,128)S(1)}, f32[256,128]{1,0:T(8,128)S(1)}, u32[]{:S(2)}, u32[]{:S(2)}) collective-permute-start(f32[256,128]{1,0:T(8,128)S(1)} %get-tuple-element.77), channel_id=1, source_target_pairs={{0,2},{1,5},{2,0},{3,7},{4,6},{5,1},{6,4},{7,3},{8,10},{9,13},{10,... | collective-permute-start | bytes 393224 | tf_op jit(solution)/shard_map/ppermute | solution.py:546
  14.6 9.3 %collective-permute-done.10.got.refs_1_ = f32[264,128]{1,0:T(8,128)S(1)} collective-permute-done((f32[264,128]{1,0:T(8,128)S(1)}, f32[264,128]{1,0:T(8,128)S(1)}, u32[]{:S(2)}, u32[]{:S(2)}) %collective-permute-start.10) | collective-permute-done | bytes 135200 | tf_op jit(solution)/shard_map/ppermute | solution.py:546
  24.0 4.0 %collective-permute-start.3 = (f32[128,128]{1,0:T(8,128)S(1)}, f32[128,128]{1,0:T(8,128)S(1)}, u32[]{:S(2)}, u32[]{:S(2)}) collective-permute-start(f32[128,128]{1,0:T(8,128)S(1)} %get-tuple-element.79), channel_id=1, source_target_pairs={{0,4},{1,3},{2,6},{3,1},{4,0},{5,7},{6,2},{7,5},{8,12},{9,11},{10,... | collective-permute-start | bytes 196616 | tf_op jit(solution)/shard_map/ppermute | solution.py:546
  28.3 4.8 %collective-permute-start.12 = (f32[136,128]{1,0:T(8,128)S(1)}, f32[136,128]{1,0:T(8,128)S(1)}, u32[]{:S(2)}, u32[]{:S(2)}) collective-permute-start(f32[136,128]{1,0:T(8,128)S(1)} %step_pass.23.held.refs_0_), channel_id=1, source_target_pairs={{0,16},{1,17},{2,18},{3,19},{4,20},{5,21},{6,22},{7,23},{8,24},{9,... | collective-permute-start | bytes 208904 | tf_op jit(solution)/shard_map/ppermute | solution.py:546
  33.1 1.6 %collective-permute-start.4 = (f32[128,128]{1,0:T(8,128)S(1)}, f32[128,128]{1,0:T(8,128)S(1)}, u32[]{:S(2)}, u32[]{:S(2)}) collective-permute-start(f32[128,128]{1,0:T(8,128)S(1)} %step_pass.19.held), channel_id=1, source_target_pairs={{0,8},{1,9},{2,10},{3,11},{4,12},{5,13},{6,14},{7,15},{8,0},{9,1},... | collective-permute-start | bytes 196616 | tf_op jit(solution)/shard_map/ppermute | solution.py:546
  35.4 2.0 %collective-permute-start.13 = (f32[136,128]{1,0:T(8,128)S(1)}, f32[136,128]{1,0:T(8,128)S(1)}, u32[]{:S(2)}, u32[]{:S(2)}) collective-permute-start(f32[136,128]{1,0:T(8,128)S(1)} %step_pass.24.held.refs_0_), channel_id=1, source_target_pairs={{0,8},{1,9},{2,10},{3,11},{4,12},{5,13},{6,14},{7,15},{8,0},{9,1},... | collective-permute-start | bytes 208904 | tf_op jit(solution)/shard_map/ppermute | solution.py:546
  38.0 2.7 %collective-permute-start.5 = (f32[128,128]{1,0:T(8,128)S(1)}, f32[128,128]{1,0:T(8,128)S(1)}, u32[]{:S(2)}, u32[]{:S(2)}) collective-permute-start(f32[128,128]{1,0:T(8,128)S(1)} %step_pass.20.held), channel_id=1, source_target_pairs={{0,16},{1,17},{2,18},{3,19},{4,20},{5,21},{6,22},{7,23},{8,24},{9,... | collective-permute-start | bytes 196616 | tf_op jit(solution)/shard_map/ppermute | solution.py:546
  40.8 3.2 %collective-permute-done.5.got = f32[128,128]{1,0:T(8,128)S(1)} collective-permute-done((f32[128,128]{1,0:T(8,128)S(1)}, f32[128,128]{1,0:T(8,128)S(1)}, u32[]{:S(2)}, u32[]{:S(2)}) %collective-permute-start.5) | collective-permute-done | bytes 65568 | tf_op jit(solution)/shard_map/ppermute | solution.py:546
  45.2 2.4 %tile_pass.4 = (f32[384,256]{1,0:T(8,128)S(1)}, f32[384,256]{1,0:T(8,128)S(1)}, f32[384,256]{1,0:T(8,128)S(1)}, f32[384,256]{1,0:T(8,128)S(1)}, f32[8,128]{1,0:T...) custom-call(s32[1,3,6]{2,1,0:T(4,128)S(1)} %copy.12.codes, s32[1,3]{1,0:T(1,128)S(1)} %copy-done.8, ...), custom_call_target="tpu_custom_call" | custom-call | flops 226492416 | bytes 1572864 | tf_op jit(solution)/shard_map/tile_pass/pallas_call | solution.py:150
  49.5 1.4 %collective-permute-start.15 = (f32[256,128]{1,0:T(8,128)S(1)}, f32[256,128]{1,0:T(8,128)S(1)}, u32[]{:S(2)}, u32[]{:S(2)}) collective-permute-start(f32[256,128]{1,0:T(8,128)S(1)} %gather_pass.5.part), channel_id=1, source_target_pairs={{0,4},{1,3},{2,6},{3,1},{4,0},{5,7},{6,2},{7,5},{8,12},{9,11},{10,... | collective-permute-start | bytes 393224 | tf_op jit(solution)/shard_map/ppermute | solution.py:546
  52.6 1.4 %collective-permute-done.7.got = f32[256,128]{1,0:T(8,128)S(1)} collective-permute-done((f32[256,128]{1,0:T(8,128)S(1)}, f32[256,128]{1,0:T(8,128)S(1)}, u32[]{:S(2)}, u32[]{:S(2)}) %collective-permute-start.7) | collective-permute-done | bytes 131104 | tf_op jit(solution)/shard_map/ppermute | solution.py:546
  55.6 1.8 %collective-permute-start.26 = (f32[264,128]{1,0:T(8,128)S(1)}, f32[264,128]{1,0:T(8,128)S(1)}, u32[]{:S(2)}, u32[]{:S(2)}) collective-permute-start(f32[264,128]{1,0:T(8,128)S(1)} %get-tuple-element.106.refs_0_), channel_id=1, source_target_pairs={{0,4},{1,3},{2,6},{3,1},{4,0},{5,7},{6,2},{7,5},{8,12},{9,11},{10,... | collective-permute-start | bytes 405512 | tf_op jit(solution)/shard_map/ppermute | solution.py:546
  58.6 10.1 %collective-permute-done.26.got.refs_1_ = f32[264,128]{1,0:T(8,128)S(1)} collective-permute-done((f32[264,128]{1,0:T(8,128)S(1)}, f32[264,128]{1,0:T(8,128)S(1)}, u32[]{:S(2)}, u32[]{:S(2)}) %collective-permute-start.26) | collective-permute-done | bytes 135200 | tf_op jit(solution)/shard_map/ppermute | solution.py:546
  69.4 3.9 %collective-permute-done.27.got.refs_1_ = f32[136,128]{1,0:T(8,128)S(1)} collective-permute-done((f32[136,128]{1,0:T(8,128)S(1)}, f32[136,128]{1,0:T(8,128)S(1)}, u32[]{:S(2)}, u32[]{:S(2)}) %collective-permute-start.27) | collective-permute-done | bytes 69664 | tf_op jit(solution)/shard_map/ppermute | solution.py:546
  73.6 5.1 %collective-permute-start.21 = (f32[128,128]{1,0:T(8,128)S(1)}, f32[128,128]{1,0:T(8,128)S(1)}, u32[]{:S(2)}, u32[]{:S(2)}) collective-permute-start(f32[128,128]{1,0:T(8,128)S(1)} %step_pass.26.held), channel_id=1, source_target_pairs={{0,8},{1,9},{2,10},{3,11},{4,12},{5,13},{6,14},{7,15},{8,0},{9,1},... | collective-permute-start | bytes 196616 | tf_op jit(solution)/shard_map/ppermute | solution.py:546
  78.7 2.4 %collective-permute-start.29 = (f32[136,128]{1,0:T(8,128)S(1)}, f32[136,128]{1,0:T(8,128)S(1)}, u32[]{:S(2)}, u32[]{:S(2)}) collective-permute-start(f32[136,128]{1,0:T(8,128)S(1)} %step_pass.30.held.refs_0_), channel_id=1, source_target_pairs={{0,8},{1,9},{2,10},{3,11},{4,12},{5,13},{6,14},{7,15},{8,0},{9,1},... | collective-permute-start | bytes 208904 | tf_op jit(solution)/shard_map/ppermute | solution.py:546
  81.2 2.8 %collective-permute-start.22 = (f32[128,128]{1,0:T(8,128)S(1)}, f32[128,128]{1,0:T(8,128)S(1)}, u32[]{:S(2)}, u32[]{:S(2)}) collective-permute-start(f32[128,128]{1,0:T(8,128)S(1)} %step_pass.27.held), channel_id=1, source_target_pairs={{0,16},{1,17},{2,18},{3,19},{4,20},{5,21},{6,22},{7,23},{8,24},{9,... | collective-permute-start | bytes 196616 | tf_op jit(solution)/shard_map/ppermute | solution.py:546
  84.0 2.4 %collective-permute-done.22.got = f32[128,128]{1,0:T(8,128)S(1)} collective-permute-done((f32[128,128]{1,0:T(8,128)S(1)}, f32[128,128]{1,0:T(8,128)S(1)}, u32[]{:S(2)}, u32[]{:S(2)}) %collective-permute-start.22) | collective-permute-done | bytes 65568 | tf_op jit(solution)/shard_map/ppermute | solution.py:546
  87.8 2.4 %tile_pass.5 = (f32[384,256]{1,0:T(8,128)S(1)}, f32[384,256]{1,0:T(8,128)S(1)}, f32[384,256]{1,0:T(8,128)S(1)}, f32[384,256]{1,0:T(8,128)S(1)}, f32[8,128]{1,0:T...) custom-call(s32[1,3,6]{2,1,0:T(4,128)S(1)} %copy.12.codes, s32[1,3]{1,0:T(1,128)S(1)} %copy-done.8, ...), custom_call_target="tpu_custom_call" | custom-call | flops 226492416 | bytes 1572864 | tf_op jit(solution)/shard_map/tile_pass/pallas_call | solution.py:150
  90.8 1.3 %collective-permute-start.24 = (f32[256,128]{1,0:T(8,128)S(1)}, f32[256,128]{1,0:T(8,128)S(1)}, u32[]{:S(2)}, u32[]{:S(2)}) collective-permute-start(f32[256,128]{1,0:T(8,128)S(1)} %gather_pass.6.part.first_part), channel_id=1, source_target_pairs={{0,2},{1,5},{2,0},{3,7},{4,6},{5,1},{6,4},{7,3},{8,10},{9,13},{10,... | collective-permute-start | bytes 393224 | tf_op jit(solution)/shard_map/ppermute | solution.py:546
  93.3 3.9 %collective-permute-done.24.got.first_got = f32[256,128]{1,0:T(8,128)S(1)} collective-permute-done((f32[256,128]{1,0:T(8,128)S(1)}, f32[256,128]{1,0:T(8,128)S(1)}, u32[]{:S(2)}, u32[]{:S(2)}) %collective-permute-start.24) | collective-permute-done | bytes 131104 | tf_op jit(solution)/shard_map/ppermute | solution.py:546
  97.6 1.2 %final_pass.1 = (f32[384,128]{1,0:T(8,128)S(1)}, f32[384,128]{1,0:T(8,128)S(1)}, f32[520,128]{1,0:T(8,128)S(1)}, f32[512,128]{1,0:T(8,128)S(1)}, f32[64,128]{1,0:T(8,128)S(1)}) custom-call(bf16[768,1024]{1,0:T(8,128)(2,1)S(1)} %get-tuple-element.72.feats, bf16[1024,768]{1,0:T(8,128)(2,1)S(1)} %get-tuple-element.73.turned, f32[768,128]{1,0:T(8,128)S(1)} %part_pass.3.begun, ...), custom_call_target="tpu_custom_call" | custom-call | flops 402653184 | bytes 3145728 | tf_op jit(solution)/shard_map/final_pass/pallas_call | solution.py:373
  99.8 5.5 %collective-permute-done.37.got.refs_1_ = f32[520,128]{1,0:T(8,128)S(1)} collective-permute-done((f32[520,128]{1,0:T(8,128)S(1)}, f32[520,128]{1,0:T(8,128)S(1)}, u32[]{:S(2)}, u32[]{:S(2)}) %collective-permute-start.37) | collective-permute-done | bytes 266272 | tf_op jit(solution)/shard_map/ppermute | solution.py:546
  106.3 4.1 %collective-permute-done.38.got.refs_1_ = f32[264,128]{1,0:T(8,128)S(1)} collective-permute-done((f32[264,128]{1,0:T(8,128)S(1)}, f32[264,128]{1,0:T(8,128)S(1)}, u32[]{:S(2)}, u32[]{:S(2)}) %collective-permute-start.38) | collective-permute-done | bytes 135200 | tf_op jit(solution)/shard_map/ppermute | solution.py:546
  110.4 1.9 %collective-permute-start.39 = (f32[136,128]{1,0:T(8,128)S(1)}, f32[136,128]{1,0:T(8,128)S(1)}, u32[]{:S(2)}, u32[]{:S(2)}) collective-permute-start(f32[136,128]{1,0:T(8,128)S(1)} %get-tuple-element.125.refs_0_), channel_id=1, source_target_pairs={{0,8},{1,9},{2,10},{3,11},{4,12},{5,13},{6,14},{7,15},{8,0},{9,1},... | collective-permute-start | bytes 208904 | tf_op jit(solution)/shard_map/ppermute | solution.py:546
  112.3 2.5 %collective-permute-done.39.got.refs_1_ = f32[136,128]{1,0:T(8,128)S(1)} collective-permute-done((f32[136,128]{1,0:T(8,128)S(1)}, f32[136,128]{1,0:T(8,128)S(1)}, u32[]{:S(2)}, u32[]{:S(2)}) %collective-permute-start.39) | collective-permute-done | bytes 69664 | tf_op jit(solution)/shard_map/ppermute | solution.py:546
  114.8 3.1 %collective-permute-start.40 = (f32[72,128]{1,0:T(8,128)S(1)}, f32[72,128]{1,0:T(8,128)S(1)}, u32[]{:S(2)}, u32[]{:S(2)}) collective-permute-start(f32[72,128]{1,0:T(8,128)S(1)} %get-tuple-element.127.refs_0_), channel_id=1, source_target_pairs={{0,16},{1,17},{2,18},{3,19},{4,20},{5,21},{6,22},{7,23},{8,24},{9,... | collective-permute-start | bytes 110600 | tf_op jit(solution)/shard_map/ppermute | solution.py:546
  117.9 1.9 %collective-permute-done.40.got = f32[72,128]{1,0:T(8,128)S(1)} collective-permute-done((f32[72,128]{1,0:T(8,128)S(1)}, f32[72,128]{1,0:T(8,128)S(1)}, u32[]{:S(2)}, u32[]{:S(2)}) %collective-permute-start.40) | collective-permute-done | bytes 36896 | tf_op jit(solution)/shard_map/ppermute | solution.py:546
  (115 shorter events, 22.1 us)
Async XLA Ops:
  2.0 48.8 %collective-permute-start = (f32[384,1024]{1,0:T(8,128)S(1)}, f32[384,1024]{1,0:T(8,128)S(1)}, u32[]{:S(2)}, u32[]{:S(2)}) collective-permute-start(f32[384,1024]{1,0:T(8,128)S(1)} %widen_pass.1), channel_id=1, source_target_pairs={{0,1},{1,0},{2,3},{3,2},{4,5},{5,4},{6,7},{7,6},{8,9},{9,8},{10,11... | collective-permute-start | bytes 4718600 | tf_op jit(solution)/shard_map/ppermute | solution.py:536
  4.9 6.4 %collective-permute-start.8 = (f32[512,128]{1,0:T(8,128)S(1)}, f32[512,128]{1,0:T(8,128)S(1)}, u32[]{:S(2)}, u32[]{:S(2)}) collective-permute-start(f32[512,128]{1,0:T(8,128)S(1)} %get-tuple-element.82), channel_id=1, source_target_pairs={{0,1},{1,0},{2,3},{3,2},{4,5},{5,4},{6,7},{7,6},{8,9},{9,8},{10,11... | collective-permute-start | bytes 786440 | tf_op jit(solution)/shard_map/ppermute | solution.py:536
  5.4 7.6 %collective-permute-start.1 = (f32[512,128]{1,0:T(8,128)S(1)}, f32[512,128]{1,0:T(8,128)S(1)}, u32[]{:S(2)}, u32[]{:S(2)}) collective-permute-start(f32[512,128]{1,0:T(8,128)S(1)} %get-tuple-element.75), channel_id=1, source_target_pairs={{0,1},{1,0},{2,3},{3,2},{4,5},{5,4},{6,7},{7,6},{8,9},{9,8},{10,11... | collective-permute-start | bytes 786440 | tf_op jit(solution)/shard_map/ppermute | solution.py:536
  8.6 36.6 %collective-permute-start.16 = (f32[384,256]{1,0:T(8,128)S(1)}, f32[384,256]{1,0:T(8,128)S(1)}, u32[]{:S(2)}, u32[]{:S(2)}) collective-permute-start(f32[384,256]{1,0:T(8,128)S(1)} %get-tuple-element.95), channel_id=1, source_target_pairs={{0,1},{1,2},{2,3},{3,4},{4,5},{5,6},{6,7},{7,8},{8,9},{9,10},{10,1... | collective-permute-start | bytes 1179656 | tf_op jit(solution)/shard_map/ppermute | solution.py:540
  9.5 35.8 %collective-permute-start.17 = (f32[384,256]{1,0:T(8,128)S(1)}, f32[384,256]{1,0:T(8,128)S(1)}, u32[]{:S(2)}, u32[]{:S(2)}) collective-permute-start(f32[384,256]{1,0:T(8,128)S(1)} %get-tuple-element.96), channel_id=1, source_target_pairs={{0,1},{1,2},{2,3},{3,4},{4,5},{5,6},{6,7},{7,8},{8,9},{9,10},{10,1... | collective-permute-start | bytes 1179656 | tf_op jit(solution)/shard_map/ppermute | solution.py:540
  11.4 12.5 %collective-permute-start.10 = (f32[264,128]{1,0:T(8,128)S(1)}, f32[264,128]{1,0:T(8,128)S(1)}, u32[]{:S(2)}, u32[]{:S(2)}) collective-permute-start(f32[264,128]{1,0:T(8,128)S(1)} %get-tuple-element.85.refs_0_), channel_id=1, source_target_pairs={{0,4},{1,3},{2,6},{3,1},{4,0},{5,7},{6,2},{7,5},{8,12},{9,11},{10,... | collective-permute-start | bytes 405512 | tf_op jit(solution)/shard_map/ppermute | solution.py:546
  13.0 11.0 %collective-permute-start.2 = (f32[256,128]{1,0:T(8,128)S(1)}, f32[256,128]{1,0:T(8,128)S(1)}, u32[]{:S(2)}, u32[]{:S(2)}) collective-permute-start(f32[256,128]{1,0:T(8,128)S(1)} %get-tuple-element.77), channel_id=1, source_target_pairs={{0,2},{1,5},{2,0},{3,7},{4,6},{5,1},{6,4},{7,3},{8,10},{9,13},{10,... | collective-permute-start | bytes 393224 | tf_op jit(solution)/shard_map/ppermute | solution.py:546
  24.0 9.1 %collective-permute-start.3 = (f32[128,128]{1,0:T(8,128)S(1)}, f32[128,128]{1,0:T(8,128)S(1)}, u32[]{:S(2)}, u32[]{:S(2)}) collective-permute-start(f32[128,128]{1,0:T(8,128)S(1)} %get-tuple-element.79), channel_id=1, source_target_pairs={{0,4},{1,3},{2,6},{3,1},{4,0},{5,7},{6,2},{7,5},{8,12},{9,11},{10,... | collective-permute-start | bytes 196616 | tf_op jit(solution)/shard_map/ppermute | solution.py:546
  28.3 7.1 %collective-permute-start.12 = (f32[136,128]{1,0:T(8,128)S(1)}, f32[136,128]{1,0:T(8,128)S(1)}, u32[]{:S(2)}, u32[]{:S(2)}) collective-permute-start(f32[136,128]{1,0:T(8,128)S(1)} %step_pass.23.held.refs_0_), channel_id=1, source_target_pairs={{0,16},{1,17},{2,18},{3,19},{4,20},{5,21},{6,22},{7,23},{8,24},{9,... | collective-permute-start | bytes 208904 | tf_op jit(solution)/shard_map/ppermute | solution.py:546
  33.1 4.9 %collective-permute-start.4 = (f32[128,128]{1,0:T(8,128)S(1)}, f32[128,128]{1,0:T(8,128)S(1)}, u32[]{:S(2)}, u32[]{:S(2)}) collective-permute-start(f32[128,128]{1,0:T(8,128)S(1)} %step_pass.19.held), channel_id=1, source_target_pairs={{0,8},{1,9},{2,10},{3,11},{4,12},{5,13},{6,14},{7,15},{8,0},{9,1},... | collective-permute-start | bytes 196616 | tf_op jit(solution)/shard_map/ppermute | solution.py:546
  35.4 8.7 %collective-permute-start.13 = (f32[136,128]{1,0:T(8,128)S(1)}, f32[136,128]{1,0:T(8,128)S(1)}, u32[]{:S(2)}, u32[]{:S(2)}) collective-permute-start(f32[136,128]{1,0:T(8,128)S(1)} %step_pass.24.held.refs_0_), channel_id=1, source_target_pairs={{0,8},{1,9},{2,10},{3,11},{4,12},{5,13},{6,14},{7,15},{8,0},{9,1},... | collective-permute-start | bytes 208904 | tf_op jit(solution)/shard_map/ppermute | solution.py:546
  38.0 5.9 %collective-permute-start.5 = (f32[128,128]{1,0:T(8,128)S(1)}, f32[128,128]{1,0:T(8,128)S(1)}, u32[]{:S(2)}, u32[]{:S(2)}) collective-permute-start(f32[128,128]{1,0:T(8,128)S(1)} %step_pass.20.held), channel_id=1, source_target_pairs={{0,16},{1,17},{2,18},{3,19},{4,20},{5,21},{6,22},{7,23},{8,24},{9,... | collective-permute-start | bytes 196616 | tf_op jit(solution)/shard_map/ppermute | solution.py:546
  44.1 5.4 %collective-permute-start.14 = (f32[128,128]{1,0:T(8,128)S(1)}, f32[128,128]{1,0:T(8,128)S(1)}, u32[]{:S(2)}, u32[]{:S(2)}) collective-permute-start(f32[128,128]{1,0:T(8,128)S(1)} %get-tuple-element.89.part.old), channel_id=1, source_target_pairs={{0,2},{1,5},{2,0},{3,7},{4,6},{5,1},{6,4},{7,3},{8,10},{9,13},{10,... | collective-permute-start | bytes 196616 | tf_op jit(solution)/shard_map/ppermute | solution.py:546
  47.6 6.9 %collective-permute-start.18 = (f32[384,128]{1,0:T(8,128)S(1)}, f32[384,128]{1,0:T(8,128)S(1)}, u32[]{:S(2)}, u32[]{:S(2)}) collective-permute-start(f32[384,128]{1,0:T(8,128)S(1)} %get-tuple-element.98), channel_id=1, source_target_pairs={{0,1},{1,0},{2,3},{3,2},{4,5},{5,4},{6,7},{7,6},{8,9},{9,8},{10,11... | collective-permute-start | bytes 589832 | tf_op jit(solution)/shard_map/ppermute | solution.py:536
  48.3 5.7 %collective-permute-start.7 = (f32[256,128]{1,0:T(8,128)S(1)}, f32[256,128]{1,0:T(8,128)S(1)}, u32[]{:S(2)}, u32[]{:S(2)}) collective-permute-start(f32[256,128]{1,0:T(8,128)S(1)} %gather_pass.4.part), channel_id=1, source_target_pairs={{0,2},{1,5},{2,0},{3,7},{4,6},{5,1},{6,4},{7,3},{8,10},{9,13},{10,... | collective-permute-start | bytes 393224 | tf_op jit(solution)/shard_map/ppermute | solution.py:546
  49.5 5.0 %collective-permute-start.15 = (f32[256,128]{1,0:T(8,128)S(1)}, f32[256,128]{1,0:T(8,128)S(1)}, u32[]{:S(2)}, u32[]{:S(2)}) collective-permute-start(f32[256,128]{1,0:T(8,128)S(1)} %gather_pass.5.part), channel_id=1, source_target_pairs={{0,4},{1,3},{2,6},{3,1},{4,0},{5,7},{6,2},{7,5},{8,12},{9,11},{10,... | collective-permute-start | bytes 393224 | tf_op jit(solution)/shard_map/ppermute | solution.py:546
  50.9 36.9 %collective-permute-start.33 = (f32[384,256]{1,0:T(8,128)S(1)}, f32[384,256]{1,0:T(8,128)S(1)}, u32[]{:S(2)}, u32[]{:S(2)}) collective-permute-start(f32[384,256]{1,0:T(8,128)S(1)} %get-tuple-element.115), channel_id=1, source_target_pairs={{0,1},{1,2},{2,3},{3,4},{4,5},{5,6},{6,7},{7,8},{8,9},{9,10},{10,1... | collective-permute-start | bytes 1179656 | tf_op jit(solution)/shard_map/ppermute | solution.py:540
  50.9 36.9 %collective-permute-start.34 = (f32[384,256]{1,0:T(8,128)S(1)}, f32[384,256]{1,0:T(8,128)S(1)}, u32[]{:S(2)}, u32[]{:S(2)}) collective-permute-start(f32[384,256]{1,0:T(8,128)S(1)} %get-tuple-element.116), channel_id=1, source_target_pairs={{0,1},{1,2},{2,3},{3,4},{4,5},{5,6},{6,7},{7,8},{8,9},{9,10},{10,1... | collective-permute-start | bytes 1179656 | tf_op jit(solution)/shard_map/ppermute | solution.py:540
  55.6 13.1 %collective-permute-start.26 = (f32[264,128]{1,0:T(8,128)S(1)}, f32[264,128]{1,0:T(8,128)S(1)}, u32[]{:S(2)}, u32[]{:S(2)}) collective-permute-start(f32[264,128]{1,0:T(8,128)S(1)} %get-tuple-element.106.refs_0_), channel_id=1, source_target_pairs={{0,4},{1,3},{2,6},{3,1},{4,0},{5,7},{6,2},{7,5},{8,12},{9,11},{10,... | collective-permute-start | bytes 405512 | tf_op jit(solution)/shard_map/ppermute | solution.py:546
  57.4 11.4 %collective-permute-start.19 = (f32[256,128]{1,0:T(8,128)S(1)}, f32[256,128]{1,0:T(8,128)S(1)}, u32[]{:S(2)}, u32[]{:S(2)}) collective-permute-start(f32[256,128]{1,0:T(8,128)S(1)} %get-tuple-element.100), channel_id=1, source_target_pairs={{0,2},{1,5},{2,0},{3,7},{4,6},{5,1},{6,4},{7,3},{8,10},{9,13},{10,... | collective-permute-start | bytes 393224 | tf_op jit(solution)/shard_map/ppermute | solution.py:546
  69.4 18.4 %collective-permute-start.32 = (f32[384,128]{1,0:T(8,128)S(1)}, f32[384,128]{1,0:T(8,128)S(1)}, u32[]{:S(2)}, u32[]{:S(2)}) collective-permute-start(f32[384,128]{1,0:T(8,128)S(1)} %get-tuple-element.113), channel_id=1, source_target_pairs={{0,1},{1,0},{2,3},{3,2},{4,5},{5,4},{6,7},{7,6},{8,9},{9,8},{10,11... | collective-permute-start | bytes 589832 | tf_op jit(solution)/shard_map/ppermute | solution.py:536
  73.3 5.4 %collective-permute-start.28 = (f32[136,128]{1,0:T(8,128)S(1)}, f32[136,128]{1,0:T(8,128)S(1)}, u32[]{:S(2)}, u32[]{:S(2)}) collective-permute-start(f32[136,128]{1,0:T(8,128)S(1)} %step_pass.29.held.refs_0_), channel_id=1, source_target_pairs={{0,16},{1,17},{2,18},{3,19},{4,20},{5,21},{6,22},{7,23},{8,24},{9,... | collective-permute-start | bytes 208904 | tf_op jit(solution)/shard_map/ppermute | solution.py:546
  73.6 7.6 %collective-permute-start.21 = (f32[128,128]{1,0:T(8,128)S(1)}, f32[128,128]{1,0:T(8,128)S(1)}, u32[]{:S(2)}, u32[]{:S(2)}) collective-permute-start(f32[128,128]{1,0:T(8,128)S(1)} %step_pass.26.held), channel_id=1, source_target_pairs={{0,8},{1,9},{2,10},{3,11},{4,12},{5,13},{6,14},{7,15},{8,0},{9,1},... | collective-permute-start | bytes 196616 | tf_op jit(solution)/shard_map/ppermute | solution.py:546
  78.7 8.7 %collective-permute-start.29 = (f32[136,128]{1,0:T(8,128)S(1)}, f32[136,128]{1,0:T(8,128)S(1)}, u32[]{:S(2)}, u32[]{:S(2)}) collective-permute-start(f32[136,128]{1,0:T(8,128)S(1)} %step_pass.30.held.refs_0_), channel_id=1, source_target_pairs={{0,8},{1,9},{2,10},{3,11},{4,12},{5,13},{6,14},{7,15},{8,0},{9,1},... | collective-permute-start | bytes 208904 | tf_op jit(solution)/shard_map/ppermute | solution.py:546
  81.2 5.2 %collective-permute-start.22 = (f32[128,128]{1,0:T(8,128)S(1)}, f32[128,128]{1,0:T(8,128)S(1)}, u32[]{:S(2)}, u32[]{:S(2)}) collective-permute-start(f32[128,128]{1,0:T(8,128)S(1)} %step_pass.27.held), channel_id=1, source_target_pairs={{0,16},{1,17},{2,18},{3,19},{4,20},{5,21},{6,22},{7,23},{8,24},{9,... | collective-permute-start | bytes 196616 | tf_op jit(solution)/shard_map/ppermute | solution.py:546
  90.2 7.4 %collective-permute-start.35 = (f32[384,128]{1,0:T(8,128)S(1)}, f32[384,128]{1,0:T(8,128)S(1)}, u32[]{:S(2)}, u32[]{:S(2)}) collective-permute-start(f32[384,128]{1,0:T(8,128)S(1)} %get-tuple-element.118), channel_id=1, source_target_pairs={{0,1},{1,0},{2,3},{3,2},{4,5},{5,4},{6,7},{7,6},{8,9},{9,8},{10,11... | collective-permute-start | bytes 589832 | tf_op jit(solution)/shard_map/ppermute | solution.py:536
  90.8 6.4 %collective-permute-start.24 = (f32[256,128]{1,0:T(8,128)S(1)}, f32[256,128]{1,0:T(8,128)S(1)}, u32[]{:S(2)}, u32[]{:S(2)}) collective-permute-start(f32[256,128]{1,0:T(8,128)S(1)} %gather_pass.6.part.first_part), channel_id=1, source_target_pairs={{0,2},{1,5},{2,0},{3,7},{4,6},{5,1},{6,4},{7,3},{8,10},{9,13},{10,... | collective-permute-start | bytes 393224 | tf_op jit(solution)/shard_map/ppermute | solution.py:546
  92.1 5.4 %collective-permute-start.31 = (f32[256,128]{1,0:T(8,128)S(1)}, f32[256,128]{1,0:T(8,128)S(1)}, u32[]{:S(2)}, u32[]{:S(2)}) collective-permute-start(f32[256,128]{1,0:T(8,128)S(1)} %gather_pass.7.part), channel_id=1, source_target_pairs={{0,4},{1,3},{2,6},{3,1},{4,0},{5,7},{6,2},{7,5},{8,12},{9,11},{10,... | collective-permute-start | bytes 393224 | tf_op jit(solution)/shard_map/ppermute | solution.py:546
  98.8 6.5 %collective-permute-start.37 = (f32[520,128]{1,0:T(8,128)S(1)}, f32[520,128]{1,0:T(8,128)S(1)}, u32[]{:S(2)}, u32[]{:S(2)}) collective-permute-start(f32[520,128]{1,0:T(8,128)S(1)} %get-tuple-element.121.refs_0_), channel_id=1, source_target_pairs={{0,2},{1,5},{2,0},{3,7},{4,6},{5,1},{6,4},{7,3},{8,10},{9,13},{10,... | collective-permute-start | bytes 798728 | tf_op jit(solution)/shard_map/ppermute | solution.py:546
  105.3 5.1 %collective-permute-start.38 = (f32[264,128]{1,0:T(8,128)S(1)}, f32[264,128]{1,0:T(8,128)S(1)}, u32[]{:S(2)}, u32[]{:S(2)}) collective-permute-start(f32[264,128]{1,0:T(8,128)S(1)} %get-tuple-element.123.refs_0_), channel_id=1, source_target_pairs={{0,4},{1,3},{2,6},{3,1},{4,0},{5,7},{6,2},{7,5},{8,12},{9,11},{10,... | collective-permute-start | bytes 405512 | tf_op jit(solution)/shard_map/ppermute | solution.py:546
  106.3 13.6 %collective-permute-start.41 = (f32[384,128]{1,0:T(8,128)S(1)}, f32[384,128]{1,0:T(8,128)S(1)}, u32[]{:S(2)}, u32[]{:S(2)}) collective-permute-start(f32[384,128]{1,0:T(8,128)S(1)} %get-tuple-element.133), channel_id=1, source_target_pairs={{0,1},{1,0},{2,3},{3,2},{4,5},{5,4},{6,7},{7,6},{8,9},{9,8},{10,11... | collective-permute-start | bytes 589832 | tf_op jit(solution)/shard_map/ppermute | solution.py:536
  114.8 5.0 %collective-permute-start.40 = (f32[72,128]{1,0:T(8,128)S(1)}, f32[72,128]{1,0:T(8,128)S(1)}, u32[]{:S(2)}, u32[]{:S(2)}) collective-permute-start(f32[72,128]{1,0:T(8,128)S(1)} %get-tuple-element.127.refs_0_), channel_id=1, source_target_pairs={{0,16},{1,17},{2,18},{3,19},{4,20},{5,21},{6,22},{7,23},{8,24},{9,... | collective-permute-start | bytes 110600 | tf_op jit(solution)/shard_map/ppermute | solution.py:546
  (21 other events, 70.8 us)

commit v8 on v7

--- a/solution.py
+++ b/solution.py
@@ -17,6 +17,8 @@
 CORES = 2
 CHUNKS = 2
 RIDERS = 8
+BASE_BY = 1
+PULL_BY = 1
 NN = (((1,), (0,)), ((), ()))
 NT = (((1,), (1,)), ((), ()))
 TN = (((0,), (0,)), ((), ()))
@@ -66,13 +68,13 @@
 def tile_kernel(stratum, noise_scale, devices, codes, count, ratings, user_noise, item_noise, *refs):
     if stratum == 0:
         users_in, items_in = refs[:2]
-        base_u, grad_u, base_v, grad_v, stats = refs[2:7]
+        base_u, grad_u, err_b, user_b, stats = refs[2:7]
         refs = refs[7:]
     else:
         old_base, old_grad, own_mean, other_mean, old_stats, old_base_v, old_grad_v = refs[:7]
-        base_u, grad_u, base_v, grad_v, stats, own_cols, other_cols = refs[7:14]
-        refs = refs[14:]
-    tiles, noise_u, noise_v, users, items, pred, err_b, sems = refs
+        base_u, grad_u, err_b, user_b, stats, own_cols, other_cols, base_v = refs[8:16]
+        refs = refs[16:]
+    tiles, noise_u, noise_v, users, items, pred, sems = refs
     core = where_am_i(devices)[0]
     rows, rank = users.shape
     width = rank // CORES
@@ -84,16 +86,19 @@
             [
                 (ratings.at[0, stratum], tiles),
                 (user_noise.at[stratum], noise_u),
-                (item_noise.at[stratum], noise_v),
             ]
-            + ([(users_in, users), (items_in, items)] if stratum == 0 else [])
+            + (
+                [(users_in, users), (items_in, items)]
+                if stratum == 0
+                else [(item_noise.at[stratum], noise_v)]
+            )
         )
     ]
     for copy in copies[::-1]:
         copy.start()
     if stratum == 0:
-        copies[4].wait()
         copies[3].wait()
+        copies[2].wait()
     else:
         precision = precision_of(old_stats[...])
         precision = jnp.concatenate([precision] * CORES, 1)
@@ -107,9 +112,9 @@
         users[:, width:] = new[:, width:] + pull * right
         own_cols[...] = half_of(users, core)
         other_cols[...] = half_of(users, 1 - core)
-    user_b = users[...].astype(bf16)
+    user_b[...] = users[...].astype(bf16)
     item_b = items[...].astype(bf16)
-    pred[...] = dot(user_b, item_b, NT)
+    pred[...] = dot(user_b[...], item_b, NT)
     err_b[...] = jnp.zeros_like(err_b)
     live_slots = count[0, stratum]
     sse = jnp.zeros((tile, tile), f32)
@@ -128,15 +133,63 @@
     row = lax.broadcasted_iota(jnp.int32, stats.shape, 0)
     stats[...] = jnp.where(row == 0, total, jnp.where(row == 1, counted, 0.0))
     grad_u[...] = step_size * dot(err_all, item_b)
-    grad_v[...] = step_size * dot(err_all, user_b, TN)
-    copies[2].wait()
-    base_v[...] = (1.0 - step_size * item_prec) * items[...] + noise_scale * noise_v[...].astype(
-        f32
-    )
     copies[1].wait()
     base_u[...] = (1.0 - step_size * prior_prec) * users[...] + noise_scale * noise_u[...].astype(
         f32
     )
+    if stratum:
+        copies[2].wait()
+        base_v[...] = item_base(noise_scale, items, noise_v)
+
+
+def item_base(noise_scale, items, noise):
+    return (1.0 - step_size * item_prec) * items[...] + noise_scale * noise[...].astype(f32)
+
+
+def base_kernel(noise_scale, items_in, noise_in, base, items, noise, sems):
+    copies = [
+        pltpu.make_async_copy(items_in, items, sems.at[0]),
+        pltpu.make_async_copy(noise_in.at[0], noise, sems.at[1]),
+    ]
+    for copy in copies:
+        copy.start()
+    for copy in copies:
+        copy.wait()
+    base[...] = item_base(noise_scale, items, noise)
+
+
+def base_pass(items, item_noise):
+    return pl.pallas_call(
+        functools.partial(base_kernel, math.sqrt(2.0 * step_size)),
+        out_shape=shape(*items.shape),
+        in_specs=[HBM] * 2,
+        out_specs=VMEM,
+        scratch_shapes=[
+            pltpu.VMEM(items.shape, f32),
+            pltpu.VMEM(items.shape, bf16),
+            pltpu.SemaphoreType.DMA((2,)),
+        ],
+        compiler_params=PARAMS,
+        cost_estimate=cost(2 * items.size, 10 * items.size),
+        name="base_pass",
+    )(items, item_noise)
+
+
+def pull_kernel(err_b, user_b, *refs):
+    refs[-1][...] = step_size * dot(err_b[...], user_b[...], TN)
+
+
+def pull_pass(err_b, user_b, later):
+    rows, rank = user_b.shape
+    return pl.pallas_call(
+        pull_kernel,
+        out_shape=shape(rows, rank),
+        in_specs=[VMEM] * 2 + [ANY] * len(later),
+        out_specs=VMEM,
+        compiler_params=PARAMS,
+        cost_estimate=cost(2 * rows * rows * rank, 8 * rows * rank),
+        name="pull_pass",
+    )(err_b, user_b, *later)
 
 
 def tile_pass(stratum, devices, codes, count, ratings, user_noise, item_noise, *state):
@@ -144,13 +197,19 @@
     rows, rank = user_noise.shape[1:]
     noise_scale = math.sqrt(2.0 * step_size)
     width = rank // CORES
-    outs = [shape(rows, rank)] * 4 + [shape(RIDERS, width)]
+    outs = [
+        shape(rows, rank),
+        shape(rows, rank),
+        shape(rows, rows, dtype=bf16),
+        shape(rows, rank, dtype=bf16),
+        shape(RIDERS, width),
+    ]
     if stratum:
-        outs += [shape(rows, width)] * 2
+        outs += [shape(rows, width), shape(rows, width), shape(rows, rank)]
     return pl.pallas_call(
         functools.partial(tile_kernel, stratum, noise_scale, devices),
         out_shape=tuple(outs),
-        in_specs=[SMEM] * 2 + [HBM] * 3 + [VMEM if stratum else HBM] * len(state),
+        in_specs=[SMEM] * 2 + [HBM] * 3 + ([VMEM] * 7 + [ANY] if stratum else [HBM] * 2),
         out_specs=(VMEM,) * len(outs),
         scratch_shapes=[
             pltpu.VMEM((slots, tile, tile), bf16),
@@ -159,8 +218,7 @@
             pltpu.VMEM((rows, rank), f32),
             pltpu.VMEM((rows, rank), f32),
             pltpu.VMEM((rows, rows), f32),
-            pltpu.VMEM((rows, rows), bf16),
-            pltpu.SemaphoreType.DMA((5,)),
+            pltpu.SemaphoreType.DMA((4,)),
         ],
         compiler_params=PARAMS,
         cost_estimate=cost(6 * rows * rows * rank, 16 * rows * rank),
@@ -441,24 +499,25 @@
     )(held, got, old, *([sent] if riding else []), *later)
 
 
-def gather_kernel(stage, chunk, devices, part, got, both):
+def gather_kernel(stage, chunk, devices, part, got, *refs):
+    both = refs[-1]
     rows = part.shape[0]
     bit = where_am_i(devices, chunk)[1 + stage]
     both[rows_at(bit, rows), :] = part[...]
     both[rows_at(1 - bit, rows), :] = got[...]
 
 
-def gather_pass(stage, chunk, devices, part, got):
+def gather_pass(stage, chunk, devices, part, got, later=()):
     rows, width = part.shape
     return pl.pallas_call(
         functools.partial(gather_kernel, stage, chunk, devices),
         out_shape=shape(2 * rows, width),
-        in_specs=[VMEM, VMEM],
+        in_specs=[VMEM, VMEM] + [ANY] * len(later),
         out_specs=VMEM,
         compiler_params=PARAMS,
         cost_estimate=cost(rows * width, 16 * rows * width),
         name="gather_pass",
-    )(part, got)
+    )(part, got, *later)
 
 
 def split_kernel(devices, both, mine, other):
@@ -580,12 +639,13 @@
 
     both = range(CHUNKS)
     depth = feat // CHUNKS
+    base_v = base_pass(item_factors, item_noise)
     own_mean, other_mean, *outs = first_pass(
         devices, side_features, prior_weights, user_factors
     )
     helds, olds = outs[CHUNKS : 2 * CHUNKS], outs[2 * CHUNKS :]
     gots = [swap(send, devices) for send in outs[:CHUNKS]]
-    base, grad, base_v, grad_v, stats = tile_pass(0, *tables, user_factors, item_factors)
+    base, grad, err_b, user_b, stats = tile_pass(0, *tables, user_factors, item_factors)
     more = swap(stats, devices)
     sends = [None] * CHUNKS
     for c in both:
@@ -593,29 +653,35 @@
         sends[c], helds[c] = step_pass(True, 0, c, devices, helds[c], gots[c], depth, riders)
     feats, turned = join_pass(side_features, swap(widen_pass(side_features), devices))
     for stratum in range(strata - 1):
-        base_v, grad_v = roll(base_v, devices), roll(grad_v, devices)
+        base_v = roll(base_v, devices)
         for stage in range(stages - 1):
-            for c in both:
+            for c in (1, 0):
                 gots[c] = exchange(sends[c], devices, stage, c)
                 riders = (sends[c], gots[c]) if c else ()
                 rows = gots[c].shape[0] - RIDERS * c
+                later = [] if c else [sends[1]] + ([base_v] if stage == BASE_BY else [])
                 if stage < 1:
-                    sends[c], helds[c] = step_pass(True, stage + 1, c, devices, helds[c], gots[c], rows, riders)
+                    sends[c], helds[c] = step_pass(
+                        True, stage + 1, c, devices, helds[c], gots[c], rows, riders, later
+                    )
                 else:
-                    (sends[c],) = step_pass(False, 0, c, devices, helds[c], gots[c], rows, riders)
+                    (sends[c],) = step_pass(False, 0, c, devices, helds[c], gots[c], rows, riders, later)
                     helds[c] = sends[c]
-        for c in both:
+            if stage == PULL_BY:
+                grad_v = roll(pull_pass(err_b, user_b, sends[:1]), devices)
+        for c in (1, 0):
             gots[c] = exchange(sends[c], devices, stages - 1, c)
             if c:
                 olds[c], stats = update_pass(rate, helds[c], gots[c], olds[c], sends[c])
             else:
-                olds[c] = update_pass(rate, helds[c], gots[c], olds[c])
+                olds[c] = update_pass(rate, helds[c], gots[c], olds[c], None, olds[1:])
         parts = list(olds)
-        for c in both:
-            parts[c] = gather_pass(1, c, devices, parts[c], exchange(parts[c], devices, 1, c))
+        for c in (1, 0):
+            got = exchange(parts[c], devices, 1, c)
+            parts[c] = gather_pass(1, c, devices, parts[c], got, [] if c else parts[1:])
         gots = [exchange(parts[c], devices, 0, c) for c in both]
-        base, grad, base_v, grad_v, stats, own_cols, other_cols = tile_pass(
-            stratum + 1, *tables, base, grad, own_mean, other_mean, stats, base_v, grad_v
+        base, grad, err_b, user_b, stats, own_cols, other_cols, base_v = tile_pass(
+            stratum + 1, *tables, base, grad, own_mean, other_mean, stats, base_v, grad_v, olds[0]
         )
         more = swap(stats, devices)
         other_cols = swap(other_cols, devices)
@@ -649,6 +715,7 @@
     part, stats = update_pass(rate, held, got, old, send)
     mine, other = split_pass(devices, part)
     got = swap(other, devices)
+    grad_v = pull_pass(err_b, user_b, [part])
     users, items = last_pass(devices, stats, base, grad, own_mean, other_mean, base_v, grad_v)
     return (users, items, across_pass(devices, mine, got))
 

time: 122 us -> 122 us (level)
  starting transfers between devices: 52.2 us -> 41.5 us
  waiting for transfers between devices: 51.8 us -> 61.3 us
    ppermute x28, starting transfers between devices: 47.2 us -> 32.9 us  [exchange(): return lax.ppermute(array, 'user', pairs)]
    ppermute x28, waiting for transfers between devices: 50.9 us -> 60.4 us  [exchange(): return lax.ppermute(array, 'user', pairs)]
    ppermute x11, starting transfers between devices: 1.83 us -> 7.98 us  [swap(): return lax.ppermute(array, 'user', [(i, i ^ 1) for i in range(devices)])]
    ppermute x4, starting transfers between devices: 3.13 us -> 0.66 us  [roll(): lax.ppermute(array, 'user', [(i, (i + 1) % devices) for i in range(device...]
    pallas_call x0 -> x4, Pallas kernels: none -> 1.43 us  [the longest x3 0.92 us: pull_pass(): pl.pallas_call(pull_kernel, out_shape=shape(rows, rank), in_specs=[VMEM]...]
  transfers between devices with their start and end apart: 43 -> 43, of which waited for: 19 -> 22; matrix products, arithmetic and copies ran while one was open for 0% -> 0% of each run, Pallas kernels for 11% -> 11%
where the time goes in v8:
time: 122 us
  waiting for transfers between devices  61.3 us (50%)
  starting transfers between devices  41.5 us (34%)
  Pallas kernels  16 us (13%)
  local copies, waits for them, and re-layouts  1.76 us (1%)
    ppermute x28, waiting for transfers between devices, exchange(): return lax.ppermute(array, 'user', pairs)  60.4 us
    ppermute x28, starting transfers between devices, exchange(): return lax.ppermute(array, 'user', pairs)  32.9 us
    ppermute x11, starting transfers between devices, swap(): return lax.ppermute(array, 'user', [(i, i ^ 1) for i in range(devices)])  7.98 us
    pallas_call x3, Pallas kernels, tile_pass(): pl.pallas_call(functools.partial(tile_kernel, stratum, noise_scale, devic...  7 us
  transfers between devices with their start and end apart: 43, of which 22 were waited for; matrix products, arithmetic and copies ran while one was open for 0% of the time, Pallas kernels for 11%

profile of v8, /device:TPU:0, one launch (start us, length us, event | category | flops | bytes accessed | tf_op | source)
XLA Modules:
  0.0 121.7 jit_solution(1616567911369616207)
XLA Ops:
  3.1 1.8 %first_pass.1 = (f32[384,128]{1,0:T(8,128)S(1)}, f32[384,128]{1,0:T(8,128)S(1)}, f32[512,128]{1,0:T(8,128)S(1)}, f32[512,128]{1,0:T(8,128)S(1)}, f32[512,128]{1,...) custom-call(bf16[384,1024]{1,0:T(8,128)(2,1)S(1)} %copy-done.1, ...), custom_call_target="tpu_custom_call" | custom-call | flops 402653184 | bytes 2097152 | tf_op jit(solution)/shard_map/first_pass/pallas_call | solution.py:265
  6.5 2.2 %tile_pass.3 = (f32[384,256]{1,0:T(8,128)S(1)}, f32[384,256]{1,0:T(8,128)S(1)}, bf16[384,384]{1,0:T(8,128)(2,1)S(1)}, bf16[384,256]{1,0:T(8,128)(2,1)S(1)}, f32[8,128]{1,0:T(8,128)S(1)}) custom-call(s32[1,3,6]{2,1,0:T(4,128)S(1)} %copy.12.codes, s32[1,3]{1,0:T(1,128)S(1)} %copy-done.8, bf16[1,3,6,128,128]{4,3,2,1,0:T(8,128)(2,1)S(1)} %copy-done.3, ...), custom_call_target="tpu_custom_call" | custom-call | flops 226492416 | bytes 1572864 | tf_op jit(solution)/shard_map/tile_pass/pallas_call | solution.py:209
  8.7 2.7 %collective-permute-start.4 = (f32[8,128]{1,0:T(8,128)S(1)}, f32[8,128]{1,0:T(8,128)S(1)}, u32[]{:S(2)}, u32[]{:S(2)}) collective-permute-start(f32[8,128]{1,0:T(8,128)S(1)} %get-tuple-element.82.refs_0_), channel_id=1, source_target_pairs={{0,1},{1,0},{2,3},{3,2},{4,5},{5,4},{6,7},{7,6},{8,9},{9,8},{10,11... | collective-permute-start | bytes 12296 | tf_op jit(solution)/shard_map/ppermute | solution.py:595
  12.2 1.6 %collective-permute-start.5 = (f32[264,128]{1,0:T(8,128)S(1)}, f32[264,128]{1,0:T(8,128)S(1)}, u32[]{:S(2)}, u32[]{:S(2)}) collective-permute-start(f32[264,128]{1,0:T(8,128)S(1)} %get-tuple-element.84.refs_0_), channel_id=1, source_target_pairs={{0,4},{1,3},{2,6},{3,1},{4,0},{5,7},{6,2},{7,5},{8,12},{9,11},{10,... | collective-permute-start | bytes 405512 | tf_op jit(solution)/shard_map/ppermute | solution.py:605
  13.8 1.6 %collective-permute-start.2 = (f32[256,128]{1,0:T(8,128)S(1)}, f32[256,128]{1,0:T(8,128)S(1)}, u32[]{:S(2)}, u32[]{:S(2)}) collective-permute-start(f32[256,128]{1,0:T(8,128)S(1)} %get-tuple-element.79), channel_id=1, source_target_pairs={{0,2},{1,5},{2,0},{3,7},{4,6},{5,1},{6,4},{7,3},{8,10},{9,13},{10,... | collective-permute-start | bytes 393224 | tf_op jit(solution)/shard_map/ppermute | solution.py:605
  15.4 5.5 %collective-permute-done.5.got.refs_1_ = f32[264,128]{1,0:T(8,128)S(1)} collective-permute-done((f32[264,128]{1,0:T(8,128)S(1)}, f32[264,128]{1,0:T(8,128)S(1)}, u32[]{:S(2)}, u32[]{:S(2)}) %collective-permute-start.5) | collective-permute-done | bytes 135200 | tf_op jit(solution)/shard_map/ppermute | solution.py:605
  21.6 3.9 %collective-permute-done.7.got.refs_1_ = f32[136,128]{1,0:T(8,128)S(1)} collective-permute-done((f32[136,128]{1,0:T(8,128)S(1)}, f32[136,128]{1,0:T(8,128)S(1)}, u32[]{:S(2)}, u32[]{:S(2)}) %collective-permute-start.7) | collective-permute-done | bytes 69664 | tf_op jit(solution)/shard_map/ppermute | solution.py:605
  26.0 1.5 %collective-permute-start.10 = (f32[136,128]{1,0:T(8,128)S(1)}, f32[136,128]{1,0:T(8,128)S(1)}, u32[]{:S(2)}, u32[]{:S(2)}) collective-permute-start(f32[136,128]{1,0:T(8,128)S(1)} %step_pass.21.refs_0_.held), channel_id=1, source_target_pairs={{0,16},{1,17},{2,18},{3,19},{4,20},{5,21},{6,22},{7,23},{8,24},{9,... | collective-permute-start | bytes 208904 | tf_op jit(solution)/shard_map/ppermute | solution.py:605
  27.4 1.6 %collective-permute-start.9 = (f32[128,128]{1,0:T(8,128)S(1)}, f32[128,128]{1,0:T(8,128)S(1)}, u32[]{:S(2)}, u32[]{:S(2)}) collective-permute-start(f32[128,128]{1,0:T(8,128)S(1)} %step_pass.22.held.refs_0_), channel_id=1, source_target_pairs={{0,8},{1,9},{2,10},{3,11},{4,12},{5,13},{6,14},{7,15},{8,0},{9,1},... | collective-permute-start | bytes 196616 | tf_op jit(solution)/shard_map/ppermute | solution.py:605
  29.0 4.3 %collective-permute-done.10.got.refs_1_ = f32[136,128]{1,0:T(8,128)S(1)} collective-permute-done((f32[136,128]{1,0:T(8,128)S(1)}, f32[136,128]{1,0:T(8,128)S(1)}, u32[]{:S(2)}, u32[]{:S(2)}) %collective-permute-start.10) | collective-permute-done | bytes 69664 | tf_op jit(solution)/shard_map/ppermute | solution.py:605
  33.7 2.8 %collective-permute-start.11 = (f32[128,128]{1,0:T(8,128)S(1)}, f32[128,128]{1,0:T(8,128)S(1)}, u32[]{:S(2)}, u32[]{:S(2)}) collective-permute-start(f32[128,128]{1,0:T(8,128)S(1)} %step_pass.24.held), channel_id=1, source_target_pairs={{0,16},{1,17},{2,18},{3,19},{4,20},{5,21},{6,22},{7,23},{8,24},{9,... | collective-permute-start | bytes 196616 | tf_op jit(solution)/shard_map/ppermute | solution.py:605
  36.4 2.1 %collective-permute-done.12.got = f32[136,128]{1,0:T(8,128)S(1)} collective-permute-done((f32[136,128]{1,0:T(8,128)S(1)}, f32[136,128]{1,0:T(8,128)S(1)}, u32[]{:S(2)}, u32[]{:S(2)}) %collective-permute-start.12) | collective-permute-done | bytes 69664 | tf_op jit(solution)/shard_map/ppermute | solution.py:605
  40.8 2.4 %tile_pass.4 = (f32[384,256]{1,0:T(8,128)S(1)}, f32[384,256]{1,0:T(8,128)S(1)}, bf16[384,384]{1,0:T(8,128)(2,1)S(1)}, bf16[384,256]{1,0:T(8,128)(2,1)S(1)}, f32[...) custom-call(s32[1,3,6]{2,1,0:T(4,128)S(1)} %copy.12.codes, ...), custom_call_target="tpu_custom_call" | custom-call | flops 226492416 | bytes 1572864 | tf_op jit(solution)/shard_map/tile_pass/pallas_call | solution.py:209
  44.7 4.4 %collective-permute-start.15 = (f32[256,128]{1,0:T(8,128)S(1)}, f32[256,128]{1,0:T(8,128)S(1)}, u32[]{:S(2)}, u32[]{:S(2)}) collective-permute-start(f32[256,128]{1,0:T(8,128)S(1)} %gather_pass.5.part), channel_id=1, source_target_pairs={{0,2},{1,5},{2,0},{3,7},{4,6},{5,1},{6,4},{7,3},{8,10},{9,13},{10,... | collective-permute-start | bytes 393224 | tf_op jit(solution)/shard_map/ppermute | solution.py:605
  50.9 2.5 %collective-permute-done.15.got = f32[256,128]{1,0:T(8,128)S(1)} collective-permute-done((f32[256,128]{1,0:T(8,128)S(1)}, f32[256,128]{1,0:T(8,128)S(1)}, u32[]{:S(2)}, u32[]{:S(2)}) %collective-permute-start.15) | collective-permute-done | bytes 131104 | tf_op jit(solution)/shard_map/ppermute | solution.py:605
  53.8 4.0 %collective-permute-done.16.got = f32[256,128]{1,0:T(8,128)S(1)} collective-permute-done((f32[256,128]{1,0:T(8,128)S(1)}, f32[256,128]{1,0:T(8,128)S(1)}, u32[]{:S(2)}, u32[]{:S(2)}) %collective-permute-start.16) | collective-permute-done | bytes 131104 | tf_op jit(solution)/shard_map/ppermute | solution.py:605
  59.8 5.0 %collective-permute-done.21.got.refs_1_ = f32[264,128]{1,0:T(8,128)S(1)} collective-permute-done((f32[264,128]{1,0:T(8,128)S(1)}, f32[264,128]{1,0:T(8,128)S(1)}, u32[]{:S(2)}, u32[]{:S(2)}) %collective-permute-start.21) | collective-permute-done | bytes 135200 | tf_op jit(solution)/shard_map/ppermute | solution.py:605
  66.0 3.2 %collective-permute-done.23.got.refs_1_ = f32[136,128]{1,0:T(8,128)S(1)} collective-permute-done((f32[136,128]{1,0:T(8,128)S(1)}, f32[136,128]{1,0:T(8,128)S(1)}, u32[]{:S(2)}, u32[]{:S(2)}) %collective-permute-start.23) | collective-permute-done | bytes 69664 | tf_op jit(solution)/shard_map/ppermute | solution.py:605
  69.7 2.1 %collective-permute-start.33 = (f32[384,128]{1,0:T(8,128)S(1)}, f32[384,128]{1,0:T(8,128)S(1)}, u32[]{:S(2)}, u32[]{:S(2)}) collective-permute-start(f32[384,128]{1,0:T(8,128)S(1)} %get-tuple-element.116), channel_id=1, source_target_pairs={{0,1},{1,0},{2,3},{3,2},{4,5},{5,4},{6,7},{7,6},{8,9},{9,8},{10,11... | collective-permute-start | bytes 589832 | tf_op jit(solution)/shard_map/ppermute | solution.py:595
  71.8 5.3 %collective-permute-done.26.got.refs_1_ = f32[136,128]{1,0:T(8,128)S(1)} collective-permute-done((f32[136,128]{1,0:T(8,128)S(1)}, f32[136,128]{1,0:T(8,128)S(1)}, u32[]{:S(2)}, u32[]{:S(2)}) %collective-permute-start.26) | collective-permute-done | bytes 69664 | tf_op jit(solution)/shard_map/ppermute | solution.py:605
  77.5 1.6 %collective-permute-start.27 = (f32[128,128]{1,0:T(8,128)S(1)}, f32[128,128]{1,0:T(8,128)S(1)}, u32[]{:S(2)}, u32[]{:S(2)}) collective-permute-start(f32[128,128]{1,0:T(8,128)S(1)} %step_pass.30.held), channel_id=1, source_target_pairs={{0,16},{1,17},{2,18},{3,19},{4,20},{5,21},{6,22},{7,23},{8,24},{9,... | collective-permute-start | bytes 196616 | tf_op jit(solution)/shard_map/ppermute | solution.py:605
  79.1 2.4 %collective-permute-done.28.got = f32[136,128]{1,0:T(8,128)S(1)} collective-permute-done((f32[136,128]{1,0:T(8,128)S(1)}, f32[136,128]{1,0:T(8,128)S(1)}, u32[]{:S(2)}, u32[]{:S(2)}) %collective-permute-start.28) | collective-permute-done | bytes 69664 | tf_op jit(solution)/shard_map/ppermute | solution.py:605
  82.9 1.6 %collective-permute-start.29 = (f32[128,128]{1,0:T(8,128)S(1)}, f32[128,128]{1,0:T(8,128)S(1)}, u32[]{:S(2)}, u32[]{:S(2)}) collective-permute-start(f32[128,128]{1,0:T(8,128)S(1)} %update_pass.8.part.refs_7_), channel_id=1, source_target_pairs={{0,4},{1,3},{2,6},{3,1},{4,0},{5,7},{6,2},{7,5},{8,12},{9,11},{10,... | collective-permute-start | bytes 196616 | tf_op jit(solution)/shard_map/ppermute | solution.py:605
  84.5 2.4 %tile_pass.5 = (f32[384,256]{1,0:T(8,128)S(1)}, f32[384,256]{1,0:T(8,128)S(1)}, bf16[384,384]{1,0:T(8,128)(2,1)S(1)}, bf16[384,256]{1,0:T(8,128)(2,1)S(1)}, f32[...) custom-call(s32[1,3,6]{2,1,0:T(4,128)S(1)} %copy.12.codes, ...), custom_call_target="tpu_custom_call" | custom-call | flops 226492416 | bytes 1572864 | tf_op jit(solution)/shard_map/tile_pass/pallas_call | solution.py:209
  87.9 4.3 %collective-permute-start.31 = (f32[256,128]{1,0:T(8,128)S(1)}, f32[256,128]{1,0:T(8,128)S(1)}, u32[]{:S(2)}, u32[]{:S(2)}) collective-permute-start(f32[256,128]{1,0:T(8,128)S(1)} %gather_pass.7.part.first_part), channel_id=1, source_target_pairs={{0,2},{1,5},{2,0},{3,7},{4,6},{5,1},{6,4},{7,3},{8,10},{9,13},{10,... | collective-permute-start | bytes 393224 | tf_op jit(solution)/shard_map/ppermute | solution.py:605
  92.2 1.7 %collective-permute-start.32 = (f32[256,128]{1,0:T(8,128)S(1)}, f32[256,128]{1,0:T(8,128)S(1)}, u32[]{:S(2)}, u32[]{:S(2)}) collective-permute-start(f32[256,128]{1,0:T(8,128)S(1)} %gather_pass.6.refs_0_.part), channel_id=1, source_target_pairs={{0,4},{1,3},{2,6},{3,1},{4,0},{5,7},{6,2},{7,5},{8,12},{9,11},{10,... | collective-permute-start | bytes 393224 | tf_op jit(solution)/shard_map/ppermute | solution.py:605
  93.9 2.1 %collective-permute-done.31.got.first_got = f32[256,128]{1,0:T(8,128)S(1)} collective-permute-done((f32[256,128]{1,0:T(8,128)S(1)}, f32[256,128]{1,0:T(8,128)S(1)}, u32[]{:S(2)}, u32[]{:S(2)}) %collective-permute-start.31) | collective-permute-done | bytes 131104 | tf_op jit(solution)/shard_map/ppermute | solution.py:605
  99.9 5.0 %collective-permute-done.37.got.refs_1_ = f32[520,128]{1,0:T(8,128)S(1)} collective-permute-done((f32[520,128]{1,0:T(8,128)S(1)}, f32[520,128]{1,0:T(8,128)S(1)}, u32[]{:S(2)}, u32[]{:S(2)}) %collective-permute-start.37) | collective-permute-done | bytes 266272 | tf_op jit(solution)/shard_map/ppermute | solution.py:605
  104.9 1.8 %collective-permute-start.38 = (f32[264,128]{1,0:T(8,128)S(1)}, f32[264,128]{1,0:T(8,128)S(1)}, u32[]{:S(2)}, u32[]{:S(2)}) collective-permute-start(f32[264,128]{1,0:T(8,128)S(1)} %get-tuple-element.126.refs_0_), channel_id=1, source_target_pairs={{0,4},{1,3},{2,6},{3,1},{4,0},{5,7},{6,2},{7,5},{8,12},{9,11},{10,... | collective-permute-start | bytes 405512 | tf_op jit(solution)/shard_map/ppermute | solution.py:605
  106.7 3.3 %collective-permute-done.38.got.refs_1_ = f32[264,128]{1,0:T(8,128)S(1)} collective-permute-done((f32[264,128]{1,0:T(8,128)S(1)}, f32[264,128]{1,0:T(8,128)S(1)}, u32[]{:S(2)}, u32[]{:S(2)}) %collective-permute-start.38) | collective-permute-done | bytes 135200 | tf_op jit(solution)/shard_map/ppermute | solution.py:605
  110.1 4.3 %collective-permute-done.39.got.refs_1_ = f32[136,128]{1,0:T(8,128)S(1)} collective-permute-done((f32[136,128]{1,0:T(8,128)S(1)}, f32[136,128]{1,0:T(8,128)S(1)}, u32[]{:S(2)}, u32[]{:S(2)}) %collective-permute-start.39) | collective-permute-done | bytes 69664 | tf_op jit(solution)/shard_map/ppermute | solution.py:605
  115.0 4.5 %collective-permute-done.40.got = f32[72,128]{1,0:T(8,128)S(1)} collective-permute-done((f32[72,128]{1,0:T(8,128)S(1)}, f32[72,128]{1,0:T(8,128)S(1)}, u32[]{:S(2)}, u32[]{:S(2)}) %collective-permute-start.40) | collective-permute-done | bytes 36896 | tf_op jit(solution)/shard_map/ppermute | solution.py:605
  (119 shorter events, 25.2 us)
Async XLA Ops:
  2.0 48.3 %collective-permute-start = (f32[384,1024]{1,0:T(8,128)S(1)}, f32[384,1024]{1,0:T(8,128)S(1)}, u32[]{:S(2)}, u32[]{:S(2)}) collective-permute-start(f32[384,1024]{1,0:T(8,128)S(1)} %widen_pass.1), channel_id=1, source_target_pairs={{0,1},{1,0},{2,3},{3,2},{4,5},{5,4},{6,7},{7,6},{8,9},{9,8},{10,11... | collective-permute-start | bytes 4718600 | tf_op jit(solution)/shard_map/ppermute | solution.py:595
  4.9 7.3 %collective-permute-start.3 = (f32[512,128]{1,0:T(8,128)S(1)}, f32[512,128]{1,0:T(8,128)S(1)}, u32[]{:S(2)}, u32[]{:S(2)}) collective-permute-start(f32[512,128]{1,0:T(8,128)S(1)} %get-tuple-element.81), channel_id=1, source_target_pairs={{0,1},{1,0},{2,3},{3,2},{4,5},{5,4},{6,7},{7,6},{8,9},{9,8},{10,11... | collective-permute-start | bytes 786440 | tf_op jit(solution)/shard_map/ppermute | solution.py:595
  5.4 8.4 %collective-permute-start.1 = (f32[512,128]{1,0:T(8,128)S(1)}, f32[512,128]{1,0:T(8,128)S(1)}, u32[]{:S(2)}, u32[]{:S(2)}) collective-permute-start(f32[512,128]{1,0:T(8,128)S(1)} %get-tuple-element.77), channel_id=1, source_target_pairs={{0,1},{1,0},{2,3},{3,2},{4,5},{5,4},{6,7},{7,6},{8,9},{9,8},{10,11... | collective-permute-start | bytes 786440 | tf_op jit(solution)/shard_map/ppermute | solution.py:595
  6.0 19.5 %collective-permute-start.8 = (f32[384,256]{1,0:T(8,128)S(1)}, f32[384,256]{1,0:T(8,128)S(1)}, u32[]{:S(2)}, u32[]{:S(2)}) collective-permute-start(f32[384,256]{1,0:T(8,128)S(1)} %base_pass.1), channel_id=1, source_target_pairs={{0,1},{1,2},{2,3},{3,4},{4,5},{5,6},{6,7},{7,8},{8,9},{9,10},{10,1... | collective-permute-start | bytes 1179656 | tf_op jit(solution)/shard_map/ppermute | solution.py:599
  12.2 8.7 %collective-permute-start.5 = (f32[264,128]{1,0:T(8,128)S(1)}, f32[264,128]{1,0:T(8,128)S(1)}, u32[]{:S(2)}, u32[]{:S(2)}) collective-permute-start(f32[264,128]{1,0:T(8,128)S(1)} %get-tuple-element.84.refs_0_), channel_id=1, source_target_pairs={{0,4},{1,3},{2,6},{3,1},{4,0},{5,7},{6,2},{7,5},{8,12},{9,11},{10,... | collective-permute-start | bytes 405512 | tf_op jit(solution)/shard_map/ppermute | solution.py:605
  13.8 7.2 %collective-permute-start.2 = (f32[256,128]{1,0:T(8,128)S(1)}, f32[256,128]{1,0:T(8,128)S(1)}, u32[]{:S(2)}, u32[]{:S(2)}) collective-permute-start(f32[256,128]{1,0:T(8,128)S(1)} %get-tuple-element.79), channel_id=1, source_target_pairs={{0,2},{1,5},{2,0},{3,7},{4,6},{5,1},{6,4},{7,3},{8,10},{9,13},{10,... | collective-permute-start | bytes 393224 | tf_op jit(solution)/shard_map/ppermute | solution.py:605
  25.9 14.9 %collective-permute-start.17 = (f32[384,256]{1,0:T(8,128)S(1)}, f32[384,256]{1,0:T(8,128)S(1)}, u32[]{:S(2)}, u32[]{:S(2)}) collective-permute-start(f32[384,256]{1,0:T(8,128)S(1)} %pull_pass.3), channel_id=1, source_target_pairs={{0,1},{1,2},{2,3},{3,4},{4,5},{5,6},{6,7},{7,8},{8,9},{9,10},{10,1... | collective-permute-start | bytes 1179656 | tf_op jit(solution)/shard_map/ppermute | solution.py:599
  26.0 7.3 %collective-permute-start.10 = (f32[136,128]{1,0:T(8,128)S(1)}, f32[136,128]{1,0:T(8,128)S(1)}, u32[]{:S(2)}, u32[]{:S(2)}) collective-permute-start(f32[136,128]{1,0:T(8,128)S(1)} %step_pass.21.refs_0_.held), channel_id=1, source_target_pairs={{0,16},{1,17},{2,18},{3,19},{4,20},{5,21},{6,22},{7,23},{8,24},{9,... | collective-permute-start | bytes 208904 | tf_op jit(solution)/shard_map/ppermute | solution.py:605
  27.4 6.2 %collective-permute-start.9 = (f32[128,128]{1,0:T(8,128)S(1)}, f32[128,128]{1,0:T(8,128)S(1)}, u32[]{:S(2)}, u32[]{:S(2)}) collective-permute-start(f32[128,128]{1,0:T(8,128)S(1)} %step_pass.22.held.refs_0_), channel_id=1, source_target_pairs={{0,8},{1,9},{2,10},{3,11},{4,12},{5,13},{6,14},{7,15},{8,0},{9,1},... | collective-permute-start | bytes 196616 | tf_op jit(solution)/shard_map/ppermute | solution.py:605
  33.3 5.2 %collective-permute-start.12 = (f32[136,128]{1,0:T(8,128)S(1)}, f32[136,128]{1,0:T(8,128)S(1)}, u32[]{:S(2)}, u32[]{:S(2)}) collective-permute-start(f32[136,128]{1,0:T(8,128)S(1)} %step_pass.23.refs_0_.held), channel_id=1, source_target_pairs={{0,8},{1,9},{2,10},{3,11},{4,12},{5,13},{6,14},{7,15},{8,0},{9,1},... | collective-permute-start | bytes 208904 | tf_op jit(solution)/shard_map/ppermute | solution.py:605
  33.7 6.7 %collective-permute-start.11 = (f32[128,128]{1,0:T(8,128)S(1)}, f32[128,128]{1,0:T(8,128)S(1)}, u32[]{:S(2)}, u32[]{:S(2)}) collective-permute-start(f32[128,128]{1,0:T(8,128)S(1)} %step_pass.24.held), channel_id=1, source_target_pairs={{0,16},{1,17},{2,18},{3,19},{4,20},{5,21},{6,22},{7,23},{8,24},{9,... | collective-permute-start | bytes 196616 | tf_op jit(solution)/shard_map/ppermute | solution.py:605
  38.6 5.7 %collective-permute-start.14 = (f32[128,128]{1,0:T(8,128)S(1)}, f32[128,128]{1,0:T(8,128)S(1)}, u32[]{:S(2)}, u32[]{:S(2)}) collective-permute-start(f32[128,128]{1,0:T(8,128)S(1)} %get-tuple-element.91.refs_0_.part.old), channel_id=1, source_target_pairs={{0,2},{1,5},{2,0},{3,7},{4,6},{5,1},{6,4},{7,3},{8,10},{9,13},{10,... | collective-permute-start | bytes 196616 | tf_op jit(solution)/shard_map/ppermute | solution.py:605
  43.2 14.6 %collective-permute-start.18 = (f32[384,128]{1,0:T(8,128)S(1)}, f32[384,128]{1,0:T(8,128)S(1)}, u32[]{:S(2)}, u32[]{:S(2)}) collective-permute-start(f32[384,128]{1,0:T(8,128)S(1)} %get-tuple-element.100), channel_id=1, source_target_pairs={{0,1},{1,0},{2,3},{3,2},{4,5},{5,4},{6,7},{7,6},{8,9},{9,8},{10,11... | collective-permute-start | bytes 589832 | tf_op jit(solution)/shard_map/ppermute | solution.py:595
  44.2 25.0 %collective-permute-start.24 = (f32[384,256]{1,0:T(8,128)S(1)}, f32[384,256]{1,0:T(8,128)S(1)}, u32[]{:S(2)}, u32[]{:S(2)}) collective-permute-start(f32[384,256]{1,0:T(8,128)S(1)} %get-tuple-element.111), channel_id=1, source_target_pairs={{0,1},{1,2},{2,3},{3,4},{4,5},{5,6},{6,7},{7,8},{8,9},{9,10},{10,1... | collective-permute-start | bytes 1179656 | tf_op jit(solution)/shard_map/ppermute | solution.py:599
  44.7 8.7 %collective-permute-start.15 = (f32[256,128]{1,0:T(8,128)S(1)}, f32[256,128]{1,0:T(8,128)S(1)}, u32[]{:S(2)}, u32[]{:S(2)}) collective-permute-start(f32[256,128]{1,0:T(8,128)S(1)} %gather_pass.5.part), channel_id=1, source_target_pairs={{0,2},{1,5},{2,0},{3,7},{4,6},{5,1},{6,4},{7,3},{8,10},{9,13},{10,... | collective-permute-start | bytes 393224 | tf_op jit(solution)/shard_map/ppermute | solution.py:605
  49.2 8.7 %collective-permute-start.16 = (f32[256,128]{1,0:T(8,128)S(1)}, f32[256,128]{1,0:T(8,128)S(1)}, u32[]{:S(2)}, u32[]{:S(2)}) collective-permute-start(f32[256,128]{1,0:T(8,128)S(1)} %gather_pass.4.refs_0_.part), channel_id=1, source_target_pairs={{0,4},{1,3},{2,6},{3,1},{4,0},{5,7},{6,2},{7,5},{8,12},{9,11},{10,... | collective-permute-start | bytes 393224 | tf_op jit(solution)/shard_map/ppermute | solution.py:605
  50.4 8.2 %collective-permute-start.20 = (f32[8,128]{1,0:T(8,128)S(1)}, f32[8,128]{1,0:T(8,128)S(1)}, u32[]{:S(2)}, u32[]{:S(2)}) collective-permute-start(f32[8,128]{1,0:T(8,128)S(1)} %get-tuple-element.104.stats), channel_id=1, source_target_pairs={{0,1},{1,0},{2,3},{3,2},{4,5},{5,4},{6,7},{7,6},{8,9},{9,8},{10,11... | collective-permute-start | bytes 12296 | tf_op jit(solution)/shard_map/ppermute | solution.py:595
  58.9 6.0 %collective-permute-start.21 = (f32[264,128]{1,0:T(8,128)S(1)}, f32[264,128]{1,0:T(8,128)S(1)}, u32[]{:S(2)}, u32[]{:S(2)}) collective-permute-start(f32[264,128]{1,0:T(8,128)S(1)} %get-tuple-element.106.refs_0_), channel_id=1, source_target_pairs={{0,4},{1,3},{2,6},{3,1},{4,0},{5,7},{6,2},{7,5},{8,12},{9,11},{10,... | collective-permute-start | bytes 405512 | tf_op jit(solution)/shard_map/ppermute | solution.py:605
  59.8 5.1 %collective-permute-start.19 = (f32[256,128]{1,0:T(8,128)S(1)}, f32[256,128]{1,0:T(8,128)S(1)}, u32[]{:S(2)}, u32[]{:S(2)}) collective-permute-start(f32[256,128]{1,0:T(8,128)S(1)} %get-tuple-element.102), channel_id=1, source_target_pairs={{0,2},{1,5},{2,0},{3,7},{4,6},{5,1},{6,4},{7,3},{8,10},{9,13},{10,... | collective-permute-start | bytes 393224 | tf_op jit(solution)/shard_map/ppermute | solution.py:605
  69.7 14.8 %collective-permute-start.34 = (f32[384,256]{1,0:T(8,128)S(1)}, f32[384,256]{1,0:T(8,128)S(1)}, u32[]{:S(2)}, u32[]{:S(2)}) collective-permute-start(f32[384,256]{1,0:T(8,128)S(1)} %pull_pass.4), channel_id=1, source_target_pairs={{0,1},{1,2},{2,3},{3,4},{4,5},{5,6},{6,7},{7,8},{8,9},{9,10},{10,1... | collective-permute-start | bytes 1179656 | tf_op jit(solution)/shard_map/ppermute | solution.py:599
  69.7 14.7 %collective-permute-start.33 = (f32[384,128]{1,0:T(8,128)S(1)}, f32[384,128]{1,0:T(8,128)S(1)}, u32[]{:S(2)}, u32[]{:S(2)}) collective-permute-start(f32[384,128]{1,0:T(8,128)S(1)} %get-tuple-element.116), channel_id=1, source_target_pairs={{0,1},{1,0},{2,3},{3,2},{4,5},{5,4},{6,7},{7,6},{8,9},{9,8},{10,11... | collective-permute-start | bytes 589832 | tf_op jit(solution)/shard_map/ppermute | solution.py:595
  71.8 5.3 %collective-permute-start.26 = (f32[136,128]{1,0:T(8,128)S(1)}, f32[136,128]{1,0:T(8,128)S(1)}, u32[]{:S(2)}, u32[]{:S(2)}) collective-permute-start(f32[136,128]{1,0:T(8,128)S(1)} %step_pass.27.refs_0_.held), channel_id=1, source_target_pairs={{0,16},{1,17},{2,18},{3,19},{4,20},{5,21},{6,22},{7,23},{8,24},{9,... | collective-permute-start | bytes 208904 | tf_op jit(solution)/shard_map/ppermute | solution.py:605
  71.8 5.7 %collective-permute-start.25 = (f32[128,128]{1,0:T(8,128)S(1)}, f32[128,128]{1,0:T(8,128)S(1)}, u32[]{:S(2)}, u32[]{:S(2)}) collective-permute-start(f32[128,128]{1,0:T(8,128)S(1)} %step_pass.28.held.refs_0_), channel_id=1, source_target_pairs={{0,8},{1,9},{2,10},{3,11},{4,12},{5,13},{6,14},{7,15},{8,0},{9,1},... | collective-permute-start | bytes 196616 | tf_op jit(solution)/shard_map/ppermute | solution.py:605
  77.5 5.3 %collective-permute-start.27 = (f32[128,128]{1,0:T(8,128)S(1)}, f32[128,128]{1,0:T(8,128)S(1)}, u32[]{:S(2)}, u32[]{:S(2)}) collective-permute-start(f32[128,128]{1,0:T(8,128)S(1)} %step_pass.30.held), channel_id=1, source_target_pairs={{0,16},{1,17},{2,18},{3,19},{4,20},{5,21},{6,22},{7,23},{8,24},{9,... | collective-permute-start | bytes 196616 | tf_op jit(solution)/shard_map/ppermute | solution.py:605
  81.5 6.4 %collective-permute-start.30 = (f32[128,128]{1,0:T(8,128)S(1)}, f32[128,128]{1,0:T(8,128)S(1)}, u32[]{:S(2)}, u32[]{:S(2)}) collective-permute-start(f32[128,128]{1,0:T(8,128)S(1)} %get-tuple-element.112.refs_0_.part), channel_id=1, source_target_pairs={{0,2},{1,5},{2,0},{3,7},{4,6},{5,1},{6,4},{7,3},{8,10},{9,13},{10,... | collective-permute-start | bytes 196616 | tf_op jit(solution)/shard_map/ppermute | solution.py:605
  82.9 5.0 %collective-permute-start.29 = (f32[128,128]{1,0:T(8,128)S(1)}, f32[128,128]{1,0:T(8,128)S(1)}, u32[]{:S(2)}, u32[]{:S(2)}) collective-permute-start(f32[128,128]{1,0:T(8,128)S(1)} %update_pass.8.part.refs_7_), channel_id=1, source_target_pairs={{0,4},{1,3},{2,6},{3,1},{4,0},{5,7},{6,2},{7,5},{8,12},{9,11},{10,... | collective-permute-start | bytes 196616 | tf_op jit(solution)/shard_map/ppermute | solution.py:605
  86.9 10.3 %collective-permute-start.35 = (f32[384,128]{1,0:T(8,128)S(1)}, f32[384,128]{1,0:T(8,128)S(1)}, u32[]{:S(2)}, u32[]{:S(2)}) collective-permute-start(f32[384,128]{1,0:T(8,128)S(1)} %get-tuple-element.121), channel_id=1, source_target_pairs={{0,1},{1,0},{2,3},{3,2},{4,5},{5,4},{6,7},{7,6},{8,9},{9,8},{10,11... | collective-permute-start | bytes 589832 | tf_op jit(solution)/shard_map/ppermute | solution.py:595
  87.9 8.1 %collective-permute-start.31 = (f32[256,128]{1,0:T(8,128)S(1)}, f32[256,128]{1,0:T(8,128)S(1)}, u32[]{:S(2)}, u32[]{:S(2)}) collective-permute-start(f32[256,128]{1,0:T(8,128)S(1)} %gather_pass.7.part.first_part), channel_id=1, source_target_pairs={{0,2},{1,5},{2,0},{3,7},{4,6},{5,1},{6,4},{7,3},{8,10},{9,13},{10,... | collective-permute-start | bytes 393224 | tf_op jit(solution)/shard_map/ppermute | solution.py:605
  98.4 6.5 %collective-permute-start.37 = (f32[520,128]{1,0:T(8,128)S(1)}, f32[520,128]{1,0:T(8,128)S(1)}, u32[]{:S(2)}, u32[]{:S(2)}) collective-permute-start(f32[520,128]{1,0:T(8,128)S(1)} %get-tuple-element.124.refs_0_), channel_id=1, source_target_pairs={{0,2},{1,5},{2,0},{3,7},{4,6},{5,1},{6,4},{7,3},{8,10},{9,13},{10,... | collective-permute-start | bytes 798728 | tf_op jit(solution)/shard_map/ppermute | solution.py:605
  104.9 5.1 %collective-permute-start.38 = (f32[264,128]{1,0:T(8,128)S(1)}, f32[264,128]{1,0:T(8,128)S(1)}, u32[]{:S(2)}, u32[]{:S(2)}) collective-permute-start(f32[264,128]{1,0:T(8,128)S(1)} %get-tuple-element.126.refs_0_), channel_id=1, source_target_pairs={{0,4},{1,3},{2,6},{3,1},{4,0},{5,7},{6,2},{7,5},{8,12},{9,11},{10,... | collective-permute-start | bytes 405512 | tf_op jit(solution)/shard_map/ppermute | solution.py:605
  106.7 13.3 %collective-permute-start.41 = (f32[384,128]{1,0:T(8,128)S(1)}, f32[384,128]{1,0:T(8,128)S(1)}, u32[]{:S(2)}, u32[]{:S(2)}) collective-permute-start(f32[384,128]{1,0:T(8,128)S(1)} %get-tuple-element.136), channel_id=1, source_target_pairs={{0,1},{1,0},{2,3},{3,2},{4,5},{5,4},{6,7},{7,6},{8,9},{9,8},{10,11... | collective-permute-start | bytes 589832 | tf_op jit(solution)/shard_map/ppermute | solution.py:595
  114.5 5.1 %collective-permute-start.40 = (f32[72,128]{1,0:T(8,128)S(1)}, f32[72,128]{1,0:T(8,128)S(1)}, u32[]{:S(2)}, u32[]{:S(2)}) collective-permute-start(f32[72,128]{1,0:T(8,128)S(1)} %get-tuple-element.130.refs_0_), channel_id=1, source_target_pairs={{0,16},{1,17},{2,18},{3,19},{4,20},{5,21},{6,22},{7,23},{8,24},{9,... | collective-permute-start | bytes 110600 | tf_op jit(solution)/shard_map/ppermute | solution.py:605
  (21 other events, 82.2 us)

commit v9 on v7

--- a/solution.py
+++ b/solution.py
@@ -63,50 +63,28 @@
     return (1.0 + stats[1:2, :] / 2.0) / (1.0 + stats[0:1, :] / 2.0)
 
 
-def tile_kernel(stratum, noise_scale, devices, codes, count, ratings, user_noise, item_noise, *refs):
-    if stratum == 0:
-        users_in, items_in = refs[:2]
-        base_u, grad_u, base_v, grad_v, stats = refs[2:7]
-        refs = refs[7:]
-    else:
-        old_base, old_grad, own_mean, other_mean, old_stats, old_base_v, old_grad_v = refs[:7]
-        base_u, grad_u, base_v, grad_v, stats, own_cols, other_cols = refs[7:14]
-        refs = refs[14:]
-    tiles, noise_u, noise_v, users, items, pred, err_b, sems = refs
-    core = where_am_i(devices)[0]
-    rows, rank = users.shape
-    width = rank // CORES
+def tile_kernel(stratum, noise_scale, codes, count, ratings, user_noise, item_noise, *refs):
+    users_in, items_in, base_u, grad_u, base_v, grad_v, stats = refs[:7]
+    tiles, noise_u, noise_v, pred, err_b, sems = refs[7:13]
+    rows = err_b.shape[0]
     tile = tiles.shape[-1]
     grid = rows // tile
+    moves = [
+        (ratings.at[0, stratum], tiles),
+        (user_noise.at[stratum], noise_u),
+        (item_noise.at[stratum], noise_v),
+    ]
+    users, items = users_in, items_in
+    if stratum == 0:
+        users, items = refs[13:]
+        moves += [(users_in, users), (items_in, items)]
     copies = [
-        pltpu.make_async_copy(source, target, sems.at[n])
-        for n, (source, target) in enumerate(
-            [
-                (ratings.at[0, stratum], tiles),
-                (user_noise.at[stratum], noise_u),
-                (item_noise.at[stratum], noise_v),
-            ]
-            + ([(users_in, users), (items_in, items)] if stratum == 0 else [])
-        )
+        pltpu.make_async_copy(source, target, sems.at[n]) for n, (source, target) in enumerate(moves)
     ]
     for copy in copies[::-1]:
         copy.start()
-    if stratum == 0:
-        copies[4].wait()
-        copies[3].wait()
-    else:
-        precision = precision_of(old_stats[...])
-        precision = jnp.concatenate([precision] * CORES, 1)
-        items[...] = old_base_v[...] + precision * old_grad_v[...]
-        new = old_base[...] + precision * old_grad[...]
-        here = core == 0
-        pull = step_size * prior_prec
-        left = jnp.where(here, own_mean[...], other_mean[...])
-        right = jnp.where(here, other_mean[...], own_mean[...])
-        users[:, :width] = new[:, :width] + pull * left
-        users[:, width:] = new[:, width:] + pull * right
-        own_cols[...] = half_of(users, core)
-        other_cols[...] = half_of(users, 1 - core)
+    for copy in copies[3:]:
+        copy.wait()
     user_b = users[...].astype(bf16)
     item_b = items[...].astype(bf16)
     pred[...] = dot(user_b, item_b, NT)
@@ -116,8 +94,8 @@
     copies[0].wait()
     for slot in range(tiles.shape[0]):
         code = codes[0, stratum, slot]
-        at_rows = pl.ds(pl.multiple_of(code // grid * tile, tile), tile)
-        at_cols = pl.ds(pl.multiple_of(code % grid * tile, tile), tile)
+        at_rows = rows_at(code // grid, tile)
+        at_cols = rows_at(code % grid, tile)
         live = (slot < live_slots).astype(f32)
         err = (tiles[slot].astype(f32) - pred[at_rows, at_cols]) * live
         sse = sse + err * err
@@ -129,43 +107,36 @@
     stats[...] = jnp.where(row == 0, total, jnp.where(row == 1, counted, 0.0))
     grad_u[...] = step_size * dot(err_all, item_b)
     grad_v[...] = step_size * dot(err_all, user_b, TN)
-    copies[2].wait()
-    base_v[...] = (1.0 - step_size * item_prec) * items[...] + noise_scale * noise_v[...].astype(
-        f32
-    )
     copies[1].wait()
     base_u[...] = (1.0 - step_size * prior_prec) * users[...] + noise_scale * noise_u[...].astype(
         f32
     )
-
-
-def tile_pass(stratum, devices, codes, count, ratings, user_noise, item_noise, *state):
+    copies[2].wait()
+    base_v[...] = (1.0 - step_size * item_prec) * items[...] + noise_scale * noise_v[...].astype(f32)
+
+
+def tile_pass(stratum, codes, count, ratings, user_noise, item_noise, users, items):
     slots, tile = ratings.shape[2:4]
-    rows, rank = user_noise.shape[1:]
-    noise_scale = math.sqrt(2.0 * step_size)
-    width = rank // CORES
-    outs = [shape(rows, rank)] * 4 + [shape(RIDERS, width)]
-    if stratum:
-        outs += [shape(rows, width)] * 2
-    return pl.pallas_call(
-        functools.partial(tile_kernel, stratum, noise_scale, devices),
-        out_shape=tuple(outs),
-        in_specs=[SMEM] * 2 + [HBM] * 3 + [VMEM if stratum else HBM] * len(state),
-        out_specs=(VMEM,) * len(outs),
+    rows, rank = users.shape
+    first = stratum == 0
+    return pl.pallas_call(
+        functools.partial(tile_kernel, stratum, math.sqrt(2.0 * step_size)),
+        out_shape=(shape(rows, rank),) * 4 + (shape(RIDERS, rank // CORES),),
+        in_specs=[SMEM] * 2 + [HBM] * 3 + [HBM if first else VMEM] * 2,
+        out_specs=(VMEM,) * 5,
         scratch_shapes=[
             pltpu.VMEM((slots, tile, tile), bf16),
             pltpu.VMEM((rows, rank), bf16),
             pltpu.VMEM((rows, rank), bf16),
-            pltpu.VMEM((rows, rank), f32),
-            pltpu.VMEM((rows, rank), f32),
             pltpu.VMEM((rows, rows), f32),
             pltpu.VMEM((rows, rows), bf16),
             pltpu.SemaphoreType.DMA((5,)),
-        ],
+        ]
+        + [pltpu.VMEM((rows, rank), f32)] * (2 if first else 0),
         compiler_params=PARAMS,
         cost_estimate=cost(6 * rows * rows * rank, 16 * rows * rank),
         name="tile_pass",
-    )(codes, count, ratings, user_noise, item_noise, *state)
+    )(codes, count, ratings, user_noise, item_noise, users, items)
 
 
 def first_kernel(devices, feats_in, weights_in, users_in, own_mean, other_mean, *refs):
@@ -344,38 +315,47 @@
     )(turned, offset, stats, more_stats)
 
 
-def final_kernel(places, devices, feats, turned, begun, part, got, first_part, first_got, own_cols, other_cols, stats, more_stats, own_mean, other_mean, send, keep, old, full, offset):
+def final_kernel(places, devices, feats, turned, begun, part, got, first_part, first_got, own_cols, other_cols, stats, more_stats, own_mean, other_mean, *refs):
+    sends, keeps, olds = refs[:CHUNKS], refs[CHUNKS : 2 * CHUNKS], refs[2 * CHUNKS : 3 * CHUNKS]
+    full, offset = refs[3 * CHUNKS :]
     find_offset(devices, feats, begun, part, got, own_cols, other_cols, own_mean, other_mean, offset)
-    send[keep.shape[0] :, :] = stats[...] + more_stats[...]
+    sends[-1][keeps[-1].shape[0] :, :] = stats[...] + more_stats[...]
     rows = part.shape[0]
-    place = where_am_i(devices)
     for chunk, mine, theirs in ((0, first_part, first_got), (1, part, got)):
         bit = where_am_i(devices, chunk)[1]
         full[rows_at(2 * chunk + bit, rows), :] = mine[...]
         full[rows_at(2 * chunk + 1 - bit, rows), :] = theirs[...]
-    old[...] = full[rows_at(place[-1], old.shape[0]), :]
+    core, *_, chip = where_am_i(devices)
+    for chunk, old in enumerate(olds):
+        old[...] = full[rows_at(CHUNKS * chip + chunk, old.shape[0]), :]
     full[...] = dot(turned[...], offset[...])
-    core, bit = place[0], place[1]
-    blocks = len(places[0])
-    block = full.shape[0] // blocks
-    for ref, which in ((send, 1 - bit), (keep, bit)):
-        for n in range(blocks // 2):
-            source = jnp.int32(0)
-            for c, order in enumerate(places):
-                for b in range(2):
-                    source = jnp.where((core == c) & (which == b), order[b * blocks // 2 + n], source)
-            ref[n * block : (n + 1) * block, :] = full[rows_at(source, block), :]
+    for chunk, (send, keep) in enumerate(zip(sends, keeps, strict=True)):
+        bit = where_am_i(devices, chunk)[1]
+        zero, one = places[chunk]
+        blocks = len(zero) // 2
+        block = keep.shape[0] // blocks
+        for ref, which in ((send, 1 - bit), (keep, bit)):
+            for n in range(blocks):
+                source = jnp.where(
+                    core == 0,
+                    jnp.where(which == 0, zero[n], zero[blocks + n]),
+                    jnp.where(which == 0, one[n], one[blocks + n]),
+                )
+                ref[n * block : (n + 1) * block, :] = full[rows_at(source, block), :]
 
 
 def final_pass(places, devices, feats, turned, begun, part, got, first_part, first_got, own_cols, other_cols, stats, more_stats):
     rows, width = own_cols.shape
     feat = feats.shape[1]
+    quarter = feat // (2 * CHUNKS)
     return pl.pallas_call(
         functools.partial(final_kernel, places, devices),
         out_shape=(shape(rows, width),) * 2
-        + (shape(feat // 2 + RIDERS, width), shape(feat // 2, width), shape(feat // len(places[0]), width)),
+        + (shape(quarter, width), shape(quarter + RIDERS, width))
+        + (shape(quarter, width),) * CHUNKS
+        + (shape(feat // devices, width),) * CHUNKS,
         in_specs=[VMEM] * 11,
-        out_specs=(VMEM,) * 5,
+        out_specs=(VMEM,) * (2 + 3 * CHUNKS),
         scratch_shapes=[pltpu.VMEM((feat, width), f32), pltpu.VMEM((CORES * rows, width), bf16)],
         compiler_params=PARAMS,
         cost_estimate=cost(8 * rows * feat * width, 8 * rows * feat),
@@ -441,51 +421,49 @@
     )(held, got, old, *([sent] if riding else []), *later)
 
 
-def gather_kernel(stage, chunk, devices, part, got, both):
+def gather_kernel(stage, chunk, devices, part, got, *refs):
+    both = refs[-1]
     rows = part.shape[0]
     bit = where_am_i(devices, chunk)[1 + stage]
     both[rows_at(bit, rows), :] = part[...]
     both[rows_at(1 - bit, rows), :] = got[...]
 
 
-def gather_pass(stage, chunk, devices, part, got):
+def gather_pass(stage, chunk, devices, part, got, later=()):
     rows, width = part.shape
     return pl.pallas_call(
         functools.partial(gather_kernel, stage, chunk, devices),
         out_shape=shape(2 * rows, width),
-        in_specs=[VMEM, VMEM],
+        in_specs=[VMEM, VMEM] + [ANY] * len(later),
         out_specs=VMEM,
         compiler_params=PARAMS,
         cost_estimate=cost(rows * width, 16 * rows * width),
         name="gather_pass",
-    )(part, got)
-
-
-def split_kernel(devices, both, mine, other):
-    place = where_am_i(devices)
-    rows = mine.shape[0]
-    for ref, which in ((mine, place[0]), (other, 1 - place[0])):
-        at = pl.ds(pl.multiple_of(which * rows, 8), rows) if rows % 8 == 0 else pl.ds(which * rows, rows)
-        ref[...] = both[at, :]
-
-
-def split_pass(devices, both):
-    rows, width = both.shape
+    )(part, got, *later)
+
+
+def split_kernel(devices, first, second, mine, other):
+    core = where_am_i(devices)[0]
+    mine[...] = jnp.where(core == 0, first[...], second[...])
+    other[...] = jnp.where(core == 0, second[...], first[...])
+
+
+def split_pass(devices, first, second):
     return pl.pallas_call(
         functools.partial(split_kernel, devices),
-        out_shape=(shape(rows // CORES, width),) * 2,
-        in_specs=[VMEM],
+        out_shape=(shape(*first.shape),) * 2,
+        in_specs=[VMEM, VMEM],
         out_specs=(VMEM,) * 2,
         compiler_params=PARAMS,
         name="split_pass",
-    )(both)
+    )(first, second)
 
 
 def across_kernel(devices, mine, other, both):
-    place = where_am_i(devices)
+    core = where_am_i(devices)[0]
     width = mine.shape[1]
-    both[:, pl.ds(pl.multiple_of(place[0] * width, width), width)] = mine[...]
-    both[:, pl.ds(pl.multiple_of((1 - place[0]) * width, width), width)] = other[...]
+    both[:, rows_at(core, width)] = mine[...]
+    both[:, rows_at(1 - core, width)] = other[...]
 
 
 def across_pass(devices, mine, other):
@@ -500,29 +478,33 @@
     )(mine, other)
 
 
-def last_kernel(devices, stats, base, grad, own_mean, other_mean, base_v, grad_v, users, items):
-    place = where_am_i(devices)
+def renew_kernel(devices, stats, base_u, grad_u, own_mean, other_mean, base_v, grad_v, users, items, *cols):
+    core = where_am_i(devices)[0]
     width = own_mean.shape[1]
     precision = precision_of(stats[...])
     precision = jnp.concatenate([precision] * CORES, 1)
     items[...] = base_v[...] + precision * grad_v[...]
-    users[...] = base[...] + precision * grad[...]
+    new = base_u[...] + precision * grad_u[...]
     pull = step_size * prior_prec
-    for mean, which in ((own_mean, place[0]), (other_mean, 1 - place[0])):
-        at = pl.ds(pl.multiple_of(which * width, width), width)
-        users[:, at] = users[:, at] + pull * mean[...]
-
-
-def last_pass(devices, stats, base, *state):
-    return pl.pallas_call(
-        functools.partial(last_kernel, devices),
-        out_shape=(shape(*base.shape),) * 2,
+    left = jnp.where(core == 0, own_mean[...], other_mean[...])
+    right = jnp.where(core == 0, other_mean[...], own_mean[...])
+    users[:, :width] = new[:, :width] + pull * left
+    users[:, width:] = new[:, width:] + pull * right
+    for ref, which in zip(cols, (core, 1 - core), strict=False):
+        ref[...] = half_of(users, which)
+
+
+def renew_pass(devices, last, stats, base_u, grad_u, own_mean, *state):
+    outs = [shape(*base_u.shape)] * 2 + ([] if last else [shape(*own_mean.shape)] * 2)
+    return pl.pallas_call(
+        functools.partial(renew_kernel, devices),
+        out_shape=tuple(outs),
         in_specs=[VMEM] * 7,
-        out_specs=(VMEM,) * 2,
-        compiler_params=PARAMS,
-        cost_estimate=cost(8 * base.size, 32 * base.size),
-        name="last_pass",
-    )(stats, base, *state)
+        out_specs=(VMEM,) * len(outs),
+        compiler_params=PARAMS,
+        cost_estimate=cost(8 * base_u.size, 32 * base_u.size),
+        name="renew_pass",
+    )(stats, base_u, grad_u, own_mean, *state)
 
 
 def bit_order(devices, core, chunk=0):
@@ -546,13 +528,14 @@
     return lax.ppermute(array, "user", pairs)
 
 
-def final_places(devices):
+def final_places(devices, chunk):
     bits = devices.bit_length() - 1
     return [
         [
-            sum(
-                ((place >> (bits - 2 - n)) & 1) << (bit - 1)
-                for n, bit in enumerate(bit_order(devices, core))
+            chunk
+            | sum(
+                ((place >> (bits - 2 - n)) & 1) << bit
+                for n, bit in enumerate(bit_order(devices, core, chunk))
             )
             for place in range(devices // 2)
         ]
@@ -576,49 +559,58 @@
     strata = ratings.shape[1]
     feat = prior_weights.shape[0]
     rate = rate_scale / (user_factors.shape[0] * devices)
-    tables = (devices, tile_index, tile_count, ratings, user_noise, item_noise)
-
+    tables = (tile_index, tile_count, ratings, user_noise, item_noise)
     both = range(CHUNKS)
     depth = feat // CHUNKS
+
+    def stage_of(stage, sends, helds, halving):
+        for c in (1, 0):
+            got = exchange(sends[c], devices, stage, c)
+            riders = (sends[c], got) if c else ()
+            rows = got.shape[0] - RIDERS * c
+            later = [sends[1 - c]]
+            outs = step_pass(halving, stage + 1, c, devices, helds[c], got, rows, riders, later)
+            sends[c], helds[c] = outs if halving else outs * 2
+
+    def update_of(sends, helds, olds):
+        news = list(olds)
+        for c in (1, 0):
+            got = exchange(sends[c], devices, stages - 1, c)
+            if c:
+                news[c], stats = update_pass(rate, helds[c], got, olds[c], sends[c], sends[:1])
+            else:
+                news[c] = update_pass(rate, helds[c], got, olds[c], None, news[1:])
+        return news, stats
+
     own_mean, other_mean, *outs = first_pass(
         devices, side_features, prior_weights, user_factors
     )
-    helds, olds = outs[CHUNKS : 2 * CHUNKS], outs[2 * CHUNKS :]
+    keeps, olds = outs[CHUNKS : 2 * CHUNKS], outs[2 * CHUNKS :]
     gots = [swap(send, devices) for send in outs[:CHUNKS]]
-    base, grad, base_v, grad_v, stats = tile_pass(0, *tables, user_factors, item_factors)
+    *state, stats = tile_pass(0, *tables, user_factors, item_factors)
     more = swap(stats, devices)
-    sends = [None] * CHUNKS
-    for c in both:
+    sends, helds = [None] * CHUNKS, [None] * CHUNKS
+    for c in (1, 0):
         riders = (stats, more) if c else ()
-        sends[c], helds[c] = step_pass(True, 0, c, devices, helds[c], gots[c], depth, riders)
+        later = [] if c else [sends[1]]
+        sends[c], helds[c] = step_pass(True, 0, c, devices, keeps[c], gots[c], depth, riders, later)
     feats, turned = join_pass(side_features, swap(widen_pass(side_features), devices))
     for stratum in range(strata - 1):
-        base_v, grad_v = roll(base_v, devices), roll(grad_v, devices)
         for stage in range(stages - 1):
-            for c in both:
-                gots[c] = exchange(sends[c], devices, stage, c)
-                riders = (sends[c], gots[c]) if c else ()
-                rows = gots[c].shape[0] - RIDERS * c
-                if stage < 1:
-                    sends[c], helds[c] = step_pass(True, stage + 1, c, devices, helds[c], gots[c], rows, riders)
-                else:
-                    (sends[c],) = step_pass(False, 0, c, devices, helds[c], gots[c], rows, riders)
-                    helds[c] = sends[c]
-        for c in both:
-            gots[c] = exchange(sends[c], devices, stages - 1, c)
-            if c:
-                olds[c], stats = update_pass(rate, helds[c], gots[c], olds[c], sends[c])
-            else:
-                olds[c] = update_pass(rate, helds[c], gots[c], olds[c])
+            stage_of(stage, sends, helds, stage < 1)
+        olds, stats = update_of(sends, helds, olds)
+        users, items, own_cols, other_cols = renew_pass(
+            devices, False, stats, *state[:2], own_mean, other_mean, *state[2:]
+        )
+        items = roll(items, devices)
+        other_cols = swap(other_cols, devices)
         parts = list(olds)
-        for c in both:
-            parts[c] = gather_pass(1, c, devices, parts[c], exchange(parts[c], devices, 1, c))
+        for c in (1, 0):
+            got = exchange(parts[c], devices, 1, c)
+            parts[c] = gather_pass(1, c, devices, parts[c], got, [parts[1 - c]])
         gots = [exchange(parts[c], devices, 0, c) for c in both]
-        base, grad, base_v, grad_v, stats, own_cols, other_cols = tile_pass(
-            stratum + 1, *tables, base, grad, own_mean, other_mean, stats, base_v, grad_v
-        )
+        *state, stats = tile_pass(stratum + 1, *tables, users, items)
         more = swap(stats, devices)
-        other_cols = swap(other_cols, devices)
         begun = part_pass(devices, feats, parts[0], gots[0])
         if stratum + 2 < strata:
             own_mean, other_mean, offset, sends[0], helds[0] = prior_pass(
@@ -626,8 +618,8 @@
             )
             sends[1], helds[1] = rest_pass(devices, turned, offset, stats, more)
         else:
-            own_mean, other_mean, send, held, old = final_pass(
-                final_places(devices),
+            own_mean, other_mean, *outs = final_pass(
+                [final_places(devices, c) for c in both],
                 devices,
                 feats,
                 turned,
@@ -641,15 +633,14 @@
                 stats,
                 more,
             )
+            sends, helds, olds = outs[:CHUNKS], outs[CHUNKS : 2 * CHUNKS], outs[2 * CHUNKS :]
         other_mean = swap(other_mean, devices)
     for stage in range(stages - 1):
-        got = exchange(send, devices, stage)
-        send, held = step_pass(True, stage + 1, 0, devices, held, got, got.shape[0] - RIDERS, (send, got))
-    got = exchange(send, devices, stages - 1)
-    part, stats = update_pass(rate, held, got, old, send)
-    mine, other = split_pass(devices, part)
+        stage_of(stage, sends, helds, True)
+    news, stats = update_of(sends, helds, olds)
+    mine, other = split_pass(devices, *news)
     got = swap(other, devices)
-    users, items = last_pass(devices, stats, base, grad, own_mean, other_mean, base_v, grad_v)
+    users, items = renew_pass(devices, True, stats, *state[:2], own_mean, other_mean, *state[2:])
     return (users, items, across_pass(devices, mine, got))
 
 

time: 122 us -> 123 us (level)
  waiting for transfers between devices: 51.8 us -> 54.5 us
  starting transfers between devices: 52.2 us -> 49.9 us
    ppermute x11, starting transfers between devices: 1.83 us -> 5.38 us  [swap(): return lax.ppermute(array, 'user', [(i, i ^ 1) for i in range(devices)])]
    ppermute x4 -> x2, starting transfers between devices: 3.13 us -> 0.12 us  [roll(): lax.ppermute(array, 'user', [(i, (i + 1) % devices) for i in range(device...]
    ppermute x28 -> x32, starting transfers between devices: 47.2 us -> 44.4 us  [exchange(): return lax.ppermute(array, 'user', pairs)]
    ppermute x28 -> x32, waiting for transfers between devices: 50.9 us -> 53.1 us  [exchange(): return lax.ppermute(array, 'user', pairs)]
    pallas_call x4 -> x6, Pallas kernels: 8.43 us -> 8.62 us  [the longest x3 7.14 us: tile_pass(): pl.pallas_call(functools.partial(tile_kernel, stratum, math.sqrt(2.0 * st...]
  transfers between devices with their start and end apart: 43 -> 45, of which waited for: 19 -> 23; matrix products, arithmetic and copies ran while one was open for 0% -> 0% of each run, Pallas kernels for 11% -> 10%
where the time goes in v9:
time: 123 us; the launch traced here: 122 us
  waiting for transfers between devices  54.5 us (44%)
  starting transfers between devices  49.9 us (41%)
  Pallas kernels  15.2 us (12%)
  local copies, waits for them, and re-layouts  1.76 us (1%)
    ppermute x32, waiting for transfers between devices, exchange(): return lax.ppermute(array, 'user', pairs)  53.1 us
    ppermute x32, starting transfers between devices, exchange(): return lax.ppermute(array, 'user', pairs)  44.4 us
    pallas_call x3, Pallas kernels, tile_pass(): pl.pallas_call(functools.partial(tile_kernel, stratum, math.sqrt(2.0 * st...  7.14 us
    ppermute x11, starting transfers between devices, swap(): return lax.ppermute(array, 'user', [(i, i ^ 1) for i in range(devices)])  5.38 us
  transfers between devices with their start and end apart: 45, of which 23 were waited for; matrix products, arithmetic and copies ran while one was open for 0% of the time, Pallas kernels for 10%

profile of v9, /device:TPU:0, one launch (start us, length us, event | category | flops | bytes accessed | tf_op | source)
XLA Modules:
  0.0 122.4 jit_solution(12882612250085860501)
XLA Ops:
  3.1 1.8 %first_pass.1 = (f32[384,128]{1,0:T(8,128)S(1)}, f32[384,128]{1,0:T(8,128)S(1)}, f32[512,128]{1,0:T(8,128)S(1)}, f32[512,128]{1,0:T(8,128)S(1)}, f32[512,128]{1,...) custom-call(bf16[384,1024]{1,0:T(8,128)(2,1)S(1)} %copy-done, ...), custom_call_target="tpu_custom_call" | custom-call | flops 402653184 | bytes 2097152 | tf_op jit(solution)/shard_map/first_pass/pallas_call | solution.py:178
  5.5 2.6 %tile_pass.3 = (f32[384,256]{1,0:T(8,128)S(1)}, f32[384,256]{1,0:T(8,128)S(1)}, f32[384,256]{1,0:T(8,128)S(1)}, f32[384,256]{1,0:T(8,128)S(1)}, f32[8,128]{1,0:T(8,128)S(1)}) custom-call(s32[1,3,6]{2,1,0:T(4,128)S(1)} %copy.12.codes, s32[1,3]{1,0:T(1,128)S(1)} %copy-done.8, bf16[1,3,6,128,128]{4,3,2,1,0:T(8,128)(2,1)S(1)} %copy-done.2, ...), custom_call_target="tpu_custom_call" | custom-call | flops 226492416 | bytes 1572864 | tf_op jit(solution)/shard_map/tile_pass/pallas_call | solution.py:122
  9.5 2.9 %collective-permute-start.5 = (f32[264,128]{1,0:T(8,128)S(1)}, f32[264,128]{1,0:T(8,128)S(1)}, u32[]{:S(2)}, u32[]{:S(2)}) collective-permute-start(f32[264,128]{1,0:T(8,128)S(1)} %get-tuple-element.92.refs_0_), channel_id=1, source_target_pairs={{0,4},{1,3},{2,6},{3,1},{4,0},{5,7},{6,2},{7,5},{8,12},{9,11},{10,... | collective-permute-start | bytes 405512 | tf_op jit(solution)/shard_map/ppermute | solution.py:528
  14.0 2.0 %collective-permute-done.5.got.refs_1_ = f32[264,128]{1,0:T(8,128)S(1)} collective-permute-done((f32[264,128]{1,0:T(8,128)S(1)}, f32[264,128]{1,0:T(8,128)S(1)}, u32[]{:S(2)}, u32[]{:S(2)}) %collective-permute-start.5) | collective-permute-done | bytes 135200 | tf_op jit(solution)/shard_map/ppermute | solution.py:528
  16.0 2.3 %collective-permute-start.7 = (f32[136,128]{1,0:T(8,128)S(1)}, f32[136,128]{1,0:T(8,128)S(1)}, u32[]{:S(2)}, u32[]{:S(2)}) collective-permute-start(f32[136,128]{1,0:T(8,128)S(1)} %get-tuple-element.96.refs_0_), channel_id=1, source_target_pairs={{0,2},{1,5},{2,0},{3,7},{4,6},{5,1},{6,4},{7,3},{8,10},{9,13},{10,... | collective-permute-start | bytes 208904 | tf_op jit(solution)/shard_map/ppermute | solution.py:528
  18.3 2.3 %collective-permute-done.7.got.refs_1_ = f32[136,128]{1,0:T(8,128)S(1)} collective-permute-done((f32[136,128]{1,0:T(8,128)S(1)}, f32[136,128]{1,0:T(8,128)S(1)}, u32[]{:S(2)}, u32[]{:S(2)}) %collective-permute-start.7) | collective-permute-done | bytes 69664 | tf_op jit(solution)/shard_map/ppermute | solution.py:528
  20.6 3.4 %collective-permute-start.9 = (f32[136,128]{1,0:T(8,128)S(1)}, f32[136,128]{1,0:T(8,128)S(1)}, u32[]{:S(2)}, u32[]{:S(2)}) collective-permute-start(f32[136,128]{1,0:T(8,128)S(1)} %step_pass.24.refs_0_.held), channel_id=1, source_target_pairs={{0,16},{1,17},{2,18},{3,19},{4,20},{5,21},{6,22},{7,23},{8,24},{9,... | collective-permute-start | bytes 208904 | tf_op jit(solution)/shard_map/ppermute | solution.py:528
  25.5 2.8 %collective-permute-done.6.got = f32[128,128]{1,0:T(8,128)S(1)} collective-permute-done((f32[128,128]{1,0:T(8,128)S(1)}, f32[128,128]{1,0:T(8,128)S(1)}, u32[]{:S(2)}, u32[]{:S(2)}) %collective-permute-start.6) | collective-permute-done | bytes 65568 | tf_op jit(solution)/shard_map/ppermute | solution.py:528
  28.3 1.8 %collective-permute-start.11 = (f32[136,128]{1,0:T(8,128)S(1)}, f32[136,128]{1,0:T(8,128)S(1)}, u32[]{:S(2)}, u32[]{:S(2)}) collective-permute-start(f32[136,128]{1,0:T(8,128)S(1)} %step_pass.26.refs_0_.held), channel_id=1, source_target_pairs={{0,8},{1,9},{2,10},{3,11},{4,12},{5,13},{6,14},{7,15},{8,0},{9,1},... | collective-permute-start | bytes 208904 | tf_op jit(solution)/shard_map/ppermute | solution.py:528
  30.4 4.0 %collective-permute-done.8.got = f32[128,128]{1,0:T(8,128)S(1)} collective-permute-done((f32[128,128]{1,0:T(8,128)S(1)}, f32[128,128]{1,0:T(8,128)S(1)}, u32[]{:S(2)}, u32[]{:S(2)}) %collective-permute-start.8) | collective-permute-done | bytes 65568 | tf_op jit(solution)/shard_map/ppermute | solution.py:528
  37.8 3.9 %collective-permute-done.10.got = f32[128,128]{1,0:T(8,128)S(1)} collective-permute-done((f32[128,128]{1,0:T(8,128)S(1)}, f32[128,128]{1,0:T(8,128)S(1)}, u32[]{:S(2)}, u32[]{:S(2)}) %collective-permute-start.10) | collective-permute-done | bytes 65568 | tf_op jit(solution)/shard_map/ppermute | solution.py:528
  41.8 1.6 %collective-permute-start.12 = (f32[128,128]{1,0:T(8,128)S(1)}, f32[128,128]{1,0:T(8,128)S(1)}, u32[]{:S(2)}, u32[]{:S(2)}) collective-permute-start(f32[128,128]{1,0:T(8,128)S(1)} %update_pass.7.refs_0_.part.old), channel_id=1, source_target_pairs={{0,4},{1,3},{2,6},{3,1},{4,0},{5,7},{6,2},{7,5},{8,12},{9,11},{10,... | collective-permute-start | bytes 196616 | tf_op jit(solution)/shard_map/ppermute | solution.py:528
  43.4 3.5 %collective-permute-done.12.got = f32[128,128]{1,0:T(8,128)S(1)} collective-permute-done((f32[128,128]{1,0:T(8,128)S(1)}, f32[128,128]{1,0:T(8,128)S(1)}, u32[]{:S(2)}, u32[]{:S(2)}) %collective-permute-start.12) | collective-permute-done | bytes 65568 | tf_op jit(solution)/shard_map/ppermute | solution.py:528
  47.0 4.5 %collective-permute-start.14 = (f32[256,128]{1,0:T(8,128)S(1)}, f32[256,128]{1,0:T(8,128)S(1)}, u32[]{:S(2)}, u32[]{:S(2)}) collective-permute-start(f32[256,128]{1,0:T(8,128)S(1)} %gather_pass.5.part), channel_id=1, source_target_pairs={{0,2},{1,5},{2,0},{3,7},{4,6},{5,1},{6,4},{7,3},{8,10},{9,13},{10,... | collective-permute-start | bytes 393224 | tf_op jit(solution)/shard_map/ppermute | solution.py:528
  51.4 2.0 %collective-permute-start.15 = (f32[256,128]{1,0:T(8,128)S(1)}, f32[256,128]{1,0:T(8,128)S(1)}, u32[]{:S(2)}, u32[]{:S(2)}) collective-permute-start(f32[256,128]{1,0:T(8,128)S(1)} %gather_pass.4.refs_0_.part), channel_id=1, source_target_pairs={{0,4},{1,3},{2,6},{3,1},{4,0},{5,7},{6,2},{7,5},{8,12},{9,11},{10,... | collective-permute-start | bytes 393224 | tf_op jit(solution)/shard_map/ppermute | solution.py:528
  53.5 2.3 %tile_pass.4 = (f32[384,256]{1,0:T(8,128)S(1)}, f32[384,256]{1,0:T(8,128)S(1)}, f32[384,256]{1,0:T(8,128)S(1)}, f32[384,256]{1,0:T(8,128)S(1)}, f32[8,128]{1,0:T(8,128)S(1)}) custom-call(s32[1,3,6]{2,1,0:T(4,128)S(1)} %copy.12.codes, s32[1,3]{1,0:T(1,128)S(1)} %copy-done.8, bf16[1,3,6,128,128]{4,3,2,1,0:T(8,128)(2,1)S(1)} %copy-done.2, ...), custom_call_target="tpu_custom_call" | custom-call | flops 226492416 | bytes 1572864 | tf_op jit(solution)/shard_map/tile_pass/pallas_call | solution.py:122
  57.9 1.7 %collective-permute-start.20 = (f32[264,128]{1,0:T(8,128)S(1)}, f32[264,128]{1,0:T(8,128)S(1)}, u32[]{:S(2)}, u32[]{:S(2)}) collective-permute-start(f32[264,128]{1,0:T(8,128)S(1)} %get-tuple-element.119.refs_0_), channel_id=1, source_target_pairs={{0,4},{1,3},{2,6},{3,1},{4,0},{5,7},{6,2},{7,5},{8,12},{9,11},{10,... | collective-permute-start | bytes 405512 | tf_op jit(solution)/shard_map/ppermute | solution.py:528
  60.0 4.0 %collective-permute-done.20.got.refs_1_ = f32[264,128]{1,0:T(8,128)S(1)} collective-permute-done((f32[264,128]{1,0:T(8,128)S(1)}, f32[264,128]{1,0:T(8,128)S(1)}, u32[]{:S(2)}, u32[]{:S(2)}) %collective-permute-start.20) | collective-permute-done | bytes 135200 | tf_op jit(solution)/shard_map/ppermute | solution.py:528
  65.2 3.2 %collective-permute-done.22.got.refs_1_ = f32[136,128]{1,0:T(8,128)S(1)} collective-permute-done((f32[136,128]{1,0:T(8,128)S(1)}, f32[136,128]{1,0:T(8,128)S(1)}, u32[]{:S(2)}, u32[]{:S(2)}) %collective-permute-start.22) | collective-permute-done | bytes 69664 | tf_op jit(solution)/shard_map/ppermute | solution.py:528
  69.1 3.6 %collective-permute-done.21.got = f32[128,128]{1,0:T(8,128)S(1)} collective-permute-done((f32[128,128]{1,0:T(8,128)S(1)}, f32[128,128]{1,0:T(8,128)S(1)}, u32[]{:S(2)}, u32[]{:S(2)}) %collective-permute-start.21) | collective-permute-done | bytes 65568 | tf_op jit(solution)/shard_map/ppermute | solution.py:528
  73.7 2.0 %collective-permute-start.23 = (f32[128,128]{1,0:T(8,128)S(1)}, f32[128,128]{1,0:T(8,128)S(1)}, u32[]{:S(2)}, u32[]{:S(2)}) collective-permute-start(f32[128,128]{1,0:T(8,128)S(1)} %step_pass.31.refs_2_.held), channel_id=1, source_target_pairs={{0,8},{1,9},{2,10},{3,11},{4,12},{5,13},{6,14},{7,15},{8,0},{9,1},... | collective-permute-start | bytes 196616 | tf_op jit(solution)/shard_map/ppermute | solution.py:528
  75.7 3.0 %collective-permute-done.23.got = f32[128,128]{1,0:T(8,128)S(1)} collective-permute-done((f32[128,128]{1,0:T(8,128)S(1)}, f32[128,128]{1,0:T(8,128)S(1)}, u32[]{:S(2)}, u32[]{:S(2)}) %collective-permute-start.23) | collective-permute-done | bytes 65568 | tf_op jit(solution)/shard_map/ppermute | solution.py:528
  79.1 2.1 %collective-permute-start.25 = (f32[128,128]{1,0:T(8,128)S(1)}, f32[128,128]{1,0:T(8,128)S(1)}, u32[]{:S(2)}, u32[]{:S(2)}) collective-permute-start(f32[128,128]{1,0:T(8,128)S(1)} %step_pass.33.refs_1_.held), channel_id=1, source_target_pairs={{0,16},{1,17},{2,18},{3,19},{4,20},{5,21},{6,22},{7,23},{8,24},{9,... | collective-permute-start | bytes 196616 | tf_op jit(solution)/shard_map/ppermute | solution.py:528
  82.4 3.7 %collective-permute-done.25.got = f32[128,128]{1,0:T(8,128)S(1)} collective-permute-done((f32[128,128]{1,0:T(8,128)S(1)}, f32[128,128]{1,0:T(8,128)S(1)}, u32[]{:S(2)}, u32[]{:S(2)}) %collective-permute-start.25) | collective-permute-done | bytes 65568 | tf_op jit(solution)/shard_map/ppermute | solution.py:528
  87.4 4.0 %collective-permute-done.27.got = f32[128,128]{1,0:T(8,128)S(1)} collective-permute-done((f32[128,128]{1,0:T(8,128)S(1)}, f32[128,128]{1,0:T(8,128)S(1)}, u32[]{:S(2)}, u32[]{:S(2)}) %collective-permute-start.27) | collective-permute-done | bytes 65568 | tf_op jit(solution)/shard_map/ppermute | solution.py:528
  93.2 2.3 %tile_pass.5 = (f32[384,256]{1,0:T(8,128)S(1)}, f32[384,256]{1,0:T(8,128)S(1)}, f32[384,256]{1,0:T(8,128)S(1)}, f32[384,256]{1,0:T(8,128)S(1)}, f32[8,128]{1,0:T(8,128)S(1)}) custom-call(s32[1,3,6]{2,1,0:T(4,128)S(1)} %copy.12.codes, s32[1,3]{1,0:T(1,128)S(1)} %copy-done.8, bf16[1,3,6,128,128]{4,3,2,1,0:T(8,128)(2,1)S(1)} %copy-done.2, ...), custom_call_target="tpu_custom_call" | custom-call | flops 226492416 | bytes 1572864 | tf_op jit(solution)/shard_map/tile_pass/pallas_call | solution.py:122
  95.4 2.5 %collective-permute-start.34 = (f32[8,128]{1,0:T(8,128)S(1)}, f32[8,128]{1,0:T(8,128)S(1)}, u32[]{:S(2)}, u32[]{:S(2)}) collective-permute-start(f32[8,128]{1,0:T(8,128)S(1)} %get-tuple-element.136.stats), channel_id=1, source_target_pairs={{0,1},{1,0},{2,3},{3,2},{4,5},{5,4},{6,7},{7,6},{8,9},{9,8},{10,11... | collective-permute-start | bytes 12296 | tf_op jit(solution)/shard_map/ppermute | solution.py:518
  100.6 1.7 %collective-permute-start.37 = (f32[256,128]{1,0:T(8,128)S(1)}, f32[256,128]{1,0:T(8,128)S(1)}, u32[]{:S(2)}, u32[]{:S(2)}) collective-permute-start(f32[256,128]{1,0:T(8,128)S(1)} %get-tuple-element.139.refs_2_), channel_id=1, source_target_pairs={{0,2},{1,5},{2,0},{3,7},{4,6},{5,1},{6,4},{7,3},{8,10},{9,13},{10,... | collective-permute-start | bytes 393224 | tf_op jit(solution)/shard_map/ppermute | solution.py:528
  102.2 4.0 %collective-permute-done.35.got.refs_1_ = f32[264,128]{1,0:T(8,128)S(1)} collective-permute-done((f32[264,128]{1,0:T(8,128)S(1)}, f32[264,128]{1,0:T(8,128)S(1)}, u32[]{:S(2)}, u32[]{:S(2)}) %collective-permute-start.35) | collective-permute-done | bytes 135200 | tf_op jit(solution)/shard_map/ppermute | solution.py:528
  108.5 2.1 %collective-permute-done.36.got.refs_1_ = f32[136,128]{1,0:T(8,128)S(1)} collective-permute-done((f32[136,128]{1,0:T(8,128)S(1)}, f32[136,128]{1,0:T(8,128)S(1)}, u32[]{:S(2)}, u32[]{:S(2)}) %collective-permute-start.36) | collective-permute-done | bytes 69664 | tf_op jit(solution)/shard_map/ppermute | solution.py:528
  113.1 2.4 %collective-permute-done.38.got.refs_1_ = f32[72,128]{1,0:T(8,128)S(1)} collective-permute-done((f32[72,128]{1,0:T(8,128)S(1)}, f32[72,128]{1,0:T(8,128)S(1)}, u32[]{:S(2)}, u32[]{:S(2)}) %collective-permute-start.38) | collective-permute-done | bytes 36896 | tf_op jit(solution)/shard_map/ppermute | solution.py:528
  115.9 2.2 %collective-permute-start.43 = (f32[32,128]{1,0:T(8,128)S(1)}, f32[32,128]{1,0:T(8,128)S(1)}, u32[]{:S(2)}, u32[]{:S(2)}) collective-permute-start(f32[32,128]{1,0:T(8,128)S(1)} %get-tuple-element.152.refs_1_), channel_id=1, source_target_pairs={{0,16},{1,17},{2,18},{3,19},{4,20},{5,21},{6,22},{7,23},{8,24},{9,... | collective-permute-start | bytes 49160 | tf_op jit(solution)/shard_map/ppermute | solution.py:528
  (125 shorter events, 33.6 us)
Async XLA Ops:
  2.0 53.8 %collective-permute-start = (f32[384,1024]{1,0:T(8,128)S(1)}, f32[384,1024]{1,0:T(8,128)S(1)}, u32[]{:S(2)}, u32[]{:S(2)}) collective-permute-start(f32[384,1024]{1,0:T(8,128)S(1)} %widen_pass.1), channel_id=1, source_target_pairs={{0,1},{1,0},{2,3},{3,2},{4,5},{5,4},{6,7},{7,6},{8,9},{9,8},{10,11... | collective-permute-start | bytes 4718600 | tf_op jit(solution)/shard_map/ppermute | solution.py:518
  4.9 4.6 %collective-permute-start.2 = (f32[512,128]{1,0:T(8,128)S(1)}, f32[512,128]{1,0:T(8,128)S(1)}, u32[]{:S(2)}, u32[]{:S(2)}) collective-permute-start(f32[512,128]{1,0:T(8,128)S(1)} %get-tuple-element.90), channel_id=1, source_target_pairs={{0,1},{1,0},{2,3},{3,2},{4,5},{5,4},{6,7},{7,6},{8,9},{9,8},{10,11... | collective-permute-start | bytes 786440 | tf_op jit(solution)/shard_map/ppermute | solution.py:518
  5.4 7.0 %collective-permute-start.1 = (f32[512,128]{1,0:T(8,128)S(1)}, f32[512,128]{1,0:T(8,128)S(1)}, u32[]{:S(2)}, u32[]{:S(2)}) collective-permute-start(f32[512,128]{1,0:T(8,128)S(1)} %get-tuple-element.88), channel_id=1, source_target_pairs={{0,1},{1,0},{2,3},{3,2},{4,5},{5,4},{6,7},{7,6},{8,9},{9,8},{10,11... | collective-permute-start | bytes 786440 | tf_op jit(solution)/shard_map/ppermute | solution.py:518
  9.5 6.5 %collective-permute-start.5 = (f32[264,128]{1,0:T(8,128)S(1)}, f32[264,128]{1,0:T(8,128)S(1)}, u32[]{:S(2)}, u32[]{:S(2)}) collective-permute-start(f32[264,128]{1,0:T(8,128)S(1)} %get-tuple-element.92.refs_0_), channel_id=1, source_target_pairs={{0,4},{1,3},{2,6},{3,1},{4,0},{5,7},{6,2},{7,5},{8,12},{9,11},{10,... | collective-permute-start | bytes 405512 | tf_op jit(solution)/shard_map/ppermute | solution.py:528
  12.5 5.8 %collective-permute-start.4 = (f32[256,128]{1,0:T(8,128)S(1)}, f32[256,128]{1,0:T(8,128)S(1)}, u32[]{:S(2)}, u32[]{:S(2)}) collective-permute-start(f32[256,128]{1,0:T(8,128)S(1)} %get-tuple-element.94.refs_2_), channel_id=1, source_target_pairs={{0,2},{1,5},{2,0},{3,7},{4,6},{5,1},{6,4},{7,3},{8,10},{9,13},{10,... | collective-permute-start | bytes 393224 | tf_op jit(solution)/shard_map/ppermute | solution.py:528
  20.6 7.7 %collective-permute-start.9 = (f32[136,128]{1,0:T(8,128)S(1)}, f32[136,128]{1,0:T(8,128)S(1)}, u32[]{:S(2)}, u32[]{:S(2)}) collective-permute-start(f32[136,128]{1,0:T(8,128)S(1)} %step_pass.24.refs_0_.held), channel_id=1, source_target_pairs={{0,16},{1,17},{2,18},{3,19},{4,20},{5,21},{6,22},{7,23},{8,24},{9,... | collective-permute-start | bytes 208904 | tf_op jit(solution)/shard_map/ppermute | solution.py:528
  28.3 6.1 %collective-permute-start.11 = (f32[136,128]{1,0:T(8,128)S(1)}, f32[136,128]{1,0:T(8,128)S(1)}, u32[]{:S(2)}, u32[]{:S(2)}) collective-permute-start(f32[136,128]{1,0:T(8,128)S(1)} %step_pass.26.refs_0_.held), channel_id=1, source_target_pairs={{0,8},{1,9},{2,10},{3,11},{4,12},{5,13},{6,14},{7,15},{8,0},{9,1},... | collective-permute-start | bytes 208904 | tf_op jit(solution)/shard_map/ppermute | solution.py:528
  34.7 18.8 %collective-permute-start.18 = (f32[384,256]{1,0:T(8,128)S(1)}, f32[384,256]{1,0:T(8,128)S(1)}, u32[]{:S(2)}, u32[]{:S(2)}) collective-permute-start(f32[384,256]{1,0:T(8,128)S(1)} %get-tuple-element.116), channel_id=1, source_target_pairs={{0,1},{1,2},{2,3},{3,4},{4,5},{5,6},{6,7},{7,8},{8,9},{9,10},{10,1... | collective-permute-start | bytes 1179656 | tf_op jit(solution)/shard_map/ppermute | solution.py:522
  34.7 7.1 %collective-permute-start.10 = (f32[128,128]{1,0:T(8,128)S(1)}, f32[128,128]{1,0:T(8,128)S(1)}, u32[]{:S(2)}, u32[]{:S(2)}) collective-permute-start(f32[128,128]{1,0:T(8,128)S(1)} %step_pass.27.refs_1_.held), channel_id=1, source_target_pairs={{0,16},{1,17},{2,18},{3,19},{4,20},{5,21},{6,22},{7,23},{8,24},{9,... | collective-permute-start | bytes 196616 | tf_op jit(solution)/shard_map/ppermute | solution.py:528
  36.3 7.1 %collective-permute-start.13 = (f32[128,128]{1,0:T(8,128)S(1)}, f32[128,128]{1,0:T(8,128)S(1)}, u32[]{:S(2)}, u32[]{:S(2)}) collective-permute-start(f32[128,128]{1,0:T(8,128)S(1)} %get-tuple-element.102.refs_0_.part.old), channel_id=1, source_target_pairs={{0,2},{1,5},{2,0},{3,7},{4,6},{5,1},{6,4},{7,3},{8,10},{9,13},{10,... | collective-permute-start | bytes 196616 | tf_op jit(solution)/shard_map/ppermute | solution.py:528
  41.8 5.1 %collective-permute-start.12 = (f32[128,128]{1,0:T(8,128)S(1)}, f32[128,128]{1,0:T(8,128)S(1)}, u32[]{:S(2)}, u32[]{:S(2)}) collective-permute-start(f32[128,128]{1,0:T(8,128)S(1)} %update_pass.7.refs_0_.part.old), channel_id=1, source_target_pairs={{0,4},{1,3},{2,6},{3,1},{4,0},{5,7},{6,2},{7,5},{8,12},{9,11},{10,... | collective-permute-start | bytes 196616 | tf_op jit(solution)/shard_map/ppermute | solution.py:528
  43.4 13.4 %collective-permute-start.16 = (f32[384,128]{1,0:T(8,128)S(1)}, f32[384,128]{1,0:T(8,128)S(1)}, u32[]{:S(2)}, u32[]{:S(2)}) collective-permute-start(f32[384,128]{1,0:T(8,128)S(1)} %get-tuple-element.111), channel_id=1, source_target_pairs={{0,1},{1,0},{2,3},{3,2},{4,5},{5,4},{6,7},{7,6},{8,9},{9,8},{10,11... | collective-permute-start | bytes 589832 | tf_op jit(solution)/shard_map/ppermute | solution.py:518
  47.0 9.4 %collective-permute-start.14 = (f32[256,128]{1,0:T(8,128)S(1)}, f32[256,128]{1,0:T(8,128)S(1)}, u32[]{:S(2)}, u32[]{:S(2)}) collective-permute-start(f32[256,128]{1,0:T(8,128)S(1)} %gather_pass.5.part), channel_id=1, source_target_pairs={{0,2},{1,5},{2,0},{3,7},{4,6},{5,1},{6,4},{7,3},{8,10},{9,13},{10,... | collective-permute-start | bytes 393224 | tf_op jit(solution)/shard_map/ppermute | solution.py:528
  51.4 5.3 %collective-permute-start.15 = (f32[256,128]{1,0:T(8,128)S(1)}, f32[256,128]{1,0:T(8,128)S(1)}, u32[]{:S(2)}, u32[]{:S(2)}) collective-permute-start(f32[256,128]{1,0:T(8,128)S(1)} %gather_pass.4.refs_0_.part), channel_id=1, source_target_pairs={{0,4},{1,3},{2,6},{3,1},{4,0},{5,7},{6,2},{7,5},{8,12},{9,11},{10,... | collective-permute-start | bytes 393224 | tf_op jit(solution)/shard_map/ppermute | solution.py:528
  57.9 6.1 %collective-permute-start.20 = (f32[264,128]{1,0:T(8,128)S(1)}, f32[264,128]{1,0:T(8,128)S(1)}, u32[]{:S(2)}, u32[]{:S(2)}) collective-permute-start(f32[264,128]{1,0:T(8,128)S(1)} %get-tuple-element.119.refs_0_), channel_id=1, source_target_pairs={{0,4},{1,3},{2,6},{3,1},{4,0},{5,7},{6,2},{7,5},{8,12},{9,11},{10,... | collective-permute-start | bytes 405512 | tf_op jit(solution)/shard_map/ppermute | solution.py:528
  59.6 5.6 %collective-permute-start.17 = (f32[256,128]{1,0:T(8,128)S(1)}, f32[256,128]{1,0:T(8,128)S(1)}, u32[]{:S(2)}, u32[]{:S(2)}) collective-permute-start(f32[256,128]{1,0:T(8,128)S(1)} %get-tuple-element.113.refs_2_), channel_id=1, source_target_pairs={{0,2},{1,5},{2,0},{3,7},{4,6},{5,1},{6,4},{7,3},{8,10},{9,13},{10,... | collective-permute-start | bytes 393224 | tf_op jit(solution)/shard_map/ppermute | solution.py:528
  65.1 13.6 %collective-permute-start.31 = (f32[384,128]{1,0:T(8,128)S(1)}, f32[384,128]{1,0:T(8,128)S(1)}, u32[]{:S(2)}, u32[]{:S(2)}) collective-permute-start(f32[384,128]{1,0:T(8,128)S(1)} %get-tuple-element.129), channel_id=1, source_target_pairs={{0,1},{1,0},{2,3},{3,2},{4,5},{5,4},{6,7},{7,6},{8,9},{9,8},{10,11... | collective-permute-start | bytes 589832 | tf_op jit(solution)/shard_map/ppermute | solution.py:518
  68.3 5.3 %collective-permute-start.24 = (f32[136,128]{1,0:T(8,128)S(1)}, f32[136,128]{1,0:T(8,128)S(1)}, u32[]{:S(2)}, u32[]{:S(2)}) collective-permute-start(f32[136,128]{1,0:T(8,128)S(1)} %step_pass.30.refs_0_.held), channel_id=1, source_target_pairs={{0,16},{1,17},{2,18},{3,19},{4,20},{5,21},{6,22},{7,23},{8,24},{9,... | collective-permute-start | bytes 208904 | tf_op jit(solution)/shard_map/ppermute | solution.py:528
  73.7 5.1 %collective-permute-start.26 = (f32[136,128]{1,0:T(8,128)S(1)}, f32[136,128]{1,0:T(8,128)S(1)}, u32[]{:S(2)}, u32[]{:S(2)}) collective-permute-start(f32[136,128]{1,0:T(8,128)S(1)} %step_pass.32.refs_0_.held), channel_id=1, source_target_pairs={{0,8},{1,9},{2,10},{3,11},{4,12},{5,13},{6,14},{7,15},{8,0},{9,1},... | collective-permute-start | bytes 208904 | tf_op jit(solution)/shard_map/ppermute | solution.py:528
  73.7 5.0 %collective-permute-start.23 = (f32[128,128]{1,0:T(8,128)S(1)}, f32[128,128]{1,0:T(8,128)S(1)}, u32[]{:S(2)}, u32[]{:S(2)}) collective-permute-start(f32[128,128]{1,0:T(8,128)S(1)} %step_pass.31.refs_2_.held), channel_id=1, source_target_pairs={{0,8},{1,9},{2,10},{3,11},{4,12},{5,13},{6,14},{7,15},{8,0},{9,1},... | collective-permute-start | bytes 196616 | tf_op jit(solution)/shard_map/ppermute | solution.py:528
  79.0 14.2 %collective-permute-start.33 = (f32[384,256]{1,0:T(8,128)S(1)}, f32[384,256]{1,0:T(8,128)S(1)}, u32[]{:S(2)}, u32[]{:S(2)}) collective-permute-start(f32[384,256]{1,0:T(8,128)S(1)} %get-tuple-element.135), channel_id=1, source_target_pairs={{0,1},{1,2},{2,3},{3,4},{4,5},{5,6},{6,7},{7,8},{8,9},{9,10},{10,1... | collective-permute-start | bytes 1179656 | tf_op jit(solution)/shard_map/ppermute | solution.py:522
  79.1 7.0 %collective-permute-start.25 = (f32[128,128]{1,0:T(8,128)S(1)}, f32[128,128]{1,0:T(8,128)S(1)}, u32[]{:S(2)}, u32[]{:S(2)}) collective-permute-start(f32[128,128]{1,0:T(8,128)S(1)} %step_pass.33.refs_1_.held), channel_id=1, source_target_pairs={{0,16},{1,17},{2,18},{3,19},{4,20},{5,21},{6,22},{7,23},{8,24},{9,... | collective-permute-start | bytes 196616 | tf_op jit(solution)/shard_map/ppermute | solution.py:528
  81.1 6.2 %collective-permute-start.28 = (f32[128,128]{1,0:T(8,128)S(1)}, f32[128,128]{1,0:T(8,128)S(1)}, u32[]{:S(2)}, u32[]{:S(2)}) collective-permute-start(f32[128,128]{1,0:T(8,128)S(1)} %get-tuple-element.124.refs_0_.part), channel_id=1, source_target_pairs={{0,2},{1,5},{2,0},{3,7},{4,6},{5,1},{6,4},{7,3},{8,10},{9,13},{10,... | collective-permute-start | bytes 196616 | tf_op jit(solution)/shard_map/ppermute | solution.py:528
  86.1 5.2 %collective-permute-start.27 = (f32[128,128]{1,0:T(8,128)S(1)}, f32[128,128]{1,0:T(8,128)S(1)}, u32[]{:S(2)}, u32[]{:S(2)}) collective-permute-start(f32[128,128]{1,0:T(8,128)S(1)} %update_pass.9.refs_0_.part), channel_id=1, source_target_pairs={{0,4},{1,3},{2,6},{3,1},{4,0},{5,7},{6,2},{7,5},{8,12},{9,11},{10,... | collective-permute-start | bytes 196616 | tf_op jit(solution)/shard_map/ppermute | solution.py:528
  86.2 12.1 %collective-permute-start.32 = (f32[384,128]{1,0:T(8,128)S(1)}, f32[384,128]{1,0:T(8,128)S(1)}, u32[]{:S(2)}, u32[]{:S(2)}) collective-permute-start(f32[384,128]{1,0:T(8,128)S(1)} %get-tuple-element.133), channel_id=1, source_target_pairs={{0,1},{1,0},{2,3},{3,2},{4,5},{5,4},{6,7},{7,6},{8,9},{9,8},{10,11... | collective-permute-start | bytes 589832 | tf_op jit(solution)/shard_map/ppermute | solution.py:518
  91.3 6.6 %collective-permute-start.29 = (f32[256,128]{1,0:T(8,128)S(1)}, f32[256,128]{1,0:T(8,128)S(1)}, u32[]{:S(2)}, u32[]{:S(2)}) collective-permute-start(f32[256,128]{1,0:T(8,128)S(1)} %gather_pass.7.part.first_part), channel_id=1, source_target_pairs={{0,2},{1,5},{2,0},{3,7},{4,6},{5,1},{6,4},{7,3},{8,10},{9,13},{10,... | collective-permute-start | bytes 393224 | tf_op jit(solution)/shard_map/ppermute | solution.py:528
  92.0 6.3 %collective-permute-start.30 = (f32[256,128]{1,0:T(8,128)S(1)}, f32[256,128]{1,0:T(8,128)S(1)}, u32[]{:S(2)}, u32[]{:S(2)}) collective-permute-start(f32[256,128]{1,0:T(8,128)S(1)} %gather_pass.6.refs_0_.part), channel_id=1, source_target_pairs={{0,4},{1,3},{2,6},{3,1},{4,0},{5,7},{6,2},{7,5},{8,12},{9,11},{10,... | collective-permute-start | bytes 393224 | tf_op jit(solution)/shard_map/ppermute | solution.py:528
  100.0 6.2 %collective-permute-start.35 = (f32[264,128]{1,0:T(8,128)S(1)}, f32[264,128]{1,0:T(8,128)S(1)}, u32[]{:S(2)}, u32[]{:S(2)}) collective-permute-start(f32[264,128]{1,0:T(8,128)S(1)} %get-tuple-element.138.refs_0_), channel_id=1, source_target_pairs={{0,4},{1,3},{2,6},{3,1},{4,0},{5,7},{6,2},{7,5},{8,12},{9,11},{10,... | collective-permute-start | bytes 405512 | tf_op jit(solution)/shard_map/ppermute | solution.py:528
  100.6 7.0 %collective-permute-start.37 = (f32[256,128]{1,0:T(8,128)S(1)}, f32[256,128]{1,0:T(8,128)S(1)}, u32[]{:S(2)}, u32[]{:S(2)}) collective-permute-start(f32[256,128]{1,0:T(8,128)S(1)} %get-tuple-element.139.refs_2_), channel_id=1, source_target_pairs={{0,2},{1,5},{2,0},{3,7},{4,6},{5,1},{6,4},{7,3},{8,10},{9,13},{10,... | collective-permute-start | bytes 393224 | tf_op jit(solution)/shard_map/ppermute | solution.py:528
  102.2 18.4 %collective-permute-start.42 = (f32[384,128]{1,0:T(8,128)S(1)}, f32[384,128]{1,0:T(8,128)S(1)}, u32[]{:S(2)}, u32[]{:S(2)}) collective-permute-start(f32[384,128]{1,0:T(8,128)S(1)} %get-tuple-element.157), channel_id=1, source_target_pairs={{0,1},{1,0},{2,3},{3,2},{4,5},{5,4},{6,7},{7,6},{8,9},{9,8},{10,11... | collective-permute-start | bytes 589832 | tf_op jit(solution)/shard_map/ppermute | solution.py:518
  110.6 4.9 %collective-permute-start.38 = (f32[72,128]{1,0:T(8,128)S(1)}, f32[72,128]{1,0:T(8,128)S(1)}, u32[]{:S(2)}, u32[]{:S(2)}) collective-permute-start(f32[72,128]{1,0:T(8,128)S(1)} %get-tuple-element.145.refs_0_), channel_id=1, source_target_pairs={{0,16},{1,17},{2,18},{3,19},{4,20},{5,21},{6,22},{7,23},{8,24},{9,... | collective-permute-start | bytes 110600 | tf_op jit(solution)/shard_map/ppermute | solution.py:528
  115.9 4.6 %collective-permute-start.43 = (f32[32,128]{1,0:T(8,128)S(1)}, f32[32,128]{1,0:T(8,128)S(1)}, u32[]{:S(2)}, u32[]{:S(2)}) collective-permute-start(f32[32,128]{1,0:T(8,128)S(1)} %get-tuple-element.152.refs_1_), channel_id=1, source_target_pairs={{0,16},{1,17},{2,18},{3,19},{4,20},{5,21},{6,22},{7,23},{8,24},{9,... | collective-permute-start | bytes 49160 | tf_op jit(solution)/shard_map/ppermute | solution.py:528
  (23 other events, 83.0 us)

commit v10 on v6

--- a/solution.py
+++ b/solution.py
@@ -48,6 +48,11 @@
     return [core, *bits, own >> 1]
 
 
+def rows_at(which, rows):
+    start = which * rows
+    return pl.ds(pl.multiple_of(start, rows) if rows % 8 == 0 else start, rows)
+
+
 def half_of(ref, core):
     width = ref.shape[1] // CORES
     return ref[:, pl.ds(pl.multiple_of(core * width, width), width)]
@@ -57,50 +62,28 @@
     return (1.0 + stats[1:2, :] / 2.0) / (1.0 + stats[0:1, :] / 2.0)
 
 
-def tile_kernel(stratum, noise_scale, devices, codes, count, ratings, user_noise, item_noise, *refs):
-    if stratum == 0:
-        users_in, items_in = refs[:2]
-        base_u, grad_u, base_v, grad_v, stats = refs[2:7]
-        refs = refs[7:]
-    else:
-        old_base, old_grad, own_mean, other_mean, old_stats, old_base_v, old_grad_v = refs[:7]
-        base_u, grad_u, base_v, grad_v, stats, own_cols, other_cols = refs[7:14]
-        refs = refs[14:]
-    tiles, noise_u, noise_v, users, items, pred, err_b, sems = refs
-    core = where_am_i(devices)[0]
-    rows, rank = users.shape
-    width = rank // CORES
+def tile_kernel(stratum, noise_scale, codes, count, ratings, user_noise, item_noise, *refs):
+    users_in, items_in, base_u, grad_u, base_v, grad_v, stats = refs[:7]
+    tiles, noise_u, noise_v, pred, err_b, sems = refs[7:13]
+    rows = err_b.shape[0]
     tile = tiles.shape[-1]
     grid = rows // tile
+    moves = [
+        (ratings.at[0, stratum], tiles),
+        (user_noise.at[stratum], noise_u),
+        (item_noise.at[stratum], noise_v),
+    ]
+    users, items = users_in, items_in
+    if stratum == 0:
+        users, items = refs[13:]
+        moves += [(users_in, users), (items_in, items)]
     copies = [
-        pltpu.make_async_copy(source, target, sems.at[n])
-        for n, (source, target) in enumerate(
-            [
-                (ratings.at[0, stratum], tiles),
-                (user_noise.at[stratum], noise_u),
-                (item_noise.at[stratum], noise_v),
-            ]
-            + ([(users_in, users), (items_in, items)] if stratum == 0 else [])
-        )
+        pltpu.make_async_copy(source, target, sems.at[n]) for n, (source, target) in enumerate(moves)
     ]
     for copy in copies[::-1]:
         copy.start()
-    if stratum == 0:
-        copies[4].wait()
-        copies[3].wait()
-    else:
-        precision = precision_of(old_stats[...])
-        precision = jnp.concatenate([precision] * CORES, 1)
-        items[...] = old_base_v[...] + precision * old_grad_v[...]
-        new = old_base[...] + precision * old_grad[...]
-        here = core == 0
-        pull = step_size * prior_prec
-        left = jnp.where(here, own_mean[...], other_mean[...])
-        right = jnp.where(here, other_mean[...], own_mean[...])
-        users[:, :width] = new[:, :width] + pull * left
-        users[:, width:] = new[:, width:] + pull * right
-        own_cols[...] = half_of(users, core)
-        other_cols[...] = half_of(users, 1 - core)
+    for copy in copies[3:]:
+        copy.wait()
     user_b = users[...].astype(bf16)
     item_b = items[...].astype(bf16)
     pred[...] = dot(user_b, item_b, NT)
@@ -110,8 +93,8 @@
     copies[0].wait()
     for slot in range(tiles.shape[0]):
         code = codes[0, stratum, slot]
-        at_rows = pl.ds(pl.multiple_of(code // grid * tile, tile), tile)
-        at_cols = pl.ds(pl.multiple_of(code % grid * tile, tile), tile)
+        at_rows = rows_at(code // grid, tile)
+        at_cols = rows_at(code % grid, tile)
         live = (slot < live_slots).astype(f32)
         err = (tiles[slot].astype(f32) - pred[at_rows, at_cols]) * live
         sse = sse + err * err
@@ -123,43 +106,36 @@
     stats[...] = jnp.where(row == 0, total, jnp.where(row == 1, counted, 0.0))
     grad_u[...] = step_size * dot(err_all, item_b)
     grad_v[...] = step_size * dot(err_all, user_b, TN)
-    copies[2].wait()
-    base_v[...] = (1.0 - step_size * item_prec) * items[...] + noise_scale * noise_v[...].astype(
-        f32
-    )
     copies[1].wait()
     base_u[...] = (1.0 - step_size * prior_prec) * users[...] + noise_scale * noise_u[...].astype(
         f32
     )
-
-
-def tile_pass(stratum, devices, codes, count, ratings, user_noise, item_noise, *state):
+    copies[2].wait()
+    base_v[...] = (1.0 - step_size * item_prec) * items[...] + noise_scale * noise_v[...].astype(f32)
+
+
+def tile_pass(stratum, codes, count, ratings, user_noise, item_noise, users, items):
     slots, tile = ratings.shape[2:4]
-    rows, rank = user_noise.shape[1:]
-    noise_scale = math.sqrt(2.0 * step_size)
-    width = rank // CORES
-    outs = [shape(rows, rank)] * 4 + [shape(RIDERS, width)]
-    if stratum:
-        outs += [shape(rows, width)] * 2
-    return pl.pallas_call(
-        functools.partial(tile_kernel, stratum, noise_scale, devices),
-        out_shape=tuple(outs),
-        in_specs=[SMEM] * 2 + [HBM] * 3 + [VMEM if stratum else HBM] * len(state),
-        out_specs=(VMEM,) * len(outs),
+    rows, rank = users.shape
+    first = stratum == 0
+    return pl.pallas_call(
+        functools.partial(tile_kernel, stratum, math.sqrt(2.0 * step_size)),
+        out_shape=(shape(rows, rank),) * 4 + (shape(RIDERS, rank // CORES),),
+        in_specs=[SMEM] * 2 + [HBM] * 3 + [HBM if first else VMEM] * 2,
+        out_specs=(VMEM,) * 5,
         scratch_shapes=[
             pltpu.VMEM((slots, tile, tile), bf16),
             pltpu.VMEM((rows, rank), bf16),
             pltpu.VMEM((rows, rank), bf16),
-            pltpu.VMEM((rows, rank), f32),
-            pltpu.VMEM((rows, rank), f32),
             pltpu.VMEM((rows, rows), f32),
             pltpu.VMEM((rows, rows), bf16),
             pltpu.SemaphoreType.DMA((5,)),
-        ],
+        ]
+        + [pltpu.VMEM((rows, rank), f32)] * (2 if first else 0),
         compiler_params=PARAMS,
         cost_estimate=cost(6 * rows * rows * rank, 16 * rows * rank),
         name="tile_pass",
-    )(codes, count, ratings, user_noise, item_noise, *state)
+    )(codes, count, ratings, user_noise, item_noise, users, items)
 
 
 def first_kernel(devices, feats_in, weights_in, users_in, own_mean, other_mean, send, keep, old, mean, feats, weights, users, sems):
@@ -441,29 +417,33 @@
     )(mine, other)
 
 
-def last_kernel(devices, stats, base, grad, own_mean, other_mean, base_v, grad_v, users, items):
-    place = where_am_i(devices)
+def renew_kernel(devices, stats, base_u, grad_u, own_mean, other_mean, base_v, grad_v, users, items, *cols):
+    core = where_am_i(devices)[0]
     width = own_mean.shape[1]
     precision = precision_of(stats[...])
     precision = jnp.concatenate([precision] * CORES, 1)
     items[...] = base_v[...] + precision * grad_v[...]
-    users[...] = base[...] + precision * grad[...]
+    new = base_u[...] + precision * grad_u[...]
     pull = step_size * prior_prec
-    for mean, which in ((own_mean, place[0]), (other_mean, 1 - place[0])):
-        at = pl.ds(pl.multiple_of(which * width, width), width)
-        users[:, at] = users[:, at] + pull * mean[...]
-
-
-def last_pass(devices, stats, base, *state):
-    return pl.pallas_call(
-        functools.partial(last_kernel, devices),
-        out_shape=(shape(*base.shape),) * 2,
+    left = jnp.where(core == 0, own_mean[...], other_mean[...])
+    right = jnp.where(core == 0, other_mean[...], own_mean[...])
+    users[:, :width] = new[:, :width] + pull * left
+    users[:, width:] = new[:, width:] + pull * right
+    for ref, which in zip(cols, (core, 1 - core), strict=False):
+        ref[...] = half_of(users, which)
+
+
+def renew_pass(devices, last, stats, base_u, grad_u, own_mean, *state):
+    outs = [shape(*base_u.shape)] * 2 + ([] if last else [shape(*own_mean.shape)] * 2)
+    return pl.pallas_call(
+        functools.partial(renew_kernel, devices),
+        out_shape=tuple(outs),
         in_specs=[VMEM] * 7,
-        out_specs=(VMEM,) * 2,
-        compiler_params=PARAMS,
-        cost_estimate=cost(8 * base.size, 32 * base.size),
-        name="last_pass",
-    )(stats, base, *state)
+        out_specs=(VMEM,) * len(outs),
+        compiler_params=PARAMS,
+        cost_estimate=cost(8 * base_u.size, 32 * base_u.size),
+        name="renew_pass",
+    )(stats, base_u, grad_u, own_mean, *state)
 
 
 def bit_order(devices, core):
@@ -516,46 +496,42 @@
     strata = ratings.shape[1]
     feat = prior_weights.shape[0]
     rate = rate_scale / (user_factors.shape[0] * devices)
-    tables = (devices, tile_index, tile_count, ratings, user_noise, item_noise)
+    tables = (tile_index, tile_count, ratings, user_noise, item_noise)
 
     own_mean, other_mean, send, held, old = first_pass(
         devices, side_features, prior_weights, user_factors
     )
     got = swap(send, devices)
-    base, grad, base_v, grad_v, stats = tile_pass(0, *tables, user_factors, item_factors)
+    *state, stats = tile_pass(0, *tables, user_factors, item_factors)
     more = swap(stats, devices)
     send, held = step_pass(True, 0, devices, held, got, stats, more, feat)
     feats, turned = join_pass(side_features, swap(widen_pass(side_features), devices))
     for stratum in range(strata):
         last = stratum + 1 == strata
-        if not last:
-            base_v, grad_v = roll(base_v, devices), roll(grad_v, devices)
-        got = exchange(send, devices, 0)
-        send, held = step_pass(True, 1, devices, held, got, send, got, feat // 2)
-        for stage in range(1, stages - 1):
+        for stage in range(stages - 1):
             got = exchange(send, devices, stage)
             rows = got.shape[0] - RIDERS
-            if last:
+            if last or stage < 1:
                 send, held = step_pass(True, stage + 1, devices, held, got, send, got, rows)
             else:
-                later = (base_v,) if stage == 1 else ()
-                (send,) = step_pass(False, 0, devices, held, got, send, got, rows, later)
+                (send,) = step_pass(False, 0, devices, held, got, send, got, rows)
                 held = send
         got = exchange(send, devices, stages - 1)
-        part, stats = update_pass(rate, held, got, send, old, () if last else (grad_v,))
+        part, stats = update_pass(rate, held, got, send, old)
+        users, items, *cols = renew_pass(
+            devices, last, stats, *state[:2], own_mean, other_mean, *state[2:]
+        )
         if last:
             break
         old = part
-        got = exchange(part, devices, 1)
-        part = gather_pass(1, devices, part, got)
+        items = roll(items, devices)
+        own_cols, other_cols = cols[0], swap(cols[1], devices)
+        part = gather_pass(1, devices, part, exchange(part, devices, 1))
         got = exchange(part, devices, 0)
+        *state, stats = tile_pass(stratum + 1, *tables, users, items)
+        more = swap(stats, devices)
         begun = part_pass(devices, feats, part)
-        base, grad, base_v, grad_v, stats, own_cols, other_cols = tile_pass(
-            stratum + 1, *tables, base, grad, own_mean, other_mean, stats, base_v, grad_v
-        )
-        more = swap(stats, devices)
-        other_cols = swap(other_cols, devices)
-        outs = prior_pass(
+        own_mean, other_mean, send, held, *olds = prior_pass(
             devices,
             feats,
             turned,
@@ -568,14 +544,11 @@
             more,
             final_places(devices) if stratum + 2 == strata else None,
         )
-        own_mean, other_mean, send, held = outs[:4]
-        if len(outs) > 4:
-            old = outs[4]
+        if olds:
+            (old,) = olds
         other_mean = swap(other_mean, devices)
     mine, other = split_pass(devices, part)
-    got = swap(other, devices)
-    users, items = last_pass(devices, stats, base, grad, own_mean, other_mean, base_v, grad_v)
-    return (users, items, across_pass(devices, mine, got))
+    return (users, items, across_pass(devices, mine, swap(other, devices)))
 
 
 def solution(mesh):

time: 129 us -> 118 us (0.915)
  waiting for transfers between devices: 75.7 us -> 67.4 us
  starting transfers between devices: 33.2 us -> 30.6 us
    ppermute x16, waiting for transfers between devices: 71.6 us -> 65.5 us  [exchange(): return lax.ppermute(array, 'user', pairs)]
    ppermute x16, starting transfers between devices: 30.8 us -> 25.3 us  [exchange(): return lax.ppermute(array, 'user', pairs)]
    ppermute x10, starting transfers between devices: 2.37 us -> 5.17 us  [swap(): return lax.ppermute(array, 'user', [(i, i ^ 1) for i in range(devices)])]
    ppermute x4 -> x2, waiting for transfers between devices: 2.55 us -> 0.86 us  [roll(): lax.ppermute(array, 'user', [(i, (i + 1) % devices) for i in range(device...]
    pallas_call x4 -> x6, Pallas kernels: 8.46 us -> 8.62 us  [the longest x3 7.14 us: tile_pass(): pl.pallas_call(functools.partial(tile_kernel, stratum, math.sqrt(2.0 * st...]
  transfers between devices with their start and end apart: 30 -> 28, of which waited for: 20 -> 19; matrix products, arithmetic and copies ran while one was open for 0% -> 0% of each run, Pallas kernels for 8% -> 9%
where the time goes in v10:
time: 118 us
  waiting for transfers between devices  67.4 us (57%)
  starting transfers between devices  30.6 us (26%)
  Pallas kernels  14.8 us (13%)
  local copies, waits for them, and re-layouts  4.04 us (3%)
    ppermute x16, waiting for transfers between devices, exchange(): return lax.ppermute(array, 'user', pairs)  65.5 us
    ppermute x16, starting transfers between devices, exchange(): return lax.ppermute(array, 'user', pairs)  25.3 us
    pallas_call x3, Pallas kernels, tile_pass(): pl.pallas_call(functools.partial(tile_kernel, stratum, math.sqrt(2.0 * st...  7.14 us
    ppermute x10, starting transfers between devices, swap(): return lax.ppermute(array, 'user', [(i, i ^ 1) for i in range(devices)])  5.17 us
    unnamed x23, local copies, waits for them, and re-layouts  4.04 us
  transfers between devices with their start and end apart: 28, of which 19 were waited for; matrix products, arithmetic and copies ran while one was open for 0% of the time, Pallas kernels for 9%

profile of v10, /device:TPU:0, one launch (start us, length us, event | category | flops | bytes accessed | tf_op | source)
XLA Modules:
  0.0 117.8 jit_solution(15359897756300271969)
XLA Ops:
  2.8 1.2 %copy-done.7 = f32[1024,256]{1,0:T(8,128)S(1)} copy-done((f32[1024,256]{1,0:T(8,128)S(1)}, f32[1024,256]{1,0:T(8,128)}, u32[]{:S(2)}) %copy-start.7) | copy-done | bytes 1048600
  4.0 1.6 %first_pass.1 = (f32[384,128]{1,0:T(8,128)S(1)}, f32[384,128]{1,0:T(8,128)S(1)}, f32[1024,128]{1,0:T(8,128)S(1)}, f32[1024,128]{1,0:T(8,128)S(1)}, f32[256,128]{1,0:T(8,128)S(1)}) custom-call(bf16[384,1024]{1,0:T(8,128)(2,1)S(1)} %copy-done, f32[1024,256]{1,0:T(8,128)S(1)} %copy-done.7, f32[384,256]{1,0:T(8,128)S(1)} %copy-done.5), custom_call_target="tpu_custom_call" | custom-call | flops 402653184 | bytes 2097152 | tf_op jit(solution)/shard_map/first_pass/pallas_call | solution.py:172
  7.2 2.6 %tile_pass.3 = (f32[384,256]{1,0:T(8,128)S(1)}, f32[384,256]{1,0:T(8,128)S(1)}, f32[384,256]{1,0:T(8,128)S(1)}, f32[384,256]{1,0:T(8,128)S(1)}, f32[8,128]{1,0:T(8,128)S(1)}) custom-call(s32[1,3,6]{2,1,0:T(4,128)S(1)} %copy.12.codes, s32[1,3]{1,0:T(1,128)S(1)} %copy-done.9, bf16[1,3,6,128,128]{4,3,2,1,0:T(8,128)(2,1)S(1)} %copy-done.2, ...), custom_call_target="tpu_custom_call" | custom-call | flops 226492416 | bytes 1572864 | tf_op jit(solution)/shard_map/tile_pass/pallas_call | solution.py:121
  11.2 2.9 %collective-permute-start.3 = (f32[520,128]{1,0:T(8,128)S(1)}, f32[520,128]{1,0:T(8,128)S(1)}, u32[]{:S(2)}, u32[]{:S(2)}) collective-permute-start(f32[520,128]{1,0:T(8,128)S(1)} %get-tuple-element.70.sent), channel_id=1, source_target_pairs={{0,2},{1,5},{2,0},{3,7},{4,6},{5,1},{6,4},{7,3},{8,10},{9,13},{10,... | collective-permute-start | bytes 798728 | tf_op jit(solution)/shard_map/ppermute | solution.py:466
  14.1 4.4 %collective-permute-done.3.got.more = f32[520,128]{1,0:T(8,128)S(1)} collective-permute-done((f32[520,128]{1,0:T(8,128)S(1)}, f32[520,128]{1,0:T(8,128)S(1)}, u32[]{:S(2)}, u32[]{:S(2)}) %collective-permute-start.3) | collective-permute-done | bytes 266272 | tf_op jit(solution)/shard_map/ppermute | solution.py:466
  18.5 2.1 %collective-permute-start.4 = (f32[264,128]{1,0:T(8,128)S(1)}, f32[264,128]{1,0:T(8,128)S(1)}, u32[]{:S(2)}, u32[]{:S(2)}) collective-permute-start(f32[264,128]{1,0:T(8,128)S(1)} %get-tuple-element.72.sent), channel_id=1, source_target_pairs={{0,4},{1,3},{2,6},{3,1},{4,0},{5,7},{6,2},{7,5},{8,12},{9,11},{10,... | collective-permute-start | bytes 405512 | tf_op jit(solution)/shard_map/ppermute | solution.py:466
  20.6 3.0 %collective-permute-done.4.got.more = f32[264,128]{1,0:T(8,128)S(1)} collective-permute-done((f32[264,128]{1,0:T(8,128)S(1)}, f32[264,128]{1,0:T(8,128)S(1)}, u32[]{:S(2)}, u32[]{:S(2)}) %collective-permute-start.4) | collective-permute-done | bytes 135200 | tf_op jit(solution)/shard_map/ppermute | solution.py:466
  23.7 2.1 %collective-permute-start.5 = (f32[264,128]{1,0:T(8,128)S(1)}, f32[264,128]{1,0:T(8,128)S(1)}, u32[]{:S(2)}, u32[]{:S(2)}) collective-permute-start(f32[264,128]{1,0:T(8,128)S(1)} %step_pass.12.held.sent), channel_id=1, source_target_pairs={{0,8},{1,17},{2,10},{3,19},{4,12},{5,21},{6,14},{7,23},{8,0},{9,25... | collective-permute-start | bytes 405512 | tf_op jit(solution)/shard_map/ppermute | solution.py:466
  25.8 3.4 %collective-permute-done.5.got.more = f32[264,128]{1,0:T(8,128)S(1)} collective-permute-done((f32[264,128]{1,0:T(8,128)S(1)}, f32[264,128]{1,0:T(8,128)S(1)}, u32[]{:S(2)}, u32[]{:S(2)}) %collective-permute-start.5) | collective-permute-done | bytes 135200 | tf_op jit(solution)/shard_map/ppermute | solution.py:466
  29.2 2.7 %collective-permute-start.6 = (f32[264,128]{1,0:T(8,128)S(1)}, f32[264,128]{1,0:T(8,128)S(1)}, u32[]{:S(2)}, u32[]{:S(2)}) collective-permute-start(f32[264,128]{1,0:T(8,128)S(1)} %step_pass.13.held.sent), channel_id=1, source_target_pairs={{0,16},{1,9},{2,18},{3,11},{4,20},{5,13},{6,22},{7,15},{8,24},{9,1... | collective-permute-start | bytes 405512 | tf_op jit(solution)/shard_map/ppermute | solution.py:466
  31.9 3.3 %collective-permute-done.6.got = f32[264,128]{1,0:T(8,128)S(1)} collective-permute-done((f32[264,128]{1,0:T(8,128)S(1)}, f32[264,128]{1,0:T(8,128)S(1)}, u32[]{:S(2)}, u32[]{:S(2)}) %collective-permute-start.6) | collective-permute-done | bytes 135200 | tf_op jit(solution)/shard_map/ppermute | solution.py:466
  35.6 3.4 %collective-permute-start.7 = (f32[256,128]{1,0:T(8,128)S(1)}, f32[256,128]{1,0:T(8,128)S(1)}, u32[]{:S(2)}, u32[]{:S(2)}) collective-permute-start(f32[256,128]{1,0:T(8,128)S(1)} %get-tuple-element.74.part.old), channel_id=1, source_target_pairs={{0,4},{1,3},{2,6},{3,1},{4,0},{5,7},{6,2},{7,5},{8,12},{9,11},{10,... | collective-permute-start | bytes 393224 | tf_op jit(solution)/shard_map/ppermute | solution.py:466
  39.0 6.7 %collective-permute-done.7.got = f32[256,128]{1,0:T(8,128)S(1)} collective-permute-done((f32[256,128]{1,0:T(8,128)S(1)}, f32[256,128]{1,0:T(8,128)S(1)}, u32[]{:S(2)}, u32[]{:S(2)}) %collective-permute-start.7) | collective-permute-done | bytes 131104 | tf_op jit(solution)/shard_map/ppermute | solution.py:466
  45.8 2.3 %collective-permute-start.9 = (f32[384,128]{1,0:T(8,128)S(1)}, f32[384,128]{1,0:T(8,128)S(1)}, u32[]{:S(2)}, u32[]{:S(2)}) collective-permute-start(f32[384,128]{1,0:T(8,128)S(1)} %get-tuple-element.83), channel_id=1, source_target_pairs={{0,1},{1,0},{2,3},{3,2},{4,5},{5,4},{6,7},{7,6},{8,9},{9,8},{10,11... | collective-permute-start | bytes 589832 | tf_op jit(solution)/shard_map/ppermute | solution.py:456
  48.7 2.3 %tile_pass.4 = (f32[384,256]{1,0:T(8,128)S(1)}, f32[384,256]{1,0:T(8,128)S(1)}, f32[384,256]{1,0:T(8,128)S(1)}, f32[384,256]{1,0:T(8,128)S(1)}, f32[8,128]{1,0:T(8,128)S(1)}) custom-call(s32[1,3,6]{2,1,0:T(4,128)S(1)} %copy.12.codes, s32[1,3]{1,0:T(1,128)S(1)} %copy-done.9, bf16[1,3,6,128,128]{4,3,2,1,0:T(8,128)(2,1)S(1)} %copy-done.2, ...), custom_call_target="tpu_custom_call" | custom-call | flops 226492416 | bytes 1572864 | tf_op jit(solution)/shard_map/tile_pass/pallas_call | solution.py:121
  53.6 5.9 %collective-permute-done.12.got.more = f32[520,128]{1,0:T(8,128)S(1)} collective-permute-done((f32[520,128]{1,0:T(8,128)S(1)}, f32[520,128]{1,0:T(8,128)S(1)}, u32[]{:S(2)}, u32[]{:S(2)}) %collective-permute-start.12) | collective-permute-done | bytes 266272 | tf_op jit(solution)/shard_map/ppermute | solution.py:466
  59.5 2.5 %collective-permute-start.13 = (f32[264,128]{1,0:T(8,128)S(1)}, f32[264,128]{1,0:T(8,128)S(1)}, u32[]{:S(2)}, u32[]{:S(2)}) collective-permute-start(f32[264,128]{1,0:T(8,128)S(1)} %get-tuple-element.90.sent), channel_id=1, source_target_pairs={{0,4},{1,3},{2,6},{3,1},{4,0},{5,7},{6,2},{7,5},{8,12},{9,11},{10,... | collective-permute-start | bytes 405512 | tf_op jit(solution)/shard_map/ppermute | solution.py:466
  62.0 3.0 %collective-permute-done.13.got.more = f32[264,128]{1,0:T(8,128)S(1)} collective-permute-done((f32[264,128]{1,0:T(8,128)S(1)}, f32[264,128]{1,0:T(8,128)S(1)}, u32[]{:S(2)}, u32[]{:S(2)}) %collective-permute-start.13) | collective-permute-done | bytes 135200 | tf_op jit(solution)/shard_map/ppermute | solution.py:466
  66.0 4.7 %collective-permute-done.14.got.more = f32[264,128]{1,0:T(8,128)S(1)} collective-permute-done((f32[264,128]{1,0:T(8,128)S(1)}, f32[264,128]{1,0:T(8,128)S(1)}, u32[]{:S(2)}, u32[]{:S(2)}) %collective-permute-start.14) | collective-permute-done | bytes 135200 | tf_op jit(solution)/shard_map/ppermute | solution.py:466
  70.7 1.7 %collective-permute-start.15 = (f32[264,128]{1,0:T(8,128)S(1)}, f32[264,128]{1,0:T(8,128)S(1)}, u32[]{:S(2)}, u32[]{:S(2)}) collective-permute-start(f32[264,128]{1,0:T(8,128)S(1)} %step_pass.16.held.sent), channel_id=1, source_target_pairs={{0,16},{1,9},{2,18},{3,11},{4,20},{5,13},{6,22},{7,15},{8,24},{9,1... | collective-permute-start | bytes 405512 | tf_op jit(solution)/shard_map/ppermute | solution.py:466
  72.4 5.7 %collective-permute-done.15.got = f32[264,128]{1,0:T(8,128)S(1)} collective-permute-done((f32[264,128]{1,0:T(8,128)S(1)}, f32[264,128]{1,0:T(8,128)S(1)}, u32[]{:S(2)}, u32[]{:S(2)}) %collective-permute-start.15) | collective-permute-done | bytes 135200 | tf_op jit(solution)/shard_map/ppermute | solution.py:466
  78.5 1.6 %collective-permute-start.16 = (f32[256,128]{1,0:T(8,128)S(1)}, f32[256,128]{1,0:T(8,128)S(1)}, u32[]{:S(2)}, u32[]{:S(2)}) collective-permute-start(f32[256,128]{1,0:T(8,128)S(1)} %get-tuple-element.91.part), channel_id=1, source_target_pairs={{0,4},{1,3},{2,6},{3,1},{4,0},{5,7},{6,2},{7,5},{8,12},{9,11},{10,... | collective-permute-start | bytes 393224 | tf_op jit(solution)/shard_map/ppermute | solution.py:466
  80.1 6.7 %collective-permute-done.16.got = f32[256,128]{1,0:T(8,128)S(1)} collective-permute-done((f32[256,128]{1,0:T(8,128)S(1)}, f32[256,128]{1,0:T(8,128)S(1)}, u32[]{:S(2)}, u32[]{:S(2)}) %collective-permute-start.16) | collective-permute-done | bytes 131104 | tf_op jit(solution)/shard_map/ppermute | solution.py:466
  86.9 1.5 %collective-permute-start.19 = (f32[384,128]{1,0:T(8,128)S(1)}, f32[384,128]{1,0:T(8,128)S(1)}, u32[]{:S(2)}, u32[]{:S(2)}) collective-permute-start(f32[384,128]{1,0:T(8,128)S(1)} %get-tuple-element.100), channel_id=1, source_target_pairs={{0,1},{1,0},{2,3},{3,2},{4,5},{5,4},{6,7},{7,6},{8,9},{9,8},{10,11... | collective-permute-start | bytes 589832 | tf_op jit(solution)/shard_map/ppermute | solution.py:456
  89.3 2.3 %tile_pass.5 = (f32[384,256]{1,0:T(8,128)S(1)}, f32[384,256]{1,0:T(8,128)S(1)}, f32[384,256]{1,0:T(8,128)S(1)}, f32[384,256]{1,0:T(8,128)S(1)}, f32[8,128]{1,0:T(8,128)S(1)}) custom-call(s32[1,3,6]{2,1,0:T(4,128)S(1)} %copy.12.codes, s32[1,3]{1,0:T(1,128)S(1)} %copy-done.9, bf16[1,3,6,128,128]{4,3,2,1,0:T(8,128)(2,1)S(1)} %copy-done.2, ...), custom_call_target="tpu_custom_call" | custom-call | flops 226492416 | bytes 1572864 | tf_op jit(solution)/shard_map/tile_pass/pallas_call | solution.py:121
  92.0 1.3 %collective-permute-done.17.got = f32[512,128]{1,0:T(8,128)S(1)} collective-permute-done((f32[512,128]{1,0:T(8,128)S(1)}, f32[512,128]{1,0:T(8,128)S(1)}, u32[]{:S(2)}, u32[]{:S(2)}) %collective-permute-start.17) | collective-permute-done | bytes 262176 | tf_op jit(solution)/shard_map/ppermute | solution.py:466
  94.6 6.4 %collective-permute-done.22.got.more = f32[520,128]{1,0:T(8,128)S(1)} collective-permute-done((f32[520,128]{1,0:T(8,128)S(1)}, f32[520,128]{1,0:T(8,128)S(1)}, u32[]{:S(2)}, u32[]{:S(2)}) %collective-permute-start.22) | collective-permute-done | bytes 266272 | tf_op jit(solution)/shard_map/ppermute | solution.py:466
  101.0 2.5 %collective-permute-start.23 = (f32[264,128]{1,0:T(8,128)S(1)}, f32[264,128]{1,0:T(8,128)S(1)}, u32[]{:S(2)}, u32[]{:S(2)}) collective-permute-start(f32[264,128]{1,0:T(8,128)S(1)} %get-tuple-element.107.sent), channel_id=1, source_target_pairs={{0,4},{1,3},{2,6},{3,1},{4,0},{5,7},{6,2},{7,5},{8,12},{9,11},{10,... | collective-permute-start | bytes 405512 | tf_op jit(solution)/shard_map/ppermute | solution.py:466
  103.6 3.0 %collective-permute-done.23.got.more = f32[264,128]{1,0:T(8,128)S(1)} collective-permute-done((f32[264,128]{1,0:T(8,128)S(1)}, f32[264,128]{1,0:T(8,128)S(1)}, u32[]{:S(2)}, u32[]{:S(2)}) %collective-permute-start.23) | collective-permute-done | bytes 135200 | tf_op jit(solution)/shard_map/ppermute | solution.py:466
  106.8 4.1 %collective-permute-done.24.got.more = f32[136,128]{1,0:T(8,128)S(1)} collective-permute-done((f32[136,128]{1,0:T(8,128)S(1)}, f32[136,128]{1,0:T(8,128)S(1)}, u32[]{:S(2)}, u32[]{:S(2)}) %collective-permute-start.24) | collective-permute-done | bytes 69664 | tf_op jit(solution)/shard_map/ppermute | solution.py:466
  111.0 1.6 %collective-permute-start.25 = (f32[72,128]{1,0:T(8,128)S(1)}, f32[72,128]{1,0:T(8,128)S(1)}, u32[]{:S(2)}, u32[]{:S(2)}) collective-permute-start(f32[72,128]{1,0:T(8,128)S(1)} %get-tuple-element.111.sent), channel_id=1, source_target_pairs={{0,16},{1,9},{2,18},{3,11},{4,20},{5,13},{6,22},{7,15},{8,24},{9,1... | collective-permute-start | bytes 110600 | tf_op jit(solution)/shard_map/ppermute | solution.py:466
  112.6 3.3 %collective-permute-done.25.got = f32[72,128]{1,0:T(8,128)S(1)} collective-permute-done((f32[72,128]{1,0:T(8,128)S(1)}, f32[72,128]{1,0:T(8,128)S(1)}, u32[]{:S(2)}, u32[]{:S(2)}) %collective-permute-start.25) | collective-permute-done | bytes 36896 | tf_op jit(solution)/shard_map/ppermute | solution.py:466
  (77 shorter events, 15.0 us)
Async XLA Ops:
  4.0 2.5 %copy-start.8 = (f32[384,256]{1,0:T(8,128)S(1)}, f32[384,256]{1,0:T(8,128)}, u32[]{:S(2)}) copy-start(f32[384,256]{1,0:T(8,128)} %refs_1_.1) | copy-start | bytes 1179652
  5.7 1.5 %copy-start.6 = (f32[384,256]{1,0:T(8,128)S(1)}, f32[384,256]{1,0:T(8,128)}, u32[]{:S(2)}) copy-start(f32[384,256]{1,0:T(8,128)} %refs_0_.1) | copy-start | bytes 1179652
  5.7 1.5 %copy-start.9 = (s32[1,3]{1,0:T(1,128)S(1)}, s32[1,3]{1,0:T(1,128)}, u32[]{:S(2)}) copy-start(s32[1,3]{1,0:T(1,128)} %count.5) | copy-start | bytes 40
  5.7 5.5 %collective-permute-start.1 = (f32[1024,128]{1,0:T(8,128)S(1)}, f32[1024,128]{1,0:T(8,128)S(1)}, u32[]{:S(2)}, u32[]{:S(2)}) collective-permute-start(f32[1024,128]{1,0:T(8,128)S(1)} %get-tuple-element.67), channel_id=1, source_target_pairs={{0,1},{1,0},{2,3},{3,2},{4,5},{5,4},{6,7},{7,6},{8,9},{9,8},{10,11... | collective-permute-start | bytes 1572872 | tf_op jit(solution)/shard_map/ppermute | solution.py:456
  6.4 41.7 %collective-permute-start = (f32[384,1024]{1,0:T(8,128)S(1)}, f32[384,1024]{1,0:T(8,128)S(1)}, u32[]{:S(2)}, u32[]{:S(2)}) collective-permute-start(f32[384,1024]{1,0:T(8,128)S(1)} %widen_pass.1), channel_id=1, source_target_pairs={{0,1},{1,0},{2,3},{3,2},{4,5},{5,4},{6,7},{7,6},{8,9},{9,8},{10,11... | collective-permute-start | bytes 4718600 | tf_op jit(solution)/shard_map/ppermute | solution.py:456
  9.8 1.3 %collective-permute-start.2 = (f32[8,128]{1,0:T(8,128)S(1)}, f32[8,128]{1,0:T(8,128)S(1)}, u32[]{:S(2)}, u32[]{:S(2)}) collective-permute-start(f32[8,128]{1,0:T(8,128)S(1)} %get-tuple-element.68.sent), channel_id=1, source_target_pairs={{0,1},{1,0},{2,3},{3,2},{4,5},{5,4},{6,7},{7,6},{8,9},{9,8},{10,11... | collective-permute-start | bytes 12296 | tf_op jit(solution)/shard_map/ppermute | solution.py:456
  11.2 7.3 %collective-permute-start.3 = (f32[520,128]{1,0:T(8,128)S(1)}, f32[520,128]{1,0:T(8,128)S(1)}, u32[]{:S(2)}, u32[]{:S(2)}) collective-permute-start(f32[520,128]{1,0:T(8,128)S(1)} %get-tuple-element.70.sent), channel_id=1, source_target_pairs={{0,2},{1,5},{2,0},{3,7},{4,6},{5,1},{6,4},{7,3},{8,10},{9,13},{10,... | collective-permute-start | bytes 798728 | tf_op jit(solution)/shard_map/ppermute | solution.py:466
  18.5 5.1 %collective-permute-start.4 = (f32[264,128]{1,0:T(8,128)S(1)}, f32[264,128]{1,0:T(8,128)S(1)}, u32[]{:S(2)}, u32[]{:S(2)}) collective-permute-start(f32[264,128]{1,0:T(8,128)S(1)} %get-tuple-element.72.sent), channel_id=1, source_target_pairs={{0,4},{1,3},{2,6},{3,1},{4,0},{5,7},{6,2},{7,5},{8,12},{9,11},{10,... | collective-permute-start | bytes 405512 | tf_op jit(solution)/shard_map/ppermute | solution.py:466
  23.7 5.5 %collective-permute-start.5 = (f32[264,128]{1,0:T(8,128)S(1)}, f32[264,128]{1,0:T(8,128)S(1)}, u32[]{:S(2)}, u32[]{:S(2)}) collective-permute-start(f32[264,128]{1,0:T(8,128)S(1)} %step_pass.12.held.sent), channel_id=1, source_target_pairs={{0,8},{1,17},{2,10},{3,19},{4,12},{5,21},{6,14},{7,23},{8,0},{9,25... | collective-permute-start | bytes 405512 | tf_op jit(solution)/shard_map/ppermute | solution.py:466
  29.2 18.9 %copy-start.1 = (bf16[384,1024]{1,0:T(8,128)(2,1)S(1)}, bf16[384,1024]{1,0:T(8,128)(2,1)}, u32[]{:S(2)}) copy-start(bf16[384,1024]{1,0:T(8,128)(2,1)} %feats_in.1) | copy-start | bytes 2359300
  29.2 6.0 %collective-permute-start.6 = (f32[264,128]{1,0:T(8,128)S(1)}, f32[264,128]{1,0:T(8,128)S(1)}, u32[]{:S(2)}, u32[]{:S(2)}) collective-permute-start(f32[264,128]{1,0:T(8,128)S(1)} %step_pass.13.held.sent), channel_id=1, source_target_pairs={{0,16},{1,9},{2,18},{3,11},{4,20},{5,13},{6,22},{7,15},{8,24},{9,1... | collective-permute-start | bytes 405512 | tf_op jit(solution)/shard_map/ppermute | solution.py:466
  35.5 13.2 %collective-permute-start.10 = (f32[384,256]{1,0:T(8,128)S(1)}, f32[384,256]{1,0:T(8,128)S(1)}, u32[]{:S(2)}, u32[]{:S(2)}) collective-permute-start(f32[384,256]{1,0:T(8,128)S(1)} %get-tuple-element.85), channel_id=1, source_target_pairs={{0,1},{1,2},{2,3},{3,4},{4,5},{5,6},{6,7},{7,8},{8,9},{9,10},{10,1... | collective-permute-start | bytes 1179656 | tf_op jit(solution)/shard_map/ppermute | solution.py:460
  35.6 10.1 %collective-permute-start.7 = (f32[256,128]{1,0:T(8,128)S(1)}, f32[256,128]{1,0:T(8,128)S(1)}, u32[]{:S(2)}, u32[]{:S(2)}) collective-permute-start(f32[256,128]{1,0:T(8,128)S(1)} %get-tuple-element.74.part.old), channel_id=1, source_target_pairs={{0,4},{1,3},{2,6},{3,1},{4,0},{5,7},{6,2},{7,5},{8,12},{9,11},{10,... | collective-permute-start | bytes 393224 | tf_op jit(solution)/shard_map/ppermute | solution.py:466
  45.7 6.4 %collective-permute-start.8 = (f32[512,128]{1,0:T(8,128)S(1)}, f32[512,128]{1,0:T(8,128)S(1)}, u32[]{:S(2)}, u32[]{:S(2)}) collective-permute-start(f32[512,128]{1,0:T(8,128)S(1)} %gather_pass.2.part), channel_id=1, source_target_pairs={{0,2},{1,5},{2,0},{3,7},{4,6},{5,1},{6,4},{7,3},{8,10},{9,13},{10,... | collective-permute-start | bytes 786440 | tf_op jit(solution)/shard_map/ppermute | solution.py:466
  45.8 5.6 %collective-permute-start.9 = (f32[384,128]{1,0:T(8,128)S(1)}, f32[384,128]{1,0:T(8,128)S(1)}, u32[]{:S(2)}, u32[]{:S(2)}) collective-permute-start(f32[384,128]{1,0:T(8,128)S(1)} %get-tuple-element.83), channel_id=1, source_target_pairs={{0,1},{1,0},{2,3},{3,2},{4,5},{5,4},{6,7},{7,6},{8,9},{9,8},{10,11... | collective-permute-start | bytes 589832 | tf_op jit(solution)/shard_map/ppermute | solution.py:456
  50.9 1.2 %collective-permute-start.11 = (f32[8,128]{1,0:T(8,128)S(1)}, f32[8,128]{1,0:T(8,128)S(1)}, u32[]{:S(2)}, u32[]{:S(2)}) collective-permute-start(f32[8,128]{1,0:T(8,128)S(1)} %get-tuple-element.86.stats), channel_id=1, source_target_pairs={{0,1},{1,0},{2,3},{3,2},{4,5},{5,4},{6,7},{7,6},{8,9},{9,8},{10,11... | collective-permute-start | bytes 12296 | tf_op jit(solution)/shard_map/ppermute | solution.py:456
  53.0 6.5 %collective-permute-start.12 = (f32[520,128]{1,0:T(8,128)S(1)}, f32[520,128]{1,0:T(8,128)S(1)}, u32[]{:S(2)}, u32[]{:S(2)}) collective-permute-start(f32[520,128]{1,0:T(8,128)S(1)} %get-tuple-element.88.sent), channel_id=1, source_target_pairs={{0,2},{1,5},{2,0},{3,7},{4,6},{5,1},{6,4},{7,3},{8,10},{9,13},{10,... | collective-permute-start | bytes 798728 | tf_op jit(solution)/shard_map/ppermute | solution.py:466
  59.5 5.5 %collective-permute-start.13 = (f32[264,128]{1,0:T(8,128)S(1)}, f32[264,128]{1,0:T(8,128)S(1)}, u32[]{:S(2)}, u32[]{:S(2)}) collective-permute-start(f32[264,128]{1,0:T(8,128)S(1)} %get-tuple-element.90.sent), channel_id=1, source_target_pairs={{0,4},{1,3},{2,6},{3,1},{4,0},{5,7},{6,2},{7,5},{8,12},{9,11},{10,... | collective-permute-start | bytes 405512 | tf_op jit(solution)/shard_map/ppermute | solution.py:466
  65.0 5.6 %collective-permute-start.14 = (f32[264,128]{1,0:T(8,128)S(1)}, f32[264,128]{1,0:T(8,128)S(1)}, u32[]{:S(2)}, u32[]{:S(2)}) collective-permute-start(f32[264,128]{1,0:T(8,128)S(1)} %step_pass.15.held.sent), channel_id=1, source_target_pairs={{0,8},{1,17},{2,10},{3,19},{4,12},{5,21},{6,14},{7,23},{8,0},{9,25... | collective-permute-start | bytes 405512 | tf_op jit(solution)/shard_map/ppermute | solution.py:466
  66.0 12.2 %collective-permute-start.18 = (f32[384,128]{1,0:T(8,128)S(1)}, f32[384,128]{1,0:T(8,128)S(1)}, u32[]{:S(2)}, u32[]{:S(2)}) collective-permute-start(f32[384,128]{1,0:T(8,128)S(1)} %get-tuple-element.96), channel_id=1, source_target_pairs={{0,1},{1,0},{2,3},{3,2},{4,5},{5,4},{6,7},{7,6},{8,9},{9,8},{10,11... | collective-permute-start | bytes 589832 | tf_op jit(solution)/shard_map/ppermute | solution.py:456
  70.7 7.4 %collective-permute-start.15 = (f32[264,128]{1,0:T(8,128)S(1)}, f32[264,128]{1,0:T(8,128)S(1)}, u32[]{:S(2)}, u32[]{:S(2)}) collective-permute-start(f32[264,128]{1,0:T(8,128)S(1)} %step_pass.16.held.sent), channel_id=1, source_target_pairs={{0,16},{1,9},{2,18},{3,11},{4,20},{5,13},{6,22},{7,15},{8,24},{9,1... | collective-permute-start | bytes 405512 | tf_op jit(solution)/shard_map/ppermute | solution.py:466
  78.4 10.8 %collective-permute-start.20 = (f32[384,256]{1,0:T(8,128)S(1)}, f32[384,256]{1,0:T(8,128)S(1)}, u32[]{:S(2)}, u32[]{:S(2)}) collective-permute-start(f32[384,256]{1,0:T(8,128)S(1)} %get-tuple-element.102), channel_id=1, source_target_pairs={{0,1},{1,2},{2,3},{3,4},{4,5},{5,6},{6,7},{7,8},{8,9},{9,10},{10,1... | collective-permute-start | bytes 1179656 | tf_op jit(solution)/shard_map/ppermute | solution.py:460
  78.5 8.3 %collective-permute-start.16 = (f32[256,128]{1,0:T(8,128)S(1)}, f32[256,128]{1,0:T(8,128)S(1)}, u32[]{:S(2)}, u32[]{:S(2)}) collective-permute-start(f32[256,128]{1,0:T(8,128)S(1)} %get-tuple-element.91.part), channel_id=1, source_target_pairs={{0,4},{1,3},{2,6},{3,1},{4,0},{5,7},{6,2},{7,5},{8,12},{9,11},{10,... | collective-permute-start | bytes 393224 | tf_op jit(solution)/shard_map/ppermute | solution.py:466
  86.8 6.4 %collective-permute-start.17 = (f32[512,128]{1,0:T(8,128)S(1)}, f32[512,128]{1,0:T(8,128)S(1)}, u32[]{:S(2)}, u32[]{:S(2)}) collective-permute-start(f32[512,128]{1,0:T(8,128)S(1)} %gather_pass.3.part), channel_id=1, source_target_pairs={{0,2},{1,5},{2,0},{3,7},{4,6},{5,1},{6,4},{7,3},{8,10},{9,13},{10,... | collective-permute-start | bytes 786440 | tf_op jit(solution)/shard_map/ppermute | solution.py:466
  86.9 5.1 %collective-permute-start.19 = (f32[384,128]{1,0:T(8,128)S(1)}, f32[384,128]{1,0:T(8,128)S(1)}, u32[]{:S(2)}, u32[]{:S(2)}) collective-permute-start(f32[384,128]{1,0:T(8,128)S(1)} %get-tuple-element.100), channel_id=1, source_target_pairs={{0,1},{1,0},{2,3},{3,2},{4,5},{5,4},{6,7},{7,6},{8,9},{9,8},{10,11... | collective-permute-start | bytes 589832 | tf_op jit(solution)/shard_map/ppermute | solution.py:456
  91.5 1.7 %collective-permute-start.21 = (f32[8,128]{1,0:T(8,128)S(1)}, f32[8,128]{1,0:T(8,128)S(1)}, u32[]{:S(2)}, u32[]{:S(2)}) collective-permute-start(f32[8,128]{1,0:T(8,128)S(1)} %get-tuple-element.103.stats), channel_id=1, source_target_pairs={{0,1},{1,0},{2,3},{3,2},{4,5},{5,4},{6,7},{7,6},{8,9},{9,8},{10,11... | collective-permute-start | bytes 12296 | tf_op jit(solution)/shard_map/ppermute | solution.py:456
  94.5 6.5 %collective-permute-start.22 = (f32[520,128]{1,0:T(8,128)S(1)}, f32[520,128]{1,0:T(8,128)S(1)}, u32[]{:S(2)}, u32[]{:S(2)}) collective-permute-start(f32[520,128]{1,0:T(8,128)S(1)} %get-tuple-element.105.sent), channel_id=1, source_target_pairs={{0,2},{1,5},{2,0},{3,7},{4,6},{5,1},{6,4},{7,3},{8,10},{9,13},{10,... | collective-permute-start | bytes 798728 | tf_op jit(solution)/shard_map/ppermute | solution.py:466
  101.0 5.5 %collective-permute-start.23 = (f32[264,128]{1,0:T(8,128)S(1)}, f32[264,128]{1,0:T(8,128)S(1)}, u32[]{:S(2)}, u32[]{:S(2)}) collective-permute-start(f32[264,128]{1,0:T(8,128)S(1)} %get-tuple-element.107.sent), channel_id=1, source_target_pairs={{0,4},{1,3},{2,6},{3,1},{4,0},{5,7},{6,2},{7,5},{8,12},{9,11},{10,... | collective-permute-start | bytes 405512 | tf_op jit(solution)/shard_map/ppermute | solution.py:466
  103.6 12.4 %collective-permute-start.26 = (f32[384,128]{1,0:T(8,128)S(1)}, f32[384,128]{1,0:T(8,128)S(1)}, u32[]{:S(2)}, u32[]{:S(2)}) collective-permute-start(f32[384,128]{1,0:T(8,128)S(1)} %get-tuple-element.117), channel_id=1, source_target_pairs={{0,1},{1,0},{2,3},{3,2},{4,5},{5,4},{6,7},{7,6},{8,9},{9,8},{10,11... | collective-permute-start | bytes 589832 | tf_op jit(solution)/shard_map/ppermute | solution.py:456
  106.6 4.4 %collective-permute-start.24 = (f32[136,128]{1,0:T(8,128)S(1)}, f32[136,128]{1,0:T(8,128)S(1)}, u32[]{:S(2)}, u32[]{:S(2)}) collective-permute-start(f32[136,128]{1,0:T(8,128)S(1)} %get-tuple-element.109.sent), channel_id=1, source_target_pairs={{0,8},{1,17},{2,10},{3,19},{4,12},{5,21},{6,14},{7,23},{8,0},{9,25... | collective-permute-start | bytes 208904 | tf_op jit(solution)/shard_map/ppermute | solution.py:466
  111.0 4.9 %collective-permute-start.25 = (f32[72,128]{1,0:T(8,128)S(1)}, f32[72,128]{1,0:T(8,128)S(1)}, u32[]{:S(2)}, u32[]{:S(2)}) collective-permute-start(f32[72,128]{1,0:T(8,128)S(1)} %get-tuple-element.111.sent), channel_id=1, source_target_pairs={{0,16},{1,9},{2,18},{3,11},{4,20},{5,13},{6,22},{7,15},{8,24},{9,1... | collective-permute-start | bytes 110600 | tf_op jit(solution)/shard_map/ppermute | solution.py:466
  115.9 1.2 %collective-permute-start.27 = (f32[32,128]{1,0:T(8,128)S(1)}, f32[32,128]{1,0:T(8,128)S(1)}, u32[]{:S(2)}, u32[]{:S(2)}) collective-permute-start(f32[32,128]{1,0:T(8,128)S(1)} %get-tuple-element.124), channel_id=1, source_target_pairs={{0,1},{1,0},{2,3},{3,2},{4,5},{5,4},{6,7},{7,6},{8,9},{9,8},{10,11... | collective-permute-start | bytes 49160 | tf_op jit(solution)/shard_map/ppermute | solution.py:456
  (7 other events, 8.0 us)

commit v11 on v10

--- a/solution.py
+++ b/solution.py
@@ -16,12 +16,12 @@
 
 CORES = 2
 RIDERS = 8
+ITEM_PARTS = 2
 NN = (((1,), (0,)), ((), ()))
 NT = (((1,), (1,)), ((), ()))
 TN = (((0,), (0,)), ((), ()))
 VMEM = pl.BlockSpec(memory_space=pltpu.VMEM)
 SMEM = pl.BlockSpec(memory_space=pltpu.SMEM)
-HBM = pl.BlockSpec(memory_space=pltpu.HBM)
 ANY = pl.BlockSpec(memory_space=pl.ANY)
 PARAMS = pltpu.CompilerParams(vmem_limit_bytes=8 << 20)
 f32 = jnp.float32
@@ -62,135 +62,104 @@
     return (1.0 + stats[1:2, :] / 2.0) / (1.0 + stats[0:1, :] / 2.0)
 
 
-def tile_kernel(stratum, noise_scale, codes, count, ratings, user_noise, item_noise, *refs):
-    users_in, items_in, base_u, grad_u, base_v, grad_v, stats = refs[:7]
-    tiles, noise_u, noise_v, pred, err_b, sems = refs[7:13]
-    rows = err_b.shape[0]
-    tile = tiles.shape[-1]
-    grid = rows // tile
-    moves = [
-        (ratings.at[0, stratum], tiles),
-        (user_noise.at[stratum], noise_u),
-        (item_noise.at[stratum], noise_v),
-    ]
-    users, items = users_in, items_in
-    if stratum == 0:
-        users, items = refs[13:]
-        moves += [(users_in, users), (items_in, items)]
-    copies = [
-        pltpu.make_async_copy(source, target, sems.at[n]) for n, (source, target) in enumerate(moves)
-    ]
-    for copy in copies[::-1]:
-        copy.start()
-    for copy in copies[3:]:
-        copy.wait()
+def error_kernel(stratum, codes, count, ratings, users, *refs):
+    items, (err_b, stats, pred) = refs[:-3], refs[-3:]
+    tile = ratings.shape[-1]
+    grid = users.shape[0] // tile
     user_b = users[...].astype(bf16)
-    item_b = items[...].astype(bf16)
-    pred[...] = dot(user_b, item_b, NT)
+    start = 0
+    for part in items:
+        pred[:, start : start + part.shape[0]] = dot(user_b, part[...].astype(bf16), NT)
+        start += part.shape[0]
     err_b[...] = jnp.zeros_like(err_b)
     live_slots = count[0, stratum]
     sse = jnp.zeros((tile, tile), f32)
-    copies[0].wait()
-    for slot in range(tiles.shape[0]):
+    for slot in range(ratings.shape[2]):
         code = codes[0, stratum, slot]
         at_rows = rows_at(code // grid, tile)
         at_cols = rows_at(code % grid, tile)
         live = (slot < live_slots).astype(f32)
-        err = (tiles[slot].astype(f32) - pred[at_rows, at_cols]) * live
+        err = (ratings[0, stratum, slot].astype(f32) - pred[at_rows, at_cols]) * live
         sse = sse + err * err
         err_b[at_rows, at_cols] = err.astype(bf16)
-    err_all = err_b[...]
     total = jnp.sum(sse)
     counted = live_slots.astype(f32) * float(tile * tile)
     row = lax.broadcasted_iota(jnp.int32, stats.shape, 0)
     stats[...] = jnp.where(row == 0, total, jnp.where(row == 1, counted, 0.0))
-    grad_u[...] = step_size * dot(err_all, item_b)
-    grad_v[...] = step_size * dot(err_all, user_b, TN)
-    copies[1].wait()
-    base_u[...] = (1.0 - step_size * prior_prec) * users[...] + noise_scale * noise_u[...].astype(
-        f32
-    )
-    copies[2].wait()
-    base_v[...] = (1.0 - step_size * item_prec) * items[...] + noise_scale * noise_v[...].astype(f32)
-
-
-def tile_pass(stratum, codes, count, ratings, user_noise, item_noise, users, items):
-    slots, tile = ratings.shape[2:4]
+
+
+def error_pass(stratum, codes, count, ratings, users, *items):
     rows, rank = users.shape
-    first = stratum == 0
-    return pl.pallas_call(
-        functools.partial(tile_kernel, stratum, math.sqrt(2.0 * step_size)),
-        out_shape=(shape(rows, rank),) * 4 + (shape(RIDERS, rank // CORES),),
-        in_specs=[SMEM] * 2 + [HBM] * 3 + [HBM if first else VMEM] * 2,
-        out_specs=(VMEM,) * 5,
-        scratch_shapes=[
-            pltpu.VMEM((slots, tile, tile), bf16),
-            pltpu.VMEM((rows, rank), bf16),
-            pltpu.VMEM((rows, rank), bf16),
-            pltpu.VMEM((rows, rows), f32),
-            pltpu.VMEM((rows, rows), bf16),
-            pltpu.SemaphoreType.DMA((5,)),
-        ]
-        + [pltpu.VMEM((rows, rank), f32)] * (2 if first else 0),
-        compiler_params=PARAMS,
-        cost_estimate=cost(6 * rows * rows * rank, 16 * rows * rank),
-        name="tile_pass",
-    )(codes, count, ratings, user_noise, item_noise, users, items)
-
-
-def first_kernel(devices, feats_in, weights_in, users_in, own_mean, other_mean, send, keep, old, mean, feats, weights, users, sems):
-    copies = [
-        pltpu.make_async_copy(source, target, sems.at[n])
-        for n, (source, target) in enumerate(
-            [(weights_in, weights), (feats_in, feats), (users_in, users)]
-        )
-    ]
-    for copy in copies:
-        copy.start()
+    return pl.pallas_call(
+        functools.partial(error_kernel, stratum),
+        out_shape=(shape(rows, rows, dtype=bf16), shape(RIDERS, rank // CORES)),
+        in_specs=[SMEM] * 2 + [VMEM] * (2 + len(items)),
+        out_specs=(VMEM,) * 2,
+        scratch_shapes=[pltpu.VMEM((rows, rows), f32)],
+        compiler_params=PARAMS,
+        cost_estimate=cost(24 * rows * rows * rank, 64 * rows * rank),
+        name="error_pass",
+    )(codes, count, ratings, users, *items)
+
+
+def grad_kernel(stratum, noise_scale, err_b, user_noise, item_noise, users, *refs):
+    items, (base_u, grad_u, base_v, grad_v) = refs[:-4], refs[-4:]
+    item_b = jnp.concatenate([part[...].astype(bf16) for part in items], 0)
+    grad_u[...] = step_size * dot(err_b[...], item_b)
+    grad_v[...] = step_size * dot(err_b[...], users[...].astype(bf16), TN)
+    noise = noise_scale * user_noise[stratum].astype(f32)
+    base_u[...] = (1.0 - step_size * prior_prec) * users[...] + noise
+    start = 0
+    for part in items:
+        at = slice(start, start + part.shape[0])
+        noise = noise_scale * item_noise[stratum, at].astype(f32)
+        base_v[at, :] = (1.0 - step_size * item_prec) * part[...] + noise
+        start += part.shape[0]
+
+
+def grad_pass(stratum, err_b, user_noise, item_noise, users, *items):
+    rows, rank = users.shape
+    return pl.pallas_call(
+        functools.partial(grad_kernel, stratum, math.sqrt(2.0 * step_size)),
+        out_shape=(shape(rows, rank),) * 4,
+        in_specs=[VMEM] * (4 + len(items)),
+        out_specs=(VMEM,) * 4,
+        compiler_params=PARAMS,
+        cost_estimate=cost(4 * rows * rows * rank, 28 * rows * rank),
+        name="grad_pass",
+    )(err_b, user_noise, item_noise, users, *items)
+
+
+def first_kernel(devices, feats, weights, users, later, own_mean, other_mean, send, keep, old, mean):
     place = where_am_i(devices)
     here = place[0]
-    copies[0].wait()
-    weights_b = weights[...].astype(bf16)
-    copies[1].wait()
-    mean[...] = dot(feats[...], weights_b)
-    copies[2].wait()
+    mean[...] = dot(feats[...], weights[...].astype(bf16))
     for grad, means, which in ((send, other_mean, 1 - here), (keep, own_mean, here)):
         mean_now = half_of(mean, which)
         means[...] = mean_now
         offset = (half_of(users, which) - mean_now).astype(bf16)
         grad[...] = dot(feats[...], offset, TN)
     rows, width = old.shape
-    start = place[1] * (weights.shape[0] // 2) + place[2] * rows
-    cols = pl.ds(pl.multiple_of(here * width, width), width)
-    old[...] = weights[pl.ds(pl.multiple_of(start, rows), rows), cols]
-
-
-def first_pass(devices, feats, weights, users):
+    old[...] = weights[rows_at(2 * place[1] + place[2], rows), rows_at(here, width)]
+
+
+def first_pass(devices, feats, weights, users, later):
     rows, rank = users.shape
     feat = weights.shape[0]
     width = rank // CORES
     return pl.pallas_call(
         functools.partial(first_kernel, devices),
         out_shape=(shape(rows, width),) * 2 + (shape(feat, width),) * 2 + (shape(feat // 4, width),),
-        in_specs=[HBM] * 3,
+        in_specs=[VMEM] * 3 + [ANY],
         out_specs=(VMEM,) * 5,
-        scratch_shapes=[
-            pltpu.VMEM(users.shape, f32),
-            pltpu.VMEM(feats.shape, bf16),
-            pltpu.VMEM(weights.shape, f32),
-            pltpu.VMEM(users.shape, f32),
-            pltpu.SemaphoreType.DMA((3,)),
-        ],
+        scratch_shapes=[pltpu.VMEM(users.shape, f32)],
         compiler_params=PARAMS,
         cost_estimate=cost(4 * rows * feat * rank, 8 * feat * rank),
         name="first_pass",
-    )(feats, weights, users)
-
-
-def widen_kernel(narrow_in, wide, narrow, sem):
-    copy = pltpu.make_async_copy(narrow_in, narrow, sem.at[0])
-    copy.start()
-    copy.wait()
+    )(feats, weights, users, later)
+
+
+def widen_kernel(narrow, wide):
     wide[...] = narrow[...].astype(f32)
 
 
@@ -198,9 +167,8 @@
     return pl.pallas_call(
         widen_kernel,
         out_shape=shape(*narrow.shape),
-        in_specs=[HBM],
+        in_specs=[VMEM],
         out_specs=VMEM,
-        scratch_shapes=[pltpu.VMEM(narrow.shape, bf16), pltpu.SemaphoreType.DMA((1,))],
         compiler_params=PARAMS,
         name="widen_pass",
     )(narrow)
@@ -417,24 +385,33 @@
     )(mine, other)
 
 
-def renew_kernel(devices, stats, base_u, grad_u, own_mean, other_mean, base_v, grad_v, users, items, *cols):
+def renew_kernel(devices, stats, base_u, grad_u, own_mean, other_mean, base_v, grad_v, users, *outs):
     core = where_am_i(devices)[0]
     width = own_mean.shape[1]
     precision = precision_of(stats[...])
     precision = jnp.concatenate([precision] * CORES, 1)
-    items[...] = base_v[...] + precision * grad_v[...]
+    parts = 1 if len(outs) == 1 else ITEM_PARTS
+    rows = base_v.shape[0] // parts
+    for n, items in enumerate(outs[:parts]):
+        at = slice(n * rows, (n + 1) * rows)
+        items[...] = base_v[at, :] + precision * grad_v[at, :]
     new = base_u[...] + precision * grad_u[...]
     pull = step_size * prior_prec
     left = jnp.where(core == 0, own_mean[...], other_mean[...])
     right = jnp.where(core == 0, other_mean[...], own_mean[...])
     users[:, :width] = new[:, :width] + pull * left
     users[:, width:] = new[:, width:] + pull * right
-    for ref, which in zip(cols, (core, 1 - core), strict=False):
+    for ref, which in zip(outs[parts:], (core, 1 - core), strict=False):
         ref[...] = half_of(users, which)
 
 
 def renew_pass(devices, last, stats, base_u, grad_u, own_mean, *state):
-    outs = [shape(*base_u.shape)] * 2 + ([] if last else [shape(*own_mean.shape)] * 2)
+    rows, rank = base_u.shape
+    outs = [shape(rows, rank)]
+    if last:
+        outs.append(shape(rows, rank))
+    else:
+        outs += [shape(rows // ITEM_PARTS, rank)] * ITEM_PARTS + [shape(*own_mean.shape)] * 2
     return pl.pallas_call(
         functools.partial(renew_kernel, devices),
         out_shape=tuple(outs),
@@ -496,40 +473,45 @@
     strata = ratings.shape[1]
     feat = prior_weights.shape[0]
     rate = rate_scale / (user_factors.shape[0] * devices)
-    tables = (tile_index, tile_count, ratings, user_noise, item_noise)
-
+    def errors_of(stratum, users, *items):
+        err_b, stats = error_pass(stratum, tile_index, tile_count, ratings, users, *items)
+        return err_b, stats, swap(stats, devices)
+
+    wide = widen_pass(side_features)
     own_mean, other_mean, send, held, old = first_pass(
-        devices, side_features, prior_weights, user_factors
+        devices, side_features, prior_weights, user_factors, wide
     )
     got = swap(send, devices)
-    *state, stats = tile_pass(0, *tables, user_factors, item_factors)
-    more = swap(stats, devices)
+    users, items = user_factors, [item_factors]
+    err_b, stats, more = errors_of(0, users, *items)
     send, held = step_pass(True, 0, devices, held, got, stats, more, feat)
-    feats, turned = join_pass(side_features, swap(widen_pass(side_features), devices))
+    feats, turned = join_pass(side_features, swap(wide, devices))
     for stratum in range(strata):
         last = stratum + 1 == strata
+        state = grad_pass(stratum, err_b, user_noise, item_noise, users, *items)
         for stage in range(stages - 1):
             got = exchange(send, devices, stage)
             rows = got.shape[0] - RIDERS
+            later = state[:1] if stage == 0 else ()
             if last or stage < 1:
-                send, held = step_pass(True, stage + 1, devices, held, got, send, got, rows)
+                send, held = step_pass(True, stage + 1, devices, held, got, send, got, rows, later)
             else:
                 (send,) = step_pass(False, 0, devices, held, got, send, got, rows)
                 held = send
         got = exchange(send, devices, stages - 1)
         part, stats = update_pass(rate, held, got, send, old)
-        users, items, *cols = renew_pass(
+        users, *items = renew_pass(
             devices, last, stats, *state[:2], own_mean, other_mean, *state[2:]
         )
         if last:
             break
         old = part
-        items = roll(items, devices)
-        own_cols, other_cols = cols[0], swap(cols[1], devices)
+        *items, own_cols, other_cols = items
+        items = [roll(part, devices) for part in items]
+        other_cols = swap(other_cols, devices)
         part = gather_pass(1, devices, part, exchange(part, devices, 1))
         got = exchange(part, devices, 0)
-        *state, stats = tile_pass(stratum + 1, *tables, users, items)
-        more = swap(stats, devices)
+        err_b, stats, more = errors_of(stratum + 1, users, *items)
         begun = part_pass(devices, feats, part)
         own_mean, other_mean, send, held, *olds = prior_pass(
             devices,
@@ -548,7 +530,7 @@
             (old,) = olds
         other_mean = swap(other_mean, devices)
     mine, other = split_pass(devices, part)
-    return (users, items, across_pass(devices, mine, swap(other, devices)))
+    return (users, *items, across_pass(devices, mine, swap(other, devices)))
 
 
 def solution(mesh):

time: 118 us -> 119 us (level)
  waiting for transfers between devices: 67.4 us -> 70.6 us
  Pallas kernels: 14.8 us -> 12 us
  starting transfers between devices: 30.6 us -> 33.2 us
  local copies, waits for them, and re-layouts: 4.04 us -> 2.4 us
    ppermute x2 -> x4, waiting for transfers between devices: 0.86 us -> 6.57 us  [roll(): lax.ppermute(array, 'user', [(i, (i + 1) % devices) for i in range(device...]
    ppermute x16, waiting for transfers between devices: 65.5 us -> 60.8 us  [exchange(): return lax.ppermute(array, 'user', pairs)]
    ppermute x16, starting transfers between devices: 25.3 us -> 29.9 us  [exchange(): return lax.ppermute(array, 'user', pairs)]
    ppermute x10, starting transfers between devices: 5.17 us -> 1.46 us  [swap(): return lax.ppermute(array, 'user', [(i, i ^ 1) for i in range(devices)])]
    pallas_call x4 -> x7, Pallas kernels: 7.3 us -> 4.94 us  [the longest x3 3.32 us: error_pass(): pl.pallas_call(functools.partial(error_kernel, stratum), out_shape=(shape...]
    ppermute x10, waiting for transfers between devices: 1.04 us -> 3.22 us  [swap(): return lax.ppermute(array, 'user', [(i, i ^ 1) for i in range(devices)])]
    ppermute x2 -> x4, starting transfers between devices: 0.12 us -> 1.77 us  [roll(): lax.ppermute(array, 'user', [(i, (i + 1) % devices) for i in range(device...]
    unnamed x23 -> x21, local copies, waits for them, and re-layouts: 4.04 us -> 2.4 us
  transfers between devices with their start and end apart: 28 -> 30, of which waited for: 19 -> 24; matrix products, arithmetic and copies ran while one was open for 0% -> 0% of each run, Pallas kernels for 9% -> 7%
where the time goes in v11:
time: 119 us
  waiting for transfers between devices  70.6 us (59%)
  starting transfers between devices  33.2 us (28%)
  Pallas kernels  12 us (10%)
  local copies, waits for them, and re-layouts  2.4 us (2%)
    ppermute x16, waiting for transfers between devices, exchange(): return lax.ppermute(array, 'user', pairs)  60.8 us
    ppermute x16, starting transfers between devices, exchange(): return lax.ppermute(array, 'user', pairs)  29.9 us
    ppermute x4, waiting for transfers between devices, roll(): lax.ppermute(array, 'user', [(i, (i + 1) % devices) for i in range(device...  6.57 us
    pallas_call x3, Pallas kernels, error_pass(): pl.pallas_call(functools.partial(error_kernel, stratum), out_shape=(shape...  3.32 us
    ppermute x10, waiting for transfers between devices, swap(): return lax.ppermute(array, 'user', [(i, i ^ 1) for i in range(devices)])  3.22 us
    unnamed x21, local copies, waits for them, and re-layouts  2.4 us
  transfers between devices with their start and end apart: 30, of which 24 were waited for; matrix products, arithmetic and copies ran while one was open for 0% of the time, Pallas kernels for 7%

profile of v11, /device:TPU:0, one launch (start us, length us, event | category | flops | bytes accessed | tf_op | source)
XLA Modules:
  0.0 119.1 jit_solution(5529672952404114122)
XLA Ops:
  3.1 1.2 %first_pass.1 = (f32[384,128]{1,0:T(8,128)S(1)}, f32[384,128]{1,0:T(8,128)S(1)}, f32[1024,128]{1,0:T(8,128)S(1)}, f32[1024,128]{1,0:T(8,128)S(1)}, f32[256,128]{1,0:T(8,128)S(1)}) custom-call(bf16[384,1024]{1,0:T(8,128)(2,1)S(1)} %copy-done, f32[1024,256]{1,0:T(8,128)S(1)} %copy-done.5, f32[384,256]{1,0:T(8,128)S(1)} %copy-done.4, ...), custom_call_target="tpu_custom_call" | custom-call | flops 402653184 | bytes 2097152 | tf_op jit(solution)/shard_map/first_pass/pallas_call | solution.py:150
  6.6 2.1 %collective-permute-done.2.more = f32[8,128]{1,0:T(8,128)S(1)} collective-permute-done((f32[8,128]{1,0:T(8,128)S(1)}, f32[8,128]{1,0:T(8,128)S(1)}, u32[]{:S(2)}, u32[]{:S(2)}) %collective-permute-start.2) | collective-permute-done | bytes 4128 | tf_op jit(solution)/shard_map/ppermute | solution.py:433
  8.8 2.9 %collective-permute-start.3 = (f32[520,128]{1,0:T(8,128)S(1)}, f32[520,128]{1,0:T(8,128)S(1)}, u32[]{:S(2)}, u32[]{:S(2)}) collective-permute-start(f32[520,128]{1,0:T(8,128)S(1)} %get-tuple-element.75.sent), channel_id=1, source_target_pairs={{0,2},{1,5},{2,0},{3,7},{4,6},{5,1},{6,4},{7,3},{8,10},{9,13},{10,... | collective-permute-start | bytes 798728 | tf_op jit(solution)/shard_map/ppermute | solution.py:443
  12.2 3.9 %collective-permute-done.3.got.more = f32[520,128]{1,0:T(8,128)S(1)} collective-permute-done((f32[520,128]{1,0:T(8,128)S(1)}, f32[520,128]{1,0:T(8,128)S(1)}, u32[]{:S(2)}, u32[]{:S(2)}) %collective-permute-start.3) | collective-permute-done | bytes 266272 | tf_op jit(solution)/shard_map/ppermute | solution.py:443
  16.1 2.1 %collective-permute-start.4 = (f32[264,128]{1,0:T(8,128)S(1)}, f32[264,128]{1,0:T(8,128)S(1)}, u32[]{:S(2)}, u32[]{:S(2)}) collective-permute-start(f32[264,128]{1,0:T(8,128)S(1)} %get-tuple-element.79.sent), channel_id=1, source_target_pairs={{0,4},{1,3},{2,6},{3,1},{4,0},{5,7},{6,2},{7,5},{8,12},{9,11},{10,... | collective-permute-start | bytes 405512 | tf_op jit(solution)/shard_map/ppermute | solution.py:443
  18.2 3.0 %collective-permute-done.4.got.more = f32[264,128]{1,0:T(8,128)S(1)} collective-permute-done((f32[264,128]{1,0:T(8,128)S(1)}, f32[264,128]{1,0:T(8,128)S(1)}, u32[]{:S(2)}, u32[]{:S(2)}) %collective-permute-start.4) | collective-permute-done | bytes 135200 | tf_op jit(solution)/shard_map/ppermute | solution.py:443
  21.2 2.1 %collective-permute-start.5 = (f32[264,128]{1,0:T(8,128)S(1)}, f32[264,128]{1,0:T(8,128)S(1)}, u32[]{:S(2)}, u32[]{:S(2)}) collective-permute-start(f32[264,128]{1,0:T(8,128)S(1)} %step_pass.12.held.sent), channel_id=1, source_target_pairs={{0,8},{1,17},{2,10},{3,19},{4,12},{5,21},{6,14},{7,23},{8,0},{9,25... | collective-permute-start | bytes 405512 | tf_op jit(solution)/shard_map/ppermute | solution.py:443
  23.4 3.4 %collective-permute-done.5.got.more = f32[264,128]{1,0:T(8,128)S(1)} collective-permute-done((f32[264,128]{1,0:T(8,128)S(1)}, f32[264,128]{1,0:T(8,128)S(1)}, u32[]{:S(2)}, u32[]{:S(2)}) %collective-permute-start.5) | collective-permute-done | bytes 135200 | tf_op jit(solution)/shard_map/ppermute | solution.py:443
  26.8 2.7 %collective-permute-start.6 = (f32[264,128]{1,0:T(8,128)S(1)}, f32[264,128]{1,0:T(8,128)S(1)}, u32[]{:S(2)}, u32[]{:S(2)}) collective-permute-start(f32[264,128]{1,0:T(8,128)S(1)} %step_pass.13.held.sent), channel_id=1, source_target_pairs={{0,16},{1,9},{2,18},{3,11},{4,20},{5,13},{6,22},{7,15},{8,24},{9,1... | collective-permute-start | bytes 405512 | tf_op jit(solution)/shard_map/ppermute | solution.py:443
  29.5 3.3 %collective-permute-done.6.got = f32[264,128]{1,0:T(8,128)S(1)} collective-permute-done((f32[264,128]{1,0:T(8,128)S(1)}, f32[264,128]{1,0:T(8,128)S(1)}, u32[]{:S(2)}, u32[]{:S(2)}) %collective-permute-start.6) | collective-permute-done | bytes 135200 | tf_op jit(solution)/shard_map/ppermute | solution.py:443
  32.8 3.4 %collective-permute-start.7 = (f32[256,128]{1,0:T(8,128)S(1)}, f32[256,128]{1,0:T(8,128)S(1)}, u32[]{:S(2)}, u32[]{:S(2)}) collective-permute-start(f32[256,128]{1,0:T(8,128)S(1)} %get-tuple-element.81.part.old), channel_id=1, source_target_pairs={{0,4},{1,3},{2,6},{3,1},{4,0},{5,7},{6,2},{7,5},{8,12},{9,11},{10,... | collective-permute-start | bytes 393224 | tf_op jit(solution)/shard_map/ppermute | solution.py:443
  36.5 1.6 %collective-permute-start.11 = (f32[192,256]{1,0:T(8,128)S(1)}, f32[192,256]{1,0:T(8,128)S(1)}, u32[]{:S(2)}, u32[]{:S(2)}) collective-permute-start(f32[192,256]{1,0:T(8,128)S(1)} %get-tuple-element.92), channel_id=1, source_target_pairs={{0,1},{1,2},{2,3},{3,4},{4,5},{5,6},{6,7},{7,8},{8,9},{9,10},{10,1... | collective-permute-start | bytes 589832 | tf_op jit(solution)/shard_map/ppermute | solution.py:437
  38.1 5.4 %collective-permute-done.7.got = f32[256,128]{1,0:T(8,128)S(1)} collective-permute-done((f32[256,128]{1,0:T(8,128)S(1)}, f32[256,128]{1,0:T(8,128)S(1)}, u32[]{:S(2)}, u32[]{:S(2)}) %collective-permute-start.7) | collective-permute-done | bytes 131104 | tf_op jit(solution)/shard_map/ppermute | solution.py:443
  43.7 1.6 %collective-permute-done.10.refs_0_ = f32[192,256]{1,0:T(8,128)S(1)} collective-permute-done((f32[192,256]{1,0:T(8,128)S(1)}, f32[192,256]{1,0:T(8,128)S(1)}, u32[]{:S(2)}, u32[]{:S(2)}) %collective-permute-start.10) | collective-permute-done | bytes 196640 | tf_op jit(solution)/shard_map/ppermute | solution.py:437
  45.3 2.1 %collective-permute-done.11.refs_1_ = f32[192,256]{1,0:T(8,128)S(1)} collective-permute-done((f32[192,256]{1,0:T(8,128)S(1)}, f32[192,256]{1,0:T(8,128)S(1)}, u32[]{:S(2)}, u32[]{:S(2)}) %collective-permute-start.11) | collective-permute-done | bytes 196640 | tf_op jit(solution)/shard_map/ppermute | solution.py:437
  51.4 5.9 %collective-permute-done.13.got.more = f32[520,128]{1,0:T(8,128)S(1)} collective-permute-done((f32[520,128]{1,0:T(8,128)S(1)}, f32[520,128]{1,0:T(8,128)S(1)}, u32[]{:S(2)}, u32[]{:S(2)}) %collective-permute-start.13) | collective-permute-done | bytes 266272 | tf_op jit(solution)/shard_map/ppermute | solution.py:443
  57.3 3.0 %collective-permute-start.14 = (f32[264,128]{1,0:T(8,128)S(1)}, f32[264,128]{1,0:T(8,128)S(1)}, u32[]{:S(2)}, u32[]{:S(2)}) collective-permute-start(f32[264,128]{1,0:T(8,128)S(1)} %get-tuple-element.99.sent), channel_id=1, source_target_pairs={{0,4},{1,3},{2,6},{3,1},{4,0},{5,7},{6,2},{7,5},{8,12},{9,11},{10,... | collective-permute-start | bytes 405512 | tf_op jit(solution)/shard_map/ppermute | solution.py:443
  60.3 3.0 %collective-permute-done.14.got.more = f32[264,128]{1,0:T(8,128)S(1)} collective-permute-done((f32[264,128]{1,0:T(8,128)S(1)}, f32[264,128]{1,0:T(8,128)S(1)}, u32[]{:S(2)}, u32[]{:S(2)}) %collective-permute-start.14) | collective-permute-done | bytes 135200 | tf_op jit(solution)/shard_map/ppermute | solution.py:443
  64.2 4.4 %collective-permute-done.15.got.more = f32[264,128]{1,0:T(8,128)S(1)} collective-permute-done((f32[264,128]{1,0:T(8,128)S(1)}, f32[264,128]{1,0:T(8,128)S(1)}, u32[]{:S(2)}, u32[]{:S(2)}) %collective-permute-start.15) | collective-permute-done | bytes 135200 | tf_op jit(solution)/shard_map/ppermute | solution.py:443
  68.7 2.9 %collective-permute-start.16 = (f32[264,128]{1,0:T(8,128)S(1)}, f32[264,128]{1,0:T(8,128)S(1)}, u32[]{:S(2)}, u32[]{:S(2)}) collective-permute-start(f32[264,128]{1,0:T(8,128)S(1)} %step_pass.16.held.sent), channel_id=1, source_target_pairs={{0,16},{1,9},{2,18},{3,11},{4,20},{5,13},{6,22},{7,15},{8,24},{9,1... | collective-permute-start | bytes 405512 | tf_op jit(solution)/shard_map/ppermute | solution.py:443
  71.6 3.1 %collective-permute-done.16.got = f32[264,128]{1,0:T(8,128)S(1)} collective-permute-done((f32[264,128]{1,0:T(8,128)S(1)}, f32[264,128]{1,0:T(8,128)S(1)}, u32[]{:S(2)}, u32[]{:S(2)}) %collective-permute-start.16) | collective-permute-done | bytes 135200 | tf_op jit(solution)/shard_map/ppermute | solution.py:443
  74.7 3.8 %collective-permute-start.17 = (f32[256,128]{1,0:T(8,128)S(1)}, f32[256,128]{1,0:T(8,128)S(1)}, u32[]{:S(2)}, u32[]{:S(2)}) collective-permute-start(f32[256,128]{1,0:T(8,128)S(1)} %get-tuple-element.100.part), channel_id=1, source_target_pairs={{0,4},{1,3},{2,6},{3,1},{4,0},{5,7},{6,2},{7,5},{8,12},{9,11},{10,... | collective-permute-start | bytes 393224 | tf_op jit(solution)/shard_map/ppermute | solution.py:443
  78.8 7.7 %collective-permute-done.17.got = f32[256,128]{1,0:T(8,128)S(1)} collective-permute-done((f32[256,128]{1,0:T(8,128)S(1)}, f32[256,128]{1,0:T(8,128)S(1)}, u32[]{:S(2)}, u32[]{:S(2)}) %collective-permute-start.17) | collective-permute-done | bytes 131104 | tf_op jit(solution)/shard_map/ppermute | solution.py:443
  87.4 2.1 %collective-permute-done.22.refs_1_ = f32[192,256]{1,0:T(8,128)S(1)} collective-permute-done((f32[192,256]{1,0:T(8,128)S(1)}, f32[192,256]{1,0:T(8,128)S(1)}, u32[]{:S(2)}, u32[]{:S(2)}) %collective-permute-start.22) | collective-permute-done | bytes 196640 | tf_op jit(solution)/shard_map/ppermute | solution.py:437
  89.5 1.1 error_pass.5
  92.9 1.2 %prior_pass.3 = (f32[384,128]{1,0:T(8,128)S(1)}, f32[384,128]{1,0:T(8,128)S(1)}, f32[520,128]{1,0:T(8,128)S(1)}, f32[512,128]{1,0:T(8,128)S(1)}, f32[64,128]{1,0:T(8,128)S(1)}) custom-call(bf16[768,1024]{1,0:T(8,128)(2,1)S(1)} %get-tuple-element.69.feats, bf16[1024,768]{1,0:T(8,128)(2,1)S(1)} %get-tuple-element.70.turned, f32[768,128]{1,0:T(8,128)S(1)} %part_pass.3.begun, ...), custom_call_target="tpu_custom_call" | custom-call | flops 402653184 | bytes 3145728 | tf_op jit(solution)/shard_map/prior_pass/pallas_call | solution.py:267
  94.8 5.9 %collective-permute-done.24.got.more = f32[520,128]{1,0:T(8,128)S(1)} collective-permute-done((f32[520,128]{1,0:T(8,128)S(1)}, f32[520,128]{1,0:T(8,128)S(1)}, u32[]{:S(2)}, u32[]{:S(2)}) %collective-permute-start.24) | collective-permute-done | bytes 266272 | tf_op jit(solution)/shard_map/ppermute | solution.py:443
  100.7 3.8 %collective-permute-start.25 = (f32[264,128]{1,0:T(8,128)S(1)}, f32[264,128]{1,0:T(8,128)S(1)}, u32[]{:S(2)}, u32[]{:S(2)}) collective-permute-start(f32[264,128]{1,0:T(8,128)S(1)} %get-tuple-element.118.sent), channel_id=1, source_target_pairs={{0,4},{1,3},{2,6},{3,1},{4,0},{5,7},{6,2},{7,5},{8,12},{9,11},{10,... | collective-permute-start | bytes 405512 | tf_op jit(solution)/shard_map/ppermute | solution.py:443
  104.5 3.0 %collective-permute-done.25.got.more = f32[264,128]{1,0:T(8,128)S(1)} collective-permute-done((f32[264,128]{1,0:T(8,128)S(1)}, f32[264,128]{1,0:T(8,128)S(1)}, u32[]{:S(2)}, u32[]{:S(2)}) %collective-permute-start.25) | collective-permute-done | bytes 135200 | tf_op jit(solution)/shard_map/ppermute | solution.py:443
  107.8 4.1 %collective-permute-done.26.got.more = f32[136,128]{1,0:T(8,128)S(1)} collective-permute-done((f32[136,128]{1,0:T(8,128)S(1)}, f32[136,128]{1,0:T(8,128)S(1)}, u32[]{:S(2)}, u32[]{:S(2)}) %collective-permute-start.26) | collective-permute-done | bytes 69664 | tf_op jit(solution)/shard_map/ppermute | solution.py:443
  111.9 1.7 %collective-permute-start.27 = (f32[72,128]{1,0:T(8,128)S(1)}, f32[72,128]{1,0:T(8,128)S(1)}, u32[]{:S(2)}, u32[]{:S(2)}) collective-permute-start(f32[72,128]{1,0:T(8,128)S(1)} %get-tuple-element.122.sent), channel_id=1, source_target_pairs={{0,16},{1,9},{2,18},{3,11},{4,20},{5,13},{6,22},{7,15},{8,24},{9,1... | collective-permute-start | bytes 110600 | tf_op jit(solution)/shard_map/ppermute | solution.py:443
  113.6 3.6 %collective-permute-done.27.got = f32[72,128]{1,0:T(8,128)S(1)} collective-permute-done((f32[72,128]{1,0:T(8,128)S(1)}, f32[72,128]{1,0:T(8,128)S(1)}, u32[]{:S(2)}, u32[]{:S(2)}) %collective-permute-start.27) | collective-permute-done | bytes 36896 | tf_op jit(solution)/shard_map/ppermute | solution.py:443
  (82 shorter events, 17.1 us)
Async XLA Ops:
  4.4 4.3 %collective-permute-start.1 = (f32[1024,128]{1,0:T(8,128)S(1)}, f32[1024,128]{1,0:T(8,128)S(1)}, u32[]{:S(2)}, u32[]{:S(2)}) collective-permute-start(f32[1024,128]{1,0:T(8,128)S(1)} %get-tuple-element.72), channel_id=1, source_target_pairs={{0,1},{1,0},{2,3},{3,2},{4,5},{5,4},{6,7},{7,6},{8,9},{9,8},{10,11... | collective-permute-start | bytes 1572872 | tf_op jit(solution)/shard_map/ppermute | solution.py:433
  4.9 43.7 %collective-permute-start = (f32[384,1024]{1,0:T(8,128)S(1)}, f32[384,1024]{1,0:T(8,128)S(1)}, u32[]{:S(2)}, u32[]{:S(2)}) collective-permute-start(f32[384,1024]{1,0:T(8,128)S(1)} %widen_pass.1.later), channel_id=1, source_target_pairs={{0,1},{1,0},{2,3},{3,2},{4,5},{5,4},{6,7},{7,6},{8,9},{9,8},{10,11... | collective-permute-start | bytes 4718600 | tf_op jit(solution)/shard_map/ppermute | solution.py:433
  5.0 6.7 %copy-start.2 = (bf16[3,384,256]{2,1,0:T(8,128)(2,1)S(1)}, bf16[3,384,256]{2,1,0:T(8,128)(2,1)}, u32[]{:S(2)}) copy-start(bf16[3,384,256]{2,1,0:T(8,128)(2,1)} %user_noise.5) | copy-start | bytes 1769476
  5.0 6.7 %copy-start.3 = (bf16[3,384,256]{2,1,0:T(8,128)(2,1)S(1)}, bf16[3,384,256]{2,1,0:T(8,128)(2,1)}, u32[]{:S(2)}) copy-start(bf16[3,384,256]{2,1,0:T(8,128)(2,1)} %item_noise.5) | copy-start | bytes 1769476
  6.1 2.6 %collective-permute-start.2 = (f32[8,128]{1,0:T(8,128)S(1)}, f32[8,128]{1,0:T(8,128)S(1)}, u32[]{:S(2)}, u32[]{:S(2)}) collective-permute-start(f32[8,128]{1,0:T(8,128)S(1)} %get-tuple-element.73.sent), channel_id=1, source_target_pairs={{0,1},{1,0},{2,3},{3,2},{4,5},{5,4},{6,7},{7,6},{8,9},{9,8},{10,11... | collective-permute-start | bytes 12296 | tf_op jit(solution)/shard_map/ppermute | solution.py:433
  8.8 7.3 %collective-permute-start.3 = (f32[520,128]{1,0:T(8,128)S(1)}, f32[520,128]{1,0:T(8,128)S(1)}, u32[]{:S(2)}, u32[]{:S(2)}) collective-permute-start(f32[520,128]{1,0:T(8,128)S(1)} %get-tuple-element.75.sent), channel_id=1, source_target_pairs={{0,2},{1,5},{2,0},{3,7},{4,6},{5,1},{6,4},{7,3},{8,10},{9,13},{10,... | collective-permute-start | bytes 798728 | tf_op jit(solution)/shard_map/ppermute | solution.py:443
  16.1 5.1 %collective-permute-start.4 = (f32[264,128]{1,0:T(8,128)S(1)}, f32[264,128]{1,0:T(8,128)S(1)}, u32[]{:S(2)}, u32[]{:S(2)}) collective-permute-start(f32[264,128]{1,0:T(8,128)S(1)} %get-tuple-element.79.sent), channel_id=1, source_target_pairs={{0,4},{1,3},{2,6},{3,1},{4,0},{5,7},{6,2},{7,5},{8,12},{9,11},{10,... | collective-permute-start | bytes 405512 | tf_op jit(solution)/shard_map/ppermute | solution.py:443
  21.2 5.5 %collective-permute-start.5 = (f32[264,128]{1,0:T(8,128)S(1)}, f32[264,128]{1,0:T(8,128)S(1)}, u32[]{:S(2)}, u32[]{:S(2)}) collective-permute-start(f32[264,128]{1,0:T(8,128)S(1)} %step_pass.12.held.sent), channel_id=1, source_target_pairs={{0,8},{1,17},{2,10},{3,19},{4,12},{5,21},{6,14},{7,23},{8,0},{9,25... | collective-permute-start | bytes 405512 | tf_op jit(solution)/shard_map/ppermute | solution.py:443
  26.8 6.0 %collective-permute-start.6 = (f32[264,128]{1,0:T(8,128)S(1)}, f32[264,128]{1,0:T(8,128)S(1)}, u32[]{:S(2)}, u32[]{:S(2)}) collective-permute-start(f32[264,128]{1,0:T(8,128)S(1)} %step_pass.13.held.sent), channel_id=1, source_target_pairs={{0,16},{1,9},{2,18},{3,11},{4,20},{5,13},{6,22},{7,15},{8,24},{9,1... | collective-permute-start | bytes 405512 | tf_op jit(solution)/shard_map/ppermute | solution.py:443
  32.8 10.7 %collective-permute-start.7 = (f32[256,128]{1,0:T(8,128)S(1)}, f32[256,128]{1,0:T(8,128)S(1)}, u32[]{:S(2)}, u32[]{:S(2)}) collective-permute-start(f32[256,128]{1,0:T(8,128)S(1)} %get-tuple-element.81.part.old), channel_id=1, source_target_pairs={{0,4},{1,3},{2,6},{3,1},{4,0},{5,7},{6,2},{7,5},{8,12},{9,11},{10,... | collective-permute-start | bytes 393224 | tf_op jit(solution)/shard_map/ppermute | solution.py:443
  36.4 8.8 %collective-permute-start.10 = (f32[192,256]{1,0:T(8,128)S(1)}, f32[192,256]{1,0:T(8,128)S(1)}, u32[]{:S(2)}, u32[]{:S(2)}) collective-permute-start(f32[192,256]{1,0:T(8,128)S(1)} %get-tuple-element.91), channel_id=1, source_target_pairs={{0,1},{1,2},{2,3},{3,4},{4,5},{5,6},{6,7},{7,8},{8,9},{9,10},{10,1... | collective-permute-start | bytes 589832 | tf_op jit(solution)/shard_map/ppermute | solution.py:437
  36.5 10.9 %collective-permute-start.11 = (f32[192,256]{1,0:T(8,128)S(1)}, f32[192,256]{1,0:T(8,128)S(1)}, u32[]{:S(2)}, u32[]{:S(2)}) collective-permute-start(f32[192,256]{1,0:T(8,128)S(1)} %get-tuple-element.92), channel_id=1, source_target_pairs={{0,1},{1,2},{2,3},{3,4},{4,5},{5,6},{6,7},{7,8},{8,9},{9,10},{10,1... | collective-permute-start | bytes 589832 | tf_op jit(solution)/shard_map/ppermute | solution.py:437
  43.5 6.4 %collective-permute-start.8 = (f32[512,128]{1,0:T(8,128)S(1)}, f32[512,128]{1,0:T(8,128)S(1)}, u32[]{:S(2)}, u32[]{:S(2)}) collective-permute-start(f32[512,128]{1,0:T(8,128)S(1)} %gather_pass.2.part), channel_id=1, source_target_pairs={{0,2},{1,5},{2,0},{3,7},{4,6},{5,1},{6,4},{7,3},{8,10},{9,13},{10,... | collective-permute-start | bytes 786440 | tf_op jit(solution)/shard_map/ppermute | solution.py:443
  43.6 6.0 %collective-permute-start.9 = (f32[384,128]{1,0:T(8,128)S(1)}, f32[384,128]{1,0:T(8,128)S(1)}, u32[]{:S(2)}, u32[]{:S(2)}) collective-permute-start(f32[384,128]{1,0:T(8,128)S(1)} %get-tuple-element.89), channel_id=1, source_target_pairs={{0,1},{1,0},{2,3},{3,2},{4,5},{5,4},{6,7},{7,6},{8,9},{9,8},{10,11... | collective-permute-start | bytes 589832 | tf_op jit(solution)/shard_map/ppermute | solution.py:433
  48.5 1.2 %collective-permute-start.12 = (f32[8,128]{1,0:T(8,128)S(1)}, f32[8,128]{1,0:T(8,128)S(1)}, u32[]{:S(2)}, u32[]{:S(2)}) collective-permute-start(f32[8,128]{1,0:T(8,128)S(1)} %get-tuple-element.93.stats), channel_id=1, source_target_pairs={{0,1},{1,0},{2,3},{3,2},{4,5},{5,4},{6,7},{7,6},{8,9},{9,8},{10,11... | collective-permute-start | bytes 12296 | tf_op jit(solution)/shard_map/ppermute | solution.py:433
  50.8 6.5 %collective-permute-start.13 = (f32[520,128]{1,0:T(8,128)S(1)}, f32[520,128]{1,0:T(8,128)S(1)}, u32[]{:S(2)}, u32[]{:S(2)}) collective-permute-start(f32[520,128]{1,0:T(8,128)S(1)} %get-tuple-element.95.sent), channel_id=1, source_target_pairs={{0,2},{1,5},{2,0},{3,7},{4,6},{5,1},{6,4},{7,3},{8,10},{9,13},{10,... | collective-permute-start | bytes 798728 | tf_op jit(solution)/shard_map/ppermute | solution.py:443
  57.3 6.0 %collective-permute-start.14 = (f32[264,128]{1,0:T(8,128)S(1)}, f32[264,128]{1,0:T(8,128)S(1)}, u32[]{:S(2)}, u32[]{:S(2)}) collective-permute-start(f32[264,128]{1,0:T(8,128)S(1)} %get-tuple-element.99.sent), channel_id=1, source_target_pairs={{0,4},{1,3},{2,6},{3,1},{4,0},{5,7},{6,2},{7,5},{8,12},{9,11},{10,... | collective-permute-start | bytes 405512 | tf_op jit(solution)/shard_map/ppermute | solution.py:443
  63.4 5.3 %collective-permute-start.15 = (f32[264,128]{1,0:T(8,128)S(1)}, f32[264,128]{1,0:T(8,128)S(1)}, u32[]{:S(2)}, u32[]{:S(2)}) collective-permute-start(f32[264,128]{1,0:T(8,128)S(1)} %step_pass.15.held.sent), channel_id=1, source_target_pairs={{0,8},{1,17},{2,10},{3,19},{4,12},{5,21},{6,14},{7,23},{8,0},{9,25... | collective-permute-start | bytes 405512 | tf_op jit(solution)/shard_map/ppermute | solution.py:443
  68.7 6.0 %collective-permute-start.16 = (f32[264,128]{1,0:T(8,128)S(1)}, f32[264,128]{1,0:T(8,128)S(1)}, u32[]{:S(2)}, u32[]{:S(2)}) collective-permute-start(f32[264,128]{1,0:T(8,128)S(1)} %step_pass.16.held.sent), channel_id=1, source_target_pairs={{0,16},{1,9},{2,18},{3,11},{4,20},{5,13},{6,22},{7,15},{8,24},{9,1... | collective-permute-start | bytes 405512 | tf_op jit(solution)/shard_map/ppermute | solution.py:443
  71.6 6.9 %collective-permute-start.19 = (f32[384,128]{1,0:T(8,128)S(1)}, f32[384,128]{1,0:T(8,128)S(1)}, u32[]{:S(2)}, u32[]{:S(2)}) collective-permute-start(f32[384,128]{1,0:T(8,128)S(1)} %get-tuple-element.104), channel_id=1, source_target_pairs={{0,1},{1,0},{2,3},{3,2},{4,5},{5,4},{6,7},{7,6},{8,9},{9,8},{10,11... | collective-permute-start | bytes 589832 | tf_op jit(solution)/shard_map/ppermute | solution.py:433
  74.7 11.8 %collective-permute-start.17 = (f32[256,128]{1,0:T(8,128)S(1)}, f32[256,128]{1,0:T(8,128)S(1)}, u32[]{:S(2)}, u32[]{:S(2)}) collective-permute-start(f32[256,128]{1,0:T(8,128)S(1)} %get-tuple-element.100.part), channel_id=1, source_target_pairs={{0,4},{1,3},{2,6},{3,1},{4,0},{5,7},{6,2},{7,5},{8,12},{9,11},{10,... | collective-permute-start | bytes 393224 | tf_op jit(solution)/shard_map/ppermute | solution.py:443
  78.7 8.7 %collective-permute-start.21 = (f32[192,256]{1,0:T(8,128)S(1)}, f32[192,256]{1,0:T(8,128)S(1)}, u32[]{:S(2)}, u32[]{:S(2)}) collective-permute-start(f32[192,256]{1,0:T(8,128)S(1)} %get-tuple-element.110), channel_id=1, source_target_pairs={{0,1},{1,2},{2,3},{3,4},{4,5},{5,6},{6,7},{7,8},{8,9},{9,10},{10,1... | collective-permute-start | bytes 589832 | tf_op jit(solution)/shard_map/ppermute | solution.py:437
  78.8 10.8 %collective-permute-start.22 = (f32[192,256]{1,0:T(8,128)S(1)}, f32[192,256]{1,0:T(8,128)S(1)}, u32[]{:S(2)}, u32[]{:S(2)}) collective-permute-start(f32[192,256]{1,0:T(8,128)S(1)} %get-tuple-element.111), channel_id=1, source_target_pairs={{0,1},{1,2},{2,3},{3,4},{4,5},{5,6},{6,7},{7,8},{8,9},{9,10},{10,1... | collective-permute-start | bytes 589832 | tf_op jit(solution)/shard_map/ppermute | solution.py:437
  86.5 6.4 %collective-permute-start.18 = (f32[512,128]{1,0:T(8,128)S(1)}, f32[512,128]{1,0:T(8,128)S(1)}, u32[]{:S(2)}, u32[]{:S(2)}) collective-permute-start(f32[512,128]{1,0:T(8,128)S(1)} %gather_pass.3.part), channel_id=1, source_target_pairs={{0,2},{1,5},{2,0},{3,7},{4,6},{5,1},{6,4},{7,3},{8,10},{9,13},{10,... | collective-permute-start | bytes 786440 | tf_op jit(solution)/shard_map/ppermute | solution.py:443
  86.6 4.5 %collective-permute-start.20 = (f32[384,128]{1,0:T(8,128)S(1)}, f32[384,128]{1,0:T(8,128)S(1)}, u32[]{:S(2)}, u32[]{:S(2)}) collective-permute-start(f32[384,128]{1,0:T(8,128)S(1)} %get-tuple-element.108), channel_id=1, source_target_pairs={{0,1},{1,0},{2,3},{3,2},{4,5},{5,4},{6,7},{7,6},{8,9},{9,8},{10,11... | collective-permute-start | bytes 589832 | tf_op jit(solution)/shard_map/ppermute | solution.py:433
  90.7 1.2 %collective-permute-start.23 = (f32[8,128]{1,0:T(8,128)S(1)}, f32[8,128]{1,0:T(8,128)S(1)}, u32[]{:S(2)}, u32[]{:S(2)}) collective-permute-start(f32[8,128]{1,0:T(8,128)S(1)} %get-tuple-element.112.stats), channel_id=1, source_target_pairs={{0,1},{1,0},{2,3},{3,2},{4,5},{5,4},{6,7},{7,6},{8,9},{9,8},{10,11... | collective-permute-start | bytes 12296 | tf_op jit(solution)/shard_map/ppermute | solution.py:433
  94.2 6.5 %collective-permute-start.24 = (f32[520,128]{1,0:T(8,128)S(1)}, f32[520,128]{1,0:T(8,128)S(1)}, u32[]{:S(2)}, u32[]{:S(2)}) collective-permute-start(f32[520,128]{1,0:T(8,128)S(1)} %get-tuple-element.114.sent), channel_id=1, source_target_pairs={{0,2},{1,5},{2,0},{3,7},{4,6},{5,1},{6,4},{7,3},{8,10},{9,13},{10,... | collective-permute-start | bytes 798728 | tf_op jit(solution)/shard_map/ppermute | solution.py:443
  100.7 6.8 %collective-permute-start.25 = (f32[264,128]{1,0:T(8,128)S(1)}, f32[264,128]{1,0:T(8,128)S(1)}, u32[]{:S(2)}, u32[]{:S(2)}) collective-permute-start(f32[264,128]{1,0:T(8,128)S(1)} %get-tuple-element.118.sent), channel_id=1, source_target_pairs={{0,4},{1,3},{2,6},{3,1},{4,0},{5,7},{6,2},{7,5},{8,12},{9,11},{10,... | collective-permute-start | bytes 405512 | tf_op jit(solution)/shard_map/ppermute | solution.py:443
  104.5 12.8 %collective-permute-start.28 = (f32[384,128]{1,0:T(8,128)S(1)}, f32[384,128]{1,0:T(8,128)S(1)}, u32[]{:S(2)}, u32[]{:S(2)}) collective-permute-start(f32[384,128]{1,0:T(8,128)S(1)} %get-tuple-element.127), channel_id=1, source_target_pairs={{0,1},{1,0},{2,3},{3,2},{4,5},{5,4},{6,7},{7,6},{8,9},{9,8},{10,11... | collective-permute-start | bytes 589832 | tf_op jit(solution)/shard_map/ppermute | solution.py:433
  107.5 4.4 %collective-permute-start.26 = (f32[136,128]{1,0:T(8,128)S(1)}, f32[136,128]{1,0:T(8,128)S(1)}, u32[]{:S(2)}, u32[]{:S(2)}) collective-permute-start(f32[136,128]{1,0:T(8,128)S(1)} %get-tuple-element.120.sent), channel_id=1, source_target_pairs={{0,8},{1,17},{2,10},{3,19},{4,12},{5,21},{6,14},{7,23},{8,0},{9,25... | collective-permute-start | bytes 208904 | tf_op jit(solution)/shard_map/ppermute | solution.py:443
  111.9 5.3 %collective-permute-start.27 = (f32[72,128]{1,0:T(8,128)S(1)}, f32[72,128]{1,0:T(8,128)S(1)}, u32[]{:S(2)}, u32[]{:S(2)}) collective-permute-start(f32[72,128]{1,0:T(8,128)S(1)} %get-tuple-element.122.sent), channel_id=1, source_target_pairs={{0,16},{1,9},{2,18},{3,11},{4,20},{5,13},{6,22},{7,15},{8,24},{9,1... | collective-permute-start | bytes 110600 | tf_op jit(solution)/shard_map/ppermute | solution.py:443
  117.3 1.2 %collective-permute-start.29 = (f32[32,128]{1,0:T(8,128)S(1)}, f32[32,128]{1,0:T(8,128)S(1)}, u32[]{:S(2)}, u32[]{:S(2)}) collective-permute-start(f32[32,128]{1,0:T(8,128)S(1)} %get-tuple-element.134), channel_id=1, source_target_pairs={{0,1},{1,0},{2,3},{3,2},{4,5},{5,4},{6,7},{7,6},{8,9},{9,8},{10,11... | collective-permute-start | bytes 49160 | tf_op jit(solution)/shard_map/ppermute | solution.py:433
  (8 other events, 12.1 us)

commit v12 on v11

--- a/solution.py
+++ b/solution.py
@@ -16,7 +16,7 @@
 
 CORES = 2
 RIDERS = 8
-ITEM_PARTS = 2
+ITEM_PARTS = 1
 NN = (((1,), (0,)), ((), ()))
 NT = (((1,), (1,)), ((), ()))
 TN = (((0,), (0,)), ((), ()))
@@ -63,7 +63,7 @@
 
 
 def error_kernel(stratum, codes, count, ratings, users, *refs):
-    items, (err_b, stats, pred) = refs[:-3], refs[-3:]
+    items, (err_b, stats, pred) = refs[1:-3], refs[-3:]
     tile = ratings.shape[-1]
     grid = users.shape[0] // tile
     user_b = users[...].astype(bf16)
@@ -88,18 +88,18 @@
     stats[...] = jnp.where(row == 0, total, jnp.where(row == 1, counted, 0.0))
 
 
-def error_pass(stratum, codes, count, ratings, users, *items):
+def error_pass(stratum, codes, count, ratings, users, later, *items):
     rows, rank = users.shape
     return pl.pallas_call(
         functools.partial(error_kernel, stratum),
         out_shape=(shape(rows, rows, dtype=bf16), shape(RIDERS, rank // CORES)),
-        in_specs=[SMEM] * 2 + [VMEM] * (2 + len(items)),
+        in_specs=[SMEM] * 2 + [VMEM] * 2 + [ANY] + [VMEM] * len(items),
         out_specs=(VMEM,) * 2,
         scratch_shapes=[pltpu.VMEM((rows, rows), f32)],
         compiler_params=PARAMS,
         cost_estimate=cost(24 * rows * rows * rank, 64 * rows * rank),
         name="error_pass",
-    )(codes, count, ratings, users, *items)
+    )(codes, count, ratings, users, later, *items)
 
 
 def grad_kernel(stratum, noise_scale, err_b, user_noise, item_noise, users, *refs):
@@ -130,7 +130,24 @@
     )(err_b, user_noise, item_noise, users, *items)
 
 
-def first_kernel(devices, feats, weights, users, later, own_mean, other_mean, send, keep, old, mean):
+def turn_kernel(feats, turned):
+    turned[...] = feats[...].T
+
+
+def turn_pass(feats):
+    rows, feat = feats.shape
+    return pl.pallas_call(
+        turn_kernel,
+        out_shape=shape(feat, rows, dtype=bf16),
+        in_specs=[VMEM],
+        out_specs=VMEM,
+        compiler_params=PARAMS,
+        cost_estimate=cost(rows * feat, 4 * rows * feat),
+        name="turn_pass",
+    )(feats)
+
+
+def first_kernel(devices, feats, turned, weights, users, own_mean, other_mean, send, keep, old, mean):
     place = where_am_i(devices)
     here = place[0]
     mean[...] = dot(feats[...], weights[...].astype(bf16))
@@ -138,61 +155,61 @@
         mean_now = half_of(mean, which)
         means[...] = mean_now
         offset = (half_of(users, which) - mean_now).astype(bf16)
-        grad[...] = dot(feats[...], offset, TN)
+        grad[...] = dot(turned[...], offset)
     rows, width = old.shape
     old[...] = weights[rows_at(2 * place[1] + place[2], rows), rows_at(here, width)]
 
 
-def first_pass(devices, feats, weights, users, later):
+def first_pass(devices, feats, turned, weights, users):
     rows, rank = users.shape
     feat = weights.shape[0]
     width = rank // CORES
     return pl.pallas_call(
         functools.partial(first_kernel, devices),
         out_shape=(shape(rows, width),) * 2 + (shape(feat, width),) * 2 + (shape(feat // 4, width),),
-        in_specs=[VMEM] * 3 + [ANY],
+        in_specs=[VMEM] * 4,
         out_specs=(VMEM,) * 5,
         scratch_shapes=[pltpu.VMEM(users.shape, f32)],
         compiler_params=PARAMS,
         cost_estimate=cost(4 * rows * feat * rank, 8 * feat * rank),
         name="first_pass",
-    )(feats, weights, users, later)
-
-
-def widen_kernel(narrow, wide):
+    )(feats, turned, weights, users)
+
+
+def widen_kernel(narrow, later, wide):
     wide[...] = narrow[...].astype(f32)
 
 
-def widen_pass(narrow):
+def widen_pass(narrow, later):
     return pl.pallas_call(
         widen_kernel,
         out_shape=shape(*narrow.shape),
-        in_specs=[VMEM],
+        in_specs=[VMEM, ANY],
         out_specs=VMEM,
         compiler_params=PARAMS,
         name="widen_pass",
-    )(narrow)
-
-
-def join_kernel(own, other, both, turned):
+    )(narrow, later)
+
+
+def join_kernel(own, own_turned, other, both, turned):
     rows = other.shape[0]
     both[:rows, :] = own[...]
     both[rows:, :] = other[...].astype(bf16)
-    turned[:, :rows] = own[...].T
+    turned[:, :rows] = own_turned[...]
     turned[:, rows:] = other[...].T.astype(bf16)
 
 
-def join_pass(own, other):
+def join_pass(own, own_turned, other):
     rows, feat = own.shape
     return pl.pallas_call(
         join_kernel,
         out_shape=(shape(CORES * rows, feat, dtype=bf16), shape(feat, CORES * rows, dtype=bf16)),
-        in_specs=[VMEM, VMEM],
+        in_specs=[VMEM] * 3,
         out_specs=(VMEM, VMEM),
         compiler_params=PARAMS,
         cost_estimate=cost(rows * feat, 12 * rows * feat),
         name="join_pass",
-    )(own, other)
+    )(own, own_turned, other)
 
 
 def part_kernel(devices, feats, part, mean):
@@ -216,7 +233,7 @@
     )(feats, part)
 
 
-def prior_kernel(places, devices, feats, turned, begun, part, got, own_cols, other_cols, stats, more_stats, own_mean, other_mean, send, keep, *refs):
+def prior_kernel(places, devices, feats, turned, begun, part, got, own_cols, other_cols, own_mean, other_mean, send, keep, *refs):
     rows = own_cols.shape[0]
     half = keep.shape[0]
     place = where_am_i(devices)
@@ -229,9 +246,8 @@
     other_mean[...] = mean[rows:]
     offset[:rows, :] = (own_cols[...] - mean[:rows]).astype(bf16)
     offset[rows:, :] = (other_cols[...] - mean[rows:]).astype(bf16)
-    send[half:, :] = stats[...] + more_stats[...]
     if places is None:
-        send[:half, :] = dot(turned[there, :], offset[...])
+        send[...] = dot(turned[there, :], offset[...])
         keep[...] = dot(turned[here, :], offset[...])
         return
     old, full = refs[:2]
@@ -256,10 +272,10 @@
             ref[n * block : (n + 1) * block, :] = full[pl.ds(source, block), :]
 
 
-def prior_pass(devices, feats, turned, begun, part, got, own_cols, other_cols, stats, more_stats, places=None):
+def prior_pass(devices, feats, turned, begun, part, got, own_cols, other_cols, places=None):
     rows, width = own_cols.shape
     half = part.shape[0]
-    outs = [shape(rows, width)] * 2 + [shape(half + stats.shape[0], width), shape(half, width)]
+    outs = [shape(rows, width)] * 2 + [shape(half, width)] * 2
     scratch = [pltpu.VMEM((CORES * rows, width), bf16)]
     if places is not None:
         outs.append(shape(2 * half // len(places[0]), width))
@@ -267,42 +283,43 @@
     return pl.pallas_call(
         functools.partial(prior_kernel, places, devices),
         out_shape=tuple(outs),
-        in_specs=[VMEM] * 9,
+        in_specs=[VMEM] * 7,
         out_specs=(VMEM,) * len(outs),
         scratch_shapes=scratch,
         compiler_params=PARAMS,
         cost_estimate=cost(16 * rows * half * width, 16 * rows * half),
         name="prior_pass",
-    )(feats, turned, begun, part, got, own_cols, other_cols, stats, more_stats)
-
-
-def step_kernel(halving, slot, devices, held, got, sent, more, *refs):
+    )(feats, turned, begun, part, got, own_cols, other_cols)
+
+
+def step_kernel(halving, stage, under, devices, held, got, *refs):
     send = refs[-2] if halving else refs[-1]
-    riders = sent.shape[0] - RIDERS, more.shape[0] - RIDERS
-    rider = sent[riders[0] :, :] + more[riders[1] :, :]
-    rows = send.shape[0] - RIDERS
+    rows = send.shape[0] - under
     if halving:
-        bit = where_am_i(devices)[slot]
+        bit = where_am_i(devices)[1 + stage]
         for ref, which in ((send, 1 - bit), (refs[-1], bit)):
-            at = pl.ds(pl.multiple_of(which * rows, 8), rows) if rows % 8 == 0 else pl.ds(which * rows, rows)
+            at = rows_at(which, rows)
             ref[:rows, :] = held[at, :] + got[at, :]
     else:
         send[:rows, :] = held[:rows, :] + got[:rows, :]
-    send[rows:, :] = rider
-
-
-def step_pass(halving, stage, devices, held, got, sent, more, rows, later=()):
+    if under:
+        sent, more = refs[:2]
+        send[rows:, :] = sent[sent.shape[0] - under :, :] + more[more.shape[0] - under :, :]
+
+
+def step_pass(halving, stage, devices, held, got, rows, riders=(), later=()):
     width = held.shape[1]
-    outs = [shape(rows // 2 + RIDERS, width), shape(rows // 2, width)] if halving else [shape(rows + RIDERS, width)]
-    return pl.pallas_call(
-        functools.partial(step_kernel, halving, 1 + stage, devices),
+    under = RIDERS if riders else 0
+    outs = [shape(rows // 2 + under, width), shape(rows // 2, width)] if halving else [shape(rows + under, width)]
+    return pl.pallas_call(
+        functools.partial(step_kernel, halving, stage, under, devices),
         out_shape=tuple(outs),
-        in_specs=[VMEM] * 4 + [ANY] * len(later),
+        in_specs=[VMEM] * (2 + len(riders)) + [ANY] * len(later),
         out_specs=(VMEM,) * len(outs),
         compiler_params=PARAMS,
         cost_estimate=cost(rows * width, 12 * rows * width),
         name="step_pass",
-    )(held, got, sent, more, *later)
+    )(held, got, *riders, *later)
 
 
 def update_kernel(rate, held, got, sent, old, *refs):
@@ -326,24 +343,25 @@
     )(held, got, sent, old, *later)
 
 
-def gather_kernel(slot, devices, part, got, both):
+def gather_kernel(slot, devices, part, got, *refs):
+    both = refs[-1]
     rows = part.shape[0]
     bit = where_am_i(devices)[slot]
     both[pl.ds(pl.multiple_of(bit * rows, rows), rows), :] = part[...]
     both[pl.ds(pl.multiple_of((1 - bit) * rows, rows), rows), :] = got[...]
 
 
-def gather_pass(stage, devices, part, got):
+def gather_pass(stage, devices, part, got, later=()):
     rows, width = part.shape
     return pl.pallas_call(
         functools.partial(gather_kernel, 1 + stage, devices),
         out_shape=shape(2 * rows, width),
-        in_specs=[VMEM, VMEM],
+        in_specs=[VMEM, VMEM] + [ANY] * len(later),
         out_specs=VMEM,
         compiler_params=PARAMS,
         cost_estimate=cost(rows * width, 16 * rows * width),
         name="gather_pass",
-    )(part, got)
+    )(part, got, *later)
 
 
 def split_kernel(devices, both, mine, other):
@@ -385,10 +403,10 @@
     )(mine, other)
 
 
-def renew_kernel(devices, stats, base_u, grad_u, own_mean, other_mean, base_v, grad_v, users, *outs):
+def renew_kernel(devices, stats, more, base_u, grad_u, own_mean, other_mean, base_v, grad_v, users, *outs):
     core = where_am_i(devices)[0]
     width = own_mean.shape[1]
-    precision = precision_of(stats[...])
+    precision = precision_of(stats[...] + more[...])
     precision = jnp.concatenate([precision] * CORES, 1)
     parts = 1 if len(outs) == 1 else ITEM_PARTS
     rows = base_v.shape[0] // parts
@@ -405,7 +423,7 @@
         ref[...] = half_of(users, which)
 
 
-def renew_pass(devices, last, stats, base_u, grad_u, own_mean, *state):
+def renew_pass(devices, last, stats, more, base_u, grad_u, own_mean, *state):
     rows, rank = base_u.shape
     outs = [shape(rows, rank)]
     if last:
@@ -415,12 +433,12 @@
     return pl.pallas_call(
         functools.partial(renew_kernel, devices),
         out_shape=tuple(outs),
-        in_specs=[VMEM] * 7,
+        in_specs=[VMEM] * 8,
         out_specs=(VMEM,) * len(outs),
         compiler_params=PARAMS,
         cost_estimate=cost(8 * base_u.size, 32 * base_u.size),
         name="renew_pass",
-    )(stats, base_u, grad_u, own_mean, *state)
+    )(stats, more, base_u, grad_u, own_mean, *state)
 
 
 def bit_order(devices, core):
@@ -473,45 +491,45 @@
     strata = ratings.shape[1]
     feat = prior_weights.shape[0]
     rate = rate_scale / (user_factors.shape[0] * devices)
-    def errors_of(stratum, users, *items):
-        err_b, stats = error_pass(stratum, tile_index, tile_count, ratings, users, *items)
-        return err_b, stats, swap(stats, devices)
-
-    wide = widen_pass(side_features)
+    own_turned = turn_pass(side_features)
     own_mean, other_mean, send, held, old = first_pass(
-        devices, side_features, prior_weights, user_factors, wide
+        devices, side_features, own_turned, prior_weights, user_factors
     )
-    got = swap(send, devices)
+    send, held = step_pass(True, 0, devices, held, swap(send, devices), feat)
     users, items = user_factors, [item_factors]
-    err_b, stats, more = errors_of(0, users, *items)
-    send, held = step_pass(True, 0, devices, held, got, stats, more, feat)
-    feats, turned = join_pass(side_features, swap(wide, devices))
     for stratum in range(strata):
         last = stratum + 1 == strata
+        got = exchange(send, devices, 0)
+        later = send if stratum else own_turned
+        err_b, stats = error_pass(stratum, tile_index, tile_count, ratings, users, later, *items)
         state = grad_pass(stratum, err_b, user_noise, item_noise, users, *items)
-        for stage in range(stages - 1):
+        riders = (stats, exchange(stats, devices, 0))
+        send, held = step_pass(True, 1, devices, held, got, got.shape[0], riders)
+        if stratum == 0:
+            wide = swap(widen_pass(side_features, state[0]), devices)
+            feats, turned = join_pass(side_features, own_turned, wide)
+        for stage in range(1, stages - 1):
             got = exchange(send, devices, stage)
             rows = got.shape[0] - RIDERS
-            later = state[:1] if stage == 0 else ()
-            if last or stage < 1:
-                send, held = step_pass(True, stage + 1, devices, held, got, send, got, rows, later)
+            later = state[:1] if stage == 1 else ()
+            if last:
+                send, held = step_pass(True, stage + 1, devices, held, got, rows, (send, got), later)
             else:
-                (send,) = step_pass(False, 0, devices, held, got, send, got, rows)
+                (send,) = step_pass(False, 0, devices, held, got, rows, (send, got), later)
                 held = send
         got = exchange(send, devices, stages - 1)
         part, stats = update_pass(rate, held, got, send, old)
         users, *items = renew_pass(
-            devices, last, stats, *state[:2], own_mean, other_mean, *state[2:]
+            devices, last, stats, swap(stats, devices), *state[:2], own_mean, other_mean, *state[2:]
         )
         if last:
             break
         old = part
         *items, own_cols, other_cols = items
-        items = [roll(part, devices) for part in items]
+        items = [roll(rows, devices) for rows in items]
         other_cols = swap(other_cols, devices)
-        part = gather_pass(1, devices, part, exchange(part, devices, 1))
+        part = gather_pass(1, devices, part, exchange(part, devices, 1), [users])
         got = exchange(part, devices, 0)
-        err_b, stats, more = errors_of(stratum + 1, users, *items)
         begun = part_pass(devices, feats, part)
         own_mean, other_mean, send, held, *olds = prior_pass(
             devices,
@@ -522,8 +540,6 @@
             got,
             own_cols,
             other_cols,
-            stats,
-            more,
             final_places(devices) if stratum + 2 == strata else None,
         )
         if olds:

time: 119 us -> 116 us (0.975)
  waiting for transfers between devices: 70.6 us -> 56.8 us
  starting transfers between devices: 33.2 us -> 43.3 us
    ppermute x16 -> x19, starting transfers between devices: 29.9 us -> 41 us  [exchange(): return lax.ppermute(array, 'user', pairs)]
    ppermute x16 -> x19, waiting for transfers between devices: 60.8 us -> 51.4 us  [exchange(): return lax.ppermute(array, 'user', pairs)]
    ppermute x4 -> x2, waiting for transfers between devices: 6.57 us -> 1.55 us  [roll(): lax.ppermute(array, 'user', [(i, (i + 1) % devices) for i in range(device...]
  transfers between devices with their start and end apart: 30 -> 31, of which waited for: 24 -> 23; matrix products, arithmetic and copies ran while one was open for 0% -> 0% of each run, Pallas kernels for 7% -> 8%
where the time goes in v12:
time: 116 us
  waiting for transfers between devices  56.8 us (49%)
  starting transfers between devices  43.3 us (37%)
  Pallas kernels  11.9 us (10%)
  local copies, waits for them, and re-layouts  2.89 us (2%)
    ppermute x19, waiting for transfers between devices, exchange(): return lax.ppermute(array, 'user', pairs)  51.4 us
    ppermute x19, starting transfers between devices, exchange(): return lax.ppermute(array, 'user', pairs)  41 us
    ppermute x10, waiting for transfers between devices, swap(): return lax.ppermute(array, 'user', [(i, i ^ 1) for i in range(devices)])  3.86 us
    pallas_call x3, Pallas kernels, error_pass(): pl.pallas_call(functools.partial(error_kernel, stratum), out_shape=(shape...  3.19 us
    unnamed x21, local copies, waits for them, and re-layouts  2.89 us
  transfers between devices with their start and end apart: 31, of which 23 were waited for; matrix products, arithmetic and copies ran while one was open for 0% of the time, Pallas kernels for 8%

profile of v12, /device:TPU:0, one launch (start us, length us, event | category | flops | bytes accessed | tf_op | source)
XLA Modules:
  0.0 115.8 jit_solution(3933497501647498029)
XLA Ops:
  7.4 3.0 %collective-permute-start.2 = (f32[512,128]{1,0:T(8,128)S(1)}, f32[512,128]{1,0:T(8,128)S(1)}, u32[]{:S(2)}, u32[]{:S(2)}) collective-permute-start(f32[512,128]{1,0:T(8,128)S(1)} %get-tuple-element.74), channel_id=1, source_target_pairs={{0,2},{1,5},{2,0},{3,7},{4,6},{5,1},{6,4},{7,3},{8,10},{9,13},{10,... | collective-permute-start | bytes 786440 | tf_op jit(solution)/shard_map/ppermute | solution.py:461
  10.5 4.3 %collective-permute-done.3.refs_1_ = f32[8,128]{1,0:T(8,128)S(1)} collective-permute-done((f32[8,128]{1,0:T(8,128)S(1)}, f32[8,128]{1,0:T(8,128)S(1)}, u32[]{:S(2)}, u32[]{:S(2)}) %collective-permute-start.3) | collective-permute-done | bytes 4128 | tf_op jit(solution)/shard_map/ppermute | solution.py:461
  14.9 2.1 %collective-permute-start.4 = (f32[264,128]{1,0:T(8,128)S(1)}, f32[264,128]{1,0:T(8,128)S(1)}, u32[]{:S(2)}, u32[]{:S(2)}) collective-permute-start(f32[264,128]{1,0:T(8,128)S(1)} %get-tuple-element.77.refs_0_), channel_id=1, source_target_pairs={{0,4},{1,3},{2,6},{3,1},{4,0},{5,7},{6,2},{7,5},{8,12},{9,11},{10,... | collective-permute-start | bytes 405512 | tf_op jit(solution)/shard_map/ppermute | solution.py:461
  17.0 3.0 %collective-permute-done.4.got.refs_1_ = f32[264,128]{1,0:T(8,128)S(1)} collective-permute-done((f32[264,128]{1,0:T(8,128)S(1)}, f32[264,128]{1,0:T(8,128)S(1)}, u32[]{:S(2)}, u32[]{:S(2)}) %collective-permute-start.4) | collective-permute-done | bytes 135200 | tf_op jit(solution)/shard_map/ppermute | solution.py:461
  20.0 2.1 %collective-permute-start.5 = (f32[264,128]{1,0:T(8,128)S(1)}, f32[264,128]{1,0:T(8,128)S(1)}, u32[]{:S(2)}, u32[]{:S(2)}) collective-permute-start(f32[264,128]{1,0:T(8,128)S(1)} %step_pass.12.held.refs_0_), channel_id=1, source_target_pairs={{0,8},{1,17},{2,10},{3,19},{4,12},{5,21},{6,14},{7,23},{8,0},{9,25... | collective-permute-start | bytes 405512 | tf_op jit(solution)/shard_map/ppermute | solution.py:461
  22.1 3.3 %collective-permute-done.5.got.refs_1_ = f32[264,128]{1,0:T(8,128)S(1)} collective-permute-done((f32[264,128]{1,0:T(8,128)S(1)}, f32[264,128]{1,0:T(8,128)S(1)}, u32[]{:S(2)}, u32[]{:S(2)}) %collective-permute-start.5) | collective-permute-done | bytes 135200 | tf_op jit(solution)/shard_map/ppermute | solution.py:461
  25.4 2.8 %collective-permute-start.6 = (f32[264,128]{1,0:T(8,128)S(1)}, f32[264,128]{1,0:T(8,128)S(1)}, u32[]{:S(2)}, u32[]{:S(2)}) collective-permute-start(f32[264,128]{1,0:T(8,128)S(1)} %step_pass.13.held.sent), channel_id=1, source_target_pairs={{0,16},{1,9},{2,18},{3,11},{4,20},{5,13},{6,22},{7,15},{8,24},{9,1... | collective-permute-start | bytes 405512 | tf_op jit(solution)/shard_map/ppermute | solution.py:461
  28.2 3.2 %collective-permute-done.6.got = f32[264,128]{1,0:T(8,128)S(1)} collective-permute-done((f32[264,128]{1,0:T(8,128)S(1)}, f32[264,128]{1,0:T(8,128)S(1)}, u32[]{:S(2)}, u32[]{:S(2)}) %collective-permute-start.6) | collective-permute-done | bytes 135200 | tf_op jit(solution)/shard_map/ppermute | solution.py:461
  31.4 3.5 %collective-permute-start.7 = (f32[256,128]{1,0:T(8,128)S(1)}, f32[256,128]{1,0:T(8,128)S(1)}, u32[]{:S(2)}, u32[]{:S(2)}) collective-permute-start(f32[256,128]{1,0:T(8,128)S(1)} %get-tuple-element.79.part.old), channel_id=1, source_target_pairs={{0,4},{1,3},{2,6},{3,1},{4,0},{5,7},{6,2},{7,5},{8,12},{9,11},{10,... | collective-permute-start | bytes 393224 | tf_op jit(solution)/shard_map/ppermute | solution.py:461
  36.4 1.5 %collective-permute-done.7.got = f32[256,128]{1,0:T(8,128)S(1)} collective-permute-done((f32[256,128]{1,0:T(8,128)S(1)}, f32[256,128]{1,0:T(8,128)S(1)}, u32[]{:S(2)}, u32[]{:S(2)}) %collective-permute-start.7) | collective-permute-done | bytes 131104 | tf_op jit(solution)/shard_map/ppermute | solution.py:461
  37.9 2.1 %collective-permute-start.9 = (f32[512,128]{1,0:T(8,128)S(1)}, f32[512,128]{1,0:T(8,128)S(1)}, u32[]{:S(2)}, u32[]{:S(2)}) collective-permute-start(f32[512,128]{1,0:T(8,128)S(1)} %gather_pass.2.part), channel_id=1, source_target_pairs={{0,2},{1,5},{2,0},{3,7},{4,6},{5,1},{6,4},{7,3},{8,10},{9,13},{10,... | collective-permute-start | bytes 786440 | tf_op jit(solution)/shard_map/ppermute | solution.py:461
  41.4 5.3 %collective-permute-done.9.got = f32[512,128]{1,0:T(8,128)S(1)} collective-permute-done((f32[512,128]{1,0:T(8,128)S(1)}, f32[512,128]{1,0:T(8,128)S(1)}, u32[]{:S(2)}, u32[]{:S(2)}) %collective-permute-start.9) | collective-permute-done | bytes 262176 | tf_op jit(solution)/shard_map/ppermute | solution.py:461
  47.5 2.5 %collective-permute-start.11 = (f32[512,128]{1,0:T(8,128)S(1)}, f32[512,128]{1,0:T(8,128)S(1)}, u32[]{:S(2)}, u32[]{:S(2)}) collective-permute-start(f32[512,128]{1,0:T(8,128)S(1)} %get-tuple-element.90.refs_0_), channel_id=1, source_target_pairs={{0,2},{1,5},{2,0},{3,7},{4,6},{5,1},{6,4},{7,3},{8,10},{9,13},{10,... | collective-permute-start | bytes 786440 | tf_op jit(solution)/shard_map/ppermute | solution.py:461
  52.1 3.6 %collective-permute-done.13.refs_1_ = f32[8,128]{1,0:T(8,128)S(1)} collective-permute-done((f32[8,128]{1,0:T(8,128)S(1)}, f32[8,128]{1,0:T(8,128)S(1)}, u32[]{:S(2)}, u32[]{:S(2)}) %collective-permute-start.13) | collective-permute-done | bytes 4128 | tf_op jit(solution)/shard_map/ppermute | solution.py:461
  57.1 3.7 %collective-permute-done.14.got.refs_1_ = f32[264,128]{1,0:T(8,128)S(1)} collective-permute-done((f32[264,128]{1,0:T(8,128)S(1)}, f32[264,128]{1,0:T(8,128)S(1)}, u32[]{:S(2)}, u32[]{:S(2)}) %collective-permute-start.14) | collective-permute-done | bytes 135200 | tf_op jit(solution)/shard_map/ppermute | solution.py:461
  60.8 2.2 %collective-permute-start.15 = (f32[264,128]{1,0:T(8,128)S(1)}, f32[264,128]{1,0:T(8,128)S(1)}, u32[]{:S(2)}, u32[]{:S(2)}) collective-permute-start(f32[264,128]{1,0:T(8,128)S(1)} %step_pass.15.held.refs_0_), channel_id=1, source_target_pairs={{0,8},{1,17},{2,10},{3,19},{4,12},{5,21},{6,14},{7,23},{8,0},{9,25... | collective-permute-start | bytes 405512 | tf_op jit(solution)/shard_map/ppermute | solution.py:461
  63.0 3.4 %collective-permute-done.15.got.refs_1_ = f32[264,128]{1,0:T(8,128)S(1)} collective-permute-done((f32[264,128]{1,0:T(8,128)S(1)}, f32[264,128]{1,0:T(8,128)S(1)}, u32[]{:S(2)}, u32[]{:S(2)}) %collective-permute-start.15) | collective-permute-done | bytes 135200 | tf_op jit(solution)/shard_map/ppermute | solution.py:461
  66.5 3.0 %collective-permute-start.16 = (f32[264,128]{1,0:T(8,128)S(1)}, f32[264,128]{1,0:T(8,128)S(1)}, u32[]{:S(2)}, u32[]{:S(2)}) collective-permute-start(f32[264,128]{1,0:T(8,128)S(1)} %step_pass.16.held.sent), channel_id=1, source_target_pairs={{0,16},{1,9},{2,18},{3,11},{4,20},{5,13},{6,22},{7,15},{8,24},{9,1... | collective-permute-start | bytes 405512 | tf_op jit(solution)/shard_map/ppermute | solution.py:461
  69.5 3.0 %collective-permute-done.16.got = f32[264,128]{1,0:T(8,128)S(1)} collective-permute-done((f32[264,128]{1,0:T(8,128)S(1)}, f32[264,128]{1,0:T(8,128)S(1)}, u32[]{:S(2)}, u32[]{:S(2)}) %collective-permute-start.16) | collective-permute-done | bytes 135200 | tf_op jit(solution)/shard_map/ppermute | solution.py:461
  72.5 3.9 %collective-permute-start.17 = (f32[256,128]{1,0:T(8,128)S(1)}, f32[256,128]{1,0:T(8,128)S(1)}, u32[]{:S(2)}, u32[]{:S(2)}) collective-permute-start(f32[256,128]{1,0:T(8,128)S(1)} %get-tuple-element.97.part), channel_id=1, source_target_pairs={{0,4},{1,3},{2,6},{3,1},{4,0},{5,7},{6,2},{7,5},{8,12},{9,11},{10,... | collective-permute-start | bytes 393224 | tf_op jit(solution)/shard_map/ppermute | solution.py:461
  77.8 1.5 %collective-permute-done.17.got = f32[256,128]{1,0:T(8,128)S(1)} collective-permute-done((f32[256,128]{1,0:T(8,128)S(1)}, f32[256,128]{1,0:T(8,128)S(1)}, u32[]{:S(2)}, u32[]{:S(2)}) %collective-permute-start.17) | collective-permute-done | bytes 131104 | tf_op jit(solution)/shard_map/ppermute | solution.py:461
  79.4 1.5 %collective-permute-start.20 = (f32[512,128]{1,0:T(8,128)S(1)}, f32[512,128]{1,0:T(8,128)S(1)}, u32[]{:S(2)}, u32[]{:S(2)}) collective-permute-start(f32[512,128]{1,0:T(8,128)S(1)} %gather_pass.3.part), channel_id=1, source_target_pairs={{0,2},{1,5},{2,0},{3,7},{4,6},{5,1},{6,4},{7,3},{8,10},{9,13},{10,... | collective-permute-start | bytes 786440 | tf_op jit(solution)/shard_map/ppermute | solution.py:461
  82.4 5.2 %collective-permute-done.20.got = f32[512,128]{1,0:T(8,128)S(1)} collective-permute-done((f32[512,128]{1,0:T(8,128)S(1)}, f32[512,128]{1,0:T(8,128)S(1)}, u32[]{:S(2)}, u32[]{:S(2)}) %collective-permute-start.20) | collective-permute-done | bytes 262176 | tf_op jit(solution)/shard_map/ppermute | solution.py:461
  87.6 1.2 %prior_pass.3 = (f32[384,128]{1,0:T(8,128)S(1)}, f32[384,128]{1,0:T(8,128)S(1)}, f32[512,128]{1,0:T(8,128)S(1)}, f32[512,128]{1,0:T(8,128)S(1)}, f32[64,128]{1,0:T(8,128)S(1)}) custom-call(bf16[768,1024]{1,0:T(8,128)(2,1)S(1)} %get-tuple-element.69.feats, bf16[1024,768]{1,0:T(8,128)(2,1)S(1)} %get-tuple-element.70.turned, f32[768,128]{1,0:T(8,128)S(1)} %part_pass.3.begun, ...), custom_call_target="tpu_custom_call" | custom-call | flops 402653184 | bytes 3145728 | tf_op jit(solution)/shard_map/prior_pass/pallas_call | solution.py:283
  88.8 2.5 %collective-permute-start.22 = (f32[512,128]{1,0:T(8,128)S(1)}, f32[512,128]{1,0:T(8,128)S(1)}, u32[]{:S(2)}, u32[]{:S(2)}) collective-permute-start(f32[512,128]{1,0:T(8,128)S(1)} %get-tuple-element.108.refs_0_), channel_id=1, source_target_pairs={{0,2},{1,5},{2,0},{3,7},{4,6},{5,1},{6,4},{7,3},{8,10},{9,13},{10,... | collective-permute-start | bytes 786440 | tf_op jit(solution)/shard_map/ppermute | solution.py:461
  93.2 3.6 %collective-permute-done.24.refs_1_ = f32[8,128]{1,0:T(8,128)S(1)} collective-permute-done((f32[8,128]{1,0:T(8,128)S(1)}, f32[8,128]{1,0:T(8,128)S(1)}, u32[]{:S(2)}, u32[]{:S(2)}) %collective-permute-start.24) | collective-permute-done | bytes 4128 | tf_op jit(solution)/shard_map/ppermute | solution.py:461
  96.9 2.4 %collective-permute-start.25 = (f32[264,128]{1,0:T(8,128)S(1)}, f32[264,128]{1,0:T(8,128)S(1)}, u32[]{:S(2)}, u32[]{:S(2)}) collective-permute-start(f32[264,128]{1,0:T(8,128)S(1)} %get-tuple-element.112.refs_0_), channel_id=1, source_target_pairs={{0,4},{1,3},{2,6},{3,1},{4,0},{5,7},{6,2},{7,5},{8,12},{9,11},{10,... | collective-permute-start | bytes 405512 | tf_op jit(solution)/shard_map/ppermute | solution.py:461
  99.8 2.5 %collective-permute-done.25.got.refs_1_ = f32[264,128]{1,0:T(8,128)S(1)} collective-permute-done((f32[264,128]{1,0:T(8,128)S(1)}, f32[264,128]{1,0:T(8,128)S(1)}, u32[]{:S(2)}, u32[]{:S(2)}) %collective-permute-start.25) | collective-permute-done | bytes 135200 | tf_op jit(solution)/shard_map/ppermute | solution.py:461
  102.3 2.7 %collective-permute-start.26 = (f32[136,128]{1,0:T(8,128)S(1)}, f32[136,128]{1,0:T(8,128)S(1)}, u32[]{:S(2)}, u32[]{:S(2)}) collective-permute-start(f32[136,128]{1,0:T(8,128)S(1)} %get-tuple-element.116.refs_0_), channel_id=1, source_target_pairs={{0,8},{1,17},{2,10},{3,19},{4,12},{5,21},{6,14},{7,23},{8,0},{9,25... | collective-permute-start | bytes 208904 | tf_op jit(solution)/shard_map/ppermute | solution.py:461
  105.0 2.3 %collective-permute-done.26.got.refs_1_ = f32[136,128]{1,0:T(8,128)S(1)} collective-permute-done((f32[136,128]{1,0:T(8,128)S(1)}, f32[136,128]{1,0:T(8,128)S(1)}, u32[]{:S(2)}, u32[]{:S(2)}) %collective-permute-start.26) | collective-permute-done | bytes 69664 | tf_op jit(solution)/shard_map/ppermute | solution.py:461
  107.3 3.4 %collective-permute-start.27 = (f32[72,128]{1,0:T(8,128)S(1)}, f32[72,128]{1,0:T(8,128)S(1)}, u32[]{:S(2)}, u32[]{:S(2)}) collective-permute-start(f32[72,128]{1,0:T(8,128)S(1)} %get-tuple-element.118.sent), channel_id=1, source_target_pairs={{0,16},{1,9},{2,18},{3,11},{4,20},{5,13},{6,22},{7,15},{8,24},{9,1... | collective-permute-start | bytes 110600 | tf_op jit(solution)/shard_map/ppermute | solution.py:461
  110.8 1.9 %collective-permute-done.27.got = f32[72,128]{1,0:T(8,128)S(1)} collective-permute-done((f32[72,128]{1,0:T(8,128)S(1)}, f32[72,128]{1,0:T(8,128)S(1)}, u32[]{:S(2)}, u32[]{:S(2)}) %collective-permute-start.27) | collective-permute-done | bytes 36896 | tf_op jit(solution)/shard_map/ppermute | solution.py:461
  (85 shorter events, 22.3 us)
Async XLA Ops:
  3.1 1.7 %copy-start.8 = (s32[1,3]{1,0:T(1,128)S(1)}, s32[1,3]{1,0:T(1,128)}, u32[]{:S(2)}) copy-start(s32[1,3]{1,0:T(1,128)} %count.5) | copy-start | bytes 40
  4.3 3.0 %collective-permute-start.1 = (f32[1024,128]{1,0:T(8,128)S(1)}, f32[1024,128]{1,0:T(8,128)S(1)}, u32[]{:S(2)}, u32[]{:S(2)}) collective-permute-start(f32[1024,128]{1,0:T(8,128)S(1)} %get-tuple-element.72), channel_id=1, source_target_pairs={{0,1},{1,0},{2,3},{3,2},{4,5},{5,4},{6,7},{7,6},{8,9},{9,8},{10,11... | collective-permute-start | bytes 1572872 | tf_op jit(solution)/shard_map/ppermute | solution.py:451
  7.2 33.3 %collective-permute-start = (f32[384,1024]{1,0:T(8,128)S(1)}, f32[384,1024]{1,0:T(8,128)S(1)}, u32[]{:S(2)}, u32[]{:S(2)}) collective-permute-start(f32[384,1024]{1,0:T(8,128)S(1)} %widen_pass.1), channel_id=1, source_target_pairs={{0,1},{1,0},{2,3},{3,2},{4,5},{5,4},{6,7},{7,6},{8,9},{9,8},{10,11... | collective-permute-start | bytes 4718600 | tf_op jit(solution)/shard_map/ppermute | solution.py:451
  7.4 7.4 %collective-permute-start.2 = (f32[512,128]{1,0:T(8,128)S(1)}, f32[512,128]{1,0:T(8,128)S(1)}, u32[]{:S(2)}, u32[]{:S(2)}) collective-permute-start(f32[512,128]{1,0:T(8,128)S(1)} %get-tuple-element.74), channel_id=1, source_target_pairs={{0,2},{1,5},{2,0},{3,7},{4,6},{5,1},{6,4},{7,3},{8,10},{9,13},{10,... | collective-permute-start | bytes 786440 | tf_op jit(solution)/shard_map/ppermute | solution.py:461
  10.4 4.4 %collective-permute-start.3 = (f32[8,128]{1,0:T(8,128)S(1)}, f32[8,128]{1,0:T(8,128)S(1)}, u32[]{:S(2)}, u32[]{:S(2)}) collective-permute-start(f32[8,128]{1,0:T(8,128)S(1)} %get-tuple-element.75.refs_0_), channel_id=1, source_target_pairs={{0,2},{1,5},{2,0},{3,7},{4,6},{5,1},{6,4},{7,3},{8,10},{9,13},{10,... | collective-permute-start | bytes 12296 | tf_op jit(solution)/shard_map/ppermute | solution.py:461
  14.9 5.1 %collective-permute-start.4 = (f32[264,128]{1,0:T(8,128)S(1)}, f32[264,128]{1,0:T(8,128)S(1)}, u32[]{:S(2)}, u32[]{:S(2)}) collective-permute-start(f32[264,128]{1,0:T(8,128)S(1)} %get-tuple-element.77.refs_0_), channel_id=1, source_target_pairs={{0,4},{1,3},{2,6},{3,1},{4,0},{5,7},{6,2},{7,5},{8,12},{9,11},{10,... | collective-permute-start | bytes 405512 | tf_op jit(solution)/shard_map/ppermute | solution.py:461
  20.0 5.4 %collective-permute-start.5 = (f32[264,128]{1,0:T(8,128)S(1)}, f32[264,128]{1,0:T(8,128)S(1)}, u32[]{:S(2)}, u32[]{:S(2)}) collective-permute-start(f32[264,128]{1,0:T(8,128)S(1)} %step_pass.12.held.refs_0_), channel_id=1, source_target_pairs={{0,8},{1,17},{2,10},{3,19},{4,12},{5,21},{6,14},{7,23},{8,0},{9,25... | collective-permute-start | bytes 405512 | tf_op jit(solution)/shard_map/ppermute | solution.py:461
  25.4 6.0 %collective-permute-start.6 = (f32[264,128]{1,0:T(8,128)S(1)}, f32[264,128]{1,0:T(8,128)S(1)}, u32[]{:S(2)}, u32[]{:S(2)}) collective-permute-start(f32[264,128]{1,0:T(8,128)S(1)} %step_pass.13.held.sent), channel_id=1, source_target_pairs={{0,16},{1,9},{2,18},{3,11},{4,20},{5,13},{6,22},{7,15},{8,24},{9,1... | collective-permute-start | bytes 405512 | tf_op jit(solution)/shard_map/ppermute | solution.py:461
  31.4 6.5 %collective-permute-start.7 = (f32[256,128]{1,0:T(8,128)S(1)}, f32[256,128]{1,0:T(8,128)S(1)}, u32[]{:S(2)}, u32[]{:S(2)}) collective-permute-start(f32[256,128]{1,0:T(8,128)S(1)} %get-tuple-element.79.part.old), channel_id=1, source_target_pairs={{0,4},{1,3},{2,6},{3,1},{4,0},{5,7},{6,2},{7,5},{8,12},{9,11},{10,... | collective-permute-start | bytes 393224 | tf_op jit(solution)/shard_map/ppermute | solution.py:461
  35.0 1.2 %collective-permute-start.8 = (f32[8,128]{1,0:T(8,128)S(1)}, f32[8,128]{1,0:T(8,128)S(1)}, u32[]{:S(2)}, u32[]{:S(2)}) collective-permute-start(f32[8,128]{1,0:T(8,128)S(1)} %get-tuple-element.80.stats), channel_id=1, source_target_pairs={{0,1},{1,0},{2,3},{3,2},{4,5},{5,4},{6,7},{7,6},{8,9},{9,8},{10,11... | collective-permute-start | bytes 12296 | tf_op jit(solution)/shard_map/ppermute | solution.py:451
  37.9 8.8 %collective-permute-start.9 = (f32[512,128]{1,0:T(8,128)S(1)}, f32[512,128]{1,0:T(8,128)S(1)}, u32[]{:S(2)}, u32[]{:S(2)}) collective-permute-start(f32[512,128]{1,0:T(8,128)S(1)} %gather_pass.2.part), channel_id=1, source_target_pairs={{0,2},{1,5},{2,0},{3,7},{4,6},{5,1},{6,4},{7,3},{8,10},{9,13},{10,... | collective-permute-start | bytes 786440 | tf_op jit(solution)/shard_map/ppermute | solution.py:461
  40.0 1.4 %collective-permute-start.10 = (f32[384,128]{1,0:T(8,128)S(1)}, f32[384,128]{1,0:T(8,128)S(1)}, u32[]{:S(2)}, u32[]{:S(2)}) collective-permute-start(f32[384,128]{1,0:T(8,128)S(1)} %get-tuple-element.88), channel_id=1, source_target_pairs={{0,1},{1,0},{2,3},{3,2},{4,5},{5,4},{6,7},{7,6},{8,9},{9,8},{10,11... | collective-permute-start | bytes 589832 | tf_op jit(solution)/shard_map/ppermute | solution.py:451
  40.0 10.9 %collective-permute-start.12 = (f32[384,256]{1,0:T(8,128)S(1)}, f32[384,256]{1,0:T(8,128)S(1)}, u32[]{:S(2)}, u32[]{:S(2)}) collective-permute-start(f32[384,256]{1,0:T(8,128)S(1)} %get-tuple-element.91), channel_id=1, source_target_pairs={{0,1},{1,2},{2,3},{3,4},{4,5},{5,6},{6,7},{7,8},{8,9},{9,10},{10,1... | collective-permute-start | bytes 1179656 | tf_op jit(solution)/shard_map/ppermute | solution.py:455
  47.5 8.2 %collective-permute-start.11 = (f32[512,128]{1,0:T(8,128)S(1)}, f32[512,128]{1,0:T(8,128)S(1)}, u32[]{:S(2)}, u32[]{:S(2)}) collective-permute-start(f32[512,128]{1,0:T(8,128)S(1)} %get-tuple-element.90.refs_0_), channel_id=1, source_target_pairs={{0,2},{1,5},{2,0},{3,7},{4,6},{5,1},{6,4},{7,3},{8,10},{9,13},{10,... | collective-permute-start | bytes 786440 | tf_op jit(solution)/shard_map/ppermute | solution.py:461
  52.0 3.7 %collective-permute-start.13 = (f32[8,128]{1,0:T(8,128)S(1)}, f32[8,128]{1,0:T(8,128)S(1)}, u32[]{:S(2)}, u32[]{:S(2)}) collective-permute-start(f32[8,128]{1,0:T(8,128)S(1)} %get-tuple-element.92.refs_0_), channel_id=1, source_target_pairs={{0,2},{1,5},{2,0},{3,7},{4,6},{5,1},{6,4},{7,3},{8,10},{9,13},{10,... | collective-permute-start | bytes 12296 | tf_op jit(solution)/shard_map/ppermute | solution.py:461
  55.7 5.1 %collective-permute-start.14 = (f32[264,128]{1,0:T(8,128)S(1)}, f32[264,128]{1,0:T(8,128)S(1)}, u32[]{:S(2)}, u32[]{:S(2)}) collective-permute-start(f32[264,128]{1,0:T(8,128)S(1)} %get-tuple-element.94.refs_0_), channel_id=1, source_target_pairs={{0,4},{1,3},{2,6},{3,1},{4,0},{5,7},{6,2},{7,5},{8,12},{9,11},{10,... | collective-permute-start | bytes 405512 | tf_op jit(solution)/shard_map/ppermute | solution.py:461
  60.8 5.6 %collective-permute-start.15 = (f32[264,128]{1,0:T(8,128)S(1)}, f32[264,128]{1,0:T(8,128)S(1)}, u32[]{:S(2)}, u32[]{:S(2)}) collective-permute-start(f32[264,128]{1,0:T(8,128)S(1)} %step_pass.15.held.refs_0_), channel_id=1, source_target_pairs={{0,8},{1,17},{2,10},{3,19},{4,12},{5,21},{6,14},{7,23},{8,0},{9,25... | collective-permute-start | bytes 405512 | tf_op jit(solution)/shard_map/ppermute | solution.py:461
  66.5 6.0 %collective-permute-start.16 = (f32[264,128]{1,0:T(8,128)S(1)}, f32[264,128]{1,0:T(8,128)S(1)}, u32[]{:S(2)}, u32[]{:S(2)}) collective-permute-start(f32[264,128]{1,0:T(8,128)S(1)} %step_pass.16.held.sent), channel_id=1, source_target_pairs={{0,16},{1,9},{2,18},{3,11},{4,20},{5,13},{6,22},{7,15},{8,24},{9,1... | collective-permute-start | bytes 405512 | tf_op jit(solution)/shard_map/ppermute | solution.py:461
  69.5 7.0 %collective-permute-start.19 = (f32[384,128]{1,0:T(8,128)S(1)}, f32[384,128]{1,0:T(8,128)S(1)}, u32[]{:S(2)}, u32[]{:S(2)}) collective-permute-start(f32[384,128]{1,0:T(8,128)S(1)} %get-tuple-element.101), channel_id=1, source_target_pairs={{0,1},{1,0},{2,3},{3,2},{4,5},{5,4},{6,7},{7,6},{8,9},{9,8},{10,11... | collective-permute-start | bytes 589832 | tf_op jit(solution)/shard_map/ppermute | solution.py:451
  72.5 6.9 %collective-permute-start.17 = (f32[256,128]{1,0:T(8,128)S(1)}, f32[256,128]{1,0:T(8,128)S(1)}, u32[]{:S(2)}, u32[]{:S(2)}) collective-permute-start(f32[256,128]{1,0:T(8,128)S(1)} %get-tuple-element.97.part), channel_id=1, source_target_pairs={{0,4},{1,3},{2,6},{3,1},{4,0},{5,7},{6,2},{7,5},{8,12},{9,11},{10,... | collective-permute-start | bytes 393224 | tf_op jit(solution)/shard_map/ppermute | solution.py:461
  76.4 1.2 %collective-permute-start.18 = (f32[8,128]{1,0:T(8,128)S(1)}, f32[8,128]{1,0:T(8,128)S(1)}, u32[]{:S(2)}, u32[]{:S(2)}) collective-permute-start(f32[8,128]{1,0:T(8,128)S(1)} %get-tuple-element.98.stats), channel_id=1, source_target_pairs={{0,1},{1,0},{2,3},{3,2},{4,5},{5,4},{6,7},{7,6},{8,9},{9,8},{10,11... | collective-permute-start | bytes 12296 | tf_op jit(solution)/shard_map/ppermute | solution.py:451
  79.4 8.2 %collective-permute-start.20 = (f32[512,128]{1,0:T(8,128)S(1)}, f32[512,128]{1,0:T(8,128)S(1)}, u32[]{:S(2)}, u32[]{:S(2)}) collective-permute-start(f32[512,128]{1,0:T(8,128)S(1)} %gather_pass.3.part), channel_id=1, source_target_pairs={{0,2},{1,5},{2,0},{3,7},{4,6},{5,1},{6,4},{7,3},{8,10},{9,13},{10,... | collective-permute-start | bytes 786440 | tf_op jit(solution)/shard_map/ppermute | solution.py:461
  80.9 1.4 %collective-permute-start.21 = (f32[384,128]{1,0:T(8,128)S(1)}, f32[384,128]{1,0:T(8,128)S(1)}, u32[]{:S(2)}, u32[]{:S(2)}) collective-permute-start(f32[384,128]{1,0:T(8,128)S(1)} %get-tuple-element.106), channel_id=1, source_target_pairs={{0,1},{1,0},{2,3},{3,2},{4,5},{5,4},{6,7},{7,6},{8,9},{9,8},{10,11... | collective-permute-start | bytes 589832 | tf_op jit(solution)/shard_map/ppermute | solution.py:451
  80.9 11.1 %collective-permute-start.23 = (f32[384,256]{1,0:T(8,128)S(1)}, f32[384,256]{1,0:T(8,128)S(1)}, u32[]{:S(2)}, u32[]{:S(2)}) collective-permute-start(f32[384,256]{1,0:T(8,128)S(1)} %get-tuple-element.109), channel_id=1, source_target_pairs={{0,1},{1,2},{2,3},{3,4},{4,5},{5,6},{6,7},{7,8},{8,9},{9,10},{10,1... | collective-permute-start | bytes 1179656 | tf_op jit(solution)/shard_map/ppermute | solution.py:455
  88.8 8.0 %collective-permute-start.22 = (f32[512,128]{1,0:T(8,128)S(1)}, f32[512,128]{1,0:T(8,128)S(1)}, u32[]{:S(2)}, u32[]{:S(2)}) collective-permute-start(f32[512,128]{1,0:T(8,128)S(1)} %get-tuple-element.108.refs_0_), channel_id=1, source_target_pairs={{0,2},{1,5},{2,0},{3,7},{4,6},{5,1},{6,4},{7,3},{8,10},{9,13},{10,... | collective-permute-start | bytes 786440 | tf_op jit(solution)/shard_map/ppermute | solution.py:461
  93.2 3.7 %collective-permute-start.24 = (f32[8,128]{1,0:T(8,128)S(1)}, f32[8,128]{1,0:T(8,128)S(1)}, u32[]{:S(2)}, u32[]{:S(2)}) collective-permute-start(f32[8,128]{1,0:T(8,128)S(1)} %get-tuple-element.110.refs_0_), channel_id=1, source_target_pairs={{0,2},{1,5},{2,0},{3,7},{4,6},{5,1},{6,4},{7,3},{8,10},{9,13},{10,... | collective-permute-start | bytes 12296 | tf_op jit(solution)/shard_map/ppermute | solution.py:461
  96.9 5.4 %collective-permute-start.25 = (f32[264,128]{1,0:T(8,128)S(1)}, f32[264,128]{1,0:T(8,128)S(1)}, u32[]{:S(2)}, u32[]{:S(2)}) collective-permute-start(f32[264,128]{1,0:T(8,128)S(1)} %get-tuple-element.112.refs_0_), channel_id=1, source_target_pairs={{0,4},{1,3},{2,6},{3,1},{4,0},{5,7},{6,2},{7,5},{8,12},{9,11},{10,... | collective-permute-start | bytes 405512 | tf_op jit(solution)/shard_map/ppermute | solution.py:461
  99.3 14.0 %collective-permute-start.29 = (f32[384,128]{1,0:T(8,128)S(1)}, f32[384,128]{1,0:T(8,128)S(1)}, u32[]{:S(2)}, u32[]{:S(2)}) collective-permute-start(f32[384,128]{1,0:T(8,128)S(1)} %get-tuple-element.123), channel_id=1, source_target_pairs={{0,1},{1,0},{2,3},{3,2},{4,5},{5,4},{6,7},{7,6},{8,9},{9,8},{10,11... | collective-permute-start | bytes 589832 | tf_op jit(solution)/shard_map/ppermute | solution.py:451
  102.3 5.0 %collective-permute-start.26 = (f32[136,128]{1,0:T(8,128)S(1)}, f32[136,128]{1,0:T(8,128)S(1)}, u32[]{:S(2)}, u32[]{:S(2)}) collective-permute-start(f32[136,128]{1,0:T(8,128)S(1)} %get-tuple-element.116.refs_0_), channel_id=1, source_target_pairs={{0,8},{1,17},{2,10},{3,19},{4,12},{5,21},{6,14},{7,23},{8,0},{9,25... | collective-permute-start | bytes 208904 | tf_op jit(solution)/shard_map/ppermute | solution.py:461
  107.3 5.4 %collective-permute-start.27 = (f32[72,128]{1,0:T(8,128)S(1)}, f32[72,128]{1,0:T(8,128)S(1)}, u32[]{:S(2)}, u32[]{:S(2)}) collective-permute-start(f32[72,128]{1,0:T(8,128)S(1)} %get-tuple-element.118.sent), channel_id=1, source_target_pairs={{0,16},{1,9},{2,18},{3,11},{4,20},{5,13},{6,22},{7,15},{8,24},{9,1... | collective-permute-start | bytes 110600 | tf_op jit(solution)/shard_map/ppermute | solution.py:461
  112.7 2.4 %collective-permute-start.30 = (f32[32,128]{1,0:T(8,128)S(1)}, f32[32,128]{1,0:T(8,128)S(1)}, u32[]{:S(2)}, u32[]{:S(2)}) collective-permute-start(f32[32,128]{1,0:T(8,128)S(1)} %get-tuple-element.130), channel_id=1, source_target_pairs={{0,1},{1,0},{2,3},{3,2},{4,5},{5,4},{6,7},{7,6},{8,9},{9,8},{10,11... | collective-permute-start | bytes 49160 | tf_op jit(solution)/shard_map/ppermute | solution.py:451
  112.8 1.3 %collective-permute-start.28 = (f32[8,128]{1,0:T(8,128)S(1)}, f32[8,128]{1,0:T(8,128)S(1)}, u32[]{:S(2)}, u32[]{:S(2)}) collective-permute-start(f32[8,128]{1,0:T(8,128)S(1)} %get-tuple-element.120.stats), channel_id=1, source_target_pairs={{0,1},{1,0},{2,3},{3,2},{4,5},{5,4},{6,7},{7,6},{8,9},{9,8},{10,11... | collective-permute-start | bytes 12296 | tf_op jit(solution)/shard_map/ppermute | solution.py:451
  (9 other events, 12.2 us)

commit v13 on v12

--- a/solution.py
+++ b/solution.py
@@ -63,7 +63,7 @@
 
 
 def error_kernel(stratum, codes, count, ratings, users, *refs):
-    items, (err_b, stats, pred) = refs[1:-3], refs[-3:]
+    items, (err_b, stats, pred) = refs[:-3], refs[-3:]
     tile = ratings.shape[-1]
     grid = users.shape[0] // tile
     user_b = users[...].astype(bf16)
@@ -88,18 +88,18 @@
     stats[...] = jnp.where(row == 0, total, jnp.where(row == 1, counted, 0.0))
 
 
-def error_pass(stratum, codes, count, ratings, users, later, *items):
+def error_pass(stratum, codes, count, ratings, users, *items):
     rows, rank = users.shape
     return pl.pallas_call(
         functools.partial(error_kernel, stratum),
         out_shape=(shape(rows, rows, dtype=bf16), shape(RIDERS, rank // CORES)),
-        in_specs=[SMEM] * 2 + [VMEM] * 2 + [ANY] + [VMEM] * len(items),
+        in_specs=[SMEM] * 2 + [VMEM] * (2 + len(items)),
         out_specs=(VMEM,) * 2,
         scratch_shapes=[pltpu.VMEM((rows, rows), f32)],
         compiler_params=PARAMS,
         cost_estimate=cost(24 * rows * rows * rank, 64 * rows * rank),
         name="error_pass",
-    )(codes, count, ratings, users, later, *items)
+    )(codes, count, ratings, users, *items)
 
 
 def grad_kernel(stratum, noise_scale, err_b, user_noise, item_noise, users, *refs):
@@ -233,7 +233,7 @@
     )(feats, part)
 
 
-def prior_kernel(places, devices, feats, turned, begun, part, got, own_cols, other_cols, own_mean, other_mean, send, keep, *refs):
+def prior_kernel(places, devices, feats, turned, begun, part, got, own_cols, other_cols, stats, more_stats, own_mean, other_mean, send, keep, *refs):
     rows = own_cols.shape[0]
     half = keep.shape[0]
     place = where_am_i(devices)
@@ -246,8 +246,9 @@
     other_mean[...] = mean[rows:]
     offset[:rows, :] = (own_cols[...] - mean[:rows]).astype(bf16)
     offset[rows:, :] = (other_cols[...] - mean[rows:]).astype(bf16)
+    send[half:, :] = stats[...] + more_stats[...]
     if places is None:
-        send[...] = dot(turned[there, :], offset[...])
+        send[:half, :] = dot(turned[there, :], offset[...])
         keep[...] = dot(turned[here, :], offset[...])
         return
     old, full = refs[:2]
@@ -272,10 +273,10 @@
             ref[n * block : (n + 1) * block, :] = full[pl.ds(source, block), :]
 
 
-def prior_pass(devices, feats, turned, begun, part, got, own_cols, other_cols, places=None):
+def prior_pass(devices, feats, turned, begun, part, got, own_cols, other_cols, stats, more_stats, places=None):
     rows, width = own_cols.shape
     half = part.shape[0]
-    outs = [shape(rows, width)] * 2 + [shape(half, width)] * 2
+    outs = [shape(rows, width)] * 2 + [shape(half + RIDERS, width), shape(half, width)]
     scratch = [pltpu.VMEM((CORES * rows, width), bf16)]
     if places is not None:
         outs.append(shape(2 * half // len(places[0]), width))
@@ -283,36 +284,44 @@
     return pl.pallas_call(
         functools.partial(prior_kernel, places, devices),
         out_shape=tuple(outs),
-        in_specs=[VMEM] * 7,
+        in_specs=[VMEM] * 9,
         out_specs=(VMEM,) * len(outs),
         scratch_shapes=scratch,
         compiler_params=PARAMS,
         cost_estimate=cost(16 * rows * half * width, 16 * rows * half),
         name="prior_pass",
-    )(feats, turned, begun, part, got, own_cols, other_cols)
-
-
-def step_kernel(halving, stage, under, devices, held, got, *refs):
-    send = refs[-2] if halving else refs[-1]
-    rows = send.shape[0] - under
+    )(feats, turned, begun, part, got, own_cols, other_cols, stats, more_stats)
+
+
+def step_kernel(halving, stage, under, apart, devices, held, got, *refs):
+    outs = refs[-(1 + halving + apart) :]
+    send = outs[0]
+    rows = send.shape[0] - (0 if apart else under)
     if halving:
         bit = where_am_i(devices)[1 + stage]
-        for ref, which in ((send, 1 - bit), (refs[-1], bit)):
+        for ref, which in ((send, 1 - bit), (outs[1], bit)):
             at = rows_at(which, rows)
             ref[:rows, :] = held[at, :] + got[at, :]
     else:
         send[:rows, :] = held[:rows, :] + got[:rows, :]
     if under:
         sent, more = refs[:2]
-        send[rows:, :] = sent[sent.shape[0] - under :, :] + more[more.shape[0] - under :, :]
-
-
-def step_pass(halving, stage, devices, held, got, rows, riders=(), later=()):
+        rider = sent[sent.shape[0] - under :, :] + more[more.shape[0] - under :, :]
+        if apart:
+            outs[-1][...] = rider
+        else:
+            send[rows:, :] = rider
+
+
+def step_pass(halving, stage, devices, held, got, rows, riders=(), later=(), apart=False):
     width = held.shape[1]
     under = RIDERS if riders else 0
-    outs = [shape(rows // 2 + under, width), shape(rows // 2, width)] if halving else [shape(rows + under, width)]
-    return pl.pallas_call(
-        functools.partial(step_kernel, halving, stage, under, devices),
+    below = 0 if apart else under
+    outs = [shape(rows // 2 + below, width), shape(rows // 2, width)] if halving else [shape(rows + below, width)]
+    if apart:
+        outs.append(shape(RIDERS, width))
+    return pl.pallas_call(
+        functools.partial(step_kernel, halving, stage, under, apart, devices),
         out_shape=tuple(outs),
         in_specs=[VMEM] * (2 + len(riders)) + [ANY] * len(later),
         out_specs=(VMEM,) * len(outs),
@@ -322,25 +331,23 @@
     )(held, got, *riders, *later)
 
 
-def update_kernel(rate, held, got, sent, old, *refs):
-    new, stats = refs[-2:]
+def update_kernel(rate, held, got, old, new):
     rows = old.shape[0]
-    total = held[:rows, :] + got[:rows, :]
+    total = held[:rows, :] + got[...]
     before = old[...]
     new[...] = before + rate * (prior_prec * total - weight_decay * before)
-    stats[...] = sent[sent.shape[0] - RIDERS :, :] + got[rows:, :]
-
-
-def update_pass(rate, held, got, sent, old, later=()):
+
+
+def update_pass(rate, held, got, old):
     return pl.pallas_call(
         functools.partial(update_kernel, rate),
-        out_shape=(shape(*old.shape), shape(RIDERS, old.shape[1])),
-        in_specs=[VMEM] * 4 + [ANY] * len(later),
-        out_specs=(VMEM,) * 2,
+        out_shape=shape(*old.shape),
+        in_specs=[VMEM] * 3,
+        out_specs=VMEM,
         compiler_params=PARAMS,
         cost_estimate=cost(4 * old.size, 16 * old.size),
         name="update_pass",
-    )(held, got, sent, old, *later)
+    )(held, got, old)
 
 
 def gather_kernel(slot, devices, part, got, *refs):
@@ -403,10 +410,10 @@
     )(mine, other)
 
 
-def renew_kernel(devices, stats, more, base_u, grad_u, own_mean, other_mean, base_v, grad_v, users, *outs):
+def renew_kernel(devices, stats, base_u, grad_u, own_mean, other_mean, base_v, grad_v, users, *outs):
     core = where_am_i(devices)[0]
     width = own_mean.shape[1]
-    precision = precision_of(stats[...] + more[...])
+    precision = precision_of(stats[...])
     precision = jnp.concatenate([precision] * CORES, 1)
     parts = 1 if len(outs) == 1 else ITEM_PARTS
     rows = base_v.shape[0] // parts
@@ -423,7 +430,7 @@
         ref[...] = half_of(users, which)
 
 
-def renew_pass(devices, last, stats, more, base_u, grad_u, own_mean, *state):
+def renew_pass(devices, last, stats, base_u, grad_u, own_mean, *state):
     rows, rank = base_u.shape
     outs = [shape(rows, rank)]
     if last:
@@ -433,12 +440,12 @@
     return pl.pallas_call(
         functools.partial(renew_kernel, devices),
         out_shape=tuple(outs),
-        in_specs=[VMEM] * 8,
+        in_specs=[VMEM] * 7,
         out_specs=(VMEM,) * len(outs),
         compiler_params=PARAMS,
         cost_estimate=cost(8 * base_u.size, 32 * base_u.size),
         name="renew_pass",
-    )(stats, more, base_u, grad_u, own_mean, *state)
+    )(stats, base_u, grad_u, own_mean, *state)
 
 
 def bit_order(devices, core):
@@ -491,45 +498,50 @@
     strata = ratings.shape[1]
     feat = prior_weights.shape[0]
     rate = rate_scale / (user_factors.shape[0] * devices)
+    def errors_of(stratum, users, *items):
+        err_b, stats = error_pass(stratum, tile_index, tile_count, ratings, users, *items)
+        stats = stats + swap(stats, devices)
+        return err_b, (stats, exchange(stats, devices, stages - 1))
+
+    users, items = user_factors, [item_factors]
+    err_b, riders = errors_of(0, users, *items)
     own_turned = turn_pass(side_features)
     own_mean, other_mean, send, held, old = first_pass(
         devices, side_features, own_turned, prior_weights, user_factors
     )
-    send, held = step_pass(True, 0, devices, held, swap(send, devices), feat)
-    users, items = user_factors, [item_factors]
+    send, held = step_pass(True, 0, devices, held, swap(send, devices), feat, (), riders[:1])
     for stratum in range(strata):
         last = stratum + 1 == strata
+        state = grad_pass(stratum, err_b, user_noise, item_noise, users, *items)
         got = exchange(send, devices, 0)
-        later = send if stratum else own_turned
-        err_b, stats = error_pass(stratum, tile_index, tile_count, ratings, users, later, *items)
-        state = grad_pass(stratum, err_b, user_noise, item_noise, users, *items)
-        riders = (stats, exchange(stats, devices, 0))
-        send, held = step_pass(True, 1, devices, held, got, got.shape[0], riders)
+        if stratum:
+            riders = send, got
+        else:
+            stats = riders[0] + riders[1]
+            riders = stats, exchange(stats, devices, 0)
+        send, held = step_pass(True, 1, devices, held, got, feat // 2, riders, state[:1])
         if stratum == 0:
-            wide = swap(widen_pass(side_features, state[0]), devices)
+            wide = swap(widen_pass(side_features, send), devices)
             feats, turned = join_pass(side_features, own_turned, wide)
         for stage in range(1, stages - 1):
             got = exchange(send, devices, stage)
             rows = got.shape[0] - RIDERS
-            later = state[:1] if stage == 1 else ()
-            if last:
-                send, held = step_pass(True, stage + 1, devices, held, got, rows, (send, got), later)
-            else:
-                (send,) = step_pass(False, 0, devices, held, got, rows, (send, got), later)
-                held = send
+            apart = stage == stages - 2
+            outs = step_pass(last, stage + 1, devices, held, got, rows, (send, got), (), apart)
+            send, held = outs[0], outs[1 if last else 0]
+        stats = outs[-1]
         got = exchange(send, devices, stages - 1)
-        part, stats = update_pass(rate, held, got, send, old)
-        users, *items = renew_pass(
-            devices, last, stats, swap(stats, devices), *state[:2], own_mean, other_mean, *state[2:]
-        )
+        users, *items = renew_pass(devices, last, stats, *state[:2], own_mean, other_mean, *state[2:])
+        part = update_pass(rate, held, got, old)
         if last:
             break
         old = part
         *items, own_cols, other_cols = items
         items = [roll(rows, devices) for rows in items]
         other_cols = swap(other_cols, devices)
-        part = gather_pass(1, devices, part, exchange(part, devices, 1), [users])
+        part = gather_pass(1, devices, part, exchange(part, devices, 1))
         got = exchange(part, devices, 0)
+        err_b, riders = errors_of(stratum + 1, users, *items)
         begun = part_pass(devices, feats, part)
         own_mean, other_mean, send, held, *olds = prior_pass(
             devices,
@@ -540,6 +552,7 @@
             got,
             own_cols,
             other_cols,
+            *riders,
             final_places(devices) if stratum + 2 == strata else None,
         )
         if olds:

time: 116 us -> 119 us (1.026)
  waiting for transfers between devices: 56.8 us -> 76.9 us
  starting transfers between devices: 43.3 us -> 26.4 us
    ppermute x19 -> x20, waiting for transfers between devices: 51.4 us -> 73.9 us  [exchange(): return lax.ppermute(array, 'user', pairs)]
    ppermute x19 -> x20, starting transfers between devices: 41 us -> 24.2 us  [exchange(): return lax.ppermute(array, 'user', pairs)]
    ppermute x2, waiting for transfers between devices: 1.55 us -> 0.01 us  [roll(): lax.ppermute(array, 'user', [(i, (i + 1) % devices) for i in range(device...]
  transfers between devices with their start and end apart: 31 -> 32, of which waited for: 23 -> 21; matrix products, arithmetic and copies ran while one was open for 0% -> 0% of each run, Pallas kernels for 8% -> 6%
where the time goes in v13:
time: 119 us; the launch traced here: 118 us
  waiting for transfers between devices  76.9 us (65%)
  starting transfers between devices  26.4 us (22%)
  Pallas kernels  11.9 us (10%)
  local copies, waits for them, and re-layouts  2.25 us (2%)
    ppermute x20, waiting for transfers between devices, exchange(): return lax.ppermute(array, 'user', pairs)  73.9 us
    ppermute x20, starting transfers between devices, exchange(): return lax.ppermute(array, 'user', pairs)  24.2 us
    pallas_call x3, Pallas kernels, error_pass(): pl.pallas_call(functools.partial(error_kernel, stratum), out_shape=(shape...  3.19 us
    ppermute x10, waiting for transfers between devices, swap(): return lax.ppermute(array, 'user', [(i, i ^ 1) for i in range(devices)])  2.92 us
  transfers between devices with their start and end apart: 32, of which 21 were waited for; matrix products, arithmetic and copies ran while one was open for 0% of the time, Pallas kernels for 6%

profile of v13, /device:TPU:0, one launch (start us, length us, event | category | flops | bytes accessed | tf_op | source)
XLA Modules:
  0.0 118.4 jit_solution(12208746463784947955)
XLA Ops:
  0.6 1.1 copy-done
  3.1 1.2 first_pass.1
  6.1 1.1 collective-permute-done.1
  7.3 2.7 %collective-permute-start.2 = (f32[512,128]{1,0:T(8,128)S(1)}, f32[512,128]{1,0:T(8,128)S(1)}, u32[]{:S(2)}, u32[]{:S(2)}) collective-permute-start(f32[512,128]{1,0:T(8,128)S(1)} %get-tuple-element.70), channel_id=1, source_target_pairs={{0,2},{1,5},{2,0},{3,7},{4,6},{5,1},{6,4},{7,3},{8,10},{9,13},{10,... | collective-permute-start | bytes 786440 | tf_op jit(solution)/shard_map/ppermute | solution.py:468
  10.0 2.6 %collective-permute-start.3 = (f32[8,128]{1,0:T(8,128)S(1)}, f32[8,128]{1,0:T(8,128)S(1)}, u32[]{:S(2)}, u32[]{:S(2)}) collective-permute-start(f32[8,128]{1,0:T(8,128)S(1)} %add.12.refs_0_), channel_id=1, source_target_pairs={{0,16},{1,9},{2,18},{3,11},{4,20},{5,13},{6,22},{7,15},{8,24},{9,1... | collective-permute-start | bytes 12296 | tf_op jit(solution)/shard_map/ppermute | solution.py:468
  12.6 1.9 %collective-permute-done.3 = f32[8,128]{1,0:T(8,128)S(1)} collective-permute-done((f32[8,128]{1,0:T(8,128)S(1)}, f32[8,128]{1,0:T(8,128)S(1)}, u32[]{:S(2)}, u32[]{:S(2)}) %collective-permute-start.3) | collective-permute-done | bytes 4128 | tf_op jit(solution)/shard_map/ppermute | solution.py:468
  15.2 2.9 %collective-permute-done.4.refs_1_ = f32[8,128]{1,0:T(8,128)S(1)} collective-permute-done((f32[8,128]{1,0:T(8,128)S(1)}, f32[8,128]{1,0:T(8,128)S(1)}, u32[]{:S(2)}, u32[]{:S(2)}) %collective-permute-start.4) | collective-permute-done | bytes 4128 | tf_op jit(solution)/shard_map/ppermute | solution.py:468
  18.3 1.6 %collective-permute-start.6 = (f32[264,128]{1,0:T(8,128)S(1)}, f32[264,128]{1,0:T(8,128)S(1)}, u32[]{:S(2)}, u32[]{:S(2)}) collective-permute-start(f32[264,128]{1,0:T(8,128)S(1)} %get-tuple-element.73.later.refs_0_), channel_id=1, source_target_pairs={{0,4},{1,3},{2,6},{3,1},{4,0},{5,7},{6,2},{7,5},{8,12},{9,11},{10,... | collective-permute-start | bytes 405512 | tf_op jit(solution)/shard_map/ppermute | solution.py:468
  19.9 3.5 %collective-permute-done.6.got.refs_1_ = f32[264,128]{1,0:T(8,128)S(1)} collective-permute-done((f32[264,128]{1,0:T(8,128)S(1)}, f32[264,128]{1,0:T(8,128)S(1)}, u32[]{:S(2)}, u32[]{:S(2)}) %collective-permute-start.6) | collective-permute-done | bytes 135200 | tf_op jit(solution)/shard_map/ppermute | solution.py:468
  23.4 1.6 %collective-permute-start.7 = (f32[264,128]{1,0:T(8,128)S(1)}, f32[264,128]{1,0:T(8,128)S(1)}, u32[]{:S(2)}, u32[]{:S(2)}) collective-permute-start(f32[264,128]{1,0:T(8,128)S(1)} %step_pass.12.held.refs_0_), channel_id=1, source_target_pairs={{0,8},{1,17},{2,10},{3,19},{4,12},{5,21},{6,14},{7,23},{8,0},{9,25... | collective-permute-start | bytes 405512 | tf_op jit(solution)/shard_map/ppermute | solution.py:468
  25.1 4.1 %collective-permute-done.7.got.refs_1_ = f32[264,128]{1,0:T(8,128)S(1)} collective-permute-done((f32[264,128]{1,0:T(8,128)S(1)}, f32[264,128]{1,0:T(8,128)S(1)}, u32[]{:S(2)}, u32[]{:S(2)}) %collective-permute-start.7) | collective-permute-done | bytes 135200 | tf_op jit(solution)/shard_map/ppermute | solution.py:468
  29.2 2.4 %collective-permute-start.8 = (f32[256,128]{1,0:T(8,128)S(1)}, f32[256,128]{1,0:T(8,128)S(1)}, u32[]{:S(2)}, u32[]{:S(2)}) collective-permute-start(f32[256,128]{1,0:T(8,128)S(1)} %get-tuple-element.77.held), channel_id=1, source_target_pairs={{0,16},{1,9},{2,18},{3,11},{4,20},{5,13},{6,22},{7,15},{8,24},{9,1... | collective-permute-start | bytes 393224 | tf_op jit(solution)/shard_map/ppermute | solution.py:468
  31.9 3.2 %collective-permute-done.8.got = f32[256,128]{1,0:T(8,128)S(1)} collective-permute-done((f32[256,128]{1,0:T(8,128)S(1)}, f32[256,128]{1,0:T(8,128)S(1)}, u32[]{:S(2)}, u32[]{:S(2)}) %collective-permute-start.8) | collective-permute-done | bytes 131104 | tf_op jit(solution)/shard_map/ppermute | solution.py:468
  35.1 1.6 %collective-permute-start.9 = (f32[256,128]{1,0:T(8,128)S(1)}, f32[256,128]{1,0:T(8,128)S(1)}, u32[]{:S(2)}, u32[]{:S(2)}) collective-permute-start(f32[256,128]{1,0:T(8,128)S(1)} %update_pass.3.part.old), channel_id=1, source_target_pairs={{0,4},{1,3},{2,6},{3,1},{4,0},{5,7},{6,2},{7,5},{8,12},{9,11},{10,... | collective-permute-start | bytes 393224 | tf_op jit(solution)/shard_map/ppermute | solution.py:468
  36.7 7.5 %collective-permute-done.9.got = f32[256,128]{1,0:T(8,128)S(1)} collective-permute-done((f32[256,128]{1,0:T(8,128)S(1)}, f32[256,128]{1,0:T(8,128)S(1)}, u32[]{:S(2)}, u32[]{:S(2)}) %collective-permute-start.9) | collective-permute-done | bytes 131104 | tf_op jit(solution)/shard_map/ppermute | solution.py:468
  46.9 1.2 collective-permute-start.14
  48.8 2.5 %collective-permute-done.14.more_stats = f32[8,128]{1,0:T(8,128)S(1)} collective-permute-done((f32[8,128]{1,0:T(8,128)S(1)}, f32[8,128]{1,0:T(8,128)S(1)}, u32[]{:S(2)}, u32[]{:S(2)}) %collective-permute-start.14) | collective-permute-done | bytes 4128 | tf_op jit(solution)/shard_map/ppermute | solution.py:468
  52.2 2.0 %collective-permute-start.15 = (f32[520,128]{1,0:T(8,128)S(1)}, f32[520,128]{1,0:T(8,128)S(1)}, u32[]{:S(2)}, u32[]{:S(2)}) collective-permute-start(f32[520,128]{1,0:T(8,128)S(1)} %get-tuple-element.91.refs_0_), channel_id=1, source_target_pairs={{0,2},{1,5},{2,0},{3,7},{4,6},{5,1},{6,4},{7,3},{8,10},{9,13},{10,... | collective-permute-start | bytes 798728 | tf_op jit(solution)/shard_map/ppermute | solution.py:468
  54.7 4.0 %collective-permute-done.15.got.refs_1_ = f32[520,128]{1,0:T(8,128)S(1)} collective-permute-done((f32[520,128]{1,0:T(8,128)S(1)}, f32[520,128]{1,0:T(8,128)S(1)}, u32[]{:S(2)}, u32[]{:S(2)}) %collective-permute-start.15) | collective-permute-done | bytes 266272 | tf_op jit(solution)/shard_map/ppermute | solution.py:468
  58.9 4.9 %collective-permute-done.16.got.refs_1_ = f32[264,128]{1,0:T(8,128)S(1)} collective-permute-done((f32[264,128]{1,0:T(8,128)S(1)}, f32[264,128]{1,0:T(8,128)S(1)}, u32[]{:S(2)}, u32[]{:S(2)}) %collective-permute-start.16) | collective-permute-done | bytes 135200 | tf_op jit(solution)/shard_map/ppermute | solution.py:468
  63.8 1.2 %collective-permute-start.17 = (f32[264,128]{1,0:T(8,128)S(1)}, f32[264,128]{1,0:T(8,128)S(1)}, u32[]{:S(2)}, u32[]{:S(2)}) collective-permute-start(f32[264,128]{1,0:T(8,128)S(1)} %step_pass.15.held.refs_0_), channel_id=1, source_target_pairs={{0,8},{1,17},{2,10},{3,19},{4,12},{5,21},{6,14},{7,23},{8,0},{9,25... | collective-permute-start | bytes 405512 | tf_op jit(solution)/shard_map/ppermute | solution.py:468
  65.0 4.6 %collective-permute-done.17.got.refs_1_ = f32[264,128]{1,0:T(8,128)S(1)} collective-permute-done((f32[264,128]{1,0:T(8,128)S(1)}, f32[264,128]{1,0:T(8,128)S(1)}, u32[]{:S(2)}, u32[]{:S(2)}) %collective-permute-start.17) | collective-permute-done | bytes 135200 | tf_op jit(solution)/shard_map/ppermute | solution.py:468
  70.5 6.3 %collective-permute-done.18.got = f32[256,128]{1,0:T(8,128)S(1)} collective-permute-done((f32[256,128]{1,0:T(8,128)S(1)}, f32[256,128]{1,0:T(8,128)S(1)}, u32[]{:S(2)}, u32[]{:S(2)}) %collective-permute-start.18) | collective-permute-done | bytes 131104 | tf_op jit(solution)/shard_map/ppermute | solution.py:468
  76.9 6.0 %collective-permute-done.19.got = f32[256,128]{1,0:T(8,128)S(1)} collective-permute-done((f32[256,128]{1,0:T(8,128)S(1)}, f32[256,128]{1,0:T(8,128)S(1)}, u32[]{:S(2)}, u32[]{:S(2)}) %collective-permute-start.19) | collective-permute-done | bytes 131104 | tf_op jit(solution)/shard_map/ppermute | solution.py:468
  82.9 4.4 %collective-permute-start.20 = (f32[512,128]{1,0:T(8,128)S(1)}, f32[512,128]{1,0:T(8,128)S(1)}, u32[]{:S(2)}, u32[]{:S(2)}) collective-permute-start(f32[512,128]{1,0:T(8,128)S(1)} %gather_pass.3.part), channel_id=1, source_target_pairs={{0,2},{1,5},{2,0},{3,7},{4,6},{5,1},{6,4},{7,3},{8,10},{9,13},{10,... | collective-permute-start | bytes 786440 | tf_op jit(solution)/shard_map/ppermute | solution.py:468
  90.1 4.1 %collective-permute-done.25.more_stats = f32[8,128]{1,0:T(8,128)S(1)} collective-permute-done((f32[8,128]{1,0:T(8,128)S(1)}, f32[8,128]{1,0:T(8,128)S(1)}, u32[]{:S(2)}, u32[]{:S(2)}) %collective-permute-start.25) | collective-permute-done | bytes 4128 | tf_op jit(solution)/shard_map/ppermute | solution.py:468
  94.3 1.2 %prior_pass.3 = (f32[384,128]{1,0:T(8,128)S(1)}, f32[384,128]{1,0:T(8,128)S(1)}, f32[520,128]{1,0:T(8,128)S(1)}, f32[512,128]{1,0:T(8,128)S(1)}, f32[64,128]{1,0:T(8,128)S(1)}) custom-call(bf16[768,1024]{1,0:T(8,128)(2,1)S(1)} %get-tuple-element.74.feats, bf16[1024,768]{1,0:T(8,128)(2,1)S(1)} %get-tuple-element.75.turned, f32[768,128]{1,0:T(8,128)S(1)} %part_pass.3.begun, ...), custom_call_target="tpu_custom_call" | custom-call | flops 402653184 | bytes 3145728 | tf_op jit(solution)/shard_map/prior_pass/pallas_call | solution.py:284
  96.1 5.8 %collective-permute-done.26.got.refs_1_ = f32[520,128]{1,0:T(8,128)S(1)} collective-permute-done((f32[520,128]{1,0:T(8,128)S(1)}, f32[520,128]{1,0:T(8,128)S(1)}, u32[]{:S(2)}, u32[]{:S(2)}) %collective-permute-start.26) | collective-permute-done | bytes 266272 | tf_op jit(solution)/shard_map/ppermute | solution.py:468
  102.0 1.1 collective-permute-start.27
  103.1 4.0 %collective-permute-done.27.got.refs_1_ = f32[264,128]{1,0:T(8,128)S(1)} collective-permute-done((f32[264,128]{1,0:T(8,128)S(1)}, f32[264,128]{1,0:T(8,128)S(1)}, u32[]{:S(2)}, u32[]{:S(2)}) %collective-permute-start.27) | collective-permute-done | bytes 135200 | tf_op jit(solution)/shard_map/ppermute | solution.py:468
  107.2 4.4 %collective-permute-done.28.got.refs_1_ = f32[136,128]{1,0:T(8,128)S(1)} collective-permute-done((f32[136,128]{1,0:T(8,128)S(1)}, f32[136,128]{1,0:T(8,128)S(1)}, u32[]{:S(2)}, u32[]{:S(2)}) %collective-permute-start.28) | collective-permute-done | bytes 69664 | tf_op jit(solution)/shard_map/ppermute | solution.py:468
  112.1 4.4 %collective-permute-done.30.got = f32[64,128]{1,0:T(8,128)S(1)} collective-permute-done((f32[64,128]{1,0:T(8,128)S(1)}, f32[64,128]{1,0:T(8,128)S(1)}, u32[]{:S(2)}, u32[]{:S(2)}) %collective-permute-start.30) | collective-permute-done | bytes 32800 | tf_op jit(solution)/shard_map/ppermute | solution.py:468
  (91 shorter events, 16.5 us)
Async XLA Ops:
  4.3 2.9 %collective-permute-start = (f32[1024,128]{1,0:T(8,128)S(1)}, f32[1024,128]{1,0:T(8,128)S(1)}, u32[]{:S(2)}, u32[]{:S(2)}) collective-permute-start(f32[1024,128]{1,0:T(8,128)S(1)} %get-tuple-element.67), channel_id=1, source_target_pairs={{0,1},{1,0},{2,3},{3,2},{4,5},{5,4},{6,7},{7,6},{8,9},{9,8},{10,11... | collective-permute-start | bytes 1572872 | tf_op jit(solution)/shard_map/ppermute | solution.py:458
  6.0 1.2 %collective-permute-start.1 = (f32[8,128]{1,0:T(8,128)S(1)}, f32[8,128]{1,0:T(8,128)S(1)}, u32[]{:S(2)}, u32[]{:S(2)}) collective-permute-start(f32[8,128]{1,0:T(8,128)S(1)} %get-tuple-element.68), channel_id=1, source_target_pairs={{0,1},{1,0},{2,3},{3,2},{4,5},{5,4},{6,7},{7,6},{8,9},{9,8},{10,11... | collective-permute-start | bytes 12296 | tf_op jit(solution)/shard_map/ppermute | solution.py:458
  7.3 10.8 %collective-permute-start.2 = (f32[512,128]{1,0:T(8,128)S(1)}, f32[512,128]{1,0:T(8,128)S(1)}, u32[]{:S(2)}, u32[]{:S(2)}) collective-permute-start(f32[512,128]{1,0:T(8,128)S(1)} %get-tuple-element.70), channel_id=1, source_target_pairs={{0,2},{1,5},{2,0},{3,7},{4,6},{5,1},{6,4},{7,3},{8,10},{9,13},{10,... | collective-permute-start | bytes 786440 | tf_op jit(solution)/shard_map/ppermute | solution.py:468
  10.0 4.5 %collective-permute-start.3 = (f32[8,128]{1,0:T(8,128)S(1)}, f32[8,128]{1,0:T(8,128)S(1)}, u32[]{:S(2)}, u32[]{:S(2)}) collective-permute-start(f32[8,128]{1,0:T(8,128)S(1)} %add.12.refs_0_), channel_id=1, source_target_pairs={{0,16},{1,9},{2,18},{3,11},{4,20},{5,13},{6,22},{7,15},{8,24},{9,1... | collective-permute-start | bytes 12296 | tf_op jit(solution)/shard_map/ppermute | solution.py:468
  14.5 3.6 %collective-permute-start.4 = (f32[8,128]{1,0:T(8,128)S(1)}, f32[8,128]{1,0:T(8,128)S(1)}, u32[]{:S(2)}, u32[]{:S(2)}) collective-permute-start(f32[8,128]{1,0:T(8,128)S(1)} %add.13.refs_0_), channel_id=1, source_target_pairs={{0,2},{1,5},{2,0},{3,7},{4,6},{5,1},{6,4},{7,3},{8,10},{9,13},{10,... | collective-permute-start | bytes 12296 | tf_op jit(solution)/shard_map/ppermute | solution.py:468
  18.3 29.8 %collective-permute-start.5 = (f32[384,1024]{1,0:T(8,128)S(1)}, f32[384,1024]{1,0:T(8,128)S(1)}, u32[]{:S(2)}, u32[]{:S(2)}) collective-permute-start(f32[384,1024]{1,0:T(8,128)S(1)} %widen_pass.1), channel_id=1, source_target_pairs={{0,1},{1,0},{2,3},{3,2},{4,5},{5,4},{6,7},{7,6},{8,9},{9,8},{10,11... | collective-permute-start | bytes 4718600 | tf_op jit(solution)/shard_map/ppermute | solution.py:458
  18.3 5.1 %collective-permute-start.6 = (f32[264,128]{1,0:T(8,128)S(1)}, f32[264,128]{1,0:T(8,128)S(1)}, u32[]{:S(2)}, u32[]{:S(2)}) collective-permute-start(f32[264,128]{1,0:T(8,128)S(1)} %get-tuple-element.73.later.refs_0_), channel_id=1, source_target_pairs={{0,4},{1,3},{2,6},{3,1},{4,0},{5,7},{6,2},{7,5},{8,12},{9,11},{10,... | collective-permute-start | bytes 405512 | tf_op jit(solution)/shard_map/ppermute | solution.py:468
  23.4 5.7 %collective-permute-start.7 = (f32[264,128]{1,0:T(8,128)S(1)}, f32[264,128]{1,0:T(8,128)S(1)}, u32[]{:S(2)}, u32[]{:S(2)}) collective-permute-start(f32[264,128]{1,0:T(8,128)S(1)} %step_pass.12.held.refs_0_), channel_id=1, source_target_pairs={{0,8},{1,17},{2,10},{3,19},{4,12},{5,21},{6,14},{7,23},{8,0},{9,25... | collective-permute-start | bytes 405512 | tf_op jit(solution)/shard_map/ppermute | solution.py:468
  29.2 5.9 %collective-permute-start.8 = (f32[256,128]{1,0:T(8,128)S(1)}, f32[256,128]{1,0:T(8,128)S(1)}, u32[]{:S(2)}, u32[]{:S(2)}) collective-permute-start(f32[256,128]{1,0:T(8,128)S(1)} %get-tuple-element.77.held), channel_id=1, source_target_pairs={{0,16},{1,9},{2,18},{3,11},{4,20},{5,13},{6,22},{7,15},{8,24},{9,1... | collective-permute-start | bytes 393224 | tf_op jit(solution)/shard_map/ppermute | solution.py:468
  31.8 12.6 %collective-permute-start.12 = (f32[384,256]{1,0:T(8,128)S(1)}, f32[384,256]{1,0:T(8,128)S(1)}, u32[]{:S(2)}, u32[]{:S(2)}) collective-permute-start(f32[384,256]{1,0:T(8,128)S(1)} %get-tuple-element.88), channel_id=1, source_target_pairs={{0,1},{1,2},{2,3},{3,4},{4,5},{5,6},{6,7},{7,8},{8,9},{9,10},{10,1... | collective-permute-start | bytes 1179656 | tf_op jit(solution)/shard_map/ppermute | solution.py:462
  35.1 9.1 %collective-permute-start.9 = (f32[256,128]{1,0:T(8,128)S(1)}, f32[256,128]{1,0:T(8,128)S(1)}, u32[]{:S(2)}, u32[]{:S(2)}) collective-permute-start(f32[256,128]{1,0:T(8,128)S(1)} %update_pass.3.part.old), channel_id=1, source_target_pairs={{0,4},{1,3},{2,6},{3,1},{4,0},{5,7},{6,2},{7,5},{8,12},{9,11},{10,... | collective-permute-start | bytes 393224 | tf_op jit(solution)/shard_map/ppermute | solution.py:468
  44.2 7.1 %collective-permute-start.10 = (f32[512,128]{1,0:T(8,128)S(1)}, f32[512,128]{1,0:T(8,128)S(1)}, u32[]{:S(2)}, u32[]{:S(2)}) collective-permute-start(f32[512,128]{1,0:T(8,128)S(1)} %gather_pass.2.part), channel_id=1, source_target_pairs={{0,2},{1,5},{2,0},{3,7},{4,6},{5,1},{6,4},{7,3},{8,10},{9,13},{10,... | collective-permute-start | bytes 786440 | tf_op jit(solution)/shard_map/ppermute | solution.py:468
  44.3 4.5 %collective-permute-start.11 = (f32[384,128]{1,0:T(8,128)S(1)}, f32[384,128]{1,0:T(8,128)S(1)}, u32[]{:S(2)}, u32[]{:S(2)}) collective-permute-start(f32[384,128]{1,0:T(8,128)S(1)} %get-tuple-element.86), channel_id=1, source_target_pairs={{0,1},{1,0},{2,3},{3,2},{4,5},{5,4},{6,7},{7,6},{8,9},{9,8},{10,11... | collective-permute-start | bytes 589832 | tf_op jit(solution)/shard_map/ppermute | solution.py:458
  45.5 1.4 %collective-permute-start.13 = (f32[8,128]{1,0:T(8,128)S(1)}, f32[8,128]{1,0:T(8,128)S(1)}, u32[]{:S(2)}, u32[]{:S(2)}) collective-permute-start(f32[8,128]{1,0:T(8,128)S(1)} %get-tuple-element.89), channel_id=1, source_target_pairs={{0,1},{1,0},{2,3},{3,2},{4,5},{5,4},{6,7},{7,6},{8,9},{9,8},{10,11... | collective-permute-start | bytes 12296 | tf_op jit(solution)/shard_map/ppermute | solution.py:458
  46.9 4.5 %collective-permute-start.14 = (f32[8,128]{1,0:T(8,128)S(1)}, f32[8,128]{1,0:T(8,128)S(1)}, u32[]{:S(2)}, u32[]{:S(2)}) collective-permute-start(f32[8,128]{1,0:T(8,128)S(1)} %add.14.stats), channel_id=1, source_target_pairs={{0,16},{1,9},{2,18},{3,11},{4,20},{5,13},{6,22},{7,15},{8,24},{9,1... | collective-permute-start | bytes 12296 | tf_op jit(solution)/shard_map/ppermute | solution.py:468
  52.2 6.5 %collective-permute-start.15 = (f32[520,128]{1,0:T(8,128)S(1)}, f32[520,128]{1,0:T(8,128)S(1)}, u32[]{:S(2)}, u32[]{:S(2)}) collective-permute-start(f32[520,128]{1,0:T(8,128)S(1)} %get-tuple-element.91.refs_0_), channel_id=1, source_target_pairs={{0,2},{1,5},{2,0},{3,7},{4,6},{5,1},{6,4},{7,3},{8,10},{9,13},{10,... | collective-permute-start | bytes 798728 | tf_op jit(solution)/shard_map/ppermute | solution.py:468
  58.7 5.1 %collective-permute-start.16 = (f32[264,128]{1,0:T(8,128)S(1)}, f32[264,128]{1,0:T(8,128)S(1)}, u32[]{:S(2)}, u32[]{:S(2)}) collective-permute-start(f32[264,128]{1,0:T(8,128)S(1)} %get-tuple-element.95.refs_0_), channel_id=1, source_target_pairs={{0,4},{1,3},{2,6},{3,1},{4,0},{5,7},{6,2},{7,5},{8,12},{9,11},{10,... | collective-permute-start | bytes 405512 | tf_op jit(solution)/shard_map/ppermute | solution.py:468
  58.8 11.4 %collective-permute-start.21 = (f32[384,128]{1,0:T(8,128)S(1)}, f32[384,128]{1,0:T(8,128)S(1)}, u32[]{:S(2)}, u32[]{:S(2)}) collective-permute-start(f32[384,128]{1,0:T(8,128)S(1)} %get-tuple-element.100), channel_id=1, source_target_pairs={{0,1},{1,0},{2,3},{3,2},{4,5},{5,4},{6,7},{7,6},{8,9},{9,8},{10,11... | collective-permute-start | bytes 589832 | tf_op jit(solution)/shard_map/ppermute | solution.py:458
  63.8 5.8 %collective-permute-start.17 = (f32[264,128]{1,0:T(8,128)S(1)}, f32[264,128]{1,0:T(8,128)S(1)}, u32[]{:S(2)}, u32[]{:S(2)}) collective-permute-start(f32[264,128]{1,0:T(8,128)S(1)} %step_pass.15.held.refs_0_), channel_id=1, source_target_pairs={{0,8},{1,17},{2,10},{3,19},{4,12},{5,21},{6,14},{7,23},{8,0},{9,25... | collective-permute-start | bytes 405512 | tf_op jit(solution)/shard_map/ppermute | solution.py:468
  69.6 7.2 %collective-permute-start.18 = (f32[256,128]{1,0:T(8,128)S(1)}, f32[256,128]{1,0:T(8,128)S(1)}, u32[]{:S(2)}, u32[]{:S(2)}) collective-permute-start(f32[256,128]{1,0:T(8,128)S(1)} %get-tuple-element.96.held), channel_id=1, source_target_pairs={{0,16},{1,9},{2,18},{3,11},{4,20},{5,13},{6,22},{7,15},{8,24},{9,1... | collective-permute-start | bytes 393224 | tf_op jit(solution)/shard_map/ppermute | solution.py:468
  70.5 16.8 %collective-permute-start.23 = (f32[384,256]{1,0:T(8,128)S(1)}, f32[384,256]{1,0:T(8,128)S(1)}, u32[]{:S(2)}, u32[]{:S(2)}) collective-permute-start(f32[384,256]{1,0:T(8,128)S(1)} %get-tuple-element.106), channel_id=1, source_target_pairs={{0,1},{1,2},{2,3},{3,4},{4,5},{5,6},{6,7},{7,8},{8,9},{9,10},{10,1... | collective-permute-start | bytes 1179656 | tf_op jit(solution)/shard_map/ppermute | solution.py:462
  76.8 6.0 %collective-permute-start.19 = (f32[256,128]{1,0:T(8,128)S(1)}, f32[256,128]{1,0:T(8,128)S(1)}, u32[]{:S(2)}, u32[]{:S(2)}) collective-permute-start(f32[256,128]{1,0:T(8,128)S(1)} %update_pass.4.part), channel_id=1, source_target_pairs={{0,4},{1,3},{2,6},{3,1},{4,0},{5,7},{6,2},{7,5},{8,12},{9,11},{10,... | collective-permute-start | bytes 393224 | tf_op jit(solution)/shard_map/ppermute | solution.py:468
  82.9 11.4 %collective-permute-start.20 = (f32[512,128]{1,0:T(8,128)S(1)}, f32[512,128]{1,0:T(8,128)S(1)}, u32[]{:S(2)}, u32[]{:S(2)}) collective-permute-start(f32[512,128]{1,0:T(8,128)S(1)} %gather_pass.3.part), channel_id=1, source_target_pairs={{0,2},{1,5},{2,0},{3,7},{4,6},{5,1},{6,4},{7,3},{8,10},{9,13},{10,... | collective-permute-start | bytes 786440 | tf_op jit(solution)/shard_map/ppermute | solution.py:468
  87.3 2.9 %collective-permute-start.22 = (f32[384,128]{1,0:T(8,128)S(1)}, f32[384,128]{1,0:T(8,128)S(1)}, u32[]{:S(2)}, u32[]{:S(2)}) collective-permute-start(f32[384,128]{1,0:T(8,128)S(1)} %get-tuple-element.104), channel_id=1, source_target_pairs={{0,1},{1,0},{2,3},{3,2},{4,5},{5,4},{6,7},{7,6},{8,9},{9,8},{10,11... | collective-permute-start | bytes 589832 | tf_op jit(solution)/shard_map/ppermute | solution.py:458
  88.4 1.4 %collective-permute-start.24 = (f32[8,128]{1,0:T(8,128)S(1)}, f32[8,128]{1,0:T(8,128)S(1)}, u32[]{:S(2)}, u32[]{:S(2)}) collective-permute-start(f32[8,128]{1,0:T(8,128)S(1)} %get-tuple-element.107), channel_id=1, source_target_pairs={{0,1},{1,0},{2,3},{3,2},{4,5},{5,4},{6,7},{7,6},{8,9},{9,8},{10,11... | collective-permute-start | bytes 12296 | tf_op jit(solution)/shard_map/ppermute | solution.py:458
  89.8 4.5 %collective-permute-start.25 = (f32[8,128]{1,0:T(8,128)S(1)}, f32[8,128]{1,0:T(8,128)S(1)}, u32[]{:S(2)}, u32[]{:S(2)}) collective-permute-start(f32[8,128]{1,0:T(8,128)S(1)} %add.15.stats), channel_id=1, source_target_pairs={{0,16},{1,9},{2,18},{3,11},{4,20},{5,13},{6,22},{7,15},{8,24},{9,1... | collective-permute-start | bytes 12296 | tf_op jit(solution)/shard_map/ppermute | solution.py:468
  95.5 6.5 %collective-permute-start.26 = (f32[520,128]{1,0:T(8,128)S(1)}, f32[520,128]{1,0:T(8,128)S(1)}, u32[]{:S(2)}, u32[]{:S(2)}) collective-permute-start(f32[520,128]{1,0:T(8,128)S(1)} %get-tuple-element.109.refs_0_), channel_id=1, source_target_pairs={{0,2},{1,5},{2,0},{3,7},{4,6},{5,1},{6,4},{7,3},{8,10},{9,13},{10,... | collective-permute-start | bytes 798728 | tf_op jit(solution)/shard_map/ppermute | solution.py:468
  102.0 5.1 %collective-permute-start.27 = (f32[264,128]{1,0:T(8,128)S(1)}, f32[264,128]{1,0:T(8,128)S(1)}, u32[]{:S(2)}, u32[]{:S(2)}) collective-permute-start(f32[264,128]{1,0:T(8,128)S(1)} %get-tuple-element.113.refs_0_), channel_id=1, source_target_pairs={{0,4},{1,3},{2,6},{3,1},{4,0},{5,7},{6,2},{7,5},{8,12},{9,11},{10,... | collective-permute-start | bytes 405512 | tf_op jit(solution)/shard_map/ppermute | solution.py:468
  103.1 13.5 %collective-permute-start.29 = (f32[384,128]{1,0:T(8,128)S(1)}, f32[384,128]{1,0:T(8,128)S(1)}, u32[]{:S(2)}, u32[]{:S(2)}) collective-permute-start(f32[384,128]{1,0:T(8,128)S(1)} %get-tuple-element.119), channel_id=1, source_target_pairs={{0,1},{1,0},{2,3},{3,2},{4,5},{5,4},{6,7},{7,6},{8,9},{9,8},{10,11... | collective-permute-start | bytes 589832 | tf_op jit(solution)/shard_map/ppermute | solution.py:458
  107.1 4.4 %collective-permute-start.28 = (f32[136,128]{1,0:T(8,128)S(1)}, f32[136,128]{1,0:T(8,128)S(1)}, u32[]{:S(2)}, u32[]{:S(2)}) collective-permute-start(f32[136,128]{1,0:T(8,128)S(1)} %get-tuple-element.115.refs_0_), channel_id=1, source_target_pairs={{0,8},{1,17},{2,10},{3,19},{4,12},{5,21},{6,14},{7,23},{8,0},{9,25... | collective-permute-start | bytes 208904 | tf_op jit(solution)/shard_map/ppermute | solution.py:468
  111.6 5.0 %collective-permute-start.30 = (f32[64,128]{1,0:T(8,128)S(1)}, f32[64,128]{1,0:T(8,128)S(1)}, u32[]{:S(2)}, u32[]{:S(2)}) collective-permute-start(f32[64,128]{1,0:T(8,128)S(1)} %get-tuple-element.125), channel_id=1, source_target_pairs={{0,16},{1,9},{2,18},{3,11},{4,20},{5,13},{6,22},{7,15},{8,24},{9,1... | collective-permute-start | bytes 98312 | tf_op jit(solution)/shard_map/ppermute | solution.py:468
  116.6 1.2 %collective-permute-start.31 = (f32[32,128]{1,0:T(8,128)S(1)}, f32[32,128]{1,0:T(8,128)S(1)}, u32[]{:S(2)}, u32[]{:S(2)}) collective-permute-start(f32[32,128]{1,0:T(8,128)S(1)} %get-tuple-element.128), channel_id=1, source_target_pairs={{0,1},{1,0},{2,3},{3,2},{4,5},{5,4},{6,7},{7,6},{8,9},{9,8},{10,11... | collective-permute-start | bytes 49160 | tf_op jit(solution)/shard_map/ppermute | solution.py:458
  (10 other events, 33.5 us)

commit v14 on v12

--- a/solution.py
+++ b/solution.py
@@ -233,7 +233,7 @@
     )(feats, part)
 
 
-def prior_kernel(places, devices, feats, turned, begun, part, got, own_cols, other_cols, own_mean, other_mean, send, keep, *refs):
+def prior_kernel(places, devices, feats, turned, begun, part, got, own_cols, other_cols, later, own_mean, other_mean, send, keep, *refs):
     rows = own_cols.shape[0]
     half = keep.shape[0]
     place = where_am_i(devices)
@@ -272,7 +272,7 @@
             ref[n * block : (n + 1) * block, :] = full[pl.ds(source, block), :]
 
 
-def prior_pass(devices, feats, turned, begun, part, got, own_cols, other_cols, places=None):
+def prior_pass(devices, feats, turned, begun, part, got, own_cols, other_cols, later, places=None):
     rows, width = own_cols.shape
     half = part.shape[0]
     outs = [shape(rows, width)] * 2 + [shape(half, width)] * 2
@@ -283,13 +283,13 @@
     return pl.pallas_call(
         functools.partial(prior_kernel, places, devices),
         out_shape=tuple(outs),
-        in_specs=[VMEM] * 7,
+        in_specs=[VMEM] * 7 + [ANY],
         out_specs=(VMEM,) * len(outs),
         scratch_shapes=scratch,
         compiler_params=PARAMS,
         cost_estimate=cost(16 * rows * half * width, 16 * rows * half),
         name="prior_pass",
-    )(feats, turned, begun, part, got, own_cols, other_cols)
+    )(feats, turned, begun, part, got, own_cols, other_cols, later)
 
 
 def step_kernel(halving, stage, under, devices, held, got, *refs):
@@ -505,9 +505,6 @@
         state = grad_pass(stratum, err_b, user_noise, item_noise, users, *items)
         riders = (stats, exchange(stats, devices, 0))
         send, held = step_pass(True, 1, devices, held, got, got.shape[0], riders)
-        if stratum == 0:
-            wide = swap(widen_pass(side_features, state[0]), devices)
-            feats, turned = join_pass(side_features, own_turned, wide)
         for stage in range(1, stages - 1):
             got = exchange(send, devices, stage)
             rows = got.shape[0] - RIDERS
@@ -517,6 +514,9 @@
             else:
                 (send,) = step_pass(False, 0, devices, held, got, rows, (send, got), later)
                 held = send
+            if stratum == 0 and stage == 1:
+                wide = swap(widen_pass(side_features, send), devices)
+                feats, turned = join_pass(side_features, own_turned, wide)
         got = exchange(send, devices, stages - 1)
         part, stats = update_pass(rate, held, got, send, old)
         users, *items = renew_pass(
@@ -540,6 +540,7 @@
             got,
             own_cols,
             other_cols,
+            items[0],
             final_places(devices) if stratum + 2 == strata else None,
         )
         if olds:

time: 116 us -> 112 us (0.966)
  starting transfers between devices: 43.3 us -> 29.3 us
  waiting for transfers between devices: 56.8 us -> 67.6 us
    ppermute x19, starting transfers between devices: 41 us -> 26.7 us  [exchange(): return lax.ppermute(array, 'user', pairs)]
    ppermute x19, waiting for transfers between devices: 51.4 us -> 62.9 us  [exchange(): return lax.ppermute(array, 'user', pairs)]
  transfers between devices with their start and end apart: 31 -> 31, of which waited for: 23 -> 22; matrix products, arithmetic and copies ran while one was open for 0% -> 0% of each run, Pallas kernels for 8% -> 7%
where the time goes in v14:
time: 112 us
  waiting for transfers between devices  67.6 us (60%)
  starting transfers between devices  29.3 us (26%)
  Pallas kernels  11.9 us (11%)
  local copies, waits for them, and re-layouts  2.25 us (2%)
    ppermute x19, waiting for transfers between devices, exchange(): return lax.ppermute(array, 'user', pairs)  62.9 us
    ppermute x19, starting transfers between devices, exchange(): return lax.ppermute(array, 'user', pairs)  26.7 us
    ppermute x10, waiting for transfers between devices, swap(): return lax.ppermute(array, 'user', [(i, i ^ 1) for i in range(devices)])  3.72 us
    pallas_call x3, Pallas kernels, error_pass(): pl.pallas_call(functools.partial(error_kernel, stratum), out_shape=(shape...  3.19 us
    ppermute x10, starting transfers between devices, swap(): return lax.ppermute(array, 'user', [(i, i ^ 1) for i in range(devices)])  2.39 us
    unnamed x21, local copies, waits for them, and re-layouts  2.25 us
  transfers between devices with their start and end apart: 31, of which 22 were waited for; matrix products, arithmetic and copies ran while one was open for 0% of the time, Pallas kernels for 7%

profile of v14, /device:TPU:0, one launch (start us, length us, event | category | flops | bytes accessed | tf_op | source)
XLA Modules:
  0.0 112.0 jit_solution(7837742986966179703)
XLA Ops:
  0.6 1.1 %copy-done = bf16[384,1024]{1,0:T(8,128)(2,1)S(1)} copy-done((bf16[384,1024]{1,0:T(8,128)(2,1)S(1)}, bf16[384,1024]{1,0:T(8,128)(2,1)}, u32[]{:S(2)}) %copy-start) | copy-done | bytes 786456
  3.1 1.2 %first_pass.1 = (f32[384,128]{1,0:T(8,128)S(1)}, f32[384,128]{1,0:T(8,128)S(1)}, f32[1024,128]{1,0:T(8,128)S(1)}, f32[1024,128]{1,0:T(8,128)S(1)}, f32[256,128]{1,0:T(8,128)S(1)}) custom-call(bf16[384,1024]{1,0:T(8,128)(2,1)S(1)} %copy-done, bf16[1024,384]{1,0:T(8,128)(2,1)S(1)} %turn_pass.1.turned.refs_0_.own_turned, f32[1024,256]{1,0:T(8,128)S(1)} %copy-done.5, ...), custom_call_target="tpu_custom_call" | custom-call | flops 402653184 | bytes 2097152 | tf_op jit(solution)/shard_map/first_pass/pallas_call | solution.py:167
  4.8 1.5 %collective-permute-done.got = f32[1024,128]{1,0:T(8,128)S(1)} collective-permute-done((f32[1024,128]{1,0:T(8,128)S(1)}, f32[1024,128]{1,0:T(8,128)S(1)}, u32[]{:S(2)}, u32[]{:S(2)}) %collective-permute-start) | collective-permute-done | bytes 524320 | tf_op jit(solution)/shard_map/ppermute | solution.py:451
  6.4 2.9 %collective-permute-start.1 = (f32[512,128]{1,0:T(8,128)S(1)}, f32[512,128]{1,0:T(8,128)S(1)}, u32[]{:S(2)}, u32[]{:S(2)}) collective-permute-start(f32[512,128]{1,0:T(8,128)S(1)} %get-tuple-element.70), channel_id=1, source_target_pairs={{0,2},{1,5},{2,0},{3,7},{4,6},{5,1},{6,4},{7,3},{8,10},{9,13},{10,... | collective-permute-start | bytes 786440 | tf_op jit(solution)/shard_map/ppermute | solution.py:461
  9.4 1.1 error_pass.3
  10.6 3.6 %collective-permute-done.2.refs_1_ = f32[8,128]{1,0:T(8,128)S(1)} collective-permute-done((f32[8,128]{1,0:T(8,128)S(1)}, f32[8,128]{1,0:T(8,128)S(1)}, u32[]{:S(2)}, u32[]{:S(2)}) %collective-permute-start.2) | collective-permute-done | bytes 4128 | tf_op jit(solution)/shard_map/ppermute | solution.py:461
  14.2 1.7 %collective-permute-start.3 = (f32[264,128]{1,0:T(8,128)S(1)}, f32[264,128]{1,0:T(8,128)S(1)}, u32[]{:S(2)}, u32[]{:S(2)}) collective-permute-start(f32[264,128]{1,0:T(8,128)S(1)} %get-tuple-element.73.refs_0_), channel_id=1, source_target_pairs={{0,4},{1,3},{2,6},{3,1},{4,0},{5,7},{6,2},{7,5},{8,12},{9,11},{10,... | collective-permute-start | bytes 405512 | tf_op jit(solution)/shard_map/ppermute | solution.py:461
  16.4 2.8 %collective-permute-done.3.got.refs_1_ = f32[264,128]{1,0:T(8,128)S(1)} collective-permute-done((f32[264,128]{1,0:T(8,128)S(1)}, f32[264,128]{1,0:T(8,128)S(1)}, u32[]{:S(2)}, u32[]{:S(2)}) %collective-permute-start.3) | collective-permute-done | bytes 135200 | tf_op jit(solution)/shard_map/ppermute | solution.py:461
  19.5 1.8 %collective-permute-start.5 = (f32[264,128]{1,0:T(8,128)S(1)}, f32[264,128]{1,0:T(8,128)S(1)}, u32[]{:S(2)}, u32[]{:S(2)}) collective-permute-start(f32[264,128]{1,0:T(8,128)S(1)} %step_pass.12.later.held.refs_0_), channel_id=1, source_target_pairs={{0,8},{1,17},{2,10},{3,19},{4,12},{5,21},{6,14},{7,23},{8,0},{9,25... | collective-permute-start | bytes 405512 | tf_op jit(solution)/shard_map/ppermute | solution.py:461
  21.3 4.7 %collective-permute-done.5.got.refs_1_ = f32[264,128]{1,0:T(8,128)S(1)} collective-permute-done((f32[264,128]{1,0:T(8,128)S(1)}, f32[264,128]{1,0:T(8,128)S(1)}, u32[]{:S(2)}, u32[]{:S(2)}) %collective-permute-start.5) | collective-permute-done | bytes 135200 | tf_op jit(solution)/shard_map/ppermute | solution.py:461
  26.0 2.2 %collective-permute-start.6 = (f32[264,128]{1,0:T(8,128)S(1)}, f32[264,128]{1,0:T(8,128)S(1)}, u32[]{:S(2)}, u32[]{:S(2)}) collective-permute-start(f32[264,128]{1,0:T(8,128)S(1)} %step_pass.13.held.sent), channel_id=1, source_target_pairs={{0,16},{1,9},{2,18},{3,11},{4,20},{5,13},{6,22},{7,15},{8,24},{9,1... | collective-permute-start | bytes 405512 | tf_op jit(solution)/shard_map/ppermute | solution.py:461
  28.2 4.5 %collective-permute-done.6.got = f32[264,128]{1,0:T(8,128)S(1)} collective-permute-done((f32[264,128]{1,0:T(8,128)S(1)}, f32[264,128]{1,0:T(8,128)S(1)}, u32[]{:S(2)}, u32[]{:S(2)}) %collective-permute-start.6) | collective-permute-done | bytes 135200 | tf_op jit(solution)/shard_map/ppermute | solution.py:461
  32.8 1.9 %collective-permute-start.7 = (f32[256,128]{1,0:T(8,128)S(1)}, f32[256,128]{1,0:T(8,128)S(1)}, u32[]{:S(2)}, u32[]{:S(2)}) collective-permute-start(f32[256,128]{1,0:T(8,128)S(1)} %get-tuple-element.79.part.old), channel_id=1, source_target_pairs={{0,4},{1,3},{2,6},{3,1},{4,0},{5,7},{6,2},{7,5},{8,12},{9,11},{10,... | collective-permute-start | bytes 393224 | tf_op jit(solution)/shard_map/ppermute | solution.py:461
  35.1 2.7 %collective-permute-done.7.got = f32[256,128]{1,0:T(8,128)S(1)} collective-permute-done((f32[256,128]{1,0:T(8,128)S(1)}, f32[256,128]{1,0:T(8,128)S(1)}, u32[]{:S(2)}, u32[]{:S(2)}) %collective-permute-start.7) | collective-permute-done | bytes 131104 | tf_op jit(solution)/shard_map/ppermute | solution.py:461
  37.8 1.9 %collective-permute-start.9 = (f32[512,128]{1,0:T(8,128)S(1)}, f32[512,128]{1,0:T(8,128)S(1)}, u32[]{:S(2)}, u32[]{:S(2)}) collective-permute-start(f32[512,128]{1,0:T(8,128)S(1)} %gather_pass.2.part), channel_id=1, source_target_pairs={{0,2},{1,5},{2,0},{3,7},{4,6},{5,1},{6,4},{7,3},{8,10},{9,13},{10,... | collective-permute-start | bytes 786440 | tf_op jit(solution)/shard_map/ppermute | solution.py:461
  41.1 4.3 %collective-permute-done.9.got = f32[512,128]{1,0:T(8,128)S(1)} collective-permute-done((f32[512,128]{1,0:T(8,128)S(1)}, f32[512,128]{1,0:T(8,128)S(1)}, u32[]{:S(2)}, u32[]{:S(2)}) %collective-permute-start.9) | collective-permute-done | bytes 262176 | tf_op jit(solution)/shard_map/ppermute | solution.py:461
  48.4 1.6 %collective-permute-start.13 = (f32[8,128]{1,0:T(8,128)S(1)}, f32[8,128]{1,0:T(8,128)S(1)}, u32[]{:S(2)}, u32[]{:S(2)}) collective-permute-start(f32[8,128]{1,0:T(8,128)S(1)} %get-tuple-element.92.refs_0_), channel_id=1, source_target_pairs={{0,2},{1,5},{2,0},{3,7},{4,6},{5,1},{6,4},{7,3},{8,10},{9,13},{10,... | collective-permute-start | bytes 12296 | tf_op jit(solution)/shard_map/ppermute | solution.py:461
  50.0 3.3 %collective-permute-done.13.refs_1_ = f32[8,128]{1,0:T(8,128)S(1)} collective-permute-done((f32[8,128]{1,0:T(8,128)S(1)}, f32[8,128]{1,0:T(8,128)S(1)}, u32[]{:S(2)}, u32[]{:S(2)}) %collective-permute-start.13) | collective-permute-done | bytes 4128 | tf_op jit(solution)/shard_map/ppermute | solution.py:461
  53.3 3.6 %collective-permute-start.14 = (f32[264,128]{1,0:T(8,128)S(1)}, f32[264,128]{1,0:T(8,128)S(1)}, u32[]{:S(2)}, u32[]{:S(2)}) collective-permute-start(f32[264,128]{1,0:T(8,128)S(1)} %get-tuple-element.94.refs_0_), channel_id=1, source_target_pairs={{0,4},{1,3},{2,6},{3,1},{4,0},{5,7},{6,2},{7,5},{8,12},{9,11},{10,... | collective-permute-start | bytes 405512 | tf_op jit(solution)/shard_map/ppermute | solution.py:461
  57.4 2.5 %collective-permute-done.14.got.refs_1_ = f32[264,128]{1,0:T(8,128)S(1)} collective-permute-done((f32[264,128]{1,0:T(8,128)S(1)}, f32[264,128]{1,0:T(8,128)S(1)}, u32[]{:S(2)}, u32[]{:S(2)}) %collective-permute-start.14) | collective-permute-done | bytes 135200 | tf_op jit(solution)/shard_map/ppermute | solution.py:461
  60.0 5.2 %collective-permute-done.15.got.refs_1_ = f32[264,128]{1,0:T(8,128)S(1)} collective-permute-done((f32[264,128]{1,0:T(8,128)S(1)}, f32[264,128]{1,0:T(8,128)S(1)}, u32[]{:S(2)}, u32[]{:S(2)}) %collective-permute-start.15) | collective-permute-done | bytes 135200 | tf_op jit(solution)/shard_map/ppermute | solution.py:461
  65.4 6.4 %collective-permute-done.16.got = f32[264,128]{1,0:T(8,128)S(1)} collective-permute-done((f32[264,128]{1,0:T(8,128)S(1)}, f32[264,128]{1,0:T(8,128)S(1)}, u32[]{:S(2)}, u32[]{:S(2)}) %collective-permute-start.16) | collective-permute-done | bytes 135200 | tf_op jit(solution)/shard_map/ppermute | solution.py:461
  71.9 2.1 %collective-permute-start.17 = (f32[256,128]{1,0:T(8,128)S(1)}, f32[256,128]{1,0:T(8,128)S(1)}, u32[]{:S(2)}, u32[]{:S(2)}) collective-permute-start(f32[256,128]{1,0:T(8,128)S(1)} %get-tuple-element.97.part), channel_id=1, source_target_pairs={{0,4},{1,3},{2,6},{3,1},{4,0},{5,7},{6,2},{7,5},{8,12},{9,11},{10,... | collective-permute-start | bytes 393224 | tf_op jit(solution)/shard_map/ppermute | solution.py:461
  74.3 2.6 %collective-permute-done.17.got = f32[256,128]{1,0:T(8,128)S(1)} collective-permute-done((f32[256,128]{1,0:T(8,128)S(1)}, f32[256,128]{1,0:T(8,128)S(1)}, u32[]{:S(2)}, u32[]{:S(2)}) %collective-permute-start.17) | collective-permute-done | bytes 131104 | tf_op jit(solution)/shard_map/ppermute | solution.py:461
  79.5 5.4 %collective-permute-done.20.got = f32[512,128]{1,0:T(8,128)S(1)} collective-permute-done((f32[512,128]{1,0:T(8,128)S(1)}, f32[512,128]{1,0:T(8,128)S(1)}, u32[]{:S(2)}, u32[]{:S(2)}) %collective-permute-start.20) | collective-permute-done | bytes 262176 | tf_op jit(solution)/shard_map/ppermute | solution.py:461
  85.3 1.2 %prior_pass.3 = (f32[384,128]{1,0:T(8,128)S(1)}, f32[384,128]{1,0:T(8,128)S(1)}, f32[512,128]{1,0:T(8,128)S(1)}, f32[512,128]{1,0:T(8,128)S(1)}, f32[64,128]{1,0:T(8,128)S(1)}) custom-call(bf16[768,1024]{1,0:T(8,128)(2,1)S(1)} %get-tuple-element.76.feats, bf16[1024,768]{1,0:T(8,128)(2,1)S(1)} %get-tuple-element.77.turned, f32[768,128]{1,0:T(8,128)S(1)} %part_pass.3.begun, ...), custom_call_target="tpu_custom_call" | custom-call | flops 402653184 | bytes 3145728 | tf_op jit(solution)/shard_map/prior_pass/pallas_call | solution.py:283
  87.7 2.1 %collective-permute-start.24 = (f32[8,128]{1,0:T(8,128)S(1)}, f32[8,128]{1,0:T(8,128)S(1)}, u32[]{:S(2)}, u32[]{:S(2)}) collective-permute-start(f32[8,128]{1,0:T(8,128)S(1)} %get-tuple-element.110.refs_0_), channel_id=1, source_target_pairs={{0,2},{1,5},{2,0},{3,7},{4,6},{5,1},{6,4},{7,3},{8,10},{9,13},{10,... | collective-permute-start | bytes 12296 | tf_op jit(solution)/shard_map/ppermute | solution.py:461
  89.8 3.3 %collective-permute-done.24.refs_1_ = f32[8,128]{1,0:T(8,128)S(1)} collective-permute-done((f32[8,128]{1,0:T(8,128)S(1)}, f32[8,128]{1,0:T(8,128)S(1)}, u32[]{:S(2)}, u32[]{:S(2)}) %collective-permute-start.24) | collective-permute-done | bytes 4128 | tf_op jit(solution)/shard_map/ppermute | solution.py:461
  93.1 3.6 %collective-permute-start.25 = (f32[264,128]{1,0:T(8,128)S(1)}, f32[264,128]{1,0:T(8,128)S(1)}, u32[]{:S(2)}, u32[]{:S(2)}) collective-permute-start(f32[264,128]{1,0:T(8,128)S(1)} %get-tuple-element.112.refs_0_), channel_id=1, source_target_pairs={{0,4},{1,3},{2,6},{3,1},{4,0},{5,7},{6,2},{7,5},{8,12},{9,11},{10,... | collective-permute-start | bytes 405512 | tf_op jit(solution)/shard_map/ppermute | solution.py:461
  97.1 2.5 %collective-permute-done.25.got.refs_1_ = f32[264,128]{1,0:T(8,128)S(1)} collective-permute-done((f32[264,128]{1,0:T(8,128)S(1)}, f32[264,128]{1,0:T(8,128)S(1)}, u32[]{:S(2)}, u32[]{:S(2)}) %collective-permute-start.25) | collective-permute-done | bytes 135200 | tf_op jit(solution)/shard_map/ppermute | solution.py:461
  99.7 4.3 %collective-permute-done.26.got.refs_1_ = f32[136,128]{1,0:T(8,128)S(1)} collective-permute-done((f32[136,128]{1,0:T(8,128)S(1)}, f32[136,128]{1,0:T(8,128)S(1)}, u32[]{:S(2)}, u32[]{:S(2)}) %collective-permute-start.26) | collective-permute-done | bytes 69664 | tf_op jit(solution)/shard_map/ppermute | solution.py:461
  104.1 4.8 %collective-permute-done.27.got = f32[72,128]{1,0:T(8,128)S(1)} collective-permute-done((f32[72,128]{1,0:T(8,128)S(1)}, f32[72,128]{1,0:T(8,128)S(1)}, u32[]{:S(2)}, u32[]{:S(2)}) %collective-permute-start.27) | collective-permute-done | bytes 36896 | tf_op jit(solution)/shard_map/ppermute | solution.py:461
  (85 shorter events, 16.7 us)
Async XLA Ops:
  4.3 2.1 %collective-permute-start = (f32[1024,128]{1,0:T(8,128)S(1)}, f32[1024,128]{1,0:T(8,128)S(1)}, u32[]{:S(2)}, u32[]{:S(2)}) collective-permute-start(f32[1024,128]{1,0:T(8,128)S(1)} %get-tuple-element.68), channel_id=1, source_target_pairs={{0,1},{1,0},{2,3},{3,2},{4,5},{5,4},{6,7},{7,6},{8,9},{9,8},{10,11... | collective-permute-start | bytes 1572872 | tf_op jit(solution)/shard_map/ppermute | solution.py:451
  6.4 7.7 %collective-permute-start.1 = (f32[512,128]{1,0:T(8,128)S(1)}, f32[512,128]{1,0:T(8,128)S(1)}, u32[]{:S(2)}, u32[]{:S(2)}) collective-permute-start(f32[512,128]{1,0:T(8,128)S(1)} %get-tuple-element.70), channel_id=1, source_target_pairs={{0,2},{1,5},{2,0},{3,7},{4,6},{5,1},{6,4},{7,3},{8,10},{9,13},{10,... | collective-permute-start | bytes 786440 | tf_op jit(solution)/shard_map/ppermute | solution.py:461
  9.4 6.5 %copy-start.2 = (bf16[3,384,256]{2,1,0:T(8,128)(2,1)S(1)}, bf16[3,384,256]{2,1,0:T(8,128)(2,1)}, u32[]{:S(2)}) copy-start(bf16[3,384,256]{2,1,0:T(8,128)(2,1)} %user_noise.5) | copy-start | bytes 1769476
  10.5 3.7 %collective-permute-start.2 = (f32[8,128]{1,0:T(8,128)S(1)}, f32[8,128]{1,0:T(8,128)S(1)}, u32[]{:S(2)}, u32[]{:S(2)}) collective-permute-start(f32[8,128]{1,0:T(8,128)S(1)} %get-tuple-element.71.refs_0_), channel_id=1, source_target_pairs={{0,2},{1,5},{2,0},{3,7},{4,6},{5,1},{6,4},{7,3},{8,10},{9,13},{10,... | collective-permute-start | bytes 12296 | tf_op jit(solution)/shard_map/ppermute | solution.py:461
  14.2 5.1 %collective-permute-start.3 = (f32[264,128]{1,0:T(8,128)S(1)}, f32[264,128]{1,0:T(8,128)S(1)}, u32[]{:S(2)}, u32[]{:S(2)}) collective-permute-start(f32[264,128]{1,0:T(8,128)S(1)} %get-tuple-element.73.refs_0_), channel_id=1, source_target_pairs={{0,4},{1,3},{2,6},{3,1},{4,0},{5,7},{6,2},{7,5},{8,12},{9,11},{10,... | collective-permute-start | bytes 405512 | tf_op jit(solution)/shard_map/ppermute | solution.py:461
  19.4 20.3 %collective-permute-start.4 = (f32[384,1024]{1,0:T(8,128)S(1)}, f32[384,1024]{1,0:T(8,128)S(1)}, u32[]{:S(2)}, u32[]{:S(2)}) collective-permute-start(f32[384,1024]{1,0:T(8,128)S(1)} %widen_pass.1), channel_id=1, source_target_pairs={{0,1},{1,0},{2,3},{3,2},{4,5},{5,4},{6,7},{7,6},{8,9},{9,8},{10,11... | collective-permute-start | bytes 4718600 | tf_op jit(solution)/shard_map/ppermute | solution.py:451
  19.5 6.5 %collective-permute-start.5 = (f32[264,128]{1,0:T(8,128)S(1)}, f32[264,128]{1,0:T(8,128)S(1)}, u32[]{:S(2)}, u32[]{:S(2)}) collective-permute-start(f32[264,128]{1,0:T(8,128)S(1)} %step_pass.12.later.held.refs_0_), channel_id=1, source_target_pairs={{0,8},{1,17},{2,10},{3,19},{4,12},{5,21},{6,14},{7,23},{8,0},{9,25... | collective-permute-start | bytes 405512 | tf_op jit(solution)/shard_map/ppermute | solution.py:461
  26.0 6.7 %collective-permute-start.6 = (f32[264,128]{1,0:T(8,128)S(1)}, f32[264,128]{1,0:T(8,128)S(1)}, u32[]{:S(2)}, u32[]{:S(2)}) collective-permute-start(f32[264,128]{1,0:T(8,128)S(1)} %step_pass.13.held.sent), channel_id=1, source_target_pairs={{0,16},{1,9},{2,18},{3,11},{4,20},{5,13},{6,22},{7,15},{8,24},{9,1... | collective-permute-start | bytes 405512 | tf_op jit(solution)/shard_map/ppermute | solution.py:461
  32.7 2.0 %collective-permute-start.8 = (f32[8,128]{1,0:T(8,128)S(1)}, f32[8,128]{1,0:T(8,128)S(1)}, u32[]{:S(2)}, u32[]{:S(2)}) collective-permute-start(f32[8,128]{1,0:T(8,128)S(1)} %get-tuple-element.80.stats), channel_id=1, source_target_pairs={{0,1},{1,0},{2,3},{3,2},{4,5},{5,4},{6,7},{7,6},{8,9},{9,8},{10,11... | collective-permute-start | bytes 12296 | tf_op jit(solution)/shard_map/ppermute | solution.py:451
  32.8 5.0 %collective-permute-start.7 = (f32[256,128]{1,0:T(8,128)S(1)}, f32[256,128]{1,0:T(8,128)S(1)}, u32[]{:S(2)}, u32[]{:S(2)}) collective-permute-start(f32[256,128]{1,0:T(8,128)S(1)} %get-tuple-element.79.part.old), channel_id=1, source_target_pairs={{0,4},{1,3},{2,6},{3,1},{4,0},{5,7},{6,2},{7,5},{8,12},{9,11},{10,... | collective-permute-start | bytes 393224 | tf_op jit(solution)/shard_map/ppermute | solution.py:461
  34.9 11.1 %collective-permute-start.11 = (f32[384,256]{1,0:T(8,128)S(1)}, f32[384,256]{1,0:T(8,128)S(1)}, u32[]{:S(2)}, u32[]{:S(2)}) collective-permute-start(f32[384,256]{1,0:T(8,128)S(1)} %get-tuple-element.89), channel_id=1, source_target_pairs={{0,1},{1,2},{2,3},{3,4},{4,5},{5,6},{6,7},{7,8},{8,9},{9,10},{10,1... | collective-permute-start | bytes 1179656 | tf_op jit(solution)/shard_map/ppermute | solution.py:455
  37.8 7.7 %collective-permute-start.9 = (f32[512,128]{1,0:T(8,128)S(1)}, f32[512,128]{1,0:T(8,128)S(1)}, u32[]{:S(2)}, u32[]{:S(2)}) collective-permute-start(f32[512,128]{1,0:T(8,128)S(1)} %gather_pass.2.part), channel_id=1, source_target_pairs={{0,2},{1,5},{2,0},{3,7},{4,6},{5,1},{6,4},{7,3},{8,10},{9,13},{10,... | collective-permute-start | bytes 786440 | tf_op jit(solution)/shard_map/ppermute | solution.py:461
  39.7 1.4 %collective-permute-start.10 = (f32[384,128]{1,0:T(8,128)S(1)}, f32[384,128]{1,0:T(8,128)S(1)}, u32[]{:S(2)}, u32[]{:S(2)}) collective-permute-start(f32[384,128]{1,0:T(8,128)S(1)} %get-tuple-element.88), channel_id=1, source_target_pairs={{0,1},{1,0},{2,3},{3,2},{4,5},{5,4},{6,7},{7,6},{8,9},{9,8},{10,11... | collective-permute-start | bytes 589832 | tf_op jit(solution)/shard_map/ppermute | solution.py:451
  46.8 6.5 %collective-permute-start.12 = (f32[512,128]{1,0:T(8,128)S(1)}, f32[512,128]{1,0:T(8,128)S(1)}, u32[]{:S(2)}, u32[]{:S(2)}) collective-permute-start(f32[512,128]{1,0:T(8,128)S(1)} %get-tuple-element.91.refs_0_), channel_id=1, source_target_pairs={{0,2},{1,5},{2,0},{3,7},{4,6},{5,1},{6,4},{7,3},{8,10},{9,13},{10,... | collective-permute-start | bytes 786440 | tf_op jit(solution)/shard_map/ppermute | solution.py:461
  48.4 4.8 %collective-permute-start.13 = (f32[8,128]{1,0:T(8,128)S(1)}, f32[8,128]{1,0:T(8,128)S(1)}, u32[]{:S(2)}, u32[]{:S(2)}) collective-permute-start(f32[8,128]{1,0:T(8,128)S(1)} %get-tuple-element.92.refs_0_), channel_id=1, source_target_pairs={{0,2},{1,5},{2,0},{3,7},{4,6},{5,1},{6,4},{7,3},{8,10},{9,13},{10,... | collective-permute-start | bytes 12296 | tf_op jit(solution)/shard_map/ppermute | solution.py:461
  53.3 6.5 %collective-permute-start.14 = (f32[264,128]{1,0:T(8,128)S(1)}, f32[264,128]{1,0:T(8,128)S(1)}, u32[]{:S(2)}, u32[]{:S(2)}) collective-permute-start(f32[264,128]{1,0:T(8,128)S(1)} %get-tuple-element.94.refs_0_), channel_id=1, source_target_pairs={{0,4},{1,3},{2,6},{3,1},{4,0},{5,7},{6,2},{7,5},{8,12},{9,11},{10,... | collective-permute-start | bytes 405512 | tf_op jit(solution)/shard_map/ppermute | solution.py:461
  59.9 5.4 %collective-permute-start.15 = (f32[264,128]{1,0:T(8,128)S(1)}, f32[264,128]{1,0:T(8,128)S(1)}, u32[]{:S(2)}, u32[]{:S(2)}) collective-permute-start(f32[264,128]{1,0:T(8,128)S(1)} %step_pass.15.held.refs_0_), channel_id=1, source_target_pairs={{0,8},{1,17},{2,10},{3,19},{4,12},{5,21},{6,14},{7,23},{8,0},{9,25... | collective-permute-start | bytes 405512 | tf_op jit(solution)/shard_map/ppermute | solution.py:461
  59.9 14.1 %collective-permute-start.19 = (f32[384,128]{1,0:T(8,128)S(1)}, f32[384,128]{1,0:T(8,128)S(1)}, u32[]{:S(2)}, u32[]{:S(2)}) collective-permute-start(f32[384,128]{1,0:T(8,128)S(1)} %get-tuple-element.101), channel_id=1, source_target_pairs={{0,1},{1,0},{2,3},{3,2},{4,5},{5,4},{6,7},{7,6},{8,9},{9,8},{10,11... | collective-permute-start | bytes 589832 | tf_op jit(solution)/shard_map/ppermute | solution.py:451
  65.3 6.5 %collective-permute-start.16 = (f32[264,128]{1,0:T(8,128)S(1)}, f32[264,128]{1,0:T(8,128)S(1)}, u32[]{:S(2)}, u32[]{:S(2)}) collective-permute-start(f32[264,128]{1,0:T(8,128)S(1)} %step_pass.16.held.sent), channel_id=1, source_target_pairs={{0,16},{1,9},{2,18},{3,11},{4,20},{5,13},{6,22},{7,15},{8,24},{9,1... | collective-permute-start | bytes 405512 | tf_op jit(solution)/shard_map/ppermute | solution.py:461
  71.9 2.2 %collective-permute-start.18 = (f32[8,128]{1,0:T(8,128)S(1)}, f32[8,128]{1,0:T(8,128)S(1)}, u32[]{:S(2)}, u32[]{:S(2)}) collective-permute-start(f32[8,128]{1,0:T(8,128)S(1)} %get-tuple-element.98.stats), channel_id=1, source_target_pairs={{0,1},{1,0},{2,3},{3,2},{4,5},{5,4},{6,7},{7,6},{8,9},{9,8},{10,11... | collective-permute-start | bytes 12296 | tf_op jit(solution)/shard_map/ppermute | solution.py:451
  71.9 5.0 %collective-permute-start.17 = (f32[256,128]{1,0:T(8,128)S(1)}, f32[256,128]{1,0:T(8,128)S(1)}, u32[]{:S(2)}, u32[]{:S(2)}) collective-permute-start(f32[256,128]{1,0:T(8,128)S(1)} %get-tuple-element.97.part), channel_id=1, source_target_pairs={{0,4},{1,3},{2,6},{3,1},{4,0},{5,7},{6,2},{7,5},{8,12},{9,11},{10,... | collective-permute-start | bytes 393224 | tf_op jit(solution)/shard_map/ppermute | solution.py:461
  74.3 11.1 %collective-permute-start.22 = (f32[384,256]{1,0:T(8,128)S(1)}, f32[384,256]{1,0:T(8,128)S(1)}, u32[]{:S(2)}, u32[]{:S(2)}) collective-permute-start(f32[384,256]{1,0:T(8,128)S(1)} %get-tuple-element.107), channel_id=1, source_target_pairs={{0,1},{1,2},{2,3},{3,4},{4,5},{5,6},{6,7},{7,8},{8,9},{9,10},{10,1... | collective-permute-start | bytes 1179656 | tf_op jit(solution)/shard_map/ppermute | solution.py:455
  77.0 7.8 %collective-permute-start.20 = (f32[512,128]{1,0:T(8,128)S(1)}, f32[512,128]{1,0:T(8,128)S(1)}, u32[]{:S(2)}, u32[]{:S(2)}) collective-permute-start(f32[512,128]{1,0:T(8,128)S(1)} %gather_pass.3.part), channel_id=1, source_target_pairs={{0,2},{1,5},{2,0},{3,7},{4,6},{5,1},{6,4},{7,3},{8,10},{9,13},{10,... | collective-permute-start | bytes 786440 | tf_op jit(solution)/shard_map/ppermute | solution.py:461
  77.4 2.1 %collective-permute-start.21 = (f32[384,128]{1,0:T(8,128)S(1)}, f32[384,128]{1,0:T(8,128)S(1)}, u32[]{:S(2)}, u32[]{:S(2)}) collective-permute-start(f32[384,128]{1,0:T(8,128)S(1)} %get-tuple-element.106), channel_id=1, source_target_pairs={{0,1},{1,0},{2,3},{3,2},{4,5},{5,4},{6,7},{7,6},{8,9},{9,8},{10,11... | collective-permute-start | bytes 589832 | tf_op jit(solution)/shard_map/ppermute | solution.py:451
  86.5 6.5 %collective-permute-start.23 = (f32[512,128]{1,0:T(8,128)S(1)}, f32[512,128]{1,0:T(8,128)S(1)}, u32[]{:S(2)}, u32[]{:S(2)}) collective-permute-start(f32[512,128]{1,0:T(8,128)S(1)} %get-tuple-element.109.refs_0_), channel_id=1, source_target_pairs={{0,2},{1,5},{2,0},{3,7},{4,6},{5,1},{6,4},{7,3},{8,10},{9,13},{10,... | collective-permute-start | bytes 786440 | tf_op jit(solution)/shard_map/ppermute | solution.py:461
  87.7 5.3 %collective-permute-start.24 = (f32[8,128]{1,0:T(8,128)S(1)}, f32[8,128]{1,0:T(8,128)S(1)}, u32[]{:S(2)}, u32[]{:S(2)}) collective-permute-start(f32[8,128]{1,0:T(8,128)S(1)} %get-tuple-element.110.refs_0_), channel_id=1, source_target_pairs={{0,2},{1,5},{2,0},{3,7},{4,6},{5,1},{6,4},{7,3},{8,10},{9,13},{10,... | collective-permute-start | bytes 12296 | tf_op jit(solution)/shard_map/ppermute | solution.py:461
  93.1 6.5 %collective-permute-start.25 = (f32[264,128]{1,0:T(8,128)S(1)}, f32[264,128]{1,0:T(8,128)S(1)}, u32[]{:S(2)}, u32[]{:S(2)}) collective-permute-start(f32[264,128]{1,0:T(8,128)S(1)} %get-tuple-element.112.refs_0_), channel_id=1, source_target_pairs={{0,4},{1,3},{2,6},{3,1},{4,0},{5,7},{6,2},{7,5},{8,12},{9,11},{10,... | collective-permute-start | bytes 405512 | tf_op jit(solution)/shard_map/ppermute | solution.py:461
  96.6 12.9 %collective-permute-start.29 = (f32[384,128]{1,0:T(8,128)S(1)}, f32[384,128]{1,0:T(8,128)S(1)}, u32[]{:S(2)}, u32[]{:S(2)}) collective-permute-start(f32[384,128]{1,0:T(8,128)S(1)} %get-tuple-element.123), channel_id=1, source_target_pairs={{0,1},{1,0},{2,3},{3,2},{4,5},{5,4},{6,7},{7,6},{8,9},{9,8},{10,11... | collective-permute-start | bytes 589832 | tf_op jit(solution)/shard_map/ppermute | solution.py:451
  99.6 4.4 %collective-permute-start.26 = (f32[136,128]{1,0:T(8,128)S(1)}, f32[136,128]{1,0:T(8,128)S(1)}, u32[]{:S(2)}, u32[]{:S(2)}) collective-permute-start(f32[136,128]{1,0:T(8,128)S(1)} %get-tuple-element.116.refs_0_), channel_id=1, source_target_pairs={{0,8},{1,17},{2,10},{3,19},{4,12},{5,21},{6,14},{7,23},{8,0},{9,25... | collective-permute-start | bytes 208904 | tf_op jit(solution)/shard_map/ppermute | solution.py:461
  104.0 4.9 %collective-permute-start.27 = (f32[72,128]{1,0:T(8,128)S(1)}, f32[72,128]{1,0:T(8,128)S(1)}, u32[]{:S(2)}, u32[]{:S(2)}) collective-permute-start(f32[72,128]{1,0:T(8,128)S(1)} %get-tuple-element.118.sent), channel_id=1, source_target_pairs={{0,16},{1,9},{2,18},{3,11},{4,20},{5,13},{6,22},{7,15},{8,24},{9,1... | collective-permute-start | bytes 110600 | tf_op jit(solution)/shard_map/ppermute | solution.py:461
  109.0 2.4 %collective-permute-start.30 = (f32[32,128]{1,0:T(8,128)S(1)}, f32[32,128]{1,0:T(8,128)S(1)}, u32[]{:S(2)}, u32[]{:S(2)}) collective-permute-start(f32[32,128]{1,0:T(8,128)S(1)} %get-tuple-element.130), channel_id=1, source_target_pairs={{0,1},{1,0},{2,3},{3,2},{4,5},{5,4},{6,7},{7,6},{8,9},{9,8},{10,11... | collective-permute-start | bytes 49160 | tf_op jit(solution)/shard_map/ppermute | solution.py:451
  109.1 1.3 %collective-permute-start.28 = (f32[8,128]{1,0:T(8,128)S(1)}, f32[8,128]{1,0:T(8,128)S(1)}, u32[]{:S(2)}, u32[]{:S(2)}) collective-permute-start(f32[8,128]{1,0:T(8,128)S(1)} %get-tuple-element.120.stats), channel_id=1, source_target_pairs={{0,1},{1,0},{2,3},{3,2},{4,5},{5,4},{6,7},{7,6},{8,9},{9,8},{10,11... | collective-permute-start | bytes 12296 | tf_op jit(solution)/shard_map/ppermute | solution.py:451
  (9 other events, 38.4 us)

commit v15 on v14

--- a/solution.py
+++ b/solution.py
@@ -17,6 +17,7 @@
 CORES = 2
 RIDERS = 8
 ITEM_PARTS = 1
+FEAT_PARTS = 3
 NN = (((1,), (0,)), ((), ()))
 NT = (((1,), (1,)), ((), ()))
 TN = (((0,), (0,)), ((), ()))
@@ -176,40 +177,47 @@
     )(feats, turned, weights, users)
 
 
-def widen_kernel(narrow, later, wide):
-    wide[...] = narrow[...].astype(f32)
+def widen_kernel(narrow, later, *wide):
+    rows = wide[0].shape[0]
+    for n, ref in enumerate(wide):
+        ref[...] = narrow[n * rows : (n + 1) * rows, :].astype(f32)
 
 
 def widen_pass(narrow, later):
+    rows, feat = narrow.shape
     return pl.pallas_call(
         widen_kernel,
-        out_shape=shape(*narrow.shape),
+        out_shape=(shape(rows // FEAT_PARTS, feat),) * FEAT_PARTS,
         in_specs=[VMEM, ANY],
-        out_specs=VMEM,
+        out_specs=(VMEM,) * FEAT_PARTS,
         compiler_params=PARAMS,
         name="widen_pass",
     )(narrow, later)
 
 
-def join_kernel(own, own_turned, other, both, turned):
-    rows = other.shape[0]
+def join_kernel(own, own_turned, *refs):
+    others, (both, turned) = refs[:-2], refs[-2:]
+    rows = own.shape[0]
     both[:rows, :] = own[...]
-    both[rows:, :] = other[...].astype(bf16)
     turned[:, :rows] = own_turned[...]
-    turned[:, rows:] = other[...].T.astype(bf16)
-
-
-def join_pass(own, own_turned, other):
+    for other in others:
+        at = slice(rows, rows + other.shape[0])
+        both[at, :] = other[...].astype(bf16)
+        turned[:, at] = other[...].T.astype(bf16)
+        rows += other.shape[0]
+
+
+def join_pass(own, own_turned, *others):
     rows, feat = own.shape
     return pl.pallas_call(
         join_kernel,
         out_shape=(shape(CORES * rows, feat, dtype=bf16), shape(feat, CORES * rows, dtype=bf16)),
-        in_specs=[VMEM] * 3,
+        in_specs=[VMEM] * (2 + len(others)),
         out_specs=(VMEM, VMEM),
         compiler_params=PARAMS,
         cost_estimate=cost(rows * feat, 12 * rows * feat),
         name="join_pass",
-    )(own, own_turned, other)
+    )(own, own_turned, *others)
 
 
 def part_kernel(devices, feats, part, mean):
@@ -364,72 +372,54 @@
     )(part, got, *later)
 
 
-def split_kernel(devices, both, mine, other):
-    place = where_am_i(devices)
+def split_kernel(devices, both, stats, mine, other):
     rows = mine.shape[0]
-    for ref, which in ((mine, place[0]), (other, 1 - place[0])):
-        at = pl.ds(pl.multiple_of(which * rows, 8), rows) if rows % 8 == 0 else pl.ds(which * rows, rows)
-        ref[...] = both[at, :]
-
-
-def split_pass(devices, both):
+    core = where_am_i(devices)[0]
+    mine[...] = both[rows_at(core, rows), :]
+    other[:rows, :] = both[rows_at(1 - core, rows), :]
+    other[rows:, :] = stats[...]
+
+
+def split_pass(devices, both, stats):
     rows, width = both.shape
+    rows = rows // CORES
     return pl.pallas_call(
         functools.partial(split_kernel, devices),
-        out_shape=(shape(rows // CORES, width),) * 2,
-        in_specs=[VMEM],
+        out_shape=(shape(rows, width), shape(rows + RIDERS, width)),
+        in_specs=[VMEM] * 2,
         out_specs=(VMEM,) * 2,
         compiler_params=PARAMS,
         name="split_pass",
-    )(both)
-
-
-def across_kernel(devices, mine, other, both):
-    place = where_am_i(devices)
-    width = mine.shape[1]
-    both[:, pl.ds(pl.multiple_of(place[0] * width, width), width)] = mine[...]
-    both[:, pl.ds(pl.multiple_of((1 - place[0]) * width, width), width)] = other[...]
-
-
-def across_pass(devices, mine, other):
-    rows, width = mine.shape
-    return pl.pallas_call(
-        functools.partial(across_kernel, devices),
-        out_shape=shape(rows, CORES * width),
-        in_specs=[VMEM, VMEM],
-        out_specs=VMEM,
-        compiler_params=PARAMS,
-        name="across_pass",
-    )(mine, other)
-
-
-def renew_kernel(devices, stats, more, base_u, grad_u, own_mean, other_mean, base_v, grad_v, users, *outs):
-    core = where_am_i(devices)[0]
+    )(both, stats)
+
+
+def renew(core, stats, base_u, grad_u, own_mean, other_mean, base_v, grad_v, users, *items):
     width = own_mean.shape[1]
-    precision = precision_of(stats[...] + more[...])
+    precision = precision_of(stats)
     precision = jnp.concatenate([precision] * CORES, 1)
-    parts = 1 if len(outs) == 1 else ITEM_PARTS
-    rows = base_v.shape[0] // parts
-    for n, items in enumerate(outs[:parts]):
+    rows = base_v.shape[0] // len(items)
+    for n, ref in enumerate(items):
         at = slice(n * rows, (n + 1) * rows)
-        items[...] = base_v[at, :] + precision * grad_v[at, :]
+        ref[...] = base_v[at, :] + precision * grad_v[at, :]
     new = base_u[...] + precision * grad_u[...]
     pull = step_size * prior_prec
     left = jnp.where(core == 0, own_mean[...], other_mean[...])
     right = jnp.where(core == 0, other_mean[...], own_mean[...])
     users[:, :width] = new[:, :width] + pull * left
     users[:, width:] = new[:, width:] + pull * right
-    for ref, which in zip(outs[parts:], (core, 1 - core), strict=False):
+
+
+def renew_kernel(devices, stats, more, *refs):
+    core = where_am_i(devices)[0]
+    renew(core, stats[...] + more[...], *refs[:-2])
+    users = refs[6]
+    for ref, which in zip(refs[-2:], (core, 1 - core), strict=True):
         ref[...] = half_of(users, which)
 
 
-def renew_pass(devices, last, stats, more, base_u, grad_u, own_mean, *state):
+def renew_pass(devices, stats, more, base_u, grad_u, own_mean, *state):
     rows, rank = base_u.shape
-    outs = [shape(rows, rank)]
-    if last:
-        outs.append(shape(rows, rank))
-    else:
-        outs += [shape(rows // ITEM_PARTS, rank)] * ITEM_PARTS + [shape(*own_mean.shape)] * 2
+    outs = [shape(rows, rank)] + [shape(rows // ITEM_PARTS, rank)] * ITEM_PARTS + [shape(*own_mean.shape)] * 2
     return pl.pallas_call(
         functools.partial(renew_kernel, devices),
         out_shape=tuple(outs),
@@ -439,6 +429,28 @@
         cost_estimate=cost(8 * base_u.size, 32 * base_u.size),
         name="renew_pass",
     )(stats, more, base_u, grad_u, own_mean, *state)
+
+
+def last_kernel(devices, stats, mine, got, *refs):
+    core = where_am_i(devices)[0]
+    weights = refs[-1]
+    rows, width = mine.shape
+    weights[:, rows_at(core, width)] = mine[...]
+    weights[:, rows_at(1 - core, width)] = got[:rows, :]
+    renew(core, stats[...] + got[rows:, :], *refs[:-1])
+
+
+def last_pass(devices, stats, mine, got, base_u, *state):
+    rows, width = mine.shape
+    return pl.pallas_call(
+        functools.partial(last_kernel, devices),
+        out_shape=(shape(*base_u.shape),) * 2 + (shape(rows, CORES * width),),
+        in_specs=[VMEM] * 9,
+        out_specs=(VMEM,) * 3,
+        compiler_params=PARAMS,
+        cost_estimate=cost(8 * base_u.size, 32 * base_u.size),
+        name="last_pass",
+    )(stats, mine, got, base_u, *state)
 
 
 def bit_order(devices, core):
@@ -515,15 +527,15 @@
                 (send,) = step_pass(False, 0, devices, held, got, rows, (send, got), later)
                 held = send
             if stratum == 0 and stage == 1:
-                wide = swap(widen_pass(side_features, send), devices)
-                feats, turned = join_pass(side_features, own_turned, wide)
+                wide = [swap(part, devices) for part in widen_pass(side_features, send)]
+                feats, turned = join_pass(side_features, own_turned, *wide)
         got = exchange(send, devices, stages - 1)
         part, stats = update_pass(rate, held, got, send, old)
-        users, *items = renew_pass(
-            devices, last, stats, swap(stats, devices), *state[:2], own_mean, other_mean, *state[2:]
-        )
         if last:
             break
+        users, *items = renew_pass(
+            devices, stats, swap(stats, devices), *state[:2], own_mean, other_mean, *state[2:]
+        )
         old = part
         *items, own_cols, other_cols = items
         items = [roll(rows, devices) for rows in items]
@@ -546,8 +558,10 @@
         if olds:
             (old,) = olds
         other_mean = swap(other_mean, devices)
-    mine, other = split_pass(devices, part)
-    return (users, *items, across_pass(devices, mine, swap(other, devices)))
+    mine, other = split_pass(devices, part, stats)
+    return last_pass(
+        devices, stats, mine, swap(other, devices), *state[:2], own_mean, other_mean, *state[2:]
+    )
 
 
 def solution(mesh):

time: 112 us -> 111 us (level)
    ppermute x19, waiting for transfers between devices: 62.9 us -> 61.8 us  [exchange(): return lax.ppermute(array, 'user', pairs)]
    ppermute x10 -> x11, starting transfers between devices: 2.39 us -> 3.06 us  [swap(): return lax.ppermute(array, 'user', [(i, i ^ 1) for i in range(devices)])]
    ppermute x10 -> x11, waiting for transfers between devices: 3.72 us -> 4.05 us  [swap(): return lax.ppermute(array, 'user', [(i, i ^ 1) for i in range(devices)])]
  transfers between devices with their start and end apart: 31 -> 32, of which waited for: 22 -> 22; matrix products, arithmetic and copies ran while one was open for 0% -> 0% of each run, Pallas kernels for 7% -> 6%
where the time goes in v15:
time: 111 us
  waiting for transfers between devices  66.8 us (60%)
  starting transfers between devices  29.9 us (27%)
  Pallas kernels  11.3 us (10%)
  local copies, waits for them, and re-layouts  2.25 us (2%)
    ppermute x19, waiting for transfers between devices, exchange(): return lax.ppermute(array, 'user', pairs)  61.8 us
    ppermute x19, starting transfers between devices, exchange(): return lax.ppermute(array, 'user', pairs)  26.7 us
    ppermute x11, waiting for transfers between devices, swap(): return lax.ppermute(array, 'user', [(i, i ^ 1) for i in range(devices)])  4.05 us
    pallas_call x3, Pallas kernels, error_pass(): pl.pallas_call(functools.partial(error_kernel, stratum), out_shape=(shape...  3.19 us
    ppermute x11, starting transfers between devices, swap(): return lax.ppermute(array, 'user', [(i, i ^ 1) for i in range(devices)])  3.06 us
    unnamed x21, local copies, waits for them, and re-layouts  2.25 us
  transfers between devices with their start and end apart: 32, of which 22 were waited for; matrix products, arithmetic and copies ran while one was open for 0% of the time, Pallas kernels for 6%

profile of v15, /device:TPU:0, one launch (start us, length us, event | category | flops | bytes accessed | tf_op | source)
XLA Modules:
  0.0 111.3 jit_solution(15390864157677828043)
XLA Ops:
  3.1 1.2 %first_pass.1 = (f32[384,128]{1,0:T(8,128)S(1)}, f32[384,128]{1,0:T(8,128)S(1)}, f32[1024,128]{1,0:T(8,128)S(1)}, f32[1024,128]{1,0:T(8,128)S(1)}, f32[256,128]{1,0:T(8,128)S(1)}) custom-call(bf16[384,1024]{1,0:T(8,128)(2,1)S(1)} %copy-done, bf16[1024,384]{1,0:T(8,128)(2,1)S(1)} %turn_pass.1.turned.refs_0_.own_turned, f32[1024,256]{1,0:T(8,128)S(1)} %copy-done.5, ...), custom_call_target="tpu_custom_call" | custom-call | flops 402653184 | bytes 2097152 | tf_op jit(solution)/shard_map/first_pass/pallas_call | solution.py:168
  4.8 1.5 %collective-permute-done.got = f32[1024,128]{1,0:T(8,128)S(1)} collective-permute-done((f32[1024,128]{1,0:T(8,128)S(1)}, f32[1024,128]{1,0:T(8,128)S(1)}, u32[]{:S(2)}, u32[]{:S(2)}) %collective-permute-start) | collective-permute-done | bytes 524320 | tf_op jit(solution)/shard_map/ppermute | solution.py:463
  6.4 2.9 %collective-permute-start.1 = (f32[512,128]{1,0:T(8,128)S(1)}, f32[512,128]{1,0:T(8,128)S(1)}, u32[]{:S(2)}, u32[]{:S(2)}) collective-permute-start(f32[512,128]{1,0:T(8,128)S(1)} %get-tuple-element.71), channel_id=1, source_target_pairs={{0,2},{1,5},{2,0},{3,7},{4,6},{5,1},{6,4},{7,3},{8,10},{9,13},{10,... | collective-permute-start | bytes 786440 | tf_op jit(solution)/shard_map/ppermute | solution.py:473
  10.6 3.6 %collective-permute-done.2.refs_1_ = f32[8,128]{1,0:T(8,128)S(1)} collective-permute-done((f32[8,128]{1,0:T(8,128)S(1)}, f32[8,128]{1,0:T(8,128)S(1)}, u32[]{:S(2)}, u32[]{:S(2)}) %collective-permute-start.2) | collective-permute-done | bytes 4128 | tf_op jit(solution)/shard_map/ppermute | solution.py:473
  14.2 1.7 %collective-permute-start.3 = (f32[264,128]{1,0:T(8,128)S(1)}, f32[264,128]{1,0:T(8,128)S(1)}, u32[]{:S(2)}, u32[]{:S(2)}) collective-permute-start(f32[264,128]{1,0:T(8,128)S(1)} %get-tuple-element.74.refs_0_), channel_id=1, source_target_pairs={{0,4},{1,3},{2,6},{3,1},{4,0},{5,7},{6,2},{7,5},{8,12},{9,11},{10,... | collective-permute-start | bytes 405512 | tf_op jit(solution)/shard_map/ppermute | solution.py:473
  16.4 2.8 %collective-permute-done.3.got.refs_1_ = f32[264,128]{1,0:T(8,128)S(1)} collective-permute-done((f32[264,128]{1,0:T(8,128)S(1)}, f32[264,128]{1,0:T(8,128)S(1)}, u32[]{:S(2)}, u32[]{:S(2)}) %collective-permute-start.3) | collective-permute-done | bytes 135200 | tf_op jit(solution)/shard_map/ppermute | solution.py:473
  19.5 1.8 %collective-permute-start.7 = (f32[264,128]{1,0:T(8,128)S(1)}, f32[264,128]{1,0:T(8,128)S(1)}, u32[]{:S(2)}, u32[]{:S(2)}) collective-permute-start(f32[264,128]{1,0:T(8,128)S(1)} %step_pass.12.later.held.refs_0_), channel_id=1, source_target_pairs={{0,8},{1,17},{2,10},{3,19},{4,12},{5,21},{6,14},{7,23},{8,0},{9,25... | collective-permute-start | bytes 405512 | tf_op jit(solution)/shard_map/ppermute | solution.py:473
  21.3 1.2 %collective-permute-start.5 = (f32[128,1024]{1,0:T(8,128)S(1)}, f32[128,1024]{1,0:T(8,128)S(1)}, u32[]{:S(2)}, u32[]{:S(2)}) collective-permute-start(f32[128,1024]{1,0:T(8,128)S(1)} %get-tuple-element.78), channel_id=1, source_target_pairs={{0,1},{1,0},{2,3},{3,2},{4,5},{5,4},{6,7},{7,6},{8,9},{9,8},{10,11... | collective-permute-start | bytes 1572872 | tf_op jit(solution)/shard_map/ppermute | solution.py:463
  22.4 3.5 %collective-permute-done.7.got.refs_1_ = f32[264,128]{1,0:T(8,128)S(1)} collective-permute-done((f32[264,128]{1,0:T(8,128)S(1)}, f32[264,128]{1,0:T(8,128)S(1)}, u32[]{:S(2)}, u32[]{:S(2)}) %collective-permute-start.7) | collective-permute-done | bytes 135200 | tf_op jit(solution)/shard_map/ppermute | solution.py:473
  26.0 2.2 %collective-permute-start.8 = (f32[264,128]{1,0:T(8,128)S(1)}, f32[264,128]{1,0:T(8,128)S(1)}, u32[]{:S(2)}, u32[]{:S(2)}) collective-permute-start(f32[264,128]{1,0:T(8,128)S(1)} %step_pass.13.held.sent), channel_id=1, source_target_pairs={{0,16},{1,9},{2,18},{3,11},{4,20},{5,13},{6,22},{7,15},{8,24},{9,1... | collective-permute-start | bytes 405512 | tf_op jit(solution)/shard_map/ppermute | solution.py:473
  28.2 4.5 %collective-permute-done.8.got = f32[264,128]{1,0:T(8,128)S(1)} collective-permute-done((f32[264,128]{1,0:T(8,128)S(1)}, f32[264,128]{1,0:T(8,128)S(1)}, u32[]{:S(2)}, u32[]{:S(2)}) %collective-permute-start.8) | collective-permute-done | bytes 135200 | tf_op jit(solution)/shard_map/ppermute | solution.py:473
  32.8 1.9 %collective-permute-start.9 = (f32[256,128]{1,0:T(8,128)S(1)}, f32[256,128]{1,0:T(8,128)S(1)}, u32[]{:S(2)}, u32[]{:S(2)}) collective-permute-start(f32[256,128]{1,0:T(8,128)S(1)} %get-tuple-element.83.part.old), channel_id=1, source_target_pairs={{0,4},{1,3},{2,6},{3,1},{4,0},{5,7},{6,2},{7,5},{8,12},{9,11},{10,... | collective-permute-start | bytes 393224 | tf_op jit(solution)/shard_map/ppermute | solution.py:473
  35.1 2.7 %collective-permute-done.9.got = f32[256,128]{1,0:T(8,128)S(1)} collective-permute-done((f32[256,128]{1,0:T(8,128)S(1)}, f32[256,128]{1,0:T(8,128)S(1)}, u32[]{:S(2)}, u32[]{:S(2)}) %collective-permute-start.9) | collective-permute-done | bytes 131104 | tf_op jit(solution)/shard_map/ppermute | solution.py:473
  37.8 1.9 %collective-permute-start.11 = (f32[512,128]{1,0:T(8,128)S(1)}, f32[512,128]{1,0:T(8,128)S(1)}, u32[]{:S(2)}, u32[]{:S(2)}) collective-permute-start(f32[512,128]{1,0:T(8,128)S(1)} %gather_pass.2.part), channel_id=1, source_target_pairs={{0,2},{1,5},{2,0},{3,7},{4,6},{5,1},{6,4},{7,3},{8,10},{9,13},{10,... | collective-permute-start | bytes 786440 | tf_op jit(solution)/shard_map/ppermute | solution.py:473
  41.1 4.3 %collective-permute-done.11.got = f32[512,128]{1,0:T(8,128)S(1)} collective-permute-done((f32[512,128]{1,0:T(8,128)S(1)}, f32[512,128]{1,0:T(8,128)S(1)}, u32[]{:S(2)}, u32[]{:S(2)}) %collective-permute-start.11) | collective-permute-done | bytes 262176 | tf_op jit(solution)/shard_map/ppermute | solution.py:473
  48.4 1.6 %collective-permute-start.15 = (f32[8,128]{1,0:T(8,128)S(1)}, f32[8,128]{1,0:T(8,128)S(1)}, u32[]{:S(2)}, u32[]{:S(2)}) collective-permute-start(f32[8,128]{1,0:T(8,128)S(1)} %get-tuple-element.96.refs_0_), channel_id=1, source_target_pairs={{0,2},{1,5},{2,0},{3,7},{4,6},{5,1},{6,4},{7,3},{8,10},{9,13},{10,... | collective-permute-start | bytes 12296 | tf_op jit(solution)/shard_map/ppermute | solution.py:473
  50.0 3.3 %collective-permute-done.15.refs_1_ = f32[8,128]{1,0:T(8,128)S(1)} collective-permute-done((f32[8,128]{1,0:T(8,128)S(1)}, f32[8,128]{1,0:T(8,128)S(1)}, u32[]{:S(2)}, u32[]{:S(2)}) %collective-permute-start.15) | collective-permute-done | bytes 4128 | tf_op jit(solution)/shard_map/ppermute | solution.py:473
  53.3 3.6 %collective-permute-start.16 = (f32[264,128]{1,0:T(8,128)S(1)}, f32[264,128]{1,0:T(8,128)S(1)}, u32[]{:S(2)}, u32[]{:S(2)}) collective-permute-start(f32[264,128]{1,0:T(8,128)S(1)} %get-tuple-element.98.refs_0_), channel_id=1, source_target_pairs={{0,4},{1,3},{2,6},{3,1},{4,0},{5,7},{6,2},{7,5},{8,12},{9,11},{10,... | collective-permute-start | bytes 405512 | tf_op jit(solution)/shard_map/ppermute | solution.py:473
  57.4 2.5 %collective-permute-done.16.got.refs_1_ = f32[264,128]{1,0:T(8,128)S(1)} collective-permute-done((f32[264,128]{1,0:T(8,128)S(1)}, f32[264,128]{1,0:T(8,128)S(1)}, u32[]{:S(2)}, u32[]{:S(2)}) %collective-permute-start.16) | collective-permute-done | bytes 135200 | tf_op jit(solution)/shard_map/ppermute | solution.py:473
  60.0 5.2 %collective-permute-done.17.got.refs_1_ = f32[264,128]{1,0:T(8,128)S(1)} collective-permute-done((f32[264,128]{1,0:T(8,128)S(1)}, f32[264,128]{1,0:T(8,128)S(1)}, u32[]{:S(2)}, u32[]{:S(2)}) %collective-permute-start.17) | collective-permute-done | bytes 135200 | tf_op jit(solution)/shard_map/ppermute | solution.py:473
  65.4 6.4 %collective-permute-done.18.got = f32[264,128]{1,0:T(8,128)S(1)} collective-permute-done((f32[264,128]{1,0:T(8,128)S(1)}, f32[264,128]{1,0:T(8,128)S(1)}, u32[]{:S(2)}, u32[]{:S(2)}) %collective-permute-start.18) | collective-permute-done | bytes 135200 | tf_op jit(solution)/shard_map/ppermute | solution.py:473
  71.9 2.1 %collective-permute-start.19 = (f32[256,128]{1,0:T(8,128)S(1)}, f32[256,128]{1,0:T(8,128)S(1)}, u32[]{:S(2)}, u32[]{:S(2)}) collective-permute-start(f32[256,128]{1,0:T(8,128)S(1)} %get-tuple-element.101.part), channel_id=1, source_target_pairs={{0,4},{1,3},{2,6},{3,1},{4,0},{5,7},{6,2},{7,5},{8,12},{9,11},{10,... | collective-permute-start | bytes 393224 | tf_op jit(solution)/shard_map/ppermute | solution.py:473
  74.3 2.6 %collective-permute-done.19.got = f32[256,128]{1,0:T(8,128)S(1)} collective-permute-done((f32[256,128]{1,0:T(8,128)S(1)}, f32[256,128]{1,0:T(8,128)S(1)}, u32[]{:S(2)}, u32[]{:S(2)}) %collective-permute-start.19) | collective-permute-done | bytes 131104 | tf_op jit(solution)/shard_map/ppermute | solution.py:473
  79.5 5.4 %collective-permute-done.22.got = f32[512,128]{1,0:T(8,128)S(1)} collective-permute-done((f32[512,128]{1,0:T(8,128)S(1)}, f32[512,128]{1,0:T(8,128)S(1)}, u32[]{:S(2)}, u32[]{:S(2)}) %collective-permute-start.22) | collective-permute-done | bytes 262176 | tf_op jit(solution)/shard_map/ppermute | solution.py:473
  85.3 1.2 %prior_pass.3 = (f32[384,128]{1,0:T(8,128)S(1)}, f32[384,128]{1,0:T(8,128)S(1)}, f32[512,128]{1,0:T(8,128)S(1)}, f32[512,128]{1,0:T(8,128)S(1)}, f32[64,128]{1,0:T(8,128)S(1)}) custom-call(bf16[768,1024]{1,0:T(8,128)(2,1)S(1)} %get-tuple-element.80.feats, bf16[1024,768]{1,0:T(8,128)(2,1)S(1)} %get-tuple-element.81.turned, f32[768,128]{1,0:T(8,128)S(1)} %part_pass.3.begun, ...), custom_call_target="tpu_custom_call" | custom-call | flops 402653184 | bytes 3145728 | tf_op jit(solution)/shard_map/prior_pass/pallas_call | solution.py:291
  87.7 2.1 %collective-permute-start.26 = (f32[8,128]{1,0:T(8,128)S(1)}, f32[8,128]{1,0:T(8,128)S(1)}, u32[]{:S(2)}, u32[]{:S(2)}) collective-permute-start(f32[8,128]{1,0:T(8,128)S(1)} %get-tuple-element.114.refs_0_), channel_id=1, source_target_pairs={{0,2},{1,5},{2,0},{3,7},{4,6},{5,1},{6,4},{7,3},{8,10},{9,13},{10,... | collective-permute-start | bytes 12296 | tf_op jit(solution)/shard_map/ppermute | solution.py:473
  89.8 3.3 %collective-permute-done.26.refs_1_ = f32[8,128]{1,0:T(8,128)S(1)} collective-permute-done((f32[8,128]{1,0:T(8,128)S(1)}, f32[8,128]{1,0:T(8,128)S(1)}, u32[]{:S(2)}, u32[]{:S(2)}) %collective-permute-start.26) | collective-permute-done | bytes 4128 | tf_op jit(solution)/shard_map/ppermute | solution.py:473
  93.1 3.5 %collective-permute-start.27 = (f32[264,128]{1,0:T(8,128)S(1)}, f32[264,128]{1,0:T(8,128)S(1)}, u32[]{:S(2)}, u32[]{:S(2)}) collective-permute-start(f32[264,128]{1,0:T(8,128)S(1)} %get-tuple-element.116.refs_0_), channel_id=1, source_target_pairs={{0,4},{1,3},{2,6},{3,1},{4,0},{5,7},{6,2},{7,5},{8,12},{9,11},{10,... | collective-permute-start | bytes 405512 | tf_op jit(solution)/shard_map/ppermute | solution.py:473
  97.1 2.5 %collective-permute-done.27.got.refs_1_ = f32[264,128]{1,0:T(8,128)S(1)} collective-permute-done((f32[264,128]{1,0:T(8,128)S(1)}, f32[264,128]{1,0:T(8,128)S(1)}, u32[]{:S(2)}, u32[]{:S(2)}) %collective-permute-start.27) | collective-permute-done | bytes 135200 | tf_op jit(solution)/shard_map/ppermute | solution.py:473
  99.7 4.3 %collective-permute-done.28.got.refs_1_ = f32[136,128]{1,0:T(8,128)S(1)} collective-permute-done((f32[136,128]{1,0:T(8,128)S(1)}, f32[136,128]{1,0:T(8,128)S(1)}, u32[]{:S(2)}, u32[]{:S(2)}) %collective-permute-start.28) | collective-permute-done | bytes 69664 | tf_op jit(solution)/shard_map/ppermute | solution.py:473
  104.1 4.8 %collective-permute-done.29.got = f32[72,128]{1,0:T(8,128)S(1)} collective-permute-done((f32[72,128]{1,0:T(8,128)S(1)}, f32[72,128]{1,0:T(8,128)S(1)}, u32[]{:S(2)}, u32[]{:S(2)}) %collective-permute-start.29) | collective-permute-done | bytes 36896 | tf_op jit(solution)/shard_map/ppermute | solution.py:473
  109.1 1.2 %collective-permute-done.30.got = f32[40,128]{1,0:T(8,128)S(1)} collective-permute-done((f32[40,128]{1,0:T(8,128)S(1)}, f32[40,128]{1,0:T(8,128)S(1)}, u32[]{:S(2)}, u32[]{:S(2)}) %collective-permute-start.30) | collective-permute-done | bytes 20512 | tf_op jit(solution)/shard_map/ppermute | solution.py:463
  (86 shorter events, 17.1 us)
Async XLA Ops:
  4.3 2.1 %collective-permute-start = (f32[1024,128]{1,0:T(8,128)S(1)}, f32[1024,128]{1,0:T(8,128)S(1)}, u32[]{:S(2)}, u32[]{:S(2)}) collective-permute-start(f32[1024,128]{1,0:T(8,128)S(1)} %get-tuple-element.69), channel_id=1, source_target_pairs={{0,1},{1,0},{2,3},{3,2},{4,5},{5,4},{6,7},{7,6},{8,9},{9,8},{10,11... | collective-permute-start | bytes 1572872 | tf_op jit(solution)/shard_map/ppermute | solution.py:463
  6.4 7.7 %collective-permute-start.1 = (f32[512,128]{1,0:T(8,128)S(1)}, f32[512,128]{1,0:T(8,128)S(1)}, u32[]{:S(2)}, u32[]{:S(2)}) collective-permute-start(f32[512,128]{1,0:T(8,128)S(1)} %get-tuple-element.71), channel_id=1, source_target_pairs={{0,2},{1,5},{2,0},{3,7},{4,6},{5,1},{6,4},{7,3},{8,10},{9,13},{10,... | collective-permute-start | bytes 786440 | tf_op jit(solution)/shard_map/ppermute | solution.py:473
  10.5 3.7 %collective-permute-start.2 = (f32[8,128]{1,0:T(8,128)S(1)}, f32[8,128]{1,0:T(8,128)S(1)}, u32[]{:S(2)}, u32[]{:S(2)}) collective-permute-start(f32[8,128]{1,0:T(8,128)S(1)} %get-tuple-element.72.refs_0_), channel_id=1, source_target_pairs={{0,2},{1,5},{2,0},{3,7},{4,6},{5,1},{6,4},{7,3},{8,10},{9,13},{10,... | collective-permute-start | bytes 12296 | tf_op jit(solution)/shard_map/ppermute | solution.py:473
  14.2 5.1 %collective-permute-start.3 = (f32[264,128]{1,0:T(8,128)S(1)}, f32[264,128]{1,0:T(8,128)S(1)}, u32[]{:S(2)}, u32[]{:S(2)}) collective-permute-start(f32[264,128]{1,0:T(8,128)S(1)} %get-tuple-element.74.refs_0_), channel_id=1, source_target_pairs={{0,4},{1,3},{2,6},{3,1},{4,0},{5,7},{6,2},{7,5},{8,12},{9,11},{10,... | collective-permute-start | bytes 405512 | tf_op jit(solution)/shard_map/ppermute | solution.py:473
  19.4 20.3 %collective-permute-start.4 = (f32[128,1024]{1,0:T(8,128)S(1)}, f32[128,1024]{1,0:T(8,128)S(1)}, u32[]{:S(2)}, u32[]{:S(2)}) collective-permute-start(f32[128,1024]{1,0:T(8,128)S(1)} %get-tuple-element.77), channel_id=1, source_target_pairs={{0,1},{1,0},{2,3},{3,2},{4,5},{5,4},{6,7},{7,6},{8,9},{9,8},{10,11... | collective-permute-start | bytes 1572872 | tf_op jit(solution)/shard_map/ppermute | solution.py:463
  19.5 6.5 %collective-permute-start.7 = (f32[264,128]{1,0:T(8,128)S(1)}, f32[264,128]{1,0:T(8,128)S(1)}, u32[]{:S(2)}, u32[]{:S(2)}) collective-permute-start(f32[264,128]{1,0:T(8,128)S(1)} %step_pass.12.later.held.refs_0_), channel_id=1, source_target_pairs={{0,8},{1,17},{2,10},{3,19},{4,12},{5,21},{6,14},{7,23},{8,0},{9,25... | collective-permute-start | bytes 405512 | tf_op jit(solution)/shard_map/ppermute | solution.py:473
  21.3 18.4 %collective-permute-start.5 = (f32[128,1024]{1,0:T(8,128)S(1)}, f32[128,1024]{1,0:T(8,128)S(1)}, u32[]{:S(2)}, u32[]{:S(2)}) collective-permute-start(f32[128,1024]{1,0:T(8,128)S(1)} %get-tuple-element.78), channel_id=1, source_target_pairs={{0,1},{1,0},{2,3},{3,2},{4,5},{5,4},{6,7},{7,6},{8,9},{9,8},{10,11... | collective-permute-start | bytes 1572872 | tf_op jit(solution)/shard_map/ppermute | solution.py:463
  22.4 17.3 %collective-permute-start.6 = (f32[128,1024]{1,0:T(8,128)S(1)}, f32[128,1024]{1,0:T(8,128)S(1)}, u32[]{:S(2)}, u32[]{:S(2)}) collective-permute-start(f32[128,1024]{1,0:T(8,128)S(1)} %get-tuple-element.79), channel_id=1, source_target_pairs={{0,1},{1,0},{2,3},{3,2},{4,5},{5,4},{6,7},{7,6},{8,9},{9,8},{10,11... | collective-permute-start | bytes 1572872 | tf_op jit(solution)/shard_map/ppermute | solution.py:463
  26.0 6.7 %collective-permute-start.8 = (f32[264,128]{1,0:T(8,128)S(1)}, f32[264,128]{1,0:T(8,128)S(1)}, u32[]{:S(2)}, u32[]{:S(2)}) collective-permute-start(f32[264,128]{1,0:T(8,128)S(1)} %step_pass.13.held.sent), channel_id=1, source_target_pairs={{0,16},{1,9},{2,18},{3,11},{4,20},{5,13},{6,22},{7,15},{8,24},{9,1... | collective-permute-start | bytes 405512 | tf_op jit(solution)/shard_map/ppermute | solution.py:473
  32.7 2.0 %collective-permute-start.10 = (f32[8,128]{1,0:T(8,128)S(1)}, f32[8,128]{1,0:T(8,128)S(1)}, u32[]{:S(2)}, u32[]{:S(2)}) collective-permute-start(f32[8,128]{1,0:T(8,128)S(1)} %get-tuple-element.84.stats), channel_id=1, source_target_pairs={{0,1},{1,0},{2,3},{3,2},{4,5},{5,4},{6,7},{7,6},{8,9},{9,8},{10,11... | collective-permute-start | bytes 12296 | tf_op jit(solution)/shard_map/ppermute | solution.py:463
  32.8 5.0 %collective-permute-start.9 = (f32[256,128]{1,0:T(8,128)S(1)}, f32[256,128]{1,0:T(8,128)S(1)}, u32[]{:S(2)}, u32[]{:S(2)}) collective-permute-start(f32[256,128]{1,0:T(8,128)S(1)} %get-tuple-element.83.part.old), channel_id=1, source_target_pairs={{0,4},{1,3},{2,6},{3,1},{4,0},{5,7},{6,2},{7,5},{8,12},{9,11},{10,... | collective-permute-start | bytes 393224 | tf_op jit(solution)/shard_map/ppermute | solution.py:473
  34.9 11.0 %collective-permute-start.13 = (f32[384,256]{1,0:T(8,128)S(1)}, f32[384,256]{1,0:T(8,128)S(1)}, u32[]{:S(2)}, u32[]{:S(2)}) collective-permute-start(f32[384,256]{1,0:T(8,128)S(1)} %get-tuple-element.93), channel_id=1, source_target_pairs={{0,1},{1,2},{2,3},{3,4},{4,5},{5,6},{6,7},{7,8},{8,9},{9,10},{10,1... | collective-permute-start | bytes 1179656 | tf_op jit(solution)/shard_map/ppermute | solution.py:467
  37.8 7.7 %collective-permute-start.11 = (f32[512,128]{1,0:T(8,128)S(1)}, f32[512,128]{1,0:T(8,128)S(1)}, u32[]{:S(2)}, u32[]{:S(2)}) collective-permute-start(f32[512,128]{1,0:T(8,128)S(1)} %gather_pass.2.part), channel_id=1, source_target_pairs={{0,2},{1,5},{2,0},{3,7},{4,6},{5,1},{6,4},{7,3},{8,10},{9,13},{10,... | collective-permute-start | bytes 786440 | tf_op jit(solution)/shard_map/ppermute | solution.py:473
  39.7 1.4 %collective-permute-start.12 = (f32[384,128]{1,0:T(8,128)S(1)}, f32[384,128]{1,0:T(8,128)S(1)}, u32[]{:S(2)}, u32[]{:S(2)}) collective-permute-start(f32[384,128]{1,0:T(8,128)S(1)} %get-tuple-element.92), channel_id=1, source_target_pairs={{0,1},{1,0},{2,3},{3,2},{4,5},{5,4},{6,7},{7,6},{8,9},{9,8},{10,11... | collective-permute-start | bytes 589832 | tf_op jit(solution)/shard_map/ppermute | solution.py:463
  46.8 6.5 %collective-permute-start.14 = (f32[512,128]{1,0:T(8,128)S(1)}, f32[512,128]{1,0:T(8,128)S(1)}, u32[]{:S(2)}, u32[]{:S(2)}) collective-permute-start(f32[512,128]{1,0:T(8,128)S(1)} %get-tuple-element.95.refs_0_), channel_id=1, source_target_pairs={{0,2},{1,5},{2,0},{3,7},{4,6},{5,1},{6,4},{7,3},{8,10},{9,13},{10,... | collective-permute-start | bytes 786440 | tf_op jit(solution)/shard_map/ppermute | solution.py:473
  48.4 4.8 %collective-permute-start.15 = (f32[8,128]{1,0:T(8,128)S(1)}, f32[8,128]{1,0:T(8,128)S(1)}, u32[]{:S(2)}, u32[]{:S(2)}) collective-permute-start(f32[8,128]{1,0:T(8,128)S(1)} %get-tuple-element.96.refs_0_), channel_id=1, source_target_pairs={{0,2},{1,5},{2,0},{3,7},{4,6},{5,1},{6,4},{7,3},{8,10},{9,13},{10,... | collective-permute-start | bytes 12296 | tf_op jit(solution)/shard_map/ppermute | solution.py:473
  53.3 6.6 %collective-permute-start.16 = (f32[264,128]{1,0:T(8,128)S(1)}, f32[264,128]{1,0:T(8,128)S(1)}, u32[]{:S(2)}, u32[]{:S(2)}) collective-permute-start(f32[264,128]{1,0:T(8,128)S(1)} %get-tuple-element.98.refs_0_), channel_id=1, source_target_pairs={{0,4},{1,3},{2,6},{3,1},{4,0},{5,7},{6,2},{7,5},{8,12},{9,11},{10,... | collective-permute-start | bytes 405512 | tf_op jit(solution)/shard_map/ppermute | solution.py:473
  59.9 5.4 %collective-permute-start.17 = (f32[264,128]{1,0:T(8,128)S(1)}, f32[264,128]{1,0:T(8,128)S(1)}, u32[]{:S(2)}, u32[]{:S(2)}) collective-permute-start(f32[264,128]{1,0:T(8,128)S(1)} %step_pass.15.held.refs_0_), channel_id=1, source_target_pairs={{0,8},{1,17},{2,10},{3,19},{4,12},{5,21},{6,14},{7,23},{8,0},{9,25... | collective-permute-start | bytes 405512 | tf_op jit(solution)/shard_map/ppermute | solution.py:473
  59.9 14.1 %collective-permute-start.21 = (f32[384,128]{1,0:T(8,128)S(1)}, f32[384,128]{1,0:T(8,128)S(1)}, u32[]{:S(2)}, u32[]{:S(2)}) collective-permute-start(f32[384,128]{1,0:T(8,128)S(1)} %get-tuple-element.105), channel_id=1, source_target_pairs={{0,1},{1,0},{2,3},{3,2},{4,5},{5,4},{6,7},{7,6},{8,9},{9,8},{10,11... | collective-permute-start | bytes 589832 | tf_op jit(solution)/shard_map/ppermute | solution.py:463
  65.3 6.6 %collective-permute-start.18 = (f32[264,128]{1,0:T(8,128)S(1)}, f32[264,128]{1,0:T(8,128)S(1)}, u32[]{:S(2)}, u32[]{:S(2)}) collective-permute-start(f32[264,128]{1,0:T(8,128)S(1)} %step_pass.16.held.sent), channel_id=1, source_target_pairs={{0,16},{1,9},{2,18},{3,11},{4,20},{5,13},{6,22},{7,15},{8,24},{9,1... | collective-permute-start | bytes 405512 | tf_op jit(solution)/shard_map/ppermute | solution.py:473
  71.9 2.2 %collective-permute-start.20 = (f32[8,128]{1,0:T(8,128)S(1)}, f32[8,128]{1,0:T(8,128)S(1)}, u32[]{:S(2)}, u32[]{:S(2)}) collective-permute-start(f32[8,128]{1,0:T(8,128)S(1)} %get-tuple-element.102.stats), channel_id=1, source_target_pairs={{0,1},{1,0},{2,3},{3,2},{4,5},{5,4},{6,7},{7,6},{8,9},{9,8},{10,11... | collective-permute-start | bytes 12296 | tf_op jit(solution)/shard_map/ppermute | solution.py:463
  71.9 5.0 %collective-permute-start.19 = (f32[256,128]{1,0:T(8,128)S(1)}, f32[256,128]{1,0:T(8,128)S(1)}, u32[]{:S(2)}, u32[]{:S(2)}) collective-permute-start(f32[256,128]{1,0:T(8,128)S(1)} %get-tuple-element.101.part), channel_id=1, source_target_pairs={{0,4},{1,3},{2,6},{3,1},{4,0},{5,7},{6,2},{7,5},{8,12},{9,11},{10,... | collective-permute-start | bytes 393224 | tf_op jit(solution)/shard_map/ppermute | solution.py:473
  74.3 11.1 %collective-permute-start.24 = (f32[384,256]{1,0:T(8,128)S(1)}, f32[384,256]{1,0:T(8,128)S(1)}, u32[]{:S(2)}, u32[]{:S(2)}) collective-permute-start(f32[384,256]{1,0:T(8,128)S(1)} %get-tuple-element.111), channel_id=1, source_target_pairs={{0,1},{1,2},{2,3},{3,4},{4,5},{5,6},{6,7},{7,8},{8,9},{9,10},{10,1... | collective-permute-start | bytes 1179656 | tf_op jit(solution)/shard_map/ppermute | solution.py:467
  77.0 7.8 %collective-permute-start.22 = (f32[512,128]{1,0:T(8,128)S(1)}, f32[512,128]{1,0:T(8,128)S(1)}, u32[]{:S(2)}, u32[]{:S(2)}) collective-permute-start(f32[512,128]{1,0:T(8,128)S(1)} %gather_pass.3.part), channel_id=1, source_target_pairs={{0,2},{1,5},{2,0},{3,7},{4,6},{5,1},{6,4},{7,3},{8,10},{9,13},{10,... | collective-permute-start | bytes 786440 | tf_op jit(solution)/shard_map/ppermute | solution.py:473
  77.4 2.1 %collective-permute-start.23 = (f32[384,128]{1,0:T(8,128)S(1)}, f32[384,128]{1,0:T(8,128)S(1)}, u32[]{:S(2)}, u32[]{:S(2)}) collective-permute-start(f32[384,128]{1,0:T(8,128)S(1)} %get-tuple-element.110), channel_id=1, source_target_pairs={{0,1},{1,0},{2,3},{3,2},{4,5},{5,4},{6,7},{7,6},{8,9},{9,8},{10,11... | collective-permute-start | bytes 589832 | tf_op jit(solution)/shard_map/ppermute | solution.py:463
  86.5 6.5 %collective-permute-start.25 = (f32[512,128]{1,0:T(8,128)S(1)}, f32[512,128]{1,0:T(8,128)S(1)}, u32[]{:S(2)}, u32[]{:S(2)}) collective-permute-start(f32[512,128]{1,0:T(8,128)S(1)} %get-tuple-element.113.refs_0_), channel_id=1, source_target_pairs={{0,2},{1,5},{2,0},{3,7},{4,6},{5,1},{6,4},{7,3},{8,10},{9,13},{10,... | collective-permute-start | bytes 786440 | tf_op jit(solution)/shard_map/ppermute | solution.py:473
  87.7 5.3 %collective-permute-start.26 = (f32[8,128]{1,0:T(8,128)S(1)}, f32[8,128]{1,0:T(8,128)S(1)}, u32[]{:S(2)}, u32[]{:S(2)}) collective-permute-start(f32[8,128]{1,0:T(8,128)S(1)} %get-tuple-element.114.refs_0_), channel_id=1, source_target_pairs={{0,2},{1,5},{2,0},{3,7},{4,6},{5,1},{6,4},{7,3},{8,10},{9,13},{10,... | collective-permute-start | bytes 12296 | tf_op jit(solution)/shard_map/ppermute | solution.py:473
  93.1 6.5 %collective-permute-start.27 = (f32[264,128]{1,0:T(8,128)S(1)}, f32[264,128]{1,0:T(8,128)S(1)}, u32[]{:S(2)}, u32[]{:S(2)}) collective-permute-start(f32[264,128]{1,0:T(8,128)S(1)} %get-tuple-element.116.refs_0_), channel_id=1, source_target_pairs={{0,4},{1,3},{2,6},{3,1},{4,0},{5,7},{6,2},{7,5},{8,12},{9,11},{10,... | collective-permute-start | bytes 405512 | tf_op jit(solution)/shard_map/ppermute | solution.py:473
  96.6 12.4 %collective-permute-start.31 = (f32[384,128]{1,0:T(8,128)S(1)}, f32[384,128]{1,0:T(8,128)S(1)}, u32[]{:S(2)}, u32[]{:S(2)}) collective-permute-start(f32[384,128]{1,0:T(8,128)S(1)} %get-tuple-element.130), channel_id=1, source_target_pairs={{0,1},{1,0},{2,3},{3,2},{4,5},{5,4},{6,7},{7,6},{8,9},{9,8},{10,11... | collective-permute-start | bytes 589832 | tf_op jit(solution)/shard_map/ppermute | solution.py:463
  99.6 4.4 %collective-permute-start.28 = (f32[136,128]{1,0:T(8,128)S(1)}, f32[136,128]{1,0:T(8,128)S(1)}, u32[]{:S(2)}, u32[]{:S(2)}) collective-permute-start(f32[136,128]{1,0:T(8,128)S(1)} %get-tuple-element.120.refs_0_), channel_id=1, source_target_pairs={{0,8},{1,17},{2,10},{3,19},{4,12},{5,21},{6,14},{7,23},{8,0},{9,25... | collective-permute-start | bytes 208904 | tf_op jit(solution)/shard_map/ppermute | solution.py:473
  104.0 4.9 %collective-permute-start.29 = (f32[72,128]{1,0:T(8,128)S(1)}, f32[72,128]{1,0:T(8,128)S(1)}, u32[]{:S(2)}, u32[]{:S(2)}) collective-permute-start(f32[72,128]{1,0:T(8,128)S(1)} %get-tuple-element.122.sent), channel_id=1, source_target_pairs={{0,16},{1,9},{2,18},{3,11},{4,20},{5,13},{6,22},{7,15},{8,24},{9,1... | collective-permute-start | bytes 110600 | tf_op jit(solution)/shard_map/ppermute | solution.py:473
  109.0 1.3 %collective-permute-start.30 = (f32[40,128]{1,0:T(8,128)S(1)}, f32[40,128]{1,0:T(8,128)S(1)}, u32[]{:S(2)}, u32[]{:S(2)}) collective-permute-start(f32[40,128]{1,0:T(8,128)S(1)} %get-tuple-element.127), channel_id=1, source_target_pairs={{0,1},{1,0},{2,3},{3,2},{4,5},{5,4},{6,7},{7,6},{8,9},{9,8},{10,11... | collective-permute-start | bytes 61448 | tf_op jit(solution)/shard_map/ppermute | solution.py:463
  (10 other events, 44.9 us)

commit v16 on v15

--- a/solution.py
+++ b/solution.py
@@ -148,15 +148,14 @@
     )(feats)
 
 
-def first_kernel(devices, feats, turned, weights, users, own_mean, other_mean, send, keep, old, mean):
+def first_kernel(devices, feats, turned, weights, users, own_mean, other_mean, send, offset, old, mean):
     place = where_am_i(devices)
     here = place[0]
     mean[...] = dot(feats[...], weights[...].astype(bf16))
-    for grad, means, which in ((send, other_mean, 1 - here), (keep, own_mean, here)):
-        mean_now = half_of(mean, which)
-        means[...] = mean_now
-        offset = (half_of(users, which) - mean_now).astype(bf16)
-        grad[...] = dot(turned[...], offset)
+    other_mean[...] = half_of(mean, 1 - here)
+    send[...] = dot(turned[...], (half_of(users, 1 - here) - other_mean[...]).astype(bf16))
+    own_mean[...] = half_of(mean, here)
+    offset[...] = (half_of(users, here) - own_mean[...]).astype(bf16)
     rows, width = old.shape
     old[...] = weights[rows_at(2 * place[1] + place[2], rows), rows_at(here, width)]
 
@@ -167,14 +166,33 @@
     width = rank // CORES
     return pl.pallas_call(
         functools.partial(first_kernel, devices),
-        out_shape=(shape(rows, width),) * 2 + (shape(feat, width),) * 2 + (shape(feat // 4, width),),
+        out_shape=(shape(rows, width),) * 2
+        + (shape(feat, width), shape(rows, width, dtype=bf16), shape(feat // 4, width)),
         in_specs=[VMEM] * 4,
         out_specs=(VMEM,) * 5,
         scratch_shapes=[pltpu.VMEM(users.shape, f32)],
         compiler_params=PARAMS,
-        cost_estimate=cost(4 * rows * feat * rank, 8 * feat * rank),
+        cost_estimate=cost(3 * rows * feat * rank, 8 * feat * rank),
         name="first_pass",
     )(feats, turned, weights, users)
+
+
+def keep_kernel(turned, offset, grad):
+    grad[...] = dot(turned[...], offset[...])
+
+
+def keep_pass(turned, offset):
+    feat, rows = turned.shape
+    width = offset.shape[1]
+    return pl.pallas_call(
+        keep_kernel,
+        out_shape=shape(feat, width),
+        in_specs=[VMEM] * 2,
+        out_specs=VMEM,
+        compiler_params=PARAMS,
+        cost_estimate=cost(2 * rows * feat * width, 4 * feat * width),
+        name="keep_pass",
+    )(turned, offset)
 
 
 def widen_kernel(narrow, later, *wide):
@@ -456,7 +474,7 @@
 def bit_order(devices, core):
     bits = devices.bit_length() - 1
     far = list(range(3, bits))
-    return [1, 2] + far if core == 0 else [2, 1] + far[::-1]
+    return [2, 1] + far if core == 0 else [1, 2] + far[::-1]
 
 
 def swap(array, devices):
@@ -504,9 +522,10 @@
     feat = prior_weights.shape[0]
     rate = rate_scale / (user_factors.shape[0] * devices)
     own_turned = turn_pass(side_features)
-    own_mean, other_mean, send, held, old = first_pass(
+    own_mean, other_mean, send, offset, old = first_pass(
         devices, side_features, own_turned, prior_weights, user_factors
     )
+    held = keep_pass(own_turned, offset)
     send, held = step_pass(True, 0, devices, held, swap(send, devices), feat)
     users, items = user_factors, [item_factors]
     for stratum in range(strata):

time: 111 us -> 113 us (1.018)
  waiting for transfers between devices: 66.8 us -> 78.4 us
  starting transfers between devices: 29.9 us -> 19.8 us
    ppermute x19, waiting for transfers between devices: 61.8 us -> 73.3 us  [exchange(): return lax.ppermute(array, 'user', pairs)]
    ppermute x19, starting transfers between devices: 26.7 us -> 17.2 us  [exchange(): return lax.ppermute(array, 'user', pairs)]
  transfers between devices with their start and end apart: 32 -> 32, of which waited for: 22 -> 21; matrix products, arithmetic and copies ran while one was open for 0% -> 0% of each run, Pallas kernels for 6% -> 6%
where the time goes in v16:
time: 113 us
  waiting for transfers between devices  78.4 us (69%)
  starting transfers between devices  19.8 us (18%)
  Pallas kernels  11.7 us (10%)
  local copies, waits for them, and re-layouts  2.26 us (2%)
    ppermute x19, waiting for transfers between devices, exchange(): return lax.ppermute(array, 'user', pairs)  73.3 us
    ppermute x19, starting transfers between devices, exchange(): return lax.ppermute(array, 'user', pairs)  17.2 us
    ppermute x11, waiting for transfers between devices, swap(): return lax.ppermute(array, 'user', [(i, i ^ 1) for i in range(devices)])  5.09 us
    pallas_call x3, Pallas kernels, error_pass(): pl.pallas_call(functools.partial(error_kernel, stratum), out_shape=(shape...  3.19 us
    unnamed x21, local copies, waits for them, and re-layouts  2.26 us
  transfers between devices with their start and end apart: 32, of which 21 were waited for; matrix products, arithmetic and copies ran while one was open for 0% of the time, Pallas kernels for 6%

profile of v16, /device:TPU:0, one launch (start us, length us, event | category | flops | bytes accessed | tf_op | source)
XLA Modules:
  0.0 113.2 jit_solution(6872604499544435192)
XLA Ops:
  0.6 1.1 copy-done
  3.1 1.1 first_pass.1
  5.2 1.2 %collective-permute-done.got = f32[1024,128]{1,0:T(8,128)S(1)} collective-permute-done((f32[1024,128]{1,0:T(8,128)S(1)}, f32[1024,128]{1,0:T(8,128)S(1)}, u32[]{:S(2)}, u32[]{:S(2)}) %collective-permute-start) | collective-permute-done | bytes 524320 | tf_op jit(solution)/shard_map/ppermute | solution.py:481
  6.4 3.0 %collective-permute-start.1 = (f32[512,128]{1,0:T(8,128)S(1)}, f32[512,128]{1,0:T(8,128)S(1)}, u32[]{:S(2)}, u32[]{:S(2)}) collective-permute-start(f32[512,128]{1,0:T(8,128)S(1)} %get-tuple-element.71), channel_id=1, source_target_pairs={{0,4},{1,3},{2,6},{3,1},{4,0},{5,7},{6,2},{7,5},{8,12},{9,11},{10,... | collective-permute-start | bytes 786440 | tf_op jit(solution)/shard_map/ppermute | solution.py:491
  9.4 1.1 error_pass.3
  10.6 3.6 %collective-permute-done.2.refs_1_ = f32[8,128]{1,0:T(8,128)S(1)} collective-permute-done((f32[8,128]{1,0:T(8,128)S(1)}, f32[8,128]{1,0:T(8,128)S(1)}, u32[]{:S(2)}, u32[]{:S(2)}) %collective-permute-start.2) | collective-permute-done | bytes 4128 | tf_op jit(solution)/shard_map/ppermute | solution.py:491
  14.2 1.7 %collective-permute-start.3 = (f32[264,128]{1,0:T(8,128)S(1)}, f32[264,128]{1,0:T(8,128)S(1)}, u32[]{:S(2)}, u32[]{:S(2)}) collective-permute-start(f32[264,128]{1,0:T(8,128)S(1)} %get-tuple-element.74.refs_0_), channel_id=1, source_target_pairs={{0,2},{1,5},{2,0},{3,7},{4,6},{5,1},{6,4},{7,3},{8,10},{9,13},{10,... | collective-permute-start | bytes 405512 | tf_op jit(solution)/shard_map/ppermute | solution.py:491
  16.4 2.9 %collective-permute-done.3.got.refs_1_ = f32[264,128]{1,0:T(8,128)S(1)} collective-permute-done((f32[264,128]{1,0:T(8,128)S(1)}, f32[264,128]{1,0:T(8,128)S(1)}, u32[]{:S(2)}, u32[]{:S(2)}) %collective-permute-start.3) | collective-permute-done | bytes 135200 | tf_op jit(solution)/shard_map/ppermute | solution.py:491
  19.5 1.7 %collective-permute-start.7 = (f32[264,128]{1,0:T(8,128)S(1)}, f32[264,128]{1,0:T(8,128)S(1)}, u32[]{:S(2)}, u32[]{:S(2)}) collective-permute-start(f32[264,128]{1,0:T(8,128)S(1)} %step_pass.12.later.held.refs_0_), channel_id=1, source_target_pairs={{0,8},{1,17},{2,10},{3,19},{4,12},{5,21},{6,14},{7,23},{8,0},{9,25... | collective-permute-start | bytes 405512 | tf_op jit(solution)/shard_map/ppermute | solution.py:491
  21.2 1.2 %collective-permute-start.5 = (f32[128,1024]{1,0:T(8,128)S(1)}, f32[128,1024]{1,0:T(8,128)S(1)}, u32[]{:S(2)}, u32[]{:S(2)}) collective-permute-start(f32[128,1024]{1,0:T(8,128)S(1)} %get-tuple-element.78), channel_id=1, source_target_pairs={{0,1},{1,0},{2,3},{3,2},{4,5},{5,4},{6,7},{7,6},{8,9},{9,8},{10,11... | collective-permute-start | bytes 1572872 | tf_op jit(solution)/shard_map/ppermute | solution.py:481
  22.4 3.6 %collective-permute-done.7.got.refs_1_ = f32[264,128]{1,0:T(8,128)S(1)} collective-permute-done((f32[264,128]{1,0:T(8,128)S(1)}, f32[264,128]{1,0:T(8,128)S(1)}, u32[]{:S(2)}, u32[]{:S(2)}) %collective-permute-start.7) | collective-permute-done | bytes 135200 | tf_op jit(solution)/shard_map/ppermute | solution.py:491
  26.0 2.1 %collective-permute-start.8 = (f32[264,128]{1,0:T(8,128)S(1)}, f32[264,128]{1,0:T(8,128)S(1)}, u32[]{:S(2)}, u32[]{:S(2)}) collective-permute-start(f32[264,128]{1,0:T(8,128)S(1)} %step_pass.13.held.sent), channel_id=1, source_target_pairs={{0,16},{1,9},{2,18},{3,11},{4,20},{5,13},{6,22},{7,15},{8,24},{9,1... | collective-permute-start | bytes 405512 | tf_op jit(solution)/shard_map/ppermute | solution.py:491
  28.1 4.6 %collective-permute-done.8.got = f32[264,128]{1,0:T(8,128)S(1)} collective-permute-done((f32[264,128]{1,0:T(8,128)S(1)}, f32[264,128]{1,0:T(8,128)S(1)}, u32[]{:S(2)}, u32[]{:S(2)}) %collective-permute-start.8) | collective-permute-done | bytes 135200 | tf_op jit(solution)/shard_map/ppermute | solution.py:491
  32.8 1.8 %collective-permute-start.9 = (f32[256,128]{1,0:T(8,128)S(1)}, f32[256,128]{1,0:T(8,128)S(1)}, u32[]{:S(2)}, u32[]{:S(2)}) collective-permute-start(f32[256,128]{1,0:T(8,128)S(1)} %get-tuple-element.83.part.old), channel_id=1, source_target_pairs={{0,2},{1,5},{2,0},{3,7},{4,6},{5,1},{6,4},{7,3},{8,10},{9,13},{10,... | collective-permute-start | bytes 393224 | tf_op jit(solution)/shard_map/ppermute | solution.py:491
  35.1 2.8 %collective-permute-done.9.got = f32[256,128]{1,0:T(8,128)S(1)} collective-permute-done((f32[256,128]{1,0:T(8,128)S(1)}, f32[256,128]{1,0:T(8,128)S(1)}, u32[]{:S(2)}, u32[]{:S(2)}) %collective-permute-start.9) | collective-permute-done | bytes 131104 | tf_op jit(solution)/shard_map/ppermute | solution.py:491
  37.9 1.8 %collective-permute-start.11 = (f32[512,128]{1,0:T(8,128)S(1)}, f32[512,128]{1,0:T(8,128)S(1)}, u32[]{:S(2)}, u32[]{:S(2)}) collective-permute-start(f32[512,128]{1,0:T(8,128)S(1)} %gather_pass.2.part), channel_id=1, source_target_pairs={{0,4},{1,3},{2,6},{3,1},{4,0},{5,7},{6,2},{7,5},{8,12},{9,11},{10,... | collective-permute-start | bytes 786440 | tf_op jit(solution)/shard_map/ppermute | solution.py:491
  41.1 7.4 %collective-permute-done.11.got = f32[512,128]{1,0:T(8,128)S(1)} collective-permute-done((f32[512,128]{1,0:T(8,128)S(1)}, f32[512,128]{1,0:T(8,128)S(1)}, u32[]{:S(2)}, u32[]{:S(2)}) %collective-permute-start.11) | collective-permute-done | bytes 262176 | tf_op jit(solution)/shard_map/ppermute | solution.py:491
  50.5 2.1 %collective-permute-start.15 = (f32[8,128]{1,0:T(8,128)S(1)}, f32[8,128]{1,0:T(8,128)S(1)}, u32[]{:S(2)}, u32[]{:S(2)}) collective-permute-start(f32[8,128]{1,0:T(8,128)S(1)} %get-tuple-element.96.refs_0_), channel_id=1, source_target_pairs={{0,4},{1,3},{2,6},{3,1},{4,0},{5,7},{6,2},{7,5},{8,12},{9,11},{10,... | collective-permute-start | bytes 12296 | tf_op jit(solution)/shard_map/ppermute | solution.py:491
  52.6 3.3 %collective-permute-done.15.refs_1_ = f32[8,128]{1,0:T(8,128)S(1)} collective-permute-done((f32[8,128]{1,0:T(8,128)S(1)}, f32[8,128]{1,0:T(8,128)S(1)}, u32[]{:S(2)}, u32[]{:S(2)}) %collective-permute-start.15) | collective-permute-done | bytes 4128 | tf_op jit(solution)/shard_map/ppermute | solution.py:491
  56.5 4.5 %collective-permute-done.16.got.refs_1_ = f32[264,128]{1,0:T(8,128)S(1)} collective-permute-done((f32[264,128]{1,0:T(8,128)S(1)}, f32[264,128]{1,0:T(8,128)S(1)}, u32[]{:S(2)}, u32[]{:S(2)}) %collective-permute-start.16) | collective-permute-done | bytes 135200 | tf_op jit(solution)/shard_map/ppermute | solution.py:491
  61.2 4.9 %collective-permute-done.17.got.refs_1_ = f32[264,128]{1,0:T(8,128)S(1)} collective-permute-done((f32[264,128]{1,0:T(8,128)S(1)}, f32[264,128]{1,0:T(8,128)S(1)}, u32[]{:S(2)}, u32[]{:S(2)}) %collective-permute-start.17) | collective-permute-done | bytes 135200 | tf_op jit(solution)/shard_map/ppermute | solution.py:491
  66.4 6.6 %collective-permute-done.18.got = f32[264,128]{1,0:T(8,128)S(1)} collective-permute-done((f32[264,128]{1,0:T(8,128)S(1)}, f32[264,128]{1,0:T(8,128)S(1)}, u32[]{:S(2)}, u32[]{:S(2)}) %collective-permute-start.18) | collective-permute-done | bytes 135200 | tf_op jit(solution)/shard_map/ppermute | solution.py:491
  74.7 4.3 %collective-permute-done.19.got = f32[256,128]{1,0:T(8,128)S(1)} collective-permute-done((f32[256,128]{1,0:T(8,128)S(1)}, f32[256,128]{1,0:T(8,128)S(1)}, u32[]{:S(2)}, u32[]{:S(2)}) %collective-permute-start.19) | collective-permute-done | bytes 131104 | tf_op jit(solution)/shard_map/ppermute | solution.py:491
  80.6 7.6 %collective-permute-done.22.got = f32[512,128]{1,0:T(8,128)S(1)} collective-permute-done((f32[512,128]{1,0:T(8,128)S(1)}, f32[512,128]{1,0:T(8,128)S(1)}, u32[]{:S(2)}, u32[]{:S(2)}) %collective-permute-start.22) | collective-permute-done | bytes 262176 | tf_op jit(solution)/shard_map/ppermute | solution.py:491
  88.2 1.2 %prior_pass.3 = (f32[384,128]{1,0:T(8,128)S(1)}, f32[384,128]{1,0:T(8,128)S(1)}, f32[512,128]{1,0:T(8,128)S(1)}, f32[512,128]{1,0:T(8,128)S(1)}, f32[64,128]{1,0:T(8,128)S(1)}) custom-call(bf16[768,1024]{1,0:T(8,128)(2,1)S(1)} %get-tuple-element.80.feats, bf16[1024,768]{1,0:T(8,128)(2,1)S(1)} %get-tuple-element.81.turned, f32[768,128]{1,0:T(8,128)S(1)} %part_pass.3.begun, ...), custom_call_target="tpu_custom_call" | custom-call | flops 402653184 | bytes 3145728 | tf_op jit(solution)/shard_map/prior_pass/pallas_call | solution.py:309
  89.5 1.1 error_pass.5
  90.6 2.1 %collective-permute-start.26 = (f32[8,128]{1,0:T(8,128)S(1)}, f32[8,128]{1,0:T(8,128)S(1)}, u32[]{:S(2)}, u32[]{:S(2)}) collective-permute-start(f32[8,128]{1,0:T(8,128)S(1)} %get-tuple-element.114.refs_0_), channel_id=1, source_target_pairs={{0,4},{1,3},{2,6},{3,1},{4,0},{5,7},{6,2},{7,5},{8,12},{9,11},{10,... | collective-permute-start | bytes 12296 | tf_op jit(solution)/shard_map/ppermute | solution.py:491
  92.7 3.7 %collective-permute-done.26.refs_1_ = f32[8,128]{1,0:T(8,128)S(1)} collective-permute-done((f32[8,128]{1,0:T(8,128)S(1)}, f32[8,128]{1,0:T(8,128)S(1)}, u32[]{:S(2)}, u32[]{:S(2)}) %collective-permute-start.26) | collective-permute-done | bytes 4128 | tf_op jit(solution)/shard_map/ppermute | solution.py:491
  97.1 4.4 %collective-permute-done.27.got.refs_1_ = f32[264,128]{1,0:T(8,128)S(1)} collective-permute-done((f32[264,128]{1,0:T(8,128)S(1)}, f32[264,128]{1,0:T(8,128)S(1)}, u32[]{:S(2)}, u32[]{:S(2)}) %collective-permute-start.27) | collective-permute-done | bytes 135200 | tf_op jit(solution)/shard_map/ppermute | solution.py:491
  101.7 4.3 %collective-permute-done.28.got.refs_1_ = f32[136,128]{1,0:T(8,128)S(1)} collective-permute-done((f32[136,128]{1,0:T(8,128)S(1)}, f32[136,128]{1,0:T(8,128)S(1)}, u32[]{:S(2)}, u32[]{:S(2)}) %collective-permute-start.28) | collective-permute-done | bytes 69664 | tf_op jit(solution)/shard_map/ppermute | solution.py:491
  106.0 4.8 %collective-permute-done.29.got = f32[72,128]{1,0:T(8,128)S(1)} collective-permute-done((f32[72,128]{1,0:T(8,128)S(1)}, f32[72,128]{1,0:T(8,128)S(1)}, u32[]{:S(2)}, u32[]{:S(2)}) %collective-permute-start.29) | collective-permute-done | bytes 36896 | tf_op jit(solution)/shard_map/ppermute | solution.py:491
  111.0 1.2 %collective-permute-done.30.got = f32[40,128]{1,0:T(8,128)S(1)} collective-permute-done((f32[40,128]{1,0:T(8,128)S(1)}, f32[40,128]{1,0:T(8,128)S(1)}, u32[]{:S(2)}, u32[]{:S(2)}) %collective-permute-start.30) | collective-permute-done | bytes 20512 | tf_op jit(solution)/shard_map/ppermute | solution.py:481
  (87 shorter events, 13.6 us)
Async XLA Ops:
  4.3 2.0 %collective-permute-start = (f32[1024,128]{1,0:T(8,128)S(1)}, f32[1024,128]{1,0:T(8,128)S(1)}, u32[]{:S(2)}, u32[]{:S(2)}) collective-permute-start(f32[1024,128]{1,0:T(8,128)S(1)} %get-tuple-element.69), channel_id=1, source_target_pairs={{0,1},{1,0},{2,3},{3,2},{4,5},{5,4},{6,7},{7,6},{8,9},{9,8},{10,11... | collective-permute-start | bytes 1572872 | tf_op jit(solution)/shard_map/ppermute | solution.py:481
  6.4 7.8 %collective-permute-start.1 = (f32[512,128]{1,0:T(8,128)S(1)}, f32[512,128]{1,0:T(8,128)S(1)}, u32[]{:S(2)}, u32[]{:S(2)}) collective-permute-start(f32[512,128]{1,0:T(8,128)S(1)} %get-tuple-element.71), channel_id=1, source_target_pairs={{0,4},{1,3},{2,6},{3,1},{4,0},{5,7},{6,2},{7,5},{8,12},{9,11},{10,... | collective-permute-start | bytes 786440 | tf_op jit(solution)/shard_map/ppermute | solution.py:491
  10.5 3.7 %collective-permute-start.2 = (f32[8,128]{1,0:T(8,128)S(1)}, f32[8,128]{1,0:T(8,128)S(1)}, u32[]{:S(2)}, u32[]{:S(2)}) collective-permute-start(f32[8,128]{1,0:T(8,128)S(1)} %get-tuple-element.72.refs_0_), channel_id=1, source_target_pairs={{0,4},{1,3},{2,6},{3,1},{4,0},{5,7},{6,2},{7,5},{8,12},{9,11},{10,... | collective-permute-start | bytes 12296 | tf_op jit(solution)/shard_map/ppermute | solution.py:491
  14.2 5.1 %collective-permute-start.3 = (f32[264,128]{1,0:T(8,128)S(1)}, f32[264,128]{1,0:T(8,128)S(1)}, u32[]{:S(2)}, u32[]{:S(2)}) collective-permute-start(f32[264,128]{1,0:T(8,128)S(1)} %get-tuple-element.74.refs_0_), channel_id=1, source_target_pairs={{0,2},{1,5},{2,0},{3,7},{4,6},{5,1},{6,4},{7,3},{8,10},{9,13},{10,... | collective-permute-start | bytes 405512 | tf_op jit(solution)/shard_map/ppermute | solution.py:491
  19.4 20.3 %collective-permute-start.4 = (f32[128,1024]{1,0:T(8,128)S(1)}, f32[128,1024]{1,0:T(8,128)S(1)}, u32[]{:S(2)}, u32[]{:S(2)}) collective-permute-start(f32[128,1024]{1,0:T(8,128)S(1)} %get-tuple-element.77), channel_id=1, source_target_pairs={{0,1},{1,0},{2,3},{3,2},{4,5},{5,4},{6,7},{7,6},{8,9},{9,8},{10,11... | collective-permute-start | bytes 1572872 | tf_op jit(solution)/shard_map/ppermute | solution.py:481
  19.5 6.5 %collective-permute-start.7 = (f32[264,128]{1,0:T(8,128)S(1)}, f32[264,128]{1,0:T(8,128)S(1)}, u32[]{:S(2)}, u32[]{:S(2)}) collective-permute-start(f32[264,128]{1,0:T(8,128)S(1)} %step_pass.12.later.held.refs_0_), channel_id=1, source_target_pairs={{0,8},{1,17},{2,10},{3,19},{4,12},{5,21},{6,14},{7,23},{8,0},{9,25... | collective-permute-start | bytes 405512 | tf_op jit(solution)/shard_map/ppermute | solution.py:491
  21.2 18.5 %collective-permute-start.5 = (f32[128,1024]{1,0:T(8,128)S(1)}, f32[128,1024]{1,0:T(8,128)S(1)}, u32[]{:S(2)}, u32[]{:S(2)}) collective-permute-start(f32[128,1024]{1,0:T(8,128)S(1)} %get-tuple-element.78), channel_id=1, source_target_pairs={{0,1},{1,0},{2,3},{3,2},{4,5},{5,4},{6,7},{7,6},{8,9},{9,8},{10,11... | collective-permute-start | bytes 1572872 | tf_op jit(solution)/shard_map/ppermute | solution.py:481
  22.4 17.3 %collective-permute-start.6 = (f32[128,1024]{1,0:T(8,128)S(1)}, f32[128,1024]{1,0:T(8,128)S(1)}, u32[]{:S(2)}, u32[]{:S(2)}) collective-permute-start(f32[128,1024]{1,0:T(8,128)S(1)} %get-tuple-element.79), channel_id=1, source_target_pairs={{0,1},{1,0},{2,3},{3,2},{4,5},{5,4},{6,7},{7,6},{8,9},{9,8},{10,11... | collective-permute-start | bytes 1572872 | tf_op jit(solution)/shard_map/ppermute | solution.py:481
  26.0 6.7 %collective-permute-start.8 = (f32[264,128]{1,0:T(8,128)S(1)}, f32[264,128]{1,0:T(8,128)S(1)}, u32[]{:S(2)}, u32[]{:S(2)}) collective-permute-start(f32[264,128]{1,0:T(8,128)S(1)} %step_pass.13.held.sent), channel_id=1, source_target_pairs={{0,16},{1,9},{2,18},{3,11},{4,20},{5,13},{6,22},{7,15},{8,24},{9,1... | collective-permute-start | bytes 405512 | tf_op jit(solution)/shard_map/ppermute | solution.py:491
  32.8 1.8 %collective-permute-start.10 = (f32[8,128]{1,0:T(8,128)S(1)}, f32[8,128]{1,0:T(8,128)S(1)}, u32[]{:S(2)}, u32[]{:S(2)}) collective-permute-start(f32[8,128]{1,0:T(8,128)S(1)} %get-tuple-element.84.stats), channel_id=1, source_target_pairs={{0,1},{1,0},{2,3},{3,2},{4,5},{5,4},{6,7},{7,6},{8,9},{9,8},{10,11... | collective-permute-start | bytes 12296 | tf_op jit(solution)/shard_map/ppermute | solution.py:481
  32.8 5.0 %collective-permute-start.9 = (f32[256,128]{1,0:T(8,128)S(1)}, f32[256,128]{1,0:T(8,128)S(1)}, u32[]{:S(2)}, u32[]{:S(2)}) collective-permute-start(f32[256,128]{1,0:T(8,128)S(1)} %get-tuple-element.83.part.old), channel_id=1, source_target_pairs={{0,2},{1,5},{2,0},{3,7},{4,6},{5,1},{6,4},{7,3},{8,10},{9,13},{10,... | collective-permute-start | bytes 393224 | tf_op jit(solution)/shard_map/ppermute | solution.py:491
  34.8 13.7 %collective-permute-start.13 = (f32[384,256]{1,0:T(8,128)S(1)}, f32[384,256]{1,0:T(8,128)S(1)}, u32[]{:S(2)}, u32[]{:S(2)}) collective-permute-start(f32[384,256]{1,0:T(8,128)S(1)} %get-tuple-element.93), channel_id=1, source_target_pairs={{0,1},{1,2},{2,3},{3,4},{4,5},{5,6},{6,7},{7,8},{8,9},{9,10},{10,1... | collective-permute-start | bytes 1179656 | tf_op jit(solution)/shard_map/ppermute | solution.py:485
  37.9 10.6 %collective-permute-start.11 = (f32[512,128]{1,0:T(8,128)S(1)}, f32[512,128]{1,0:T(8,128)S(1)}, u32[]{:S(2)}, u32[]{:S(2)}) collective-permute-start(f32[512,128]{1,0:T(8,128)S(1)} %gather_pass.2.part), channel_id=1, source_target_pairs={{0,4},{1,3},{2,6},{3,1},{4,0},{5,7},{6,2},{7,5},{8,12},{9,11},{10,... | collective-permute-start | bytes 786440 | tf_op jit(solution)/shard_map/ppermute | solution.py:491
  39.7 1.4 %collective-permute-start.12 = (f32[384,128]{1,0:T(8,128)S(1)}, f32[384,128]{1,0:T(8,128)S(1)}, u32[]{:S(2)}, u32[]{:S(2)}) collective-permute-start(f32[384,128]{1,0:T(8,128)S(1)} %get-tuple-element.92), channel_id=1, source_target_pairs={{0,1},{1,0},{2,3},{3,2},{4,5},{5,4},{6,7},{7,6},{8,9},{9,8},{10,11... | collective-permute-start | bytes 589832 | tf_op jit(solution)/shard_map/ppermute | solution.py:481
  49.4 6.5 %collective-permute-start.14 = (f32[512,128]{1,0:T(8,128)S(1)}, f32[512,128]{1,0:T(8,128)S(1)}, u32[]{:S(2)}, u32[]{:S(2)}) collective-permute-start(f32[512,128]{1,0:T(8,128)S(1)} %get-tuple-element.95.refs_0_), channel_id=1, source_target_pairs={{0,4},{1,3},{2,6},{3,1},{4,0},{5,7},{6,2},{7,5},{8,12},{9,11},{10,... | collective-permute-start | bytes 786440 | tf_op jit(solution)/shard_map/ppermute | solution.py:491
  50.5 5.3 %collective-permute-start.15 = (f32[8,128]{1,0:T(8,128)S(1)}, f32[8,128]{1,0:T(8,128)S(1)}, u32[]{:S(2)}, u32[]{:S(2)}) collective-permute-start(f32[8,128]{1,0:T(8,128)S(1)} %get-tuple-element.96.refs_0_), channel_id=1, source_target_pairs={{0,4},{1,3},{2,6},{3,1},{4,0},{5,7},{6,2},{7,5},{8,12},{9,11},{10,... | collective-permute-start | bytes 12296 | tf_op jit(solution)/shard_map/ppermute | solution.py:491
  55.9 5.1 %collective-permute-start.16 = (f32[264,128]{1,0:T(8,128)S(1)}, f32[264,128]{1,0:T(8,128)S(1)}, u32[]{:S(2)}, u32[]{:S(2)}) collective-permute-start(f32[264,128]{1,0:T(8,128)S(1)} %get-tuple-element.98.refs_0_), channel_id=1, source_target_pairs={{0,2},{1,5},{2,0},{3,7},{4,6},{5,1},{6,4},{7,3},{8,10},{9,13},{10,... | collective-permute-start | bytes 405512 | tf_op jit(solution)/shard_map/ppermute | solution.py:491
  61.0 5.1 %collective-permute-start.17 = (f32[264,128]{1,0:T(8,128)S(1)}, f32[264,128]{1,0:T(8,128)S(1)}, u32[]{:S(2)}, u32[]{:S(2)}) collective-permute-start(f32[264,128]{1,0:T(8,128)S(1)} %step_pass.15.held.refs_0_), channel_id=1, source_target_pairs={{0,8},{1,17},{2,10},{3,19},{4,12},{5,21},{6,14},{7,23},{8,0},{9,25... | collective-permute-start | bytes 405512 | tf_op jit(solution)/shard_map/ppermute | solution.py:491
  61.1 12.1 %collective-permute-start.21 = (f32[384,128]{1,0:T(8,128)S(1)}, f32[384,128]{1,0:T(8,128)S(1)}, u32[]{:S(2)}, u32[]{:S(2)}) collective-permute-start(f32[384,128]{1,0:T(8,128)S(1)} %get-tuple-element.105), channel_id=1, source_target_pairs={{0,1},{1,0},{2,3},{3,2},{4,5},{5,4},{6,7},{7,6},{8,9},{9,8},{10,11... | collective-permute-start | bytes 589832 | tf_op jit(solution)/shard_map/ppermute | solution.py:481
  66.1 6.9 %collective-permute-start.18 = (f32[264,128]{1,0:T(8,128)S(1)}, f32[264,128]{1,0:T(8,128)S(1)}, u32[]{:S(2)}, u32[]{:S(2)}) collective-permute-start(f32[264,128]{1,0:T(8,128)S(1)} %step_pass.16.held.sent), channel_id=1, source_target_pairs={{0,16},{1,9},{2,18},{3,11},{4,20},{5,13},{6,22},{7,15},{8,24},{9,1... | collective-permute-start | bytes 405512 | tf_op jit(solution)/shard_map/ppermute | solution.py:491
  73.0 1.2 %collective-permute-start.20 = (f32[8,128]{1,0:T(8,128)S(1)}, f32[8,128]{1,0:T(8,128)S(1)}, u32[]{:S(2)}, u32[]{:S(2)}) collective-permute-start(f32[8,128]{1,0:T(8,128)S(1)} %get-tuple-element.102.stats), channel_id=1, source_target_pairs={{0,1},{1,0},{2,3},{3,2},{4,5},{5,4},{6,7},{7,6},{8,9},{9,8},{10,11... | collective-permute-start | bytes 12296 | tf_op jit(solution)/shard_map/ppermute | solution.py:481
  73.1 5.9 %collective-permute-start.19 = (f32[256,128]{1,0:T(8,128)S(1)}, f32[256,128]{1,0:T(8,128)S(1)}, u32[]{:S(2)}, u32[]{:S(2)}) collective-permute-start(f32[256,128]{1,0:T(8,128)S(1)} %get-tuple-element.101.part), channel_id=1, source_target_pairs={{0,2},{1,5},{2,0},{3,7},{4,6},{5,1},{6,4},{7,3},{8,10},{9,13},{10,... | collective-permute-start | bytes 393224 | tf_op jit(solution)/shard_map/ppermute | solution.py:491
  74.5 13.8 %collective-permute-start.24 = (f32[384,256]{1,0:T(8,128)S(1)}, f32[384,256]{1,0:T(8,128)S(1)}, u32[]{:S(2)}, u32[]{:S(2)}) collective-permute-start(f32[384,256]{1,0:T(8,128)S(1)} %get-tuple-element.111), channel_id=1, source_target_pairs={{0,1},{1,2},{2,3},{3,4},{4,5},{5,6},{6,7},{7,8},{8,9},{9,10},{10,1... | collective-permute-start | bytes 1179656 | tf_op jit(solution)/shard_map/ppermute | solution.py:485
  79.0 9.2 %collective-permute-start.22 = (f32[512,128]{1,0:T(8,128)S(1)}, f32[512,128]{1,0:T(8,128)S(1)}, u32[]{:S(2)}, u32[]{:S(2)}) collective-permute-start(f32[512,128]{1,0:T(8,128)S(1)} %gather_pass.3.part), channel_id=1, source_target_pairs={{0,4},{1,3},{2,6},{3,1},{4,0},{5,7},{6,2},{7,5},{8,12},{9,11},{10,... | collective-permute-start | bytes 786440 | tf_op jit(solution)/shard_map/ppermute | solution.py:491
  79.1 1.5 %collective-permute-start.23 = (f32[384,128]{1,0:T(8,128)S(1)}, f32[384,128]{1,0:T(8,128)S(1)}, u32[]{:S(2)}, u32[]{:S(2)}) collective-permute-start(f32[384,128]{1,0:T(8,128)S(1)} %get-tuple-element.110), channel_id=1, source_target_pairs={{0,1},{1,0},{2,3},{3,2},{4,5},{5,4},{6,7},{7,6},{8,9},{9,8},{10,11... | collective-permute-start | bytes 589832 | tf_op jit(solution)/shard_map/ppermute | solution.py:481
  89.5 7.0 %collective-permute-start.25 = (f32[512,128]{1,0:T(8,128)S(1)}, f32[512,128]{1,0:T(8,128)S(1)}, u32[]{:S(2)}, u32[]{:S(2)}) collective-permute-start(f32[512,128]{1,0:T(8,128)S(1)} %get-tuple-element.113.refs_0_), channel_id=1, source_target_pairs={{0,4},{1,3},{2,6},{3,1},{4,0},{5,7},{6,2},{7,5},{8,12},{9,11},{10,... | collective-permute-start | bytes 786440 | tf_op jit(solution)/shard_map/ppermute | solution.py:491
  90.6 5.8 %collective-permute-start.26 = (f32[8,128]{1,0:T(8,128)S(1)}, f32[8,128]{1,0:T(8,128)S(1)}, u32[]{:S(2)}, u32[]{:S(2)}) collective-permute-start(f32[8,128]{1,0:T(8,128)S(1)} %get-tuple-element.114.refs_0_), channel_id=1, source_target_pairs={{0,4},{1,3},{2,6},{3,1},{4,0},{5,7},{6,2},{7,5},{8,12},{9,11},{10,... | collective-permute-start | bytes 12296 | tf_op jit(solution)/shard_map/ppermute | solution.py:491
  96.5 5.1 %collective-permute-start.27 = (f32[264,128]{1,0:T(8,128)S(1)}, f32[264,128]{1,0:T(8,128)S(1)}, u32[]{:S(2)}, u32[]{:S(2)}) collective-permute-start(f32[264,128]{1,0:T(8,128)S(1)} %get-tuple-element.116.refs_0_), channel_id=1, source_target_pairs={{0,2},{1,5},{2,0},{3,7},{4,6},{5,1},{6,4},{7,3},{8,10},{9,13},{10,... | collective-permute-start | bytes 405512 | tf_op jit(solution)/shard_map/ppermute | solution.py:491
  96.5 14.5 %collective-permute-start.31 = (f32[384,128]{1,0:T(8,128)S(1)}, f32[384,128]{1,0:T(8,128)S(1)}, u32[]{:S(2)}, u32[]{:S(2)}) collective-permute-start(f32[384,128]{1,0:T(8,128)S(1)} %get-tuple-element.130), channel_id=1, source_target_pairs={{0,1},{1,0},{2,3},{3,2},{4,5},{5,4},{6,7},{7,6},{8,9},{9,8},{10,11... | collective-permute-start | bytes 589832 | tf_op jit(solution)/shard_map/ppermute | solution.py:481
  101.6 4.4 %collective-permute-start.28 = (f32[136,128]{1,0:T(8,128)S(1)}, f32[136,128]{1,0:T(8,128)S(1)}, u32[]{:S(2)}, u32[]{:S(2)}) collective-permute-start(f32[136,128]{1,0:T(8,128)S(1)} %get-tuple-element.120.refs_0_), channel_id=1, source_target_pairs={{0,8},{1,17},{2,10},{3,19},{4,12},{5,21},{6,14},{7,23},{8,0},{9,25... | collective-permute-start | bytes 208904 | tf_op jit(solution)/shard_map/ppermute | solution.py:491
  106.0 4.9 %collective-permute-start.29 = (f32[72,128]{1,0:T(8,128)S(1)}, f32[72,128]{1,0:T(8,128)S(1)}, u32[]{:S(2)}, u32[]{:S(2)}) collective-permute-start(f32[72,128]{1,0:T(8,128)S(1)} %get-tuple-element.122.sent), channel_id=1, source_target_pairs={{0,16},{1,9},{2,18},{3,11},{4,20},{5,13},{6,22},{7,15},{8,24},{9,1... | collective-permute-start | bytes 110600 | tf_op jit(solution)/shard_map/ppermute | solution.py:491
  110.9 1.3 %collective-permute-start.30 = (f32[40,128]{1,0:T(8,128)S(1)}, f32[40,128]{1,0:T(8,128)S(1)}, u32[]{:S(2)}, u32[]{:S(2)}) collective-permute-start(f32[40,128]{1,0:T(8,128)S(1)} %get-tuple-element.127), channel_id=1, source_target_pairs={{0,1},{1,0},{2,3},{3,2},{4,5},{5,4},{6,7},{7,6},{8,9},{9,8},{10,11... | collective-permute-start | bytes 61448 | tf_op jit(solution)/shard_map/ppermute | solution.py:481
  (10 other events, 40.3 us)

commit v17 on v15

--- a/solution.py
+++ b/solution.py
@@ -456,7 +456,7 @@
 def bit_order(devices, core):
     bits = devices.bit_length() - 1
     far = list(range(3, bits))
-    return [1, 2] + far if core == 0 else [2, 1] + far[::-1]
+    return [1, 2] + far[::-1] if core == 0 else [2, 1] + far
 
 
 def swap(array, devices):

time: 111 us -> 114 us (1.027)
  waiting for transfers between devices: 66.8 us -> 68.9 us
    ppermute x19, waiting for transfers between devices: 61.8 us -> 63.9 us  [exchange(): return lax.ppermute(array, 'user', pairs)]
    ppermute x19, starting transfers between devices: 26.7 us -> 28.1 us  [exchange(): return lax.ppermute(array, 'user', pairs)]
    ppermute x11, starting transfers between devices: 3.06 us -> 1.67 us  [swap(): return lax.ppermute(array, 'user', [(i, i ^ 1) for i in range(devices)])]
where the time goes in v17:
time: 114 us
  waiting for transfers between devices  68.9 us (60%)
  starting transfers between devices  30 us (26%)
  Pallas kernels  11.3 us (10%)
  local copies, waits for them, and re-layouts  2.25 us (2%)
    ppermute x19, waiting for transfers between devices, exchange(): return lax.ppermute(array, 'user', pairs)  63.9 us
    ppermute x19, starting transfers between devices, exchange(): return lax.ppermute(array, 'user', pairs)  28.1 us
    ppermute x11, waiting for transfers between devices, swap(): return lax.ppermute(array, 'user', [(i, i ^ 1) for i in range(devices)])  4.14 us
    pallas_call x3, Pallas kernels, error_pass(): pl.pallas_call(functools.partial(error_kernel, stratum), out_shape=(shape...  3.2 us
  transfers between devices with their start and end apart: 32, of which 22 were waited for; matrix products, arithmetic and copies ran while one was open for 0% of the time, Pallas kernels for 6%

profile of v17, /device:TPU:0, one launch (start us, length us, event | category | flops | bytes accessed | tf_op | source)
XLA Modules:
  0.0 113.5 jit_solution(14131937354447578049)
XLA Ops:
  0.6 1.1 copy-done
  3.1 1.2 %first_pass.1 = (f32[384,128]{1,0:T(8,128)S(1)}, f32[384,128]{1,0:T(8,128)S(1)}, f32[1024,128]{1,0:T(8,128)S(1)}, f32[1024,128]{1,0:T(8,128)S(1)}, f32[256,128]{1,0:T(8,128)S(1)}) custom-call(bf16[384,1024]{1,0:T(8,128)(2,1)S(1)} %copy-done, bf16[1024,384]{1,0:T(8,128)(2,1)S(1)} %turn_pass.1.turned.refs_0_.own_turned, f32[1024,256]{1,0:T(8,128)S(1)} %copy-done.5, ...), custom_call_target="tpu_custom_call" | custom-call | flops 402653184 | bytes 2097152 | tf_op jit(solution)/shard_map/first_pass/pallas_call | solution.py:168
  4.8 1.5 %collective-permute-done.got = f32[1024,128]{1,0:T(8,128)S(1)} collective-permute-done((f32[1024,128]{1,0:T(8,128)S(1)}, f32[1024,128]{1,0:T(8,128)S(1)}, u32[]{:S(2)}, u32[]{:S(2)}) %collective-permute-start) | collective-permute-done | bytes 524320 | tf_op jit(solution)/shard_map/ppermute | solution.py:463
  6.4 2.9 %collective-permute-start.1 = (f32[512,128]{1,0:T(8,128)S(1)}, f32[512,128]{1,0:T(8,128)S(1)}, u32[]{:S(2)}, u32[]{:S(2)}) collective-permute-start(f32[512,128]{1,0:T(8,128)S(1)} %get-tuple-element.71), channel_id=1, source_target_pairs={{0,2},{1,5},{2,0},{3,7},{4,6},{5,1},{6,4},{7,3},{8,10},{9,13},{10,... | collective-permute-start | bytes 786440 | tf_op jit(solution)/shard_map/ppermute | solution.py:473
  10.6 3.6 %collective-permute-done.2.refs_1_ = f32[8,128]{1,0:T(8,128)S(1)} collective-permute-done((f32[8,128]{1,0:T(8,128)S(1)}, f32[8,128]{1,0:T(8,128)S(1)}, u32[]{:S(2)}, u32[]{:S(2)}) %collective-permute-start.2) | collective-permute-done | bytes 4128 | tf_op jit(solution)/shard_map/ppermute | solution.py:473
  14.2 1.7 %collective-permute-start.3 = (f32[264,128]{1,0:T(8,128)S(1)}, f32[264,128]{1,0:T(8,128)S(1)}, u32[]{:S(2)}, u32[]{:S(2)}) collective-permute-start(f32[264,128]{1,0:T(8,128)S(1)} %get-tuple-element.74.refs_0_), channel_id=1, source_target_pairs={{0,4},{1,3},{2,6},{3,1},{4,0},{5,7},{6,2},{7,5},{8,12},{9,11},{10,... | collective-permute-start | bytes 405512 | tf_op jit(solution)/shard_map/ppermute | solution.py:473
  16.4 2.8 %collective-permute-done.3.got.refs_1_ = f32[264,128]{1,0:T(8,128)S(1)} collective-permute-done((f32[264,128]{1,0:T(8,128)S(1)}, f32[264,128]{1,0:T(8,128)S(1)}, u32[]{:S(2)}, u32[]{:S(2)}) %collective-permute-start.3) | collective-permute-done | bytes 135200 | tf_op jit(solution)/shard_map/ppermute | solution.py:473
  19.5 2.8 %collective-permute-start.7 = (f32[264,128]{1,0:T(8,128)S(1)}, f32[264,128]{1,0:T(8,128)S(1)}, u32[]{:S(2)}, u32[]{:S(2)}) collective-permute-start(f32[264,128]{1,0:T(8,128)S(1)} %step_pass.12.later.held.refs_0_), channel_id=1, source_target_pairs={{0,16},{1,9},{2,18},{3,11},{4,20},{5,13},{6,22},{7,15},{8,24},{9,1... | collective-permute-start | bytes 405512 | tf_op jit(solution)/shard_map/ppermute | solution.py:473
  22.8 3.1 %collective-permute-done.7.got.refs_1_ = f32[264,128]{1,0:T(8,128)S(1)} collective-permute-done((f32[264,128]{1,0:T(8,128)S(1)}, f32[264,128]{1,0:T(8,128)S(1)}, u32[]{:S(2)}, u32[]{:S(2)}) %collective-permute-start.7) | collective-permute-done | bytes 135200 | tf_op jit(solution)/shard_map/ppermute | solution.py:473
  25.9 2.4 %collective-permute-start.8 = (f32[264,128]{1,0:T(8,128)S(1)}, f32[264,128]{1,0:T(8,128)S(1)}, u32[]{:S(2)}, u32[]{:S(2)}) collective-permute-start(f32[264,128]{1,0:T(8,128)S(1)} %step_pass.13.held.sent), channel_id=1, source_target_pairs={{0,8},{1,17},{2,10},{3,19},{4,12},{5,21},{6,14},{7,23},{8,0},{9,25... | collective-permute-start | bytes 405512 | tf_op jit(solution)/shard_map/ppermute | solution.py:473
  28.3 4.4 %collective-permute-done.8.got = f32[264,128]{1,0:T(8,128)S(1)} collective-permute-done((f32[264,128]{1,0:T(8,128)S(1)}, f32[264,128]{1,0:T(8,128)S(1)}, u32[]{:S(2)}, u32[]{:S(2)}) %collective-permute-start.8) | collective-permute-done | bytes 135200 | tf_op jit(solution)/shard_map/ppermute | solution.py:473
  32.7 1.6 %collective-permute-start.9 = (f32[256,128]{1,0:T(8,128)S(1)}, f32[256,128]{1,0:T(8,128)S(1)}, u32[]{:S(2)}, u32[]{:S(2)}) collective-permute-start(f32[256,128]{1,0:T(8,128)S(1)} %get-tuple-element.83.part.old), channel_id=1, source_target_pairs={{0,4},{1,3},{2,6},{3,1},{4,0},{5,7},{6,2},{7,5},{8,12},{9,11},{10,... | collective-permute-start | bytes 393224 | tf_op jit(solution)/shard_map/ppermute | solution.py:473
  34.8 3.0 %collective-permute-done.9.got = f32[256,128]{1,0:T(8,128)S(1)} collective-permute-done((f32[256,128]{1,0:T(8,128)S(1)}, f32[256,128]{1,0:T(8,128)S(1)}, u32[]{:S(2)}, u32[]{:S(2)}) %collective-permute-start.9) | collective-permute-done | bytes 131104 | tf_op jit(solution)/shard_map/ppermute | solution.py:473
  37.8 1.6 %collective-permute-start.11 = (f32[512,128]{1,0:T(8,128)S(1)}, f32[512,128]{1,0:T(8,128)S(1)}, u32[]{:S(2)}, u32[]{:S(2)}) collective-permute-start(f32[512,128]{1,0:T(8,128)S(1)} %gather_pass.2.part), channel_id=1, source_target_pairs={{0,2},{1,5},{2,0},{3,7},{4,6},{5,1},{6,4},{7,3},{8,10},{9,13},{10,... | collective-permute-start | bytes 786440 | tf_op jit(solution)/shard_map/ppermute | solution.py:473
  40.8 4.3 %collective-permute-done.11.got = f32[512,128]{1,0:T(8,128)S(1)} collective-permute-done((f32[512,128]{1,0:T(8,128)S(1)}, f32[512,128]{1,0:T(8,128)S(1)}, u32[]{:S(2)}, u32[]{:S(2)}) %collective-permute-start.11) | collective-permute-done | bytes 262176 | tf_op jit(solution)/shard_map/ppermute | solution.py:473
  48.1 1.6 %collective-permute-start.15 = (f32[8,128]{1,0:T(8,128)S(1)}, f32[8,128]{1,0:T(8,128)S(1)}, u32[]{:S(2)}, u32[]{:S(2)}) collective-permute-start(f32[8,128]{1,0:T(8,128)S(1)} %get-tuple-element.96.refs_0_), channel_id=1, source_target_pairs={{0,2},{1,5},{2,0},{3,7},{4,6},{5,1},{6,4},{7,3},{8,10},{9,13},{10,... | collective-permute-start | bytes 12296 | tf_op jit(solution)/shard_map/ppermute | solution.py:473
  49.7 3.3 %collective-permute-done.15.refs_1_ = f32[8,128]{1,0:T(8,128)S(1)} collective-permute-done((f32[8,128]{1,0:T(8,128)S(1)}, f32[8,128]{1,0:T(8,128)S(1)}, u32[]{:S(2)}, u32[]{:S(2)}) %collective-permute-start.15) | collective-permute-done | bytes 4128 | tf_op jit(solution)/shard_map/ppermute | solution.py:473
  53.0 3.3 %collective-permute-start.16 = (f32[264,128]{1,0:T(8,128)S(1)}, f32[264,128]{1,0:T(8,128)S(1)}, u32[]{:S(2)}, u32[]{:S(2)}) collective-permute-start(f32[264,128]{1,0:T(8,128)S(1)} %get-tuple-element.98.refs_0_), channel_id=1, source_target_pairs={{0,4},{1,3},{2,6},{3,1},{4,0},{5,7},{6,2},{7,5},{8,12},{9,11},{10,... | collective-permute-start | bytes 405512 | tf_op jit(solution)/shard_map/ppermute | solution.py:473
  56.8 2.5 %collective-permute-done.16.got.refs_1_ = f32[264,128]{1,0:T(8,128)S(1)} collective-permute-done((f32[264,128]{1,0:T(8,128)S(1)}, f32[264,128]{1,0:T(8,128)S(1)}, u32[]{:S(2)}, u32[]{:S(2)}) %collective-permute-start.16) | collective-permute-done | bytes 135200 | tf_op jit(solution)/shard_map/ppermute | solution.py:473
  59.4 8.3 %collective-permute-done.17.got.refs_1_ = f32[264,128]{1,0:T(8,128)S(1)} collective-permute-done((f32[264,128]{1,0:T(8,128)S(1)}, f32[264,128]{1,0:T(8,128)S(1)}, u32[]{:S(2)}, u32[]{:S(2)}) %collective-permute-start.17) | collective-permute-done | bytes 135200 | tf_op jit(solution)/shard_map/ppermute | solution.py:473
  67.9 5.0 %collective-permute-done.18.got = f32[264,128]{1,0:T(8,128)S(1)} collective-permute-done((f32[264,128]{1,0:T(8,128)S(1)}, f32[264,128]{1,0:T(8,128)S(1)}, u32[]{:S(2)}, u32[]{:S(2)}) %collective-permute-start.18) | collective-permute-done | bytes 135200 | tf_op jit(solution)/shard_map/ppermute | solution.py:473
  73.0 2.5 %collective-permute-start.19 = (f32[256,128]{1,0:T(8,128)S(1)}, f32[256,128]{1,0:T(8,128)S(1)}, u32[]{:S(2)}, u32[]{:S(2)}) collective-permute-start(f32[256,128]{1,0:T(8,128)S(1)} %get-tuple-element.101.part), channel_id=1, source_target_pairs={{0,4},{1,3},{2,6},{3,1},{4,0},{5,7},{6,2},{7,5},{8,12},{9,11},{10,... | collective-permute-start | bytes 393224 | tf_op jit(solution)/shard_map/ppermute | solution.py:473
  75.8 2.6 %collective-permute-done.19.got = f32[256,128]{1,0:T(8,128)S(1)} collective-permute-done((f32[256,128]{1,0:T(8,128)S(1)}, f32[256,128]{1,0:T(8,128)S(1)}, u32[]{:S(2)}, u32[]{:S(2)}) %collective-permute-start.19) | collective-permute-done | bytes 131104 | tf_op jit(solution)/shard_map/ppermute | solution.py:473
  81.0 5.3 %collective-permute-done.22.got = f32[512,128]{1,0:T(8,128)S(1)} collective-permute-done((f32[512,128]{1,0:T(8,128)S(1)}, f32[512,128]{1,0:T(8,128)S(1)}, u32[]{:S(2)}, u32[]{:S(2)}) %collective-permute-start.22) | collective-permute-done | bytes 262176 | tf_op jit(solution)/shard_map/ppermute | solution.py:473
  86.8 1.2 %prior_pass.3 = (f32[384,128]{1,0:T(8,128)S(1)}, f32[384,128]{1,0:T(8,128)S(1)}, f32[512,128]{1,0:T(8,128)S(1)}, f32[512,128]{1,0:T(8,128)S(1)}, f32[64,128]{1,0:T(8,128)S(1)}) custom-call(bf16[768,1024]{1,0:T(8,128)(2,1)S(1)} %get-tuple-element.80.feats, bf16[1024,768]{1,0:T(8,128)(2,1)S(1)} %get-tuple-element.81.turned, f32[768,128]{1,0:T(8,128)S(1)} %part_pass.3.begun, ...), custom_call_target="tpu_custom_call" | custom-call | flops 402653184 | bytes 3145728 | tf_op jit(solution)/shard_map/prior_pass/pallas_call | solution.py:291
  89.2 2.1 %collective-permute-start.26 = (f32[8,128]{1,0:T(8,128)S(1)}, f32[8,128]{1,0:T(8,128)S(1)}, u32[]{:S(2)}, u32[]{:S(2)}) collective-permute-start(f32[8,128]{1,0:T(8,128)S(1)} %get-tuple-element.114.refs_0_), channel_id=1, source_target_pairs={{0,2},{1,5},{2,0},{3,7},{4,6},{5,1},{6,4},{7,3},{8,10},{9,13},{10,... | collective-permute-start | bytes 12296 | tf_op jit(solution)/shard_map/ppermute | solution.py:473
  91.2 3.3 %collective-permute-done.26.refs_1_ = f32[8,128]{1,0:T(8,128)S(1)} collective-permute-done((f32[8,128]{1,0:T(8,128)S(1)}, f32[8,128]{1,0:T(8,128)S(1)}, u32[]{:S(2)}, u32[]{:S(2)}) %collective-permute-start.26) | collective-permute-done | bytes 4128 | tf_op jit(solution)/shard_map/ppermute | solution.py:473
  94.5 3.5 %collective-permute-start.27 = (f32[264,128]{1,0:T(8,128)S(1)}, f32[264,128]{1,0:T(8,128)S(1)}, u32[]{:S(2)}, u32[]{:S(2)}) collective-permute-start(f32[264,128]{1,0:T(8,128)S(1)} %get-tuple-element.116.refs_0_), channel_id=1, source_target_pairs={{0,4},{1,3},{2,6},{3,1},{4,0},{5,7},{6,2},{7,5},{8,12},{9,11},{10,... | collective-permute-start | bytes 405512 | tf_op jit(solution)/shard_map/ppermute | solution.py:473
  98.6 2.5 %collective-permute-done.27.got.refs_1_ = f32[264,128]{1,0:T(8,128)S(1)} collective-permute-done((f32[264,128]{1,0:T(8,128)S(1)}, f32[264,128]{1,0:T(8,128)S(1)}, u32[]{:S(2)}, u32[]{:S(2)}) %collective-permute-start.27) | collective-permute-done | bytes 135200 | tf_op jit(solution)/shard_map/ppermute | solution.py:473
  101.2 6.0 %collective-permute-done.28.got.refs_1_ = f32[136,128]{1,0:T(8,128)S(1)} collective-permute-done((f32[136,128]{1,0:T(8,128)S(1)}, f32[136,128]{1,0:T(8,128)S(1)}, u32[]{:S(2)}, u32[]{:S(2)}) %collective-permute-start.28) | collective-permute-done | bytes 69664 | tf_op jit(solution)/shard_map/ppermute | solution.py:473
  107.2 3.9 %collective-permute-done.29.got = f32[72,128]{1,0:T(8,128)S(1)} collective-permute-done((f32[72,128]{1,0:T(8,128)S(1)}, f32[72,128]{1,0:T(8,128)S(1)}, u32[]{:S(2)}, u32[]{:S(2)}) %collective-permute-start.29) | collective-permute-done | bytes 36896 | tf_op jit(solution)/shard_map/ppermute | solution.py:473
  111.3 1.2 %collective-permute-done.30.got = f32[40,128]{1,0:T(8,128)S(1)} collective-permute-done((f32[40,128]{1,0:T(8,128)S(1)}, f32[40,128]{1,0:T(8,128)S(1)}, u32[]{:S(2)}, u32[]{:S(2)}) %collective-permute-start.30) | collective-permute-done | bytes 20512 | tf_op jit(solution)/shard_map/ppermute | solution.py:463
  (86 shorter events, 16.5 us)
Async XLA Ops:
  4.3 2.1 %collective-permute-start = (f32[1024,128]{1,0:T(8,128)S(1)}, f32[1024,128]{1,0:T(8,128)S(1)}, u32[]{:S(2)}, u32[]{:S(2)}) collective-permute-start(f32[1024,128]{1,0:T(8,128)S(1)} %get-tuple-element.69), channel_id=1, source_target_pairs={{0,1},{1,0},{2,3},{3,2},{4,5},{5,4},{6,7},{7,6},{8,9},{9,8},{10,11... | collective-permute-start | bytes 1572872 | tf_op jit(solution)/shard_map/ppermute | solution.py:463
  6.4 7.7 %collective-permute-start.1 = (f32[512,128]{1,0:T(8,128)S(1)}, f32[512,128]{1,0:T(8,128)S(1)}, u32[]{:S(2)}, u32[]{:S(2)}) collective-permute-start(f32[512,128]{1,0:T(8,128)S(1)} %get-tuple-element.71), channel_id=1, source_target_pairs={{0,2},{1,5},{2,0},{3,7},{4,6},{5,1},{6,4},{7,3},{8,10},{9,13},{10,... | collective-permute-start | bytes 786440 | tf_op jit(solution)/shard_map/ppermute | solution.py:473
  10.5 3.7 %collective-permute-start.2 = (f32[8,128]{1,0:T(8,128)S(1)}, f32[8,128]{1,0:T(8,128)S(1)}, u32[]{:S(2)}, u32[]{:S(2)}) collective-permute-start(f32[8,128]{1,0:T(8,128)S(1)} %get-tuple-element.72.refs_0_), channel_id=1, source_target_pairs={{0,2},{1,5},{2,0},{3,7},{4,6},{5,1},{6,4},{7,3},{8,10},{9,13},{10,... | collective-permute-start | bytes 12296 | tf_op jit(solution)/shard_map/ppermute | solution.py:473
  14.2 5.1 %collective-permute-start.3 = (f32[264,128]{1,0:T(8,128)S(1)}, f32[264,128]{1,0:T(8,128)S(1)}, u32[]{:S(2)}, u32[]{:S(2)}) collective-permute-start(f32[264,128]{1,0:T(8,128)S(1)} %get-tuple-element.74.refs_0_), channel_id=1, source_target_pairs={{0,4},{1,3},{2,6},{3,1},{4,0},{5,7},{6,2},{7,5},{8,12},{9,11},{10,... | collective-permute-start | bytes 405512 | tf_op jit(solution)/shard_map/ppermute | solution.py:473
  19.4 20.0 %collective-permute-start.4 = (f32[128,1024]{1,0:T(8,128)S(1)}, f32[128,1024]{1,0:T(8,128)S(1)}, u32[]{:S(2)}, u32[]{:S(2)}) collective-permute-start(f32[128,1024]{1,0:T(8,128)S(1)} %get-tuple-element.77), channel_id=1, source_target_pairs={{0,1},{1,0},{2,3},{3,2},{4,5},{5,4},{6,7},{7,6},{8,9},{9,8},{10,11... | collective-permute-start | bytes 1572872 | tf_op jit(solution)/shard_map/ppermute | solution.py:463
  19.5 6.4 %collective-permute-start.7 = (f32[264,128]{1,0:T(8,128)S(1)}, f32[264,128]{1,0:T(8,128)S(1)}, u32[]{:S(2)}, u32[]{:S(2)}) collective-permute-start(f32[264,128]{1,0:T(8,128)S(1)} %step_pass.12.later.held.refs_0_), channel_id=1, source_target_pairs={{0,16},{1,9},{2,18},{3,11},{4,20},{5,13},{6,22},{7,15},{8,24},{9,1... | collective-permute-start | bytes 405512 | tf_op jit(solution)/shard_map/ppermute | solution.py:473
  22.3 17.1 %collective-permute-start.5 = (f32[128,1024]{1,0:T(8,128)S(1)}, f32[128,1024]{1,0:T(8,128)S(1)}, u32[]{:S(2)}, u32[]{:S(2)}) collective-permute-start(f32[128,1024]{1,0:T(8,128)S(1)} %get-tuple-element.78), channel_id=1, source_target_pairs={{0,1},{1,0},{2,3},{3,2},{4,5},{5,4},{6,7},{7,6},{8,9},{9,8},{10,11... | collective-permute-start | bytes 1572872 | tf_op jit(solution)/shard_map/ppermute | solution.py:463
  22.3 17.1 %collective-permute-start.6 = (f32[128,1024]{1,0:T(8,128)S(1)}, f32[128,1024]{1,0:T(8,128)S(1)}, u32[]{:S(2)}, u32[]{:S(2)}) collective-permute-start(f32[128,1024]{1,0:T(8,128)S(1)} %get-tuple-element.79), channel_id=1, source_target_pairs={{0,1},{1,0},{2,3},{3,2},{4,5},{5,4},{6,7},{7,6},{8,9},{9,8},{10,11... | collective-permute-start | bytes 1572872 | tf_op jit(solution)/shard_map/ppermute | solution.py:463
  25.9 6.8 %collective-permute-start.8 = (f32[264,128]{1,0:T(8,128)S(1)}, f32[264,128]{1,0:T(8,128)S(1)}, u32[]{:S(2)}, u32[]{:S(2)}) collective-permute-start(f32[264,128]{1,0:T(8,128)S(1)} %step_pass.13.held.sent), channel_id=1, source_target_pairs={{0,8},{1,17},{2,10},{3,19},{4,12},{5,21},{6,14},{7,23},{8,0},{9,25... | collective-permute-start | bytes 405512 | tf_op jit(solution)/shard_map/ppermute | solution.py:473
  32.7 1.7 %collective-permute-start.10 = (f32[8,128]{1,0:T(8,128)S(1)}, f32[8,128]{1,0:T(8,128)S(1)}, u32[]{:S(2)}, u32[]{:S(2)}) collective-permute-start(f32[8,128]{1,0:T(8,128)S(1)} %get-tuple-element.84.stats), channel_id=1, source_target_pairs={{0,1},{1,0},{2,3},{3,2},{4,5},{5,4},{6,7},{7,6},{8,9},{9,8},{10,11... | collective-permute-start | bytes 12296 | tf_op jit(solution)/shard_map/ppermute | solution.py:463
  32.7 5.0 %collective-permute-start.9 = (f32[256,128]{1,0:T(8,128)S(1)}, f32[256,128]{1,0:T(8,128)S(1)}, u32[]{:S(2)}, u32[]{:S(2)}) collective-permute-start(f32[256,128]{1,0:T(8,128)S(1)} %get-tuple-element.83.part.old), channel_id=1, source_target_pairs={{0,4},{1,3},{2,6},{3,1},{4,0},{5,7},{6,2},{7,5},{8,12},{9,11},{10,... | collective-permute-start | bytes 393224 | tf_op jit(solution)/shard_map/ppermute | solution.py:473
  34.6 11.0 %collective-permute-start.13 = (f32[384,256]{1,0:T(8,128)S(1)}, f32[384,256]{1,0:T(8,128)S(1)}, u32[]{:S(2)}, u32[]{:S(2)}) collective-permute-start(f32[384,256]{1,0:T(8,128)S(1)} %get-tuple-element.93), channel_id=1, source_target_pairs={{0,1},{1,2},{2,3},{3,4},{4,5},{5,6},{6,7},{7,8},{8,9},{9,10},{10,1... | collective-permute-start | bytes 1179656 | tf_op jit(solution)/shard_map/ppermute | solution.py:467
  37.8 7.3 %collective-permute-start.11 = (f32[512,128]{1,0:T(8,128)S(1)}, f32[512,128]{1,0:T(8,128)S(1)}, u32[]{:S(2)}, u32[]{:S(2)}) collective-permute-start(f32[512,128]{1,0:T(8,128)S(1)} %gather_pass.2.part), channel_id=1, source_target_pairs={{0,2},{1,5},{2,0},{3,7},{4,6},{5,1},{6,4},{7,3},{8,10},{9,13},{10,... | collective-permute-start | bytes 786440 | tf_op jit(solution)/shard_map/ppermute | solution.py:473
  39.4 1.4 %collective-permute-start.12 = (f32[384,128]{1,0:T(8,128)S(1)}, f32[384,128]{1,0:T(8,128)S(1)}, u32[]{:S(2)}, u32[]{:S(2)}) collective-permute-start(f32[384,128]{1,0:T(8,128)S(1)} %get-tuple-element.92), channel_id=1, source_target_pairs={{0,1},{1,0},{2,3},{3,2},{4,5},{5,4},{6,7},{7,6},{8,9},{9,8},{10,11... | collective-permute-start | bytes 589832 | tf_op jit(solution)/shard_map/ppermute | solution.py:463
  46.5 6.5 %collective-permute-start.14 = (f32[512,128]{1,0:T(8,128)S(1)}, f32[512,128]{1,0:T(8,128)S(1)}, u32[]{:S(2)}, u32[]{:S(2)}) collective-permute-start(f32[512,128]{1,0:T(8,128)S(1)} %get-tuple-element.95.refs_0_), channel_id=1, source_target_pairs={{0,2},{1,5},{2,0},{3,7},{4,6},{5,1},{6,4},{7,3},{8,10},{9,13},{10,... | collective-permute-start | bytes 786440 | tf_op jit(solution)/shard_map/ppermute | solution.py:473
  48.1 4.8 %collective-permute-start.15 = (f32[8,128]{1,0:T(8,128)S(1)}, f32[8,128]{1,0:T(8,128)S(1)}, u32[]{:S(2)}, u32[]{:S(2)}) collective-permute-start(f32[8,128]{1,0:T(8,128)S(1)} %get-tuple-element.96.refs_0_), channel_id=1, source_target_pairs={{0,2},{1,5},{2,0},{3,7},{4,6},{5,1},{6,4},{7,3},{8,10},{9,13},{10,... | collective-permute-start | bytes 12296 | tf_op jit(solution)/shard_map/ppermute | solution.py:473
  53.0 6.3 %collective-permute-start.16 = (f32[264,128]{1,0:T(8,128)S(1)}, f32[264,128]{1,0:T(8,128)S(1)}, u32[]{:S(2)}, u32[]{:S(2)}) collective-permute-start(f32[264,128]{1,0:T(8,128)S(1)} %get-tuple-element.98.refs_0_), channel_id=1, source_target_pairs={{0,4},{1,3},{2,6},{3,1},{4,0},{5,7},{6,2},{7,5},{8,12},{9,11},{10,... | collective-permute-start | bytes 405512 | tf_op jit(solution)/shard_map/ppermute | solution.py:473
  59.3 8.5 %collective-permute-start.17 = (f32[264,128]{1,0:T(8,128)S(1)}, f32[264,128]{1,0:T(8,128)S(1)}, u32[]{:S(2)}, u32[]{:S(2)}) collective-permute-start(f32[264,128]{1,0:T(8,128)S(1)} %step_pass.15.held.refs_0_), channel_id=1, source_target_pairs={{0,16},{1,9},{2,18},{3,11},{4,20},{5,13},{6,22},{7,15},{8,24},{9,1... | collective-permute-start | bytes 405512 | tf_op jit(solution)/shard_map/ppermute | solution.py:473
  59.4 16.1 %collective-permute-start.21 = (f32[384,128]{1,0:T(8,128)S(1)}, f32[384,128]{1,0:T(8,128)S(1)}, u32[]{:S(2)}, u32[]{:S(2)}) collective-permute-start(f32[384,128]{1,0:T(8,128)S(1)} %get-tuple-element.105), channel_id=1, source_target_pairs={{0,1},{1,0},{2,3},{3,2},{4,5},{5,4},{6,7},{7,6},{8,9},{9,8},{10,11... | collective-permute-start | bytes 589832 | tf_op jit(solution)/shard_map/ppermute | solution.py:463
  67.8 5.1 %collective-permute-start.18 = (f32[264,128]{1,0:T(8,128)S(1)}, f32[264,128]{1,0:T(8,128)S(1)}, u32[]{:S(2)}, u32[]{:S(2)}) collective-permute-start(f32[264,128]{1,0:T(8,128)S(1)} %step_pass.16.held.sent), channel_id=1, source_target_pairs={{0,8},{1,17},{2,10},{3,19},{4,12},{5,21},{6,14},{7,23},{8,0},{9,25... | collective-permute-start | bytes 405512 | tf_op jit(solution)/shard_map/ppermute | solution.py:473
  72.9 2.6 %collective-permute-start.20 = (f32[8,128]{1,0:T(8,128)S(1)}, f32[8,128]{1,0:T(8,128)S(1)}, u32[]{:S(2)}, u32[]{:S(2)}) collective-permute-start(f32[8,128]{1,0:T(8,128)S(1)} %get-tuple-element.102.stats), channel_id=1, source_target_pairs={{0,1},{1,0},{2,3},{3,2},{4,5},{5,4},{6,7},{7,6},{8,9},{9,8},{10,11... | collective-permute-start | bytes 12296 | tf_op jit(solution)/shard_map/ppermute | solution.py:463
  73.0 5.5 %collective-permute-start.19 = (f32[256,128]{1,0:T(8,128)S(1)}, f32[256,128]{1,0:T(8,128)S(1)}, u32[]{:S(2)}, u32[]{:S(2)}) collective-permute-start(f32[256,128]{1,0:T(8,128)S(1)} %get-tuple-element.101.part), channel_id=1, source_target_pairs={{0,4},{1,3},{2,6},{3,1},{4,0},{5,7},{6,2},{7,5},{8,12},{9,11},{10,... | collective-permute-start | bytes 393224 | tf_op jit(solution)/shard_map/ppermute | solution.py:473
  75.7 11.1 %collective-permute-start.24 = (f32[384,256]{1,0:T(8,128)S(1)}, f32[384,256]{1,0:T(8,128)S(1)}, u32[]{:S(2)}, u32[]{:S(2)}) collective-permute-start(f32[384,256]{1,0:T(8,128)S(1)} %get-tuple-element.111), channel_id=1, source_target_pairs={{0,1},{1,2},{2,3},{3,4},{4,5},{5,6},{6,7},{7,8},{8,9},{9,10},{10,1... | collective-permute-start | bytes 1179656 | tf_op jit(solution)/shard_map/ppermute | solution.py:467
  78.5 7.8 %collective-permute-start.22 = (f32[512,128]{1,0:T(8,128)S(1)}, f32[512,128]{1,0:T(8,128)S(1)}, u32[]{:S(2)}, u32[]{:S(2)}) collective-permute-start(f32[512,128]{1,0:T(8,128)S(1)} %gather_pass.3.part), channel_id=1, source_target_pairs={{0,2},{1,5},{2,0},{3,7},{4,6},{5,1},{6,4},{7,3},{8,10},{9,13},{10,... | collective-permute-start | bytes 786440 | tf_op jit(solution)/shard_map/ppermute | solution.py:473
  79.6 1.4 %collective-permute-start.23 = (f32[384,128]{1,0:T(8,128)S(1)}, f32[384,128]{1,0:T(8,128)S(1)}, u32[]{:S(2)}, u32[]{:S(2)}) collective-permute-start(f32[384,128]{1,0:T(8,128)S(1)} %get-tuple-element.110), channel_id=1, source_target_pairs={{0,1},{1,0},{2,3},{3,2},{4,5},{5,4},{6,7},{7,6},{8,9},{9,8},{10,11... | collective-permute-start | bytes 589832 | tf_op jit(solution)/shard_map/ppermute | solution.py:463
  88.0 6.5 %collective-permute-start.25 = (f32[512,128]{1,0:T(8,128)S(1)}, f32[512,128]{1,0:T(8,128)S(1)}, u32[]{:S(2)}, u32[]{:S(2)}) collective-permute-start(f32[512,128]{1,0:T(8,128)S(1)} %get-tuple-element.113.refs_0_), channel_id=1, source_target_pairs={{0,2},{1,5},{2,0},{3,7},{4,6},{5,1},{6,4},{7,3},{8,10},{9,13},{10,... | collective-permute-start | bytes 786440 | tf_op jit(solution)/shard_map/ppermute | solution.py:473
  89.2 5.3 %collective-permute-start.26 = (f32[8,128]{1,0:T(8,128)S(1)}, f32[8,128]{1,0:T(8,128)S(1)}, u32[]{:S(2)}, u32[]{:S(2)}) collective-permute-start(f32[8,128]{1,0:T(8,128)S(1)} %get-tuple-element.114.refs_0_), channel_id=1, source_target_pairs={{0,2},{1,5},{2,0},{3,7},{4,6},{5,1},{6,4},{7,3},{8,10},{9,13},{10,... | collective-permute-start | bytes 12296 | tf_op jit(solution)/shard_map/ppermute | solution.py:473
  94.5 6.5 %collective-permute-start.27 = (f32[264,128]{1,0:T(8,128)S(1)}, f32[264,128]{1,0:T(8,128)S(1)}, u32[]{:S(2)}, u32[]{:S(2)}) collective-permute-start(f32[264,128]{1,0:T(8,128)S(1)} %get-tuple-element.116.refs_0_), channel_id=1, source_target_pairs={{0,4},{1,3},{2,6},{3,1},{4,0},{5,7},{6,2},{7,5},{8,12},{9,11},{10,... | collective-permute-start | bytes 405512 | tf_op jit(solution)/shard_map/ppermute | solution.py:473
  98.1 13.2 %collective-permute-start.31 = (f32[384,128]{1,0:T(8,128)S(1)}, f32[384,128]{1,0:T(8,128)S(1)}, u32[]{:S(2)}, u32[]{:S(2)}) collective-permute-start(f32[384,128]{1,0:T(8,128)S(1)} %get-tuple-element.130), channel_id=1, source_target_pairs={{0,1},{1,0},{2,3},{3,2},{4,5},{5,4},{6,7},{7,6},{8,9},{9,8},{10,11... | collective-permute-start | bytes 589832 | tf_op jit(solution)/shard_map/ppermute | solution.py:463
  101.1 6.1 %collective-permute-start.28 = (f32[136,128]{1,0:T(8,128)S(1)}, f32[136,128]{1,0:T(8,128)S(1)}, u32[]{:S(2)}, u32[]{:S(2)}) collective-permute-start(f32[136,128]{1,0:T(8,128)S(1)} %get-tuple-element.120.refs_0_), channel_id=1, source_target_pairs={{0,16},{1,9},{2,18},{3,11},{4,20},{5,13},{6,22},{7,15},{8,24},{9,1... | collective-permute-start | bytes 208904 | tf_op jit(solution)/shard_map/ppermute | solution.py:473
  107.2 4.0 %collective-permute-start.29 = (f32[72,128]{1,0:T(8,128)S(1)}, f32[72,128]{1,0:T(8,128)S(1)}, u32[]{:S(2)}, u32[]{:S(2)}) collective-permute-start(f32[72,128]{1,0:T(8,128)S(1)} %get-tuple-element.122.sent), channel_id=1, source_target_pairs={{0,8},{1,17},{2,10},{3,19},{4,12},{5,21},{6,14},{7,23},{8,0},{9,25... | collective-permute-start | bytes 110600 | tf_op jit(solution)/shard_map/ppermute | solution.py:473
  111.2 1.3 %collective-permute-start.30 = (f32[40,128]{1,0:T(8,128)S(1)}, f32[40,128]{1,0:T(8,128)S(1)}, u32[]{:S(2)}, u32[]{:S(2)}) collective-permute-start(f32[40,128]{1,0:T(8,128)S(1)} %get-tuple-element.127), channel_id=1, source_target_pairs={{0,1},{1,0},{2,3},{3,2},{4,5},{5,4},{6,7},{7,6},{8,9},{9,8},{10,11... | collective-permute-start | bytes 61448 | tf_op jit(solution)/shard_map/ppermute | solution.py:463
  (10 other events, 44.9 us)

commit v18 on v16

--- a/solution.py
+++ b/solution.py
@@ -474,7 +474,7 @@
 def bit_order(devices, core):
     bits = devices.bit_length() - 1
     far = list(range(3, bits))
-    return [2, 1] + far if core == 0 else [1, 2] + far[::-1]
+    return [1, 2] + far if core == 0 else [2, 1] + far[::-1]
 
 
 def swap(array, devices):

time: 113 us -> 111 us (0.982)
  waiting for transfers between devices: 78.4 us -> 66.4 us
  starting transfers between devices: 19.8 us -> 29.9 us
    ppermute x19, waiting for transfers between devices: 73.3 us -> 61.8 us  [exchange(): return lax.ppermute(array, 'user', pairs)]
    ppermute x19, starting transfers between devices: 17.2 us -> 26.6 us  [exchange(): return lax.ppermute(array, 'user', pairs)]
    ppermute x11, waiting for transfers between devices: 5.09 us -> 3.68 us  [swap(): return lax.ppermute(array, 'user', [(i, i ^ 1) for i in range(devices)])]
  transfers between devices with their start and end apart: 32 -> 32, of which waited for: 21 -> 22; matrix products, arithmetic and copies ran while one was open for 0% -> 0% of each run, Pallas kernels for 6% -> 6%
where the time goes in v18:
time: 111 us
  waiting for transfers between devices  66.4 us (60%)
  starting transfers between devices  29.9 us (27%)
  Pallas kernels  11.6 us (10%)
  local copies, waits for them, and re-layouts  2.26 us (2%)
    ppermute x19, waiting for transfers between devices, exchange(): return lax.ppermute(array, 'user', pairs)  61.8 us
    ppermute x19, starting transfers between devices, exchange(): return lax.ppermute(array, 'user', pairs)  26.6 us
    ppermute x11, waiting for transfers between devices, swap(): return lax.ppermute(array, 'user', [(i, i ^ 1) for i in range(devices)])  3.68 us
    pallas_call x3, Pallas kernels, error_pass(): pl.pallas_call(functools.partial(error_kernel, stratum), out_shape=(shape...  3.19 us
    ppermute x11, starting transfers between devices, swap(): return lax.ppermute(array, 'user', [(i, i ^ 1) for i in range(devices)])  3.05 us
    unnamed x21, local copies, waits for them, and re-layouts  2.26 us
  transfers between devices with their start and end apart: 32, of which 22 were waited for; matrix products, arithmetic and copies ran while one was open for 0% of the time, Pallas kernels for 6%

profile of v18, /device:TPU:0, one launch (start us, length us, event | category | flops | bytes accessed | tf_op | source)
XLA Modules:
  0.0 111.2 jit_solution(3972257859052128123)
XLA Ops:
  0.6 1.1 %copy-done = bf16[384,1024]{1,0:T(8,128)(2,1)S(1)} copy-done((bf16[384,1024]{1,0:T(8,128)(2,1)S(1)}, bf16[384,1024]{1,0:T(8,128)(2,1)}, u32[]{:S(2)}) %copy-start) | copy-done | bytes 786456
  5.2 1.2 %collective-permute-done.got = f32[1024,128]{1,0:T(8,128)S(1)} collective-permute-done((f32[1024,128]{1,0:T(8,128)S(1)}, f32[1024,128]{1,0:T(8,128)S(1)}, u32[]{:S(2)}, u32[]{:S(2)}) %collective-permute-start) | collective-permute-done | bytes 524320 | tf_op jit(solution)/shard_map/ppermute | solution.py:481
  6.4 2.9 %collective-permute-start.1 = (f32[512,128]{1,0:T(8,128)S(1)}, f32[512,128]{1,0:T(8,128)S(1)}, u32[]{:S(2)}, u32[]{:S(2)}) collective-permute-start(f32[512,128]{1,0:T(8,128)S(1)} %get-tuple-element.71), channel_id=1, source_target_pairs={{0,2},{1,5},{2,0},{3,7},{4,6},{5,1},{6,4},{7,3},{8,10},{9,13},{10,... | collective-permute-start | bytes 786440 | tf_op jit(solution)/shard_map/ppermute | solution.py:491
  10.6 3.6 %collective-permute-done.2.refs_1_ = f32[8,128]{1,0:T(8,128)S(1)} collective-permute-done((f32[8,128]{1,0:T(8,128)S(1)}, f32[8,128]{1,0:T(8,128)S(1)}, u32[]{:S(2)}, u32[]{:S(2)}) %collective-permute-start.2) | collective-permute-done | bytes 4128 | tf_op jit(solution)/shard_map/ppermute | solution.py:491
  14.2 1.7 %collective-permute-start.3 = (f32[264,128]{1,0:T(8,128)S(1)}, f32[264,128]{1,0:T(8,128)S(1)}, u32[]{:S(2)}, u32[]{:S(2)}) collective-permute-start(f32[264,128]{1,0:T(8,128)S(1)} %get-tuple-element.74.refs_0_), channel_id=1, source_target_pairs={{0,4},{1,3},{2,6},{3,1},{4,0},{5,7},{6,2},{7,5},{8,12},{9,11},{10,... | collective-permute-start | bytes 405512 | tf_op jit(solution)/shard_map/ppermute | solution.py:491
  16.4 2.8 %collective-permute-done.3.got.refs_1_ = f32[264,128]{1,0:T(8,128)S(1)} collective-permute-done((f32[264,128]{1,0:T(8,128)S(1)}, f32[264,128]{1,0:T(8,128)S(1)}, u32[]{:S(2)}, u32[]{:S(2)}) %collective-permute-start.3) | collective-permute-done | bytes 135200 | tf_op jit(solution)/shard_map/ppermute | solution.py:491
  19.5 1.8 %collective-permute-start.7 = (f32[264,128]{1,0:T(8,128)S(1)}, f32[264,128]{1,0:T(8,128)S(1)}, u32[]{:S(2)}, u32[]{:S(2)}) collective-permute-start(f32[264,128]{1,0:T(8,128)S(1)} %step_pass.12.later.held.refs_0_), channel_id=1, source_target_pairs={{0,8},{1,17},{2,10},{3,19},{4,12},{5,21},{6,14},{7,23},{8,0},{9,25... | collective-permute-start | bytes 405512 | tf_op jit(solution)/shard_map/ppermute | solution.py:491
  21.2 1.2 %collective-permute-start.5 = (f32[128,1024]{1,0:T(8,128)S(1)}, f32[128,1024]{1,0:T(8,128)S(1)}, u32[]{:S(2)}, u32[]{:S(2)}) collective-permute-start(f32[128,1024]{1,0:T(8,128)S(1)} %get-tuple-element.78), channel_id=1, source_target_pairs={{0,1},{1,0},{2,3},{3,2},{4,5},{5,4},{6,7},{7,6},{8,9},{9,8},{10,11... | collective-permute-start | bytes 1572872 | tf_op jit(solution)/shard_map/ppermute | solution.py:481
  22.4 3.5 %collective-permute-done.7.got.refs_1_ = f32[264,128]{1,0:T(8,128)S(1)} collective-permute-done((f32[264,128]{1,0:T(8,128)S(1)}, f32[264,128]{1,0:T(8,128)S(1)}, u32[]{:S(2)}, u32[]{:S(2)}) %collective-permute-start.7) | collective-permute-done | bytes 135200 | tf_op jit(solution)/shard_map/ppermute | solution.py:491
  26.0 2.2 %collective-permute-start.8 = (f32[264,128]{1,0:T(8,128)S(1)}, f32[264,128]{1,0:T(8,128)S(1)}, u32[]{:S(2)}, u32[]{:S(2)}) collective-permute-start(f32[264,128]{1,0:T(8,128)S(1)} %step_pass.13.held.sent), channel_id=1, source_target_pairs={{0,16},{1,9},{2,18},{3,11},{4,20},{5,13},{6,22},{7,15},{8,24},{9,1... | collective-permute-start | bytes 405512 | tf_op jit(solution)/shard_map/ppermute | solution.py:491
  28.1 4.5 %collective-permute-done.8.got = f32[264,128]{1,0:T(8,128)S(1)} collective-permute-done((f32[264,128]{1,0:T(8,128)S(1)}, f32[264,128]{1,0:T(8,128)S(1)}, u32[]{:S(2)}, u32[]{:S(2)}) %collective-permute-start.8) | collective-permute-done | bytes 135200 | tf_op jit(solution)/shard_map/ppermute | solution.py:491
  32.7 1.9 %collective-permute-start.9 = (f32[256,128]{1,0:T(8,128)S(1)}, f32[256,128]{1,0:T(8,128)S(1)}, u32[]{:S(2)}, u32[]{:S(2)}) collective-permute-start(f32[256,128]{1,0:T(8,128)S(1)} %get-tuple-element.83.part.old), channel_id=1, source_target_pairs={{0,4},{1,3},{2,6},{3,1},{4,0},{5,7},{6,2},{7,5},{8,12},{9,11},{10,... | collective-permute-start | bytes 393224 | tf_op jit(solution)/shard_map/ppermute | solution.py:491
  35.0 2.7 %collective-permute-done.9.got = f32[256,128]{1,0:T(8,128)S(1)} collective-permute-done((f32[256,128]{1,0:T(8,128)S(1)}, f32[256,128]{1,0:T(8,128)S(1)}, u32[]{:S(2)}, u32[]{:S(2)}) %collective-permute-start.9) | collective-permute-done | bytes 131104 | tf_op jit(solution)/shard_map/ppermute | solution.py:491
  37.8 1.9 %collective-permute-start.11 = (f32[512,128]{1,0:T(8,128)S(1)}, f32[512,128]{1,0:T(8,128)S(1)}, u32[]{:S(2)}, u32[]{:S(2)}) collective-permute-start(f32[512,128]{1,0:T(8,128)S(1)} %gather_pass.2.part), channel_id=1, source_target_pairs={{0,2},{1,5},{2,0},{3,7},{4,6},{5,1},{6,4},{7,3},{8,10},{9,13},{10,... | collective-permute-start | bytes 786440 | tf_op jit(solution)/shard_map/ppermute | solution.py:491
  41.1 4.3 %collective-permute-done.11.got = f32[512,128]{1,0:T(8,128)S(1)} collective-permute-done((f32[512,128]{1,0:T(8,128)S(1)}, f32[512,128]{1,0:T(8,128)S(1)}, u32[]{:S(2)}, u32[]{:S(2)}) %collective-permute-start.11) | collective-permute-done | bytes 262176 | tf_op jit(solution)/shard_map/ppermute | solution.py:491
  48.4 1.6 %collective-permute-start.15 = (f32[8,128]{1,0:T(8,128)S(1)}, f32[8,128]{1,0:T(8,128)S(1)}, u32[]{:S(2)}, u32[]{:S(2)}) collective-permute-start(f32[8,128]{1,0:T(8,128)S(1)} %get-tuple-element.96.refs_0_), channel_id=1, source_target_pairs={{0,2},{1,5},{2,0},{3,7},{4,6},{5,1},{6,4},{7,3},{8,10},{9,13},{10,... | collective-permute-start | bytes 12296 | tf_op jit(solution)/shard_map/ppermute | solution.py:491
  50.0 3.3 %collective-permute-done.15.refs_1_ = f32[8,128]{1,0:T(8,128)S(1)} collective-permute-done((f32[8,128]{1,0:T(8,128)S(1)}, f32[8,128]{1,0:T(8,128)S(1)}, u32[]{:S(2)}, u32[]{:S(2)}) %collective-permute-start.15) | collective-permute-done | bytes 4128 | tf_op jit(solution)/shard_map/ppermute | solution.py:491
  53.3 3.6 %collective-permute-start.16 = (f32[264,128]{1,0:T(8,128)S(1)}, f32[264,128]{1,0:T(8,128)S(1)}, u32[]{:S(2)}, u32[]{:S(2)}) collective-permute-start(f32[264,128]{1,0:T(8,128)S(1)} %get-tuple-element.98.refs_0_), channel_id=1, source_target_pairs={{0,4},{1,3},{2,6},{3,1},{4,0},{5,7},{6,2},{7,5},{8,12},{9,11},{10,... | collective-permute-start | bytes 405512 | tf_op jit(solution)/shard_map/ppermute | solution.py:491
  57.3 2.5 %collective-permute-done.16.got.refs_1_ = f32[264,128]{1,0:T(8,128)S(1)} collective-permute-done((f32[264,128]{1,0:T(8,128)S(1)}, f32[264,128]{1,0:T(8,128)S(1)}, u32[]{:S(2)}, u32[]{:S(2)}) %collective-permute-start.16) | collective-permute-done | bytes 135200 | tf_op jit(solution)/shard_map/ppermute | solution.py:491
  60.0 5.2 %collective-permute-done.17.got.refs_1_ = f32[264,128]{1,0:T(8,128)S(1)} collective-permute-done((f32[264,128]{1,0:T(8,128)S(1)}, f32[264,128]{1,0:T(8,128)S(1)}, u32[]{:S(2)}, u32[]{:S(2)}) %collective-permute-start.17) | collective-permute-done | bytes 135200 | tf_op jit(solution)/shard_map/ppermute | solution.py:491
  65.3 6.4 %collective-permute-done.18.got = f32[264,128]{1,0:T(8,128)S(1)} collective-permute-done((f32[264,128]{1,0:T(8,128)S(1)}, f32[264,128]{1,0:T(8,128)S(1)}, u32[]{:S(2)}, u32[]{:S(2)}) %collective-permute-start.18) | collective-permute-done | bytes 135200 | tf_op jit(solution)/shard_map/ppermute | solution.py:491
  71.9 2.1 %collective-permute-start.19 = (f32[256,128]{1,0:T(8,128)S(1)}, f32[256,128]{1,0:T(8,128)S(1)}, u32[]{:S(2)}, u32[]{:S(2)}) collective-permute-start(f32[256,128]{1,0:T(8,128)S(1)} %get-tuple-element.101.part), channel_id=1, source_target_pairs={{0,4},{1,3},{2,6},{3,1},{4,0},{5,7},{6,2},{7,5},{8,12},{9,11},{10,... | collective-permute-start | bytes 393224 | tf_op jit(solution)/shard_map/ppermute | solution.py:491
  74.3 2.6 %collective-permute-done.19.got = f32[256,128]{1,0:T(8,128)S(1)} collective-permute-done((f32[256,128]{1,0:T(8,128)S(1)}, f32[256,128]{1,0:T(8,128)S(1)}, u32[]{:S(2)}, u32[]{:S(2)}) %collective-permute-start.19) | collective-permute-done | bytes 131104 | tf_op jit(solution)/shard_map/ppermute | solution.py:491
  79.4 5.4 %collective-permute-done.22.got = f32[512,128]{1,0:T(8,128)S(1)} collective-permute-done((f32[512,128]{1,0:T(8,128)S(1)}, f32[512,128]{1,0:T(8,128)S(1)}, u32[]{:S(2)}, u32[]{:S(2)}) %collective-permute-start.22) | collective-permute-done | bytes 262176 | tf_op jit(solution)/shard_map/ppermute | solution.py:491
  85.3 1.2 %prior_pass.3 = (f32[384,128]{1,0:T(8,128)S(1)}, f32[384,128]{1,0:T(8,128)S(1)}, f32[512,128]{1,0:T(8,128)S(1)}, f32[512,128]{1,0:T(8,128)S(1)}, f32[64,128]{1,0:T(8,128)S(1)}) custom-call(bf16[768,1024]{1,0:T(8,128)(2,1)S(1)} %get-tuple-element.80.feats, bf16[1024,768]{1,0:T(8,128)(2,1)S(1)} %get-tuple-element.81.turned, f32[768,128]{1,0:T(8,128)S(1)} %part_pass.3.begun, ...), custom_call_target="tpu_custom_call" | custom-call | flops 402653184 | bytes 3145728 | tf_op jit(solution)/shard_map/prior_pass/pallas_call | solution.py:309
  87.7 2.1 %collective-permute-start.26 = (f32[8,128]{1,0:T(8,128)S(1)}, f32[8,128]{1,0:T(8,128)S(1)}, u32[]{:S(2)}, u32[]{:S(2)}) collective-permute-start(f32[8,128]{1,0:T(8,128)S(1)} %get-tuple-element.114.refs_0_), channel_id=1, source_target_pairs={{0,2},{1,5},{2,0},{3,7},{4,6},{5,1},{6,4},{7,3},{8,10},{9,13},{10,... | collective-permute-start | bytes 12296 | tf_op jit(solution)/shard_map/ppermute | solution.py:491
  89.7 3.3 %collective-permute-done.26.refs_1_ = f32[8,128]{1,0:T(8,128)S(1)} collective-permute-done((f32[8,128]{1,0:T(8,128)S(1)}, f32[8,128]{1,0:T(8,128)S(1)}, u32[]{:S(2)}, u32[]{:S(2)}) %collective-permute-start.26) | collective-permute-done | bytes 4128 | tf_op jit(solution)/shard_map/ppermute | solution.py:491
  93.0 3.5 %collective-permute-start.27 = (f32[264,128]{1,0:T(8,128)S(1)}, f32[264,128]{1,0:T(8,128)S(1)}, u32[]{:S(2)}, u32[]{:S(2)}) collective-permute-start(f32[264,128]{1,0:T(8,128)S(1)} %get-tuple-element.116.refs_0_), channel_id=1, source_target_pairs={{0,4},{1,3},{2,6},{3,1},{4,0},{5,7},{6,2},{7,5},{8,12},{9,11},{10,... | collective-permute-start | bytes 405512 | tf_op jit(solution)/shard_map/ppermute | solution.py:491
  97.1 2.5 %collective-permute-done.27.got.refs_1_ = f32[264,128]{1,0:T(8,128)S(1)} collective-permute-done((f32[264,128]{1,0:T(8,128)S(1)}, f32[264,128]{1,0:T(8,128)S(1)}, u32[]{:S(2)}, u32[]{:S(2)}) %collective-permute-start.27) | collective-permute-done | bytes 135200 | tf_op jit(solution)/shard_map/ppermute | solution.py:491
  99.7 4.3 %collective-permute-done.28.got.refs_1_ = f32[136,128]{1,0:T(8,128)S(1)} collective-permute-done((f32[136,128]{1,0:T(8,128)S(1)}, f32[136,128]{1,0:T(8,128)S(1)}, u32[]{:S(2)}, u32[]{:S(2)}) %collective-permute-start.28) | collective-permute-done | bytes 69664 | tf_op jit(solution)/shard_map/ppermute | solution.py:491
  104.1 4.8 %collective-permute-done.29.got = f32[72,128]{1,0:T(8,128)S(1)} collective-permute-done((f32[72,128]{1,0:T(8,128)S(1)}, f32[72,128]{1,0:T(8,128)S(1)}, u32[]{:S(2)}, u32[]{:S(2)}) %collective-permute-start.29) | collective-permute-done | bytes 36896 | tf_op jit(solution)/shard_map/ppermute | solution.py:491
  109.0 1.2 %collective-permute-done.30.got = f32[40,128]{1,0:T(8,128)S(1)} collective-permute-done((f32[40,128]{1,0:T(8,128)S(1)}, f32[40,128]{1,0:T(8,128)S(1)}, u32[]{:S(2)}, u32[]{:S(2)}) %collective-permute-start.30) | collective-permute-done | bytes 20512 | tf_op jit(solution)/shard_map/ppermute | solution.py:481
  (87 shorter events, 17.4 us)
Async XLA Ops:
  4.3 2.0 %collective-permute-start = (f32[1024,128]{1,0:T(8,128)S(1)}, f32[1024,128]{1,0:T(8,128)S(1)}, u32[]{:S(2)}, u32[]{:S(2)}) collective-permute-start(f32[1024,128]{1,0:T(8,128)S(1)} %get-tuple-element.69), channel_id=1, source_target_pairs={{0,1},{1,0},{2,3},{3,2},{4,5},{5,4},{6,7},{7,6},{8,9},{9,8},{10,11... | collective-permute-start | bytes 1572872 | tf_op jit(solution)/shard_map/ppermute | solution.py:481
  6.4 7.7 %collective-permute-start.1 = (f32[512,128]{1,0:T(8,128)S(1)}, f32[512,128]{1,0:T(8,128)S(1)}, u32[]{:S(2)}, u32[]{:S(2)}) collective-permute-start(f32[512,128]{1,0:T(8,128)S(1)} %get-tuple-element.71), channel_id=1, source_target_pairs={{0,2},{1,5},{2,0},{3,7},{4,6},{5,1},{6,4},{7,3},{8,10},{9,13},{10,... | collective-permute-start | bytes 786440 | tf_op jit(solution)/shard_map/ppermute | solution.py:491
  10.4 3.7 %collective-permute-start.2 = (f32[8,128]{1,0:T(8,128)S(1)}, f32[8,128]{1,0:T(8,128)S(1)}, u32[]{:S(2)}, u32[]{:S(2)}) collective-permute-start(f32[8,128]{1,0:T(8,128)S(1)} %get-tuple-element.72.refs_0_), channel_id=1, source_target_pairs={{0,2},{1,5},{2,0},{3,7},{4,6},{5,1},{6,4},{7,3},{8,10},{9,13},{10,... | collective-permute-start | bytes 12296 | tf_op jit(solution)/shard_map/ppermute | solution.py:491
  14.2 5.1 %collective-permute-start.3 = (f32[264,128]{1,0:T(8,128)S(1)}, f32[264,128]{1,0:T(8,128)S(1)}, u32[]{:S(2)}, u32[]{:S(2)}) collective-permute-start(f32[264,128]{1,0:T(8,128)S(1)} %get-tuple-element.74.refs_0_), channel_id=1, source_target_pairs={{0,4},{1,3},{2,6},{3,1},{4,0},{5,7},{6,2},{7,5},{8,12},{9,11},{10,... | collective-permute-start | bytes 405512 | tf_op jit(solution)/shard_map/ppermute | solution.py:491
  19.4 20.3 %collective-permute-start.4 = (f32[128,1024]{1,0:T(8,128)S(1)}, f32[128,1024]{1,0:T(8,128)S(1)}, u32[]{:S(2)}, u32[]{:S(2)}) collective-permute-start(f32[128,1024]{1,0:T(8,128)S(1)} %get-tuple-element.77), channel_id=1, source_target_pairs={{0,1},{1,0},{2,3},{3,2},{4,5},{5,4},{6,7},{7,6},{8,9},{9,8},{10,11... | collective-permute-start | bytes 1572872 | tf_op jit(solution)/shard_map/ppermute | solution.py:481
  19.5 6.5 %collective-permute-start.7 = (f32[264,128]{1,0:T(8,128)S(1)}, f32[264,128]{1,0:T(8,128)S(1)}, u32[]{:S(2)}, u32[]{:S(2)}) collective-permute-start(f32[264,128]{1,0:T(8,128)S(1)} %step_pass.12.later.held.refs_0_), channel_id=1, source_target_pairs={{0,8},{1,17},{2,10},{3,19},{4,12},{5,21},{6,14},{7,23},{8,0},{9,25... | collective-permute-start | bytes 405512 | tf_op jit(solution)/shard_map/ppermute | solution.py:491
  21.2 18.4 %collective-permute-start.5 = (f32[128,1024]{1,0:T(8,128)S(1)}, f32[128,1024]{1,0:T(8,128)S(1)}, u32[]{:S(2)}, u32[]{:S(2)}) collective-permute-start(f32[128,1024]{1,0:T(8,128)S(1)} %get-tuple-element.78), channel_id=1, source_target_pairs={{0,1},{1,0},{2,3},{3,2},{4,5},{5,4},{6,7},{7,6},{8,9},{9,8},{10,11... | collective-permute-start | bytes 1572872 | tf_op jit(solution)/shard_map/ppermute | solution.py:481
  22.4 17.3 %collective-permute-start.6 = (f32[128,1024]{1,0:T(8,128)S(1)}, f32[128,1024]{1,0:T(8,128)S(1)}, u32[]{:S(2)}, u32[]{:S(2)}) collective-permute-start(f32[128,1024]{1,0:T(8,128)S(1)} %get-tuple-element.79), channel_id=1, source_target_pairs={{0,1},{1,0},{2,3},{3,2},{4,5},{5,4},{6,7},{7,6},{8,9},{9,8},{10,11... | collective-permute-start | bytes 1572872 | tf_op jit(solution)/shard_map/ppermute | solution.py:481
  26.0 6.7 %collective-permute-start.8 = (f32[264,128]{1,0:T(8,128)S(1)}, f32[264,128]{1,0:T(8,128)S(1)}, u32[]{:S(2)}, u32[]{:S(2)}) collective-permute-start(f32[264,128]{1,0:T(8,128)S(1)} %step_pass.13.held.sent), channel_id=1, source_target_pairs={{0,16},{1,9},{2,18},{3,11},{4,20},{5,13},{6,22},{7,15},{8,24},{9,1... | collective-permute-start | bytes 405512 | tf_op jit(solution)/shard_map/ppermute | solution.py:491
  32.7 2.0 %collective-permute-start.10 = (f32[8,128]{1,0:T(8,128)S(1)}, f32[8,128]{1,0:T(8,128)S(1)}, u32[]{:S(2)}, u32[]{:S(2)}) collective-permute-start(f32[8,128]{1,0:T(8,128)S(1)} %get-tuple-element.84.stats), channel_id=1, source_target_pairs={{0,1},{1,0},{2,3},{3,2},{4,5},{5,4},{6,7},{7,6},{8,9},{9,8},{10,11... | collective-permute-start | bytes 12296 | tf_op jit(solution)/shard_map/ppermute | solution.py:481
  32.7 5.0 %collective-permute-start.9 = (f32[256,128]{1,0:T(8,128)S(1)}, f32[256,128]{1,0:T(8,128)S(1)}, u32[]{:S(2)}, u32[]{:S(2)}) collective-permute-start(f32[256,128]{1,0:T(8,128)S(1)} %get-tuple-element.83.part.old), channel_id=1, source_target_pairs={{0,4},{1,3},{2,6},{3,1},{4,0},{5,7},{6,2},{7,5},{8,12},{9,11},{10,... | collective-permute-start | bytes 393224 | tf_op jit(solution)/shard_map/ppermute | solution.py:491
  34.9 11.0 %collective-permute-start.13 = (f32[384,256]{1,0:T(8,128)S(1)}, f32[384,256]{1,0:T(8,128)S(1)}, u32[]{:S(2)}, u32[]{:S(2)}) collective-permute-start(f32[384,256]{1,0:T(8,128)S(1)} %get-tuple-element.93), channel_id=1, source_target_pairs={{0,1},{1,2},{2,3},{3,4},{4,5},{5,6},{6,7},{7,8},{8,9},{9,10},{10,1... | collective-permute-start | bytes 1179656 | tf_op jit(solution)/shard_map/ppermute | solution.py:485
  37.8 7.6 %collective-permute-start.11 = (f32[512,128]{1,0:T(8,128)S(1)}, f32[512,128]{1,0:T(8,128)S(1)}, u32[]{:S(2)}, u32[]{:S(2)}) collective-permute-start(f32[512,128]{1,0:T(8,128)S(1)} %gather_pass.2.part), channel_id=1, source_target_pairs={{0,2},{1,5},{2,0},{3,7},{4,6},{5,1},{6,4},{7,3},{8,10},{9,13},{10,... | collective-permute-start | bytes 786440 | tf_op jit(solution)/shard_map/ppermute | solution.py:491
  39.7 1.4 %collective-permute-start.12 = (f32[384,128]{1,0:T(8,128)S(1)}, f32[384,128]{1,0:T(8,128)S(1)}, u32[]{:S(2)}, u32[]{:S(2)}) collective-permute-start(f32[384,128]{1,0:T(8,128)S(1)} %get-tuple-element.92), channel_id=1, source_target_pairs={{0,1},{1,0},{2,3},{3,2},{4,5},{5,4},{6,7},{7,6},{8,9},{9,8},{10,11... | collective-permute-start | bytes 589832 | tf_op jit(solution)/shard_map/ppermute | solution.py:481
  46.7 6.5 %collective-permute-start.14 = (f32[512,128]{1,0:T(8,128)S(1)}, f32[512,128]{1,0:T(8,128)S(1)}, u32[]{:S(2)}, u32[]{:S(2)}) collective-permute-start(f32[512,128]{1,0:T(8,128)S(1)} %get-tuple-element.95.refs_0_), channel_id=1, source_target_pairs={{0,2},{1,5},{2,0},{3,7},{4,6},{5,1},{6,4},{7,3},{8,10},{9,13},{10,... | collective-permute-start | bytes 786440 | tf_op jit(solution)/shard_map/ppermute | solution.py:491
  48.4 4.8 %collective-permute-start.15 = (f32[8,128]{1,0:T(8,128)S(1)}, f32[8,128]{1,0:T(8,128)S(1)}, u32[]{:S(2)}, u32[]{:S(2)}) collective-permute-start(f32[8,128]{1,0:T(8,128)S(1)} %get-tuple-element.96.refs_0_), channel_id=1, source_target_pairs={{0,2},{1,5},{2,0},{3,7},{4,6},{5,1},{6,4},{7,3},{8,10},{9,13},{10,... | collective-permute-start | bytes 12296 | tf_op jit(solution)/shard_map/ppermute | solution.py:491
  53.3 6.5 %collective-permute-start.16 = (f32[264,128]{1,0:T(8,128)S(1)}, f32[264,128]{1,0:T(8,128)S(1)}, u32[]{:S(2)}, u32[]{:S(2)}) collective-permute-start(f32[264,128]{1,0:T(8,128)S(1)} %get-tuple-element.98.refs_0_), channel_id=1, source_target_pairs={{0,4},{1,3},{2,6},{3,1},{4,0},{5,7},{6,2},{7,5},{8,12},{9,11},{10,... | collective-permute-start | bytes 405512 | tf_op jit(solution)/shard_map/ppermute | solution.py:491
  59.8 5.4 %collective-permute-start.17 = (f32[264,128]{1,0:T(8,128)S(1)}, f32[264,128]{1,0:T(8,128)S(1)}, u32[]{:S(2)}, u32[]{:S(2)}) collective-permute-start(f32[264,128]{1,0:T(8,128)S(1)} %step_pass.15.held.refs_0_), channel_id=1, source_target_pairs={{0,8},{1,17},{2,10},{3,19},{4,12},{5,21},{6,14},{7,23},{8,0},{9,25... | collective-permute-start | bytes 405512 | tf_op jit(solution)/shard_map/ppermute | solution.py:491
  59.9 14.1 %collective-permute-start.21 = (f32[384,128]{1,0:T(8,128)S(1)}, f32[384,128]{1,0:T(8,128)S(1)}, u32[]{:S(2)}, u32[]{:S(2)}) collective-permute-start(f32[384,128]{1,0:T(8,128)S(1)} %get-tuple-element.105), channel_id=1, source_target_pairs={{0,1},{1,0},{2,3},{3,2},{4,5},{5,4},{6,7},{7,6},{8,9},{9,8},{10,11... | collective-permute-start | bytes 589832 | tf_op jit(solution)/shard_map/ppermute | solution.py:481
  65.3 6.5 %collective-permute-start.18 = (f32[264,128]{1,0:T(8,128)S(1)}, f32[264,128]{1,0:T(8,128)S(1)}, u32[]{:S(2)}, u32[]{:S(2)}) collective-permute-start(f32[264,128]{1,0:T(8,128)S(1)} %step_pass.16.held.sent), channel_id=1, source_target_pairs={{0,16},{1,9},{2,18},{3,11},{4,20},{5,13},{6,22},{7,15},{8,24},{9,1... | collective-permute-start | bytes 405512 | tf_op jit(solution)/shard_map/ppermute | solution.py:491
  71.8 2.2 %collective-permute-start.20 = (f32[8,128]{1,0:T(8,128)S(1)}, f32[8,128]{1,0:T(8,128)S(1)}, u32[]{:S(2)}, u32[]{:S(2)}) collective-permute-start(f32[8,128]{1,0:T(8,128)S(1)} %get-tuple-element.102.stats), channel_id=1, source_target_pairs={{0,1},{1,0},{2,3},{3,2},{4,5},{5,4},{6,7},{7,6},{8,9},{9,8},{10,11... | collective-permute-start | bytes 12296 | tf_op jit(solution)/shard_map/ppermute | solution.py:481
  71.9 5.0 %collective-permute-start.19 = (f32[256,128]{1,0:T(8,128)S(1)}, f32[256,128]{1,0:T(8,128)S(1)}, u32[]{:S(2)}, u32[]{:S(2)}) collective-permute-start(f32[256,128]{1,0:T(8,128)S(1)} %get-tuple-element.101.part), channel_id=1, source_target_pairs={{0,4},{1,3},{2,6},{3,1},{4,0},{5,7},{6,2},{7,5},{8,12},{9,11},{10,... | collective-permute-start | bytes 393224 | tf_op jit(solution)/shard_map/ppermute | solution.py:491
  74.2 11.1 %collective-permute-start.24 = (f32[384,256]{1,0:T(8,128)S(1)}, f32[384,256]{1,0:T(8,128)S(1)}, u32[]{:S(2)}, u32[]{:S(2)}) collective-permute-start(f32[384,256]{1,0:T(8,128)S(1)} %get-tuple-element.111), channel_id=1, source_target_pairs={{0,1},{1,2},{2,3},{3,4},{4,5},{5,6},{6,7},{7,8},{8,9},{9,10},{10,1... | collective-permute-start | bytes 1179656 | tf_op jit(solution)/shard_map/ppermute | solution.py:485
  77.0 7.8 %collective-permute-start.22 = (f32[512,128]{1,0:T(8,128)S(1)}, f32[512,128]{1,0:T(8,128)S(1)}, u32[]{:S(2)}, u32[]{:S(2)}) collective-permute-start(f32[512,128]{1,0:T(8,128)S(1)} %gather_pass.3.part), channel_id=1, source_target_pairs={{0,2},{1,5},{2,0},{3,7},{4,6},{5,1},{6,4},{7,3},{8,10},{9,13},{10,... | collective-permute-start | bytes 786440 | tf_op jit(solution)/shard_map/ppermute | solution.py:491
  77.4 2.1 %collective-permute-start.23 = (f32[384,128]{1,0:T(8,128)S(1)}, f32[384,128]{1,0:T(8,128)S(1)}, u32[]{:S(2)}, u32[]{:S(2)}) collective-permute-start(f32[384,128]{1,0:T(8,128)S(1)} %get-tuple-element.110), channel_id=1, source_target_pairs={{0,1},{1,0},{2,3},{3,2},{4,5},{5,4},{6,7},{7,6},{8,9},{9,8},{10,11... | collective-permute-start | bytes 589832 | tf_op jit(solution)/shard_map/ppermute | solution.py:481
  86.5 6.5 %collective-permute-start.25 = (f32[512,128]{1,0:T(8,128)S(1)}, f32[512,128]{1,0:T(8,128)S(1)}, u32[]{:S(2)}, u32[]{:S(2)}) collective-permute-start(f32[512,128]{1,0:T(8,128)S(1)} %get-tuple-element.113.refs_0_), channel_id=1, source_target_pairs={{0,2},{1,5},{2,0},{3,7},{4,6},{5,1},{6,4},{7,3},{8,10},{9,13},{10,... | collective-permute-start | bytes 786440 | tf_op jit(solution)/shard_map/ppermute | solution.py:491
  87.7 5.3 %collective-permute-start.26 = (f32[8,128]{1,0:T(8,128)S(1)}, f32[8,128]{1,0:T(8,128)S(1)}, u32[]{:S(2)}, u32[]{:S(2)}) collective-permute-start(f32[8,128]{1,0:T(8,128)S(1)} %get-tuple-element.114.refs_0_), channel_id=1, source_target_pairs={{0,2},{1,5},{2,0},{3,7},{4,6},{5,1},{6,4},{7,3},{8,10},{9,13},{10,... | collective-permute-start | bytes 12296 | tf_op jit(solution)/shard_map/ppermute | solution.py:491
  93.0 6.5 %collective-permute-start.27 = (f32[264,128]{1,0:T(8,128)S(1)}, f32[264,128]{1,0:T(8,128)S(1)}, u32[]{:S(2)}, u32[]{:S(2)}) collective-permute-start(f32[264,128]{1,0:T(8,128)S(1)} %get-tuple-element.116.refs_0_), channel_id=1, source_target_pairs={{0,4},{1,3},{2,6},{3,1},{4,0},{5,7},{6,2},{7,5},{8,12},{9,11},{10,... | collective-permute-start | bytes 405512 | tf_op jit(solution)/shard_map/ppermute | solution.py:491
  96.6 12.4 %collective-permute-start.31 = (f32[384,128]{1,0:T(8,128)S(1)}, f32[384,128]{1,0:T(8,128)S(1)}, u32[]{:S(2)}, u32[]{:S(2)}) collective-permute-start(f32[384,128]{1,0:T(8,128)S(1)} %get-tuple-element.130), channel_id=1, source_target_pairs={{0,1},{1,0},{2,3},{3,2},{4,5},{5,4},{6,7},{7,6},{8,9},{9,8},{10,11... | collective-permute-start | bytes 589832 | tf_op jit(solution)/shard_map/ppermute | solution.py:481
  99.6 4.4 %collective-permute-start.28 = (f32[136,128]{1,0:T(8,128)S(1)}, f32[136,128]{1,0:T(8,128)S(1)}, u32[]{:S(2)}, u32[]{:S(2)}) collective-permute-start(f32[136,128]{1,0:T(8,128)S(1)} %get-tuple-element.120.refs_0_), channel_id=1, source_target_pairs={{0,8},{1,17},{2,10},{3,19},{4,12},{5,21},{6,14},{7,23},{8,0},{9,25... | collective-permute-start | bytes 208904 | tf_op jit(solution)/shard_map/ppermute | solution.py:491
  104.0 4.9 %collective-permute-start.29 = (f32[72,128]{1,0:T(8,128)S(1)}, f32[72,128]{1,0:T(8,128)S(1)}, u32[]{:S(2)}, u32[]{:S(2)}) collective-permute-start(f32[72,128]{1,0:T(8,128)S(1)} %get-tuple-element.122.sent), channel_id=1, source_target_pairs={{0,16},{1,9},{2,18},{3,11},{4,20},{5,13},{6,22},{7,15},{8,24},{9,1... | collective-permute-start | bytes 110600 | tf_op jit(solution)/shard_map/ppermute | solution.py:491
  108.9 1.3 %collective-permute-start.30 = (f32[40,128]{1,0:T(8,128)S(1)}, f32[40,128]{1,0:T(8,128)S(1)}, u32[]{:S(2)}, u32[]{:S(2)}) collective-permute-start(f32[40,128]{1,0:T(8,128)S(1)} %get-tuple-element.127), channel_id=1, source_target_pairs={{0,1},{1,0},{2,3},{3,2},{4,5},{5,4},{6,7},{7,6},{8,9},{9,8},{10,11... | collective-permute-start | bytes 61448 | tf_op jit(solution)/shard_map/ppermute | solution.py:481
  (10 other events, 40.2 us)
